TPU v7x, 32 devices: a whole 2x2x4 slice. The times are simulated.
32 devices in a mesh: rep: 8 (over y, x, core), fsdp: 4 (over z).
Axes of the slice: x: 2, y: 2, z: 4, core: 2. Of those that a mesh axis runs over, the one named last changes fastest.
Arguments:
- params: float32 [8, 2560, 2560], P('rep', 'fsdp'), may hold values from -6 to 6
- push_weight: float32 [8], P('rep'), may hold values from 0.5 to 2
- inbox_params: float32 [8, 2560, 2560], P('rep', 'fsdp'), may hold values from -3 to 3
- inbox_weight: float32 [8], P('rep'), may hold values from 0.25 to 1
- heads: bfloat16 [8, 1536, 2560], P('rep', 'fsdp'), may hold values from -6 to 6
- residual: bfloat16 [8, 1536, 2560], P('rep', 'fsdp'), may hold values from -40 to 40
- cotangent: bfloat16 [8, 1536, 2560], P('rep', 'fsdp'), may hold values from -6 to 6
- gain: float32 [2560], replicated, may hold values from 0.5 to 2
- offset: int32 [8], replicated, may hold values from 1 to 4, as said below
Outputs:
- new_params: float32 [8, 2560, 2560], P('rep', 'fsdp')
- new_weight: float32 [8], P('rep')
- outbox_params: float32 [8, 2560, 2560], P('rep', 'fsdp')
- outbox_weight: float32 [8], P('rep')
- grad_heads: bfloat16 [8, 1536, 2560], P('rep', 'fsdp')
Inputs may be any that keep to these rules, and one draw needn't show every extreme that they name: `offset`: each entry a power of two below 8; 1 and 4 both occur in every plan.
All inputs are finite; a program needn't handle non-finite values.
Results may differ from a plain program's by a relative error of at most 0.0057.
Values may be sent and summed in bfloat16 or wider, within the bound.
No kernel may reach another device: no remote copies, remote signals or barrier semaphores. Data moves between devices by JAX's collectives and lax.ppermute only.
A program may use at most 192 MiB of HBM per device.

v0:
```python
from functools import partial

import jax
import jax.numpy as jnp
from jax import lax
from jax.experimental import pallas as pl
from jax.experimental.pallas import tpu as pltpu
from jax.sharding import PartitionSpec as P

STREAMS = ((96, 96), (96, 96))
MIB = 1 << 20
TOKEN = jax.ShapeDtypeStruct((8, 128), jnp.float32)


def call(body, name, grid, ins, outs, scalars=(), scratch=(), flops=0, moved=0):
    return pl.pallas_call(
        body,
        name=name,
        out_shape=[jax.ShapeDtypeStruct(shape, kind) for shape, kind, _, _ in outs],
        grid_spec=pltpu.PrefetchScalarGridSpec(
            num_scalar_prefetch=len(scalars),
            grid=grid,
            in_specs=[pl.BlockSpec(block, place) for _, block, place in ins],
            out_specs=[pl.BlockSpec(block, place) for _, _, block, place in outs],
            scratch_shapes=scratch,
        ),
        compiler_params=pltpu.CompilerParams(vmem_limit_bytes=58 * MIB),
        cost_estimate=pl.CostEstimate(flops=flops, bytes_accessed=moved, transcendentals=0),
    )(*scalars, *(array for array, _, _ in ins))


def fixed(*place):
    return lambda *_: place


def token_in(token):
    return (token, (8, 128), fixed(0, 0))


TOKEN_OUT = ((8, 128), jnp.float32, (8, 128), fixed(0, 0))


def hop(value, step, pairs):
    return lax.ppermute(value, "fsdp", [(i, i + step) for i in pairs])


def hops(right, left, rights, lefts):
    return hop(right, 1, rights), hop(left, -1, lefts)


def tile_of(width):
    return 512 if width % 512 == 0 else width


def cut_heads(heads, start, size, members, token):
    inner = heads.shape[1]
    rows = inner // members
    step = 48

    def body(heads_ref, *refs):
        for k in range(members):
            refs[-1][k] = heads_ref[:, k * rows : (k + 1) * rows]

    return call(
        body,
        "cut_heads",
        (size // step,),
        [(heads, (step, inner), lambda i: (start // step + i, 0))]
        + ([] if token is None else [token_in(token)]),
        [((members, size, rows), heads.dtype, (members, step, rows), lambda i: (0, i, 0))],
        moved=4 * size * inner,
    )[0]


def partial_products(mine, weights, token):
    members, size, rows = mine.shape
    width = weights.shape[1]
    tile = tile_of(width)

    def body(mine_ref, weights_ref, token_ref, out_ref, last_ref, first_ref):
        product = jnp.dot(
            mine_ref[...].reshape(members * size, rows),
            weights_ref[...],
            preferred_element_type=jnp.float32,
        ).astype(jnp.bfloat16)
        out_ref[...] = product.reshape(members, size, tile)
        last_ref[...] = product[(members - 1) * size :]
        first_ref[...] = product[:size]

    flat = ((size, width), jnp.bfloat16, (size, tile), lambda j: (0, j))
    return call(
        body,
        "partial_products",
        (width // tile,),
        [
            (mine, (members, size, rows), fixed(0, 0, 0)),
            (weights, (rows, tile), lambda j: (0, j)),
            token_in(token),
        ],
        [
            (
                (members, size, width),
                jnp.bfloat16,
                (members, size, tile),
                lambda j: (0, 0, j),
            ),
            flat,
            flat,
        ],
        flops=2 * members * size * rows * width,
        moved=2 * (members * size * (rows + width) + rows * width),
    )


def next_payload(right, left, parts, scalars, pick):
    members, size, width = parts.shape
    tile = tile_of(width)

    def joined(arrived, part, counts):
        if pick:
            return jnp.where(counts, part, arrived)
        weight = jnp.where(counts, 1.0, 0.0)
        return (arrived.astype(jnp.float32) + weight * part.astype(jnp.float32)).astype(
            jnp.bfloat16
        )

    def body(s, right_ref, left_ref, of_right, of_left, right_out, left_out, token_out):
        right_out[...] = joined(right_ref[...], of_right[0], s[1] > 0)
        left_out[...] = joined(left_ref[...], of_left[0], s[3] > 0)
        token_out[...] = jnp.zeros((8, 128), jnp.float32)

    here = (size, tile), lambda j, s: (0, j)
    flat = ((size, width), jnp.bfloat16) + here
    return call(
        body,
        "next_payload",
        (width // tile,),
        [
            (right,) + here,
            (left,) + here,
            (parts, (1, size, tile), lambda j, s: (s[0], 0, j)),
            (parts, (1, size, tile), lambda j, s: (s[2], 0, j)),
        ],
        [flat, flat, TOKEN_OUT],
        scalars=(scalars,),
        flops=2 * size * width,
        moved=12 * size * width,
    )


def unit_gradient(right, left, parts, place, residual, cotangent, gain, start, token):
    members, size, width = parts.shape
    step = 32

    def body(s, right_ref, left_ref, own_ref, residual_ref, cot_ref, gain_ref, *refs):
        product = (
            right_ref[...].astype(jnp.float32)
            + left_ref[...].astype(jnp.float32)
            + own_ref[0].astype(jnp.float32)
        )
        summed = residual_ref[...].astype(jnp.float32) + product
        inverse = lax.rsqrt(jnp.mean(summed * summed, axis=-1, keepdims=True) + 1e-05)
        scaled_cot = gain_ref[...] * cot_ref[...].astype(jnp.float32)
        along = jnp.mean(scaled_cot * summed, axis=-1, keepdims=True)
        refs[-1][...] = (
            inverse * scaled_cot - summed * (inverse * inverse * inverse * along)
        ).astype(jnp.bfloat16)

    here = (step, width), lambda i, s: (i, 0)
    there = (step, width), lambda i, s: (start // step + i, 0)
    return call(
        body,
        "unit_gradient",
        (size // step,),
        [
            (right,) + here,
            (left,) + here,
            (parts, (1, step, width), lambda i, s: (s[0], i, 0)),
            (residual,) + there,
            (cotangent,) + there,
            (gain, (1, width), fixed(0, 0)),
        ]
        + ([] if token is None else [token_in(token)]),
        [((size, width), jnp.bfloat16) + here],
        scalars=(place,),
        flops=12 * size * width,
        moved=12 * size * width,
    )[0]


def stack_of(refs, members, me):
    count = 2 * members - 1
    rows = []
    for c in range(len(refs) // count):
        own, rights, lefts = (
            refs[c * count],
            refs[c * count + 1 : c * count + members],
            refs[c * count + members : (c + 1) * count],
        )
        rows.append(own[...])
        for k in range(members - 1):
            rows.append(jnp.where(me > k, rights[k][...], lefts[members - 2 - k][...]))
    return jnp.concatenate(rows, axis=0)


def unit_ins(units, tile):
    return [
        (unit, (unit.shape[0], tile), lambda j, s: (0, j)) for chunk in units for unit in chunk
    ]


def mine_ins(mine):
    return [(block, block.shape, fixed(0, 0, 0)) for block in mine]


def turned_into(scratch, mine_refs, order):
    members = mine_refs[0].shape[0]
    stack = jnp.concatenate([ref[order[k]] for ref in mine_refs for k in range(members)], axis=0)
    scratch[...] = stack.T


def weight_step(units, mine, order, kept, numer, inbox):
    members, _, rows = mine[0].shape
    width = numer.shape[1] if kept is None else kept.shape[1]
    tile = tile_of(width)
    count = len(units) * len(units[0])
    chunks = len(units)
    total = sum(members * block.shape[1] for block in mine)

    def body(s, *refs):
        units_ref, mine_refs = refs[:count], refs[count : count + chunks]
        rest = refs[count + chunks : -1]
        turned = refs[-1]

        @pl.when(pl.program_id(0) == 0)
        def _():
            turned_into(turned, mine_refs, s)

        weight = jnp.dot(
            turned[...], stack_of(units_ref, members, s[0]), preferred_element_type=jnp.float32
        )
        if kept is None:
            numer_ref, kept_out, token_out = rest
            kept_out[...] = 0.5 * (numer_ref[...] - 0.004 * weight)
            token_out[...] = jnp.zeros((8, 128), jnp.float32)
        else:
            kept_ref, inbox_ref, new_out, kept_out = rest
            now = kept_ref[...] - 0.5 * 0.004 * weight
            new_out[...] = now + inbox_ref[...]
            kept_out[...] = now.astype(jnp.bfloat16)

    columns = (rows, tile), lambda j, s: (0, j)
    whole = ((rows, width), jnp.float32) + columns
    return call(
        body,
        "weight_step",
        (width // tile,),
        unit_ins(units, tile)
        + mine_ins(mine)
        + ([(numer,) + columns] if kept is None else [(kept,) + columns, (inbox,) + columns]),
        [whole, TOKEN_OUT]
        if kept is None
        else [whole, ((rows, width), jnp.bfloat16) + columns],
        scalars=(order,),
        scratch=[pltpu.VMEM((rows, total), jnp.bfloat16)],
        flops=2 * total * rows * width,
        moved=2 * count * units[0][0].shape[0] * width + 12 * rows * width,
    )


def grad_rows(units, weights, order):
    members = (len(units[0]) + 1) // 2
    sizes = [chunk[0].shape[0] for chunk in units]
    rows, width = weights.shape
    tile = tile_of(width)
    steps = width // tile
    count = len(units) * len(units[0])
    total = members * sum(sizes)

    def body(s, *refs):
        weights_ref, grad_ref, acc = refs[count:]
        j = pl.program_id(0)
        grad = lax.dot_general(
            stack_of(refs[:count], members, s[0]),
            weights_ref[...],
            (((1,), (1,)), ((), ())),
            preferred_element_type=jnp.float32,
        )

        @pl.when(j == 0)
        def _():
            acc[...] = grad

        @pl.when(j > 0)
        def _():
            acc[...] += grad

        @pl.when(j == steps - 1)
        def _():
            at, row = 0, 0
            for size in sizes:
                for k in range(members):
                    grad_ref[s[k], row : row + size] = acc[at : at + size].astype(jnp.bfloat16)
                    at += size
                row += size

    return call(
        body,
        "grad_rows",
        (steps,),
        unit_ins(units, tile) + [(weights, (rows, tile), lambda j, s: (0, j))],
        [
            (
                (members, sum(sizes), rows),
                jnp.bfloat16,
                (members, sum(sizes), rows),
                fixed(0, 0, 0),
            )
        ],
        scalars=(order,),
        scratch=[pltpu.VMEM((total, rows), jnp.float32)],
        flops=2 * total * rows * width,
        moved=2 * count * sizes[0] * width + 2 * rows * width,
    )[0]


def joined_rows(blocks):
    members, tokens, rows = blocks.shape
    step = 96

    def body(blocks_ref, out_ref):
        for k in range(members):
            out_ref[:, k * rows : (k + 1) * rows] = blocks_ref[k]

    return call(
        body,
        "joined_rows",
        (tokens // step,),
        [(blocks, (members, step, rows), lambda i: (0, i, 0))],
        [
            (
                (tokens, members * rows),
                blocks.dtype,
                (step, members * rows),
                lambda i: (i, 0),
            )
        ],
        moved=4 * members * tokens * rows,
    )[0]


def widened(value):
    rows, width = value.shape
    step = 64

    def body(value_ref, out_ref):
        out_ref[...] = value_ref[...].astype(jnp.float32)

    block = (step, width), lambda i: (i, 0)
    return call(
        body,
        "widened",
        (rows // step,),
        [(value,) + block],
        [((rows, width), jnp.float32) + block],
        moved=6 * rows * width,
    )[0]


def swapped(blocks):
    return lax.all_to_all(blocks, "fsdp", 0, 0, tiled=False)


def tail(kept, units, weights, grads, order, bit_place):
    length = lax.axis_size("rep")
    sent = lax.ppermute(
        kept, "rep", [(i, (i + (1 << bit_place)) % length) for i in range(length)]
    )
    last = grad_rows(units, weights, order)
    back = swapped(jnp.concatenate(grads + [last], axis=1))
    return sent, joined_rows(back)


def local(
    params, push_weight, inbox_params, inbox_weight, heads, residual, cotangent, gain, offset
):
    numer = params[0]
    weight_one = push_weight[0]
    members = lax.axis_size("fsdp")
    me = lax.axis_index("fsdp").astype(jnp.int32)
    tokens, inner = heads.shape[1:]
    rows, width = numer.shape
    scaling = inner ** (-0.5)
    rounds = len(STREAMS[0])
    assert sum(map(sum, STREAMS)) == tokens

    replicas = lax.axis_size("rep")
    levels = replicas.bit_length() - 1
    powers = jnp.left_shift(jnp.ones((levels,), jnp.int32), jnp.arange(levels, dtype=jnp.int32))
    level_index = jnp.sum(jnp.where(powers == offset[0], jnp.arange(levels, dtype=jnp.int32), 0))
    half_weight = 0.5 * push_weight
    arrived = [
        lax.ppermute(half_weight, "rep", [(i, (i + (1 << b)) % replicas) for i in range(replicas)])
        for b in range(levels)
    ]
    outbox_weight = arrived[0]
    for b in range(1, levels):
        outbox_weight = jnp.where(level_index == b, arrived[b], outbox_weight)

    order = jnp.mod(me - jnp.arange(members, dtype=jnp.int32), members)
    own = me[None]
    weights = (numer / weight_one * scaling).astype(jnp.bfloat16)
    everyone = range(members - 1), range(1, members)

    def scalars(t):
        ahead = members - 1 - t
        return jnp.stack(
            [
                jnp.minimum(me + ahead, members - 1),
                (me <= t).astype(jnp.int32),
                jnp.maximum(me - ahead, 0),
                (me >= ahead).astype(jnp.int32),
            ]
        )

    at = 0
    starts = []
    for e in range(rounds):
        starts.append([])
        for sizes in STREAMS:
            starts[e].append(at)
            at += sizes[e]

    count = len(STREAMS)
    mine = [[None] * count for _ in range(rounds)]
    units = [[None] * count for _ in range(rounds)]
    before = [None] * count
    hint = [jnp.broadcast_to(outbox_weight[None], (8, 128))] * count
    kept = None
    grads = []

    def fetch(e, q, token):
        piece = cut_heads(heads[0], starts[e][q], STREAMS[q][e], members, token)
        mine[e][q] = swapped(piece)

    for q in range(count):
        fetch(0, q, None)
    done = None
    for e in range(rounds):
        parts, moving = [None] * count, [None] * count
        for q in range(count):
            parts[q], last, first = partial_products(mine[e][q], weights, hint[q])
            if e == 0:
                moving[q] = hops(last, first, range(1), range(members - 1, members))
            else:
                right, left, _ = next_payload(*before[q], parts[q], scalars(0), True)
                moving[q] = hops(right, left, *everyone)
                units[e - 1][q][1].append(moving[q][0])
                units[e - 1][q][2].append(moving[q][1])
        for t in range(1, members - 1):
            for q in range(count):
                right, left, token = next_payload(*moving[q], parts[q], scalars(t), False)
                if t == 1 and e + 1 < rounds:
                    fetch(e + 1, q, token)
                hint[q] = token
                if e == 0:
                    pairs = range(t + 1), range(members - 1 - t, members)
                else:
                    pairs = everyone
                moving[q] = hops(right, left, *pairs)
                if e > 0 and t < members - 2:
                    units[e - 1][q][1].append(moving[q][0])
                    units[e - 1][q][2].append(moving[q][1])
        if e > 0:
            flat = [[u] + r + l for u, r, l in units[e - 1]]
            kept, done = weight_step(flat, mine[e - 1], order, kept, numer, None)
            grads.append(grad_rows(flat, weights, order))
        for q in range(count):
            unit = unit_gradient(
                *moving[q],
                parts[q],
                own,
                residual[0],
                cotangent[0],
                gain[None],
                starts[e][q],
                done if q == count - 1 else None,
            )
            before[q] = hops(unit, unit, *everyone)
            units[e][q] = (unit, [before[q][0]], [before[q][1]])
    for s in range(1, members - 1):
        for q in range(count):
            before[q] = hops(*before[q], range(s, members - 1), range(1, members - s))
            units[-1][q][1].append(before[q][0])
            units[-1][q][2].append(before[q][1])
    flat = [[u] + r + l for u, r, l in units[-1]]
    new_params, half = weight_step(flat, mine[-1], order, kept, None, inbox_params[0])
    new_weight = 0.5 * push_weight + inbox_weight
    branches = [partial(tail, half, flat, weights, grads, order, place) for place in range(levels)]
    sent, grad_heads = lax.switch(level_index, branches)
    return (new_params[None], new_weight, widened(sent)[None], outbox_weight, grad_heads[None])


def solution(mesh):
    placed = (
        P("rep", "fsdp", None),
        P("rep"),
        P("rep", "fsdp", None),
        P("rep"),
        P("rep", "fsdp", None),
        P("rep", "fsdp", None),
        P("rep", "fsdp", None),
        P(),
        P(),
    )
    return jax.shard_map(
        local,
        mesh=mesh,
        in_specs=placed,
        out_specs=(
            P("rep", "fsdp", None),
            P("rep"),
            P("rep", "fsdp", None),
            P("rep"),
            P("rep", "fsdp", None),
        ),
        check_vma=False,
    )
```

profile of v0, /device:TPU:0, one launch (start us, length us, event | category | flops | bytes accessed | tf_op | source)
XLA Modules:
  0.0 384.0 jit_solution(8602519895397449622)
XLA Ops:
  0.6 1.8 cut_heads.4
  2.4 6.3 %all-to-all-start.3 = ((bf16[4,96,640]{2,1,0:T(8,128)(2,1)}), bf16[4,96,640]{2,1,0:T(8,128)(2,1)S(1)}, u32[]{:S(2)}, u32[]{:S(2)}) async-start(bf16[4,96,640]{2,1,0:T(8,128)(2,1)} %cut_heads.4), calls=%async_computation.3 | async-start | bytes 983040 | tf_op jit(solution)/shard_map/all_to_all | solution.py:371
  10.4 2.8 collective-permute-start.4
  13.2 2.8 collective-permute-start.3
  16.0 1.8 cut_heads.6
  19.6 2.9 all-to-all-done.3.mine_ref.refs_14_
  22.5 4.1 %all-to-all-start.5 = ((bf16[4,96,640]{2,1,0:T(8,128)(2,1)}), bf16[4,96,640]{2,1,0:T(8,128)(2,1)}, u32[]{:S(2)}, u32[]{:S(2)}) async-start(bf16[4,96,640]{2,1,0:T(8,128)(2,1)} %cut_heads.6), calls=%async_computation.5 | async-start | bytes 983040 | tf_op jit(solution)/shard_map/all_to_all | solution.py:371
  26.7 3.6 multiply_convert_fusion.weights_ref.refs_14_
  32.8 5.0 %partial_products.4 = (bf16[4,96,2560]{2,1,0:T(8,128)(2,1)}, bf16[96,2560]{1,0:T(8,128)(2,1)}, bf16[96,2560]{1,0:T(8,128)(2,1)}) custom-call(bf16[4,96,640]{2,1,0:T(8,128)(2,1)} %copy-done.17, bf16[640,2560]{1,0:T(8,128)(2,1)S(1)} %multiply_convert_fusion.weights_ref.refs_14_, f32[8,128]{1,0:T(8,128)} %broadcast_in_dim.40.token_ref), custom_call_target="tpu_custom_call" | custom-call | flops 1258291200 | bytes 5734400 | tf_op jit(solution)/shard_map/partial_products/pallas_call | solution.py:16
  37.7 4.6 %collective-permute-start.6 = (bf16[96,2560]{1,0:T(8,128)(2,1)}, bf16[96,2560]{1,0:T(8,128)(2,1)}, u32[]{:S(2)}, u32[]{:S(2)}) collective-permute-start(bf16[96,2560]{1,0:T(8,128)(2,1)} %get-tuple-element.206), channel_id=1, source_target_pairs={{0,1},{4,5},{8,9},{12,13},{16,17},{20,21},{24,25},{28,29}} | collective-permute-start | bytes 1474568 | tf_op jit(solution)/shard_map/ppermute | solution.py:44
  43.8 5.0 %partial_products.6 = (bf16[4,96,2560]{2,1,0:T(8,128)(2,1)}, bf16[96,2560]{1,0:T(8,128)(2,1)}, bf16[96,2560]{1,0:T(8,128)(2,1)}) custom-call(bf16[4,96,640]{2,1,0:T(8,128)(2,1)} %all-to-all-done.5.mine_ref.refs_15_, bf16[640,2560]{1,0:T(8,128)(2,1)S(1)} %multiply_convert_fusion.weights_ref.refs_14_, f32[8,128]{1,0:T(8,128)} %broadcast_in_dim.40.token_ref), custom_call_target="tpu_custom_call" | custom-call | flops 1258291200 | bytes 5734400 | tf_op jit(solution)/shard_map/partial_products/pallas_call | solution.py:16
  48.8 2.1 collective-permute-start.26
  50.9 1.4 collective-permute-start.27
  53.3 4.8 %next_payload.10 = (bf16[96,2560]{1,0:T(8,128)(2,1)}, bf16[96,2560]{1,0:T(8,128)(2,1)}, f32[8,128]{1,0:T(8,128)}) custom-call(s32[4]{0:T(128)} %pad_add_fusion.1.s, bf16[96,2560]{1,0:T(8,128)(2,1)} %collective-permute-done.6.right_ref, bf16[96,2560]{1,0:T(8,128)(2,1)} %collective-permute-done.7.left_ref, ...), custom_call_target="tpu_custom_call" | custom-call | flops 491520 | bytes 2949120 | tf_op jit(solution)/shard_map/next_payload/pallas_call | solution.py:16
  58.2 5.1 %collective-permute-start.8 = (bf16[96,2560]{1,0:T(8,128)(2,1)}, bf16[96,2560]{1,0:T(8,128)(2,1)}, u32[]{:S(2)}, u32[]{:S(2)}) collective-permute-start(bf16[96,2560]{1,0:T(8,128)(2,1)} %get-tuple-element.209), channel_id=1, source_target_pairs={{0,1},{1,2},{4,5},{5,6},{8,9},{9,10},{12,13},{13,14},{16,17},{17,1... | collective-permute-start | bytes 1474568 | tf_op jit(solution)/shard_map/ppermute | solution.py:44
  64.7 1.8 cut_heads.5
  66.5 5.3 %all-to-all-start.4 = ((bf16[4,96,640]{2,1,0:T(8,128)(2,1)}), bf16[4,96,640]{2,1,0:T(8,128)(2,1)}, u32[]{:S(2)}, u32[]{:S(2)}) async-start(bf16[4,96,640]{2,1,0:T(8,128)(2,1)} %cut_heads.5), calls=%async_computation.4 | async-start | bytes 983040 | tf_op jit(solution)/shard_map/all_to_all | solution.py:371
  71.9 4.9 %next_payload.15 = (bf16[96,2560]{1,0:T(8,128)(2,1)}, bf16[96,2560]{1,0:T(8,128)(2,1)}, f32[8,128]{1,0:T(8,128)}) custom-call(s32[4]{0:T(128)} %pad_add_fusion.1.s, bf16[96,2560]{1,0:T(8,128)(2,1)} %collective-permute-done.26.right_ref, bf16[96,2560]{1,0:T(8,128)(2,1)} %collective-permute-done.27.left_ref, ...), custom_call_target="tpu_custom_call" | custom-call | flops 491520 | bytes 2949120 | tf_op jit(solution)/shard_map/next_payload/pallas_call | solution.py:16
  76.8 4.7 %collective-permute-start.28 = (bf16[96,2560]{1,0:T(8,128)(2,1)}, bf16[96,2560]{1,0:T(8,128)(2,1)}, u32[]{:S(2)}, u32[]{:S(2)}) collective-permute-start(bf16[96,2560]{1,0:T(8,128)(2,1)} %get-tuple-element.225), channel_id=1, source_target_pairs={{0,1},{1,2},{4,5},{5,6},{8,9},{9,10},{12,13},{13,14},{16,17},{17,1... | collective-permute-start | bytes 1474568 | tf_op jit(solution)/shard_map/ppermute | solution.py:44
  81.5 1.4 collective-permute-start.29
  83.6 4.8 %next_payload.11 = (bf16[96,2560]{1,0:T(8,128)(2,1)}, bf16[96,2560]{1,0:T(8,128)(2,1)}, f32[8,128]{1,0:T(8,128)}) custom-call(s32[4]{0:T(128)} %pad_add_fusion.s, bf16[96,2560]{1,0:T(8,128)(2,1)} %collective-permute-done.8.right_ref, bf16[96,2560]{1,0:T(8,128)(2,1)} %collective-permute-done.9.left_ref, ...), custom_call_target="tpu_custom_call" | custom-call | flops 491520 | bytes 2949120 | tf_op jit(solution)/shard_map/next_payload/pallas_call | solution.py:16
  88.5 3.2 collective-permute-start.10
  93.1 4.9 %next_payload.16 = (bf16[96,2560]{1,0:T(8,128)(2,1)}, bf16[96,2560]{1,0:T(8,128)(2,1)}, f32[8,128]{1,0:T(8,128)}) custom-call(s32[4]{0:T(128)} %pad_add_fusion.s, bf16[96,2560]{1,0:T(8,128)(2,1)} %collective-permute-done.28.right_ref, bf16[96,2560]{1,0:T(8,128)(2,1)} %collective-permute-done.29.left_ref, ...), custom_call_target="tpu_custom_call" | custom-call | flops 491520 | bytes 2949120 | tf_op jit(solution)/shard_map/next_payload/pallas_call | solution.py:16
  98.0 10.0 %collective-permute-start.30 = (bf16[96,2560]{1,0:T(8,128)(2,1)}, bf16[96,2560]{1,0:T(8,128)(2,1)}, u32[]{:S(2)}, u32[]{:S(2)}) collective-permute-start(bf16[96,2560]{1,0:T(8,128)(2,1)} %get-tuple-element.227), channel_id=1, source_target_pairs={{0,1},{1,2},{2,3},{4,5},{5,6},{6,7},{8,9},{9,10},{10,11},{12,13},{... | collective-permute-start | bytes 1474568 | tf_op jit(solution)/shard_map/ppermute | solution.py:44
  109.3 1.8 cut_heads.7
  111.1 4.1 %all-to-all-start.6 = ((bf16[4,96,640]{2,1,0:T(8,128)(2,1)}), bf16[4,96,640]{2,1,0:T(8,128)(2,1)}, u32[]{:S(2)}, u32[]{:S(2)}) async-start(bf16[4,96,640]{2,1,0:T(8,128)(2,1)} %cut_heads.7), calls=%async_computation.6 | async-start | bytes 983040 | tf_op jit(solution)/shard_map/all_to_all | solution.py:371
  115.9 3.7 unit_gradient.4.refs_0_
  120.9 5.9 %collective-permute-start.12 = (bf16[96,2560]{1,0:T(8,128)(2,1)}, bf16[96,2560]{1,0:T(8,128)(2,1)}, u32[]{:S(2)}, u32[]{:S(2)}) collective-permute-start(bf16[96,2560]{1,0:T(8,128)(2,1)} %unit_gradient.4.refs_0_), channel_id=1, source_target_pairs={{0,1},{1,2},{2,3},{4,5},{5,6},{6,7},{8,9},{9,10},{10,11},{12,13},{... | collective-permute-start | bytes 1474568 | tf_op jit(solution)/shard_map/ppermute | solution.py:44
  126.9 3.7 unit_gradient.6.refs_7_
  131.9 5.3 %collective-permute-start.32 = (bf16[96,2560]{1,0:T(8,128)(2,1)}, bf16[96,2560]{1,0:T(8,128)(2,1)}, u32[]{:S(2)}, u32[]{:S(2)}) collective-permute-start(bf16[96,2560]{1,0:T(8,128)(2,1)} %unit_gradient.6.refs_7_), channel_id=1, source_target_pairs={{0,1},{1,2},{2,3},{4,5},{5,6},{6,7},{8,9},{9,10},{10,11},{12,13},{... | collective-permute-start | bytes 1474568 | tf_op jit(solution)/shard_map/ppermute | solution.py:44
  137.9 5.0 %partial_products.5 = (bf16[4,96,2560]{2,1,0:T(8,128)(2,1)}, bf16[96,2560]{1,0:T(8,128)(2,1)}, bf16[96,2560]{1,0:T(8,128)(2,1)}) custom-call(bf16[4,96,640]{2,1,0:T(8,128)(2,1)} %all-to-all-done.4.mine_ref.refs_14_, bf16[640,2560]{1,0:T(8,128)(2,1)S(1)} %multiply_convert_fusion.weights_ref.refs_14_, f32[8,128]{1,0:T(8,128)} %get-tuple-element.214.token_ref), custom_call_target="tpu_custom_call" | custom-call | flops 1258291200 | bytes 5734400 | tf_op jit(solution)/shard_map/partial_products/pallas_call | solution.py:16
  142.8 4.8 %next_payload.12 = (bf16[96,2560]{1,0:T(8,128)(2,1)}, bf16[96,2560]{1,0:T(8,128)(2,1)}, f32[8,128]{1,0:T(8,128)}) custom-call(s32[4]{0:T(128)} %pad_add_fusion.2.s, bf16[96,2560]{1,0:T(8,128)(2,1)} %collective-permute-done.12.right_ref.refs_1_, bf16[96,2560]{1,0:T(8,128)(2,1)} %collective-permute-done.13.left_ref.refs_4_, ...), custom_call_target="tpu_custom_call" | custom-call | flops 491520 | bytes 2949120 | tf_op jit(solution)/shard_map/next_payload/pallas_call | solution.py:16
  147.6 4.6 %collective-permute-start.14 = (bf16[96,2560]{1,0:T(8,128)(2,1)}, bf16[96,2560]{1,0:T(8,128)(2,1)}, u32[]{:S(2)}, u32[]{:S(2)}) collective-permute-start(bf16[96,2560]{1,0:T(8,128)(2,1)} %get-tuple-element.216), channel_id=1, source_target_pairs={{0,1},{1,2},{2,3},{4,5},{5,6},{6,7},{8,9},{9,10},{10,11},{12,13},{... | collective-permute-start | bytes 1474568 | tf_op jit(solution)/shard_map/ppermute | solution.py:44
  153.5 5.1 %partial_products.7 = (bf16[4,96,2560]{2,1,0:T(8,128)(2,1)}, bf16[96,2560]{1,0:T(8,128)(2,1)}, bf16[96,2560]{1,0:T(8,128)(2,1)}) custom-call(bf16[4,96,640]{2,1,0:T(8,128)(2,1)} %all-to-all-done.6.mine_ref.refs_15_, bf16[640,2560]{1,0:T(8,128)(2,1)S(1)} %multiply_convert_fusion.weights_ref.refs_14_, f32[8,128]{1,0:T(8,128)} %get-tuple-element.230.token_ref), custom_call_target="tpu_custom_call" | custom-call | flops 1258291200 | bytes 5734400 | tf_op jit(solution)/shard_map/partial_products/pallas_call | solution.py:16
  158.6 4.9 %next_payload.17 = (bf16[96,2560]{1,0:T(8,128)(2,1)}, bf16[96,2560]{1,0:T(8,128)(2,1)}, f32[8,128]{1,0:T(8,128)}) custom-call(s32[4]{0:T(128)} %pad_add_fusion.2.s, bf16[96,2560]{1,0:T(8,128)(2,1)} %collective-permute-done.32.right_ref.refs_8_, bf16[96,2560]{1,0:T(8,128)(2,1)} %collective-permute-done.33.left_ref.refs_11_, ...), custom_call_target="tpu_custom_call" | custom-call | flops 491520 | bytes 2949120 | tf_op jit(solution)/shard_map/next_payload/pallas_call | solution.py:16
  163.5 4.6 %collective-permute-start.34 = (bf16[96,2560]{1,0:T(8,128)(2,1)}, bf16[96,2560]{1,0:T(8,128)(2,1)S(1)}, u32[]{:S(2)}, u32[]{:S(2)}) collective-permute-start(bf16[96,2560]{1,0:T(8,128)(2,1)} %get-tuple-element.232), channel_id=1, source_target_pairs={{0,1},{1,2},{2,3},{4,5},{5,6},{6,7},{8,9},{9,10},{10,11},{12,13},{... | collective-permute-start | bytes 1474568 | tf_op jit(solution)/shard_map/ppermute | solution.py:44
  169.4 4.9 %next_payload.13 = (bf16[96,2560]{1,0:T(8,128)(2,1)}, bf16[96,2560]{1,0:T(8,128)(2,1)}, f32[8,128]{1,0:T(8,128)}) custom-call(s32[4]{0:T(128)} %pad_add_fusion.1.s, bf16[96,2560]{1,0:T(8,128)(2,1)} %collective-permute-done.14.right_ref.refs_2_, bf16[96,2560]{1,0:T(8,128)(2,1)} %collective-permute-done.15.left_ref.refs_5_, ...), custom_call_target="tpu_custom_call" | custom-call | flops 491520 | bytes 2949120 | tf_op jit(solution)/shard_map/next_payload/pallas_call | solution.py:16
  174.2 4.6 %collective-permute-start.16 = (bf16[96,2560]{1,0:T(8,128)(2,1)}, bf16[96,2560]{1,0:T(8,128)(2,1)S(1)}, u32[]{:S(2)}, u32[]{:S(2)}) collective-permute-start(bf16[96,2560]{1,0:T(8,128)(2,1)} %get-tuple-element.218), channel_id=1, source_target_pairs={{0,1},{1,2},{2,3},{4,5},{5,6},{6,7},{8,9},{9,10},{10,11},{12,13},{... | collective-permute-start | bytes 1474568 | tf_op jit(solution)/shard_map/ppermute | solution.py:44
  180.1 3.7 collective-permute-done.35.left_ref.refs_12_
  184.6 4.9 %next_payload.18 = (bf16[96,2560]{1,0:T(8,128)(2,1)}, bf16[96,2560]{1,0:T(8,128)(2,1)}, f32[8,128]{1,0:T(8,128)}) custom-call(s32[4]{0:T(128)} %pad_add_fusion.1.s, bf16[96,2560]{1,0:T(8,128)(2,1)} %copy-done.10, bf16[96,2560]{1,0:T(8,128)(2,1)} %copy-done.11, bf16[4,96,2560]{2,1,0:T(8,128)(2,1)} %get-tuple-element.231.of_right.of_left.own_ref, ...), custom_call_target="tpu_custom_call" | custom-call | flops 491520 | bytes 2949120 | tf_op jit(solution)/shard_map/next_payload/pallas_call | solution.py:16
  189.5 1.7 collective-permute-start.36
  192.5 1.9 collective-permute-done.17.left_ref.refs_6_
  195.3 4.9 %next_payload.14 = (bf16[96,2560]{1,0:T(8,128)(2,1)}, bf16[96,2560]{1,0:T(8,128)(2,1)}, f32[8,128]{1,0:T(8,128)}) custom-call(s32[4]{0:T(128)} %pad_add_fusion.s, bf16[96,2560]{1,0:T(8,128)(2,1)} %copy-done.12, bf16[96,2560]{1,0:T(8,128)(2,1)} %copy-done.13, bf16[4,96,2560]{2,1,0:T(8,128)(2,1)} %get-tuple-element.215.of_right.of_left.own_ref, ...), custom_call_target="tpu_custom_call" | custom-call | flops 491520 | bytes 2949120 | tf_op jit(solution)/shard_map/next_payload/pallas_call | solution.py:16
  200.1 3.5 collective-permute-start.18
  204.9 2.5 collective-permute-done.37.left_ref.refs_13_
  208.2 4.9 %next_payload.19 = (bf16[96,2560]{1,0:T(8,128)(2,1)}, bf16[96,2560]{1,0:T(8,128)(2,1)}, f32[8,128]{1,0:T(8,128)}) custom-call(s32[4]{0:T(128)} %pad_add_fusion.s, bf16[96,2560]{1,0:T(8,128)(2,1)} %copy-done.14, bf16[96,2560]{1,0:T(8,128)(2,1)} %copy-done.15, bf16[4,96,2560]{2,1,0:T(8,128)(2,1)} %get-tuple-element.231.of_right.of_left.own_ref, ...), custom_call_target="tpu_custom_call" | custom-call | flops 491520 | bytes 2949120 | tf_op jit(solution)/shard_map/next_payload/pallas_call | solution.py:16
  213.1 2.9 collective-permute-start.38
  217.3 11.7 %weight_step.2 = (f32[640,2560]{1,0:T(8,128)}, f32[8,128]{1,0:T(8,128)}) custom-call(s32[4]{0:T(128)S(1)} %and_select_fusion.s, bf16[96,2560]{1,0:T(8,128)(2,1)} %unit_gradient.4.refs_0_, bf16[96,2560]{1,0:T(8,128)(2,1)} %collective-permute-done.12.right_ref.refs_1_, bf16[96,2560]{1,0:T(8,128)(2,1)} %collective-permute-done.14.right_ref.refs_2_, ...), custom_call_target="tpu_custom_call" | custom-call | flops 2516582400 | bytes 26542080 | tf_op jit(solution)/shard_map/weight_step/pallas_call | solution.py:16
  230.5 3.0 unit_gradient.5.refs_0_
  234.9 5.2 %collective-permute-start.20 = (bf16[96,2560]{1,0:T(8,128)(2,1)S(1)}, bf16[96,2560]{1,0:T(8,128)(2,1)S(1)}, u32[]{:S(2)}, u32[]{:S(2)}) collective-permute-start(bf16[96,2560]{1,0:T(8,128)(2,1)S(1)} %unit_gradient.5.refs_0_), channel_id=1, source_target_pairs={{0,1},{1,2},{2,3},{4,5},{5,6},{6,7},{8,9},{9,10},{10,11},{12,13},{... | collective-permute-start | bytes 1474568 | tf_op jit(solution)/shard_map/ppermute | solution.py:44
  240.9 3.0 unit_gradient.7.refs_7_
  245.2 4.6 %collective-permute-start.40 = (bf16[96,2560]{1,0:T(8,128)(2,1)S(1)}, bf16[96,2560]{1,0:T(8,128)(2,1)S(1)}, u32[]{:S(2)}, u32[]{:S(2)}) collective-permute-start(bf16[96,2560]{1,0:T(8,128)(2,1)S(1)} %unit_gradient.7.refs_7_), channel_id=1, source_target_pairs={{0,1},{1,2},{2,3},{4,5},{5,6},{6,7},{8,9},{9,10},{10,11},{12,13},{... | collective-permute-start | bytes 1474568 | tf_op jit(solution)/shard_map/ppermute | solution.py:44
  251.6 1.5 collective-permute-start.21
  253.0 7.8 %collective-permute-done.43.refs_11_ = bf16[96,2560]{1,0:T(8,128)(2,1)S(1)} collective-permute-done((bf16[96,2560]{1,0:T(8,128)(2,1)S(1)}, bf16[96,2560]{1,0:T(8,128)(2,1)S(1)}, u32[]{:S(2)}, u32[]{:S(2)}) %collective-permute-start.43) | collective-permute-done | bytes 491552 | tf_op jit(solution)/shard_map/ppermute | solution.py:44
  262.1 1.5 collective-permute-start.41
  263.6 7.8 %collective-permute-done.24.refs_5_ = bf16[96,2560]{1,0:T(8,128)(2,1)} collective-permute-done((bf16[96,2560]{1,0:T(8,128)(2,1)S(1)}, bf16[96,2560]{1,0:T(8,128)(2,1)}, u32[]{:S(2)}, u32[]{:S(2)}) %collective-permute-start.24) | collective-permute-done | bytes 491552 | tf_op jit(solution)/shard_map/ppermute | solution.py:44
  274.2 7.8 %collective-permute-done.44.refs_12_ = bf16[96,2560]{1,0:T(8,128)(2,1)} collective-permute-done((bf16[96,2560]{1,0:T(8,128)(2,1)S(1)}, bf16[96,2560]{1,0:T(8,128)(2,1)}, u32[]{:S(2)}, u32[]{:S(2)}) %collective-permute-start.44) | collective-permute-done | bytes 491552 | tf_op jit(solution)/shard_map/ppermute | solution.py:44
  286.0 8.1 %grad_rows.7 = bf16[4,192,640]{2,1,0:T(8,128)(2,1)S(1)} custom-call(s32[4]{0:T(128)} %copy-done.21, bf16[96,2560]{1,0:T(8,128)(2,1)} %unit_gradient.4.refs_0_, bf16[96,2560]{1,0:T(8,128)(2,1)} %collective-permute-done.12.right_ref.refs_1_, bf16[96,2560]{1,0:T(8,128)(2,1)} %collective-permute-done.14.right_ref.refs_2_, bf16[96,2560]{1,0:T(8,128)(2,1)} %copy-done.12, ...), custom_call_target="tpu_custom_call" | custom-call | flops 2516582400 | bytes 10158080 | tf_op jit(solution)/shard_map/grad_rows/pallas_call | solution.py:16
  294.2 13.9 %weight_step.3 = (f32[640,2560]{1,0:T(8,128)}, bf16[640,2560]{1,0:T(8,128)(2,1)}) custom-call(s32[4]{0:T(128)} %copy-done.21, bf16[96,2560]{1,0:T(8,128)(2,1)S(1)} %copy-done.1, bf16[96,2560]{1,0:T(8,128)(2,1)S(1)} %copy-done.7, bf16[96,2560]{1,0:T(8,128)(2,1)} %collective-permute-done.21.refs_2_, bf16[96,2560]{1,0:T(8,128)(2,1)} %collective-permute-done.22.refs_3_, ...), custom_call_target="tpu_custom_call" | custom-call | flops 2516582400 | bytes 26542080 | tf_op jit(solution)/shard_map/weight_step/pallas_call | solution.py:16
  308.1 65.8 %conditional.1 = (bf16[640,2560]{1,0:T(8,128)(2,1)}, bf16[1,384,2560]{2,1,0:T(8,128)(2,1)S(1)}) conditional(s32[]{:T(128)} %clamp.3, (bf16[640,2560]{1,0:T(8,128)(2,1)}, s32[4]{0:T(128)}, bf16[96,2560]{1,0:T(8,128)(2,1)S(1)}, bf16[96,2560]{1,0:T(8,128)(2,1)S(1)}, bf16[96,2560]{1,0:T(8,128)(2,1)}, ...), branch_computations={%region_1.2_spmd, %region_2.3_spmd, %region_3.4_spmd} | conditional | flops 2520514560 | bytes 35061816 | solution.py:500
  308.1 8.6 %grad_rows.4 = bf16[4,192,640]{2,1,0:T(8,128)(2,1)} custom-call(s32[4]{0:T(128)} %get-tuple-element.111.s, bf16[96,2560]{1,0:T(8,128)(2,1)S(1)} %get-tuple-element.112.refs_0_, bf16[96,2560]{1,0:T(8,128)(2,1)S(1)} %get-tuple-element.113.refs_1_, bf16[96,2560]{1,0:T(8,128)(2,1)} %get-tuple-element.114.refs_2_, bf16[96,2560]{1,0:T(8,128)(2,1)} %get-tuple-element.115.refs_3_, ...), custom_call_target="tpu_custom_call" | custom-call | flops 2516582400 | bytes 10158080 | tf_op jit(solution)/shard_map/cond/branch_0_fun/grad_rows/pallas_call | solution.py:16
  318.2 53.3 %all_to_all.32.blocks_ref = bf16[4,384,640]{2,1,0:T(8,128)(2,1)} all-to-all(bf16[4,384,640]{2,1,0:T(8,128)(2,1)S(1)} %pad_maximum_fusion), channel_id=1, replica_groups=mesh['rep'=8,'fsdp'=4] {'fsdp'}, dimensions={0} | all-to-all | bytes 3932160 | tf_op jit(solution)/shard_map/cond/branch_0_fun/all_to_all | solution.py:371
  371.5 2.4 joined_rows.3
  373.9 7.9 %widened.1 = f32[640,2560]{1,0:T(8,128)} custom-call(bf16[640,2560]{1,0:T(8,128)(2,1)} %get-tuple-element.242.value_ref), custom_call_target="tpu_custom_call" | custom-call | bytes 9830400 | tf_op jit(solution)/shard_map/widened/pallas_call | solution.py:16
  (119 shorter events, 38.3 us)
Async XLA Ops:
  0.6 17.2 %copy-start.23 = (s32[8]{0:T(128)S(1)}, s32[8]{0:T(128)}, u32[]{:S(2)}) copy-start(s32[8]{0:T(128)} %param.20) | copy-start | bytes 100
  2.4 20.1 %all-to-all-start.3 = ((bf16[4,96,640]{2,1,0:T(8,128)(2,1)}), bf16[4,96,640]{2,1,0:T(8,128)(2,1)S(1)}, u32[]{:S(2)}, u32[]{:S(2)}) async-start(bf16[4,96,640]{2,1,0:T(8,128)(2,1)} %cut_heads.4), calls=%async_computation.3 | async-start | bytes 983040 | tf_op jit(solution)/shard_map/all_to_all | solution.py:371
  9.4 20.9 %collective-permute-start.5 = (f32[1]{0:T(128)}, f32[1]{0:T(128)}, u32[]{:S(2)}, u32[]{:S(2)}) collective-permute-start(f32[1]{0:T(128)} %mul.12), channel_id=1, source_target_pairs={{0,4},{4,8},{8,12},{12,16},{16,20},{20,24},{24,28},{28,0},{1,5},{5... | collective-permute-start | bytes 20 | tf_op jit(solution)/shard_map/ppermute | solution.py:403
  10.4 19.9 %collective-permute-start.4 = (f32[1]{0:T(128)}, f32[1]{0:T(128)}, u32[]{:S(2)}, u32[]{:S(2)}) collective-permute-start(f32[1]{0:T(128)} %mul.12), channel_id=1, source_target_pairs={{0,8},{4,12},{8,16},{12,20},{16,24},{20,28},{24,0},{28,4},{1,9},{5... | collective-permute-start | bytes 20 | tf_op jit(solution)/shard_map/ppermute | solution.py:403
  13.2 18.3 %collective-permute-start.3 = (f32[1]{0:T(128)}, f32[1]{0:T(128)}, u32[]{:S(2)}, u32[]{:S(2)}) collective-permute-start(f32[1]{0:T(128)} %mul.12), channel_id=1, source_target_pairs={{0,16},{4,20},{8,24},{12,28},{16,0},{20,4},{24,8},{28,12},{1,17},{... | collective-permute-start | bytes 20 | tf_op jit(solution)/shard_map/ppermute | solution.py:403
  22.5 4.1 %copy-start.17 = (bf16[4,96,640]{2,1,0:T(8,128)(2,1)}, bf16[4,96,640]{2,1,0:T(8,128)(2,1)S(1)}, u32[]{:S(2)}) copy-start(bf16[4,96,640]{2,1,0:T(8,128)(2,1)S(1)} %all-to-all-done.3.mine_ref.refs_14_) | copy-start | bytes 1474564
  22.5 21.3 %all-to-all-start.5 = ((bf16[4,96,640]{2,1,0:T(8,128)(2,1)}), bf16[4,96,640]{2,1,0:T(8,128)(2,1)}, u32[]{:S(2)}, u32[]{:S(2)}) async-start(bf16[4,96,640]{2,1,0:T(8,128)(2,1)} %cut_heads.6), calls=%async_computation.5 | async-start | bytes 983040 | tf_op jit(solution)/shard_map/all_to_all | solution.py:371
  37.7 15.6 %collective-permute-start.6 = (bf16[96,2560]{1,0:T(8,128)(2,1)}, bf16[96,2560]{1,0:T(8,128)(2,1)}, u32[]{:S(2)}, u32[]{:S(2)}) collective-permute-start(bf16[96,2560]{1,0:T(8,128)(2,1)} %get-tuple-element.206), channel_id=1, source_target_pairs={{0,1},{4,5},{8,9},{12,13},{16,17},{20,21},{24,25},{28,29}} | collective-permute-start | bytes 1474568 | tf_op jit(solution)/shard_map/ppermute | solution.py:44
  42.4 10.9 %collective-permute-start.7 = (bf16[96,2560]{1,0:T(8,128)(2,1)}, bf16[96,2560]{1,0:T(8,128)(2,1)}, u32[]{:S(2)}, u32[]{:S(2)}) collective-permute-start(bf16[96,2560]{1,0:T(8,128)(2,1)} %get-tuple-element.207), channel_id=1, source_target_pairs={{3,2},{7,6},{11,10},{15,14},{19,18},{23,22},{27,26},{31,30}} | collective-permute-start | bytes 1474568 | tf_op jit(solution)/shard_map/ppermute | solution.py:44
  48.8 23.1 %collective-permute-start.26 = (bf16[96,2560]{1,0:T(8,128)(2,1)}, bf16[96,2560]{1,0:T(8,128)(2,1)}, u32[]{:S(2)}, u32[]{:S(2)}) collective-permute-start(bf16[96,2560]{1,0:T(8,128)(2,1)} %get-tuple-element.222), channel_id=1, source_target_pairs={{0,1},{4,5},{8,9},{12,13},{16,17},{20,21},{24,25},{28,29}} | collective-permute-start | bytes 1474568 | tf_op jit(solution)/shard_map/ppermute | solution.py:44
  50.9 21.0 %collective-permute-start.27 = (bf16[96,2560]{1,0:T(8,128)(2,1)}, bf16[96,2560]{1,0:T(8,128)(2,1)}, u32[]{:S(2)}, u32[]{:S(2)}) collective-permute-start(bf16[96,2560]{1,0:T(8,128)(2,1)} %get-tuple-element.223), channel_id=1, source_target_pairs={{3,2},{7,6},{11,10},{15,14},{19,18},{23,22},{27,26},{31,30}} | collective-permute-start | bytes 1474568 | tf_op jit(solution)/shard_map/ppermute | solution.py:44
  58.2 25.5 %collective-permute-start.8 = (bf16[96,2560]{1,0:T(8,128)(2,1)}, bf16[96,2560]{1,0:T(8,128)(2,1)}, u32[]{:S(2)}, u32[]{:S(2)}) collective-permute-start(bf16[96,2560]{1,0:T(8,128)(2,1)} %get-tuple-element.209), channel_id=1, source_target_pairs={{0,1},{1,2},{4,5},{5,6},{8,9},{9,10},{12,13},{13,14},{16,17},{17,1... | collective-permute-start | bytes 1474568 | tf_op jit(solution)/shard_map/ppermute | solution.py:44
  63.3 20.3 %collective-permute-start.9 = (bf16[96,2560]{1,0:T(8,128)(2,1)}, bf16[96,2560]{1,0:T(8,128)(2,1)}, u32[]{:S(2)}, u32[]{:S(2)}) collective-permute-start(bf16[96,2560]{1,0:T(8,128)(2,1)} %get-tuple-element.210), channel_id=1, source_target_pairs={{2,1},{3,2},{6,5},{7,6},{10,9},{11,10},{14,13},{15,14},{18,17},{19... | collective-permute-start | bytes 1474568 | tf_op jit(solution)/shard_map/ppermute | solution.py:44
  66.5 44.6 %all-to-all-start.4 = ((bf16[4,96,640]{2,1,0:T(8,128)(2,1)}), bf16[4,96,640]{2,1,0:T(8,128)(2,1)}, u32[]{:S(2)}, u32[]{:S(2)}) async-start(bf16[4,96,640]{2,1,0:T(8,128)(2,1)} %cut_heads.5), calls=%async_computation.4 | async-start | bytes 983040 | tf_op jit(solution)/shard_map/all_to_all | solution.py:371
  76.8 16.3 %collective-permute-start.28 = (bf16[96,2560]{1,0:T(8,128)(2,1)}, bf16[96,2560]{1,0:T(8,128)(2,1)}, u32[]{:S(2)}, u32[]{:S(2)}) collective-permute-start(bf16[96,2560]{1,0:T(8,128)(2,1)} %get-tuple-element.225), channel_id=1, source_target_pairs={{0,1},{1,2},{4,5},{5,6},{8,9},{9,10},{12,13},{13,14},{16,17},{17,1... | collective-permute-start | bytes 1474568 | tf_op jit(solution)/shard_map/ppermute | solution.py:44
  81.5 11.6 %collective-permute-start.29 = (bf16[96,2560]{1,0:T(8,128)(2,1)}, bf16[96,2560]{1,0:T(8,128)(2,1)}, u32[]{:S(2)}, u32[]{:S(2)}) collective-permute-start(bf16[96,2560]{1,0:T(8,128)(2,1)} %get-tuple-element.226), channel_id=1, source_target_pairs={{2,1},{3,2},{6,5},{7,6},{10,9},{11,10},{14,13},{15,14},{18,17},{19... | collective-permute-start | bytes 1474568 | tf_op jit(solution)/shard_map/ppermute | solution.py:44
  88.5 27.4 %collective-permute-start.10 = (bf16[96,2560]{1,0:T(8,128)(2,1)}, bf16[96,2560]{1,0:T(8,128)(2,1)}, u32[]{:S(2)}, u32[]{:S(2)}) collective-permute-start(bf16[96,2560]{1,0:T(8,128)(2,1)} %get-tuple-element.211), channel_id=1, source_target_pairs={{0,1},{1,2},{2,3},{4,5},{5,6},{6,7},{8,9},{9,10},{10,11},{12,13},{... | collective-permute-start | bytes 1474568 | tf_op jit(solution)/shard_map/ppermute | solution.py:44
  91.7 23.6 %copy-start.22 = (f32[2560]{0:T(1024)S(1)}, f32[2560]{0:T(1024)}, u32[]{:S(2)}) copy-start(f32[2560]{0:T(1024)} %param.19) | copy-start | bytes 30724
  91.7 24.2 %collective-permute-start.11 = (bf16[96,2560]{1,0:T(8,128)(2,1)}, bf16[96,2560]{1,0:T(8,128)(2,1)}, u32[]{:S(2)}, u32[]{:S(2)}) collective-permute-start(bf16[96,2560]{1,0:T(8,128)(2,1)} %get-tuple-element.212), channel_id=1, source_target_pairs={{1,0},{2,1},{3,2},{5,4},{6,5},{7,6},{9,8},{10,9},{11,10},{13,12},{... | collective-permute-start | bytes 1474568 | tf_op jit(solution)/shard_map/ppermute | solution.py:44
  98.0 28.9 %collective-permute-start.30 = (bf16[96,2560]{1,0:T(8,128)(2,1)}, bf16[96,2560]{1,0:T(8,128)(2,1)}, u32[]{:S(2)}, u32[]{:S(2)}) collective-permute-start(bf16[96,2560]{1,0:T(8,128)(2,1)} %get-tuple-element.227), channel_id=1, source_target_pairs={{0,1},{1,2},{2,3},{4,5},{5,6},{6,7},{8,9},{9,10},{10,11},{12,13},{... | collective-permute-start | bytes 1474568 | tf_op jit(solution)/shard_map/ppermute | solution.py:44
  108.0 18.9 %collective-permute-start.31 = (bf16[96,2560]{1,0:T(8,128)(2,1)}, bf16[96,2560]{1,0:T(8,128)(2,1)}, u32[]{:S(2)}, u32[]{:S(2)}) collective-permute-start(bf16[96,2560]{1,0:T(8,128)(2,1)} %get-tuple-element.228), channel_id=1, source_target_pairs={{1,0},{2,1},{3,2},{5,4},{6,5},{7,6},{9,8},{10,9},{11,10},{13,12},{... | collective-permute-start | bytes 1474568 | tf_op jit(solution)/shard_map/ppermute | solution.py:44
  111.1 42.4 %all-to-all-start.6 = ((bf16[4,96,640]{2,1,0:T(8,128)(2,1)}), bf16[4,96,640]{2,1,0:T(8,128)(2,1)}, u32[]{:S(2)}, u32[]{:S(2)}) async-start(bf16[4,96,640]{2,1,0:T(8,128)(2,1)} %cut_heads.7), calls=%async_computation.6 | async-start | bytes 983040 | tf_op jit(solution)/shard_map/all_to_all | solution.py:371
  119.6 23.2 %collective-permute-start.13 = (bf16[96,2560]{1,0:T(8,128)(2,1)}, bf16[96,2560]{1,0:T(8,128)(2,1)}, u32[]{:S(2)}, u32[]{:S(2)}) collective-permute-start(bf16[96,2560]{1,0:T(8,128)(2,1)} %unit_gradient.4.refs_0_), channel_id=1, source_target_pairs={{1,0},{2,1},{3,2},{5,4},{6,5},{7,6},{9,8},{10,9},{11,10},{13,12},{... | collective-permute-start | bytes 1474568 | tf_op jit(solution)/shard_map/ppermute | solution.py:44
  120.9 21.9 %collective-permute-start.12 = (bf16[96,2560]{1,0:T(8,128)(2,1)}, bf16[96,2560]{1,0:T(8,128)(2,1)}, u32[]{:S(2)}, u32[]{:S(2)}) collective-permute-start(bf16[96,2560]{1,0:T(8,128)(2,1)} %unit_gradient.4.refs_0_), channel_id=1, source_target_pairs={{0,1},{1,2},{2,3},{4,5},{5,6},{6,7},{8,9},{9,10},{10,11},{12,13},{... | collective-permute-start | bytes 1474568 | tf_op jit(solution)/shard_map/ppermute | solution.py:44
  130.6 28.0 %collective-permute-start.33 = (bf16[96,2560]{1,0:T(8,128)(2,1)}, bf16[96,2560]{1,0:T(8,128)(2,1)}, u32[]{:S(2)}, u32[]{:S(2)}) collective-permute-start(bf16[96,2560]{1,0:T(8,128)(2,1)} %unit_gradient.6.refs_7_), channel_id=1, source_target_pairs={{1,0},{2,1},{3,2},{5,4},{6,5},{7,6},{9,8},{10,9},{11,10},{13,12},{... | collective-permute-start | bytes 1474568 | tf_op jit(solution)/shard_map/ppermute | solution.py:44
  131.9 26.7 %collective-permute-start.32 = (bf16[96,2560]{1,0:T(8,128)(2,1)}, bf16[96,2560]{1,0:T(8,128)(2,1)}, u32[]{:S(2)}, u32[]{:S(2)}) collective-permute-start(bf16[96,2560]{1,0:T(8,128)(2,1)} %unit_gradient.6.refs_7_), channel_id=1, source_target_pairs={{0,1},{1,2},{2,3},{4,5},{5,6},{6,7},{8,9},{9,10},{10,11},{12,13},{... | collective-permute-start | bytes 1474568 | tf_op jit(solution)/shard_map/ppermute | solution.py:44
  147.6 21.7 %collective-permute-start.14 = (bf16[96,2560]{1,0:T(8,128)(2,1)}, bf16[96,2560]{1,0:T(8,128)(2,1)}, u32[]{:S(2)}, u32[]{:S(2)}) collective-permute-start(bf16[96,2560]{1,0:T(8,128)(2,1)} %get-tuple-element.216), channel_id=1, source_target_pairs={{0,1},{1,2},{2,3},{4,5},{5,6},{6,7},{8,9},{9,10},{10,11},{12,13},{... | collective-permute-start | bytes 1474568 | tf_op jit(solution)/shard_map/ppermute | solution.py:44
  152.2 17.1 %collective-permute-start.15 = (bf16[96,2560]{1,0:T(8,128)(2,1)}, bf16[96,2560]{1,0:T(8,128)(2,1)}, u32[]{:S(2)}, u32[]{:S(2)}) collective-permute-start(bf16[96,2560]{1,0:T(8,128)(2,1)} %get-tuple-element.217), channel_id=1, source_target_pairs={{1,0},{2,1},{3,2},{5,4},{6,5},{7,6},{9,8},{10,9},{11,10},{13,12},{... | collective-permute-start | bytes 1474568 | tf_op jit(solution)/shard_map/ppermute | solution.py:44
  163.5 16.6 %collective-permute-start.34 = (bf16[96,2560]{1,0:T(8,128)(2,1)}, bf16[96,2560]{1,0:T(8,128)(2,1)S(1)}, u32[]{:S(2)}, u32[]{:S(2)}) collective-permute-start(bf16[96,2560]{1,0:T(8,128)(2,1)} %get-tuple-element.232), channel_id=1, source_target_pairs={{0,1},{1,2},{2,3},{4,5},{5,6},{6,7},{8,9},{9,10},{10,11},{12,13},{... | collective-permute-start | bytes 1474568 | tf_op jit(solution)/shard_map/ppermute | solution.py:44
  168.0 15.7 %collective-permute-start.35 = (bf16[96,2560]{1,0:T(8,128)(2,1)}, bf16[96,2560]{1,0:T(8,128)(2,1)S(1)}, u32[]{:S(2)}, u32[]{:S(2)}) collective-permute-start(bf16[96,2560]{1,0:T(8,128)(2,1)} %get-tuple-element.233), channel_id=1, source_target_pairs={{1,0},{2,1},{3,2},{5,4},{6,5},{7,6},{9,8},{10,9},{11,10},{13,12},{... | collective-permute-start | bytes 1474568 | tf_op jit(solution)/shard_map/ppermute | solution.py:44
  174.2 18.3 %collective-permute-start.16 = (bf16[96,2560]{1,0:T(8,128)(2,1)}, bf16[96,2560]{1,0:T(8,128)(2,1)S(1)}, u32[]{:S(2)}, u32[]{:S(2)}) collective-permute-start(bf16[96,2560]{1,0:T(8,128)(2,1)} %get-tuple-element.218), channel_id=1, source_target_pairs={{0,1},{1,2},{2,3},{4,5},{5,6},{6,7},{8,9},{9,10},{10,11},{12,13},{... | collective-permute-start | bytes 1474568 | tf_op jit(solution)/shard_map/ppermute | solution.py:44
  178.8 15.7 %collective-permute-start.17 = (bf16[96,2560]{1,0:T(8,128)(2,1)}, bf16[96,2560]{1,0:T(8,128)(2,1)S(1)}, u32[]{:S(2)}, u32[]{:S(2)}) collective-permute-start(bf16[96,2560]{1,0:T(8,128)(2,1)} %get-tuple-element.219), channel_id=1, source_target_pairs={{1,0},{2,1},{3,2},{5,4},{6,5},{7,6},{9,8},{10,9},{11,10},{13,12},{... | collective-permute-start | bytes 1474568 | tf_op jit(solution)/shard_map/ppermute | solution.py:44
  180.1 3.7 copy-start.10
  189.5 15.4 %collective-permute-start.36 = (bf16[96,2560]{1,0:T(8,128)(2,1)}, bf16[96,2560]{1,0:T(8,128)(2,1)S(1)}, u32[]{:S(2)}, u32[]{:S(2)}) collective-permute-start(bf16[96,2560]{1,0:T(8,128)(2,1)} %get-tuple-element.234), channel_id=1, source_target_pairs={{0,1},{1,2},{2,3},{4,5},{5,6},{6,7},{8,9},{9,10},{10,11},{12,13},{... | collective-permute-start | bytes 1474568 | tf_op jit(solution)/shard_map/ppermute | solution.py:44
  191.2 16.2 %collective-permute-start.37 = (bf16[96,2560]{1,0:T(8,128)(2,1)}, bf16[96,2560]{1,0:T(8,128)(2,1)S(1)}, u32[]{:S(2)}, u32[]{:S(2)}) collective-permute-start(bf16[96,2560]{1,0:T(8,128)(2,1)} %get-tuple-element.235), channel_id=1, source_target_pairs={{1,0},{2,1},{3,2},{5,4},{6,5},{7,6},{9,8},{10,9},{11,10},{13,12},{... | collective-permute-start | bytes 1474568 | tf_op jit(solution)/shard_map/ppermute | solution.py:44
  200.1 28.8 %collective-permute-start.18 = (bf16[96,2560]{1,0:T(8,128)(2,1)}, bf16[96,2560]{1,0:T(8,128)(2,1)S(1)}, u32[]{:S(2)}, u32[]{:S(2)}) collective-permute-start(bf16[96,2560]{1,0:T(8,128)(2,1)} %get-tuple-element.220), channel_id=1, source_target_pairs={{0,1},{1,2},{2,3},{4,5},{5,6},{6,7},{8,9},{9,10},{10,11},{12,13},{... | collective-permute-start | bytes 1474568 | tf_op jit(solution)/shard_map/ppermute | solution.py:44
  203.6 25.4 %collective-permute-start.19 = (bf16[96,2560]{1,0:T(8,128)(2,1)}, bf16[96,2560]{1,0:T(8,128)(2,1)S(1)}, u32[]{:S(2)}, u32[]{:S(2)}) collective-permute-start(bf16[96,2560]{1,0:T(8,128)(2,1)} %get-tuple-element.221), channel_id=1, source_target_pairs={{1,0},{2,1},{3,2},{5,4},{6,5},{7,6},{9,8},{10,9},{11,10},{13,12},{... | collective-permute-start | bytes 1474568 | tf_op jit(solution)/shard_map/ppermute | solution.py:44
  213.1 27.0 %collective-permute-start.38 = (bf16[96,2560]{1,0:T(8,128)(2,1)}, bf16[96,2560]{1,0:T(8,128)(2,1)S(1)}, u32[]{:S(2)}, u32[]{:S(2)}) collective-permute-start(bf16[96,2560]{1,0:T(8,128)(2,1)} %get-tuple-element.236), channel_id=1, source_target_pairs={{0,1},{1,2},{2,3},{4,5},{5,6},{6,7},{8,9},{9,10},{10,11},{12,13},{... | collective-permute-start | bytes 1474568 | tf_op jit(solution)/shard_map/ppermute | solution.py:44
  215.9 24.2 %collective-permute-start.39 = (bf16[96,2560]{1,0:T(8,128)(2,1)}, bf16[96,2560]{1,0:T(8,128)(2,1)}, u32[]{:S(2)}, u32[]{:S(2)}) collective-permute-start(bf16[96,2560]{1,0:T(8,128)(2,1)} %get-tuple-element.237), channel_id=1, source_target_pairs={{1,0},{2,1},{3,2},{5,4},{6,5},{7,6},{9,8},{10,9},{11,10},{13,12},{... | collective-permute-start | bytes 1474568 | tf_op jit(solution)/shard_map/ppermute | solution.py:44
  217.3 11.7 %copy-start.21 = (s32[4]{0:T(128)}, s32[4]{0:T(128)S(1)}, u32[]{:S(2)}) copy-start(s32[4]{0:T(128)S(1)} %and_select_fusion.s) | copy-start | bytes 52
  233.5 10.3 %copy-start = (bf16[96,2560]{1,0:T(8,128)(2,1)}, bf16[96,2560]{1,0:T(8,128)(2,1)S(1)}, u32[]{:S(2)}) copy-start(bf16[96,2560]{1,0:T(8,128)(2,1)S(1)} %unit_gradient.5.refs_0_) | copy-start | bytes 1474564
  233.6 16.7 %collective-permute-start.23 = (bf16[96,2560]{1,0:T(8,128)(2,1)S(1)}, bf16[96,2560]{1,0:T(8,128)(2,1)S(1)}, u32[]{:S(2)}, u32[]{:S(2)}) collective-permute-start(bf16[96,2560]{1,0:T(8,128)(2,1)S(1)} %unit_gradient.5.refs_0_), channel_id=1, source_target_pairs={{1,0},{2,1},{3,2},{5,4},{6,5},{7,6},{9,8},{10,9},{11,10},{13,12},{... | collective-permute-start | bytes 1474568 | tf_op jit(solution)/shard_map/ppermute | solution.py:44
  234.9 16.7 %collective-permute-start.20 = (bf16[96,2560]{1,0:T(8,128)(2,1)S(1)}, bf16[96,2560]{1,0:T(8,128)(2,1)S(1)}, u32[]{:S(2)}, u32[]{:S(2)}) collective-permute-start(bf16[96,2560]{1,0:T(8,128)(2,1)S(1)} %unit_gradient.5.refs_0_), channel_id=1, source_target_pairs={{0,1},{1,2},{2,3},{4,5},{5,6},{6,7},{8,9},{9,10},{10,11},{12,13},{... | collective-permute-start | bytes 1474568 | tf_op jit(solution)/shard_map/ppermute | solution.py:44
  243.9 7.7 %copy-start.2 = (bf16[96,2560]{1,0:T(8,128)(2,1)}, bf16[96,2560]{1,0:T(8,128)(2,1)S(1)}, u32[]{:S(2)}) copy-start(bf16[96,2560]{1,0:T(8,128)(2,1)S(1)} %unit_gradient.7.refs_7_) | copy-start | bytes 1474564
  243.9 16.9 %collective-permute-start.43 = (bf16[96,2560]{1,0:T(8,128)(2,1)S(1)}, bf16[96,2560]{1,0:T(8,128)(2,1)S(1)}, u32[]{:S(2)}, u32[]{:S(2)}) collective-permute-start(bf16[96,2560]{1,0:T(8,128)(2,1)S(1)} %unit_gradient.7.refs_7_), channel_id=1, source_target_pairs={{1,0},{2,1},{3,2},{5,4},{6,5},{7,6},{9,8},{10,9},{11,10},{13,12},{... | collective-permute-start | bytes 1474568 | tf_op jit(solution)/shard_map/ppermute | solution.py:44
  245.2 16.9 %collective-permute-start.40 = (bf16[96,2560]{1,0:T(8,128)(2,1)S(1)}, bf16[96,2560]{1,0:T(8,128)(2,1)S(1)}, u32[]{:S(2)}, u32[]{:S(2)}) collective-permute-start(bf16[96,2560]{1,0:T(8,128)(2,1)S(1)} %unit_gradient.7.refs_7_), channel_id=1, source_target_pairs={{0,1},{1,2},{2,3},{4,5},{5,6},{6,7},{8,9},{9,10},{10,11},{12,13},{... | collective-permute-start | bytes 1474568 | tf_op jit(solution)/shard_map/ppermute | solution.py:44
  250.3 11.8 %copy-start.4 = (bf16[96,2560]{1,0:T(8,128)(2,1)}, bf16[96,2560]{1,0:T(8,128)(2,1)S(1)}, u32[]{:S(2)}) copy-start(bf16[96,2560]{1,0:T(8,128)(2,1)S(1)} %collective-permute-done.23.refs_4_) | copy-start | bytes 1474564
  250.3 21.2 %collective-permute-start.24 = (bf16[96,2560]{1,0:T(8,128)(2,1)S(1)}, bf16[96,2560]{1,0:T(8,128)(2,1)}, u32[]{:S(2)}, u32[]{:S(2)}) collective-permute-start(bf16[96,2560]{1,0:T(8,128)(2,1)S(1)} %collective-permute-done.23.refs_4_), channel_id=1, source_target_pairs={{1,0},{2,1},{5,4},{6,5},{9,8},{10,9},{13,12},{14,13},{17,16},{18,1... | collective-permute-start | bytes 1474568 | tf_op jit(solution)/shard_map/ppermute | solution.py:44
  251.6 19.9 %copy-start.6 = (bf16[96,2560]{1,0:T(8,128)(2,1)}, bf16[96,2560]{1,0:T(8,128)(2,1)S(1)}, u32[]{:S(2)}) copy-start(bf16[96,2560]{1,0:T(8,128)(2,1)S(1)} %collective-permute-done.20.refs_1_) | copy-start | bytes 1474564
  251.6 21.1 %collective-permute-start.21 = (bf16[96,2560]{1,0:T(8,128)(2,1)S(1)}, bf16[96,2560]{1,0:T(8,128)(2,1)}, u32[]{:S(2)}, u32[]{:S(2)}) collective-permute-start(bf16[96,2560]{1,0:T(8,128)(2,1)S(1)} %collective-permute-done.20.refs_1_), channel_id=1, source_target_pairs={{1,2},{2,3},{5,6},{6,7},{9,10},{10,11},{13,14},{14,15},{17,18},{18... | collective-permute-start | bytes 1474568 | tf_op jit(solution)/shard_map/ppermute | solution.py:44
  260.8 11.9 %copy-start.8 = (bf16[96,2560]{1,0:T(8,128)(2,1)}, bf16[96,2560]{1,0:T(8,128)(2,1)S(1)}, u32[]{:S(2)}) copy-start(bf16[96,2560]{1,0:T(8,128)(2,1)S(1)} %collective-permute-done.43.refs_11_) | copy-start | bytes 1474564
  260.8 21.2 %collective-permute-start.44 = (bf16[96,2560]{1,0:T(8,128)(2,1)S(1)}, bf16[96,2560]{1,0:T(8,128)(2,1)}, u32[]{:S(2)}, u32[]{:S(2)}) collective-permute-start(bf16[96,2560]{1,0:T(8,128)(2,1)S(1)} %collective-permute-done.43.refs_11_), channel_id=1, source_target_pairs={{1,0},{2,1},{5,4},{6,5},{9,8},{10,9},{13,12},{14,13},{17,16},{18,1... | collective-permute-start | bytes 1474568 | tf_op jit(solution)/shard_map/ppermute | solution.py:44
  262.1 19.9 %copy-start.9 = (bf16[96,2560]{1,0:T(8,128)(2,1)}, bf16[96,2560]{1,0:T(8,128)(2,1)S(1)}, u32[]{:S(2)}) copy-start(bf16[96,2560]{1,0:T(8,128)(2,1)S(1)} %collective-permute-done.40.refs_8_) | copy-start | bytes 1474564
  262.1 21.1 %collective-permute-start.41 = (bf16[96,2560]{1,0:T(8,128)(2,1)S(1)}, bf16[96,2560]{1,0:T(8,128)(2,1)}, u32[]{:S(2)}, u32[]{:S(2)}) collective-permute-start(bf16[96,2560]{1,0:T(8,128)(2,1)S(1)} %collective-permute-done.40.refs_8_), channel_id=1, source_target_pairs={{1,2},{2,3},{5,6},{6,7},{9,10},{10,11},{13,14},{14,15},{17,18},{18... | collective-permute-start | bytes 1474568 | tf_op jit(solution)/shard_map/ppermute | solution.py:44
  271.4 22.7 %collective-permute-start.25 = (bf16[96,2560]{1,0:T(8,128)(2,1)}, bf16[96,2560]{1,0:T(8,128)(2,1)}, u32[]{:S(2)}, u32[]{:S(2)}) collective-permute-start(bf16[96,2560]{1,0:T(8,128)(2,1)} %collective-permute-done.24.refs_5_), channel_id=1, source_target_pairs={{1,0},{5,4},{9,8},{13,12},{17,16},{21,20},{25,24},{29,28}} | collective-permute-start | bytes 1474568 | tf_op jit(solution)/shard_map/ppermute | solution.py:44
  272.7 21.4 %collective-permute-start.22 = (bf16[96,2560]{1,0:T(8,128)(2,1)}, bf16[96,2560]{1,0:T(8,128)(2,1)}, u32[]{:S(2)}, u32[]{:S(2)}) collective-permute-start(bf16[96,2560]{1,0:T(8,128)(2,1)} %collective-permute-done.21.refs_2_), channel_id=1, source_target_pairs={{2,3},{6,7},{10,11},{14,15},{18,19},{22,23},{26,27},{30,31}} | collective-permute-start | bytes 1474568 | tf_op jit(solution)/shard_map/ppermute | solution.py:44
  282.0 12.2 %collective-permute-start.45 = (bf16[96,2560]{1,0:T(8,128)(2,1)}, bf16[96,2560]{1,0:T(8,128)(2,1)}, u32[]{:S(2)}, u32[]{:S(2)}) collective-permute-start(bf16[96,2560]{1,0:T(8,128)(2,1)} %collective-permute-done.44.refs_12_), channel_id=1, source_target_pairs={{1,0},{5,4},{9,8},{13,12},{17,16},{21,20},{25,24},{29,28}} | collective-permute-start | bytes 1474568 | tf_op jit(solution)/shard_map/ppermute | solution.py:44
  283.3 10.9 %collective-permute-start.42 = (bf16[96,2560]{1,0:T(8,128)(2,1)}, bf16[96,2560]{1,0:T(8,128)(2,1)}, u32[]{:S(2)}, u32[]{:S(2)}) collective-permute-start(bf16[96,2560]{1,0:T(8,128)(2,1)} %collective-permute-done.41.refs_9_), channel_id=1, source_target_pairs={{2,3},{6,7},{10,11},{14,15},{18,19},{22,23},{26,27},{30,31}} | collective-permute-start | bytes 1474568 | tf_op jit(solution)/shard_map/ppermute | solution.py:44
  285.9 8.2 %copy-start.1 = (bf16[96,2560]{1,0:T(8,128)(2,1)S(1)}, bf16[96,2560]{1,0:T(8,128)(2,1)}, u32[]{:S(2)}) copy-start(bf16[96,2560]{1,0:T(8,128)(2,1)} %copy-done) | copy-start | bytes 1474564
  285.9 8.2 %copy-start.3 = (bf16[96,2560]{1,0:T(8,128)(2,1)S(1)}, bf16[96,2560]{1,0:T(8,128)(2,1)}, u32[]{:S(2)}) copy-start(bf16[96,2560]{1,0:T(8,128)(2,1)} %copy-done.2) | copy-start | bytes 1474564
  285.9 8.2 %copy-start.5 = (bf16[96,2560]{1,0:T(8,128)(2,1)S(1)}, bf16[96,2560]{1,0:T(8,128)(2,1)}, u32[]{:S(2)}) copy-start(bf16[96,2560]{1,0:T(8,128)(2,1)} %copy-done.4) | copy-start | bytes 1474564
  285.9 8.2 %copy-start.7 = (bf16[96,2560]{1,0:T(8,128)(2,1)S(1)}, bf16[96,2560]{1,0:T(8,128)(2,1)}, u32[]{:S(2)}) copy-start(bf16[96,2560]{1,0:T(8,128)(2,1)} %copy-done.6) | copy-start | bytes 1474564
  308.1 65.8 %collective-permute-start = (bf16[640,2560]{1,0:T(8,128)(2,1)}, bf16[640,2560]{1,0:T(8,128)(2,1)}, u32[]{:S(2)}, u32[]{:S(2)}) collective-permute-start(bf16[640,2560]{1,0:T(8,128)(2,1)} %get-tuple-element.109), channel_id=1, source_target_pairs={{0,4},{4,8},{8,12},{12,16},{16,20},{20,24},{24,28},{28,0},{1,5},{5... | collective-permute-start | bytes 9830408 | tf_op jit(solution)/shard_map/cond/branch_0_fun/ppermute | solution.py:376
  373.9 7.9 %copy-start.16 = (bf16[1,384,2560]{2,1,0:T(8,128)(2,1)}, bf16[1,384,2560]{2,1,0:T(8,128)(2,1)S(1)}, u32[]{:S(2)}) copy-start(bf16[1,384,2560]{2,1,0:T(8,128)(2,1)S(1)} %get-tuple-element.205) | copy-start | bytes 5898244
  (8 other events, 9.2 us)
where the time goes:
time: 388 us; the launch traced here: 384 us
  Pallas kernels  142 us (37%)
  starting transfers between devices  132 us (34%)
  blocking collectives  53.3 us (14%)
  waiting for transfers between devices  35.3 us (9%)
  between operations  8.41 us (2%)
  other arithmetic  7.51 us (2%)
  local copies, waits for them, and re-layouts  6.06 us (2%)
    pallas_call x28, Pallas kernels, call(): pl.pallas_call(body, name=name, out_shape=[jax.ShapeDtypeStruct(shape, ki...  142 us
    ppermute x40, starting transfers between devices, hop(): return lax.ppermute(value, 'fsdp', [(i, i + step) for i in pairs])  105 us
    all_to_all x1, blocking collectives, swapped(): return lax.all_to_all(blocks, 'fsdp', 0, 0, tiled=False)  53.3 us
    ppermute x40, waiting for transfers between devices, hop(): return lax.ppermute(value, 'fsdp', [(i, i + step) for i in pairs])  32.3 us
    all_to_all x4, starting transfers between devices, swapped(): return lax.all_to_all(blocks, 'fsdp', 0, 0, tiled=False)  19.9 us
  transfers between devices with their start and end apart: 48, of which 9 were waited for; matrix products, arithmetic and copies ran while one was open for 2% of the time, Pallas kernels for 31%

commit v1 on v0

--- a/solution.py
+++ b/solution.py
@@ -12,7 +12,7 @@
 TOKEN = jax.ShapeDtypeStruct((8, 128), jnp.float32)
 
 
-def call(body, name, grid, ins, outs, scalars=(), scratch=(), flops=0, moved=0):
+def call(body, name, grid, ins, outs, scalars=(), scratch=(), flops=0, moved=0, vmem=12):
     return pl.pallas_call(
         body,
         name=name,
@@ -24,7 +24,7 @@
             out_specs=[pl.BlockSpec(block, place) for _, _, block, place in outs],
             scratch_shapes=scratch,
         ),
-        compiler_params=pltpu.CompilerParams(vmem_limit_bytes=58 * MIB),
+        compiler_params=pltpu.CompilerParams(vmem_limit_bytes=vmem * MIB),
         cost_estimate=pl.CostEstimate(flops=flops, bytes_accessed=moved, transcendentals=0),
     )(*scalars, *(array for array, _, _ in ins))
 
@@ -48,8 +48,11 @@
     return hop(right, 1, rights), hop(left, -1, lefts)
 
 
-def tile_of(width):
-    return 512 if width % 512 == 0 else width
+def tile_of(width, most=512):
+    tile = most
+    while width % tile:
+        tile //= 2
+    return tile
 
 
 def cut_heads(heads, start, size, members, token):
@@ -75,9 +78,10 @@
 def partial_products(mine, weights, token):
     members, size, rows = mine.shape
     width = weights.shape[1]
-    tile = tile_of(width)
-
-    def body(mine_ref, weights_ref, token_ref, out_ref, last_ref, first_ref):
+    tile = tile_of(width, 1280)
+
+    def body(mine_ref, weights_ref, *refs):
+        out_ref, last_ref, first_ref = refs[-3:]
         product = jnp.dot(
             mine_ref[...].reshape(members * size, rows),
             weights_ref[...],
@@ -95,8 +99,8 @@
         [
             (mine, (members, size, rows), fixed(0, 0, 0)),
             (weights, (rows, tile), lambda j: (0, j)),
-            token_in(token),
-        ],
+        ]
+        + ([] if token is None else [token_in(token)]),
         [
             (
                 (members, size, width),
@@ -109,12 +113,13 @@
         ],
         flops=2 * members * size * rows * width,
         moved=2 * (members * size * (rows + width) + rows * width),
+        vmem=20,
     )
 
 
 def next_payload(right, left, parts, scalars, pick):
     members, size, width = parts.shape
-    tile = tile_of(width)
+    step = 48
 
     def joined(arrived, part, counts):
         if pick:
@@ -129,17 +134,17 @@
         left_out[...] = joined(left_ref[...], of_left[0], s[3] > 0)
         token_out[...] = jnp.zeros((8, 128), jnp.float32)
 
-    here = (size, tile), lambda j, s: (0, j)
+    here = (step, width), lambda i, s: (i, 0)
     flat = ((size, width), jnp.bfloat16) + here
     return call(
         body,
         "next_payload",
-        (width // tile,),
+        (size // step,),
         [
             (right,) + here,
             (left,) + here,
-            (parts, (1, size, tile), lambda j, s: (s[0], 0, j)),
-            (parts, (1, size, tile), lambda j, s: (s[2], 0, j)),
+            (parts, (1, step, width), lambda i, s: (s[0], i, 0)),
+            (parts, (1, step, width), lambda i, s: (s[2], i, 0)),
         ],
         [flat, flat, TOKEN_OUT],
         scalars=(scalars,),
@@ -150,7 +155,7 @@
 
 def unit_gradient(right, left, parts, place, residual, cotangent, gain, start, token):
     members, size, width = parts.shape
-    step = 32
+    step = 48
 
     def body(s, right_ref, left_ref, own_ref, residual_ref, cot_ref, gain_ref, *refs):
         product = (
@@ -204,9 +209,18 @@
 
 
 def unit_ins(units, tile):
-    return [
-        (unit, (unit.shape[0], tile), lambda j, s: (0, j)) for chunk in units for unit in chunk
-    ]
+    ins = []
+    for chunk in units:
+        block = (chunk[0].shape[0], tile)
+        members = (len(chunk) + 1) // 2
+        ins.append((chunk[0], block, lambda j, s: (0, j)))
+        for k in range(members - 1):
+            place = lambda j, s, k=k: (0, jnp.where(s[0] > k, j, 0))
+            ins.append((chunk[1 + k], block, place))
+        for m in range(members - 1):
+            place = lambda j, s, k=members - 2 - m: (0, jnp.where(s[0] > k, 0, j))
+            ins.append((chunk[members + m], block, place))
+    return ins
 
 
 def mine_ins(mine):
@@ -265,6 +279,7 @@
         scratch=[pltpu.VMEM((rows, total), jnp.bfloat16)],
         flops=2 * total * rows * width,
         moved=2 * count * units[0][0].shape[0] * width + 12 * rows * width,
+        vmem=26,
     )
 
 
@@ -321,6 +336,7 @@
         scratch=[pltpu.VMEM((total, rows), jnp.float32)],
         flops=2 * total * rows * width,
         moved=2 * count * sizes[0] * width + 2 * rows * width,
+        vmem=20,
     )[0]
 
 
@@ -351,7 +367,7 @@
 
 def widened(value):
     rows, width = value.shape
-    step = 64
+    step = 160
 
     def body(value_ref, out_ref):
         out_ref[...] = value_ref[...].astype(jnp.float32)
@@ -364,6 +380,7 @@
         [(value,) + block],
         [((rows, width), jnp.float32) + block],
         moved=6 * rows * width,
+        vmem=20,
     )[0]
 
 
@@ -435,7 +452,7 @@
     mine = [[None] * count for _ in range(rounds)]
     units = [[None] * count for _ in range(rounds)]
     before = [None] * count
-    hint = [jnp.broadcast_to(outbox_weight[None], (8, 128))] * count
+    hint = [None] * (count - 1) + [jnp.broadcast_to(outbox_weight[None], (8, 128))]
     kept = None
     grads = []
 

time: 388 us -> 355 us (0.915)
  Pallas kernels: 142 us -> 85.4 us
  waiting for transfers between devices: 35.3 us -> 74.6 us
  blocking collectives: 53.3 us -> 35.4 us
  local copies, waits for them, and re-layouts: 6.06 us -> 18.6 us
  starting transfers between devices: 132 us -> 125 us
    pallas_call x28, Pallas kernels: 142 us -> 85.4 us  [call(): pl.pallas_call(body, name=name, out_shape=[jax.ShapeDtypeStruct(shape, ki...]
    ppermute x40, waiting for transfers between devices: 32.3 us -> 55.4 us  [hop(): return lax.ppermute(value, 'fsdp', [(i, i + step) for i in pairs])]
    all_to_all x1, blocking collectives: 53.3 us -> 35.4 us  [swapped(): return lax.all_to_all(blocks, 'fsdp', 0, 0, tiled=False)]
    ppermute x1, waiting for transfers between devices: 0.01 us -> 14.7 us  [tail(): lax.ppermute(kept, 'rep', [(i, (i + (1 << bit_place)) % length) for i in...]
    unnamed x48 -> x104, local copies, waits for them, and re-layouts: 4.86 us -> 18.6 us
    ppermute x40, starting transfers between devices: 105 us -> 95.2 us  [hop(): return lax.ppermute(value, 'fsdp', [(i, i + step) for i in pairs])]
  transfers between devices with their start and end apart: 48 -> 48, of which waited for: 9 -> 14; matrix products, arithmetic and copies ran while one was open for 2% -> 1% of each run, Pallas kernels for 31% -> 20%
where the time goes in v1:
time: 355 us; the launch traced here: 352 us
  starting transfers between devices  125 us (35%)
  Pallas kernels  85.4 us (24%)
  waiting for transfers between devices  74.6 us (21%)
  blocking collectives  35.4 us (10%)
  local copies, waits for them, and re-layouts  18.6 us (5%)
  between operations  8.86 us (2%)
  other arithmetic  4.74 us (1%)
    ppermute x40, starting transfers between devices, hop(): return lax.ppermute(value, 'fsdp', [(i, i + step) for i in pairs])  95.2 us
    pallas_call x28, Pallas kernels, call(): pl.pallas_call(body, name=name, out_shape=[jax.ShapeDtypeStruct(shape, ki...  85.4 us
    ppermute x40, waiting for transfers between devices, hop(): return lax.ppermute(value, 'fsdp', [(i, i + step) for i in pairs])  55.4 us
    all_to_all x1, blocking collectives, swapped(): return lax.all_to_all(blocks, 'fsdp', 0, 0, tiled=False)  35.4 us
    all_to_all x4, starting transfers between devices, swapped(): return lax.all_to_all(blocks, 'fsdp', 0, 0, tiled=False)  21.3 us
    unnamed x104, local copies, waits for them, and re-layouts  18.6 us
    ppermute x1, waiting for transfers between devices, tail(): lax.ppermute(kept, 'rep', [(i, (i + (1 << bit_place)) % length) for i in...  14.7 us
  transfers between devices with their start and end apart: 48, of which 14 were waited for; matrix products, arithmetic and copies ran while one was open for 1% of the time, Pallas kernels for 20%

profile of v1, /device:TPU:0, one launch (start us, length us, event | category | flops | bytes accessed | tf_op | source)
XLA Modules:
  0.0 352.3 jit_solution(1565219951828568819)
XLA Ops:
  0.7 1.5 copy-done.10
  3.0 6.3 %all-to-all-start.3 = ((bf16[4,96,640]{2,1,0:T(8,128)(2,1)}), bf16[4,96,640]{2,1,0:T(8,128)(2,1)S(1)}, u32[]{:S(2)}, u32[]{:S(2)}) async-start(bf16[4,96,640]{2,1,0:T(8,128)(2,1)} %cut_heads.4), calls=%async_computation.3 | async-start | bytes 983040 | tf_op jit(solution)/shard_map/all_to_all | solution.py:388
  10.8 2.8 collective-permute-start.24
  13.6 2.8 collective-permute-start.23
  18.6 4.5 %all-to-all-done.3.mine_ref.refs_14_ = bf16[4,96,640]{2,1,0:T(8,128)(2,1)S(1)} async-done(((bf16[4,96,640]{2,1,0:T(8,128)(2,1)}), bf16[4,96,640]{2,1,0:T(8,128)(2,1)S(1)}, u32[]{:S(2)}, u32[]{:S(2)}) %all-to-all-start.3) | async-done | bytes 491552 | tf_op jit(solution)/shard_map/all_to_all | solution.py:388
  23.1 3.5 all-to-all-start.5
  26.6 3.6 %multiply_convert_fusion.weights_ref.refs_14_ = bf16[640,2560]{1,0:T(8,128)(2,1)S(1)} fusion(f32[]{:T(128)} %bitcast.30, f32[1,640,2560]{2,1,0:T(8,128)} %param.12), kind=kLoop, calls=%fused_computation.3 | loop fusion | flops 4915200 | bytes 9830404 | tf_op jit(solution)/shard_map/convert_element_type | solution.py:429
  30.2 3.0 partial_products.4
  33.3 3.9 %collective-permute-start.3 = (bf16[96,2560]{1,0:T(8,128)(2,1)}, bf16[96,2560]{1,0:T(8,128)(2,1)S(1)}, u32[]{:S(2)}, u32[]{:S(2)}) collective-permute-start(bf16[96,2560]{1,0:T(8,128)(2,1)} %get-tuple-element.206), channel_id=1, source_target_pairs={{0,1},{4,5},{8,9},{12,13},{16,17},{20,21},{24,25},{28,29}} | collective-permute-start | bytes 1474568 | tf_op jit(solution)/shard_map/ppermute | solution.py:44
  40.4 4.5 %partial_products.6 = (bf16[4,96,2560]{2,1,0:T(8,128)(2,1)S(1)}, bf16[96,2560]{1,0:T(8,128)(2,1)}, bf16[96,2560]{1,0:T(8,128)(2,1)}) custom-call(bf16[4,96,640]{2,1,0:T(8,128)(2,1)S(1)} %all-to-all-done.5.mine_ref.refs_15_, bf16[640,2560]{1,0:T(8,128)(2,1)} %copy-done.35, f32[8,128]{1,0:T(8,128)S(1)} %broadcast_in_dim.41.refs_0_), custom_call_target="tpu_custom_call" | custom-call | flops 1258291200 | bytes 5734400 | tf_op jit(solution)/shard_map/partial_products/pallas_call | solution.py:16
  46.2 2.1 collective-permute-start.26
  49.8 1.6 next_payload.10
  51.4 1.5 collective-permute-start.5
  54.5 5.9 %all-to-all-start.4 = ((bf16[4,96,640]{2,1,0:T(8,128)(2,1)}), bf16[4,96,640]{2,1,0:T(8,128)(2,1)S(1)}, u32[]{:S(2)}, u32[]{:S(2)}) async-start(bf16[4,96,640]{2,1,0:T(8,128)(2,1)} %cut_heads.5), calls=%async_computation.4 | async-start | bytes 983040 | tf_op jit(solution)/shard_map/all_to_all | solution.py:388
  60.4 1.5 copy-done.1
  62.0 2.8 next_payload.15
  64.8 4.7 %collective-permute-start.28 = (bf16[96,2560]{1,0:T(8,128)(2,1)}, bf16[96,2560]{1,0:T(8,128)(2,1)}, u32[]{:S(2)}, u32[]{:S(2)}) collective-permute-start(bf16[96,2560]{1,0:T(8,128)(2,1)} %get-tuple-element.225), channel_id=1, source_target_pairs={{0,1},{1,2},{4,5},{5,6},{8,9},{9,10},{12,13},{13,14},{16,17},{17,1... | collective-permute-start | bytes 1474568 | tf_op jit(solution)/shard_map/ppermute | solution.py:44
  71.0 1.6 next_payload.11
  72.6 3.5 %collective-permute-start.7 = (bf16[96,2560]{1,0:T(8,128)(2,1)}, bf16[96,2560]{1,0:T(8,128)(2,1)S(1)}, u32[]{:S(2)}, u32[]{:S(2)}) collective-permute-start(bf16[96,2560]{1,0:T(8,128)(2,1)} %get-tuple-element.211), channel_id=1, source_target_pairs={{0,1},{1,2},{2,3},{4,5},{5,6},{6,7},{8,9},{9,10},{10,11},{12,13},{... | collective-permute-start | bytes 1474568 | tf_op jit(solution)/shard_map/ppermute | solution.py:44
  77.4 11.0 %collective-permute-done.28.right_ref = bf16[96,2560]{1,0:T(8,128)(2,1)} collective-permute-done((bf16[96,2560]{1,0:T(8,128)(2,1)}, bf16[96,2560]{1,0:T(8,128)(2,1)}, u32[]{:S(2)}, u32[]{:S(2)}) %collective-permute-start.28) | collective-permute-done | bytes 491552 | tf_op jit(solution)/shard_map/ppermute | solution.py:44
  88.5 2.7 next_payload.16
  91.2 5.3 %collective-permute-start.30 = (bf16[96,2560]{1,0:T(8,128)(2,1)}, bf16[96,2560]{1,0:T(8,128)(2,1)}, u32[]{:S(2)}, u32[]{:S(2)}) collective-permute-start(bf16[96,2560]{1,0:T(8,128)(2,1)} %get-tuple-element.227), channel_id=1, source_target_pairs={{0,1},{1,2},{2,3},{4,5},{5,6},{6,7},{8,9},{9,10},{10,11},{12,13},{... | collective-permute-start | bytes 1474568 | tf_op jit(solution)/shard_map/ppermute | solution.py:44
  98.7 5.6 %all-to-all-start.6 = ((bf16[4,96,640]{2,1,0:T(8,128)(2,1)}), bf16[4,96,640]{2,1,0:T(8,128)(2,1)}, u32[]{:S(2)}, u32[]{:S(2)}) async-start(bf16[4,96,640]{2,1,0:T(8,128)(2,1)} %cut_heads.7), calls=%async_computation.6 | async-start | bytes 983040 | tf_op jit(solution)/shard_map/all_to_all | solution.py:388
  104.3 1.5 copy-done.4
  105.8 1.5 copy-done.7
  107.4 1.8 unit_gradient.4.refs_0_
  110.6 5.3 %collective-permute-start.9 = (bf16[96,2560]{1,0:T(8,128)(2,1)S(1)}, bf16[96,2560]{1,0:T(8,128)(2,1)}, u32[]{:S(2)}, u32[]{:S(2)}) collective-permute-start(bf16[96,2560]{1,0:T(8,128)(2,1)S(1)} %unit_gradient.4.refs_0_), channel_id=1, source_target_pairs={{0,1},{1,2},{2,3},{4,5},{5,6},{6,7},{8,9},{9,10},{10,11},{12,13},{... | collective-permute-start | bytes 1474568 | tf_op jit(solution)/shard_map/ppermute | solution.py:44
  115.9 2.4 unit_gradient.6.refs_7_
  119.6 6.2 %collective-permute-start.32 = (bf16[96,2560]{1,0:T(8,128)(2,1)}, bf16[96,2560]{1,0:T(8,128)(2,1)}, u32[]{:S(2)}, u32[]{:S(2)}) collective-permute-start(bf16[96,2560]{1,0:T(8,128)(2,1)} %unit_gradient.6.refs_7_), channel_id=1, source_target_pairs={{0,1},{1,2},{2,3},{4,5},{5,6},{6,7},{8,9},{9,10},{10,11},{12,13},{... | collective-permute-start | bytes 1474568 | tf_op jit(solution)/shard_map/ppermute | solution.py:44
  127.0 4.2 %partial_products.5 = (bf16[4,96,2560]{2,1,0:T(8,128)(2,1)S(1)}, bf16[96,2560]{1,0:T(8,128)(2,1)}, bf16[96,2560]{1,0:T(8,128)(2,1)}) custom-call(bf16[4,96,640]{2,1,0:T(8,128)(2,1)S(1)} %copy-done.29, bf16[640,2560]{1,0:T(8,128)(2,1)} %copy-done.35, f32[8,128]{1,0:T(8,128)S(1)} %get-tuple-element.214.refs_0_), custom_call_target="tpu_custom_call" | custom-call | flops 1258291200 | bytes 5734400 | tf_op jit(solution)/shard_map/partial_products/pallas_call | solution.py:16
  131.2 2.5 next_payload.12
  133.7 7.4 %collective-permute-start.11 = (bf16[96,2560]{1,0:T(8,128)(2,1)}, bf16[96,2560]{1,0:T(8,128)(2,1)}, u32[]{:S(2)}, u32[]{:S(2)}) collective-permute-start(bf16[96,2560]{1,0:T(8,128)(2,1)} %get-tuple-element.216), channel_id=1, source_target_pairs={{0,1},{1,2},{2,3},{4,5},{5,6},{6,7},{8,9},{9,10},{10,11},{12,13},{... | collective-permute-start | bytes 1474568 | tf_op jit(solution)/shard_map/ppermute | solution.py:44
  142.4 4.4 %partial_products.7 = (bf16[4,96,2560]{2,1,0:T(8,128)(2,1)S(1)}, bf16[96,2560]{1,0:T(8,128)(2,1)}, bf16[96,2560]{1,0:T(8,128)(2,1)}) custom-call(bf16[4,96,640]{2,1,0:T(8,128)(2,1)} %all-to-all-done.6.mine_ref.refs_15_, bf16[640,2560]{1,0:T(8,128)(2,1)} %copy-done.35, f32[8,128]{1,0:T(8,128)S(1)} %get-tuple-element.230.refs_0_), custom_call_target="tpu_custom_call" | custom-call | flops 1258291200 | bytes 5734400 | tf_op jit(solution)/shard_map/partial_products/pallas_call | solution.py:16
  146.8 2.5 next_payload.17
  149.2 4.6 %collective-permute-start.34 = (bf16[96,2560]{1,0:T(8,128)(2,1)S(1)}, bf16[96,2560]{1,0:T(8,128)(2,1)S(1)}, u32[]{:S(2)}, u32[]{:S(2)}) collective-permute-start(bf16[96,2560]{1,0:T(8,128)(2,1)S(1)} %get-tuple-element.232), channel_id=1, source_target_pairs={{0,1},{1,2},{2,3},{4,5},{5,6},{6,7},{8,9},{9,10},{10,11},{12,13},{... | collective-permute-start | bytes 1474568 | tf_op jit(solution)/shard_map/ppermute | solution.py:44
  155.9 2.5 next_payload.13
  158.4 3.7 %collective-permute-start.13 = (bf16[96,2560]{1,0:T(8,128)(2,1)S(1)}, bf16[96,2560]{1,0:T(8,128)(2,1)S(1)}, u32[]{:S(2)}, u32[]{:S(2)}) collective-permute-start(bf16[96,2560]{1,0:T(8,128)(2,1)S(1)} %get-tuple-element.218), channel_id=1, source_target_pairs={{0,1},{1,2},{2,3},{4,5},{5,6},{6,7},{8,9},{9,10},{10,11},{12,13},{... | collective-permute-start | bytes 1474568 | tf_op jit(solution)/shard_map/ppermute | solution.py:44
  164.8 5.0 %collective-permute-done.35.left_ref.refs_12_ = bf16[96,2560]{1,0:T(8,128)(2,1)S(1)} collective-permute-done((bf16[96,2560]{1,0:T(8,128)(2,1)S(1)}, bf16[96,2560]{1,0:T(8,128)(2,1)S(1)}, u32[]{:S(2)}, u32[]{:S(2)}) %collective-permute-start.35) | collective-permute-done | bytes 491552 | tf_op jit(solution)/shard_map/ppermute | solution.py:44
  171.2 2.0 collective-permute-start.36
  175.4 5.0 %collective-permute-done.14.left_ref.refs_6_ = bf16[96,2560]{1,0:T(8,128)(2,1)S(1)} collective-permute-done((bf16[96,2560]{1,0:T(8,128)(2,1)S(1)}, bf16[96,2560]{1,0:T(8,128)(2,1)S(1)}, u32[]{:S(2)}, u32[]{:S(2)}) %collective-permute-start.14) | collective-permute-done | bytes 491552 | tf_op jit(solution)/shard_map/ppermute | solution.py:44
  181.7 2.0 collective-permute-start.15
  185.9 5.0 %collective-permute-done.37.left_ref.refs_13_ = bf16[96,2560]{1,0:T(8,128)(2,1)S(1)} collective-permute-done((bf16[96,2560]{1,0:T(8,128)(2,1)S(1)}, bf16[96,2560]{1,0:T(8,128)(2,1)S(1)}, u32[]{:S(2)}, u32[]{:S(2)}) %collective-permute-start.37) | collective-permute-done | bytes 491552 | tf_op jit(solution)/shard_map/ppermute | solution.py:44
  192.2 1.9 collective-permute-start.38
  194.1 1.5 collective-permute-start.39
  195.8 7.4 %weight_step.2 = (f32[640,2560]{1,0:T(8,128)S(1)}, f32[8,128]{1,0:T(8,128)S(1)}) custom-call(s32[4]{0:T(128)S(1)} %and_select_fusion.s, bf16[96,2560]{1,0:T(8,128)(2,1)S(1)} %unit_gradient.4.refs_0_, bf16[96,2560]{1,0:T(8,128)(2,1)} %collective-permute-done.9.right_ref.refs_1_, bf16[96,2560]{1,0:T(8,128)(2,1)} %collective-permute-done.11.right_ref.refs_2_, ...), custom_call_target="tpu_custom_call" | custom-call | flops 2516582400 | bytes 26542080 | tf_op jit(solution)/shard_map/weight_step/pallas_call | solution.py:16
  203.9 2.1 copy-done.14
  207.3 5.2 %collective-permute-start.17 = (bf16[96,2560]{1,0:T(8,128)(2,1)S(1)}, bf16[96,2560]{1,0:T(8,128)(2,1)S(1)}, u32[]{:S(2)}, u32[]{:S(2)}) collective-permute-start(bf16[96,2560]{1,0:T(8,128)(2,1)S(1)} %unit_gradient.5.refs_0_), channel_id=1, source_target_pairs={{0,1},{1,2},{2,3},{4,5},{5,6},{6,7},{8,9},{9,10},{10,11},{12,13},{... | collective-permute-start | bytes 1474568 | tf_op jit(solution)/shard_map/ppermute | solution.py:44
  215.1 4.6 %collective-permute-start.40 = (bf16[96,2560]{1,0:T(8,128)(2,1)}, bf16[96,2560]{1,0:T(8,128)(2,1)S(1)}, u32[]{:S(2)}, u32[]{:S(2)}) collective-permute-start(bf16[96,2560]{1,0:T(8,128)(2,1)} %unit_gradient.7.refs_7_), channel_id=1, source_target_pairs={{0,1},{1,2},{2,3},{4,5},{5,6},{6,7},{8,9},{9,10},{10,11},{12,13},{... | collective-permute-start | bytes 1474568 | tf_op jit(solution)/shard_map/ppermute | solution.py:44
  219.7 3.0 collective-permute-done.20.refs_4_
  224.8 1.5 collective-permute-start.18
  226.2 6.9 %collective-permute-done.43.refs_11_ = bf16[96,2560]{1,0:T(8,128)(2,1)S(1)} collective-permute-done((bf16[96,2560]{1,0:T(8,128)(2,1)}, bf16[96,2560]{1,0:T(8,128)(2,1)S(1)}, u32[]{:S(2)}, u32[]{:S(2)}) %collective-permute-start.43) | collective-permute-done | bytes 491552 | tf_op jit(solution)/shard_map/ppermute | solution.py:44
  234.4 1.5 collective-permute-start.41
  235.9 7.9 %collective-permute-done.21.refs_5_ = bf16[96,2560]{1,0:T(8,128)(2,1)} collective-permute-done((bf16[96,2560]{1,0:T(8,128)(2,1)}, bf16[96,2560]{1,0:T(8,128)(2,1)}, u32[]{:S(2)}, u32[]{:S(2)}) %collective-permute-start.21) | collective-permute-done | bytes 491552 | tf_op jit(solution)/shard_map/ppermute | solution.py:44
  245.1 1.5 collective-permute-start.19
  246.5 7.8 %collective-permute-done.44.refs_12_ = bf16[96,2560]{1,0:T(8,128)(2,1)} collective-permute-done((bf16[96,2560]{1,0:T(8,128)(2,1)S(1)}, bf16[96,2560]{1,0:T(8,128)(2,1)}, u32[]{:S(2)}, u32[]{:S(2)}) %collective-permute-start.44) | collective-permute-done | bytes 491552 | tf_op jit(solution)/shard_map/ppermute | solution.py:44
  255.6 1.5 collective-permute-start.42
  264.6 8.7 %grad_rows.7 = bf16[4,192,640]{2,1,0:T(8,128)(2,1)S(1)} custom-call(s32[4]{0:T(128)S(1)} %and_select_fusion.s, bf16[96,2560]{1,0:T(8,128)(2,1)S(1)} %unit_gradient.4.refs_0_, bf16[96,2560]{1,0:T(8,128)(2,1)} %collective-permute-done.9.right_ref.refs_1_, bf16[96,2560]{1,0:T(8,128)(2,1)} %collective-permute-done.11.right_ref.refs_2_, ...), custom_call_target="tpu_custom_call" | custom-call | flops 2516582400 | bytes 10158080 | tf_op jit(solution)/shard_map/grad_rows/pallas_call | solution.py:16
  274.4 9.4 %weight_step.3 = (f32[640,2560]{1,0:T(8,128)}, bf16[640,2560]{1,0:T(8,128)(2,1)S(1)}) custom-call(s32[4]{0:T(128)S(1)} %and_select_fusion.s, bf16[96,2560]{1,0:T(8,128)(2,1)} %copy-done.37, bf16[96,2560]{1,0:T(8,128)(2,1)} %copy-done.39, bf16[96,2560]{1,0:T(8,128)(2,1)} %collective-permute-done.18.refs_2_, bf16[96,2560]{1,0:T(8,128)(2,1)} %collective-permute-done.19.refs_3_, ...), custom_call_target="tpu_custom_call" | custom-call | flops 2516582400 | bytes 26542080 | tf_op jit(solution)/shard_map/weight_step/pallas_call | solution.py:16
  283.9 60.4 %conditional.1 = (bf16[640,2560]{1,0:T(8,128)(2,1)}, bf16[1,384,2560]{2,1,0:T(8,128)(2,1)S(1)}) conditional(s32[]{:T(128)} %clamp.3, (bf16[640,2560]{1,0:T(8,128)(2,1)S(1)}, s32[4]{0:T(128)S(1)}, bf16[96,2560]{1,0:T(8,128)(2,1)S(1)}, bf16[96,2560]{1,0:T(8,128)(2,1)S(1)}, bf16[96,2560]{1,0:T(8,128)(2,1)}, ...), branch_computations={%region_1.2_spmd, %region_2.3_spmd, %region_3.4_spmd} | conditional | flops 2520514560 | bytes 35061816 | solution.py:517
  283.9 1.6 collective-permute-start.2
  285.5 8.1 %grad_rows.6 = bf16[4,192,640]{2,1,0:T(8,128)(2,1)S(1)} custom-call(s32[4]{0:T(128)S(1)} %get-tuple-element.147.s, bf16[96,2560]{1,0:T(8,128)(2,1)S(1)} %get-tuple-element.148.refs_0_, bf16[96,2560]{1,0:T(8,128)(2,1)S(1)} %get-tuple-element.149.refs_1_, bf16[96,2560]{1,0:T(8,128)(2,1)} %get-tuple-element.150.refs_2_, ...), custom_call_target="tpu_custom_call" | custom-call | flops 2516582400 | bytes 10158080 | tf_op jit(solution)/shard_map/cond/branch_2_fun/grad_rows/pallas_call | solution.py:16
  293.8 35.4 %all_to_all.34.blocks_ref = bf16[4,384,640]{2,1,0:T(8,128)(2,1)S(1)} all-to-all(bf16[4,384,640]{2,1,0:T(8,128)(2,1)S(1)} %pad_maximum_fusion.2), channel_id=1, replica_groups=mesh['rep'=8,'fsdp'=4] {'fsdp'}, dimensions={0} | all-to-all | bytes 3932160 | tf_op jit(solution)/shard_map/cond/branch_2_fun/all_to_all | solution.py:388
  329.6 14.7 %collective-permute-done.2 = bf16[640,2560]{1,0:T(8,128)(2,1)} collective-permute-done((bf16[640,2560]{1,0:T(8,128)(2,1)S(1)}, bf16[640,2560]{1,0:T(8,128)(2,1)}, u32[]{:S(2)}, u32[]{:S(2)}) %collective-permute-start.2) | collective-permute-done | bytes 3276832 | tf_op jit(solution)/shard_map/cond/branch_2_fun/ppermute | solution.py:393
  344.3 5.7 %widened.1 = f32[640,2560]{1,0:T(8,128)} custom-call(bf16[640,2560]{1,0:T(8,128)(2,1)} %get-tuple-element.242.value_ref), custom_call_target="tpu_custom_call" | custom-call | bytes 9830400 | tf_op jit(solution)/shard_map/widened/pallas_call | solution.py:16
  (177 shorter events, 49.8 us)
Async XLA Ops:
  0.6 16.6 %copy-start.47 = (s32[8]{0:T(128)S(1)}, s32[8]{0:T(128)}, u32[]{:S(2)}) copy-start(s32[8]{0:T(128)} %param.20) | copy-start | bytes 100
  2.2 14.3 %copy-start.11 = (bf16[1,384,2560]{2,1,0:T(8,128)(2,1)S(1)}, bf16[1,384,2560]{2,1,0:T(8,128)(2,1)}, u32[]{:S(2)}) copy-start(bf16[1,384,2560]{2,1,0:T(8,128)(2,1)} %param.16) | copy-start | bytes 5898244
  3.0 20.1 %all-to-all-start.3 = ((bf16[4,96,640]{2,1,0:T(8,128)(2,1)}), bf16[4,96,640]{2,1,0:T(8,128)(2,1)S(1)}, u32[]{:S(2)}, u32[]{:S(2)}) async-start(bf16[4,96,640]{2,1,0:T(8,128)(2,1)} %cut_heads.4), calls=%async_computation.3 | async-start | bytes 983040 | tf_op jit(solution)/shard_map/all_to_all | solution.py:388
  10.0 28.6 %collective-permute-start.25 = (f32[1]{0:T(128)}, f32[1]{0:T(128)}, u32[]{:S(2)}, u32[]{:S(2)}) collective-permute-start(f32[1]{0:T(128)} %mul.12), channel_id=1, source_target_pairs={{0,4},{4,8},{8,12},{12,16},{16,20},{20,24},{24,28},{28,0},{1,5},{5... | collective-permute-start | bytes 20 | tf_op jit(solution)/shard_map/ppermute | solution.py:420
  10.8 27.7 %collective-permute-start.24 = (f32[1]{0:T(128)}, f32[1]{0:T(128)}, u32[]{:S(2)}, u32[]{:S(2)}) collective-permute-start(f32[1]{0:T(128)} %mul.12), channel_id=1, source_target_pairs={{0,8},{4,12},{8,16},{12,20},{16,24},{20,28},{24,0},{28,4},{1,9},{5... | collective-permute-start | bytes 20 | tf_op jit(solution)/shard_map/ppermute | solution.py:420
  13.6 26.2 %collective-permute-start.23 = (f32[1]{0:T(128)}, f32[1]{0:T(128)}, u32[]{:S(2)}, u32[]{:S(2)}) collective-permute-start(f32[1]{0:T(128)} %mul.12), channel_id=1, source_target_pairs={{0,16},{4,20},{8,24},{12,28},{16,0},{20,4},{24,8},{28,12},{1,17},{... | collective-permute-start | bytes 20 | tf_op jit(solution)/shard_map/ppermute | solution.py:420
  23.1 17.3 %all-to-all-start.5 = ((bf16[4,96,640]{2,1,0:T(8,128)(2,1)}), bf16[4,96,640]{2,1,0:T(8,128)(2,1)S(1)}, u32[]{:S(2)}, u32[]{:S(2)}) async-start(bf16[4,96,640]{2,1,0:T(8,128)(2,1)} %cut_heads.6), calls=%async_computation.5 | async-start | bytes 983040 | tf_op jit(solution)/shard_map/all_to_all | solution.py:388
  33.3 16.5 %collective-permute-start.3 = (bf16[96,2560]{1,0:T(8,128)(2,1)}, bf16[96,2560]{1,0:T(8,128)(2,1)S(1)}, u32[]{:S(2)}, u32[]{:S(2)}) collective-permute-start(bf16[96,2560]{1,0:T(8,128)(2,1)} %get-tuple-element.206), channel_id=1, source_target_pairs={{0,1},{4,5},{8,9},{12,13},{16,17},{20,21},{24,25},{28,29}} | collective-permute-start | bytes 1474568 | tf_op jit(solution)/shard_map/ppermute | solution.py:44
  37.2 12.6 %collective-permute-start.4 = (bf16[96,2560]{1,0:T(8,128)(2,1)}, bf16[96,2560]{1,0:T(8,128)(2,1)S(1)}, u32[]{:S(2)}, u32[]{:S(2)}) collective-permute-start(bf16[96,2560]{1,0:T(8,128)(2,1)} %get-tuple-element.207), channel_id=1, source_target_pairs={{3,2},{7,6},{11,10},{15,14},{19,18},{23,22},{27,26},{31,30}} | collective-permute-start | bytes 1474568 | tf_op jit(solution)/shard_map/ppermute | solution.py:44
  46.2 14.3 %collective-permute-start.26 = (bf16[96,2560]{1,0:T(8,128)(2,1)}, bf16[96,2560]{1,0:T(8,128)(2,1)}, u32[]{:S(2)}, u32[]{:S(2)}) collective-permute-start(bf16[96,2560]{1,0:T(8,128)(2,1)} %get-tuple-element.222), channel_id=1, source_target_pairs={{0,1},{4,5},{8,9},{12,13},{16,17},{20,21},{24,25},{28,29}} | collective-permute-start | bytes 1474568 | tf_op jit(solution)/shard_map/ppermute | solution.py:44
  48.3 12.2 %collective-permute-start.27 = (bf16[96,2560]{1,0:T(8,128)(2,1)}, bf16[96,2560]{1,0:T(8,128)(2,1)}, u32[]{:S(2)}, u32[]{:S(2)}) collective-permute-start(bf16[96,2560]{1,0:T(8,128)(2,1)} %get-tuple-element.223), channel_id=1, source_target_pairs={{3,2},{7,6},{11,10},{15,14},{19,18},{23,22},{27,26},{31,30}} | collective-permute-start | bytes 1474568 | tf_op jit(solution)/shard_map/ppermute | solution.py:44
  51.4 19.6 %collective-permute-start.5 = (bf16[96,2560]{1,0:T(8,128)(2,1)}, bf16[96,2560]{1,0:T(8,128)(2,1)S(1)}, u32[]{:S(2)}, u32[]{:S(2)}) collective-permute-start(bf16[96,2560]{1,0:T(8,128)(2,1)} %get-tuple-element.209), channel_id=1, source_target_pairs={{0,1},{1,2},{4,5},{5,6},{8,9},{9,10},{12,13},{13,14},{16,17},{17,1... | collective-permute-start | bytes 1474568 | tf_op jit(solution)/shard_map/ppermute | solution.py:44
  52.9 18.1 %collective-permute-start.6 = (bf16[96,2560]{1,0:T(8,128)(2,1)}, bf16[96,2560]{1,0:T(8,128)(2,1)S(1)}, u32[]{:S(2)}, u32[]{:S(2)}) collective-permute-start(bf16[96,2560]{1,0:T(8,128)(2,1)} %get-tuple-element.210), channel_id=1, source_target_pairs={{2,1},{3,2},{6,5},{7,6},{10,9},{11,10},{14,13},{15,14},{18,17},{19... | collective-permute-start | bytes 1474568 | tf_op jit(solution)/shard_map/ppermute | solution.py:44
  54.5 44.2 %all-to-all-start.4 = ((bf16[4,96,640]{2,1,0:T(8,128)(2,1)}), bf16[4,96,640]{2,1,0:T(8,128)(2,1)S(1)}, u32[]{:S(2)}, u32[]{:S(2)}) async-start(bf16[4,96,640]{2,1,0:T(8,128)(2,1)} %cut_heads.5), calls=%async_computation.4 | async-start | bytes 983040 | tf_op jit(solution)/shard_map/all_to_all | solution.py:388
  64.8 23.7 %collective-permute-start.28 = (bf16[96,2560]{1,0:T(8,128)(2,1)}, bf16[96,2560]{1,0:T(8,128)(2,1)}, u32[]{:S(2)}, u32[]{:S(2)}) collective-permute-start(bf16[96,2560]{1,0:T(8,128)(2,1)} %get-tuple-element.225), channel_id=1, source_target_pairs={{0,1},{1,2},{4,5},{5,6},{8,9},{9,10},{12,13},{13,14},{16,17},{17,1... | collective-permute-start | bytes 1474568 | tf_op jit(solution)/shard_map/ppermute | solution.py:44
  69.5 19.0 %collective-permute-start.29 = (bf16[96,2560]{1,0:T(8,128)(2,1)}, bf16[96,2560]{1,0:T(8,128)(2,1)}, u32[]{:S(2)}, u32[]{:S(2)}) collective-permute-start(bf16[96,2560]{1,0:T(8,128)(2,1)} %get-tuple-element.226), channel_id=1, source_target_pairs={{2,1},{3,2},{6,5},{7,6},{10,9},{11,10},{14,13},{15,14},{18,17},{19... | collective-permute-start | bytes 1474568 | tf_op jit(solution)/shard_map/ppermute | solution.py:44
  70.9 17.5 %copy-start.2 = (bf16[4,96,2560]{2,1,0:T(8,128)(2,1)S(1)}, bf16[4,96,2560]{2,1,0:T(8,128)(2,1)}, u32[]{:S(2)}) copy-start(bf16[4,96,2560]{2,1,0:T(8,128)(2,1)} %copy-done) | copy-start | bytes 5898244
  72.6 25.2 %copy-start.13 = (bf16[1,384,2560]{2,1,0:T(8,128)(2,1)S(1)}, bf16[1,384,2560]{2,1,0:T(8,128)(2,1)}, u32[]{:S(2)}) copy-start(bf16[1,384,2560]{2,1,0:T(8,128)(2,1)} %param.16) | copy-start | bytes 5898244
  72.6 31.6 %collective-permute-start.7 = (bf16[96,2560]{1,0:T(8,128)(2,1)}, bf16[96,2560]{1,0:T(8,128)(2,1)S(1)}, u32[]{:S(2)}, u32[]{:S(2)}) collective-permute-start(bf16[96,2560]{1,0:T(8,128)(2,1)} %get-tuple-element.211), channel_id=1, source_target_pairs={{0,1},{1,2},{2,3},{4,5},{5,6},{6,7},{8,9},{9,10},{10,11},{12,13},{... | collective-permute-start | bytes 1474568 | tf_op jit(solution)/shard_map/ppermute | solution.py:44
  76.1 28.1 %copy-start.46 = (f32[2560]{0:T(1024)S(1)}, f32[2560]{0:T(1024)}, u32[]{:S(2)}) copy-start(f32[2560]{0:T(1024)} %param.19) | copy-start | bytes 30724
  76.1 28.1 %collective-permute-start.8 = (bf16[96,2560]{1,0:T(8,128)(2,1)}, bf16[96,2560]{1,0:T(8,128)(2,1)}, u32[]{:S(2)}, u32[]{:S(2)}) collective-permute-start(bf16[96,2560]{1,0:T(8,128)(2,1)} %get-tuple-element.212), channel_id=1, source_target_pairs={{1,0},{2,1},{3,2},{5,4},{6,5},{7,6},{9,8},{10,9},{11,10},{13,12},{... | collective-permute-start | bytes 1474568 | tf_op jit(solution)/shard_map/ppermute | solution.py:44
  91.2 24.7 %collective-permute-start.30 = (bf16[96,2560]{1,0:T(8,128)(2,1)}, bf16[96,2560]{1,0:T(8,128)(2,1)}, u32[]{:S(2)}, u32[]{:S(2)}) collective-permute-start(bf16[96,2560]{1,0:T(8,128)(2,1)} %get-tuple-element.227), channel_id=1, source_target_pairs={{0,1},{1,2},{2,3},{4,5},{5,6},{6,7},{8,9},{9,10},{10,11},{12,13},{... | collective-permute-start | bytes 1474568 | tf_op jit(solution)/shard_map/ppermute | solution.py:44
  96.5 19.4 %collective-permute-start.31 = (bf16[96,2560]{1,0:T(8,128)(2,1)}, bf16[96,2560]{1,0:T(8,128)(2,1)}, u32[]{:S(2)}, u32[]{:S(2)}) collective-permute-start(bf16[96,2560]{1,0:T(8,128)(2,1)} %get-tuple-element.228), channel_id=1, source_target_pairs={{1,0},{2,1},{3,2},{5,4},{6,5},{7,6},{9,8},{10,9},{11,10},{13,12},{... | collective-permute-start | bytes 1474568 | tf_op jit(solution)/shard_map/ppermute | solution.py:44
  98.7 43.7 %all-to-all-start.6 = ((bf16[4,96,640]{2,1,0:T(8,128)(2,1)}), bf16[4,96,640]{2,1,0:T(8,128)(2,1)}, u32[]{:S(2)}, u32[]{:S(2)}) async-start(bf16[4,96,640]{2,1,0:T(8,128)(2,1)} %cut_heads.7), calls=%async_computation.6 | async-start | bytes 983040 | tf_op jit(solution)/shard_map/all_to_all | solution.py:388
  109.1 22.0 %collective-permute-start.10 = (bf16[96,2560]{1,0:T(8,128)(2,1)S(1)}, bf16[96,2560]{1,0:T(8,128)(2,1)S(1)}, u32[]{:S(2)}, u32[]{:S(2)}) collective-permute-start(bf16[96,2560]{1,0:T(8,128)(2,1)S(1)} %unit_gradient.4.refs_0_), channel_id=1, source_target_pairs={{1,0},{2,1},{3,2},{5,4},{6,5},{7,6},{9,8},{10,9},{11,10},{13,12},{... | collective-permute-start | bytes 1474568 | tf_op jit(solution)/shard_map/ppermute | solution.py:44
  110.6 20.6 %collective-permute-start.9 = (bf16[96,2560]{1,0:T(8,128)(2,1)S(1)}, bf16[96,2560]{1,0:T(8,128)(2,1)}, u32[]{:S(2)}, u32[]{:S(2)}) collective-permute-start(bf16[96,2560]{1,0:T(8,128)(2,1)S(1)} %unit_gradient.4.refs_0_), channel_id=1, source_target_pairs={{0,1},{1,2},{2,3},{4,5},{5,6},{6,7},{8,9},{9,10},{10,11},{12,13},{... | collective-permute-start | bytes 1474568 | tf_op jit(solution)/shard_map/ppermute | solution.py:44
  118.3 28.4 %collective-permute-start.33 = (bf16[96,2560]{1,0:T(8,128)(2,1)}, bf16[96,2560]{1,0:T(8,128)(2,1)}, u32[]{:S(2)}, u32[]{:S(2)}) collective-permute-start(bf16[96,2560]{1,0:T(8,128)(2,1)} %unit_gradient.6.refs_7_), channel_id=1, source_target_pairs={{1,0},{2,1},{3,2},{5,4},{6,5},{7,6},{9,8},{10,9},{11,10},{13,12},{... | collective-permute-start | bytes 1474568 | tf_op jit(solution)/shard_map/ppermute | solution.py:44
  119.6 27.1 %collective-permute-start.32 = (bf16[96,2560]{1,0:T(8,128)(2,1)}, bf16[96,2560]{1,0:T(8,128)(2,1)}, u32[]{:S(2)}, u32[]{:S(2)}) collective-permute-start(bf16[96,2560]{1,0:T(8,128)(2,1)} %unit_gradient.6.refs_7_), channel_id=1, source_target_pairs={{0,1},{1,2},{2,3},{4,5},{5,6},{6,7},{8,9},{9,10},{10,11},{12,13},{... | collective-permute-start | bytes 1474568 | tf_op jit(solution)/shard_map/ppermute | solution.py:44
  133.7 21.4 %collective-permute-start.11 = (bf16[96,2560]{1,0:T(8,128)(2,1)}, bf16[96,2560]{1,0:T(8,128)(2,1)}, u32[]{:S(2)}, u32[]{:S(2)}) collective-permute-start(bf16[96,2560]{1,0:T(8,128)(2,1)} %get-tuple-element.216), channel_id=1, source_target_pairs={{0,1},{1,2},{2,3},{4,5},{5,6},{6,7},{8,9},{9,10},{10,11},{12,13},{... | collective-permute-start | bytes 1474568 | tf_op jit(solution)/shard_map/ppermute | solution.py:44
  141.1 14.9 %collective-permute-start.12 = (bf16[96,2560]{1,0:T(8,128)(2,1)}, bf16[96,2560]{1,0:T(8,128)(2,1)}, u32[]{:S(2)}, u32[]{:S(2)}) collective-permute-start(bf16[96,2560]{1,0:T(8,128)(2,1)} %get-tuple-element.217), channel_id=1, source_target_pairs={{1,0},{2,1},{3,2},{5,4},{6,5},{7,6},{9,8},{10,9},{11,10},{13,12},{... | collective-permute-start | bytes 1474568 | tf_op jit(solution)/shard_map/ppermute | solution.py:44
  149.2 15.6 %collective-permute-start.34 = (bf16[96,2560]{1,0:T(8,128)(2,1)S(1)}, bf16[96,2560]{1,0:T(8,128)(2,1)S(1)}, u32[]{:S(2)}, u32[]{:S(2)}) collective-permute-start(bf16[96,2560]{1,0:T(8,128)(2,1)S(1)} %get-tuple-element.232), channel_id=1, source_target_pairs={{0,1},{1,2},{2,3},{4,5},{5,6},{6,7},{8,9},{9,10},{10,11},{12,13},{... | collective-permute-start | bytes 1474568 | tf_op jit(solution)/shard_map/ppermute | solution.py:44
  153.8 16.1 %collective-permute-start.35 = (bf16[96,2560]{1,0:T(8,128)(2,1)S(1)}, bf16[96,2560]{1,0:T(8,128)(2,1)S(1)}, u32[]{:S(2)}, u32[]{:S(2)}) collective-permute-start(bf16[96,2560]{1,0:T(8,128)(2,1)S(1)} %get-tuple-element.233), channel_id=1, source_target_pairs={{1,0},{2,1},{3,2},{5,4},{6,5},{7,6},{9,8},{10,9},{11,10},{13,12},{... | collective-permute-start | bytes 1474568 | tf_op jit(solution)/shard_map/ppermute | solution.py:44
  158.4 17.0 %collective-permute-start.13 = (bf16[96,2560]{1,0:T(8,128)(2,1)S(1)}, bf16[96,2560]{1,0:T(8,128)(2,1)S(1)}, u32[]{:S(2)}, u32[]{:S(2)}) collective-permute-start(bf16[96,2560]{1,0:T(8,128)(2,1)S(1)} %get-tuple-element.218), channel_id=1, source_target_pairs={{0,1},{1,2},{2,3},{4,5},{5,6},{6,7},{8,9},{9,10},{10,11},{12,13},{... | collective-permute-start | bytes 1474568 | tf_op jit(solution)/shard_map/ppermute | solution.py:44
  162.2 18.2 %collective-permute-start.14 = (bf16[96,2560]{1,0:T(8,128)(2,1)S(1)}, bf16[96,2560]{1,0:T(8,128)(2,1)S(1)}, u32[]{:S(2)}, u32[]{:S(2)}) collective-permute-start(bf16[96,2560]{1,0:T(8,128)(2,1)S(1)} %get-tuple-element.219), channel_id=1, source_target_pairs={{1,0},{2,1},{3,2},{5,4},{6,5},{7,6},{9,8},{10,9},{11,10},{13,12},{... | collective-permute-start | bytes 1474568 | tf_op jit(solution)/shard_map/ppermute | solution.py:44
  164.8 30.8 %copy-start.16 = (bf16[96,2560]{1,0:T(8,128)(2,1)}, bf16[96,2560]{1,0:T(8,128)(2,1)S(1)}, u32[]{:S(2)}) copy-start(bf16[96,2560]{1,0:T(8,128)(2,1)S(1)} %collective-permute-done.34.right_ref.refs_9_) | copy-start | bytes 1474564
  169.8 25.8 %copy-start.18 = (bf16[96,2560]{1,0:T(8,128)(2,1)}, bf16[96,2560]{1,0:T(8,128)(2,1)S(1)}, u32[]{:S(2)}) copy-start(bf16[96,2560]{1,0:T(8,128)(2,1)S(1)} %collective-permute-done.35.left_ref.refs_12_) | copy-start | bytes 1474564
  169.8 25.8 %slice-start = ((s8[6553600]{0:T(1024)(128)(4,1)}), s8[4194304]{0:T(1024)(128)(4,1)S(1)}, s32[]{:S(2)}) async-start(s8[6553600]{0:T(1024)(128)(4,1)} %bitcast.43), calls=%async_computation.7 | async-start | bytes 8388608
  171.2 14.7 %collective-permute-start.36 = (bf16[96,2560]{1,0:T(8,128)(2,1)S(1)}, bf16[96,2560]{1,0:T(8,128)(2,1)S(1)}, u32[]{:S(2)}, u32[]{:S(2)}) collective-permute-start(bf16[96,2560]{1,0:T(8,128)(2,1)S(1)} %get-tuple-element.234), channel_id=1, source_target_pairs={{0,1},{1,2},{2,3},{4,5},{5,6},{6,7},{8,9},{9,10},{10,11},{12,13},{... | collective-permute-start | bytes 1474568 | tf_op jit(solution)/shard_map/ppermute | solution.py:44
  173.2 22.5 %slice-start.1 = ((s8[6553600]{0:T(1024)(128)(4,1)}), s8[2359296]{0:T(1024)(128)(4,1)S(1)}, s32[]{:S(2)}) async-start(s8[6553600]{0:T(1024)(128)(4,1)} %bitcast.43), calls=%async_computation.8 | async-start | bytes 4718592
  173.2 17.7 %collective-permute-start.37 = (bf16[96,2560]{1,0:T(8,128)(2,1)S(1)}, bf16[96,2560]{1,0:T(8,128)(2,1)S(1)}, u32[]{:S(2)}, u32[]{:S(2)}) collective-permute-start(bf16[96,2560]{1,0:T(8,128)(2,1)S(1)} %get-tuple-element.235), channel_id=1, source_target_pairs={{1,0},{2,1},{3,2},{5,4},{6,5},{7,6},{9,8},{10,9},{11,10},{13,12},{... | collective-permute-start | bytes 1474568 | tf_op jit(solution)/shard_map/ppermute | solution.py:44
  175.4 20.3 %copy-start.20 = (bf16[96,2560]{1,0:T(8,128)(2,1)}, bf16[96,2560]{1,0:T(8,128)(2,1)S(1)}, u32[]{:S(2)}) copy-start(bf16[96,2560]{1,0:T(8,128)(2,1)S(1)} %collective-permute-done.13.right_ref.refs_3_) | copy-start | bytes 1474564
  180.4 15.3 %copy-start.22 = (bf16[96,2560]{1,0:T(8,128)(2,1)}, bf16[96,2560]{1,0:T(8,128)(2,1)S(1)}, u32[]{:S(2)}) copy-start(bf16[96,2560]{1,0:T(8,128)(2,1)S(1)} %collective-permute-done.14.left_ref.refs_6_) | copy-start | bytes 1474564
  181.7 14.0 %copy-start.32 = (bf16[4,96,640]{2,1,0:T(8,128)(2,1)S(1)}, bf16[4,96,640]{2,1,0:T(8,128)(2,1)}, u32[]{:S(2)}) copy-start(bf16[4,96,640]{2,1,0:T(8,128)(2,1)} %copy-done.31) | copy-start | bytes 1474564
  181.7 14.0 %copy-start.34 = (bf16[4,96,640]{2,1,0:T(8,128)(2,1)S(1)}, bf16[4,96,640]{2,1,0:T(8,128)(2,1)}, u32[]{:S(2)}) copy-start(bf16[4,96,640]{2,1,0:T(8,128)(2,1)} %copy-done.33) | copy-start | bytes 1474564
  181.7 21.5 %collective-permute-start.15 = (bf16[96,2560]{1,0:T(8,128)(2,1)S(1)}, bf16[96,2560]{1,0:T(8,128)(2,1)S(1)}, u32[]{:S(2)}, u32[]{:S(2)}) collective-permute-start(bf16[96,2560]{1,0:T(8,128)(2,1)S(1)} %get-tuple-element.220), channel_id=1, source_target_pairs={{0,1},{1,2},{2,3},{4,5},{5,6},{6,7},{8,9},{9,10},{10,11},{12,13},{... | collective-permute-start | bytes 1474568 | tf_op jit(solution)/shard_map/ppermute | solution.py:44
  183.8 19.4 %collective-permute-start.16 = (bf16[96,2560]{1,0:T(8,128)(2,1)S(1)}, bf16[96,2560]{1,0:T(8,128)(2,1)S(1)}, u32[]{:S(2)}, u32[]{:S(2)}) collective-permute-start(bf16[96,2560]{1,0:T(8,128)(2,1)S(1)} %get-tuple-element.221), channel_id=1, source_target_pairs={{1,0},{2,1},{3,2},{5,4},{6,5},{7,6},{9,8},{10,9},{11,10},{13,12},{... | collective-permute-start | bytes 1474568 | tf_op jit(solution)/shard_map/ppermute | solution.py:44
  185.9 17.2 %copy-start.24 = (bf16[96,2560]{1,0:T(8,128)(2,1)}, bf16[96,2560]{1,0:T(8,128)(2,1)S(1)}, u32[]{:S(2)}) copy-start(bf16[96,2560]{1,0:T(8,128)(2,1)S(1)} %collective-permute-done.36.right_ref.refs_10_) | copy-start | bytes 1474564
  192.2 20.2 %collective-permute-start.38 = (bf16[96,2560]{1,0:T(8,128)(2,1)S(1)}, bf16[96,2560]{1,0:T(8,128)(2,1)S(1)}, u32[]{:S(2)}, u32[]{:S(2)}) collective-permute-start(bf16[96,2560]{1,0:T(8,128)(2,1)S(1)} %get-tuple-element.236), channel_id=1, source_target_pairs={{0,1},{1,2},{2,3},{4,5},{5,6},{6,7},{8,9},{9,10},{10,11},{12,13},{... | collective-permute-start | bytes 1474568 | tf_op jit(solution)/shard_map/ppermute | solution.py:44
  194.1 18.3 %collective-permute-start.39 = (bf16[96,2560]{1,0:T(8,128)(2,1)S(1)}, bf16[96,2560]{1,0:T(8,128)(2,1)S(1)}, u32[]{:S(2)}, u32[]{:S(2)}) collective-permute-start(bf16[96,2560]{1,0:T(8,128)(2,1)S(1)} %get-tuple-element.237), channel_id=1, source_target_pairs={{1,0},{2,1},{3,2},{5,4},{6,5},{7,6},{9,8},{10,9},{11,10},{13,12},{... | collective-permute-start | bytes 1474568 | tf_op jit(solution)/shard_map/ppermute | solution.py:44
  206.0 16.7 %collective-permute-start.20 = (bf16[96,2560]{1,0:T(8,128)(2,1)S(1)}, bf16[96,2560]{1,0:T(8,128)(2,1)}, u32[]{:S(2)}, u32[]{:S(2)}) collective-permute-start(bf16[96,2560]{1,0:T(8,128)(2,1)S(1)} %unit_gradient.5.refs_0_), channel_id=1, source_target_pairs={{1,0},{2,1},{3,2},{5,4},{6,5},{7,6},{9,8},{10,9},{11,10},{13,12},{... | collective-permute-start | bytes 1474568 | tf_op jit(solution)/shard_map/ppermute | solution.py:44
  207.3 16.7 %collective-permute-start.17 = (bf16[96,2560]{1,0:T(8,128)(2,1)S(1)}, bf16[96,2560]{1,0:T(8,128)(2,1)S(1)}, u32[]{:S(2)}, u32[]{:S(2)}) collective-permute-start(bf16[96,2560]{1,0:T(8,128)(2,1)S(1)} %unit_gradient.5.refs_0_), channel_id=1, source_target_pairs={{0,1},{1,2},{2,3},{4,5},{5,6},{6,7},{8,9},{9,10},{10,11},{12,13},{... | collective-permute-start | bytes 1474568 | tf_op jit(solution)/shard_map/ppermute | solution.py:44
  212.4 60.9 %slice-start.2 = ((s8[6553600]{0:T(1024)(128)(4,1)}), s8[2359296]{0:T(1024)(128)(4,1)S(1)}, s32[]{:S(2)}) async-start(s8[6553600]{0:T(1024)(128)(4,1)} %bitcast.46), calls=%async_computation.9 | async-start | bytes 4718592
  213.8 19.3 %collective-permute-start.43 = (bf16[96,2560]{1,0:T(8,128)(2,1)}, bf16[96,2560]{1,0:T(8,128)(2,1)S(1)}, u32[]{:S(2)}, u32[]{:S(2)}) collective-permute-start(bf16[96,2560]{1,0:T(8,128)(2,1)} %unit_gradient.7.refs_7_), channel_id=1, source_target_pairs={{1,0},{2,1},{3,2},{5,4},{6,5},{7,6},{9,8},{10,9},{11,10},{13,12},{... | collective-permute-start | bytes 1474568 | tf_op jit(solution)/shard_map/ppermute | solution.py:44
  215.1 19.3 %collective-permute-start.40 = (bf16[96,2560]{1,0:T(8,128)(2,1)}, bf16[96,2560]{1,0:T(8,128)(2,1)S(1)}, u32[]{:S(2)}, u32[]{:S(2)}) collective-permute-start(bf16[96,2560]{1,0:T(8,128)(2,1)} %unit_gradient.7.refs_7_), channel_id=1, source_target_pairs={{0,1},{1,2},{2,3},{4,5},{5,6},{6,7},{8,9},{9,10},{10,11},{12,13},{... | collective-permute-start | bytes 1474568 | tf_op jit(solution)/shard_map/ppermute | solution.py:44
  222.7 21.1 %collective-permute-start.21 = (bf16[96,2560]{1,0:T(8,128)(2,1)}, bf16[96,2560]{1,0:T(8,128)(2,1)}, u32[]{:S(2)}, u32[]{:S(2)}) collective-permute-start(bf16[96,2560]{1,0:T(8,128)(2,1)} %collective-permute-done.20.refs_4_), channel_id=1, source_target_pairs={{1,0},{2,1},{5,4},{6,5},{9,8},{10,9},{13,12},{14,13},{17,16},{18,1... | collective-permute-start | bytes 1474568 | tf_op jit(solution)/shard_map/ppermute | solution.py:44
  224.8 20.3 %collective-permute-start.18 = (bf16[96,2560]{1,0:T(8,128)(2,1)S(1)}, bf16[96,2560]{1,0:T(8,128)(2,1)}, u32[]{:S(2)}, u32[]{:S(2)}) collective-permute-start(bf16[96,2560]{1,0:T(8,128)(2,1)S(1)} %collective-permute-done.17.refs_1_), channel_id=1, source_target_pairs={{1,2},{2,3},{5,6},{6,7},{9,10},{10,11},{13,14},{14,15},{17,18},{18... | collective-permute-start | bytes 1474568 | tf_op jit(solution)/shard_map/ppermute | solution.py:44
  233.1 21.2 %collective-permute-start.44 = (bf16[96,2560]{1,0:T(8,128)(2,1)S(1)}, bf16[96,2560]{1,0:T(8,128)(2,1)}, u32[]{:S(2)}, u32[]{:S(2)}) collective-permute-start(bf16[96,2560]{1,0:T(8,128)(2,1)S(1)} %collective-permute-done.43.refs_11_), channel_id=1, source_target_pairs={{1,0},{2,1},{5,4},{6,5},{9,8},{10,9},{13,12},{14,13},{17,16},{18,1... | collective-permute-start | bytes 1474568 | tf_op jit(solution)/shard_map/ppermute | solution.py:44
  234.4 19.9 %copy-start.43 = (bf16[96,2560]{1,0:T(8,128)(2,1)}, bf16[96,2560]{1,0:T(8,128)(2,1)S(1)}, u32[]{:S(2)}) copy-start(bf16[96,2560]{1,0:T(8,128)(2,1)S(1)} %collective-permute-done.40.refs_8_) | copy-start | bytes 1474564
  234.4 21.2 %collective-permute-start.41 = (bf16[96,2560]{1,0:T(8,128)(2,1)S(1)}, bf16[96,2560]{1,0:T(8,128)(2,1)}, u32[]{:S(2)}, u32[]{:S(2)}) collective-permute-start(bf16[96,2560]{1,0:T(8,128)(2,1)S(1)} %collective-permute-done.40.refs_8_), channel_id=1, source_target_pairs={{1,2},{2,3},{5,6},{6,7},{9,10},{10,11},{13,14},{14,15},{17,18},{18... | collective-permute-start | bytes 1474568 | tf_op jit(solution)/shard_map/ppermute | solution.py:44
  243.8 29.5 %collective-permute-start.22 = (bf16[96,2560]{1,0:T(8,128)(2,1)}, bf16[96,2560]{1,0:T(8,128)(2,1)}, u32[]{:S(2)}, u32[]{:S(2)}) collective-permute-start(bf16[96,2560]{1,0:T(8,128)(2,1)} %collective-permute-done.21.refs_5_), channel_id=1, source_target_pairs={{1,0},{5,4},{9,8},{13,12},{17,16},{21,20},{25,24},{29,28}} | collective-permute-start | bytes 1474568 | tf_op jit(solution)/shard_map/ppermute | solution.py:44
  245.1 28.2 %collective-permute-start.19 = (bf16[96,2560]{1,0:T(8,128)(2,1)}, bf16[96,2560]{1,0:T(8,128)(2,1)}, u32[]{:S(2)}, u32[]{:S(2)}) collective-permute-start(bf16[96,2560]{1,0:T(8,128)(2,1)} %collective-permute-done.18.refs_2_), channel_id=1, source_target_pairs={{2,3},{6,7},{10,11},{14,15},{18,19},{22,23},{26,27},{30,31}} | collective-permute-start | bytes 1474568 | tf_op jit(solution)/shard_map/ppermute | solution.py:44
  254.3 19.0 %collective-permute-start.45 = (bf16[96,2560]{1,0:T(8,128)(2,1)}, bf16[96,2560]{1,0:T(8,128)(2,1)}, u32[]{:S(2)}, u32[]{:S(2)}) collective-permute-start(bf16[96,2560]{1,0:T(8,128)(2,1)} %collective-permute-done.44.refs_12_), channel_id=1, source_target_pairs={{1,0},{5,4},{9,8},{13,12},{17,16},{21,20},{25,24},{29,28}} | collective-permute-start | bytes 1474568 | tf_op jit(solution)/shard_map/ppermute | solution.py:44
  255.6 17.7 %collective-permute-start.42 = (bf16[96,2560]{1,0:T(8,128)(2,1)}, bf16[96,2560]{1,0:T(8,128)(2,1)}, u32[]{:S(2)}, u32[]{:S(2)}) collective-permute-start(bf16[96,2560]{1,0:T(8,128)(2,1)} %collective-permute-done.41.refs_9_), channel_id=1, source_target_pairs={{2,3},{6,7},{10,11},{14,15},{18,19},{22,23},{26,27},{30,31}} | collective-permute-start | bytes 1474568 | tf_op jit(solution)/shard_map/ppermute | solution.py:44
  283.9 60.3 %collective-permute-start.2 = (bf16[640,2560]{1,0:T(8,128)(2,1)S(1)}, bf16[640,2560]{1,0:T(8,128)(2,1)}, u32[]{:S(2)}, u32[]{:S(2)}) collective-permute-start(bf16[640,2560]{1,0:T(8,128)(2,1)S(1)} %get-tuple-element.145), channel_id=1, source_target_pairs={{0,16},{4,20},{8,24},{12,28},{16,0},{20,4},{24,8},{28,12},{1,17},{... | collective-permute-start | bytes 9830408 | tf_op jit(solution)/shard_map/cond/branch_2_fun/ppermute | solution.py:393
  (36 other events, 197.1 us)

commit v2 on v1

--- a/solution.py
+++ b/solution.py
@@ -75,13 +75,35 @@
     )[0]
 
 
+def scaled_weights(numer, weight_one, scaling, token):
+    rows, width = numer.shape
+    step = rows // 4
+
+    def body(numer_ref, one_ref, *refs):
+        out_ref, token_out = refs[-2:]
+        out_ref[...] = (numer_ref[...] / one_ref[...] * scaling).astype(jnp.bfloat16)
+        token_out[...] = jnp.zeros((8, 128), jnp.float32)
+
+    block = (step, width), lambda i: (i, 0)
+    return call(
+        body,
+        "scaled_weights",
+        (rows // step,),
+        [(numer,) + block, (weight_one.reshape(1, 1), (1, 1), fixed(0, 0)), token_in(token)],
+        [((rows, width), jnp.bfloat16) + block, TOKEN_OUT],
+        flops=2 * rows * width,
+        moved=6 * rows * width,
+    )[0]
+
+
 def partial_products(mine, weights, token):
-    members, size, rows = mine.shape
+    mine, index, size = mine
+    members, _, rows = mine.shape
     width = weights.shape[1]
     tile = tile_of(width, 1280)
 
     def body(mine_ref, weights_ref, *refs):
-        out_ref, last_ref, first_ref = refs[-3:]
+        out_ref, last_ref, first_ref, token_out = refs[-4:]
         product = jnp.dot(
             mine_ref[...].reshape(members * size, rows),
             weights_ref[...],
@@ -90,6 +112,7 @@
         out_ref[...] = product.reshape(members, size, tile)
         last_ref[...] = product[(members - 1) * size :]
         first_ref[...] = product[:size]
+        token_out[...] = jnp.zeros((8, 128), jnp.float32)
 
     flat = ((size, width), jnp.bfloat16, (size, tile), lambda j: (0, j))
     return call(
@@ -97,7 +120,7 @@
         "partial_products",
         (width // tile,),
         [
-            (mine, (members, size, rows), fixed(0, 0, 0)),
+            (mine, (members, size, rows), fixed(0, index, 0)),
             (weights, (rows, tile), lambda j: (0, j)),
         ]
         + ([] if token is None else [token_in(token)]),
@@ -110,6 +133,7 @@
             ),
             flat,
             flat,
+            TOKEN_OUT,
         ],
         flops=2 * members * size * rows * width,
         moved=2 * (members * size * (rows + width) + rows * width),
@@ -224,7 +248,10 @@
 
 
 def mine_ins(mine):
-    return [(block, block.shape, fixed(0, 0, 0)) for block in mine]
+    return [
+        (array, (array.shape[0], size, array.shape[2]), fixed(0, index, 0))
+        for array, index, size in mine
+    ]
 
 
 def turned_into(scratch, mine_refs, order):
@@ -234,12 +261,12 @@
 
 
 def weight_step(units, mine, order, kept, numer, inbox):
-    members, _, rows = mine[0].shape
+    members, _, rows = mine[0][0].shape
     width = numer.shape[1] if kept is None else kept.shape[1]
     tile = tile_of(width)
     count = len(units) * len(units[0])
     chunks = len(units)
-    total = sum(members * block.shape[1] for block in mine)
+    total = sum(members * size for _, _, size in mine)
 
     def body(s, *refs):
         units_ref, mine_refs = refs[:count], refs[count : count + chunks]
@@ -293,7 +320,8 @@
     total = members * sum(sizes)
 
     def body(s, *refs):
-        weights_ref, grad_ref, acc = refs[count:]
+        weights_ref, grad_ref, token_out, acc = refs[count:]
+        token_out[...] = jnp.zeros((8, 128), jnp.float32)
         j = pl.program_id(0)
         grad = lax.dot_general(
             stack_of(refs[:count], members, s[0]),
@@ -330,14 +358,35 @@
                 jnp.bfloat16,
                 (members, sum(sizes), rows),
                 fixed(0, 0, 0),
-            )
+            ),
+            TOKEN_OUT,
         ],
         scalars=(order,),
         scratch=[pltpu.VMEM((total, rows), jnp.float32)],
         flops=2 * total * rows * width,
         moved=2 * count * sizes[0] * width + 2 * rows * width,
         vmem=20,
-    )[0]
+    )
+
+
+def passed(right, left, token):
+    size, width = right.shape
+    step = 48
+
+    def body(right_ref, left_ref, token_ref, right_out, left_out):
+        right_out[...] = right_ref[...]
+        left_out[...] = left_ref[...]
+
+    here = (step, width), lambda i: (i, 0)
+    flat = ((size, width), right.dtype) + here
+    return call(
+        body,
+        "passed",
+        (size // step,),
+        [(right,) + here, (left,) + here, token_in(token)],
+        [flat, flat],
+        moved=8 * size * width,
+    )
 
 
 def joined_rows(blocks):
@@ -367,7 +416,7 @@
 
 def widened(value):
     rows, width = value.shape
-    step = 160
+    step = rows // 2
 
     def body(value_ref, out_ref):
         out_ref[...] = value_ref[...].astype(jnp.float32)
@@ -393,7 +442,7 @@
     sent = lax.ppermute(
         kept, "rep", [(i, (i + (1 << bit_place)) % length) for i in range(length)]
     )
-    last = grad_rows(units, weights, order)
+    last, _ = grad_rows(units, weights, order)
     back = swapped(jnp.concatenate(grads + [last], axis=1))
     return sent, joined_rows(back)
 
@@ -426,7 +475,9 @@
 
     order = jnp.mod(me - jnp.arange(members, dtype=jnp.int32), members)
     own = me[None]
-    weights = (numer / weight_one * scaling).astype(jnp.bfloat16)
+    weights = scaled_weights(
+        numer, weight_one, scaling, jnp.broadcast_to(outbox_weight[None], (8, 128))
+    )
     everyone = range(members - 1), range(1, members)
 
     def scalars(t):
@@ -452,21 +503,27 @@
     mine = [[None] * count for _ in range(rounds)]
     units = [[None] * count for _ in range(rounds)]
     before = [None] * count
-    hint = [None] * (count - 1) + [jnp.broadcast_to(outbox_weight[None], (8, 128))]
+    hint = [None] * count
     kept = None
     grads = []
 
-    def fetch(e, q, token):
-        piece = cut_heads(heads[0], starts[e][q], STREAMS[q][e], members, token)
-        mine[e][q] = swapped(piece)
-
-    for q in range(count):
-        fetch(0, q, None)
+    def fetch(e, members_of, token):
+        size = STREAMS[members_of[0]][e]
+        piece = cut_heads(
+            heads[0], starts[e][members_of[0]], size * len(members_of), members, token
+        )
+        array = swapped(piece)
+        for index, q in enumerate(members_of):
+            mine[e][q] = (array, index, size)
+
+    fetch(0, [0], None)
     done = None
     for e in range(rounds):
         parts, moving = [None] * count, [None] * count
         for q in range(count):
-            parts[q], last, first = partial_products(mine[e][q], weights, hint[q])
+            parts[q], last, first, token = partial_products(mine[e][q], weights, hint[q])
+            if e == 0 and q + 1 < count:
+                fetch(0, [q + 1], token)
             if e == 0:
                 moving[q] = hops(last, first, range(1), range(members - 1, members))
             else:
@@ -477,8 +534,8 @@
         for t in range(1, members - 1):
             for q in range(count):
                 right, left, token = next_payload(*moving[q], parts[q], scalars(t), False)
-                if t == 1 and e + 1 < rounds:
-                    fetch(e + 1, q, token)
+                if t == 1 and q == 0 and e + 1 < rounds:
+                    fetch(e + 1, list(range(count)), token)
                 hint[q] = token
                 if e == 0:
                     pairs = range(t + 1), range(members - 1 - t, members)
@@ -491,7 +548,8 @@
         if e > 0:
             flat = [[u] + r + l for u, r, l in units[e - 1]]
             kept, done = weight_step(flat, mine[e - 1], order, kept, numer, None)
-            grads.append(grad_rows(flat, weights, order))
+            grad, grad_done = grad_rows(flat, weights, order)
+            grads.append(grad)
         for q in range(count):
             unit = unit_gradient(
                 *moving[q],
@@ -501,12 +559,16 @@
                 cotangent[0],
                 gain[None],
                 starts[e][q],
-                done if q == count - 1 else None,
+                None,
             )
             before[q] = hops(unit, unit, *everyone)
             units[e][q] = (unit, [before[q][0]], [before[q][1]])
     for s in range(1, members - 1):
         for q in range(count):
+            if (s, q) == (1, count - 1):
+                before[q] = passed(*before[q], done)
+            if (s, q) == (2, 0):
+                before[q] = passed(*before[q], grad_done)
             before[q] = hops(*before[q], range(s, members - 1), range(1, members - s))
             units[-1][q][1].append(before[q][0])
             units[-1][q][2].append(before[q][1])

time: 355 us -> 369 us (1.039)
  starting transfers between devices: 125 us -> 136 us
  waiting for transfers between devices: 74.6 us -> 83 us
  blocking collectives: 35.4 us -> 43.2 us
  Pallas kernels: 85.4 us -> 79 us
    ppermute x40, starting transfers between devices: 95.2 us -> 113 us  [hop(): return lax.ppermute(value, 'fsdp', [(i, i + step) for i in pairs])]
    all_to_all x1, blocking collectives: 35.4 us -> 43.2 us  [swapped(): return lax.all_to_all(blocks, 'fsdp', 0, 0, tiled=False)]
    pallas_call x28 -> x30, Pallas kernels: 85.4 us -> 79 us  [call(): pl.pallas_call(body, name=name, out_shape=[jax.ShapeDtypeStruct(shape, ki...]
    all_to_all x4 -> x3, starting transfers between devices: 21.3 us -> 14.9 us  [swapped(): return lax.all_to_all(blocks, 'fsdp', 0, 0, tiled=False)]
    ppermute x40, waiting for transfers between devices: 55.4 us -> 61.3 us  [hop(): return lax.ppermute(value, 'fsdp', [(i, i + step) for i in pairs])]
    unnamed x104 -> x102, local copies, waits for them, and re-layouts: 18.6 us -> 15.6 us
  transfers between devices with their start and end apart: 48 -> 47, of which waited for: 14 -> 19; matrix products, arithmetic and copies ran while one was open for 1% -> 0% of each run, Pallas kernels for 20% -> 16%
where the time goes in v2:
time: 369 us; the launch traced here: 367 us
  starting transfers between devices  136 us (37%)
  waiting for transfers between devices  83 us (22%)
  Pallas kernels  79 us (21%)
  blocking collectives  43.2 us (12%)
  local copies, waits for them, and re-layouts  15.6 us (4%)
  between operations  8.85 us (2%)
    ppermute x40, starting transfers between devices, hop(): return lax.ppermute(value, 'fsdp', [(i, i + step) for i in pairs])  113 us
    pallas_call x30, Pallas kernels, call(): pl.pallas_call(body, name=name, out_shape=[jax.ShapeDtypeStruct(shape, ki...  79 us
    ppermute x40, waiting for transfers between devices, hop(): return lax.ppermute(value, 'fsdp', [(i, i + step) for i in pairs])  61.3 us
    all_to_all x1, blocking collectives, swapped(): return lax.all_to_all(blocks, 'fsdp', 0, 0, tiled=False)  43.2 us
    unnamed x102, local copies, waits for them, and re-layouts  15.6 us
    ppermute x1, waiting for transfers between devices, tail(): lax.ppermute(kept, 'rep', [(i, (i + (1 << bit_place)) % length) for i in...  15.2 us
    all_to_all x3, starting transfers between devices, swapped(): return lax.all_to_all(blocks, 'fsdp', 0, 0, tiled=False)  14.9 us
  transfers between devices with their start and end apart: 47, of which 19 were waited for; matrix products, arithmetic and copies ran while one was open for 0% of the time, Pallas kernels for 16%

profile of v2, /device:TPU:0, one launch (start us, length us, event | category | flops | bytes accessed | tf_op | source)
XLA Modules:
  0.0 367.4 jit_solution(5898557443992897978)
XLA Ops:
  0.7 1.5 copy-done.8
  3.0 6.3 %all-to-all-start.3 = ((bf16[4,96,640]{2,1,0:T(8,128)(2,1)}), bf16[4,96,640]{2,1,0:T(8,128)(2,1)S(1)}, u32[]{:S(2)}, u32[]{:S(2)}) async-start(bf16[4,96,640]{2,1,0:T(8,128)(2,1)} %cut_heads.3), calls=%async_computation.3 | async-start | bytes 983040 | tf_op jit(solution)/shard_map/all_to_all | solution.py:437
  10.8 2.8 collective-permute-start.4
  13.6 2.8 collective-permute-start.3
  20.2 2.9 copy-done.7
  23.1 2.7 scaled_weights.1
  25.8 4.4 %partial_products.4 = (bf16[4,96,2560]{2,1,0:T(8,128)(2,1)S(1)}, bf16[96,2560]{1,0:T(8,128)(2,1)}, bf16[96,2560]{1,0:T(8,128)(2,1)}, f32[8,128]{1,0:T(8,128)S(1)}) custom-call(bf16[4,96,640]{2,1,0:T(8,128)(2,1)S(1)} %all-to-all-done.3.mine_ref.refs_14_, bf16[640,2560]{1,0:T(8,128)(2,1)} %get-tuple-element.216.weights_ref.refs_14_), custom_call_target="tpu_custom_call" | custom-call | flops 1258291200 | bytes 5734400 | tf_op jit(solution)/shard_map/partial_products/pallas_call | solution.py:16
  31.1 5.1 %all-to-all-start.5 = ((bf16[4,96,640]{2,1,0:T(8,128)(2,1)}), bf16[4,96,640]{2,1,0:T(8,128)(2,1)S(1)}, u32[]{:S(2)}, u32[]{:S(2)}) async-start(bf16[4,96,640]{2,1,0:T(8,128)(2,1)} %cut_heads.5), calls=%async_computation.5 | async-start | bytes 983040 | tf_op jit(solution)/shard_map/all_to_all | solution.py:437
  36.2 3.9 %collective-permute-start.6 = (bf16[96,2560]{1,0:T(8,128)(2,1)}, bf16[96,2560]{1,0:T(8,128)(2,1)S(1)}, u32[]{:S(2)}, u32[]{:S(2)}) collective-permute-start(bf16[96,2560]{1,0:T(8,128)(2,1)} %get-tuple-element.217), channel_id=1, source_target_pairs={{0,1},{4,5},{8,9},{12,13},{16,17},{20,21},{24,25},{28,29}} | collective-permute-start | bytes 1474568 | tf_op jit(solution)/shard_map/ppermute | solution.py:44
  40.1 1.5 collective-permute-start.7
  41.6 6.5 %all-to-all-done.5.mine_ref.refs_15_ = bf16[4,96,640]{2,1,0:T(8,128)(2,1)S(1)} async-done(((bf16[4,96,640]{2,1,0:T(8,128)(2,1)}), bf16[4,96,640]{2,1,0:T(8,128)(2,1)S(1)}, u32[]{:S(2)}, u32[]{:S(2)}) %all-to-all-start.5) | async-done | bytes 491552 | tf_op jit(solution)/shard_map/all_to_all | solution.py:437
  48.1 4.4 %partial_products.6 = (bf16[4,96,2560]{2,1,0:T(8,128)(2,1)S(1)}, bf16[96,2560]{1,0:T(8,128)(2,1)}, bf16[96,2560]{1,0:T(8,128)(2,1)}, f32[8,128]{1,0:T(8,128)}) custom-call(bf16[4,96,640]{2,1,0:T(8,128)(2,1)S(1)} %all-to-all-done.5.mine_ref.refs_15_, bf16[640,2560]{1,0:T(8,128)(2,1)} %get-tuple-element.216.weights_ref.refs_14_), custom_call_target="tpu_custom_call" | custom-call | flops 1258291200 | bytes 5734400 | tf_op jit(solution)/shard_map/partial_products/pallas_call | solution.py:16
  53.8 4.2 %collective-permute-start.24 = (bf16[96,2560]{1,0:T(8,128)(2,1)}, bf16[96,2560]{1,0:T(8,128)(2,1)S(1)}, u32[]{:S(2)}, u32[]{:S(2)}) collective-permute-start(bf16[96,2560]{1,0:T(8,128)(2,1)} %get-tuple-element.234), channel_id=1, source_target_pairs={{0,1},{4,5},{8,9},{12,13},{16,17},{20,21},{24,25},{28,29}} | collective-permute-start | bytes 1474568 | tf_op jit(solution)/shard_map/ppermute | solution.py:44
  57.9 1.5 collective-permute-start.25
  59.5 1.9 next_payload.10
  64.1 3.5 all-to-all-start.4
  67.6 4.7 %collective-permute-start.8 = (bf16[96,2560]{1,0:T(8,128)(2,1)}, bf16[96,2560]{1,0:T(8,128)(2,1)}, u32[]{:S(2)}, u32[]{:S(2)}) collective-permute-start(bf16[96,2560]{1,0:T(8,128)(2,1)} %copy-done.20), channel_id=1, source_target_pairs={{0,1},{1,2},{4,5},{5,6},{8,9},{9,10},{12,13},{13,14},{16,17},{17,1... | collective-permute-start | bytes 1474568 | tf_op jit(solution)/shard_map/ppermute | solution.py:44
  73.7 1.5 copy-done.1
  75.3 2.6 next_payload.15
  77.9 3.3 collective-permute-start.26
  81.1 1.4 collective-permute-start.27
  82.7 12.7 %collective-permute-done.8.right_ref = bf16[96,2560]{1,0:T(8,128)(2,1)} collective-permute-done((bf16[96,2560]{1,0:T(8,128)(2,1)}, bf16[96,2560]{1,0:T(8,128)(2,1)}, u32[]{:S(2)}, u32[]{:S(2)}) %collective-permute-start.8) | collective-permute-done | bytes 491552 | tf_op jit(solution)/shard_map/ppermute | solution.py:44
  95.4 2.0 next_payload.11
  97.4 8.5 %collective-permute-start.10 = (bf16[96,2560]{1,0:T(8,128)(2,1)S(1)}, bf16[96,2560]{1,0:T(8,128)(2,1)S(1)}, u32[]{:S(2)}, u32[]{:S(2)}) collective-permute-start(bf16[96,2560]{1,0:T(8,128)(2,1)S(1)} %get-tuple-element.222), channel_id=1, source_target_pairs={{0,1},{1,2},{2,3},{4,5},{5,6},{6,7},{8,9},{9,10},{10,11},{12,13},{... | collective-permute-start | bytes 1474568 | tf_op jit(solution)/shard_map/ppermute | solution.py:44
  106.0 1.6 collective-permute-start.11
  107.6 2.0 next_payload.16
  109.6 6.9 %collective-permute-start.28 = (bf16[96,2560]{1,0:T(8,128)(2,1)S(1)}, bf16[96,2560]{1,0:T(8,128)(2,1)S(1)}, u32[]{:S(2)}, u32[]{:S(2)}) collective-permute-start(bf16[96,2560]{1,0:T(8,128)(2,1)S(1)} %get-tuple-element.239), channel_id=1, source_target_pairs={{0,1},{1,2},{2,3},{4,5},{5,6},{6,7},{8,9},{9,10},{10,11},{12,13},{... | collective-permute-start | bytes 1474568 | tf_op jit(solution)/shard_map/ppermute | solution.py:44
  120.7 7.4 %collective-permute-start.12 = (bf16[96,2560]{1,0:T(8,128)(2,1)S(1)}, bf16[96,2560]{1,0:T(8,128)(2,1)S(1)}, u32[]{:S(2)}, u32[]{:S(2)}) collective-permute-start(bf16[96,2560]{1,0:T(8,128)(2,1)S(1)} %unit_gradient.4.refs_0_), channel_id=1, source_target_pairs={{0,1},{1,2},{2,3},{4,5},{5,6},{6,7},{8,9},{9,10},{10,11},{12,13},{... | collective-permute-start | bytes 1474568 | tf_op jit(solution)/shard_map/ppermute | solution.py:44
  128.0 4.5 %collective-permute-done.29.left_ref = bf16[96,2560]{1,0:T(8,128)(2,1)S(1)} collective-permute-done((bf16[96,2560]{1,0:T(8,128)(2,1)S(1)}, bf16[96,2560]{1,0:T(8,128)(2,1)S(1)}, u32[]{:S(2)}, u32[]{:S(2)}) %collective-permute-start.29) | collective-permute-done | bytes 491552 | tf_op jit(solution)/shard_map/ppermute | solution.py:44
  134.5 5.3 %collective-permute-start.30 = (bf16[96,2560]{1,0:T(8,128)(2,1)S(1)}, bf16[96,2560]{1,0:T(8,128)(2,1)}, u32[]{:S(2)}, u32[]{:S(2)}) collective-permute-start(bf16[96,2560]{1,0:T(8,128)(2,1)S(1)} %unit_gradient.6.refs_7_), channel_id=1, source_target_pairs={{0,1},{1,2},{2,3},{4,5},{5,6},{6,7},{8,9},{9,10},{10,11},{12,13},{... | collective-permute-start | bytes 1474568 | tf_op jit(solution)/shard_map/ppermute | solution.py:44
  139.9 4.2 %partial_products.5 = (bf16[4,96,2560]{2,1,0:T(8,128)(2,1)S(1)}, bf16[96,2560]{1,0:T(8,128)(2,1)}, bf16[96,2560]{1,0:T(8,128)(2,1)}, f32[8,128]{1,0:T(8,128)}) custom-call(bf16[4,192,640]{2,1,0:T(8,128)(2,1)S(1)} %all-to-all-done.4.mine_ref.refs_14_.refs_15_, bf16[640,2560]{1,0:T(8,128)(2,1)} %get-tuple-element.216.weights_ref.refs_14_, ...), custom_call_target="tpu_custom_call" | custom-call | flops 1258291200 | bytes 5734400 | tf_op jit(solution)/shard_map/partial_products/pallas_call | solution.py:16
  145.3 2.7 collective-permute-start.14
  149.4 3.1 partial_products.7
  152.4 2.2 next_payload.17
  154.7 4.6 %collective-permute-start.32 = (bf16[96,2560]{1,0:T(8,128)(2,1)S(1)}, bf16[96,2560]{1,0:T(8,128)(2,1)S(1)}, u32[]{:S(2)}, u32[]{:S(2)}) collective-permute-start(bf16[96,2560]{1,0:T(8,128)(2,1)S(1)} %get-tuple-element.243), channel_id=1, source_target_pairs={{0,1},{1,2},{2,3},{4,5},{5,6},{6,7},{8,9},{9,10},{10,11},{12,13},{... | collective-permute-start | bytes 1474568 | tf_op jit(solution)/shard_map/ppermute | solution.py:44
  162.6 6.3 %collective-permute-start.16 = (bf16[96,2560]{1,0:T(8,128)(2,1)S(1)}, bf16[96,2560]{1,0:T(8,128)(2,1)S(1)}, u32[]{:S(2)}, u32[]{:S(2)}) collective-permute-start(bf16[96,2560]{1,0:T(8,128)(2,1)S(1)} %get-tuple-element.229), channel_id=1, source_target_pairs={{0,1},{1,2},{2,3},{4,5},{5,6},{6,7},{8,9},{9,10},{10,11},{12,13},{... | collective-permute-start | bytes 1474568 | tf_op jit(solution)/shard_map/ppermute | solution.py:44
  170.5 3.0 collective-permute-done.33.left_ref.refs_12_
  174.9 4.5 %collective-permute-start.34 = (bf16[96,2560]{1,0:T(8,128)(2,1)S(1)}, bf16[96,2560]{1,0:T(8,128)(2,1)S(1)}, u32[]{:S(2)}, u32[]{:S(2)}) collective-permute-start(bf16[96,2560]{1,0:T(8,128)(2,1)S(1)} %get-tuple-element.245), channel_id=1, source_target_pairs={{0,1},{1,2},{2,3},{4,5},{5,6},{6,7},{8,9},{9,10},{10,11},{12,13},{... | collective-permute-start | bytes 1474568 | tf_op jit(solution)/shard_map/ppermute | solution.py:44
  181.1 3.0 collective-permute-done.17.left_ref.refs_6_
  185.4 4.5 %collective-permute-start.18 = (bf16[96,2560]{1,0:T(8,128)(2,1)S(1)}, bf16[96,2560]{1,0:T(8,128)(2,1)S(1)}, u32[]{:S(2)}, u32[]{:S(2)}) collective-permute-start(bf16[96,2560]{1,0:T(8,128)(2,1)S(1)} %get-tuple-element.231), channel_id=1, source_target_pairs={{0,1},{1,2},{2,3},{4,5},{5,6},{6,7},{8,9},{9,10},{10,11},{12,13},{... | collective-permute-start | bytes 1474568 | tf_op jit(solution)/shard_map/ppermute | solution.py:44
  190.0 1.6 collective-permute-start.19
  191.6 2.7 collective-permute-done.35.refs_13_.left_ref
  195.7 5.1 %collective-permute-start.38 = (bf16[96,2560]{1,0:T(8,128)(2,1)S(1)}, bf16[96,2560]{1,0:T(8,128)(2,1)S(1)}, u32[]{:S(2)}, u32[]{:S(2)}) collective-permute-start(bf16[96,2560]{1,0:T(8,128)(2,1)S(1)} %get-tuple-element.250), channel_id=1, source_target_pairs={{0,1},{1,2},{2,3},{4,5},{5,6},{6,7},{8,9},{9,10},{10,11},{12,13},{... | collective-permute-start | bytes 1474568 | tf_op jit(solution)/shard_map/ppermute | solution.py:44
  202.2 2.5 collective-permute-done.19.left_ref
  206.9 5.6 %collective-permute-start.20 = (bf16[96,2560]{1,0:T(8,128)(2,1)S(1)}, bf16[96,2560]{1,0:T(8,128)(2,1)S(1)}, u32[]{:S(2)}, u32[]{:S(2)}) collective-permute-start(bf16[96,2560]{1,0:T(8,128)(2,1)S(1)} %unit_gradient.5.refs_0_), channel_id=1, source_target_pairs={{0,1},{1,2},{2,3},{4,5},{5,6},{6,7},{8,9},{9,10},{10,11},{12,13},{... | collective-permute-start | bytes 1474568 | tf_op jit(solution)/shard_map/ppermute | solution.py:44
  212.5 4.5 %collective-permute-done.39.left_ref = bf16[96,2560]{1,0:T(8,128)(2,1)S(1)} collective-permute-done((bf16[96,2560]{1,0:T(8,128)(2,1)S(1)}, bf16[96,2560]{1,0:T(8,128)(2,1)S(1)}, u32[]{:S(2)}, u32[]{:S(2)}) %collective-permute-start.39) | collective-permute-done | bytes 491552 | tf_op jit(solution)/shard_map/ppermute | solution.py:44
  218.9 4.6 %collective-permute-start.40 = (bf16[96,2560]{1,0:T(8,128)(2,1)S(1)}, bf16[96,2560]{1,0:T(8,128)(2,1)S(1)}, u32[]{:S(2)}, u32[]{:S(2)}) collective-permute-start(bf16[96,2560]{1,0:T(8,128)(2,1)S(1)} %unit_gradient.7.refs_7_), channel_id=1, source_target_pairs={{0,1},{1,2},{2,3},{4,5},{5,6},{6,7},{8,9},{9,10},{10,11},{12,13},{... | collective-permute-start | bytes 1474568 | tf_op jit(solution)/shard_map/ppermute | solution.py:44
  223.5 4.0 %collective-permute-done.22.refs_4_ = bf16[96,2560]{1,0:T(8,128)(2,1)S(1)} collective-permute-done((bf16[96,2560]{1,0:T(8,128)(2,1)S(1)}, bf16[96,2560]{1,0:T(8,128)(2,1)S(1)}, u32[]{:S(2)}, u32[]{:S(2)}) %collective-permute-start.22) | collective-permute-done | bytes 491552 | tf_op jit(solution)/shard_map/ppermute | solution.py:44
  229.7 6.8 %weight_step.2 = (f32[640,2560]{1,0:T(8,128)S(1)}, f32[8,128]{1,0:T(8,128)S(1)}) custom-call(s32[4]{0:T(128)S(1)} %and_select_fusion.s, bf16[96,2560]{1,0:T(8,128)(2,1)S(1)} %unit_gradient.4.refs_0_, bf16[96,2560]{1,0:T(8,128)(2,1)S(1)} %collective-permute-done.12.right_ref.refs_1_, bf16[96,2560]{1,0:T(8,128)(2,1)S(1)} %collective-permute-done.14.right_ref.refs_2_, ...), custom_call_target="tpu_custom_call" | custom-call | flops 2516582400 | bytes 26542080 | tf_op jit(solution)/shard_map/weight_step/pallas_call | solution.py:16
  236.6 1.5 collective-permute-done.41.left_ref.refs_11_
  238.2 1.6 collective-permute-start.42
  241.1 8.5 %grad_rows.7 = (bf16[4,192,640]{2,1,0:T(8,128)(2,1)}, f32[8,128]{1,0:T(8,128)S(1)}) custom-call(s32[4]{0:T(128)S(1)} %and_select_fusion.s, bf16[96,2560]{1,0:T(8,128)(2,1)S(1)} %unit_gradient.4.refs_0_, bf16[96,2560]{1,0:T(8,128)(2,1)S(1)} %collective-permute-done.12.right_ref.refs_1_, bf16[96,2560]{1,0:T(8,128)(2,1)S(1)} %collective-permute-done.14.right_ref.refs_2_, ...), custom_call_target="tpu_custom_call" | custom-call | flops 2516582400 | bytes 10158080 | tf_op jit(solution)/shard_map/grad_rows/pallas_call | solution.py:16
  252.4 5.1 %collective-permute-done.44.refs_12_ = bf16[96,2560]{1,0:T(8,128)(2,1)} collective-permute-done((bf16[96,2560]{1,0:T(8,128)(2,1)S(1)}, bf16[96,2560]{1,0:T(8,128)(2,1)}, u32[]{:S(2)}, u32[]{:S(2)}) %collective-permute-start.44) | collective-permute-done | bytes 491552 | tf_op jit(solution)/shard_map/ppermute | solution.py:44
  260.0 9.6 %collective-permute-done.37.refs_6_ = bf16[96,2560]{1,0:T(8,128)(2,1)S(1)} collective-permute-done((bf16[96,2560]{1,0:T(8,128)(2,1)S(1)}, bf16[96,2560]{1,0:T(8,128)(2,1)S(1)}, u32[]{:S(2)}, u32[]{:S(2)}) %collective-permute-start.37) | collective-permute-done | bytes 491552 | tf_op jit(solution)/shard_map/ppermute | solution.py:44
  269.7 5.7 %collective-permute-done.45.refs_13_ = bf16[96,2560]{1,0:T(8,128)(2,1)} collective-permute-done((bf16[96,2560]{1,0:T(8,128)(2,1)}, bf16[96,2560]{1,0:T(8,128)(2,1)}, u32[]{:S(2)}, u32[]{:S(2)}) %collective-permute-start.45) | collective-permute-done | bytes 491552 | tf_op jit(solution)/shard_map/ppermute | solution.py:44
  275.4 2.9 copy-done.11
  278.3 2.9 copy-done.13
  281.3 9.3 %weight_step.3 = (f32[640,2560]{1,0:T(8,128)}, bf16[640,2560]{1,0:T(8,128)(2,1)S(1)}) custom-call(s32[4]{0:T(128)S(1)} %and_select_fusion.s, bf16[96,2560]{1,0:T(8,128)(2,1)} %copy-done.23, bf16[96,2560]{1,0:T(8,128)(2,1)} %copy-done.38, bf16[96,2560]{1,0:T(8,128)(2,1)} %copy-done.33, bf16[96,2560]{1,0:T(8,128)(2,1)} %copy-done.40, ...), custom_call_target="tpu_custom_call" | custom-call | flops 2516582400 | bytes 26542080 | tf_op jit(solution)/shard_map/weight_step/pallas_call | solution.py:16
  290.7 69.3 %conditional.1 = (bf16[640,2560]{1,0:T(8,128)(2,1)}, bf16[1,384,2560]{2,1,0:T(8,128)(2,1)S(1)}) conditional(s32[]{:T(128)} %clamp.3, (bf16[640,2560]{1,0:T(8,128)(2,1)S(1)}, s32[4]{0:T(128)S(1)}, bf16[96,2560]{1,0:T(8,128)(2,1)S(1)}, bf16[96,2560]{1,0:T(8,128)(2,1)S(1)}, bf16[96,2560]{1,0:T(8,128)(2,1)S(1)}, ...), branch_computations={%region_1.2_spmd, %region_2.3_spmd, %region_3.4_spmd} | conditional | flops 2520514560 | bytes 35061816 | solution.py:579
  290.7 2.0 collective-permute-start.1
  292.7 8.3 %grad_rows.5 = (bf16[4,192,640]{2,1,0:T(8,128)(2,1)S(1)}, f32[8,128]{1,0:T(8,128)}) custom-call(s32[4]{0:T(128)S(1)} %get-tuple-element.130.s, bf16[96,2560]{1,0:T(8,128)(2,1)S(1)} %get-tuple-element.131.refs_0_, bf16[96,2560]{1,0:T(8,128)(2,1)S(1)} %get-tuple-element.132.refs_1_, bf16[96,2560]{1,0:T(8,128)(2,1)S(1)} %get-tuple-element.133.refs_2_, ...), custom_call_target="tpu_custom_call" | custom-call | flops 2516582400 | bytes 10158080 | tf_op jit(solution)/shard_map/cond/branch_1_fun/grad_rows/pallas_call | solution.py:16
  301.1 43.2 %all_to_all.28.blocks_ref = bf16[4,384,640]{2,1,0:T(8,128)(2,1)S(1)} all-to-all(bf16[4,384,640]{2,1,0:T(8,128)(2,1)S(1)} %pad_maximum_fusion.1), channel_id=1, replica_groups=mesh['rep'=8,'fsdp'=4] {'fsdp'}, dimensions={0} | all-to-all | bytes 3932160 | tf_op jit(solution)/shard_map/cond/branch_1_fun/all_to_all | solution.py:437
  344.8 15.2 %collective-permute-done.1 = bf16[640,2560]{1,0:T(8,128)(2,1)} collective-permute-done((bf16[640,2560]{1,0:T(8,128)(2,1)S(1)}, bf16[640,2560]{1,0:T(8,128)(2,1)}, u32[]{:S(2)}, u32[]{:S(2)}) %collective-permute-start.1) | collective-permute-done | bytes 3276832 | tf_op jit(solution)/shard_map/cond/branch_1_fun/ppermute | solution.py:442
  360.0 5.1 %widened.1 = f32[640,2560]{1,0:T(8,128)} custom-call(bf16[640,2560]{1,0:T(8,128)(2,1)} %get-tuple-element.259.value_ref), custom_call_target="tpu_custom_call" | custom-call | bytes 9830400 | tf_op jit(solution)/shard_map/widened/pallas_call | solution.py:16
  (173 shorter events, 41.9 us)
Async XLA Ops:
  0.6 15.8 %copy-start.48 = (s32[8]{0:T(128)S(1)}, s32[8]{0:T(128)}, u32[]{:S(2)}) copy-start(s32[8]{0:T(128)} %param.20) | copy-start | bytes 100
  3.0 22.8 %all-to-all-start.3 = ((bf16[4,96,640]{2,1,0:T(8,128)(2,1)}), bf16[4,96,640]{2,1,0:T(8,128)(2,1)S(1)}, u32[]{:S(2)}, u32[]{:S(2)}) async-start(bf16[4,96,640]{2,1,0:T(8,128)(2,1)} %cut_heads.3), calls=%async_computation.3 | async-start | bytes 983040 | tf_op jit(solution)/shard_map/all_to_all | solution.py:437
  10.0 8.3 %collective-permute-start.5 = (f32[1]{0:T(128)}, f32[1]{0:T(128)}, u32[]{:S(2)}, u32[]{:S(2)}) collective-permute-start(f32[1]{0:T(128)} %mul.4), channel_id=1, source_target_pairs={{0,4},{4,8},{8,12},{12,16},{16,20},{20,24},{24,28},{28,0},{1,5},{5... | collective-permute-start | bytes 20 | tf_op jit(solution)/shard_map/ppermute | solution.py:469
  10.8 7.4 %collective-permute-start.4 = (f32[1]{0:T(128)}, f32[1]{0:T(128)}, u32[]{:S(2)}, u32[]{:S(2)}) collective-permute-start(f32[1]{0:T(128)} %mul.4), channel_id=1, source_target_pairs={{0,8},{4,12},{8,16},{12,20},{16,24},{20,28},{24,0},{28,4},{1,9},{5... | collective-permute-start | bytes 20 | tf_op jit(solution)/shard_map/ppermute | solution.py:469
  13.6 5.9 %collective-permute-start.3 = (f32[1]{0:T(128)}, f32[1]{0:T(128)}, u32[]{:S(2)}, u32[]{:S(2)}) collective-permute-start(f32[1]{0:T(128)} %mul.4), channel_id=1, source_target_pairs={{0,16},{4,20},{8,24},{12,28},{16,0},{20,4},{24,8},{28,12},{1,17},{... | collective-permute-start | bytes 20 | tf_op jit(solution)/shard_map/ppermute | solution.py:469
  31.1 17.0 %all-to-all-start.5 = ((bf16[4,96,640]{2,1,0:T(8,128)(2,1)}), bf16[4,96,640]{2,1,0:T(8,128)(2,1)S(1)}, u32[]{:S(2)}, u32[]{:S(2)}) async-start(bf16[4,96,640]{2,1,0:T(8,128)(2,1)} %cut_heads.5), calls=%async_computation.5 | async-start | bytes 983040 | tf_op jit(solution)/shard_map/all_to_all | solution.py:437
  36.2 23.3 %collective-permute-start.6 = (bf16[96,2560]{1,0:T(8,128)(2,1)}, bf16[96,2560]{1,0:T(8,128)(2,1)S(1)}, u32[]{:S(2)}, u32[]{:S(2)}) collective-permute-start(bf16[96,2560]{1,0:T(8,128)(2,1)} %get-tuple-element.217), channel_id=1, source_target_pairs={{0,1},{4,5},{8,9},{12,13},{16,17},{20,21},{24,25},{28,29}} | collective-permute-start | bytes 1474568 | tf_op jit(solution)/shard_map/ppermute | solution.py:44
  40.1 19.3 %collective-permute-start.7 = (bf16[96,2560]{1,0:T(8,128)(2,1)}, bf16[96,2560]{1,0:T(8,128)(2,1)}, u32[]{:S(2)}, u32[]{:S(2)}) collective-permute-start(bf16[96,2560]{1,0:T(8,128)(2,1)} %get-tuple-element.218), channel_id=1, source_target_pairs={{3,2},{7,6},{11,10},{15,14},{19,18},{23,22},{27,26},{31,30}} | collective-permute-start | bytes 1474568 | tf_op jit(solution)/shard_map/ppermute | solution.py:44
  53.8 20.0 %collective-permute-start.24 = (bf16[96,2560]{1,0:T(8,128)(2,1)}, bf16[96,2560]{1,0:T(8,128)(2,1)S(1)}, u32[]{:S(2)}, u32[]{:S(2)}) collective-permute-start(bf16[96,2560]{1,0:T(8,128)(2,1)} %get-tuple-element.234), channel_id=1, source_target_pairs={{0,1},{4,5},{8,9},{12,13},{16,17},{20,21},{24,25},{28,29}} | collective-permute-start | bytes 1474568 | tf_op jit(solution)/shard_map/ppermute | solution.py:44
  57.9 15.8 %collective-permute-start.25 = (bf16[96,2560]{1,0:T(8,128)(2,1)}, bf16[96,2560]{1,0:T(8,128)(2,1)}, u32[]{:S(2)}, u32[]{:S(2)}) collective-permute-start(bf16[96,2560]{1,0:T(8,128)(2,1)} %get-tuple-element.235), channel_id=1, source_target_pairs={{3,2},{7,6},{11,10},{15,14},{19,18},{23,22},{27,26},{31,30}} | collective-permute-start | bytes 1474568 | tf_op jit(solution)/shard_map/ppermute | solution.py:44
  64.1 75.8 %all-to-all-start.4 = ((bf16[4,192,640]{2,1,0:T(8,128)(2,1)}), bf16[4,192,640]{2,1,0:T(8,128)(2,1)S(1)}, u32[]{:S(2)}, u32[]{:S(2)}) async-start(bf16[4,192,640]{2,1,0:T(8,128)(2,1)} %copy-done.14), calls=%async_computation.4 | async-start | bytes 1966080 | tf_op jit(solution)/shard_map/all_to_all | solution.py:437
  67.6 27.8 %collective-permute-start.8 = (bf16[96,2560]{1,0:T(8,128)(2,1)}, bf16[96,2560]{1,0:T(8,128)(2,1)}, u32[]{:S(2)}, u32[]{:S(2)}) collective-permute-start(bf16[96,2560]{1,0:T(8,128)(2,1)} %copy-done.20), channel_id=1, source_target_pairs={{0,1},{1,2},{4,5},{5,6},{8,9},{9,10},{12,13},{13,14},{16,17},{17,1... | collective-permute-start | bytes 1474568 | tf_op jit(solution)/shard_map/ppermute | solution.py:44
  72.3 23.1 %collective-permute-start.9 = (bf16[96,2560]{1,0:T(8,128)(2,1)}, bf16[96,2560]{1,0:T(8,128)(2,1)}, u32[]{:S(2)}, u32[]{:S(2)}) collective-permute-start(bf16[96,2560]{1,0:T(8,128)(2,1)} %copy-done.19), channel_id=1, source_target_pairs={{2,1},{3,2},{6,5},{7,6},{10,9},{11,10},{14,13},{15,14},{18,17},{19... | collective-permute-start | bytes 1474568 | tf_op jit(solution)/shard_map/ppermute | solution.py:44
  77.9 29.7 %collective-permute-start.26 = (bf16[96,2560]{1,0:T(8,128)(2,1)}, bf16[96,2560]{1,0:T(8,128)(2,1)}, u32[]{:S(2)}, u32[]{:S(2)}) collective-permute-start(bf16[96,2560]{1,0:T(8,128)(2,1)} %get-tuple-element.237), channel_id=1, source_target_pairs={{0,1},{1,2},{4,5},{5,6},{8,9},{9,10},{12,13},{13,14},{16,17},{17,1... | collective-permute-start | bytes 1474568 | tf_op jit(solution)/shard_map/ppermute | solution.py:44
  81.1 26.4 %collective-permute-start.27 = (bf16[96,2560]{1,0:T(8,128)(2,1)}, bf16[96,2560]{1,0:T(8,128)(2,1)}, u32[]{:S(2)}, u32[]{:S(2)}) collective-permute-start(bf16[96,2560]{1,0:T(8,128)(2,1)} %get-tuple-element.238), channel_id=1, source_target_pairs={{2,1},{3,2},{6,5},{7,6},{10,9},{11,10},{14,13},{15,14},{18,17},{19... | collective-permute-start | bytes 1474568 | tf_op jit(solution)/shard_map/ppermute | solution.py:44
  82.7 24.9 %copy-start.2 = (bf16[4,96,2560]{2,1,0:T(8,128)(2,1)S(1)}, bf16[4,96,2560]{2,1,0:T(8,128)(2,1)}, u32[]{:S(2)}) copy-start(bf16[4,96,2560]{2,1,0:T(8,128)(2,1)} %copy-done) | copy-start | bytes 5898244
  97.4 20.4 %collective-permute-start.10 = (bf16[96,2560]{1,0:T(8,128)(2,1)S(1)}, bf16[96,2560]{1,0:T(8,128)(2,1)S(1)}, u32[]{:S(2)}, u32[]{:S(2)}) collective-permute-start(bf16[96,2560]{1,0:T(8,128)(2,1)S(1)} %get-tuple-element.222), channel_id=1, source_target_pairs={{0,1},{1,2},{2,3},{4,5},{5,6},{6,7},{8,9},{9,10},{10,11},{12,13},{... | collective-permute-start | bytes 1474568 | tf_op jit(solution)/shard_map/ppermute | solution.py:44
  105.9 11.8 %copy-start.47 = (f32[2560]{0:T(1024)S(1)}, f32[2560]{0:T(1024)}, u32[]{:S(2)}) copy-start(f32[2560]{0:T(1024)} %param.19) | copy-start | bytes 30724
  105.9 12.8 %copy-start.3 = (bf16[1,384,2560]{2,1,0:T(8,128)(2,1)S(1)}, bf16[1,384,2560]{2,1,0:T(8,128)(2,1)}, u32[]{:S(2)}) copy-start(bf16[1,384,2560]{2,1,0:T(8,128)(2,1)} %param.17) | copy-start | bytes 5898244
  106.0 12.8 %copy-start.5 = (bf16[1,384,2560]{2,1,0:T(8,128)(2,1)S(1)}, bf16[1,384,2560]{2,1,0:T(8,128)(2,1)}, u32[]{:S(2)}) copy-start(bf16[1,384,2560]{2,1,0:T(8,128)(2,1)} %param.18) | copy-start | bytes 5898244
  106.0 12.8 %collective-permute-start.11 = (bf16[96,2560]{1,0:T(8,128)(2,1)S(1)}, bf16[96,2560]{1,0:T(8,128)(2,1)S(1)}, u32[]{:S(2)}, u32[]{:S(2)}) collective-permute-start(bf16[96,2560]{1,0:T(8,128)(2,1)S(1)} %get-tuple-element.223), channel_id=1, source_target_pairs={{1,0},{2,1},{3,2},{5,4},{6,5},{7,6},{9,8},{10,9},{11,10},{13,12},{... | collective-permute-start | bytes 1474568 | tf_op jit(solution)/shard_map/ppermute | solution.py:44
  109.6 18.4 %collective-permute-start.28 = (bf16[96,2560]{1,0:T(8,128)(2,1)S(1)}, bf16[96,2560]{1,0:T(8,128)(2,1)S(1)}, u32[]{:S(2)}, u32[]{:S(2)}) collective-permute-start(bf16[96,2560]{1,0:T(8,128)(2,1)S(1)} %get-tuple-element.239), channel_id=1, source_target_pairs={{0,1},{1,2},{2,3},{4,5},{5,6},{6,7},{8,9},{9,10},{10,11},{12,13},{... | collective-permute-start | bytes 1474568 | tf_op jit(solution)/shard_map/ppermute | solution.py:44
  116.5 16.1 %collective-permute-start.29 = (bf16[96,2560]{1,0:T(8,128)(2,1)S(1)}, bf16[96,2560]{1,0:T(8,128)(2,1)S(1)}, u32[]{:S(2)}, u32[]{:S(2)}) collective-permute-start(bf16[96,2560]{1,0:T(8,128)(2,1)S(1)} %get-tuple-element.240), channel_id=1, source_target_pairs={{1,0},{2,1},{3,2},{5,4},{6,5},{7,6},{9,8},{10,9},{11,10},{13,12},{... | collective-permute-start | bytes 1474568 | tf_op jit(solution)/shard_map/ppermute | solution.py:44
  119.4 24.7 %collective-permute-start.13 = (bf16[96,2560]{1,0:T(8,128)(2,1)S(1)}, bf16[96,2560]{1,0:T(8,128)(2,1)S(1)}, u32[]{:S(2)}, u32[]{:S(2)}) collective-permute-start(bf16[96,2560]{1,0:T(8,128)(2,1)S(1)} %unit_gradient.4.refs_0_), channel_id=1, source_target_pairs={{1,0},{2,1},{3,2},{5,4},{6,5},{7,6},{9,8},{10,9},{11,10},{13,12},{... | collective-permute-start | bytes 1474568 | tf_op jit(solution)/shard_map/ppermute | solution.py:44
  120.7 23.4 %collective-permute-start.12 = (bf16[96,2560]{1,0:T(8,128)(2,1)S(1)}, bf16[96,2560]{1,0:T(8,128)(2,1)S(1)}, u32[]{:S(2)}, u32[]{:S(2)}) collective-permute-start(bf16[96,2560]{1,0:T(8,128)(2,1)S(1)} %unit_gradient.4.refs_0_), channel_id=1, source_target_pairs={{0,1},{1,2},{2,3},{4,5},{5,6},{6,7},{8,9},{9,10},{10,11},{12,13},{... | collective-permute-start | bytes 1474568 | tf_op jit(solution)/shard_map/ppermute | solution.py:44
  133.2 19.3 %collective-permute-start.31 = (bf16[96,2560]{1,0:T(8,128)(2,1)S(1)}, bf16[96,2560]{1,0:T(8,128)(2,1)S(1)}, u32[]{:S(2)}, u32[]{:S(2)}) collective-permute-start(bf16[96,2560]{1,0:T(8,128)(2,1)S(1)} %unit_gradient.6.refs_7_), channel_id=1, source_target_pairs={{1,0},{2,1},{3,2},{5,4},{6,5},{7,6},{9,8},{10,9},{11,10},{13,12},{... | collective-permute-start | bytes 1474568 | tf_op jit(solution)/shard_map/ppermute | solution.py:44
  134.5 18.0 %collective-permute-start.30 = (bf16[96,2560]{1,0:T(8,128)(2,1)S(1)}, bf16[96,2560]{1,0:T(8,128)(2,1)}, u32[]{:S(2)}, u32[]{:S(2)}) collective-permute-start(bf16[96,2560]{1,0:T(8,128)(2,1)S(1)} %unit_gradient.6.refs_7_), channel_id=1, source_target_pairs={{0,1},{1,2},{2,3},{4,5},{5,6},{6,7},{8,9},{9,10},{10,11},{12,13},{... | collective-permute-start | bytes 1474568 | tf_op jit(solution)/shard_map/ppermute | solution.py:44
  145.3 15.2 %collective-permute-start.14 = (bf16[96,2560]{1,0:T(8,128)(2,1)S(1)}, bf16[96,2560]{1,0:T(8,128)(2,1)S(1)}, u32[]{:S(2)}, u32[]{:S(2)}) collective-permute-start(bf16[96,2560]{1,0:T(8,128)(2,1)S(1)} %get-tuple-element.227), channel_id=1, source_target_pairs={{0,1},{1,2},{2,3},{4,5},{5,6},{6,7},{8,9},{9,10},{10,11},{12,13},{... | collective-permute-start | bytes 1474568 | tf_op jit(solution)/shard_map/ppermute | solution.py:44
  148.0 13.2 %collective-permute-start.15 = (bf16[96,2560]{1,0:T(8,128)(2,1)S(1)}, bf16[96,2560]{1,0:T(8,128)(2,1)S(1)}, u32[]{:S(2)}, u32[]{:S(2)}) collective-permute-start(bf16[96,2560]{1,0:T(8,128)(2,1)S(1)} %get-tuple-element.228), channel_id=1, source_target_pairs={{1,0},{2,1},{3,2},{5,4},{6,5},{7,6},{9,8},{10,9},{11,10},{13,12},{... | collective-permute-start | bytes 1474568 | tf_op jit(solution)/shard_map/ppermute | solution.py:44
  154.7 15.9 %collective-permute-start.32 = (bf16[96,2560]{1,0:T(8,128)(2,1)S(1)}, bf16[96,2560]{1,0:T(8,128)(2,1)S(1)}, u32[]{:S(2)}, u32[]{:S(2)}) collective-permute-start(bf16[96,2560]{1,0:T(8,128)(2,1)S(1)} %get-tuple-element.243), channel_id=1, source_target_pairs={{0,1},{1,2},{2,3},{4,5},{5,6},{6,7},{8,9},{9,10},{10,11},{12,13},{... | collective-permute-start | bytes 1474568 | tf_op jit(solution)/shard_map/ppermute | solution.py:44
  159.3 14.3 %collective-permute-start.33 = (bf16[96,2560]{1,0:T(8,128)(2,1)S(1)}, bf16[96,2560]{1,0:T(8,128)(2,1)S(1)}, u32[]{:S(2)}, u32[]{:S(2)}) collective-permute-start(bf16[96,2560]{1,0:T(8,128)(2,1)S(1)} %get-tuple-element.244), channel_id=1, source_target_pairs={{1,0},{2,1},{3,2},{5,4},{6,5},{7,6},{9,8},{10,9},{11,10},{13,12},{... | collective-permute-start | bytes 1474568 | tf_op jit(solution)/shard_map/ppermute | solution.py:44
  162.6 18.5 %collective-permute-start.16 = (bf16[96,2560]{1,0:T(8,128)(2,1)S(1)}, bf16[96,2560]{1,0:T(8,128)(2,1)S(1)}, u32[]{:S(2)}, u32[]{:S(2)}) collective-permute-start(bf16[96,2560]{1,0:T(8,128)(2,1)S(1)} %get-tuple-element.229), channel_id=1, source_target_pairs={{0,1},{1,2},{2,3},{4,5},{5,6},{6,7},{8,9},{9,10},{10,11},{12,13},{... | collective-permute-start | bytes 1474568 | tf_op jit(solution)/shard_map/ppermute | solution.py:44
  168.9 15.2 %collective-permute-start.17 = (bf16[96,2560]{1,0:T(8,128)(2,1)S(1)}, bf16[96,2560]{1,0:T(8,128)(2,1)S(1)}, u32[]{:S(2)}, u32[]{:S(2)}) collective-permute-start(bf16[96,2560]{1,0:T(8,128)(2,1)S(1)} %get-tuple-element.230), channel_id=1, source_target_pairs={{1,0},{2,1},{3,2},{5,4},{6,5},{7,6},{9,8},{10,9},{11,10},{13,12},{... | collective-permute-start | bytes 1474568 | tf_op jit(solution)/shard_map/ppermute | solution.py:44
  174.9 16.7 %collective-permute-start.34 = (bf16[96,2560]{1,0:T(8,128)(2,1)S(1)}, bf16[96,2560]{1,0:T(8,128)(2,1)S(1)}, u32[]{:S(2)}, u32[]{:S(2)}) collective-permute-start(bf16[96,2560]{1,0:T(8,128)(2,1)S(1)} %get-tuple-element.245), channel_id=1, source_target_pairs={{0,1},{1,2},{2,3},{4,5},{5,6},{6,7},{8,9},{9,10},{10,11},{12,13},{... | collective-permute-start | bytes 1474568 | tf_op jit(solution)/shard_map/ppermute | solution.py:44
  179.4 14.9 %collective-permute-start.35 = (bf16[96,2560]{1,0:T(8,128)(2,1)S(1)}, bf16[96,2560]{1,0:T(8,128)(2,1)S(1)}, u32[]{:S(2)}, u32[]{:S(2)}) collective-permute-start(bf16[96,2560]{1,0:T(8,128)(2,1)S(1)} %get-tuple-element.246), channel_id=1, source_target_pairs={{1,0},{2,1},{3,2},{5,4},{6,5},{7,6},{9,8},{10,9},{11,10},{13,12},{... | collective-permute-start | bytes 1474568 | tf_op jit(solution)/shard_map/ppermute | solution.py:44
  185.4 16.8 %collective-permute-start.18 = (bf16[96,2560]{1,0:T(8,128)(2,1)S(1)}, bf16[96,2560]{1,0:T(8,128)(2,1)S(1)}, u32[]{:S(2)}, u32[]{:S(2)}) collective-permute-start(bf16[96,2560]{1,0:T(8,128)(2,1)S(1)} %get-tuple-element.231), channel_id=1, source_target_pairs={{0,1},{1,2},{2,3},{4,5},{5,6},{6,7},{8,9},{9,10},{10,11},{12,13},{... | collective-permute-start | bytes 1474568 | tf_op jit(solution)/shard_map/ppermute | solution.py:44
  190.0 14.8 %copy-start.4 = (bf16[1,384,2560]{2,1,0:T(8,128)(2,1)S(1)}, bf16[1,384,2560]{2,1,0:T(8,128)(2,1)}, u32[]{:S(2)}) copy-start(bf16[1,384,2560]{2,1,0:T(8,128)(2,1)} %param.17) | copy-start | bytes 5898244
  190.0 14.8 %copy-start.6 = (bf16[1,384,2560]{2,1,0:T(8,128)(2,1)S(1)}, bf16[1,384,2560]{2,1,0:T(8,128)(2,1)}, u32[]{:S(2)}) copy-start(bf16[1,384,2560]{2,1,0:T(8,128)(2,1)} %param.18) | copy-start | bytes 5898244
  190.0 14.8 %collective-permute-start.19 = (bf16[96,2560]{1,0:T(8,128)(2,1)S(1)}, bf16[96,2560]{1,0:T(8,128)(2,1)S(1)}, u32[]{:S(2)}, u32[]{:S(2)}) collective-permute-start(bf16[96,2560]{1,0:T(8,128)(2,1)S(1)} %get-tuple-element.232), channel_id=1, source_target_pairs={{1,0},{2,1},{3,2},{5,4},{6,5},{7,6},{9,8},{10,9},{11,10},{13,12},{... | collective-permute-start | bytes 1474568 | tf_op jit(solution)/shard_map/ppermute | solution.py:44
  195.7 34.0 %slice-start = ((s8[6553600]{0:T(1024)(128)(4,1)}), s8[4194304]{0:T(1024)(128)(4,1)S(1)}, s32[]{:S(2)}) async-start(s8[6553600]{0:T(1024)(128)(4,1)} %bitcast.39), calls=%async_computation.6 | async-start | bytes 8388608
  195.7 16.8 %collective-permute-start.38 = (bf16[96,2560]{1,0:T(8,128)(2,1)S(1)}, bf16[96,2560]{1,0:T(8,128)(2,1)S(1)}, u32[]{:S(2)}, u32[]{:S(2)}) collective-permute-start(bf16[96,2560]{1,0:T(8,128)(2,1)S(1)} %get-tuple-element.250), channel_id=1, source_target_pairs={{0,1},{1,2},{2,3},{4,5},{5,6},{6,7},{8,9},{9,10},{10,11},{12,13},{... | collective-permute-start | bytes 1474568 | tf_op jit(solution)/shard_map/ppermute | solution.py:44
  200.8 28.9 %slice-start.1 = ((s8[6553600]{0:T(1024)(128)(4,1)}), s8[2359296]{0:T(1024)(128)(4,1)S(1)}, s32[]{:S(2)}) async-start(s8[6553600]{0:T(1024)(128)(4,1)} %bitcast.39), calls=%async_computation.7 | async-start | bytes 4718592
  200.8 16.2 %collective-permute-start.39 = (bf16[96,2560]{1,0:T(8,128)(2,1)S(1)}, bf16[96,2560]{1,0:T(8,128)(2,1)S(1)}, u32[]{:S(2)}, u32[]{:S(2)}) collective-permute-start(bf16[96,2560]{1,0:T(8,128)(2,1)S(1)} %get-tuple-element.251), channel_id=1, source_target_pairs={{1,0},{2,1},{3,2},{5,4},{6,5},{7,6},{9,8},{10,9},{11,10},{13,12},{... | collective-permute-start | bytes 1474568 | tf_op jit(solution)/shard_map/ppermute | solution.py:44
  205.4 12.2 %copy-start.23 = (bf16[96,2560]{1,0:T(8,128)(2,1)}, bf16[96,2560]{1,0:T(8,128)(2,1)S(1)}, u32[]{:S(2)}) copy-start(bf16[96,2560]{1,0:T(8,128)(2,1)S(1)} %unit_gradient.5.refs_0_) | copy-start | bytes 1474564
  205.4 24.3 %copy-start.16 = (bf16[4,96,640]{2,1,0:T(8,128)(2,1)S(1)}, bf16[4,96,640]{2,1,0:T(8,128)(2,1)}, u32[]{:S(2)}) copy-start(bf16[4,96,640]{2,1,0:T(8,128)(2,1)} %copy-done.15) | copy-start | bytes 1474564
  205.4 24.3 %copy-start.18 = (bf16[4,96,640]{2,1,0:T(8,128)(2,1)S(1)}, bf16[4,96,640]{2,1,0:T(8,128)(2,1)}, u32[]{:S(2)}) copy-start(bf16[4,96,640]{2,1,0:T(8,128)(2,1)} %copy-done.17) | copy-start | bytes 1474564
  205.4 22.1 %collective-permute-start.22 = (bf16[96,2560]{1,0:T(8,128)(2,1)S(1)}, bf16[96,2560]{1,0:T(8,128)(2,1)S(1)}, u32[]{:S(2)}, u32[]{:S(2)}) collective-permute-start(bf16[96,2560]{1,0:T(8,128)(2,1)S(1)} %unit_gradient.5.refs_0_), channel_id=1, source_target_pairs={{1,0},{2,1},{3,2},{5,4},{6,5},{7,6},{9,8},{10,9},{11,10},{13,12},{... | collective-permute-start | bytes 1474568 | tf_op jit(solution)/shard_map/ppermute | solution.py:44
  206.9 21.9 %collective-permute-start.20 = (bf16[96,2560]{1,0:T(8,128)(2,1)S(1)}, bf16[96,2560]{1,0:T(8,128)(2,1)S(1)}, u32[]{:S(2)}, u32[]{:S(2)}) collective-permute-start(bf16[96,2560]{1,0:T(8,128)(2,1)S(1)} %unit_gradient.5.refs_0_), channel_id=1, source_target_pairs={{0,1},{1,2},{2,3},{4,5},{5,6},{6,7},{8,9},{9,10},{10,11},{12,13},{... | collective-permute-start | bytes 1474568 | tf_op jit(solution)/shard_map/ppermute | solution.py:44
  217.6 18.9 %copy-start.25 = (bf16[96,2560]{1,0:T(8,128)(2,1)}, bf16[96,2560]{1,0:T(8,128)(2,1)S(1)}, u32[]{:S(2)}) copy-start(bf16[96,2560]{1,0:T(8,128)(2,1)S(1)} %unit_gradient.7.refs_7_) | copy-start | bytes 1474564
  217.6 20.4 %collective-permute-start.41 = (bf16[96,2560]{1,0:T(8,128)(2,1)S(1)}, bf16[96,2560]{1,0:T(8,128)(2,1)S(1)}, u32[]{:S(2)}, u32[]{:S(2)}) collective-permute-start(bf16[96,2560]{1,0:T(8,128)(2,1)S(1)} %unit_gradient.7.refs_7_), channel_id=1, source_target_pairs={{1,0},{2,1},{3,2},{5,4},{6,5},{7,6},{9,8},{10,9},{11,10},{13,12},{... | collective-permute-start | bytes 1474568 | tf_op jit(solution)/shard_map/ppermute | solution.py:44
  218.9 19.1 %collective-permute-start.40 = (bf16[96,2560]{1,0:T(8,128)(2,1)S(1)}, bf16[96,2560]{1,0:T(8,128)(2,1)S(1)}, u32[]{:S(2)}, u32[]{:S(2)}) collective-permute-start(bf16[96,2560]{1,0:T(8,128)(2,1)S(1)} %unit_gradient.7.refs_7_), channel_id=1, source_target_pairs={{0,1},{1,2},{2,3},{4,5},{5,6},{6,7},{8,9},{9,10},{10,11},{12,13},{... | collective-permute-start | bytes 1474568 | tf_op jit(solution)/shard_map/ppermute | solution.py:44
  227.5 22.1 %collective-permute-start.23 = (bf16[96,2560]{1,0:T(8,128)(2,1)S(1)}, bf16[96,2560]{1,0:T(8,128)(2,1)S(1)}, u32[]{:S(2)}, u32[]{:S(2)}) collective-permute-start(bf16[96,2560]{1,0:T(8,128)(2,1)S(1)} %collective-permute-done.22.refs_4_), channel_id=1, source_target_pairs={{1,0},{2,1},{5,4},{6,5},{9,8},{10,9},{13,12},{14,13},{17,16},{18,1... | collective-permute-start | bytes 1474568 | tf_op jit(solution)/shard_map/ppermute | solution.py:44
  228.8 20.8 %collective-permute-start.21 = (bf16[96,2560]{1,0:T(8,128)(2,1)S(1)}, bf16[96,2560]{1,0:T(8,128)(2,1)S(1)}, u32[]{:S(2)}, u32[]{:S(2)}) collective-permute-start(bf16[96,2560]{1,0:T(8,128)(2,1)S(1)} %collective-permute-done.20.refs_1_), channel_id=1, source_target_pairs={{1,2},{2,3},{5,6},{6,7},{9,10},{10,11},{13,14},{14,15},{17,18},{18... | collective-permute-start | bytes 1474568 | tf_op jit(solution)/shard_map/ppermute | solution.py:44
  236.6 13.0 %copy-start.12 = (f32[640,2560]{1,0:T(8,128)}, f32[640,2560]{1,0:T(8,128)S(1)}, u32[]{:S(2)}) copy-start(f32[640,2560]{1,0:T(8,128)S(1)} %get-tuple-element.255.refs_16_) | copy-start | bytes 19660804
  238.0 11.5 %copy-start.27 = (bf16[96,2560]{1,0:T(8,128)(2,1)}, bf16[96,2560]{1,0:T(8,128)(2,1)S(1)}, u32[]{:S(2)}) copy-start(bf16[96,2560]{1,0:T(8,128)(2,1)S(1)} %collective-permute-done.41.left_ref.refs_11_) | copy-start | bytes 1474564
  238.0 11.5 %copy-start.29 = (bf16[96,2560]{1,0:T(8,128)(2,1)}, bf16[96,2560]{1,0:T(8,128)(2,1)S(1)}, u32[]{:S(2)}) copy-start(bf16[96,2560]{1,0:T(8,128)(2,1)S(1)} %collective-permute-done.40.right_ref.refs_8_) | copy-start | bytes 1474564
  238.2 13.6 %collective-permute-start.42 = (bf16[96,2560]{1,0:T(8,128)(2,1)S(1)}, bf16[96,2560]{1,0:T(8,128)(2,1)}, u32[]{:S(2)}, u32[]{:S(2)}) collective-permute-start(bf16[96,2560]{1,0:T(8,128)(2,1)S(1)} %get-tuple-element.253), channel_id=1, source_target_pairs={{1,2},{2,3},{5,6},{6,7},{9,10},{10,11},{13,14},{14,15},{17,18},{18... | collective-permute-start | bytes 1474568 | tf_op jit(solution)/shard_map/ppermute | solution.py:44
  239.8 17.7 %collective-permute-start.44 = (bf16[96,2560]{1,0:T(8,128)(2,1)S(1)}, bf16[96,2560]{1,0:T(8,128)(2,1)}, u32[]{:S(2)}, u32[]{:S(2)}) collective-permute-start(bf16[96,2560]{1,0:T(8,128)(2,1)S(1)} %get-tuple-element.254), channel_id=1, source_target_pairs={{1,0},{2,1},{5,4},{6,5},{9,8},{10,9},{13,12},{14,13},{17,16},{18,1... | collective-permute-start | bytes 1474568 | tf_op jit(solution)/shard_map/ppermute | solution.py:44
  249.7 10.3 %collective-permute-start.36 = (bf16[96,2560]{1,0:T(8,128)(2,1)S(1)}, bf16[96,2560]{1,0:T(8,128)(2,1)S(1)}, u32[]{:S(2)}, u32[]{:S(2)}) collective-permute-start(bf16[96,2560]{1,0:T(8,128)(2,1)S(1)} %get-tuple-element.248), channel_id=1, source_target_pairs={{2,3},{6,7},{10,11},{14,15},{18,19},{22,23},{26,27},{30,31}} | collective-permute-start | bytes 1474568 | tf_op jit(solution)/shard_map/ppermute | solution.py:44
  250.4 19.3 %collective-permute-start.37 = (bf16[96,2560]{1,0:T(8,128)(2,1)S(1)}, bf16[96,2560]{1,0:T(8,128)(2,1)S(1)}, u32[]{:S(2)}, u32[]{:S(2)}) collective-permute-start(bf16[96,2560]{1,0:T(8,128)(2,1)S(1)} %get-tuple-element.249), channel_id=1, source_target_pairs={{1,0},{5,4},{9,8},{13,12},{17,16},{21,20},{25,24},{29,28}} | collective-permute-start | bytes 1474568 | tf_op jit(solution)/shard_map/ppermute | solution.py:44
  251.7 18.0 %collective-permute-start.43 = (bf16[96,2560]{1,0:T(8,128)(2,1)}, bf16[96,2560]{1,0:T(8,128)(2,1)S(1)}, u32[]{:S(2)}, u32[]{:S(2)}) collective-permute-start(bf16[96,2560]{1,0:T(8,128)(2,1)} %collective-permute-done.42.refs_9_), channel_id=1, source_target_pairs={{2,3},{6,7},{10,11},{14,15},{18,19},{22,23},{26,27},{30,31}} | collective-permute-start | bytes 1474568 | tf_op jit(solution)/shard_map/ppermute | solution.py:44
  257.5 17.9 %collective-permute-start.45 = (bf16[96,2560]{1,0:T(8,128)(2,1)}, bf16[96,2560]{1,0:T(8,128)(2,1)}, u32[]{:S(2)}, u32[]{:S(2)}) collective-permute-start(bf16[96,2560]{1,0:T(8,128)(2,1)} %collective-permute-done.44.refs_12_), channel_id=1, source_target_pairs={{1,0},{5,4},{9,8},{13,12},{17,16},{21,20},{25,24},{29,28}} | collective-permute-start | bytes 1474568 | tf_op jit(solution)/shard_map/ppermute | solution.py:44
  260.0 15.4 %copy-start.40 = (bf16[96,2560]{1,0:T(8,128)(2,1)}, bf16[96,2560]{1,0:T(8,128)(2,1)S(1)}, u32[]{:S(2)}) copy-start(bf16[96,2560]{1,0:T(8,128)(2,1)S(1)} %collective-permute-done.36.refs_3_) | copy-start | bytes 1474564
  290.7 69.3 %collective-permute-start.1 = (bf16[640,2560]{1,0:T(8,128)(2,1)S(1)}, bf16[640,2560]{1,0:T(8,128)(2,1)}, u32[]{:S(2)}, u32[]{:S(2)}) collective-permute-start(bf16[640,2560]{1,0:T(8,128)(2,1)S(1)} %get-tuple-element.128), channel_id=1, source_target_pairs={{0,8},{4,12},{8,16},{12,20},{16,24},{20,28},{24,0},{28,4},{1,9},{5... | collective-permute-start | bytes 9830408 | tf_op jit(solution)/shard_map/cond/branch_1_fun/ppermute | solution.py:442
  (34 other events, 208.9 us)

commit v3 on v2

--- a/solution.py
+++ b/solution.py
@@ -7,7 +7,7 @@
 from jax.experimental.pallas import tpu as pltpu
 from jax.sharding import PartitionSpec as P
 
-STREAMS = ((96, 96), (96, 96))
+STREAMS = ((64, 64, 64), (64, 64, 64))
 MIB = 1 << 20
 TOKEN = jax.ShapeDtypeStruct((8, 128), jnp.float32)
 
@@ -58,7 +58,7 @@
 def cut_heads(heads, start, size, members, token):
     inner = heads.shape[1]
     rows = inner // members
-    step = 48
+    step = size // 2
 
     def body(heads_ref, *refs):
         for k in range(members):
@@ -72,6 +72,7 @@
         + ([] if token is None else [token_in(token)]),
         [((members, size, rows), heads.dtype, (members, step, rows), lambda i: (0, i, 0))],
         moved=4 * size * inner,
+        vmem=12 if start else 56,
     )[0]
 
 
@@ -93,6 +94,7 @@
         [((rows, width), jnp.bfloat16) + block, TOKEN_OUT],
         flops=2 * rows * width,
         moved=6 * rows * width,
+        vmem=56,
     )[0]
 
 
@@ -103,7 +105,7 @@
     tile = tile_of(width, 1280)
 
     def body(mine_ref, weights_ref, *refs):
-        out_ref, last_ref, first_ref, token_out = refs[-4:]
+        out_ref, last_ref, first_ref = refs[-3:]
         product = jnp.dot(
             mine_ref[...].reshape(members * size, rows),
             weights_ref[...],
@@ -112,7 +114,6 @@
         out_ref[...] = product.reshape(members, size, tile)
         last_ref[...] = product[(members - 1) * size :]
         first_ref[...] = product[:size]
-        token_out[...] = jnp.zeros((8, 128), jnp.float32)
 
     flat = ((size, width), jnp.bfloat16, (size, tile), lambda j: (0, j))
     return call(
@@ -133,7 +134,6 @@
             ),
             flat,
             flat,
-            TOKEN_OUT,
         ],
         flops=2 * members * size * rows * width,
         moved=2 * (members * size * (rows + width) + rows * width),
@@ -143,7 +143,7 @@
 
 def next_payload(right, left, parts, scalars, pick):
     members, size, width = parts.shape
-    step = 48
+    step = size // 2
 
     def joined(arrived, part, counts):
         if pick:
@@ -177,11 +177,11 @@
     )
 
 
-def unit_gradient(right, left, parts, place, residual, cotangent, gain, start, token):
+def unit_gradient(right, left, parts, place, residual, cotangent, gain, start):
     members, size, width = parts.shape
-    step = 48
-
-    def body(s, right_ref, left_ref, own_ref, residual_ref, cot_ref, gain_ref, *refs):
+    step = size // 2
+
+    def body(s, right_ref, left_ref, own_ref, residual_ref, cot_ref, gain_ref, out_ref):
         product = (
             right_ref[...].astype(jnp.float32)
             + left_ref[...].astype(jnp.float32)
@@ -191,7 +191,7 @@
         inverse = lax.rsqrt(jnp.mean(summed * summed, axis=-1, keepdims=True) + 1e-05)
         scaled_cot = gain_ref[...] * cot_ref[...].astype(jnp.float32)
         along = jnp.mean(scaled_cot * summed, axis=-1, keepdims=True)
-        refs[-1][...] = (
+        out_ref[...] = (
             inverse * scaled_cot - summed * (inverse * inverse * inverse * along)
         ).astype(jnp.bfloat16)
 
@@ -208,8 +208,7 @@
             (residual,) + there,
             (cotangent,) + there,
             (gain, (1, width), fixed(0, 0)),
-        ]
-        + ([] if token is None else [token_in(token)]),
+        ],
         [((size, width), jnp.bfloat16) + here],
         scalars=(place,),
         flops=12 * size * width,
@@ -306,7 +305,7 @@
         scratch=[pltpu.VMEM((rows, total), jnp.bfloat16)],
         flops=2 * total * rows * width,
         moved=2 * count * units[0][0].shape[0] * width + 12 * rows * width,
-        vmem=26,
+        vmem=50,
     )
 
 
@@ -320,8 +319,7 @@
     total = members * sum(sizes)
 
     def body(s, *refs):
-        weights_ref, grad_ref, token_out, acc = refs[count:]
-        token_out[...] = jnp.zeros((8, 128), jnp.float32)
+        weights_ref, grad_ref, acc = refs[count:]
         j = pl.program_id(0)
         grad = lax.dot_general(
             stack_of(refs[:count], members, s[0]),
@@ -358,20 +356,19 @@
                 jnp.bfloat16,
                 (members, sum(sizes), rows),
                 fixed(0, 0, 0),
-            ),
-            TOKEN_OUT,
+            )
         ],
         scalars=(order,),
         scratch=[pltpu.VMEM((total, rows), jnp.float32)],
         flops=2 * total * rows * width,
         moved=2 * count * sizes[0] * width + 2 * rows * width,
-        vmem=20,
-    )
+        vmem=50,
+    )[0]
 
 
 def passed(right, left, token):
     size, width = right.shape
-    step = 48
+    step = size // 2
 
     def body(right_ref, left_ref, token_ref, right_out, left_out):
         right_out[...] = right_ref[...]
@@ -437,14 +434,12 @@
     return lax.all_to_all(blocks, "fsdp", 0, 0, tiled=False)
 
 
-def tail(kept, units, weights, grads, order, bit_place):
+def tail(kept, units, weights, order, bit_place):
     length = lax.axis_size("rep")
     sent = lax.ppermute(
         kept, "rep", [(i, (i + (1 << bit_place)) % length) for i in range(length)]
     )
-    last, _ = grad_rows(units, weights, order)
-    back = swapped(jnp.concatenate(grads + [last], axis=1))
-    return sent, joined_rows(back)
+    return sent, joined_rows(swapped(grad_rows(units, weights, order)))
 
 
 def local(
@@ -504,8 +499,6 @@
     units = [[None] * count for _ in range(rounds)]
     before = [None] * count
     hint = [None] * count
-    kept = None
-    grads = []
 
     def fetch(e, members_of, token):
         size = STREAMS[members_of[0]][e]
@@ -516,14 +509,11 @@
         for index, q in enumerate(members_of):
             mine[e][q] = (array, index, size)
 
-    fetch(0, [0], None)
-    done = None
+    fetch(0, list(range(count)), None)
     for e in range(rounds):
         parts, moving = [None] * count, [None] * count
         for q in range(count):
-            parts[q], last, first, token = partial_products(mine[e][q], weights, hint[q])
-            if e == 0 and q + 1 < count:
-                fetch(0, [q + 1], token)
+            parts[q], last, first = partial_products(mine[e][q], weights, hint[q])
             if e == 0:
                 moving[q] = hops(last, first, range(1), range(members - 1, members))
             else:
@@ -545,11 +535,6 @@
                 if e > 0 and t < members - 2:
                     units[e - 1][q][1].append(moving[q][0])
                     units[e - 1][q][2].append(moving[q][1])
-        if e > 0:
-            flat = [[u] + r + l for u, r, l in units[e - 1]]
-            kept, done = weight_step(flat, mine[e - 1], order, kept, numer, None)
-            grad, grad_done = grad_rows(flat, weights, order)
-            grads.append(grad)
         for q in range(count):
             unit = unit_gradient(
                 *moving[q],
@@ -559,23 +544,25 @@
                 cotangent[0],
                 gain[None],
                 starts[e][q],
-                None,
             )
             before[q] = hops(unit, unit, *everyone)
             units[e][q] = (unit, [before[q][0]], [before[q][1]])
+    kept = None
     for s in range(1, members - 1):
         for q in range(count):
             if (s, q) == (1, count - 1):
+                early = [[u] + r + l for of_round in units[:-1] for u, r, l in of_round]
+                kept, done = weight_step(
+                    early, [m for of_round in mine[:-1] for m in of_round], order, None, numer, None
+                )
                 before[q] = passed(*before[q], done)
-            if (s, q) == (2, 0):
-                before[q] = passed(*before[q], grad_done)
             before[q] = hops(*before[q], range(s, members - 1), range(1, members - s))
             units[-1][q][1].append(before[q][0])
             units[-1][q][2].append(before[q][1])
     flat = [[u] + r + l for u, r, l in units[-1]]
     new_params, half = weight_step(flat, mine[-1], order, kept, None, inbox_params[0])
     new_weight = 0.5 * push_weight + inbox_weight
-    branches = [partial(tail, half, flat, weights, grads, order, place) for place in range(levels)]
+    branches = [partial(tail, half, early + flat, weights, order, place) for place in range(levels)]
     sent, grad_heads = lax.switch(level_index, branches)
     return (new_params[None], new_weight, widened(sent)[None], outbox_weight, grad_heads[None])
 

time: 369 us -> 382 us (1.035)
  waiting for transfers between devices: 83 us -> 44.9 us
  Pallas kernels: 79 us -> 108 us
  starting transfers between devices: 136 us -> 162 us
  local copies, waits for them, and re-layouts: 15.6 us -> 7.38 us
  blocking collectives: 43.2 us -> 49.3 us
    pallas_call x30 -> x38, Pallas kernels: 79 us -> 108 us  [call(): pl.pallas_call(body, name=name, out_shape=[jax.ShapeDtypeStruct(shape, ki...]
    ppermute x40 -> x56, starting transfers between devices: 113 us -> 140 us  [hop(): return lax.ppermute(value, 'fsdp', [(i, i + step) for i in pairs])]
    ppermute x40 -> x56, waiting for transfers between devices: 61.3 us -> 44.8 us  [hop(): return lax.ppermute(value, 'fsdp', [(i, i + step) for i in pairs])]
    ppermute x1, waiting for transfers between devices: 15.2 us -> 0.01 us  [tail(): lax.ppermute(kept, 'rep', [(i, (i + (1 << bit_place)) % length) for i in...]
    unnamed x102 -> x172, local copies, waits for them, and re-layouts: 15.6 us -> 6.78 us
    all_to_all x3, waiting for transfers between devices: 6.49 us -> 0.1 us  [swapped(): return lax.all_to_all(blocks, 'fsdp', 0, 0, tiled=False)]
    all_to_all x1, blocking collectives: 43.2 us -> 49.3 us  [swapped(): return lax.all_to_all(blocks, 'fsdp', 0, 0, tiled=False)]
  transfers between devices with their start and end apart: 47 -> 63, of which waited for: 19 -> 16; matrix products, arithmetic and copies ran while one was open for 0% -> 0% of each run, Pallas kernels for 16% -> 22%
where the time goes in v3:
time: 382 us; the launch traced here: 383 us
  starting transfers between devices  162 us (42%)
  Pallas kernels  108 us (28%)
  blocking collectives  49.3 us (13%)
  waiting for transfers between devices  44.9 us (12%)
  between operations  9.69 us (3%)
  local copies, waits for them, and re-layouts  7.38 us (2%)
    ppermute x56, starting transfers between devices, hop(): return lax.ppermute(value, 'fsdp', [(i, i + step) for i in pairs])  140 us
    pallas_call x38, Pallas kernels, call(): pl.pallas_call(body, name=name, out_shape=[jax.ShapeDtypeStruct(shape, ki...  108 us
    all_to_all x1, blocking collectives, swapped(): return lax.all_to_all(blocks, 'fsdp', 0, 0, tiled=False)  49.3 us
    ppermute x56, waiting for transfers between devices, hop(): return lax.ppermute(value, 'fsdp', [(i, i + step) for i in pairs])  44.8 us
    all_to_all x3, starting transfers between devices, swapped(): return lax.all_to_all(blocks, 'fsdp', 0, 0, tiled=False)  15.6 us
  transfers between devices with their start and end apart: 63, of which 16 were waited for; matrix products, arithmetic and copies ran while one was open for 0% of the time, Pallas kernels for 22%

profile of v3, /device:TPU:0, one launch (start us, length us, event | category | flops | bytes accessed | tf_op | source)
XLA Modules:
  0.0 382.6 jit_solution(10225899027420235164)
XLA Ops:
  0.6 1.8 cut_heads.3
  2.5 6.3 %all-to-all-start.3 = ((bf16[4,128,640]{2,1,0:T(8,128)(2,1)}), bf16[4,128,640]{2,1,0:T(8,128)(2,1)S(1)}, u32[]{:S(2)}, u32[]{:S(2)}) async-start(bf16[4,128,640]{2,1,0:T(8,128)(2,1)} %cut_heads.3), calls=%async_computation.3 | async-start | bytes 1310720 | tf_op jit(solution)/shard_map/all_to_all | solution.py:434
  10.3 2.8 collective-permute-start.4
  13.1 2.8 collective-permute-start.3
  20.4 5.6 %scaled_weights.1 = (bf16[640,2560]{1,0:T(8,128)(2,1)}, f32[8,128]{1,0:T(8,128)}) custom-call(f32[640,2560]{1,0:T(8,128)} %bitcast.45, f32[1,1]{1,0:T(1,128)} %bitcast.29.one_ref, f32[8,128]{1,0:T(8,128)} %broadcast_in_dim.42.refs_0_), custom_call_target="tpu_custom_call" | custom-call | flops 3276800 | bytes 9830400 | tf_op jit(solution)/shard_map/scaled_weights/pallas_call | solution.py:16
  26.1 3.9 %partial_products.6 = (bf16[4,64,2560]{2,1,0:T(8,128)(2,1)S(1)}, bf16[64,2560]{1,0:T(8,128)(2,1)}, bf16[64,2560]{1,0:T(8,128)(2,1)}) custom-call(bf16[4,128,640]{2,1,0:T(8,128)(2,1)S(1)} %all-to-all-done.3.mine_ref.refs_28_.refs_29_, bf16[640,2560]{1,0:T(8,128)(2,1)} %get-tuple-element.468.weights_ref), custom_call_target="tpu_custom_call" | custom-call | flops 838860800 | bytes 4915200 | tf_op jit(solution)/shard_map/partial_products/pallas_call | solution.py:16
  30.0 4.6 %collective-permute-start.6 = (bf16[64,2560]{1,0:T(8,128)(2,1)}, bf16[64,2560]{1,0:T(8,128)(2,1)}, u32[]{:S(2)}, u32[]{:S(2)}) collective-permute-start(bf16[64,2560]{1,0:T(8,128)(2,1)} %get-tuple-element.469), channel_id=1, source_target_pairs={{0,1},{4,5},{8,9},{12,13},{16,17},{20,21},{24,25},{28,29}} | collective-permute-start | bytes 983048 | tf_op jit(solution)/shard_map/ppermute | solution.py:44
  36.0 2.5 partial_products.9
  38.5 2.0 collective-permute-start.34
  42.0 1.8 next_payload.16
  46.1 5.1 %all-to-all-start.4 = ((bf16[4,128,640]{2,1,0:T(8,128)(2,1)}), bf16[4,128,640]{2,1,0:T(8,128)(2,1)}, u32[]{:S(2)}, u32[]{:S(2)}) async-start(bf16[4,128,640]{2,1,0:T(8,128)(2,1)} %cut_heads.4), calls=%async_computation.4 | async-start | bytes 1310720 | tf_op jit(solution)/shard_map/all_to_all | solution.py:434
  51.3 4.7 %collective-permute-start.8 = (bf16[64,2560]{1,0:T(8,128)(2,1)}, bf16[64,2560]{1,0:T(8,128)(2,1)}, u32[]{:S(2)}, u32[]{:S(2)}) collective-permute-start(bf16[64,2560]{1,0:T(8,128)(2,1)} %copy-done.14), channel_id=1, source_target_pairs={{0,1},{1,2},{4,5},{5,6},{8,9},{9,10},{12,13},{13,14},{16,17},{17,1... | collective-permute-start | bytes 983048 | tf_op jit(solution)/shard_map/ppermute | solution.py:44
  57.4 2.5 next_payload.24
  60.0 3.2 collective-permute-start.36
  64.6 5.7 %collective-permute-done.8.right_ref = bf16[64,2560]{1,0:T(8,128)(2,1)} collective-permute-done((bf16[64,2560]{1,0:T(8,128)(2,1)}, bf16[64,2560]{1,0:T(8,128)(2,1)}, u32[]{:S(2)}, u32[]{:S(2)}) %collective-permute-start.8) | collective-permute-done | bytes 327712 | tf_op jit(solution)/shard_map/ppermute | solution.py:44
  70.3 1.9 next_payload.17
  72.2 7.9 %collective-permute-start.10 = (bf16[64,2560]{1,0:T(8,128)(2,1)S(1)}, bf16[64,2560]{1,0:T(8,128)(2,1)S(1)}, u32[]{:S(2)}, u32[]{:S(2)}) collective-permute-start(bf16[64,2560]{1,0:T(8,128)(2,1)S(1)} %get-tuple-element.474), channel_id=1, source_target_pairs={{0,1},{1,2},{2,3},{4,5},{5,6},{6,7},{8,9},{9,10},{10,11},{12,13},{... | collective-permute-start | bytes 983048 | tf_op jit(solution)/shard_map/ppermute | solution.py:44
  81.4 1.8 next_payload.25
  83.3 4.6 %collective-permute-start.38 = (bf16[64,2560]{1,0:T(8,128)(2,1)S(1)}, bf16[64,2560]{1,0:T(8,128)(2,1)S(1)}, u32[]{:S(2)}, u32[]{:S(2)}) collective-permute-start(bf16[64,2560]{1,0:T(8,128)(2,1)S(1)} %get-tuple-element.499), channel_id=1, source_target_pairs={{0,1},{1,2},{2,3},{4,5},{5,6},{6,7},{8,9},{9,10},{10,11},{12,13},{... | collective-permute-start | bytes 983048 | tf_op jit(solution)/shard_map/ppermute | solution.py:44
  92.6 5.3 %collective-permute-start.12 = (bf16[64,2560]{1,0:T(8,128)(2,1)}, bf16[64,2560]{1,0:T(8,128)(2,1)}, u32[]{:S(2)}, u32[]{:S(2)}) collective-permute-start(bf16[64,2560]{1,0:T(8,128)(2,1)} %unit_gradient.6.refs_0_), channel_id=1, source_target_pairs={{0,1},{1,2},{2,3},{4,5},{5,6},{6,7},{8,9},{9,10},{10,11},{12,13},{... | collective-permute-start | bytes 983048 | tf_op jit(solution)/shard_map/ppermute | solution.py:44
  97.9 2.5 collective-permute-done.39.left_ref
  102.8 5.3 %collective-permute-start.40 = (bf16[64,2560]{1,0:T(8,128)(2,1)}, bf16[64,2560]{1,0:T(8,128)(2,1)}, u32[]{:S(2)}, u32[]{:S(2)}) collective-permute-start(bf16[64,2560]{1,0:T(8,128)(2,1)} %unit_gradient.9.refs_7_), channel_id=1, source_target_pairs={{0,1},{1,2},{2,3},{4,5},{5,6},{6,7},{8,9},{9,10},{10,11},{12,13},{... | collective-permute-start | bytes 983048 | tf_op jit(solution)/shard_map/ppermute | solution.py:44
  108.2 3.7 partial_products.7
  111.9 2.6 next_payload.18
  117.3 3.3 partial_products.10
  120.6 2.5 next_payload.26
  123.1 5.4 %collective-permute-start.42 = (bf16[64,2560]{1,0:T(8,128)(2,1)}, bf16[64,2560]{1,0:T(8,128)(2,1)}, u32[]{:S(2)}, u32[]{:S(2)}) collective-permute-start(bf16[64,2560]{1,0:T(8,128)(2,1)} %get-tuple-element.503), channel_id=1, source_target_pairs={{0,1},{1,2},{2,3},{4,5},{5,6},{6,7},{8,9},{9,10},{10,11},{12,13},{... | collective-permute-start | bytes 983048 | tf_op jit(solution)/shard_map/ppermute | solution.py:44
  133.1 4.2 %all-to-all-start.5 = ((bf16[4,128,640]{2,1,0:T(8,128)(2,1)}), bf16[4,128,640]{2,1,0:T(8,128)(2,1)}, u32[]{:S(2)}, u32[]{:S(2)}) async-start(bf16[4,128,640]{2,1,0:T(8,128)(2,1)} %copy-done.12), calls=%async_computation.5 | async-start | bytes 1310720 | tf_op jit(solution)/shard_map/all_to_all | solution.py:434
  137.3 3.5 collective-permute-done.43.left_ref.refs_12_
  142.1 2.4 next_payload.27
  144.4 6.9 %collective-permute-start.44 = (bf16[64,2560]{1,0:T(8,128)(2,1)S(1)}, bf16[64,2560]{1,0:T(8,128)(2,1)S(1)}, u32[]{:S(2)}, u32[]{:S(2)}) collective-permute-start(bf16[64,2560]{1,0:T(8,128)(2,1)S(1)} %get-tuple-element.505), channel_id=1, source_target_pairs={{0,1},{1,2},{2,3},{4,5},{5,6},{6,7},{8,9},{9,10},{10,11},{12,13},{... | collective-permute-start | bytes 983048 | tf_op jit(solution)/shard_map/ppermute | solution.py:44
  152.7 4.6 %collective-permute-start.16 = (bf16[64,2560]{1,0:T(8,128)(2,1)S(1)}, bf16[64,2560]{1,0:T(8,128)(2,1)S(1)}, u32[]{:S(2)}, u32[]{:S(2)}) collective-permute-start(bf16[64,2560]{1,0:T(8,128)(2,1)S(1)} %copy-done.18), channel_id=1, source_target_pairs={{0,1},{1,2},{2,3},{4,5},{5,6},{6,7},{8,9},{9,10},{10,11},{12,13},{... | collective-permute-start | bytes 983048 | tf_op jit(solution)/shard_map/ppermute | solution.py:44
  158.6 1.8 collective-permute-done.45.left_ref.refs_13_
  161.9 3.3 collective-permute-start.46
  166.5 3.2 collective-permute-done.17.left_ref.refs_6_
  170.5 1.9 collective-permute-start.18
  173.7 4.0 %collective-permute-done.47.left_ref = bf16[64,2560]{1,0:T(8,128)(2,1)S(1)} collective-permute-done((bf16[64,2560]{1,0:T(8,128)(2,1)S(1)}, bf16[64,2560]{1,0:T(8,128)(2,1)S(1)}, u32[]{:S(2)}, u32[]{:S(2)}) %collective-permute-start.47) | collective-permute-done | bytes 327712 | tf_op jit(solution)/shard_map/ppermute | solution.py:44
  180.2 5.3 %collective-permute-start.48 = (bf16[64,2560]{1,0:T(8,128)(2,1)}, bf16[64,2560]{1,0:T(8,128)(2,1)}, u32[]{:S(2)}, u32[]{:S(2)}) collective-permute-start(bf16[64,2560]{1,0:T(8,128)(2,1)} %unit_gradient.10.refs_21_), channel_id=1, source_target_pairs={{0,1},{1,2},{2,3},{4,5},{5,6},{6,7},{8,9},{9,10},{10,11},{12,13},{... | collective-permute-start | bytes 983048 | tf_op jit(solution)/shard_map/ppermute | solution.py:44
  187.9 5.3 %collective-permute-start.20 = (bf16[64,2560]{1,0:T(8,128)(2,1)}, bf16[64,2560]{1,0:T(8,128)(2,1)}, u32[]{:S(2)}, u32[]{:S(2)}) collective-permute-start(bf16[64,2560]{1,0:T(8,128)(2,1)} %unit_gradient.7.refs_14_), channel_id=1, source_target_pairs={{0,1},{1,2},{2,3},{4,5},{5,6},{6,7},{8,9},{9,10},{10,11},{12,13},{... | collective-permute-start | bytes 983048 | tf_op jit(solution)/shard_map/ppermute | solution.py:44
  193.2 3.7 partial_products.11
  196.9 2.6 next_payload.29
  202.1 3.3 partial_products.8
  205.5 2.3 next_payload.21
  207.8 4.6 %collective-permute-start.22 = (bf16[64,2560]{1,0:T(8,128)(2,1)S(1)}, bf16[64,2560]{1,0:T(8,128)(2,1)S(1)}, u32[]{:S(2)}, u32[]{:S(2)}) collective-permute-start(bf16[64,2560]{1,0:T(8,128)(2,1)S(1)} %get-tuple-element.488), channel_id=1, source_target_pairs={{0,1},{1,2},{2,3},{4,5},{5,6},{6,7},{8,9},{9,10},{10,11},{12,13},{... | collective-permute-start | bytes 983048 | tf_op jit(solution)/shard_map/ppermute | solution.py:44
  215.0 4.6 %collective-permute-start.52 = (bf16[64,2560]{1,0:T(8,128)(2,1)S(1)}, bf16[64,2560]{1,0:T(8,128)(2,1)S(1)}, u32[]{:S(2)}, u32[]{:S(2)}) collective-permute-start(bf16[64,2560]{1,0:T(8,128)(2,1)S(1)} %get-tuple-element.513), channel_id=1, source_target_pairs={{0,1},{1,2},{2,3},{4,5},{5,6},{6,7},{8,9},{9,10},{10,11},{12,13},{... | collective-permute-start | bytes 983048 | tf_op jit(solution)/shard_map/ppermute | solution.py:44
  223.3 3.5 collective-permute-start.24
  231.0 3.2 collective-permute-start.54
  235.5 1.9 collective-permute-done.25.left_ref.refs_20_
  238.8 2.6 collective-permute-start.26
  242.8 4.0 %collective-permute-done.55.left_ref = bf16[64,2560]{1,0:T(8,128)(2,1)S(1)} collective-permute-done((bf16[64,2560]{1,0:T(8,128)(2,1)S(1)}, bf16[64,2560]{1,0:T(8,128)(2,1)S(1)}, u32[]{:S(2)}, u32[]{:S(2)}) %collective-permute-start.55) | collective-permute-done | bytes 327712 | tf_op jit(solution)/shard_map/ppermute | solution.py:44
  247.3 1.6 collective-permute-start.57
  248.9 4.6 %collective-permute-start.56 = (bf16[64,2560]{1,0:T(8,128)(2,1)S(1)}, bf16[64,2560]{1,0:T(8,128)(2,1)S(1)}, u32[]{:S(2)}, u32[]{:S(2)}) collective-permute-start(bf16[64,2560]{1,0:T(8,128)(2,1)S(1)} %unit_gradient.11.refs_7_), channel_id=1, source_target_pairs={{0,1},{1,2},{2,3},{4,5},{5,6},{6,7},{8,9},{9,10},{10,11},{12,13},{... | collective-permute-start | bytes 983048 | tf_op jit(solution)/shard_map/ppermute | solution.py:44
  255.4 4.6 %collective-permute-start.28 = (bf16[64,2560]{1,0:T(8,128)(2,1)S(1)}, bf16[64,2560]{1,0:T(8,128)(2,1)S(1)}, u32[]{:S(2)}, u32[]{:S(2)}) collective-permute-start(bf16[64,2560]{1,0:T(8,128)(2,1)S(1)} %unit_gradient.8.refs_0_), channel_id=1, source_target_pairs={{0,1},{1,2},{2,3},{4,5},{5,6},{6,7},{8,9},{9,10},{10,11},{12,13},{... | collective-permute-start | bytes 983048 | tf_op jit(solution)/shard_map/ppermute | solution.py:44
  260.1 10.8 %weight_step.2 = (f32[640,2560]{1,0:T(8,128)}, f32[8,128]{1,0:T(8,128)S(1)}) custom-call(s32[4]{0:T(128)S(1)} %and_select_fusion.s, bf16[64,2560]{1,0:T(8,128)(2,1)} %unit_gradient.6.refs_0_, bf16[64,2560]{1,0:T(8,128)(2,1)} %collective-permute-done.12.right_ref.refs_1_, bf16[64,2560]{1,0:T(8,128)(2,1)S(1)} %copy-done.32, bf16[64,2560]{1,0:T(8,128)(2,1)S(1)} %copy-done.44, ...), custom_call_target="tpu_custom_call" | custom-call | flops 3355443200 | bytes 28835840 | tf_op jit(solution)/shard_map/weight_step/pallas_call | solution.py:16
  275.1 6.5 %collective-permute-done.32.refs_5_ = bf16[64,2560]{1,0:T(8,128)(2,1)S(1)} collective-permute-done((bf16[64,2560]{1,0:T(8,128)(2,1)S(1)}, bf16[64,2560]{1,0:T(8,128)(2,1)S(1)}, u32[]{:S(2)}, u32[]{:S(2)}) %collective-permute-start.32) | collective-permute-done | bytes 327712 | tf_op jit(solution)/shard_map/ppermute | solution.py:44
  284.3 1.8 collective-permute-done.60.refs_12_
  288.7 1.8 collective-permute-done.33.refs_6_
  290.6 4.5 %collective-permute-done.61.refs_13_ = bf16[64,2560]{1,0:T(8,128)(2,1)S(1)} collective-permute-done((bf16[64,2560]{1,0:T(8,128)(2,1)S(1)}, bf16[64,2560]{1,0:T(8,128)(2,1)S(1)}, u32[]{:S(2)}, u32[]{:S(2)}) %collective-permute-start.61) | collective-permute-done | bytes 327712 | tf_op jit(solution)/shard_map/ppermute | solution.py:44
  296.1 14.1 %weight_step.3 = (f32[640,2560]{1,0:T(8,128)}, bf16[640,2560]{1,0:T(8,128)(2,1)}) custom-call(s32[4]{0:T(128)S(1)} %and_select_fusion.s, bf16[64,2560]{1,0:T(8,128)(2,1)} %copy-done.25, bf16[64,2560]{1,0:T(8,128)(2,1)} %copy-done.67, bf16[64,2560]{1,0:T(8,128)(2,1)} %copy-done.71, bf16[64,2560]{1,0:T(8,128)(2,1)} %copy-done.79, bf16[64,2560]{1,0:T(8,128)(2,1)} %copy-done.65, ...), custom_call_target="tpu_custom_call" | custom-call | flops 1677721600 | bytes 24248320 | tf_op jit(solution)/shard_map/weight_step/pallas_call | solution.py:16
  310.5 65.4 %conditional.1 = (bf16[640,2560]{1,0:T(8,128)(2,1)}, bf16[1,384,2560]{2,1,0:T(8,128)(2,1)}) conditional(s32[]{:T(128)} %clamp.3, (bf16[640,2560]{1,0:T(8,128)(2,1)}, s32[4]{0:T(128)S(1)}, bf16[64,2560]{1,0:T(8,128)(2,1)}, bf16[64,2560]{1,0:T(8,128)(2,1)}, bf16[64,2560]{1,0:T(8,128)(2,1)S(1)}, ...), branch_computations={%region_1.2_spmd, %region_2.3_spmd, %region_3.4_spmd} | conditional | flops 5033164800 | bytes 38010936 | solution.py:566
  310.6 14.1 %grad_rows.3 = bf16[4,384,640]{2,1,0:T(8,128)(2,1)S(1)} custom-call(s32[4]{0:T(128)S(1)} %get-tuple-element.272.s, bf16[64,2560]{1,0:T(8,128)(2,1)} %get-tuple-element.273.refs_0_, bf16[64,2560]{1,0:T(8,128)(2,1)} %get-tuple-element.274.refs_1_, bf16[64,2560]{1,0:T(8,128)(2,1)S(1)} %get-tuple-element.275.refs_2_, ...), custom_call_target="tpu_custom_call" | custom-call | flops 5033164800 | bytes 17039360 | tf_op jit(solution)/shard_map/cond/branch_0_fun/grad_rows/pallas_call | solution.py:16
  324.7 49.3 %all_to_all.27.blocks_ref = bf16[4,384,640]{2,1,0:T(8,128)(2,1)S(1)} all-to-all(bf16[4,384,640]{2,1,0:T(8,128)(2,1)S(1)} %grad_rows.3), channel_id=1, replica_groups=mesh['rep'=8,'fsdp'=4] {'fsdp'}, dimensions={0} | all-to-all | bytes 3932160 | tf_op jit(solution)/shard_map/cond/branch_0_fun/all_to_all | solution.py:434
  373.9 1.9 joined_rows.3
  375.9 4.4 %widened.1 = f32[640,2560]{1,0:T(8,128)} custom-call(bf16[640,2560]{1,0:T(8,128)(2,1)} %get-tuple-element.523.value_ref), custom_call_target="tpu_custom_call" | custom-call | bytes 9830400 | tf_op jit(solution)/shard_map/widened/pallas_call | solution.py:16
  (281 shorter events, 68.3 us)
Async XLA Ops:
  2.5 23.6 %all-to-all-start.3 = ((bf16[4,128,640]{2,1,0:T(8,128)(2,1)}), bf16[4,128,640]{2,1,0:T(8,128)(2,1)S(1)}, u32[]{:S(2)}, u32[]{:S(2)}) async-start(bf16[4,128,640]{2,1,0:T(8,128)(2,1)} %cut_heads.3), calls=%async_computation.3 | async-start | bytes 1310720 | tf_op jit(solution)/shard_map/all_to_all | solution.py:434
  9.5 8.4 %collective-permute-start.5 = (f32[1]{0:T(128)}, f32[1]{0:T(128)}, u32[]{:S(2)}, u32[]{:S(2)}) collective-permute-start(f32[1]{0:T(128)} %mul.4), channel_id=1, source_target_pairs={{0,4},{4,8},{8,12},{12,16},{16,20},{20,24},{24,28},{28,0},{1,5},{5... | collective-permute-start | bytes 20 | tf_op jit(solution)/shard_map/ppermute | solution.py:464
  10.3 7.6 %collective-permute-start.4 = (f32[1]{0:T(128)}, f32[1]{0:T(128)}, u32[]{:S(2)}, u32[]{:S(2)}) collective-permute-start(f32[1]{0:T(128)} %mul.4), channel_id=1, source_target_pairs={{0,8},{4,12},{8,16},{12,20},{16,24},{20,28},{24,0},{28,4},{1,9},{5... | collective-permute-start | bytes 20 | tf_op jit(solution)/shard_map/ppermute | solution.py:464
  13.1 6.1 %collective-permute-start.3 = (f32[1]{0:T(128)}, f32[1]{0:T(128)}, u32[]{:S(2)}, u32[]{:S(2)}) collective-permute-start(f32[1]{0:T(128)} %mul.4), channel_id=1, source_target_pairs={{0,16},{4,20},{8,24},{12,28},{16,0},{20,4},{24,8},{28,12},{1,17},{... | collective-permute-start | bytes 20 | tf_op jit(solution)/shard_map/ppermute | solution.py:464
  30.0 12.0 %collective-permute-start.6 = (bf16[64,2560]{1,0:T(8,128)(2,1)}, bf16[64,2560]{1,0:T(8,128)(2,1)}, u32[]{:S(2)}, u32[]{:S(2)}) collective-permute-start(bf16[64,2560]{1,0:T(8,128)(2,1)} %get-tuple-element.469), channel_id=1, source_target_pairs={{0,1},{4,5},{8,9},{12,13},{16,17},{20,21},{24,25},{28,29}} | collective-permute-start | bytes 983048 | tf_op jit(solution)/shard_map/ppermute | solution.py:44
  34.6 7.4 %collective-permute-start.7 = (bf16[64,2560]{1,0:T(8,128)(2,1)}, bf16[64,2560]{1,0:T(8,128)(2,1)}, u32[]{:S(2)}, u32[]{:S(2)}) collective-permute-start(bf16[64,2560]{1,0:T(8,128)(2,1)} %get-tuple-element.470), channel_id=1, source_target_pairs={{3,2},{7,6},{11,10},{15,14},{19,18},{23,22},{27,26},{31,30}} | collective-permute-start | bytes 983048 | tf_op jit(solution)/shard_map/ppermute | solution.py:44
  38.5 18.9 %collective-permute-start.34 = (bf16[64,2560]{1,0:T(8,128)(2,1)}, bf16[64,2560]{1,0:T(8,128)(2,1)}, u32[]{:S(2)}, u32[]{:S(2)}) collective-permute-start(bf16[64,2560]{1,0:T(8,128)(2,1)} %get-tuple-element.494), channel_id=1, source_target_pairs={{0,1},{4,5},{8,9},{12,13},{16,17},{20,21},{24,25},{28,29}} | collective-permute-start | bytes 983048 | tf_op jit(solution)/shard_map/ppermute | solution.py:44
  40.5 16.9 %collective-permute-start.35 = (bf16[64,2560]{1,0:T(8,128)(2,1)}, bf16[64,2560]{1,0:T(8,128)(2,1)}, u32[]{:S(2)}, u32[]{:S(2)}) collective-permute-start(bf16[64,2560]{1,0:T(8,128)(2,1)} %get-tuple-element.495), channel_id=1, source_target_pairs={{3,2},{7,6},{11,10},{15,14},{19,18},{23,22},{27,26},{31,30}} | collective-permute-start | bytes 983048 | tf_op jit(solution)/shard_map/ppermute | solution.py:44
  46.1 62.0 %all-to-all-start.4 = ((bf16[4,128,640]{2,1,0:T(8,128)(2,1)}), bf16[4,128,640]{2,1,0:T(8,128)(2,1)}, u32[]{:S(2)}, u32[]{:S(2)}) async-start(bf16[4,128,640]{2,1,0:T(8,128)(2,1)} %cut_heads.4), calls=%async_computation.4 | async-start | bytes 1310720 | tf_op jit(solution)/shard_map/all_to_all | solution.py:434
  51.3 19.0 %collective-permute-start.8 = (bf16[64,2560]{1,0:T(8,128)(2,1)}, bf16[64,2560]{1,0:T(8,128)(2,1)}, u32[]{:S(2)}, u32[]{:S(2)}) collective-permute-start(bf16[64,2560]{1,0:T(8,128)(2,1)} %copy-done.14), channel_id=1, source_target_pairs={{0,1},{1,2},{4,5},{5,6},{8,9},{9,10},{12,13},{13,14},{16,17},{17,1... | collective-permute-start | bytes 983048 | tf_op jit(solution)/shard_map/ppermute | solution.py:44
  56.0 14.3 %collective-permute-start.9 = (bf16[64,2560]{1,0:T(8,128)(2,1)}, bf16[64,2560]{1,0:T(8,128)(2,1)}, u32[]{:S(2)}, u32[]{:S(2)}) collective-permute-start(bf16[64,2560]{1,0:T(8,128)(2,1)} %copy-done.13), channel_id=1, source_target_pairs={{2,1},{3,2},{6,5},{7,6},{10,9},{11,10},{14,13},{15,14},{18,17},{19... | collective-permute-start | bytes 983048 | tf_op jit(solution)/shard_map/ppermute | solution.py:44
  60.0 21.5 %collective-permute-start.36 = (bf16[64,2560]{1,0:T(8,128)(2,1)}, bf16[64,2560]{1,0:T(8,128)(2,1)}, u32[]{:S(2)}, u32[]{:S(2)}) collective-permute-start(bf16[64,2560]{1,0:T(8,128)(2,1)} %get-tuple-element.497), channel_id=1, source_target_pairs={{0,1},{1,2},{4,5},{5,6},{8,9},{9,10},{12,13},{13,14},{16,17},{17,1... | collective-permute-start | bytes 983048 | tf_op jit(solution)/shard_map/ppermute | solution.py:44
  63.2 18.3 %collective-permute-start.37 = (bf16[64,2560]{1,0:T(8,128)(2,1)}, bf16[64,2560]{1,0:T(8,128)(2,1)}, u32[]{:S(2)}, u32[]{:S(2)}) collective-permute-start(bf16[64,2560]{1,0:T(8,128)(2,1)} %get-tuple-element.498), channel_id=1, source_target_pairs={{2,1},{3,2},{6,5},{7,6},{10,9},{11,10},{14,13},{15,14},{18,17},{19... | collective-permute-start | bytes 983048 | tf_op jit(solution)/shard_map/ppermute | solution.py:44
  72.2 16.9 %collective-permute-start.10 = (bf16[64,2560]{1,0:T(8,128)(2,1)S(1)}, bf16[64,2560]{1,0:T(8,128)(2,1)S(1)}, u32[]{:S(2)}, u32[]{:S(2)}) collective-permute-start(bf16[64,2560]{1,0:T(8,128)(2,1)S(1)} %get-tuple-element.474), channel_id=1, source_target_pairs={{0,1},{1,2},{2,3},{4,5},{5,6},{6,7},{8,9},{9,10},{10,11},{12,13},{... | collective-permute-start | bytes 983048 | tf_op jit(solution)/shard_map/ppermute | solution.py:44
  80.1 10.0 %collective-permute-start.11 = (bf16[64,2560]{1,0:T(8,128)(2,1)S(1)}, bf16[64,2560]{1,0:T(8,128)(2,1)S(1)}, u32[]{:S(2)}, u32[]{:S(2)}) collective-permute-start(bf16[64,2560]{1,0:T(8,128)(2,1)S(1)} %get-tuple-element.475), channel_id=1, source_target_pairs={{1,0},{2,1},{3,2},{5,4},{6,5},{7,6},{9,8},{10,9},{11,10},{13,12},{... | collective-permute-start | bytes 983048 | tf_op jit(solution)/shard_map/ppermute | solution.py:44
  83.3 14.6 %collective-permute-start.38 = (bf16[64,2560]{1,0:T(8,128)(2,1)S(1)}, bf16[64,2560]{1,0:T(8,128)(2,1)S(1)}, u32[]{:S(2)}, u32[]{:S(2)}) collective-permute-start(bf16[64,2560]{1,0:T(8,128)(2,1)S(1)} %get-tuple-element.499), channel_id=1, source_target_pairs={{0,1},{1,2},{2,3},{4,5},{5,6},{6,7},{8,9},{9,10},{10,11},{12,13},{... | collective-permute-start | bytes 983048 | tf_op jit(solution)/shard_map/ppermute | solution.py:44
  87.8 12.5 %collective-permute-start.39 = (bf16[64,2560]{1,0:T(8,128)(2,1)S(1)}, bf16[64,2560]{1,0:T(8,128)(2,1)S(1)}, u32[]{:S(2)}, u32[]{:S(2)}) collective-permute-start(bf16[64,2560]{1,0:T(8,128)(2,1)S(1)} %get-tuple-element.500), channel_id=1, source_target_pairs={{1,0},{2,1},{3,2},{5,4},{6,5},{7,6},{9,8},{10,9},{11,10},{13,12},{... | collective-permute-start | bytes 983048 | tf_op jit(solution)/shard_map/ppermute | solution.py:44
  91.3 20.6 %collective-permute-start.13 = (bf16[64,2560]{1,0:T(8,128)(2,1)}, bf16[64,2560]{1,0:T(8,128)(2,1)}, u32[]{:S(2)}, u32[]{:S(2)}) collective-permute-start(bf16[64,2560]{1,0:T(8,128)(2,1)} %unit_gradient.6.refs_0_), channel_id=1, source_target_pairs={{1,0},{2,1},{3,2},{5,4},{6,5},{7,6},{9,8},{10,9},{11,10},{13,12},{... | collective-permute-start | bytes 983048 | tf_op jit(solution)/shard_map/ppermute | solution.py:44
  92.6 19.3 %collective-permute-start.12 = (bf16[64,2560]{1,0:T(8,128)(2,1)}, bf16[64,2560]{1,0:T(8,128)(2,1)}, u32[]{:S(2)}, u32[]{:S(2)}) collective-permute-start(bf16[64,2560]{1,0:T(8,128)(2,1)} %unit_gradient.6.refs_0_), channel_id=1, source_target_pairs={{0,1},{1,2},{2,3},{4,5},{5,6},{6,7},{8,9},{9,10},{10,11},{12,13},{... | collective-permute-start | bytes 983048 | tf_op jit(solution)/shard_map/ppermute | solution.py:44
  101.5 19.1 %collective-permute-start.41 = (bf16[64,2560]{1,0:T(8,128)(2,1)}, bf16[64,2560]{1,0:T(8,128)(2,1)}, u32[]{:S(2)}, u32[]{:S(2)}) collective-permute-start(bf16[64,2560]{1,0:T(8,128)(2,1)} %unit_gradient.9.refs_7_), channel_id=1, source_target_pairs={{1,0},{2,1},{3,2},{5,4},{6,5},{7,6},{9,8},{10,9},{11,10},{13,12},{... | collective-permute-start | bytes 983048 | tf_op jit(solution)/shard_map/ppermute | solution.py:44
  102.8 17.8 %collective-permute-start.40 = (bf16[64,2560]{1,0:T(8,128)(2,1)}, bf16[64,2560]{1,0:T(8,128)(2,1)}, u32[]{:S(2)}, u32[]{:S(2)}) collective-permute-start(bf16[64,2560]{1,0:T(8,128)(2,1)} %unit_gradient.9.refs_7_), channel_id=1, source_target_pairs={{0,1},{1,2},{2,3},{4,5},{5,6},{6,7},{8,9},{9,10},{10,11},{12,13},{... | collective-permute-start | bytes 983048 | tf_op jit(solution)/shard_map/ppermute | solution.py:44
  114.5 15.3 %collective-permute-start.14 = (bf16[64,2560]{1,0:T(8,128)(2,1)S(1)}, bf16[64,2560]{1,0:T(8,128)(2,1)S(1)}, u32[]{:S(2)}, u32[]{:S(2)}) collective-permute-start(bf16[64,2560]{1,0:T(8,128)(2,1)S(1)} %get-tuple-element.479), channel_id=1, source_target_pairs={{0,1},{1,2},{2,3},{4,5},{5,6},{6,7},{8,9},{9,10},{10,11},{12,13},{... | collective-permute-start | bytes 983048 | tf_op jit(solution)/shard_map/ppermute | solution.py:44
  116.0 13.8 %collective-permute-start.15 = (bf16[64,2560]{1,0:T(8,128)(2,1)S(1)}, bf16[64,2560]{1,0:T(8,128)(2,1)S(1)}, u32[]{:S(2)}, u32[]{:S(2)}) collective-permute-start(bf16[64,2560]{1,0:T(8,128)(2,1)S(1)} %get-tuple-element.480), channel_id=1, source_target_pairs={{1,0},{2,1},{3,2},{5,4},{6,5},{7,6},{9,8},{10,9},{11,10},{13,12},{... | collective-permute-start | bytes 983048 | tf_op jit(solution)/shard_map/ppermute | solution.py:44
  123.1 14.2 %collective-permute-start.42 = (bf16[64,2560]{1,0:T(8,128)(2,1)}, bf16[64,2560]{1,0:T(8,128)(2,1)}, u32[]{:S(2)}, u32[]{:S(2)}) collective-permute-start(bf16[64,2560]{1,0:T(8,128)(2,1)} %get-tuple-element.503), channel_id=1, source_target_pairs={{0,1},{1,2},{2,3},{4,5},{5,6},{6,7},{8,9},{9,10},{10,11},{12,13},{... | collective-permute-start | bytes 983048 | tf_op jit(solution)/shard_map/ppermute | solution.py:44
  128.5 12.3 %collective-permute-start.43 = (bf16[64,2560]{1,0:T(8,128)(2,1)}, bf16[64,2560]{1,0:T(8,128)(2,1)}, u32[]{:S(2)}, u32[]{:S(2)}) collective-permute-start(bf16[64,2560]{1,0:T(8,128)(2,1)} %get-tuple-element.504), channel_id=1, source_target_pairs={{1,0},{2,1},{3,2},{5,4},{6,5},{7,6},{9,8},{10,9},{11,10},{13,12},{... | collective-permute-start | bytes 983048 | tf_op jit(solution)/shard_map/ppermute | solution.py:44
  133.1 60.1 %all-to-all-start.5 = ((bf16[4,128,640]{2,1,0:T(8,128)(2,1)}), bf16[4,128,640]{2,1,0:T(8,128)(2,1)}, u32[]{:S(2)}, u32[]{:S(2)}) async-start(bf16[4,128,640]{2,1,0:T(8,128)(2,1)} %copy-done.12), calls=%async_computation.5 | async-start | bytes 1310720 | tf_op jit(solution)/shard_map/all_to_all | solution.py:434
  144.4 14.1 %collective-permute-start.44 = (bf16[64,2560]{1,0:T(8,128)(2,1)S(1)}, bf16[64,2560]{1,0:T(8,128)(2,1)S(1)}, u32[]{:S(2)}, u32[]{:S(2)}) collective-permute-start(bf16[64,2560]{1,0:T(8,128)(2,1)S(1)} %get-tuple-element.505), channel_id=1, source_target_pairs={{0,1},{1,2},{2,3},{4,5},{5,6},{6,7},{8,9},{9,10},{10,11},{12,13},{... | collective-permute-start | bytes 983048 | tf_op jit(solution)/shard_map/ppermute | solution.py:44
  151.3 9.0 %collective-permute-start.45 = (bf16[64,2560]{1,0:T(8,128)(2,1)S(1)}, bf16[64,2560]{1,0:T(8,128)(2,1)S(1)}, u32[]{:S(2)}, u32[]{:S(2)}) collective-permute-start(bf16[64,2560]{1,0:T(8,128)(2,1)S(1)} %get-tuple-element.506), channel_id=1, source_target_pairs={{1,0},{2,1},{3,2},{5,4},{6,5},{7,6},{9,8},{10,9},{11,10},{13,12},{... | collective-permute-start | bytes 983048 | tf_op jit(solution)/shard_map/ppermute | solution.py:44
  152.7 13.8 %collective-permute-start.16 = (bf16[64,2560]{1,0:T(8,128)(2,1)S(1)}, bf16[64,2560]{1,0:T(8,128)(2,1)S(1)}, u32[]{:S(2)}, u32[]{:S(2)}) collective-permute-start(bf16[64,2560]{1,0:T(8,128)(2,1)S(1)} %copy-done.18), channel_id=1, source_target_pairs={{0,1},{1,2},{2,3},{4,5},{5,6},{6,7},{8,9},{9,10},{10,11},{12,13},{... | collective-permute-start | bytes 983048 | tf_op jit(solution)/shard_map/ppermute | solution.py:44
  157.2 12.4 %collective-permute-start.17 = (bf16[64,2560]{1,0:T(8,128)(2,1)S(1)}, bf16[64,2560]{1,0:T(8,128)(2,1)S(1)}, u32[]{:S(2)}, u32[]{:S(2)}) collective-permute-start(bf16[64,2560]{1,0:T(8,128)(2,1)S(1)} %copy-done.16), channel_id=1, source_target_pairs={{1,0},{2,1},{3,2},{5,4},{6,5},{7,6},{9,8},{10,9},{11,10},{13,12},{... | collective-permute-start | bytes 983048 | tf_op jit(solution)/shard_map/ppermute | solution.py:44
  161.9 11.8 %collective-permute-start.46 = (bf16[64,2560]{1,0:T(8,128)(2,1)S(1)}, bf16[64,2560]{1,0:T(8,128)(2,1)S(1)}, u32[]{:S(2)}, u32[]{:S(2)}) collective-permute-start(bf16[64,2560]{1,0:T(8,128)(2,1)S(1)} %get-tuple-element.507), channel_id=1, source_target_pairs={{0,1},{1,2},{2,3},{4,5},{5,6},{6,7},{8,9},{9,10},{10,11},{12,13},{... | collective-permute-start | bytes 983048 | tf_op jit(solution)/shard_map/ppermute | solution.py:44
  165.2 12.5 %collective-permute-start.47 = (bf16[64,2560]{1,0:T(8,128)(2,1)S(1)}, bf16[64,2560]{1,0:T(8,128)(2,1)S(1)}, u32[]{:S(2)}, u32[]{:S(2)}) collective-permute-start(bf16[64,2560]{1,0:T(8,128)(2,1)S(1)} %get-tuple-element.508), channel_id=1, source_target_pairs={{1,0},{2,1},{3,2},{5,4},{6,5},{7,6},{9,8},{10,9},{11,10},{13,12},{... | collective-permute-start | bytes 983048 | tf_op jit(solution)/shard_map/ppermute | solution.py:44
  170.5 15.0 %collective-permute-start.18 = (bf16[64,2560]{1,0:T(8,128)(2,1)S(1)}, bf16[64,2560]{1,0:T(8,128)(2,1)S(1)}, u32[]{:S(2)}, u32[]{:S(2)}) collective-permute-start(bf16[64,2560]{1,0:T(8,128)(2,1)S(1)} %get-tuple-element.483), channel_id=1, source_target_pairs={{0,1},{1,2},{2,3},{4,5},{5,6},{6,7},{8,9},{9,10},{10,11},{12,13},{... | collective-permute-start | bytes 983048 | tf_op jit(solution)/shard_map/ppermute | solution.py:44
  172.4 13.1 %collective-permute-start.19 = (bf16[64,2560]{1,0:T(8,128)(2,1)S(1)}, bf16[64,2560]{1,0:T(8,128)(2,1)S(1)}, u32[]{:S(2)}, u32[]{:S(2)}) collective-permute-start(bf16[64,2560]{1,0:T(8,128)(2,1)S(1)} %get-tuple-element.484), channel_id=1, source_target_pairs={{1,0},{2,1},{3,2},{5,4},{6,5},{7,6},{9,8},{10,9},{11,10},{13,12},{... | collective-permute-start | bytes 983048 | tf_op jit(solution)/shard_map/ppermute | solution.py:44
  178.9 18.1 %collective-permute-start.49 = (bf16[64,2560]{1,0:T(8,128)(2,1)}, bf16[64,2560]{1,0:T(8,128)(2,1)}, u32[]{:S(2)}, u32[]{:S(2)}) collective-permute-start(bf16[64,2560]{1,0:T(8,128)(2,1)} %unit_gradient.10.refs_21_), channel_id=1, source_target_pairs={{1,0},{2,1},{3,2},{5,4},{6,5},{7,6},{9,8},{10,9},{11,10},{13,12},{... | collective-permute-start | bytes 983048 | tf_op jit(solution)/shard_map/ppermute | solution.py:44
  180.2 16.8 %collective-permute-start.48 = (bf16[64,2560]{1,0:T(8,128)(2,1)}, bf16[64,2560]{1,0:T(8,128)(2,1)}, u32[]{:S(2)}, u32[]{:S(2)}) collective-permute-start(bf16[64,2560]{1,0:T(8,128)(2,1)} %unit_gradient.10.refs_21_), channel_id=1, source_target_pairs={{0,1},{1,2},{2,3},{4,5},{5,6},{6,7},{8,9},{9,10},{10,11},{12,13},{... | collective-permute-start | bytes 983048 | tf_op jit(solution)/shard_map/ppermute | solution.py:44
  186.6 18.8 %collective-permute-start.21 = (bf16[64,2560]{1,0:T(8,128)(2,1)}, bf16[64,2560]{1,0:T(8,128)(2,1)}, u32[]{:S(2)}, u32[]{:S(2)}) collective-permute-start(bf16[64,2560]{1,0:T(8,128)(2,1)} %unit_gradient.7.refs_14_), channel_id=1, source_target_pairs={{1,0},{2,1},{3,2},{5,4},{6,5},{7,6},{9,8},{10,9},{11,10},{13,12},{... | collective-permute-start | bytes 983048 | tf_op jit(solution)/shard_map/ppermute | solution.py:44
  187.9 17.5 %collective-permute-start.20 = (bf16[64,2560]{1,0:T(8,128)(2,1)}, bf16[64,2560]{1,0:T(8,128)(2,1)}, u32[]{:S(2)}, u32[]{:S(2)}) collective-permute-start(bf16[64,2560]{1,0:T(8,128)(2,1)} %unit_gradient.7.refs_14_), channel_id=1, source_target_pairs={{0,1},{1,2},{2,3},{4,5},{5,6},{6,7},{8,9},{9,10},{10,11},{12,13},{... | collective-permute-start | bytes 983048 | tf_op jit(solution)/shard_map/ppermute | solution.py:44
  199.5 14.1 %collective-permute-start.50 = (bf16[64,2560]{1,0:T(8,128)(2,1)S(1)}, bf16[64,2560]{1,0:T(8,128)(2,1)S(1)}, u32[]{:S(2)}, u32[]{:S(2)}) collective-permute-start(bf16[64,2560]{1,0:T(8,128)(2,1)S(1)} %get-tuple-element.511), channel_id=1, source_target_pairs={{0,1},{1,2},{2,3},{4,5},{5,6},{6,7},{8,9},{9,10},{10,11},{12,13},{... | collective-permute-start | bytes 983048 | tf_op jit(solution)/shard_map/ppermute | solution.py:44
  200.8 12.8 %collective-permute-start.51 = (bf16[64,2560]{1,0:T(8,128)(2,1)S(1)}, bf16[64,2560]{1,0:T(8,128)(2,1)S(1)}, u32[]{:S(2)}, u32[]{:S(2)}) collective-permute-start(bf16[64,2560]{1,0:T(8,128)(2,1)S(1)} %get-tuple-element.512), channel_id=1, source_target_pairs={{1,0},{2,1},{3,2},{5,4},{6,5},{7,6},{9,8},{10,9},{11,10},{13,12},{... | collective-permute-start | bytes 983048 | tf_op jit(solution)/shard_map/ppermute | solution.py:44
  207.8 13.1 %collective-permute-start.22 = (bf16[64,2560]{1,0:T(8,128)(2,1)S(1)}, bf16[64,2560]{1,0:T(8,128)(2,1)S(1)}, u32[]{:S(2)}, u32[]{:S(2)}) collective-permute-start(bf16[64,2560]{1,0:T(8,128)(2,1)S(1)} %get-tuple-element.488), channel_id=1, source_target_pairs={{0,1},{1,2},{2,3},{4,5},{5,6},{6,7},{8,9},{9,10},{10,11},{12,13},{... | collective-permute-start | bytes 983048 | tf_op jit(solution)/shard_map/ppermute | solution.py:44
  212.3 9.6 %collective-permute-start.23 = (bf16[64,2560]{1,0:T(8,128)(2,1)S(1)}, bf16[64,2560]{1,0:T(8,128)(2,1)S(1)}, u32[]{:S(2)}, u32[]{:S(2)}) collective-permute-start(bf16[64,2560]{1,0:T(8,128)(2,1)S(1)} %get-tuple-element.489), channel_id=1, source_target_pairs={{1,0},{2,1},{3,2},{5,4},{6,5},{7,6},{9,8},{10,9},{11,10},{13,12},{... | collective-permute-start | bytes 983048 | tf_op jit(solution)/shard_map/ppermute | solution.py:44
  213.7 46.3 %copy-start.49 = (bf16[64,2560]{1,0:T(8,128)(2,1)}, bf16[64,2560]{1,0:T(8,128)(2,1)S(1)}, u32[]{:S(2)}) copy-start(bf16[64,2560]{1,0:T(8,128)(2,1)S(1)} %collective-permute-done.50.right_ref.refs_23_) | copy-start | bytes 983044
  215.0 13.1 %collective-permute-start.52 = (bf16[64,2560]{1,0:T(8,128)(2,1)S(1)}, bf16[64,2560]{1,0:T(8,128)(2,1)S(1)}, u32[]{:S(2)}, u32[]{:S(2)}) collective-permute-start(bf16[64,2560]{1,0:T(8,128)(2,1)S(1)} %get-tuple-element.513), channel_id=1, source_target_pairs={{0,1},{1,2},{2,3},{4,5},{5,6},{6,7},{8,9},{9,10},{10,11},{12,13},{... | collective-permute-start | bytes 983048 | tf_op jit(solution)/shard_map/ppermute | solution.py:44
  219.6 10.1 %collective-permute-start.53 = (bf16[64,2560]{1,0:T(8,128)(2,1)S(1)}, bf16[64,2560]{1,0:T(8,128)(2,1)S(1)}, u32[]{:S(2)}, u32[]{:S(2)}) collective-permute-start(bf16[64,2560]{1,0:T(8,128)(2,1)S(1)} %get-tuple-element.514), channel_id=1, source_target_pairs={{1,0},{2,1},{3,2},{5,4},{6,5},{7,6},{9,8},{10,9},{11,10},{13,12},{... | collective-permute-start | bytes 983048 | tf_op jit(solution)/shard_map/ppermute | solution.py:44
  223.3 12.2 %collective-permute-start.24 = (bf16[64,2560]{1,0:T(8,128)(2,1)S(1)}, bf16[64,2560]{1,0:T(8,128)(2,1)S(1)}, u32[]{:S(2)}, u32[]{:S(2)}) collective-permute-start(bf16[64,2560]{1,0:T(8,128)(2,1)S(1)} %get-tuple-element.490), channel_id=1, source_target_pairs={{0,1},{1,2},{2,3},{4,5},{5,6},{6,7},{8,9},{9,10},{10,11},{12,13},{... | collective-permute-start | bytes 983048 | tf_op jit(solution)/shard_map/ppermute | solution.py:44
  226.8 10.6 %collective-permute-start.25 = (bf16[64,2560]{1,0:T(8,128)(2,1)S(1)}, bf16[64,2560]{1,0:T(8,128)(2,1)S(1)}, u32[]{:S(2)}, u32[]{:S(2)}) collective-permute-start(bf16[64,2560]{1,0:T(8,128)(2,1)S(1)} %get-tuple-element.491), channel_id=1, source_target_pairs={{1,0},{2,1},{3,2},{5,4},{6,5},{7,6},{9,8},{10,9},{11,10},{13,12},{... | collective-permute-start | bytes 983048 | tf_op jit(solution)/shard_map/ppermute | solution.py:44
  231.0 11.7 %collective-permute-start.54 = (bf16[64,2560]{1,0:T(8,128)(2,1)S(1)}, bf16[64,2560]{1,0:T(8,128)(2,1)S(1)}, u32[]{:S(2)}, u32[]{:S(2)}) collective-permute-start(bf16[64,2560]{1,0:T(8,128)(2,1)S(1)} %get-tuple-element.515), channel_id=1, source_target_pairs={{0,1},{1,2},{2,3},{4,5},{5,6},{6,7},{8,9},{9,10},{10,11},{12,13},{... | collective-permute-start | bytes 983048 | tf_op jit(solution)/shard_map/ppermute | solution.py:44
  234.2 12.5 %collective-permute-start.55 = (bf16[64,2560]{1,0:T(8,128)(2,1)S(1)}, bf16[64,2560]{1,0:T(8,128)(2,1)S(1)}, u32[]{:S(2)}, u32[]{:S(2)}) collective-permute-start(bf16[64,2560]{1,0:T(8,128)(2,1)S(1)} %get-tuple-element.516), channel_id=1, source_target_pairs={{1,0},{2,1},{3,2},{5,4},{6,5},{7,6},{9,8},{10,9},{11,10},{13,12},{... | collective-permute-start | bytes 983048 | tf_op jit(solution)/shard_map/ppermute | solution.py:44
  238.8 14.7 %collective-permute-start.26 = (bf16[64,2560]{1,0:T(8,128)(2,1)S(1)}, bf16[64,2560]{1,0:T(8,128)(2,1)S(1)}, u32[]{:S(2)}, u32[]{:S(2)}) collective-permute-start(bf16[64,2560]{1,0:T(8,128)(2,1)S(1)} %get-tuple-element.492), channel_id=1, source_target_pairs={{0,1},{1,2},{2,3},{4,5},{5,6},{6,7},{8,9},{9,10},{10,11},{12,13},{... | collective-permute-start | bytes 983048 | tf_op jit(solution)/shard_map/ppermute | solution.py:44
  241.5 12.0 %collective-permute-start.27 = (bf16[64,2560]{1,0:T(8,128)(2,1)S(1)}, bf16[64,2560]{1,0:T(8,128)(2,1)S(1)}, u32[]{:S(2)}, u32[]{:S(2)}) collective-permute-start(bf16[64,2560]{1,0:T(8,128)(2,1)S(1)} %get-tuple-element.493), channel_id=1, source_target_pairs={{1,0},{2,1},{3,2},{5,4},{6,5},{7,6},{9,8},{10,9},{11,10},{13,12},{... | collective-permute-start | bytes 983048 | tf_op jit(solution)/shard_map/ppermute | solution.py:44
  247.3 25.6 %collective-permute-start.57 = (bf16[64,2560]{1,0:T(8,128)(2,1)S(1)}, bf16[64,2560]{1,0:T(8,128)(2,1)S(1)}, u32[]{:S(2)}, u32[]{:S(2)}) collective-permute-start(bf16[64,2560]{1,0:T(8,128)(2,1)S(1)} %unit_gradient.11.refs_7_), channel_id=1, source_target_pairs={{1,0},{2,1},{3,2},{5,4},{6,5},{7,6},{9,8},{10,9},{11,10},{13,12},{... | collective-permute-start | bytes 983048 | tf_op jit(solution)/shard_map/ppermute | solution.py:44
  248.9 24.1 %collective-permute-start.56 = (bf16[64,2560]{1,0:T(8,128)(2,1)S(1)}, bf16[64,2560]{1,0:T(8,128)(2,1)S(1)}, u32[]{:S(2)}, u32[]{:S(2)}) collective-permute-start(bf16[64,2560]{1,0:T(8,128)(2,1)S(1)} %unit_gradient.11.refs_7_), channel_id=1, source_target_pairs={{0,1},{1,2},{2,3},{4,5},{5,6},{6,7},{8,9},{9,10},{10,11},{12,13},{... | collective-permute-start | bytes 983048 | tf_op jit(solution)/shard_map/ppermute | solution.py:44
  254.1 16.9 %collective-permute-start.31 = (bf16[64,2560]{1,0:T(8,128)(2,1)S(1)}, bf16[64,2560]{1,0:T(8,128)(2,1)S(1)}, u32[]{:S(2)}, u32[]{:S(2)}) collective-permute-start(bf16[64,2560]{1,0:T(8,128)(2,1)S(1)} %unit_gradient.8.refs_0_), channel_id=1, source_target_pairs={{1,0},{2,1},{3,2},{5,4},{6,5},{7,6},{9,8},{10,9},{11,10},{13,12},{... | collective-permute-start | bytes 983048 | tf_op jit(solution)/shard_map/ppermute | solution.py:44
  255.4 16.9 %collective-permute-start.28 = (bf16[64,2560]{1,0:T(8,128)(2,1)S(1)}, bf16[64,2560]{1,0:T(8,128)(2,1)S(1)}, u32[]{:S(2)}, u32[]{:S(2)}) collective-permute-start(bf16[64,2560]{1,0:T(8,128)(2,1)S(1)} %unit_gradient.8.refs_0_), channel_id=1, source_target_pairs={{0,1},{1,2},{2,3},{4,5},{5,6},{6,7},{8,9},{9,10},{10,11},{12,13},{... | collective-permute-start | bytes 983048 | tf_op jit(solution)/shard_map/ppermute | solution.py:44
  271.0 10.6 %collective-permute-start.32 = (bf16[64,2560]{1,0:T(8,128)(2,1)S(1)}, bf16[64,2560]{1,0:T(8,128)(2,1)S(1)}, u32[]{:S(2)}, u32[]{:S(2)}) collective-permute-start(bf16[64,2560]{1,0:T(8,128)(2,1)S(1)} %collective-permute-done.31.refs_4_), channel_id=1, source_target_pairs={{1,0},{2,1},{5,4},{6,5},{9,8},{10,9},{13,12},{14,13},{17,16},{18,1... | collective-permute-start | bytes 983048 | tf_op jit(solution)/shard_map/ppermute | solution.py:44
  272.3 10.6 %collective-permute-start.29 = (bf16[64,2560]{1,0:T(8,128)(2,1)S(1)}, bf16[64,2560]{1,0:T(8,128)(2,1)S(1)}, u32[]{:S(2)}, u32[]{:S(2)}) collective-permute-start(bf16[64,2560]{1,0:T(8,128)(2,1)S(1)} %collective-permute-done.28.refs_1_), channel_id=1, source_target_pairs={{1,2},{2,3},{5,6},{6,7},{9,10},{10,11},{13,14},{14,15},{17,18},{18... | collective-permute-start | bytes 983048 | tf_op jit(solution)/shard_map/ppermute | solution.py:44
  273.1 10.5 %collective-permute-start.58 = (bf16[64,2560]{1,0:T(8,128)(2,1)S(1)}, bf16[64,2560]{1,0:T(8,128)(2,1)S(1)}, u32[]{:S(2)}, u32[]{:S(2)}) collective-permute-start(bf16[64,2560]{1,0:T(8,128)(2,1)S(1)} %get-tuple-element.518), channel_id=1, source_target_pairs={{1,2},{2,3},{5,6},{6,7},{9,10},{10,11},{13,14},{14,15},{17,18},{18... | collective-permute-start | bytes 983048 | tf_op jit(solution)/shard_map/ppermute | solution.py:44
  273.8 12.3 %collective-permute-start.60 = (bf16[64,2560]{1,0:T(8,128)(2,1)S(1)}, bf16[64,2560]{1,0:T(8,128)(2,1)S(1)}, u32[]{:S(2)}, u32[]{:S(2)}) collective-permute-start(bf16[64,2560]{1,0:T(8,128)(2,1)S(1)} %get-tuple-element.519), channel_id=1, source_target_pairs={{1,0},{2,1},{5,4},{6,5},{9,8},{10,9},{13,12},{14,13},{17,16},{18,1... | collective-permute-start | bytes 983048 | tf_op jit(solution)/shard_map/ppermute | solution.py:44
  281.6 9.0 %collective-permute-start.33 = (bf16[64,2560]{1,0:T(8,128)(2,1)S(1)}, bf16[64,2560]{1,0:T(8,128)(2,1)S(1)}, u32[]{:S(2)}, u32[]{:S(2)}) collective-permute-start(bf16[64,2560]{1,0:T(8,128)(2,1)S(1)} %collective-permute-done.32.refs_5_), channel_id=1, source_target_pairs={{1,0},{5,4},{9,8},{13,12},{17,16},{21,20},{25,24},{29,28}} | collective-permute-start | bytes 983048 | tf_op jit(solution)/shard_map/ppermute | solution.py:44
  282.9 7.7 %collective-permute-start.30 = (bf16[64,2560]{1,0:T(8,128)(2,1)S(1)}, bf16[64,2560]{1,0:T(8,128)(2,1)S(1)}, u32[]{:S(2)}, u32[]{:S(2)}) collective-permute-start(bf16[64,2560]{1,0:T(8,128)(2,1)S(1)} %collective-permute-done.29.refs_2_), channel_id=1, source_target_pairs={{2,3},{6,7},{10,11},{14,15},{18,19},{22,23},{26,27},{30,31}} | collective-permute-start | bytes 983048 | tf_op jit(solution)/shard_map/ppermute | solution.py:44
  283.6 6.9 %collective-permute-start.59 = (bf16[64,2560]{1,0:T(8,128)(2,1)S(1)}, bf16[64,2560]{1,0:T(8,128)(2,1)S(1)}, u32[]{:S(2)}, u32[]{:S(2)}) collective-permute-start(bf16[64,2560]{1,0:T(8,128)(2,1)S(1)} %collective-permute-done.58.refs_9_), channel_id=1, source_target_pairs={{2,3},{6,7},{10,11},{14,15},{18,19},{22,23},{26,27},{30,31}} | collective-permute-start | bytes 983048 | tf_op jit(solution)/shard_map/ppermute | solution.py:44
  286.1 9.0 %collective-permute-start.61 = (bf16[64,2560]{1,0:T(8,128)(2,1)S(1)}, bf16[64,2560]{1,0:T(8,128)(2,1)S(1)}, u32[]{:S(2)}, u32[]{:S(2)}) collective-permute-start(bf16[64,2560]{1,0:T(8,128)(2,1)S(1)} %collective-permute-done.60.refs_12_), channel_id=1, source_target_pairs={{1,0},{5,4},{9,8},{13,12},{17,16},{21,20},{25,24},{29,28}} | collective-permute-start | bytes 983048 | tf_op jit(solution)/shard_map/ppermute | solution.py:44
  310.5 65.4 %collective-permute-start = (bf16[640,2560]{1,0:T(8,128)(2,1)}, bf16[640,2560]{1,0:T(8,128)(2,1)}, u32[]{:S(2)}, u32[]{:S(2)}) collective-permute-start(bf16[640,2560]{1,0:T(8,128)(2,1)} %get-tuple-element.271), channel_id=1, source_target_pairs={{0,4},{4,8},{8,12},{12,16},{16,20},{20,24},{24,28},{28,0},{1,5},{5... | collective-permute-start | bytes 9830408 | tf_op jit(solution)/shard_map/cond/branch_0_fun/ppermute | solution.py:439
  (85 other events, 1133.8 us)

commit v4 on v3

--- a/solution.py
+++ b/solution.py
@@ -7,7 +7,7 @@
 from jax.experimental.pallas import tpu as pltpu
 from jax.sharding import PartitionSpec as P
 
-STREAMS = ((64, 64, 64), (64, 64, 64))
+STREAMS = ((96, 96), (96, 96))
 MIB = 1 << 20
 TOKEN = jax.ShapeDtypeStruct((8, 128), jnp.float32)
 
@@ -76,44 +76,43 @@
     )[0]
 
 
-def scaled_weights(numer, weight_one, scaling, token):
+def scaled_weights(numer, weight_one, scaling):
     rows, width = numer.shape
     step = rows // 4
 
-    def body(numer_ref, one_ref, *refs):
-        out_ref, token_out = refs[-2:]
+    def body(numer_ref, one_ref, out_ref):
         out_ref[...] = (numer_ref[...] / one_ref[...] * scaling).astype(jnp.bfloat16)
-        token_out[...] = jnp.zeros((8, 128), jnp.float32)
 
     block = (step, width), lambda i: (i, 0)
     return call(
         body,
         "scaled_weights",
         (rows // step,),
-        [(numer,) + block, (weight_one.reshape(1, 1), (1, 1), fixed(0, 0)), token_in(token)],
-        [((rows, width), jnp.bfloat16) + block, TOKEN_OUT],
+        [(numer,) + block, (weight_one.reshape(1, 1), (1, 1), fixed(0, 0))],
+        [((rows, width), jnp.bfloat16) + block],
         flops=2 * rows * width,
         moved=6 * rows * width,
         vmem=56,
     )[0]
 
 
-def partial_products(mine, weights, token):
+def partial_products(mine, weights, ends):
     mine, index, size = mine
     members, _, rows = mine.shape
     width = weights.shape[1]
     tile = tile_of(width, 1280)
 
-    def body(mine_ref, weights_ref, *refs):
-        out_ref, last_ref, first_ref = refs[-3:]
+    def body(mine_ref, weights_ref, out_ref, token_out, *end_refs):
         product = jnp.dot(
             mine_ref[...].reshape(members * size, rows),
             weights_ref[...],
             preferred_element_type=jnp.float32,
         ).astype(jnp.bfloat16)
         out_ref[...] = product.reshape(members, size, tile)
-        last_ref[...] = product[(members - 1) * size :]
-        first_ref[...] = product[:size]
+        token_out[...] = jnp.zeros((8, 128), jnp.float32)
+        if ends:
+            end_refs[0][...] = product[(members - 1) * size :]
+            end_refs[1][...] = product[:size]
 
     flat = ((size, width), jnp.bfloat16, (size, tile), lambda j: (0, j))
     return call(
@@ -123,18 +122,12 @@
         [
             (mine, (members, size, rows), fixed(0, index, 0)),
             (weights, (rows, tile), lambda j: (0, j)),
+        ],
+        [
+            ((members, size, width), jnp.bfloat16, (members, size, tile), lambda j: (0, 0, j)),
+            TOKEN_OUT,
         ]
-        + ([] if token is None else [token_in(token)]),
-        [
-            (
-                (members, size, width),
-                jnp.bfloat16,
-                (members, size, tile),
-                lambda j: (0, 0, j),
-            ),
-            flat,
-            flat,
-        ],
+        + [flat, flat] * ends,
         flops=2 * members * size * rows * width,
         moved=2 * (members * size * (rows + width) + rows * width),
         vmem=20,
@@ -177,11 +170,11 @@
     )
 
 
-def unit_gradient(right, left, parts, place, residual, cotangent, gain, start):
+def unit_gradient(right, left, parts, place, residual, cotangent, gain, start, token):
     members, size, width = parts.shape
     step = size // 2
 
-    def body(s, right_ref, left_ref, own_ref, residual_ref, cot_ref, gain_ref, out_ref):
+    def body(s, right_ref, left_ref, own_ref, residual_ref, cot_ref, gain_ref, *refs):
         product = (
             right_ref[...].astype(jnp.float32)
             + left_ref[...].astype(jnp.float32)
@@ -191,7 +184,7 @@
         inverse = lax.rsqrt(jnp.mean(summed * summed, axis=-1, keepdims=True) + 1e-05)
         scaled_cot = gain_ref[...] * cot_ref[...].astype(jnp.float32)
         along = jnp.mean(scaled_cot * summed, axis=-1, keepdims=True)
-        out_ref[...] = (
+        refs[-1][...] = (
             inverse * scaled_cot - summed * (inverse * inverse * inverse * along)
         ).astype(jnp.bfloat16)
 
@@ -208,7 +201,8 @@
             (residual,) + there,
             (cotangent,) + there,
             (gain, (1, width), fixed(0, 0)),
-        ],
+        ]
+        + ([] if token is None else [token_in(token)]),
         [((size, width), jnp.bfloat16) + here],
         scalars=(place,),
         flops=12 * size * width,
@@ -259,7 +253,7 @@
     scratch[...] = stack.T
 
 
-def weight_step(units, mine, order, kept, numer, inbox):
+def weight_step(units, mine, order, kept, numer, inbox, token=None):
     members, _, rows = mine[0][0].shape
     width = numer.shape[1] if kept is None else kept.shape[1]
     tile = tile_of(width)
@@ -284,7 +278,7 @@
             kept_out[...] = 0.5 * (numer_ref[...] - 0.004 * weight)
             token_out[...] = jnp.zeros((8, 128), jnp.float32)
         else:
-            kept_ref, inbox_ref, new_out, kept_out = rest
+            kept_ref, inbox_ref, _, new_out, kept_out = rest
             now = kept_ref[...] - 0.5 * 0.004 * weight
             new_out[...] = now + inbox_ref[...]
             kept_out[...] = now.astype(jnp.bfloat16)
@@ -297,7 +291,7 @@
         (width // tile,),
         unit_ins(units, tile)
         + mine_ins(mine)
-        + ([(numer,) + columns] if kept is None else [(kept,) + columns, (inbox,) + columns]),
+        + ([(numer,) + columns] if kept is None else [(kept,) + columns, (inbox,) + columns, token_in(token)]),
         [whole, TOKEN_OUT]
         if kept is None
         else [whole, ((rows, width), jnp.bfloat16) + columns],
@@ -305,7 +299,7 @@
         scratch=[pltpu.VMEM((rows, total), jnp.bfloat16)],
         flops=2 * total * rows * width,
         moved=2 * count * units[0][0].shape[0] * width + 12 * rows * width,
-        vmem=50,
+        vmem=26,
     )
 
 
@@ -459,20 +453,21 @@
     levels = replicas.bit_length() - 1
     powers = jnp.left_shift(jnp.ones((levels,), jnp.int32), jnp.arange(levels, dtype=jnp.int32))
     level_index = jnp.sum(jnp.where(powers == offset[0], jnp.arange(levels, dtype=jnp.int32), 0))
-    half_weight = 0.5 * push_weight
-    arrived = [
-        lax.ppermute(half_weight, "rep", [(i, (i + (1 << b)) % replicas) for i in range(replicas)])
-        for b in range(levels)
-    ]
-    outbox_weight = arrived[0]
-    for b in range(1, levels):
-        outbox_weight = jnp.where(level_index == b, arrived[b], outbox_weight)
+
+    def sent_weight(token):
+        half = 0.5 * push_weight + token[0, :1]
+        arrived = [
+            lax.ppermute(half, "rep", [(i, (i + (1 << b)) % replicas) for i in range(replicas)])
+            for b in range(levels)
+        ]
+        chosen = arrived[0]
+        for b in range(1, levels):
+            chosen = jnp.where(level_index == b, arrived[b], chosen)
+        return chosen
 
     order = jnp.mod(me - jnp.arange(members, dtype=jnp.int32), members)
     own = me[None]
-    weights = scaled_weights(
-        numer, weight_one, scaling, jnp.broadcast_to(outbox_weight[None], (8, 128))
-    )
+    weights = scaled_weights(numer, weight_one, scaling)
     everyone = range(members - 1), range(1, members)
 
     def scalars(t):
@@ -510,12 +505,15 @@
             mine[e][q] = (array, index, size)
 
     fetch(0, list(range(count)), None)
+    parts = [None] * count
+    for q in range(count):
+        parts[q], _, last, first = partial_products(mine[0][q], weights, True)
+        hint[q] = (last, first)
     for e in range(rounds):
-        parts, moving = [None] * count, [None] * count
+        moving = [None] * count
         for q in range(count):
-            parts[q], last, first = partial_products(mine[e][q], weights, hint[q])
             if e == 0:
-                moving[q] = hops(last, first, range(1), range(members - 1, members))
+                moving[q] = hops(*hint[q], range(1), range(members - 1, members))
             else:
                 right, left, _ = next_payload(*before[q], parts[q], scalars(0), True)
                 moving[q] = hops(right, left, *everyone)
@@ -526,7 +524,8 @@
                 right, left, token = next_payload(*moving[q], parts[q], scalars(t), False)
                 if t == 1 and q == 0 and e + 1 < rounds:
                     fetch(e + 1, list(range(count)), token)
-                hint[q] = token
+                if t == 1 and q == 0 and e + 1 == rounds:
+                    outbox_weight = sent_weight(token)
                 if e == 0:
                     pairs = range(t + 1), range(members - 1 - t, members)
                 else:
@@ -535,7 +534,11 @@
                 if e > 0 and t < members - 2:
                     units[e - 1][q][1].append(moving[q][0])
                     units[e - 1][q][2].append(moving[q][1])
+        later = [None] * count
         for q in range(count):
+            token = None
+            if e + 1 < rounds:
+                later[q], token = partial_products(mine[e + 1][q], weights, False)
             unit = unit_gradient(
                 *moving[q],
                 parts[q],
@@ -544,9 +547,11 @@
                 cotangent[0],
                 gain[None],
                 starts[e][q],
+                token,
             )
             before[q] = hops(unit, unit, *everyone)
             units[e][q] = (unit, [before[q][0]], [before[q][1]])
+        parts = later
     kept = None
     for s in range(1, members - 1):
         for q in range(count):
@@ -560,7 +565,8 @@
             units[-1][q][1].append(before[q][0])
             units[-1][q][2].append(before[q][1])
     flat = [[u] + r + l for u, r, l in units[-1]]
-    new_params, half = weight_step(flat, mine[-1], order, kept, None, inbox_params[0])
+    late = jnp.broadcast_to(outbox_weight[None], (8, 128))
+    new_params, half = weight_step(flat, mine[-1], order, kept, None, inbox_params[0], late)
     new_weight = 0.5 * push_weight + inbox_weight
     branches = [partial(tail, half, early + flat, weights, order, place) for place in range(levels)]
     sent, grad_heads = lax.switch(level_index, branches)

time: 382 us -> 380 us (level); the launches traced: 383 us -> 375 us
  waiting for transfers between devices: 44.9 us -> 104 us
  starting transfers between devices: 162 us -> 114 us
  Pallas kernels: 108 us -> 85.3 us
  local copies, waits for them, and re-layouts: 7.38 us -> 11.7 us
    ppermute x56 -> x40, starting transfers between devices: 140 us -> 96.3 us  [hop(): return lax.ppermute(value, 'fsdp', [(i, i + step) for i in pairs])]
    ppermute x56 -> x40, waiting for transfers between devices: 44.8 us -> 76.3 us  [hop(): return lax.ppermute(value, 'fsdp', [(i, i + step) for i in pairs])]
    pallas_call x38 -> x27, Pallas kernels: 108 us -> 85.3 us  [call(): pl.pallas_call(body, name=name, out_shape=[jax.ShapeDtypeStruct(shape, ki...]
    all_to_all x3 -> x2, waiting for transfers between devices: 0.1 us -> 18.2 us  [swapped(): return lax.all_to_all(blocks, 'fsdp', 0, 0, tiled=False)]
    ppermute x3, waiting for transfers between devices: 0.01 us -> 5.61 us  [sent_weight(): lax.ppermute(half, 'rep', [(i, (i + (1 << b)) % replicas) for i in range(...]
    all_to_all x3 -> x2, starting transfers between devices: 15.6 us -> 10.8 us  [swapped(): return lax.all_to_all(blocks, 'fsdp', 0, 0, tiled=False)]
    unnamed x172 -> x102, local copies, waits for them, and re-layouts: 6.78 us -> 11.2 us
  transfers between devices with their start and end apart: 63 -> 46, of which waited for: 16 -> 24; matrix products, arithmetic and copies ran while one was open for 0% -> 0% of each run, Pallas kernels for 22% -> 17%
where the time goes in v4:
time: 380 us; the launch traced here: 375 us
  starting transfers between devices  114 us (30%)
  waiting for transfers between devices  104 us (27%)
  Pallas kernels  85.3 us (22%)
  blocking collectives  49.7 us (13%)
  local copies, waits for them, and re-layouts  11.7 us (3%)
  between operations  9.59 us (3%)
    ppermute x40, starting transfers between devices, hop(): return lax.ppermute(value, 'fsdp', [(i, i + step) for i in pairs])  96.3 us
    pallas_call x27, Pallas kernels, call(): pl.pallas_call(body, name=name, out_shape=[jax.ShapeDtypeStruct(shape, ki...  85.3 us
    ppermute x40, waiting for transfers between devices, hop(): return lax.ppermute(value, 'fsdp', [(i, i + step) for i in pairs])  76.3 us
    all_to_all x1, blocking collectives, swapped(): return lax.all_to_all(blocks, 'fsdp', 0, 0, tiled=False)  49.7 us
    all_to_all x2, waiting for transfers between devices, swapped(): return lax.all_to_all(blocks, 'fsdp', 0, 0, tiled=False)  18.2 us
    unnamed x102, local copies, waits for them, and re-layouts  11.2 us
    all_to_all x2, starting transfers between devices, swapped(): return lax.all_to_all(blocks, 'fsdp', 0, 0, tiled=False)  10.8 us
  transfers between devices with their start and end apart: 46, of which 24 were waited for; matrix products, arithmetic and copies ran while one was open for 0% of the time, Pallas kernels for 17%

profile of v4, /device:TPU:0, one launch (start us, length us, event | category | flops | bytes accessed | tf_op | source)
XLA Modules:
  0.0 374.9 jit_solution(2481459704972370759)
XLA Ops:
  0.6 2.0 cut_heads.2
  2.6 6.3 %all-to-all-start.3 = ((bf16[4,192,640]{2,1,0:T(8,128)(2,1)}), bf16[4,192,640]{2,1,0:T(8,128)(2,1)S(1)}, u32[]{:S(2)}, u32[]{:S(2)}) async-start(bf16[4,192,640]{2,1,0:T(8,128)(2,1)} %cut_heads.2), calls=%async_computation.3 | async-start | bytes 1966080 | tf_op jit(solution)/shard_map/all_to_all | solution.py:428
  9.6 5.5 %scaled_weights.1.weights_ref = bf16[640,2560]{1,0:T(8,128)(2,1)} custom-call(f32[640,2560]{1,0:T(8,128)} %bitcast.39, f32[1,1]{1,0:T(1,128)} %bitcast.30.one_ref), custom_call_target="tpu_custom_call" | custom-call | flops 3276800 | bytes 9830400 | tf_op jit(solution)/shard_map/scaled_weights/pallas_call | solution.py:16
  15.1 18.2 %all-to-all-done.3.mine_ref.refs_14_.refs_15_ = bf16[4,192,640]{2,1,0:T(8,128)(2,1)S(1)} async-done(((bf16[4,192,640]{2,1,0:T(8,128)(2,1)}), bf16[4,192,640]{2,1,0:T(8,128)(2,1)S(1)}, u32[]{:S(2)}, u32[]{:S(2)}) %all-to-all-start.3) | async-done | bytes 983072 | tf_op jit(solution)/shard_map/all_to_all | solution.py:428
  33.3 4.2 %partial_products.4 = (bf16[4,96,2560]{2,1,0:T(8,128)(2,1)S(1)}, f32[8,128]{1,0:T(8,128)}, bf16[96,2560]{1,0:T(8,128)(2,1)}, bf16[96,2560]{1,0:T(8,128)(2,1)}) custom-call(bf16[4,192,640]{2,1,0:T(8,128)(2,1)S(1)} %all-to-all-done.3.mine_ref.refs_14_.refs_15_, bf16[640,2560]{1,0:T(8,128)(2,1)} %scaled_weights.1.weights_ref), custom_call_target="tpu_custom_call" | custom-call | flops 1258291200 | bytes 5734400 | tf_op jit(solution)/shard_map/partial_products/pallas_call | solution.py:16
  40.4 8.7 %collective-permute-done.3.right_ref = bf16[96,2560]{1,0:T(8,128)(2,1)S(1)} collective-permute-done((bf16[96,2560]{1,0:T(8,128)(2,1)}, bf16[96,2560]{1,0:T(8,128)(2,1)S(1)}, u32[]{:S(2)}, u32[]{:S(2)}) %collective-permute-start.3) | collective-permute-done | bytes 491552 | tf_op jit(solution)/shard_map/ppermute | solution.py:44
  49.1 2.7 next_payload.10
  52.9 4.4 %all-to-all-start.4 = ((bf16[4,192,640]{2,1,0:T(8,128)(2,1)}), bf16[4,192,640]{2,1,0:T(8,128)(2,1)}, u32[]{:S(2)}, u32[]{:S(2)}) async-start(bf16[4,192,640]{2,1,0:T(8,128)(2,1)} %copy-done.16), calls=%async_computation.4 | async-start | bytes 1966080 | tf_op jit(solution)/shard_map/all_to_all | solution.py:428
  57.3 4.1 %partial_products.6 = (bf16[4,96,2560]{2,1,0:T(8,128)(2,1)S(1)}, f32[8,128]{1,0:T(8,128)}, bf16[96,2560]{1,0:T(8,128)(2,1)S(1)}, bf16[96,2560]{1,0:T(8,128)(2,1)S(1)}) custom-call(bf16[4,192,640]{2,1,0:T(8,128)(2,1)S(1)} %all-to-all-done.3.mine_ref.refs_14_.refs_15_, bf16[640,2560]{1,0:T(8,128)(2,1)} %scaled_weights.1.weights_ref), custom_call_target="tpu_custom_call" | custom-call | flops 1258291200 | bytes 5734400 | tf_op jit(solution)/shard_map/partial_products/pallas_call | solution.py:16
  61.4 4.1 %collective-permute-start.23 = (bf16[96,2560]{1,0:T(8,128)(2,1)S(1)}, bf16[96,2560]{1,0:T(8,128)(2,1)S(1)}, u32[]{:S(2)}, u32[]{:S(2)}) collective-permute-start(bf16[96,2560]{1,0:T(8,128)(2,1)S(1)} %get-tuple-element.341), channel_id=1, source_target_pairs={{0,1},{4,5},{8,9},{12,13},{16,17},{20,21},{24,25},{28,29}} | collective-permute-start | bytes 1474568 | tf_op jit(solution)/shard_map/ppermute | solution.py:44
  69.0 16.0 %collective-permute-done.23.right_ref = bf16[96,2560]{1,0:T(8,128)(2,1)S(1)} collective-permute-done((bf16[96,2560]{1,0:T(8,128)(2,1)S(1)}, bf16[96,2560]{1,0:T(8,128)(2,1)S(1)}, u32[]{:S(2)}, u32[]{:S(2)}) %collective-permute-start.23) | collective-permute-done | bytes 491552 | tf_op jit(solution)/shard_map/ppermute | solution.py:44
  85.1 1.6 next_payload.15
  86.7 5.2 %collective-permute-start.25 = (bf16[96,2560]{1,0:T(8,128)(2,1)}, bf16[96,2560]{1,0:T(8,128)(2,1)}, u32[]{:S(2)}, u32[]{:S(2)}) collective-permute-start(bf16[96,2560]{1,0:T(8,128)(2,1)} %get-tuple-element.344), channel_id=1, source_target_pairs={{0,1},{1,2},{4,5},{5,6},{8,9},{9,10},{12,13},{13,14},{16,17},{17,1... | collective-permute-start | bytes 1474568 | tf_op jit(solution)/shard_map/ppermute | solution.py:44
  93.4 2.3 collective-permute-done.5.right_ref
  95.7 2.6 next_payload.11
  98.3 4.3 %collective-permute-start.7 = (bf16[96,2560]{1,0:T(8,128)(2,1)}, bf16[96,2560]{1,0:T(8,128)(2,1)S(1)}, u32[]{:S(2)}, u32[]{:S(2)}) collective-permute-start(bf16[96,2560]{1,0:T(8,128)(2,1)} %get-tuple-element.330), channel_id=1, source_target_pairs={{0,1},{1,2},{2,3},{4,5},{5,6},{6,7},{8,9},{9,10},{10,11},{12,13},{... | collective-permute-start | bytes 1474568 | tf_op jit(solution)/shard_map/ppermute | solution.py:44
  103.9 2.3 collective-permute-done.25.right_ref
  106.2 2.7 next_payload.16
  109.0 5.2 %collective-permute-start.27 = (bf16[96,2560]{1,0:T(8,128)(2,1)}, bf16[96,2560]{1,0:T(8,128)(2,1)}, u32[]{:S(2)}, u32[]{:S(2)}) collective-permute-start(bf16[96,2560]{1,0:T(8,128)(2,1)} %get-tuple-element.346), channel_id=1, source_target_pairs={{0,1},{1,2},{2,3},{4,5},{5,6},{6,7},{8,9},{9,10},{10,11},{12,13},{... | collective-permute-start | bytes 1474568 | tf_op jit(solution)/shard_map/ppermute | solution.py:44
  115.5 3.7 partial_products.5
  120.8 2.4 unit_gradient.4.refs_0_
  124.8 6.1 %collective-permute-start.9 = (bf16[96,2560]{1,0:T(8,128)(2,1)}, bf16[96,2560]{1,0:T(8,128)(2,1)}, u32[]{:S(2)}, u32[]{:S(2)}) collective-permute-start(bf16[96,2560]{1,0:T(8,128)(2,1)} %unit_gradient.4.refs_0_), channel_id=1, source_target_pairs={{0,1},{1,2},{2,3},{4,5},{5,6},{6,7},{8,9},{9,10},{10,11},{12,13},{... | collective-permute-start | bytes 1474568 | tf_op jit(solution)/shard_map/ppermute | solution.py:44
  130.8 3.2 partial_products.7
  134.1 3.0 unit_gradient.6.refs_7_
  138.3 5.3 %collective-permute-start.29 = (bf16[96,2560]{1,0:T(8,128)(2,1)}, bf16[96,2560]{1,0:T(8,128)(2,1)}, u32[]{:S(2)}, u32[]{:S(2)}) collective-permute-start(bf16[96,2560]{1,0:T(8,128)(2,1)} %unit_gradient.6.refs_7_), channel_id=1, source_target_pairs={{0,1},{1,2},{2,3},{4,5},{5,6},{6,7},{8,9},{9,10},{10,11},{12,13},{... | collective-permute-start | bytes 1474568 | tf_op jit(solution)/shard_map/ppermute | solution.py:44
  143.8 2.4 next_payload.12
  146.2 2.4 collective-permute-start.11
  149.9 4.9 %collective-permute-done.29.right_ref.refs_8_ = bf16[96,2560]{1,0:T(8,128)(2,1)} collective-permute-done((bf16[96,2560]{1,0:T(8,128)(2,1)}, bf16[96,2560]{1,0:T(8,128)(2,1)}, u32[]{:S(2)}, u32[]{:S(2)}) %collective-permute-start.29) | collective-permute-done | bytes 491552 | tf_op jit(solution)/shard_map/ppermute | solution.py:44
  154.9 2.5 next_payload.17
  157.3 4.4 %collective-permute-start.31 = (bf16[96,2560]{1,0:T(8,128)(2,1)S(1)}, bf16[96,2560]{1,0:T(8,128)(2,1)S(1)}, u32[]{:S(2)}, u32[]{:S(2)}) collective-permute-start(bf16[96,2560]{1,0:T(8,128)(2,1)S(1)} %get-tuple-element.350), channel_id=1, source_target_pairs={{0,1},{1,2},{2,3},{4,5},{5,6},{6,7},{8,9},{9,10},{10,11},{12,13},{... | collective-permute-start | bytes 1474568 | tf_op jit(solution)/shard_map/ppermute | solution.py:44
  163.1 2.3 collective-permute-done.11.right_ref.refs_2_
  166.3 4.3 %collective-permute-start.13 = (bf16[96,2560]{1,0:T(8,128)(2,1)S(1)}, bf16[96,2560]{1,0:T(8,128)(2,1)S(1)}, u32[]{:S(2)}, u32[]{:S(2)}) collective-permute-start(bf16[96,2560]{1,0:T(8,128)(2,1)S(1)} %get-tuple-element.337), channel_id=1, source_target_pairs={{0,1},{1,2},{2,3},{4,5},{5,6},{6,7},{8,9},{9,10},{10,11},{12,13},{... | collective-permute-start | bytes 1474568 | tf_op jit(solution)/shard_map/ppermute | solution.py:44
  171.9 3.9 %collective-permute-done.31.right_ref.refs_9_ = bf16[96,2560]{1,0:T(8,128)(2,1)S(1)} collective-permute-done((bf16[96,2560]{1,0:T(8,128)(2,1)S(1)}, bf16[96,2560]{1,0:T(8,128)(2,1)S(1)}, u32[]{:S(2)}, u32[]{:S(2)}) %collective-permute-start.31) | collective-permute-done | bytes 491552 | tf_op jit(solution)/shard_map/ppermute | solution.py:44
  178.7 4.2 %collective-permute-start.33 = (bf16[96,2560]{1,0:T(8,128)(2,1)S(1)}, bf16[96,2560]{1,0:T(8,128)(2,1)S(1)}, u32[]{:S(2)}, u32[]{:S(2)}) collective-permute-start(bf16[96,2560]{1,0:T(8,128)(2,1)S(1)} %get-tuple-element.352), channel_id=1, source_target_pairs={{0,1},{1,2},{2,3},{4,5},{5,6},{6,7},{8,9},{9,10},{10,11},{12,13},{... | collective-permute-start | bytes 1474568 | tf_op jit(solution)/shard_map/ppermute | solution.py:44
  184.2 2.2 collective-permute-done.13.right_ref.refs_3_
  189.2 4.2 %collective-permute-start.15 = (bf16[96,2560]{1,0:T(8,128)(2,1)S(1)}, bf16[96,2560]{1,0:T(8,128)(2,1)S(1)}, u32[]{:S(2)}, u32[]{:S(2)}) collective-permute-start(bf16[96,2560]{1,0:T(8,128)(2,1)S(1)} %get-tuple-element.339), channel_id=1, source_target_pairs={{0,1},{1,2},{2,3},{4,5},{5,6},{6,7},{8,9},{9,10},{10,11},{12,13},{... | collective-permute-start | bytes 1474568 | tf_op jit(solution)/shard_map/ppermute | solution.py:44
  193.5 1.6 collective-permute-start.16
  195.0 1.9 collective-permute-done.33.right_ref.refs_10_
  196.9 2.0 collective-permute-done.34.left_ref.refs_13_
  200.3 3.9 %collective-permute-start.35 = (bf16[96,2560]{1,0:T(8,128)(2,1)S(1)}, bf16[96,2560]{1,0:T(8,128)(2,1)S(1)}, u32[]{:S(2)}, u32[]{:S(2)}) collective-permute-start(bf16[96,2560]{1,0:T(8,128)(2,1)S(1)} %get-tuple-element.354), channel_id=1, source_target_pairs={{0,1},{1,2},{2,3},{4,5},{5,6},{6,7},{8,9},{9,10},{10,11},{12,13},{... | collective-permute-start | bytes 1474568 | tf_op jit(solution)/shard_map/ppermute | solution.py:44
  205.7 1.8 collective-permute-done.15.right_ref
  207.4 2.3 collective-permute-done.16.left_ref
  211.7 4.6 %collective-permute-start.17 = (bf16[96,2560]{1,0:T(8,128)(2,1)S(1)}, bf16[96,2560]{1,0:T(8,128)(2,1)S(1)}, u32[]{:S(2)}, u32[]{:S(2)}) collective-permute-start(bf16[96,2560]{1,0:T(8,128)(2,1)S(1)} %unit_gradient.5.refs_0_), channel_id=1, source_target_pairs={{0,1},{1,2},{2,3},{4,5},{5,6},{6,7},{8,9},{9,10},{10,11},{12,13},{... | collective-permute-start | bytes 1474568 | tf_op jit(solution)/shard_map/ppermute | solution.py:44
  216.3 1.7 collective-permute-done.35.right_ref
  218.0 2.5 collective-permute-done.36.left_ref
  222.4 4.8 %collective-permute-start.37 = (bf16[96,2560]{1,0:T(8,128)(2,1)S(1)}, bf16[96,2560]{1,0:T(8,128)(2,1)S(1)}, u32[]{:S(2)}, u32[]{:S(2)}) collective-permute-start(bf16[96,2560]{1,0:T(8,128)(2,1)S(1)} %unit_gradient.7.refs_7_), channel_id=1, source_target_pairs={{0,1},{1,2},{2,3},{4,5},{5,6},{6,7},{8,9},{9,10},{10,11},{12,13},{... | collective-permute-start | bytes 1474568 | tf_op jit(solution)/shard_map/ppermute | solution.py:44
  227.3 7.0 %weight_step.2 = (f32[640,2560]{1,0:T(8,128)S(1)}, f32[8,128]{1,0:T(8,128)S(1)}) custom-call(s32[4]{0:T(128)S(1)} %and_select_fusion.s, bf16[96,2560]{1,0:T(8,128)(2,1)} %unit_gradient.4.refs_0_, bf16[96,2560]{1,0:T(8,128)(2,1)} %collective-permute-done.9.right_ref.refs_1_, bf16[96,2560]{1,0:T(8,128)(2,1)S(1)} %collective-permute-done.11.right_ref.refs_2_, ...), custom_call_target="tpu_custom_call" | custom-call | flops 2516582400 | bytes 26542080 | tf_op jit(solution)/shard_map/weight_step/pallas_call | solution.py:16
  234.3 2.8 copy-done.14
  239.1 1.7 collective-permute-done.38.left_ref.refs_11_
  243.0 10.2 %collective-permute-done.21.refs_5_ = bf16[96,2560]{1,0:T(8,128)(2,1)S(1)} collective-permute-done((bf16[96,2560]{1,0:T(8,128)(2,1)S(1)}, bf16[96,2560]{1,0:T(8,128)(2,1)S(1)}, u32[]{:S(2)}, u32[]{:S(2)}) %collective-permute-start.21) | collective-permute-done | bytes 491552 | tf_op jit(solution)/shard_map/ppermute | solution.py:44
  257.4 6.4 %collective-permute-done.41.refs_12_ = bf16[96,2560]{1,0:T(8,128)(2,1)} collective-permute-done((bf16[96,2560]{1,0:T(8,128)(2,1)S(1)}, bf16[96,2560]{1,0:T(8,128)(2,1)}, u32[]{:S(2)}, u32[]{:S(2)}) %collective-permute-start.41) | collective-permute-done | bytes 491552 | tf_op jit(solution)/shard_map/ppermute | solution.py:44
  270.4 3.0 collective-permute-done.45
  273.4 1.9 collective-permute-start.44
  275.3 2.6 collective-permute-done.44
  278.0 2.8 collective-permute-start.43
  282.7 2.9 copy-done.13
  285.6 2.9 copy-done.15
  288.5 9.9 %weight_step.3 = (f32[640,2560]{1,0:T(8,128)}, bf16[640,2560]{1,0:T(8,128)(2,1)}) custom-call(s32[4]{0:T(128)S(1)} %and_select_fusion.s, bf16[96,2560]{1,0:T(8,128)(2,1)S(1)} %copy-done.38, bf16[96,2560]{1,0:T(8,128)(2,1)} %copy-done.41, bf16[96,2560]{1,0:T(8,128)(2,1)} %copy-done.43, bf16[96,2560]{1,0:T(8,128)(2,1)} %collective-permute-done.19.refs_3_, ...), custom_call_target="tpu_custom_call" | custom-call | flops 2516582400 | bytes 26542080 | tf_op jit(solution)/shard_map/weight_step/pallas_call | solution.py:16
  298.6 69.6 %conditional.1 = (bf16[640,2560]{1,0:T(8,128)(2,1)}, bf16[1,384,2560]{2,1,0:T(8,128)(2,1)}) conditional(s32[]{:T(128)} %clamp.3, (bf16[640,2560]{1,0:T(8,128)(2,1)}, s32[4]{0:T(128)S(1)}, bf16[96,2560]{1,0:T(8,128)(2,1)}, bf16[96,2560]{1,0:T(8,128)(2,1)}, bf16[96,2560]{1,0:T(8,128)(2,1)S(1)}, ...), branch_computations={%region_1.2_spmd, %region_2.3_spmd, %region_3.4_spmd} | conditional | flops 5033164800 | bytes 38010936 | solution.py:572
  299.7 13.1 %grad_rows.5 = bf16[4,384,640]{2,1,0:T(8,128)(2,1)S(1)} custom-call(s32[4]{0:T(128)S(1)} %get-tuple-element.250.s, bf16[96,2560]{1,0:T(8,128)(2,1)} %get-tuple-element.251.refs_0_, bf16[96,2560]{1,0:T(8,128)(2,1)} %get-tuple-element.252.refs_1_, bf16[96,2560]{1,0:T(8,128)(2,1)S(1)} %get-tuple-element.253.refs_2_, ...), custom_call_target="tpu_custom_call" | custom-call | flops 5033164800 | bytes 17039360 | tf_op jit(solution)/shard_map/cond/branch_2_fun/grad_rows/pallas_call | solution.py:16
  312.8 49.7 %all_to_all.24.blocks_ref = bf16[4,384,640]{2,1,0:T(8,128)(2,1)S(1)} all-to-all(bf16[4,384,640]{2,1,0:T(8,128)(2,1)S(1)} %grad_rows.5), channel_id=1, replica_groups=mesh['rep'=8,'fsdp'=4] {'fsdp'}, dimensions={0} | all-to-all | bytes 3932160 | tf_op jit(solution)/shard_map/cond/branch_2_fun/all_to_all | solution.py:428
  362.6 1.9 joined_rows.5
  364.5 3.6 collective-permute-done.2
  368.2 4.4 %widened.1 = f32[640,2560]{1,0:T(8,128)} custom-call(bf16[640,2560]{1,0:T(8,128)(2,1)} %get-tuple-element.363.value_ref), custom_call_target="tpu_custom_call" | custom-call | bytes 9830400 | tf_op jit(solution)/shard_map/widened/pallas_call | solution.py:16
  (168 shorter events, 47.5 us)
Async XLA Ops:
  2.6 30.6 %all-to-all-start.3 = ((bf16[4,192,640]{2,1,0:T(8,128)(2,1)}), bf16[4,192,640]{2,1,0:T(8,128)(2,1)S(1)}, u32[]{:S(2)}, u32[]{:S(2)}) async-start(bf16[4,192,640]{2,1,0:T(8,128)(2,1)} %cut_heads.2), calls=%async_computation.3 | async-start | bytes 1966080 | tf_op jit(solution)/shard_map/all_to_all | solution.py:428
  37.5 58.2 %copy-start.2 = (bf16[4,96,2560]{2,1,0:T(8,128)(2,1)}, bf16[4,96,2560]{2,1,0:T(8,128)(2,1)S(1)}, u32[]{:S(2)}) copy-start(bf16[4,96,2560]{2,1,0:T(8,128)(2,1)S(1)} %get-tuple-element.327.of_right.of_left.own_ref) | copy-start | bytes 5898244
  37.5 11.6 %collective-permute-start.3 = (bf16[96,2560]{1,0:T(8,128)(2,1)}, bf16[96,2560]{1,0:T(8,128)(2,1)S(1)}, u32[]{:S(2)}, u32[]{:S(2)}) collective-permute-start(bf16[96,2560]{1,0:T(8,128)(2,1)} %get-tuple-element.325), channel_id=1, source_target_pairs={{0,1},{4,5},{8,9},{12,13},{16,17},{20,21},{24,25},{28,29}} | collective-permute-start | bytes 1474568 | tf_op jit(solution)/shard_map/ppermute | solution.py:44
  38.8 10.3 %collective-permute-start.4 = (bf16[96,2560]{1,0:T(8,128)(2,1)}, bf16[96,2560]{1,0:T(8,128)(2,1)}, u32[]{:S(2)}, u32[]{:S(2)}) collective-permute-start(bf16[96,2560]{1,0:T(8,128)(2,1)} %get-tuple-element.326), channel_id=1, source_target_pairs={{3,2},{7,6},{11,10},{15,14},{19,18},{23,22},{27,26},{31,30}} | collective-permute-start | bytes 1474568 | tf_op jit(solution)/shard_map/ppermute | solution.py:44
  52.9 62.6 %all-to-all-start.4 = ((bf16[4,192,640]{2,1,0:T(8,128)(2,1)}), bf16[4,192,640]{2,1,0:T(8,128)(2,1)}, u32[]{:S(2)}, u32[]{:S(2)}) async-start(bf16[4,192,640]{2,1,0:T(8,128)(2,1)} %copy-done.16), calls=%async_computation.4 | async-start | bytes 1966080 | tf_op jit(solution)/shard_map/all_to_all | solution.py:428
  61.4 25.3 %copy-start.4 = (bf16[4,96,2560]{2,1,0:T(8,128)(2,1)}, bf16[4,96,2560]{2,1,0:T(8,128)(2,1)S(1)}, u32[]{:S(2)}) copy-start(bf16[4,96,2560]{2,1,0:T(8,128)(2,1)S(1)} %get-tuple-element.343.of_right.of_left.own_ref) | copy-start | bytes 5898244
  61.4 23.7 %collective-permute-start.23 = (bf16[96,2560]{1,0:T(8,128)(2,1)S(1)}, bf16[96,2560]{1,0:T(8,128)(2,1)S(1)}, u32[]{:S(2)}, u32[]{:S(2)}) collective-permute-start(bf16[96,2560]{1,0:T(8,128)(2,1)S(1)} %get-tuple-element.341), channel_id=1, source_target_pairs={{0,1},{4,5},{8,9},{12,13},{16,17},{20,21},{24,25},{28,29}} | collective-permute-start | bytes 1474568 | tf_op jit(solution)/shard_map/ppermute | solution.py:44
  65.5 19.5 %collective-permute-start.24 = (bf16[96,2560]{1,0:T(8,128)(2,1)S(1)}, bf16[96,2560]{1,0:T(8,128)(2,1)S(1)}, u32[]{:S(2)}, u32[]{:S(2)}) collective-permute-start(bf16[96,2560]{1,0:T(8,128)(2,1)S(1)} %get-tuple-element.342), channel_id=1, source_target_pairs={{3,2},{7,6},{11,10},{15,14},{19,18},{23,22},{27,26},{31,30}} | collective-permute-start | bytes 1474568 | tf_op jit(solution)/shard_map/ppermute | solution.py:44
  66.2 29.5 %collective-permute-start.5 = (bf16[96,2560]{1,0:T(8,128)(2,1)}, bf16[96,2560]{1,0:T(8,128)(2,1)S(1)}, u32[]{:S(2)}, u32[]{:S(2)}) collective-permute-start(bf16[96,2560]{1,0:T(8,128)(2,1)} %get-tuple-element.328), channel_id=1, source_target_pairs={{0,1},{1,2},{4,5},{5,6},{8,9},{9,10},{12,13},{13,14},{16,17},{17,1... | collective-permute-start | bytes 1474568 | tf_op jit(solution)/shard_map/ppermute | solution.py:44
  67.6 28.1 %collective-permute-start.6 = (bf16[96,2560]{1,0:T(8,128)(2,1)}, bf16[96,2560]{1,0:T(8,128)(2,1)}, u32[]{:S(2)}, u32[]{:S(2)}) collective-permute-start(bf16[96,2560]{1,0:T(8,128)(2,1)} %get-tuple-element.329), channel_id=1, source_target_pairs={{2,1},{3,2},{6,5},{7,6},{10,9},{11,10},{14,13},{15,14},{18,17},{19... | collective-permute-start | bytes 1474568 | tf_op jit(solution)/shard_map/ppermute | solution.py:44
  86.7 19.6 %collective-permute-start.25 = (bf16[96,2560]{1,0:T(8,128)(2,1)}, bf16[96,2560]{1,0:T(8,128)(2,1)}, u32[]{:S(2)}, u32[]{:S(2)}) collective-permute-start(bf16[96,2560]{1,0:T(8,128)(2,1)} %get-tuple-element.344), channel_id=1, source_target_pairs={{0,1},{1,2},{4,5},{5,6},{8,9},{9,10},{12,13},{13,14},{16,17},{17,1... | collective-permute-start | bytes 1474568 | tf_op jit(solution)/shard_map/ppermute | solution.py:44
  91.8 14.4 %collective-permute-start.26 = (bf16[96,2560]{1,0:T(8,128)(2,1)}, bf16[96,2560]{1,0:T(8,128)(2,1)}, u32[]{:S(2)}, u32[]{:S(2)}) collective-permute-start(bf16[96,2560]{1,0:T(8,128)(2,1)} %get-tuple-element.345), channel_id=1, source_target_pairs={{2,1},{3,2},{6,5},{7,6},{10,9},{11,10},{14,13},{15,14},{18,17},{19... | collective-permute-start | bytes 1474568 | tf_op jit(solution)/shard_map/ppermute | solution.py:44
  98.3 20.9 %collective-permute-start.7 = (bf16[96,2560]{1,0:T(8,128)(2,1)}, bf16[96,2560]{1,0:T(8,128)(2,1)S(1)}, u32[]{:S(2)}, u32[]{:S(2)}) collective-permute-start(bf16[96,2560]{1,0:T(8,128)(2,1)} %get-tuple-element.330), channel_id=1, source_target_pairs={{0,1},{1,2},{2,3},{4,5},{5,6},{6,7},{8,9},{9,10},{10,11},{12,13},{... | collective-permute-start | bytes 1474568 | tf_op jit(solution)/shard_map/ppermute | solution.py:44
  102.6 16.6 %collective-permute-start.8 = (bf16[96,2560]{1,0:T(8,128)(2,1)}, bf16[96,2560]{1,0:T(8,128)(2,1)}, u32[]{:S(2)}, u32[]{:S(2)}) collective-permute-start(bf16[96,2560]{1,0:T(8,128)(2,1)} %get-tuple-element.331), channel_id=1, source_target_pairs={{1,0},{2,1},{3,2},{5,4},{6,5},{7,6},{9,8},{10,9},{11,10},{13,12},{... | collective-permute-start | bytes 1474568 | tf_op jit(solution)/shard_map/ppermute | solution.py:44
  109.0 25.1 %collective-permute-start.27 = (bf16[96,2560]{1,0:T(8,128)(2,1)}, bf16[96,2560]{1,0:T(8,128)(2,1)}, u32[]{:S(2)}, u32[]{:S(2)}) collective-permute-start(bf16[96,2560]{1,0:T(8,128)(2,1)} %get-tuple-element.346), channel_id=1, source_target_pairs={{0,1},{1,2},{2,3},{4,5},{5,6},{6,7},{8,9},{9,10},{10,11},{12,13},{... | collective-permute-start | bytes 1474568 | tf_op jit(solution)/shard_map/ppermute | solution.py:44
  114.1 19.9 %collective-permute-start.28 = (bf16[96,2560]{1,0:T(8,128)(2,1)}, bf16[96,2560]{1,0:T(8,128)(2,1)}, u32[]{:S(2)}, u32[]{:S(2)}) collective-permute-start(bf16[96,2560]{1,0:T(8,128)(2,1)} %get-tuple-element.347), channel_id=1, source_target_pairs={{1,0},{2,1},{3,2},{5,4},{6,5},{7,6},{9,8},{10,9},{11,10},{13,12},{... | collective-permute-start | bytes 1474568 | tf_op jit(solution)/shard_map/ppermute | solution.py:44
  123.2 20.5 %collective-permute-start.10 = (bf16[96,2560]{1,0:T(8,128)(2,1)}, bf16[96,2560]{1,0:T(8,128)(2,1)S(1)}, u32[]{:S(2)}, u32[]{:S(2)}) collective-permute-start(bf16[96,2560]{1,0:T(8,128)(2,1)} %unit_gradient.4.refs_0_), channel_id=1, source_target_pairs={{1,0},{2,1},{3,2},{5,4},{6,5},{7,6},{9,8},{10,9},{11,10},{13,12},{... | collective-permute-start | bytes 1474568 | tf_op jit(solution)/shard_map/ppermute | solution.py:44
  124.8 19.0 %collective-permute-start.9 = (bf16[96,2560]{1,0:T(8,128)(2,1)}, bf16[96,2560]{1,0:T(8,128)(2,1)}, u32[]{:S(2)}, u32[]{:S(2)}) collective-permute-start(bf16[96,2560]{1,0:T(8,128)(2,1)} %unit_gradient.4.refs_0_), channel_id=1, source_target_pairs={{0,1},{1,2},{2,3},{4,5},{5,6},{6,7},{8,9},{9,10},{10,11},{12,13},{... | collective-permute-start | bytes 1474568 | tf_op jit(solution)/shard_map/ppermute | solution.py:44
  137.1 12.9 %collective-permute-start.30 = (bf16[96,2560]{1,0:T(8,128)(2,1)}, bf16[96,2560]{1,0:T(8,128)(2,1)}, u32[]{:S(2)}, u32[]{:S(2)}) collective-permute-start(bf16[96,2560]{1,0:T(8,128)(2,1)} %unit_gradient.6.refs_7_), channel_id=1, source_target_pairs={{1,0},{2,1},{3,2},{5,4},{6,5},{7,6},{9,8},{10,9},{11,10},{13,12},{... | collective-permute-start | bytes 1474568 | tf_op jit(solution)/shard_map/ppermute | solution.py:44
  138.3 16.5 %collective-permute-start.29 = (bf16[96,2560]{1,0:T(8,128)(2,1)}, bf16[96,2560]{1,0:T(8,128)(2,1)}, u32[]{:S(2)}, u32[]{:S(2)}) collective-permute-start(bf16[96,2560]{1,0:T(8,128)(2,1)} %unit_gradient.6.refs_7_), channel_id=1, source_target_pairs={{0,1},{1,2},{2,3},{4,5},{5,6},{6,7},{8,9},{9,10},{10,11},{12,13},{... | collective-permute-start | bytes 1474568 | tf_op jit(solution)/shard_map/ppermute | solution.py:44
  143.8 83.4 %copy-start.19 = (bf16[96,2560]{1,0:T(8,128)(2,1)}, bf16[96,2560]{1,0:T(8,128)(2,1)S(1)}, u32[]{:S(2)}) copy-start(bf16[96,2560]{1,0:T(8,128)(2,1)S(1)} %collective-permute-done.10.left_ref.refs_4_) | copy-start | bytes 1474564
  146.2 19.1 %collective-permute-start.11 = (bf16[96,2560]{1,0:T(8,128)(2,1)S(1)}, bf16[96,2560]{1,0:T(8,128)(2,1)S(1)}, u32[]{:S(2)}, u32[]{:S(2)}) collective-permute-start(bf16[96,2560]{1,0:T(8,128)(2,1)S(1)} %get-tuple-element.335), channel_id=1, source_target_pairs={{0,1},{1,2},{2,3},{4,5},{5,6},{6,7},{8,9},{9,10},{10,11},{12,13},{... | collective-permute-start | bytes 1474568 | tf_op jit(solution)/shard_map/ppermute | solution.py:44
  148.6 16.8 %collective-permute-start.12 = (bf16[96,2560]{1,0:T(8,128)(2,1)S(1)}, bf16[96,2560]{1,0:T(8,128)(2,1)S(1)}, u32[]{:S(2)}, u32[]{:S(2)}) collective-permute-start(bf16[96,2560]{1,0:T(8,128)(2,1)S(1)} %get-tuple-element.336), channel_id=1, source_target_pairs={{1,0},{2,1},{3,2},{5,4},{6,5},{7,6},{9,8},{10,9},{11,10},{13,12},{... | collective-permute-start | bytes 1474568 | tf_op jit(solution)/shard_map/ppermute | solution.py:44
  157.3 18.5 %collective-permute-start.31 = (bf16[96,2560]{1,0:T(8,128)(2,1)S(1)}, bf16[96,2560]{1,0:T(8,128)(2,1)S(1)}, u32[]{:S(2)}, u32[]{:S(2)}) collective-permute-start(bf16[96,2560]{1,0:T(8,128)(2,1)S(1)} %get-tuple-element.350), channel_id=1, source_target_pairs={{0,1},{1,2},{2,3},{4,5},{5,6},{6,7},{8,9},{9,10},{10,11},{12,13},{... | collective-permute-start | bytes 1474568 | tf_op jit(solution)/shard_map/ppermute | solution.py:44
  161.8 15.6 %collective-permute-start.32 = (bf16[96,2560]{1,0:T(8,128)(2,1)S(1)}, bf16[96,2560]{1,0:T(8,128)(2,1)S(1)}, u32[]{:S(2)}, u32[]{:S(2)}) collective-permute-start(bf16[96,2560]{1,0:T(8,128)(2,1)S(1)} %get-tuple-element.351), channel_id=1, source_target_pairs={{1,0},{2,1},{3,2},{5,4},{6,5},{7,6},{9,8},{10,9},{11,10},{13,12},{... | collective-permute-start | bytes 1474568 | tf_op jit(solution)/shard_map/ppermute | solution.py:44
  165.3 61.9 %copy-start.21 = (bf16[96,2560]{1,0:T(8,128)(2,1)}, bf16[96,2560]{1,0:T(8,128)(2,1)S(1)}, u32[]{:S(2)}) copy-start(bf16[96,2560]{1,0:T(8,128)(2,1)S(1)} %collective-permute-done.11.right_ref.refs_2_) | copy-start | bytes 1474564
  165.4 61.8 %copy-start.23 = (bf16[96,2560]{1,0:T(8,128)(2,1)}, bf16[96,2560]{1,0:T(8,128)(2,1)S(1)}, u32[]{:S(2)}) copy-start(bf16[96,2560]{1,0:T(8,128)(2,1)S(1)} %collective-permute-done.12.left_ref.refs_5_) | copy-start | bytes 1474564
  166.3 20.1 %collective-permute-start.13 = (bf16[96,2560]{1,0:T(8,128)(2,1)S(1)}, bf16[96,2560]{1,0:T(8,128)(2,1)S(1)}, u32[]{:S(2)}, u32[]{:S(2)}) collective-permute-start(bf16[96,2560]{1,0:T(8,128)(2,1)S(1)} %get-tuple-element.337), channel_id=1, source_target_pairs={{0,1},{1,2},{2,3},{4,5},{5,6},{6,7},{8,9},{9,10},{10,11},{12,13},{... | collective-permute-start | bytes 1474568 | tf_op jit(solution)/shard_map/ppermute | solution.py:44
  170.6 17.3 %collective-permute-start.14 = (bf16[96,2560]{1,0:T(8,128)(2,1)S(1)}, bf16[96,2560]{1,0:T(8,128)(2,1)S(1)}, u32[]{:S(2)}, u32[]{:S(2)}) collective-permute-start(bf16[96,2560]{1,0:T(8,128)(2,1)S(1)} %get-tuple-element.338), channel_id=1, source_target_pairs={{1,0},{2,1},{3,2},{5,4},{6,5},{7,6},{9,8},{10,9},{11,10},{13,12},{... | collective-permute-start | bytes 1474568 | tf_op jit(solution)/shard_map/ppermute | solution.py:44
  175.8 51.4 %copy-start.25 = (bf16[96,2560]{1,0:T(8,128)(2,1)}, bf16[96,2560]{1,0:T(8,128)(2,1)S(1)}, u32[]{:S(2)}) copy-start(bf16[96,2560]{1,0:T(8,128)(2,1)S(1)} %collective-permute-done.31.right_ref.refs_9_) | copy-start | bytes 1474564
  177.4 49.8 %copy-start.27 = (bf16[96,2560]{1,0:T(8,128)(2,1)}, bf16[96,2560]{1,0:T(8,128)(2,1)S(1)}, u32[]{:S(2)}) copy-start(bf16[96,2560]{1,0:T(8,128)(2,1)S(1)} %collective-permute-done.32.left_ref.refs_12_) | copy-start | bytes 1474564
  178.7 18.2 %collective-permute-start.33 = (bf16[96,2560]{1,0:T(8,128)(2,1)S(1)}, bf16[96,2560]{1,0:T(8,128)(2,1)S(1)}, u32[]{:S(2)}, u32[]{:S(2)}) collective-permute-start(bf16[96,2560]{1,0:T(8,128)(2,1)S(1)} %get-tuple-element.352), channel_id=1, source_target_pairs={{0,1},{1,2},{2,3},{4,5},{5,6},{6,7},{8,9},{9,10},{10,11},{12,13},{... | collective-permute-start | bytes 1474568 | tf_op jit(solution)/shard_map/ppermute | solution.py:44
  182.9 16.1 %collective-permute-start.34 = (bf16[96,2560]{1,0:T(8,128)(2,1)S(1)}, bf16[96,2560]{1,0:T(8,128)(2,1)S(1)}, u32[]{:S(2)}, u32[]{:S(2)}) collective-permute-start(bf16[96,2560]{1,0:T(8,128)(2,1)S(1)} %get-tuple-element.353), channel_id=1, source_target_pairs={{1,0},{2,1},{3,2},{5,4},{6,5},{7,6},{9,8},{10,9},{11,10},{13,12},{... | collective-permute-start | bytes 1474568 | tf_op jit(solution)/shard_map/ppermute | solution.py:44
  186.4 40.8 %copy-start.29 = (bf16[96,2560]{1,0:T(8,128)(2,1)}, bf16[96,2560]{1,0:T(8,128)(2,1)S(1)}, u32[]{:S(2)}) copy-start(bf16[96,2560]{1,0:T(8,128)(2,1)S(1)} %collective-permute-done.13.right_ref.refs_3_) | copy-start | bytes 1474564
  187.9 39.3 %copy-start.31 = (bf16[96,2560]{1,0:T(8,128)(2,1)}, bf16[96,2560]{1,0:T(8,128)(2,1)S(1)}, u32[]{:S(2)}) copy-start(bf16[96,2560]{1,0:T(8,128)(2,1)S(1)} %collective-permute-done.14.left_ref.refs_6_) | copy-start | bytes 1474564
  189.2 18.2 %collective-permute-start.15 = (bf16[96,2560]{1,0:T(8,128)(2,1)S(1)}, bf16[96,2560]{1,0:T(8,128)(2,1)S(1)}, u32[]{:S(2)}, u32[]{:S(2)}) collective-permute-start(bf16[96,2560]{1,0:T(8,128)(2,1)S(1)} %get-tuple-element.339), channel_id=1, source_target_pairs={{0,1},{1,2},{2,3},{4,5},{5,6},{6,7},{8,9},{9,10},{10,11},{12,13},{... | collective-permute-start | bytes 1474568 | tf_op jit(solution)/shard_map/ppermute | solution.py:44
  193.5 16.3 %collective-permute-start.16 = (bf16[96,2560]{1,0:T(8,128)(2,1)S(1)}, bf16[96,2560]{1,0:T(8,128)(2,1)S(1)}, u32[]{:S(2)}, u32[]{:S(2)}) collective-permute-start(bf16[96,2560]{1,0:T(8,128)(2,1)S(1)} %get-tuple-element.340), channel_id=1, source_target_pairs={{1,0},{2,1},{3,2},{5,4},{6,5},{7,6},{9,8},{10,9},{11,10},{13,12},{... | collective-permute-start | bytes 1474568 | tf_op jit(solution)/shard_map/ppermute | solution.py:44
  196.9 30.3 %copy-start.33 = (bf16[96,2560]{1,0:T(8,128)(2,1)}, bf16[96,2560]{1,0:T(8,128)(2,1)S(1)}, u32[]{:S(2)}) copy-start(bf16[96,2560]{1,0:T(8,128)(2,1)S(1)} %collective-permute-done.33.right_ref.refs_10_) | copy-start | bytes 1474564
  199.0 28.3 %copy-start.35 = (bf16[96,2560]{1,0:T(8,128)(2,1)}, bf16[96,2560]{1,0:T(8,128)(2,1)S(1)}, u32[]{:S(2)}) copy-start(bf16[96,2560]{1,0:T(8,128)(2,1)S(1)} %collective-permute-done.34.left_ref.refs_13_) | copy-start | bytes 1474564
  200.3 27.0 %slice-start = ((s8[6553600]{0:T(1024)(128)(4,1)}), s8[4194304]{0:T(1024)(128)(4,1)S(1)}, s32[]{:S(2)}) async-start(s8[6553600]{0:T(1024)(128)(4,1)} %bitcast.40), calls=%async_computation.5 | async-start | bytes 8388608
  200.3 17.7 %collective-permute-start.35 = (bf16[96,2560]{1,0:T(8,128)(2,1)S(1)}, bf16[96,2560]{1,0:T(8,128)(2,1)S(1)}, u32[]{:S(2)}, u32[]{:S(2)}) collective-permute-start(bf16[96,2560]{1,0:T(8,128)(2,1)S(1)} %get-tuple-element.354), channel_id=1, source_target_pairs={{0,1},{1,2},{2,3},{4,5},{5,6},{6,7},{8,9},{9,10},{10,11},{12,13},{... | collective-permute-start | bytes 1474568 | tf_op jit(solution)/shard_map/ppermute | solution.py:44
  204.2 16.2 %collective-permute-start.36 = (bf16[96,2560]{1,0:T(8,128)(2,1)S(1)}, bf16[96,2560]{1,0:T(8,128)(2,1)S(1)}, u32[]{:S(2)}, u32[]{:S(2)}) collective-permute-start(bf16[96,2560]{1,0:T(8,128)(2,1)S(1)} %get-tuple-element.355), channel_id=1, source_target_pairs={{1,0},{2,1},{3,2},{5,4},{6,5},{7,6},{9,8},{10,9},{11,10},{13,12},{... | collective-permute-start | bytes 1474568 | tf_op jit(solution)/shard_map/ppermute | solution.py:44
  210.4 26.7 %collective-permute-start.20 = (bf16[96,2560]{1,0:T(8,128)(2,1)S(1)}, bf16[96,2560]{1,0:T(8,128)(2,1)S(1)}, u32[]{:S(2)}, u32[]{:S(2)}) collective-permute-start(bf16[96,2560]{1,0:T(8,128)(2,1)S(1)} %unit_gradient.5.refs_0_), channel_id=1, source_target_pairs={{1,0},{2,1},{3,2},{5,4},{6,5},{7,6},{9,8},{10,9},{11,10},{13,12},{... | collective-permute-start | bytes 1474568 | tf_op jit(solution)/shard_map/ppermute | solution.py:44
  211.7 26.7 %collective-permute-start.17 = (bf16[96,2560]{1,0:T(8,128)(2,1)S(1)}, bf16[96,2560]{1,0:T(8,128)(2,1)S(1)}, u32[]{:S(2)}, u32[]{:S(2)}) collective-permute-start(bf16[96,2560]{1,0:T(8,128)(2,1)S(1)} %unit_gradient.5.refs_0_), channel_id=1, source_target_pairs={{0,1},{1,2},{2,3},{4,5},{5,6},{6,7},{8,9},{9,10},{10,11},{12,13},{... | collective-permute-start | bytes 1474568 | tf_op jit(solution)/shard_map/ppermute | solution.py:44
  221.1 19.8 %collective-permute-start.38 = (bf16[96,2560]{1,0:T(8,128)(2,1)S(1)}, bf16[96,2560]{1,0:T(8,128)(2,1)S(1)}, u32[]{:S(2)}, u32[]{:S(2)}) collective-permute-start(bf16[96,2560]{1,0:T(8,128)(2,1)S(1)} %unit_gradient.7.refs_7_), channel_id=1, source_target_pairs={{1,0},{2,1},{3,2},{5,4},{6,5},{7,6},{9,8},{10,9},{11,10},{13,12},{... | collective-permute-start | bytes 1474568 | tf_op jit(solution)/shard_map/ppermute | solution.py:44
  222.4 18.5 %collective-permute-start.37 = (bf16[96,2560]{1,0:T(8,128)(2,1)S(1)}, bf16[96,2560]{1,0:T(8,128)(2,1)S(1)}, u32[]{:S(2)}, u32[]{:S(2)}) collective-permute-start(bf16[96,2560]{1,0:T(8,128)(2,1)S(1)} %unit_gradient.7.refs_7_), channel_id=1, source_target_pairs={{0,1},{1,2},{2,3},{4,5},{5,6},{6,7},{8,9},{9,10},{10,11},{12,13},{... | collective-permute-start | bytes 1474568 | tf_op jit(solution)/shard_map/ppermute | solution.py:44
  227.3 37.8 %copy-start.48 = (s32[8]{0:T(128)S(1)}, s32[8]{0:T(128)}, u32[]{:S(2)}) copy-start(s32[8]{0:T(128)} %param.20) | copy-start | bytes 100
  227.3 55.4 %copy-start.38 = (bf16[96,2560]{1,0:T(8,128)(2,1)S(1)}, bf16[96,2560]{1,0:T(8,128)(2,1)}, u32[]{:S(2)}) copy-start(bf16[96,2560]{1,0:T(8,128)(2,1)} %copy-done.37) | copy-start | bytes 1474564
  237.1 26.7 %copy-start.39 = (bf16[96,2560]{1,0:T(8,128)(2,1)}, bf16[96,2560]{1,0:T(8,128)(2,1)S(1)}, u32[]{:S(2)}) copy-start(bf16[96,2560]{1,0:T(8,128)(2,1)S(1)} %collective-permute-done.20.refs_4_) | copy-start | bytes 1474564
  237.1 16.0 %collective-permute-start.21 = (bf16[96,2560]{1,0:T(8,128)(2,1)S(1)}, bf16[96,2560]{1,0:T(8,128)(2,1)S(1)}, u32[]{:S(2)}, u32[]{:S(2)}) collective-permute-start(bf16[96,2560]{1,0:T(8,128)(2,1)S(1)} %collective-permute-done.20.refs_4_), channel_id=1, source_target_pairs={{1,0},{2,1},{5,4},{6,5},{9,8},{10,9},{13,12},{14,13},{17,16},{18,1... | collective-permute-start | bytes 1474568 | tf_op jit(solution)/shard_map/ppermute | solution.py:44
  238.4 26.7 %copy-start.41 = (bf16[96,2560]{1,0:T(8,128)(2,1)}, bf16[96,2560]{1,0:T(8,128)(2,1)S(1)}, u32[]{:S(2)}) copy-start(bf16[96,2560]{1,0:T(8,128)(2,1)S(1)} %collective-permute-done.17.refs_1_) | copy-start | bytes 1474564
  238.4 16.0 %collective-permute-start.18 = (bf16[96,2560]{1,0:T(8,128)(2,1)S(1)}, bf16[96,2560]{1,0:T(8,128)(2,1)S(1)}, u32[]{:S(2)}, u32[]{:S(2)}) collective-permute-start(bf16[96,2560]{1,0:T(8,128)(2,1)S(1)} %collective-permute-done.17.refs_1_), channel_id=1, source_target_pairs={{1,2},{2,3},{5,6},{6,7},{9,10},{10,11},{13,14},{14,15},{17,18},{18... | collective-permute-start | bytes 1474568 | tf_op jit(solution)/shard_map/ppermute | solution.py:44
  241.0 15.0 %collective-permute-start.39 = (bf16[96,2560]{1,0:T(8,128)(2,1)S(1)}, bf16[96,2560]{1,0:T(8,128)(2,1)S(1)}, u32[]{:S(2)}, u32[]{:S(2)}) collective-permute-start(bf16[96,2560]{1,0:T(8,128)(2,1)S(1)} %get-tuple-element.357), channel_id=1, source_target_pairs={{1,2},{2,3},{5,6},{6,7},{9,10},{10,11},{13,14},{14,15},{17,18},{18... | collective-permute-start | bytes 1474568 | tf_op jit(solution)/shard_map/ppermute | solution.py:44
  241.7 22.1 %collective-permute-start.41 = (bf16[96,2560]{1,0:T(8,128)(2,1)S(1)}, bf16[96,2560]{1,0:T(8,128)(2,1)}, u32[]{:S(2)}, u32[]{:S(2)}) collective-permute-start(bf16[96,2560]{1,0:T(8,128)(2,1)S(1)} %get-tuple-element.358), channel_id=1, source_target_pairs={{1,0},{2,1},{5,4},{6,5},{9,8},{10,9},{13,12},{14,13},{17,16},{18,1... | collective-permute-start | bytes 1474568 | tf_op jit(solution)/shard_map/ppermute | solution.py:44
  253.2 29.5 %collective-permute-start.22 = (bf16[96,2560]{1,0:T(8,128)(2,1)S(1)}, bf16[96,2560]{1,0:T(8,128)(2,1)}, u32[]{:S(2)}, u32[]{:S(2)}) collective-permute-start(bf16[96,2560]{1,0:T(8,128)(2,1)S(1)} %collective-permute-done.21.refs_5_), channel_id=1, source_target_pairs={{1,0},{5,4},{9,8},{13,12},{17,16},{21,20},{25,24},{29,28}} | collective-permute-start | bytes 1474568 | tf_op jit(solution)/shard_map/ppermute | solution.py:44
  254.5 28.2 %copy-start.43 = (bf16[96,2560]{1,0:T(8,128)(2,1)}, bf16[96,2560]{1,0:T(8,128)(2,1)S(1)}, u32[]{:S(2)}) copy-start(bf16[96,2560]{1,0:T(8,128)(2,1)S(1)} %collective-permute-done.18.refs_2_) | copy-start | bytes 1474564
  254.5 28.2 %collective-permute-start.19 = (bf16[96,2560]{1,0:T(8,128)(2,1)S(1)}, bf16[96,2560]{1,0:T(8,128)(2,1)}, u32[]{:S(2)}, u32[]{:S(2)}) collective-permute-start(bf16[96,2560]{1,0:T(8,128)(2,1)S(1)} %collective-permute-done.18.refs_2_), channel_id=1, source_target_pairs={{2,3},{6,7},{10,11},{14,15},{18,19},{22,23},{26,27},{30,31}} | collective-permute-start | bytes 1474568 | tf_op jit(solution)/shard_map/ppermute | solution.py:44
  255.9 26.7 %copy-start.45 = (bf16[96,2560]{1,0:T(8,128)(2,1)}, bf16[96,2560]{1,0:T(8,128)(2,1)S(1)}, u32[]{:S(2)}) copy-start(bf16[96,2560]{1,0:T(8,128)(2,1)S(1)} %collective-permute-done.39.refs_9_) | copy-start | bytes 1474564
  256.0 26.7 %collective-permute-start.40 = (bf16[96,2560]{1,0:T(8,128)(2,1)S(1)}, bf16[96,2560]{1,0:T(8,128)(2,1)}, u32[]{:S(2)}, u32[]{:S(2)}) collective-permute-start(bf16[96,2560]{1,0:T(8,128)(2,1)S(1)} %collective-permute-done.39.refs_9_), channel_id=1, source_target_pairs={{2,3},{6,7},{10,11},{14,15},{18,19},{22,23},{26,27},{30,31}} | collective-permute-start | bytes 1474568 | tf_op jit(solution)/shard_map/ppermute | solution.py:44
  263.8 18.8 %collective-permute-start.42 = (bf16[96,2560]{1,0:T(8,128)(2,1)}, bf16[96,2560]{1,0:T(8,128)(2,1)}, u32[]{:S(2)}, u32[]{:S(2)}) collective-permute-start(bf16[96,2560]{1,0:T(8,128)(2,1)} %collective-permute-done.41.refs_12_), channel_id=1, source_target_pairs={{1,0},{5,4},{9,8},{13,12},{17,16},{21,20},{25,24},{29,28}} | collective-permute-start | bytes 1474568 | tf_op jit(solution)/shard_map/ppermute | solution.py:44
  269.6 3.9 %collective-permute-start.45 = (f32[1]{0:T(128)}, f32[1]{0:T(128)}, u32[]{:S(2)}, u32[]{:S(2)}) collective-permute-start(f32[1]{0:T(128)} %add.35), channel_id=1, source_target_pairs={{0,4},{4,8},{8,12},{12,16},{16,20},{20,24},{24,28},{28,0},{1,5},{5... | collective-permute-start | bytes 20 | tf_op jit(solution)/shard_map/ppermute | solution.py:460
  273.4 4.5 %collective-permute-start.44 = (f32[1]{0:T(128)}, f32[1]{0:T(128)}, u32[]{:S(2)}, u32[]{:S(2)}) collective-permute-start(f32[1]{0:T(128)} %add.35), channel_id=1, source_target_pairs={{0,8},{4,12},{8,16},{12,20},{16,24},{20,28},{24,0},{28,4},{1,9},{5... | collective-permute-start | bytes 20 | tf_op jit(solution)/shard_map/ppermute | solution.py:460
  278.0 4.1 %collective-permute-start.43 = (f32[1]{0:T(128)}, f32[1]{0:T(128)}, u32[]{:S(2)}, u32[]{:S(2)}) collective-permute-start(f32[1]{0:T(128)} %add.35), channel_id=1, source_target_pairs={{0,16},{4,20},{8,24},{12,28},{16,0},{20,4},{24,8},{28,12},{1,17},{... | collective-permute-start | bytes 20 | tf_op jit(solution)/shard_map/ppermute | solution.py:460
  298.6 69.6 %collective-permute-start.2 = (bf16[640,2560]{1,0:T(8,128)(2,1)}, bf16[640,2560]{1,0:T(8,128)(2,1)}, u32[]{:S(2)}, u32[]{:S(2)}) collective-permute-start(bf16[640,2560]{1,0:T(8,128)(2,1)} %get-tuple-element.249), channel_id=1, source_target_pairs={{0,16},{4,20},{8,24},{12,28},{16,0},{20,4},{24,8},{28,12},{1,17},{... | collective-permute-start | bytes 9830408 | tf_op jit(solution)/shard_map/cond/branch_2_fun/ppermute | solution.py:433
  (33 other events, 299.3 us)

commit v5 on v4

--- a/solution.py
+++ b/solution.py
@@ -80,8 +80,9 @@
     rows, width = numer.shape
     step = rows // 4
 
-    def body(numer_ref, one_ref, out_ref):
+    def body(numer_ref, one_ref, out_ref, token_out):
         out_ref[...] = (numer_ref[...] / one_ref[...] * scaling).astype(jnp.bfloat16)
+        token_out[...] = jnp.zeros((8, 128), jnp.float32)
 
     block = (step, width), lambda i: (i, 0)
     return call(
@@ -89,11 +90,11 @@
         "scaled_weights",
         (rows // step,),
         [(numer,) + block, (weight_one.reshape(1, 1), (1, 1), fixed(0, 0))],
-        [((rows, width), jnp.bfloat16) + block],
+        [((rows, width), jnp.bfloat16) + block, TOKEN_OUT],
         flops=2 * rows * width,
         moved=6 * rows * width,
         vmem=56,
-    )[0]
+    )
 
 
 def partial_products(mine, weights, ends):
@@ -253,7 +254,7 @@
     scratch[...] = stack.T
 
 
-def weight_step(units, mine, order, kept, numer, inbox, token=None):
+def weight_step(units, mine, order, kept, numer, inbox):
     members, _, rows = mine[0][0].shape
     width = numer.shape[1] if kept is None else kept.shape[1]
     tile = tile_of(width)
@@ -278,7 +279,7 @@
             kept_out[...] = 0.5 * (numer_ref[...] - 0.004 * weight)
             token_out[...] = jnp.zeros((8, 128), jnp.float32)
         else:
-            kept_ref, inbox_ref, _, new_out, kept_out = rest
+            kept_ref, inbox_ref, new_out, kept_out = rest
             now = kept_ref[...] - 0.5 * 0.004 * weight
             new_out[...] = now + inbox_ref[...]
             kept_out[...] = now.astype(jnp.bfloat16)
@@ -291,7 +292,7 @@
         (width // tile,),
         unit_ins(units, tile)
         + mine_ins(mine)
-        + ([(numer,) + columns] if kept is None else [(kept,) + columns, (inbox,) + columns, token_in(token)]),
+        + ([(numer,) + columns] if kept is None else [(kept,) + columns, (inbox,) + columns]),
         [whole, TOKEN_OUT]
         if kept is None
         else [whole, ((rows, width), jnp.bfloat16) + columns],
@@ -299,7 +300,7 @@
         scratch=[pltpu.VMEM((rows, total), jnp.bfloat16)],
         flops=2 * total * rows * width,
         moved=2 * count * units[0][0].shape[0] * width + 12 * rows * width,
-        vmem=26,
+        vmem=52,
     )
 
 
@@ -467,7 +468,7 @@
 
     order = jnp.mod(me - jnp.arange(members, dtype=jnp.int32), members)
     own = me[None]
-    weights = scaled_weights(numer, weight_one, scaling)
+    weights, token = scaled_weights(numer, weight_one, scaling)
     everyone = range(members - 1), range(1, members)
 
     def scalars(t):
@@ -504,7 +505,8 @@
         for index, q in enumerate(members_of):
             mine[e][q] = (array, index, size)
 
-    fetch(0, list(range(count)), None)
+    for q in range(count):
+        fetch(0, [q], token if q else None)
     parts = [None] * count
     for q in range(count):
         parts[q], _, last, first = partial_products(mine[0][q], weights, True)
@@ -522,10 +524,8 @@
         for t in range(1, members - 1):
             for q in range(count):
                 right, left, token = next_payload(*moving[q], parts[q], scalars(t), False)
-                if t == 1 and q == 0 and e + 1 < rounds:
-                    fetch(e + 1, list(range(count)), token)
-                if t == 1 and q == 0 and e + 1 == rounds:
-                    outbox_weight = sent_weight(token)
+                if t == 1 and e + 1 < rounds:
+                    fetch(e + 1, [q], token)
                 if e == 0:
                     pairs = range(t + 1), range(members - 1 - t, members)
                 else:
@@ -561,12 +561,14 @@
                     early, [m for of_round in mine[:-1] for m in of_round], order, None, numer, None
                 )
                 before[q] = passed(*before[q], done)
+                outbox_weight = sent_weight(done)
+            if (s, q) == (2, 0):
+                before[q] = passed(*before[q], jnp.broadcast_to(outbox_weight[None], (8, 128)))
             before[q] = hops(*before[q], range(s, members - 1), range(1, members - s))
             units[-1][q][1].append(before[q][0])
             units[-1][q][2].append(before[q][1])
     flat = [[u] + r + l for u, r, l in units[-1]]
-    late = jnp.broadcast_to(outbox_weight[None], (8, 128))
-    new_params, half = weight_step(flat, mine[-1], order, kept, None, inbox_params[0], late)
+    new_params, half = weight_step(flat, mine[-1], order, kept, None, inbox_params[0])
     new_weight = 0.5 * push_weight + inbox_weight
     branches = [partial(tail, half, early + flat, weights, order, place) for place in range(levels)]
     sent, grad_heads = lax.switch(level_index, branches)

time: 380 us -> 381 us (level); the launches traced: 375 us -> 380 us
  starting transfers between devices: 114 us -> 126 us
  Pallas kernels: 85.3 us -> 94.9 us
  local copies, waits for them, and re-layouts: 11.7 us -> 4.4 us
  waiting for transfers between devices: 104 us -> 98.8 us
  blocking collectives: 49.7 us -> 45.1 us
    all_to_all x2 -> x4, waiting for transfers between devices: 18.2 us -> 5.96 us  [swapped(): return lax.all_to_all(blocks, 'fsdp', 0, 0, tiled=False)]
    pallas_call x27 -> x30, Pallas kernels: 85.3 us -> 94.9 us  [call(): pl.pallas_call(body, name=name, out_shape=[jax.ShapeDtypeStruct(shape, ki...]
    all_to_all x2 -> x4, starting transfers between devices: 10.8 us -> 20.3 us  [swapped(): return lax.all_to_all(blocks, 'fsdp', 0, 0, tiled=False)]
    unnamed x102 -> x94, local copies, waits for them, and re-layouts: 11.2 us -> 3.87 us
    ppermute x1, waiting for transfers between devices: 3.64 us -> 9.71 us  [tail(): lax.ppermute(kept, 'rep', [(i, (i + (1 << bit_place)) % length) for i in...]
    all_to_all x1, blocking collectives: 49.7 us -> 45.1 us  [swapped(): return lax.all_to_all(blocks, 'fsdp', 0, 0, tiled=False)]
    ppermute x40, starting transfers between devices: 96.3 us -> 100 us  [hop(): return lax.ppermute(value, 'fsdp', [(i, i + step) for i in pairs])]
  transfers between devices with their start and end apart: 46 -> 48, of which waited for: 24 -> 22; matrix products, arithmetic and copies ran while one was open for 0% -> 0% of each run, Pallas kernels for 17% -> 20%
where the time goes in v5:
time: 381 us; the launch traced here: 380 us
  starting transfers between devices  126 us (33%)
  waiting for transfers between devices  98.8 us (26%)
  Pallas kernels  94.9 us (25%)
  blocking collectives  45.1 us (12%)
  between operations  9.69 us (3%)
  local copies, waits for them, and re-layouts  4.4 us (1%)
    ppermute x40, starting transfers between devices, hop(): return lax.ppermute(value, 'fsdp', [(i, i + step) for i in pairs])  100 us
    pallas_call x30, Pallas kernels, call(): pl.pallas_call(body, name=name, out_shape=[jax.ShapeDtypeStruct(shape, ki...  94.9 us
    ppermute x40, waiting for transfers between devices, hop(): return lax.ppermute(value, 'fsdp', [(i, i + step) for i in pairs])  77.6 us
    all_to_all x1, blocking collectives, swapped(): return lax.all_to_all(blocks, 'fsdp', 0, 0, tiled=False)  45.1 us
    all_to_all x4, starting transfers between devices, swapped(): return lax.all_to_all(blocks, 'fsdp', 0, 0, tiled=False)  20.3 us
    ppermute x1, waiting for transfers between devices, tail(): lax.ppermute(kept, 'rep', [(i, (i + (1 << bit_place)) % length) for i in...  9.71 us
  transfers between devices with their start and end apart: 48, of which 22 were waited for; matrix products, arithmetic and copies ran while one was open for 0% of the time, Pallas kernels for 20%

profile of v5, /device:TPU:0, one launch (start us, length us, event | category | flops | bytes accessed | tf_op | source)
XLA Modules:
  0.0 380.1 jit_solution(18022330484244967423)
XLA Ops:
  0.6 1.8 cut_heads.4
  2.4 6.3 %all-to-all-start.3 = ((bf16[4,96,640]{2,1,0:T(8,128)(2,1)}), bf16[4,96,640]{2,1,0:T(8,128)(2,1)S(1)}, u32[]{:S(2)}, u32[]{:S(2)}) async-start(bf16[4,96,640]{2,1,0:T(8,128)(2,1)} %cut_heads.4), calls=%async_computation.3 | async-start | bytes 983040 | tf_op jit(solution)/shard_map/all_to_all | solution.py:429
  9.4 5.7 %scaled_weights.1 = (bf16[640,2560]{1,0:T(8,128)(2,1)}, f32[8,128]{1,0:T(8,128)}) custom-call(f32[640,2560]{1,0:T(8,128)} %bitcast.43, f32[1,1]{1,0:T(1,128)} %bitcast.30.one_ref), custom_call_target="tpu_custom_call" | custom-call | flops 3276800 | bytes 9830400 | tf_op jit(solution)/shard_map/scaled_weights/pallas_call | solution.py:16
  16.6 6.0 %all-to-all-done.3.mine_ref.refs_14_ = bf16[4,96,640]{2,1,0:T(8,128)(2,1)S(1)} async-done(((bf16[4,96,640]{2,1,0:T(8,128)(2,1)}), bf16[4,96,640]{2,1,0:T(8,128)(2,1)S(1)}, u32[]{:S(2)}, u32[]{:S(2)}) %all-to-all-start.3) | async-done | bytes 491552 | tf_op jit(solution)/shard_map/all_to_all | solution.py:429
  22.5 3.5 all-to-all-start.5
  26.0 4.2 %partial_products.4 = (bf16[4,96,2560]{2,1,0:T(8,128)(2,1)S(1)}, f32[8,128]{1,0:T(8,128)}, bf16[96,2560]{1,0:T(8,128)(2,1)}, bf16[96,2560]{1,0:T(8,128)(2,1)}) custom-call(bf16[4,96,640]{2,1,0:T(8,128)(2,1)S(1)} %all-to-all-done.3.mine_ref.refs_14_, bf16[640,2560]{1,0:T(8,128)(2,1)} %get-tuple-element.329.weights_ref), custom_call_target="tpu_custom_call" | custom-call | flops 1258291200 | bytes 5734400 | tf_op jit(solution)/shard_map/partial_products/pallas_call | solution.py:16
  30.2 3.9 %collective-permute-start.3 = (bf16[96,2560]{1,0:T(8,128)(2,1)}, bf16[96,2560]{1,0:T(8,128)(2,1)S(1)}, u32[]{:S(2)}, u32[]{:S(2)}) collective-permute-start(bf16[96,2560]{1,0:T(8,128)(2,1)} %get-tuple-element.330), channel_id=1, source_target_pairs={{0,1},{4,5},{8,9},{12,13},{16,17},{20,21},{24,25},{28,29}} | collective-permute-start | bytes 1474568 | tf_op jit(solution)/shard_map/ppermute | solution.py:44
  35.7 8.5 %collective-permute-done.3.right_ref = bf16[96,2560]{1,0:T(8,128)(2,1)S(1)} collective-permute-done((bf16[96,2560]{1,0:T(8,128)(2,1)}, bf16[96,2560]{1,0:T(8,128)(2,1)S(1)}, u32[]{:S(2)}, u32[]{:S(2)}) %collective-permute-start.3) | collective-permute-done | bytes 491552 | tf_op jit(solution)/shard_map/ppermute | solution.py:44
  44.2 2.6 next_payload.10
  47.6 5.9 %all-to-all-start.4 = ((bf16[4,96,640]{2,1,0:T(8,128)(2,1)}), bf16[4,96,640]{2,1,0:T(8,128)(2,1)S(1)}, u32[]{:S(2)}, u32[]{:S(2)}) async-start(bf16[4,96,640]{2,1,0:T(8,128)(2,1)} %cut_heads.5), calls=%async_computation.4 | async-start | bytes 983040 | tf_op jit(solution)/shard_map/all_to_all | solution.py:429
  53.5 4.1 %partial_products.6 = (bf16[4,96,2560]{2,1,0:T(8,128)(2,1)S(1)}, f32[8,128]{1,0:T(8,128)}, bf16[96,2560]{1,0:T(8,128)(2,1)S(1)}, bf16[96,2560]{1,0:T(8,128)(2,1)S(1)}) custom-call(bf16[4,96,640]{2,1,0:T(8,128)(2,1)S(1)} %all-to-all-done.5.mine_ref.refs_15_, bf16[640,2560]{1,0:T(8,128)(2,1)} %get-tuple-element.329.weights_ref), custom_call_target="tpu_custom_call" | custom-call | flops 1258291200 | bytes 5734400 | tf_op jit(solution)/shard_map/partial_products/pallas_call | solution.py:16
  57.6 3.9 %collective-permute-start.21 = (bf16[96,2560]{1,0:T(8,128)(2,1)S(1)}, bf16[96,2560]{1,0:T(8,128)(2,1)S(1)}, u32[]{:S(2)}, u32[]{:S(2)}) collective-permute-start(bf16[96,2560]{1,0:T(8,128)(2,1)S(1)} %get-tuple-element.347), channel_id=1, source_target_pairs={{0,1},{4,5},{8,9},{12,13},{16,17},{20,21},{24,25},{28,29}} | collective-permute-start | bytes 1474568 | tf_op jit(solution)/shard_map/ppermute | solution.py:44
  62.2 2.1 collective-permute-start.5
  65.7 7.4 %collective-permute-done.21.right_ref = bf16[96,2560]{1,0:T(8,128)(2,1)S(1)} collective-permute-done((bf16[96,2560]{1,0:T(8,128)(2,1)S(1)}, bf16[96,2560]{1,0:T(8,128)(2,1)S(1)}, u32[]{:S(2)}, u32[]{:S(2)}) %collective-permute-start.21) | collective-permute-done | bytes 491552 | tf_op jit(solution)/shard_map/ppermute | solution.py:44
  73.1 1.7 next_payload.15
  74.8 5.2 %collective-permute-start.23 = (bf16[96,2560]{1,0:T(8,128)(2,1)}, bf16[96,2560]{1,0:T(8,128)(2,1)}, u32[]{:S(2)}, u32[]{:S(2)}) collective-permute-start(bf16[96,2560]{1,0:T(8,128)(2,1)} %get-tuple-element.350), channel_id=1, source_target_pairs={{0,1},{1,2},{4,5},{5,6},{8,9},{9,10},{12,13},{13,14},{16,17},{17,1... | collective-permute-start | bytes 1474568 | tf_op jit(solution)/shard_map/ppermute | solution.py:44
  82.2 4.6 %all-to-all-start.6 = ((bf16[4,96,640]{2,1,0:T(8,128)(2,1)}), bf16[4,96,640]{2,1,0:T(8,128)(2,1)}, u32[]{:S(2)}, u32[]{:S(2)}) async-start(bf16[4,96,640]{2,1,0:T(8,128)(2,1)} %cut_heads.7), calls=%async_computation.6 | async-start | bytes 983040 | tf_op jit(solution)/shard_map/all_to_all | solution.py:429
  87.0 2.5 next_payload.11
  89.4 3.9 %collective-permute-start.7 = (bf16[96,2560]{1,0:T(8,128)(2,1)S(1)}, bf16[96,2560]{1,0:T(8,128)(2,1)S(1)}, u32[]{:S(2)}, u32[]{:S(2)}) collective-permute-start(bf16[96,2560]{1,0:T(8,128)(2,1)S(1)} %get-tuple-element.335), channel_id=1, source_target_pairs={{0,1},{1,2},{2,3},{4,5},{5,6},{6,7},{8,9},{9,10},{10,11},{12,13},{... | collective-permute-start | bytes 1474568 | tf_op jit(solution)/shard_map/ppermute | solution.py:44
  93.4 1.6 collective-permute-start.8
  95.0 2.8 next_payload.16
  97.8 5.6 %collective-permute-start.25 = (bf16[96,2560]{1,0:T(8,128)(2,1)}, bf16[96,2560]{1,0:T(8,128)(2,1)}, u32[]{:S(2)}, u32[]{:S(2)}) collective-permute-start(bf16[96,2560]{1,0:T(8,128)(2,1)} %get-tuple-element.352), channel_id=1, source_target_pairs={{0,1},{1,2},{2,3},{4,5},{5,6},{6,7},{8,9},{9,10},{10,11},{12,13},{... | collective-permute-start | bytes 1474568 | tf_op jit(solution)/shard_map/ppermute | solution.py:44
  104.7 2.2 partial_products.5
  107.0 5.7 %collective-permute-done.7.right_ref = bf16[96,2560]{1,0:T(8,128)(2,1)S(1)} collective-permute-done((bf16[96,2560]{1,0:T(8,128)(2,1)S(1)}, bf16[96,2560]{1,0:T(8,128)(2,1)S(1)}, u32[]{:S(2)}, u32[]{:S(2)}) %collective-permute-start.7) | collective-permute-done | bytes 491552 | tf_op jit(solution)/shard_map/ppermute | solution.py:44
  115.3 8.2 %collective-permute-start.9 = (bf16[96,2560]{1,0:T(8,128)(2,1)}, bf16[96,2560]{1,0:T(8,128)(2,1)}, u32[]{:S(2)}, u32[]{:S(2)}) collective-permute-start(bf16[96,2560]{1,0:T(8,128)(2,1)} %unit_gradient.4.refs_0_), channel_id=1, source_target_pairs={{0,1},{1,2},{2,3},{4,5},{5,6},{6,7},{8,9},{9,10},{10,11},{12,13},{... | collective-permute-start | bytes 1474568 | tf_op jit(solution)/shard_map/ppermute | solution.py:44
  123.6 3.7 partial_products.7
  127.4 2.2 copy-done.14
  129.6 2.4 unit_gradient.6.refs_7_
  133.3 5.4 %collective-permute-start.27 = (bf16[96,2560]{1,0:T(8,128)(2,1)}, bf16[96,2560]{1,0:T(8,128)(2,1)}, u32[]{:S(2)}, u32[]{:S(2)}) collective-permute-start(bf16[96,2560]{1,0:T(8,128)(2,1)} %unit_gradient.6.refs_7_), channel_id=1, source_target_pairs={{0,1},{1,2},{2,3},{4,5},{5,6},{6,7},{8,9},{9,10},{10,11},{12,13},{... | collective-permute-start | bytes 1474568 | tf_op jit(solution)/shard_map/ppermute | solution.py:44
  138.7 2.5 next_payload.12
  141.2 2.4 collective-permute-start.11
  144.9 4.8 %collective-permute-done.27.right_ref.refs_8_ = bf16[96,2560]{1,0:T(8,128)(2,1)} collective-permute-done((bf16[96,2560]{1,0:T(8,128)(2,1)}, bf16[96,2560]{1,0:T(8,128)(2,1)}, u32[]{:S(2)}, u32[]{:S(2)}) %collective-permute-start.27) | collective-permute-done | bytes 491552 | tf_op jit(solution)/shard_map/ppermute | solution.py:44
  149.7 2.5 next_payload.17
  152.2 4.4 %collective-permute-start.29 = (bf16[96,2560]{1,0:T(8,128)(2,1)S(1)}, bf16[96,2560]{1,0:T(8,128)(2,1)S(1)}, u32[]{:S(2)}, u32[]{:S(2)}) collective-permute-start(bf16[96,2560]{1,0:T(8,128)(2,1)S(1)} %get-tuple-element.357), channel_id=1, source_target_pairs={{0,1},{1,2},{2,3},{4,5},{5,6},{6,7},{8,9},{9,10},{10,11},{12,13},{... | collective-permute-start | bytes 1474568 | tf_op jit(solution)/shard_map/ppermute | solution.py:44
  157.9 2.3 collective-permute-done.11.right_ref.refs_2_
  161.5 4.4 %collective-permute-start.13 = (bf16[96,2560]{1,0:T(8,128)(2,1)S(1)}, bf16[96,2560]{1,0:T(8,128)(2,1)S(1)}, u32[]{:S(2)}, u32[]{:S(2)}) collective-permute-start(bf16[96,2560]{1,0:T(8,128)(2,1)S(1)} %get-tuple-element.342), channel_id=1, source_target_pairs={{0,1},{1,2},{2,3},{4,5},{5,6},{6,7},{8,9},{9,10},{10,11},{12,13},{... | collective-permute-start | bytes 1474568 | tf_op jit(solution)/shard_map/ppermute | solution.py:44
  167.2 3.5 collective-permute-done.29.right_ref.refs_9_
  170.7 1.7 collective-permute-done.30.left_ref.refs_12_
  173.6 3.0 collective-permute-start.31
  177.9 3.3 collective-permute-done.13.right_ref.refs_3_
  183.9 3.3 collective-permute-start.15
  187.2 1.6 collective-permute-start.16
  188.8 3.0 collective-permute-done.31.refs_10_.right_ref
  194.4 3.3 collective-permute-start.38
  199.0 3.3 collective-permute-done.15.right_ref
  205.6 5.3 %collective-permute-start.17 = (bf16[96,2560]{1,0:T(8,128)(2,1)S(1)}, bf16[96,2560]{1,0:T(8,128)(2,1)}, u32[]{:S(2)}, u32[]{:S(2)}) collective-permute-start(bf16[96,2560]{1,0:T(8,128)(2,1)S(1)} %unit_gradient.5.refs_0_), channel_id=1, source_target_pairs={{0,1},{1,2},{2,3},{4,5},{5,6},{6,7},{8,9},{9,10},{10,11},{12,13},{... | collective-permute-start | bytes 1474568 | tf_op jit(solution)/shard_map/ppermute | solution.py:44
  210.9 1.9 collective-permute-done.38.right_ref
  216.1 4.6 %collective-permute-start.40 = (bf16[96,2560]{1,0:T(8,128)(2,1)S(1)}, bf16[96,2560]{1,0:T(8,128)(2,1)S(1)}, u32[]{:S(2)}, u32[]{:S(2)}) collective-permute-start(bf16[96,2560]{1,0:T(8,128)(2,1)S(1)} %unit_gradient.7.refs_7_), channel_id=1, source_target_pairs={{0,1},{1,2},{2,3},{4,5},{5,6},{6,7},{8,9},{9,10},{10,11},{12,13},{... | collective-permute-start | bytes 1474568 | tf_op jit(solution)/shard_map/ppermute | solution.py:44
  220.7 4.1 %collective-permute-done.19.refs_4_ = bf16[96,2560]{1,0:T(8,128)(2,1)} collective-permute-done((bf16[96,2560]{1,0:T(8,128)(2,1)S(1)}, bf16[96,2560]{1,0:T(8,128)(2,1)}, u32[]{:S(2)}, u32[]{:S(2)}) %collective-permute-start.19) | collective-permute-done | bytes 491552 | tf_op jit(solution)/shard_map/ppermute | solution.py:44
  227.6 10.5 %weight_step.2 = (f32[640,2560]{1,0:T(8,128)}, f32[8,128]{1,0:T(8,128)S(1)}) custom-call(s32[4]{0:T(128)S(1)} %and_select_fusion.s, bf16[96,2560]{1,0:T(8,128)(2,1)} %unit_gradient.4.refs_0_, bf16[96,2560]{1,0:T(8,128)(2,1)} %collective-permute-done.9.right_ref.refs_1_, bf16[96,2560]{1,0:T(8,128)(2,1)S(1)} %collective-permute-done.11.right_ref.refs_2_, ...), custom_call_target="tpu_custom_call" | custom-call | flops 2516582400 | bytes 26542080 | tf_op jit(solution)/shard_map/weight_step/pallas_call | solution.py:16
  238.3 1.6 collective-permute-start.42
  245.2 3.0 collective-permute-done.35
  248.2 1.9 collective-permute-start.34
  250.1 2.5 collective-permute-done.34
  252.6 2.8 collective-permute-start.33
  264.9 16.5 %collective-permute-done.37.refs_6_ = bf16[96,2560]{1,0:T(8,128)(2,1)} collective-permute-done((bf16[96,2560]{1,0:T(8,128)(2,1)S(1)}, bf16[96,2560]{1,0:T(8,128)(2,1)}, u32[]{:S(2)}, u32[]{:S(2)}) %collective-permute-start.37) | collective-permute-done | bytes 491552 | tf_op jit(solution)/shard_map/ppermute | solution.py:44
  281.4 6.4 %collective-permute-done.45.refs_13_ = bf16[96,2560]{1,0:T(8,128)(2,1)S(1)} collective-permute-done((bf16[96,2560]{1,0:T(8,128)(2,1)}, bf16[96,2560]{1,0:T(8,128)(2,1)S(1)}, u32[]{:S(2)}, u32[]{:S(2)}) %collective-permute-start.45) | collective-permute-done | bytes 491552 | tf_op jit(solution)/shard_map/ppermute | solution.py:44
  288.7 14.4 %weight_step.3 = (f32[640,2560]{1,0:T(8,128)}, bf16[640,2560]{1,0:T(8,128)(2,1)}) custom-call(s32[4]{0:T(128)S(1)} %and_select_fusion.s, bf16[96,2560]{1,0:T(8,128)(2,1)S(1)} %copy-done.36, bf16[96,2560]{1,0:T(8,128)(2,1)} %collective-permute-done.17.refs_1_, bf16[96,2560]{1,0:T(8,128)(2,1)} %collective-permute-done.18.right_ref.refs_2_, ...), custom_call_target="tpu_custom_call" | custom-call | flops 2516582400 | bytes 26542080 | tf_op jit(solution)/shard_map/weight_step/pallas_call | solution.py:16
  303.2 70.2 %conditional.1 = (bf16[640,2560]{1,0:T(8,128)(2,1)}, bf16[1,384,2560]{2,1,0:T(8,128)(2,1)}) conditional(s32[]{:T(128)} %clamp.3, (bf16[640,2560]{1,0:T(8,128)(2,1)}, s32[4]{0:T(128)S(1)}, bf16[96,2560]{1,0:T(8,128)(2,1)}, bf16[96,2560]{1,0:T(8,128)(2,1)}, bf16[96,2560]{1,0:T(8,128)(2,1)S(1)}, ...), branch_computations={%region_1.2_spmd, %region_2.3_spmd, %region_3.4_spmd} | conditional | flops 5033164800 | bytes 38010936 | solution.py:574
  303.4 13.3 %grad_rows.4 = bf16[4,384,640]{2,1,0:T(8,128)(2,1)S(1)} custom-call(s32[4]{0:T(128)S(1)} %get-tuple-element.219.s, bf16[96,2560]{1,0:T(8,128)(2,1)} %get-tuple-element.220.refs_0_, bf16[96,2560]{1,0:T(8,128)(2,1)} %get-tuple-element.221.refs_1_, bf16[96,2560]{1,0:T(8,128)(2,1)S(1)} %get-tuple-element.222.refs_2_, ...), custom_call_target="tpu_custom_call" | custom-call | flops 5033164800 | bytes 17039360 | tf_op jit(solution)/shard_map/cond/branch_1_fun/grad_rows/pallas_call | solution.py:16
  316.7 45.1 %all_to_all.33.blocks_ref = bf16[4,384,640]{2,1,0:T(8,128)(2,1)S(1)} all-to-all(bf16[4,384,640]{2,1,0:T(8,128)(2,1)S(1)} %grad_rows.4), channel_id=1, replica_groups=mesh['rep'=8,'fsdp'=4] {'fsdp'}, dimensions={0} | all-to-all | bytes 3932160 | tf_op jit(solution)/shard_map/cond/branch_1_fun/all_to_all | solution.py:429
  361.7 1.9 joined_rows.4
  363.7 9.7 %collective-permute-done.1 = bf16[640,2560]{1,0:T(8,128)(2,1)} collective-permute-done((bf16[640,2560]{1,0:T(8,128)(2,1)}, bf16[640,2560]{1,0:T(8,128)(2,1)}, u32[]{:S(2)}, u32[]{:S(2)}) %collective-permute-start.1) | collective-permute-done | bytes 3276832 | tf_op jit(solution)/shard_map/cond/branch_1_fun/ppermute | solution.py:434
  373.4 4.4 %widened.1 = f32[640,2560]{1,0:T(8,128)} custom-call(bf16[640,2560]{1,0:T(8,128)(2,1)} %get-tuple-element.371.value_ref), custom_call_target="tpu_custom_call" | custom-call | bytes 9830400 | tf_op jit(solution)/shard_map/widened/pallas_call | solution.py:16
  (166 shorter events, 48.1 us)
Async XLA Ops:
  2.4 20.1 %all-to-all-start.3 = ((bf16[4,96,640]{2,1,0:T(8,128)(2,1)}), bf16[4,96,640]{2,1,0:T(8,128)(2,1)S(1)}, u32[]{:S(2)}, u32[]{:S(2)}) async-start(bf16[4,96,640]{2,1,0:T(8,128)(2,1)} %cut_heads.4), calls=%async_computation.3 | async-start | bytes 983040 | tf_op jit(solution)/shard_map/all_to_all | solution.py:429
  22.5 25.1 %all-to-all-start.5 = ((bf16[4,96,640]{2,1,0:T(8,128)(2,1)}), bf16[4,96,640]{2,1,0:T(8,128)(2,1)S(1)}, u32[]{:S(2)}, u32[]{:S(2)}) async-start(bf16[4,96,640]{2,1,0:T(8,128)(2,1)} %cut_heads.6), calls=%async_computation.5 | async-start | bytes 983040 | tf_op jit(solution)/shard_map/all_to_all | solution.py:429
  30.2 56.7 %copy-start.2 = (bf16[4,96,2560]{2,1,0:T(8,128)(2,1)}, bf16[4,96,2560]{2,1,0:T(8,128)(2,1)S(1)}, u32[]{:S(2)}) copy-start(bf16[4,96,2560]{2,1,0:T(8,128)(2,1)S(1)} %get-tuple-element.332.of_right.of_left.own_ref) | copy-start | bytes 5898244
  30.2 14.0 %collective-permute-start.3 = (bf16[96,2560]{1,0:T(8,128)(2,1)}, bf16[96,2560]{1,0:T(8,128)(2,1)S(1)}, u32[]{:S(2)}, u32[]{:S(2)}) collective-permute-start(bf16[96,2560]{1,0:T(8,128)(2,1)} %get-tuple-element.330), channel_id=1, source_target_pairs={{0,1},{4,5},{8,9},{12,13},{16,17},{20,21},{24,25},{28,29}} | collective-permute-start | bytes 1474568 | tf_op jit(solution)/shard_map/ppermute | solution.py:44
  34.1 10.1 %collective-permute-start.4 = (bf16[96,2560]{1,0:T(8,128)(2,1)}, bf16[96,2560]{1,0:T(8,128)(2,1)}, u32[]{:S(2)}, u32[]{:S(2)}) collective-permute-start(bf16[96,2560]{1,0:T(8,128)(2,1)} %get-tuple-element.331), channel_id=1, source_target_pairs={{3,2},{7,6},{11,10},{15,14},{19,18},{23,22},{27,26},{31,30}} | collective-permute-start | bytes 1474568 | tf_op jit(solution)/shard_map/ppermute | solution.py:44
  47.6 34.6 %all-to-all-start.4 = ((bf16[4,96,640]{2,1,0:T(8,128)(2,1)}), bf16[4,96,640]{2,1,0:T(8,128)(2,1)S(1)}, u32[]{:S(2)}, u32[]{:S(2)}) async-start(bf16[4,96,640]{2,1,0:T(8,128)(2,1)} %cut_heads.5), calls=%async_computation.4 | async-start | bytes 983040 | tf_op jit(solution)/shard_map/all_to_all | solution.py:429
  57.6 17.2 %copy-start.4 = (bf16[4,96,2560]{2,1,0:T(8,128)(2,1)}, bf16[4,96,2560]{2,1,0:T(8,128)(2,1)S(1)}, u32[]{:S(2)}) copy-start(bf16[4,96,2560]{2,1,0:T(8,128)(2,1)S(1)} %get-tuple-element.349.of_right.of_left.own_ref) | copy-start | bytes 5898244
  57.6 15.6 %collective-permute-start.21 = (bf16[96,2560]{1,0:T(8,128)(2,1)S(1)}, bf16[96,2560]{1,0:T(8,128)(2,1)S(1)}, u32[]{:S(2)}, u32[]{:S(2)}) collective-permute-start(bf16[96,2560]{1,0:T(8,128)(2,1)S(1)} %get-tuple-element.347), channel_id=1, source_target_pairs={{0,1},{4,5},{8,9},{12,13},{16,17},{20,21},{24,25},{28,29}} | collective-permute-start | bytes 1474568 | tf_op jit(solution)/shard_map/ppermute | solution.py:44
  61.5 11.6 %collective-permute-start.22 = (bf16[96,2560]{1,0:T(8,128)(2,1)S(1)}, bf16[96,2560]{1,0:T(8,128)(2,1)S(1)}, u32[]{:S(2)}, u32[]{:S(2)}) collective-permute-start(bf16[96,2560]{1,0:T(8,128)(2,1)S(1)} %get-tuple-element.348), channel_id=1, source_target_pairs={{3,2},{7,6},{11,10},{15,14},{19,18},{23,22},{27,26},{31,30}} | collective-permute-start | bytes 1474568 | tf_op jit(solution)/shard_map/ppermute | solution.py:44
  62.2 24.7 %collective-permute-start.5 = (bf16[96,2560]{1,0:T(8,128)(2,1)}, bf16[96,2560]{1,0:T(8,128)(2,1)}, u32[]{:S(2)}, u32[]{:S(2)}) collective-permute-start(bf16[96,2560]{1,0:T(8,128)(2,1)} %get-tuple-element.333), channel_id=1, source_target_pairs={{0,1},{1,2},{4,5},{5,6},{8,9},{9,10},{12,13},{13,14},{16,17},{17,1... | collective-permute-start | bytes 1474568 | tf_op jit(solution)/shard_map/ppermute | solution.py:44
  64.3 22.7 %collective-permute-start.6 = (bf16[96,2560]{1,0:T(8,128)(2,1)}, bf16[96,2560]{1,0:T(8,128)(2,1)}, u32[]{:S(2)}, u32[]{:S(2)}) collective-permute-start(bf16[96,2560]{1,0:T(8,128)(2,1)} %get-tuple-element.334), channel_id=1, source_target_pairs={{2,1},{3,2},{6,5},{7,6},{10,9},{11,10},{14,13},{15,14},{18,17},{19... | collective-permute-start | bytes 1474568 | tf_op jit(solution)/shard_map/ppermute | solution.py:44
  74.8 20.2 %collective-permute-start.23 = (bf16[96,2560]{1,0:T(8,128)(2,1)}, bf16[96,2560]{1,0:T(8,128)(2,1)}, u32[]{:S(2)}, u32[]{:S(2)}) collective-permute-start(bf16[96,2560]{1,0:T(8,128)(2,1)} %get-tuple-element.350), channel_id=1, source_target_pairs={{0,1},{1,2},{4,5},{5,6},{8,9},{9,10},{12,13},{13,14},{16,17},{17,1... | collective-permute-start | bytes 1474568 | tf_op jit(solution)/shard_map/ppermute | solution.py:44
  80.0 15.0 %collective-permute-start.24 = (bf16[96,2560]{1,0:T(8,128)(2,1)}, bf16[96,2560]{1,0:T(8,128)(2,1)}, u32[]{:S(2)}, u32[]{:S(2)}) collective-permute-start(bf16[96,2560]{1,0:T(8,128)(2,1)} %get-tuple-element.351), channel_id=1, source_target_pairs={{2,1},{3,2},{6,5},{7,6},{10,9},{11,10},{14,13},{15,14},{18,17},{19... | collective-permute-start | bytes 1474568 | tf_op jit(solution)/shard_map/ppermute | solution.py:44
  82.2 41.4 %all-to-all-start.6 = ((bf16[4,96,640]{2,1,0:T(8,128)(2,1)}), bf16[4,96,640]{2,1,0:T(8,128)(2,1)}, u32[]{:S(2)}, u32[]{:S(2)}) async-start(bf16[4,96,640]{2,1,0:T(8,128)(2,1)} %cut_heads.7), calls=%async_computation.6 | async-start | bytes 983040 | tf_op jit(solution)/shard_map/all_to_all | solution.py:429
  89.4 23.2 %collective-permute-start.7 = (bf16[96,2560]{1,0:T(8,128)(2,1)S(1)}, bf16[96,2560]{1,0:T(8,128)(2,1)S(1)}, u32[]{:S(2)}, u32[]{:S(2)}) collective-permute-start(bf16[96,2560]{1,0:T(8,128)(2,1)S(1)} %get-tuple-element.335), channel_id=1, source_target_pairs={{0,1},{1,2},{2,3},{4,5},{5,6},{6,7},{8,9},{9,10},{10,11},{12,13},{... | collective-permute-start | bytes 1474568 | tf_op jit(solution)/shard_map/ppermute | solution.py:44
  93.4 19.3 %collective-permute-start.8 = (bf16[96,2560]{1,0:T(8,128)(2,1)S(1)}, bf16[96,2560]{1,0:T(8,128)(2,1)S(1)}, u32[]{:S(2)}, u32[]{:S(2)}) collective-permute-start(bf16[96,2560]{1,0:T(8,128)(2,1)S(1)} %get-tuple-element.336), channel_id=1, source_target_pairs={{1,0},{2,1},{3,2},{5,4},{6,5},{7,6},{9,8},{10,9},{11,10},{13,12},{... | collective-permute-start | bytes 1474568 | tf_op jit(solution)/shard_map/ppermute | solution.py:44
  95.0 17.7 %copy-start.13 = (bf16[1,384,2560]{2,1,0:T(8,128)(2,1)S(1)}, bf16[1,384,2560]{2,1,0:T(8,128)(2,1)}, u32[]{:S(2)}) copy-start(bf16[1,384,2560]{2,1,0:T(8,128)(2,1)} %param.18) | copy-start | bytes 5898244
  97.8 29.5 %collective-permute-start.25 = (bf16[96,2560]{1,0:T(8,128)(2,1)}, bf16[96,2560]{1,0:T(8,128)(2,1)}, u32[]{:S(2)}, u32[]{:S(2)}) collective-permute-start(bf16[96,2560]{1,0:T(8,128)(2,1)} %get-tuple-element.352), channel_id=1, source_target_pairs={{0,1},{1,2},{2,3},{4,5},{5,6},{6,7},{8,9},{9,10},{10,11},{12,13},{... | collective-permute-start | bytes 1474568 | tf_op jit(solution)/shard_map/ppermute | solution.py:44
  103.4 23.9 %collective-permute-start.26 = (bf16[96,2560]{1,0:T(8,128)(2,1)}, bf16[96,2560]{1,0:T(8,128)(2,1)}, u32[]{:S(2)}, u32[]{:S(2)}) collective-permute-start(bf16[96,2560]{1,0:T(8,128)(2,1)} %get-tuple-element.353), channel_id=1, source_target_pairs={{1,0},{2,1},{3,2},{5,4},{6,5},{7,6},{9,8},{10,9},{11,10},{13,12},{... | collective-permute-start | bytes 1474568 | tf_op jit(solution)/shard_map/ppermute | solution.py:44
  114.1 24.6 %collective-permute-start.10 = (bf16[96,2560]{1,0:T(8,128)(2,1)}, bf16[96,2560]{1,0:T(8,128)(2,1)}, u32[]{:S(2)}, u32[]{:S(2)}) collective-permute-start(bf16[96,2560]{1,0:T(8,128)(2,1)} %unit_gradient.4.refs_0_), channel_id=1, source_target_pairs={{1,0},{2,1},{3,2},{5,4},{6,5},{7,6},{9,8},{10,9},{11,10},{13,12},{... | collective-permute-start | bytes 1474568 | tf_op jit(solution)/shard_map/ppermute | solution.py:44
  115.3 23.4 %collective-permute-start.9 = (bf16[96,2560]{1,0:T(8,128)(2,1)}, bf16[96,2560]{1,0:T(8,128)(2,1)}, u32[]{:S(2)}, u32[]{:S(2)}) collective-permute-start(bf16[96,2560]{1,0:T(8,128)(2,1)} %unit_gradient.4.refs_0_), channel_id=1, source_target_pairs={{0,1},{1,2},{2,3},{4,5},{5,6},{6,7},{8,9},{9,10},{10,11},{12,13},{... | collective-permute-start | bytes 1474568 | tf_op jit(solution)/shard_map/ppermute | solution.py:44
  132.0 12.9 %collective-permute-start.28 = (bf16[96,2560]{1,0:T(8,128)(2,1)}, bf16[96,2560]{1,0:T(8,128)(2,1)}, u32[]{:S(2)}, u32[]{:S(2)}) collective-permute-start(bf16[96,2560]{1,0:T(8,128)(2,1)} %unit_gradient.6.refs_7_), channel_id=1, source_target_pairs={{1,0},{2,1},{3,2},{5,4},{6,5},{7,6},{9,8},{10,9},{11,10},{13,12},{... | collective-permute-start | bytes 1474568 | tf_op jit(solution)/shard_map/ppermute | solution.py:44
  133.3 16.4 %collective-permute-start.27 = (bf16[96,2560]{1,0:T(8,128)(2,1)}, bf16[96,2560]{1,0:T(8,128)(2,1)}, u32[]{:S(2)}, u32[]{:S(2)}) collective-permute-start(bf16[96,2560]{1,0:T(8,128)(2,1)} %unit_gradient.6.refs_7_), channel_id=1, source_target_pairs={{0,1},{1,2},{2,3},{4,5},{5,6},{6,7},{8,9},{9,10},{10,11},{12,13},{... | collective-permute-start | bytes 1474568 | tf_op jit(solution)/shard_map/ppermute | solution.py:44
  141.2 18.9 %collective-permute-start.11 = (bf16[96,2560]{1,0:T(8,128)(2,1)S(1)}, bf16[96,2560]{1,0:T(8,128)(2,1)S(1)}, u32[]{:S(2)}, u32[]{:S(2)}) collective-permute-start(bf16[96,2560]{1,0:T(8,128)(2,1)S(1)} %get-tuple-element.340), channel_id=1, source_target_pairs={{0,1},{1,2},{2,3},{4,5},{5,6},{6,7},{8,9},{9,10},{10,11},{12,13},{... | collective-permute-start | bytes 1474568 | tf_op jit(solution)/shard_map/ppermute | solution.py:44
  143.6 16.6 %collective-permute-start.12 = (bf16[96,2560]{1,0:T(8,128)(2,1)S(1)}, bf16[96,2560]{1,0:T(8,128)(2,1)S(1)}, u32[]{:S(2)}, u32[]{:S(2)}) collective-permute-start(bf16[96,2560]{1,0:T(8,128)(2,1)S(1)} %get-tuple-element.341), channel_id=1, source_target_pairs={{1,0},{2,1},{3,2},{5,4},{6,5},{7,6},{9,8},{10,9},{11,10},{13,12},{... | collective-permute-start | bytes 1474568 | tf_op jit(solution)/shard_map/ppermute | solution.py:44
  152.2 18.5 %collective-permute-start.29 = (bf16[96,2560]{1,0:T(8,128)(2,1)S(1)}, bf16[96,2560]{1,0:T(8,128)(2,1)S(1)}, u32[]{:S(2)}, u32[]{:S(2)}) collective-permute-start(bf16[96,2560]{1,0:T(8,128)(2,1)S(1)} %get-tuple-element.357), channel_id=1, source_target_pairs={{0,1},{1,2},{2,3},{4,5},{5,6},{6,7},{8,9},{9,10},{10,11},{12,13},{... | collective-permute-start | bytes 1474568 | tf_op jit(solution)/shard_map/ppermute | solution.py:44
  156.6 15.7 %collective-permute-start.30 = (bf16[96,2560]{1,0:T(8,128)(2,1)S(1)}, bf16[96,2560]{1,0:T(8,128)(2,1)S(1)}, u32[]{:S(2)}, u32[]{:S(2)}) collective-permute-start(bf16[96,2560]{1,0:T(8,128)(2,1)S(1)} %get-tuple-element.358), channel_id=1, source_target_pairs={{1,0},{2,1},{3,2},{5,4},{6,5},{7,6},{9,8},{10,9},{11,10},{13,12},{... | collective-permute-start | bytes 1474568 | tf_op jit(solution)/shard_map/ppermute | solution.py:44
  160.1 67.5 %copy-start.19 = (bf16[96,2560]{1,0:T(8,128)(2,1)}, bf16[96,2560]{1,0:T(8,128)(2,1)S(1)}, u32[]{:S(2)}) copy-start(bf16[96,2560]{1,0:T(8,128)(2,1)S(1)} %collective-permute-done.11.right_ref.refs_2_) | copy-start | bytes 1474564
  160.1 67.4 %copy-start.21 = (bf16[96,2560]{1,0:T(8,128)(2,1)}, bf16[96,2560]{1,0:T(8,128)(2,1)S(1)}, u32[]{:S(2)}) copy-start(bf16[96,2560]{1,0:T(8,128)(2,1)S(1)} %collective-permute-done.12.left_ref.refs_5_) | copy-start | bytes 1474564
  161.5 19.7 %collective-permute-start.13 = (bf16[96,2560]{1,0:T(8,128)(2,1)S(1)}, bf16[96,2560]{1,0:T(8,128)(2,1)S(1)}, u32[]{:S(2)}, u32[]{:S(2)}) collective-permute-start(bf16[96,2560]{1,0:T(8,128)(2,1)S(1)} %get-tuple-element.342), channel_id=1, source_target_pairs={{0,1},{1,2},{2,3},{4,5},{5,6},{6,7},{8,9},{9,10},{10,11},{12,13},{... | collective-permute-start | bytes 1474568 | tf_op jit(solution)/shard_map/ppermute | solution.py:44
  165.9 16.7 %collective-permute-start.14 = (bf16[96,2560]{1,0:T(8,128)(2,1)S(1)}, bf16[96,2560]{1,0:T(8,128)(2,1)S(1)}, u32[]{:S(2)}, u32[]{:S(2)}) collective-permute-start(bf16[96,2560]{1,0:T(8,128)(2,1)S(1)} %get-tuple-element.343), channel_id=1, source_target_pairs={{1,0},{2,1},{3,2},{5,4},{6,5},{7,6},{9,8},{10,9},{11,10},{13,12},{... | collective-permute-start | bytes 1474568 | tf_op jit(solution)/shard_map/ppermute | solution.py:44
  170.7 56.9 %copy-start.23 = (bf16[96,2560]{1,0:T(8,128)(2,1)}, bf16[96,2560]{1,0:T(8,128)(2,1)S(1)}, u32[]{:S(2)}) copy-start(bf16[96,2560]{1,0:T(8,128)(2,1)S(1)} %collective-permute-done.29.right_ref.refs_9_) | copy-start | bytes 1474564
  172.3 55.3 %copy-start.25 = (bf16[96,2560]{1,0:T(8,128)(2,1)}, bf16[96,2560]{1,0:T(8,128)(2,1)S(1)}, u32[]{:S(2)}) copy-start(bf16[96,2560]{1,0:T(8,128)(2,1)S(1)} %collective-permute-done.30.left_ref.refs_12_) | copy-start | bytes 1474564
  173.6 18.1 %collective-permute-start.31 = (bf16[96,2560]{1,0:T(8,128)(2,1)S(1)}, bf16[96,2560]{1,0:T(8,128)(2,1)S(1)}, u32[]{:S(2)}, u32[]{:S(2)}) collective-permute-start(bf16[96,2560]{1,0:T(8,128)(2,1)S(1)} %get-tuple-element.359), channel_id=1, source_target_pairs={{0,1},{1,2},{2,3},{4,5},{5,6},{6,7},{8,9},{9,10},{10,11},{12,13},{... | collective-permute-start | bytes 1474568 | tf_op jit(solution)/shard_map/ppermute | solution.py:44
  176.6 16.5 %collective-permute-start.32 = (bf16[96,2560]{1,0:T(8,128)(2,1)S(1)}, bf16[96,2560]{1,0:T(8,128)(2,1)S(1)}, u32[]{:S(2)}, u32[]{:S(2)}) collective-permute-start(bf16[96,2560]{1,0:T(8,128)(2,1)S(1)} %get-tuple-element.360), channel_id=1, source_target_pairs={{1,0},{2,1},{3,2},{5,4},{6,5},{7,6},{9,8},{10,9},{11,10},{13,12},{... | collective-permute-start | bytes 1474568 | tf_op jit(solution)/shard_map/ppermute | solution.py:44
  181.2 46.4 %copy-start.27 = (bf16[96,2560]{1,0:T(8,128)(2,1)}, bf16[96,2560]{1,0:T(8,128)(2,1)S(1)}, u32[]{:S(2)}) copy-start(bf16[96,2560]{1,0:T(8,128)(2,1)S(1)} %collective-permute-done.13.right_ref.refs_3_) | copy-start | bytes 1474564
  182.6 45.0 %copy-start.29 = (bf16[96,2560]{1,0:T(8,128)(2,1)}, bf16[96,2560]{1,0:T(8,128)(2,1)S(1)}, u32[]{:S(2)}) copy-start(bf16[96,2560]{1,0:T(8,128)(2,1)S(1)} %collective-permute-done.14.left_ref.refs_6_) | copy-start | bytes 1474564
  183.9 18.4 %collective-permute-start.15 = (bf16[96,2560]{1,0:T(8,128)(2,1)S(1)}, bf16[96,2560]{1,0:T(8,128)(2,1)S(1)}, u32[]{:S(2)}, u32[]{:S(2)}) collective-permute-start(bf16[96,2560]{1,0:T(8,128)(2,1)S(1)} %get-tuple-element.344), channel_id=1, source_target_pairs={{0,1},{1,2},{2,3},{4,5},{5,6},{6,7},{8,9},{9,10},{10,11},{12,13},{... | collective-permute-start | bytes 1474568 | tf_op jit(solution)/shard_map/ppermute | solution.py:44
  187.2 16.5 %copy-start.12 = (bf16[1,384,2560]{2,1,0:T(8,128)(2,1)S(1)}, bf16[1,384,2560]{2,1,0:T(8,128)(2,1)}, u32[]{:S(2)}) copy-start(bf16[1,384,2560]{2,1,0:T(8,128)(2,1)} %param.17) | copy-start | bytes 5898244
  187.2 16.4 %copy-start.15 = (bf16[1,384,2560]{2,1,0:T(8,128)(2,1)S(1)}, bf16[1,384,2560]{2,1,0:T(8,128)(2,1)}, u32[]{:S(2)}) copy-start(bf16[1,384,2560]{2,1,0:T(8,128)(2,1)} %param.18) | copy-start | bytes 5898244
  187.2 16.4 %collective-permute-start.16 = (bf16[96,2560]{1,0:T(8,128)(2,1)S(1)}, bf16[96,2560]{1,0:T(8,128)(2,1)S(1)}, u32[]{:S(2)}, u32[]{:S(2)}) collective-permute-start(bf16[96,2560]{1,0:T(8,128)(2,1)S(1)} %get-tuple-element.345), channel_id=1, source_target_pairs={{1,0},{2,1},{3,2},{5,4},{6,5},{7,6},{9,8},{10,9},{11,10},{13,12},{... | collective-permute-start | bytes 1474568 | tf_op jit(solution)/shard_map/ppermute | solution.py:44
  191.7 35.9 %copy-start.31 = (bf16[96,2560]{1,0:T(8,128)(2,1)}, bf16[96,2560]{1,0:T(8,128)(2,1)S(1)}, u32[]{:S(2)}) copy-start(bf16[96,2560]{1,0:T(8,128)(2,1)S(1)} %collective-permute-done.31.refs_10_.right_ref) | copy-start | bytes 1474564
  193.1 34.5 %copy-start.33 = (bf16[96,2560]{1,0:T(8,128)(2,1)}, bf16[96,2560]{1,0:T(8,128)(2,1)S(1)}, u32[]{:S(2)}) copy-start(bf16[96,2560]{1,0:T(8,128)(2,1)S(1)} %collective-permute-done.32.refs_13_.left_ref) | copy-start | bytes 1474564
  194.4 18.4 %collective-permute-start.38 = (bf16[96,2560]{1,0:T(8,128)(2,1)S(1)}, bf16[96,2560]{1,0:T(8,128)(2,1)S(1)}, u32[]{:S(2)}, u32[]{:S(2)}) collective-permute-start(bf16[96,2560]{1,0:T(8,128)(2,1)S(1)} %get-tuple-element.364), channel_id=1, source_target_pairs={{0,1},{1,2},{2,3},{4,5},{5,6},{6,7},{8,9},{9,10},{10,11},{12,13},{... | collective-permute-start | bytes 1474568 | tf_op jit(solution)/shard_map/ppermute | solution.py:44
  197.7 16.5 %collective-permute-start.39 = (bf16[96,2560]{1,0:T(8,128)(2,1)S(1)}, bf16[96,2560]{1,0:T(8,128)(2,1)S(1)}, u32[]{:S(2)}, u32[]{:S(2)}) collective-permute-start(bf16[96,2560]{1,0:T(8,128)(2,1)S(1)} %get-tuple-element.365), channel_id=1, source_target_pairs={{1,0},{2,1},{3,2},{5,4},{6,5},{7,6},{9,8},{10,9},{11,10},{13,12},{... | collective-permute-start | bytes 1474568 | tf_op jit(solution)/shard_map/ppermute | solution.py:44
  204.3 20.5 %collective-permute-start.19 = (bf16[96,2560]{1,0:T(8,128)(2,1)S(1)}, bf16[96,2560]{1,0:T(8,128)(2,1)}, u32[]{:S(2)}, u32[]{:S(2)}) collective-permute-start(bf16[96,2560]{1,0:T(8,128)(2,1)S(1)} %unit_gradient.5.refs_0_), channel_id=1, source_target_pairs={{1,0},{2,1},{3,2},{5,4},{6,5},{7,6},{9,8},{10,9},{11,10},{13,12},{... | collective-permute-start | bytes 1474568 | tf_op jit(solution)/shard_map/ppermute | solution.py:44
  205.6 20.5 %collective-permute-start.17 = (bf16[96,2560]{1,0:T(8,128)(2,1)S(1)}, bf16[96,2560]{1,0:T(8,128)(2,1)}, u32[]{:S(2)}, u32[]{:S(2)}) collective-permute-start(bf16[96,2560]{1,0:T(8,128)(2,1)S(1)} %unit_gradient.5.refs_0_), channel_id=1, source_target_pairs={{0,1},{1,2},{2,3},{4,5},{5,6},{6,7},{8,9},{9,10},{10,11},{12,13},{... | collective-permute-start | bytes 1474568 | tf_op jit(solution)/shard_map/ppermute | solution.py:44
  214.8 23.3 %collective-permute-start.41 = (bf16[96,2560]{1,0:T(8,128)(2,1)S(1)}, bf16[96,2560]{1,0:T(8,128)(2,1)S(1)}, u32[]{:S(2)}, u32[]{:S(2)}) collective-permute-start(bf16[96,2560]{1,0:T(8,128)(2,1)S(1)} %unit_gradient.7.refs_7_), channel_id=1, source_target_pairs={{1,0},{2,1},{3,2},{5,4},{6,5},{7,6},{9,8},{10,9},{11,10},{13,12},{... | collective-permute-start | bytes 1474568 | tf_op jit(solution)/shard_map/ppermute | solution.py:44
  216.1 22.0 %collective-permute-start.40 = (bf16[96,2560]{1,0:T(8,128)(2,1)S(1)}, bf16[96,2560]{1,0:T(8,128)(2,1)S(1)}, u32[]{:S(2)}, u32[]{:S(2)}) collective-permute-start(bf16[96,2560]{1,0:T(8,128)(2,1)S(1)} %unit_gradient.7.refs_7_), channel_id=1, source_target_pairs={{0,1},{1,2},{2,3},{4,5},{5,6},{6,7},{8,9},{9,10},{10,11},{12,13},{... | collective-permute-start | bytes 1474568 | tf_op jit(solution)/shard_map/ppermute | solution.py:44
  220.7 20.5 %copy-start.46 = (s32[8]{0:T(128)S(1)}, s32[8]{0:T(128)}, u32[]{:S(2)}) copy-start(s32[8]{0:T(128)} %param.20) | copy-start | bytes 100
  224.8 32.6 %collective-permute-start.20 = (bf16[96,2560]{1,0:T(8,128)(2,1)}, bf16[96,2560]{1,0:T(8,128)(2,1)}, u32[]{:S(2)}, u32[]{:S(2)}) collective-permute-start(bf16[96,2560]{1,0:T(8,128)(2,1)} %collective-permute-done.19.refs_4_), channel_id=1, source_target_pairs={{1,0},{2,1},{5,4},{6,5},{9,8},{10,9},{13,12},{14,13},{17,16},{18,1... | collective-permute-start | bytes 1474568 | tf_op jit(solution)/shard_map/ppermute | solution.py:44
  226.1 31.3 %collective-permute-start.18 = (bf16[96,2560]{1,0:T(8,128)(2,1)}, bf16[96,2560]{1,0:T(8,128)(2,1)}, u32[]{:S(2)}, u32[]{:S(2)}) collective-permute-start(bf16[96,2560]{1,0:T(8,128)(2,1)} %collective-permute-done.17.refs_1_), channel_id=1, source_target_pairs={{1,2},{2,3},{5,6},{6,7},{9,10},{10,11},{13,14},{14,15},{17,18},{18... | collective-permute-start | bytes 1474568 | tf_op jit(solution)/shard_map/ppermute | solution.py:44
  238.1 50.4 %copy-start.36 = (bf16[96,2560]{1,0:T(8,128)(2,1)S(1)}, bf16[96,2560]{1,0:T(8,128)(2,1)}, u32[]{:S(2)}) copy-start(bf16[96,2560]{1,0:T(8,128)(2,1)} %copy-done.35) | copy-start | bytes 1474564
  238.1 19.3 %copy-start.37 = (bf16[96,2560]{1,0:T(8,128)(2,1)}, bf16[96,2560]{1,0:T(8,128)(2,1)S(1)}, u32[]{:S(2)}) copy-start(bf16[96,2560]{1,0:T(8,128)(2,1)S(1)} %collective-permute-done.41.left_ref.refs_11_) | copy-start | bytes 1474564
  238.3 23.3 %collective-permute-start.42 = (bf16[96,2560]{1,0:T(8,128)(2,1)S(1)}, bf16[96,2560]{1,0:T(8,128)(2,1)}, u32[]{:S(2)}, u32[]{:S(2)}) collective-permute-start(bf16[96,2560]{1,0:T(8,128)(2,1)S(1)} %get-tuple-element.366), channel_id=1, source_target_pairs={{1,2},{2,3},{5,6},{6,7},{9,10},{10,11},{13,14},{14,15},{17,18},{18... | collective-permute-start | bytes 1474568 | tf_op jit(solution)/shard_map/ppermute | solution.py:44
  239.9 22.4 %collective-permute-start.44 = (bf16[96,2560]{1,0:T(8,128)(2,1)S(1)}, bf16[96,2560]{1,0:T(8,128)(2,1)}, u32[]{:S(2)}, u32[]{:S(2)}) collective-permute-start(bf16[96,2560]{1,0:T(8,128)(2,1)S(1)} %get-tuple-element.367), channel_id=1, source_target_pairs={{1,0},{2,1},{5,4},{6,5},{9,8},{10,9},{13,12},{14,13},{17,16},{18,1... | collective-permute-start | bytes 1474568 | tf_op jit(solution)/shard_map/ppermute | solution.py:44
  244.3 3.9 %collective-permute-start.35 = (f32[1]{0:T(128)}, f32[1]{0:T(128)}, u32[]{:S(2)}, u32[]{:S(2)}) collective-permute-start(f32[1]{0:T(128)} %add.35), channel_id=1, source_target_pairs={{0,4},{4,8},{8,12},{12,16},{16,20},{20,24},{24,28},{28,0},{1,5},{5... | collective-permute-start | bytes 20 | tf_op jit(solution)/shard_map/ppermute | solution.py:461
  248.2 4.4 %collective-permute-start.34 = (f32[1]{0:T(128)}, f32[1]{0:T(128)}, u32[]{:S(2)}, u32[]{:S(2)}) collective-permute-start(f32[1]{0:T(128)} %add.35), channel_id=1, source_target_pairs={{0,8},{4,12},{8,16},{12,20},{16,24},{20,28},{24,0},{28,4},{1,9},{5... | collective-permute-start | bytes 20 | tf_op jit(solution)/shard_map/ppermute | solution.py:461
  252.6 4.2 %collective-permute-start.33 = (f32[1]{0:T(128)}, f32[1]{0:T(128)}, u32[]{:S(2)}, u32[]{:S(2)}) collective-permute-start(f32[1]{0:T(128)} %add.35), channel_id=1, source_target_pairs={{0,16},{4,20},{8,24},{12,28},{16,0},{20,4},{24,8},{28,12},{1,17},{... | collective-permute-start | bytes 20 | tf_op jit(solution)/shard_map/ppermute | solution.py:461
  258.9 6.1 %collective-permute-start.36 = (bf16[96,2560]{1,0:T(8,128)(2,1)S(1)}, bf16[96,2560]{1,0:T(8,128)(2,1)}, u32[]{:S(2)}, u32[]{:S(2)}) collective-permute-start(bf16[96,2560]{1,0:T(8,128)(2,1)S(1)} %get-tuple-element.362), channel_id=1, source_target_pairs={{2,3},{6,7},{10,11},{14,15},{18,19},{22,23},{26,27},{30,31}} | collective-permute-start | bytes 1474568 | tf_op jit(solution)/shard_map/ppermute | solution.py:44
  260.3 21.1 %collective-permute-start.37 = (bf16[96,2560]{1,0:T(8,128)(2,1)S(1)}, bf16[96,2560]{1,0:T(8,128)(2,1)}, u32[]{:S(2)}, u32[]{:S(2)}) collective-permute-start(bf16[96,2560]{1,0:T(8,128)(2,1)S(1)} %get-tuple-element.363), channel_id=1, source_target_pairs={{1,0},{5,4},{9,8},{13,12},{17,16},{21,20},{25,24},{29,28}} | collective-permute-start | bytes 1474568 | tf_op jit(solution)/shard_map/ppermute | solution.py:44
  261.6 19.8 %collective-permute-start.43 = (bf16[96,2560]{1,0:T(8,128)(2,1)}, bf16[96,2560]{1,0:T(8,128)(2,1)S(1)}, u32[]{:S(2)}, u32[]{:S(2)}) collective-permute-start(bf16[96,2560]{1,0:T(8,128)(2,1)} %collective-permute-done.42.refs_9_), channel_id=1, source_target_pairs={{2,3},{6,7},{10,11},{14,15},{18,19},{22,23},{26,27},{30,31}} | collective-permute-start | bytes 1474568 | tf_op jit(solution)/shard_map/ppermute | solution.py:44
  262.3 25.5 %collective-permute-start.45 = (bf16[96,2560]{1,0:T(8,128)(2,1)}, bf16[96,2560]{1,0:T(8,128)(2,1)S(1)}, u32[]{:S(2)}, u32[]{:S(2)}) collective-permute-start(bf16[96,2560]{1,0:T(8,128)(2,1)} %collective-permute-done.44.refs_12_), channel_id=1, source_target_pairs={{1,0},{5,4},{9,8},{13,12},{17,16},{21,20},{25,24},{29,28}} | collective-permute-start | bytes 1474568 | tf_op jit(solution)/shard_map/ppermute | solution.py:44
  303.3 70.1 %collective-permute-start.1 = (bf16[640,2560]{1,0:T(8,128)(2,1)}, bf16[640,2560]{1,0:T(8,128)(2,1)}, u32[]{:S(2)}, u32[]{:S(2)}) collective-permute-start(bf16[640,2560]{1,0:T(8,128)(2,1)} %get-tuple-element.218), channel_id=1, source_target_pairs={{0,8},{4,12},{8,16},{12,20},{16,24},{20,28},{24,0},{28,4},{1,9},{5... | collective-permute-start | bytes 9830408 | tf_op jit(solution)/shard_map/cond/branch_1_fun/ppermute | solution.py:434
  (31 other events, 299.3 us)

commit v6 on v5

--- a/solution.py
+++ b/solution.py
@@ -12,7 +12,7 @@
 TOKEN = jax.ShapeDtypeStruct((8, 128), jnp.float32)
 
 
-def call(body, name, grid, ins, outs, scalars=(), scratch=(), flops=0, moved=0, vmem=12):
+def call(body, name, grid, ins, outs, scalars=(), scratch=(), flops=0, moved=0, vmem=12, aliases=None):
     return pl.pallas_call(
         body,
         name=name,
@@ -24,6 +24,7 @@
             out_specs=[pl.BlockSpec(block, place) for _, _, block, place in outs],
             scratch_shapes=scratch,
         ),
+        input_output_aliases=aliases or {},
         compiler_params=pltpu.CompilerParams(vmem_limit_bytes=vmem * MIB),
         cost_estimate=pl.CostEstimate(flops=flops, bytes_accessed=moved, transcendentals=0),
     )(*scalars, *(array for array, _, _ in ins))
@@ -97,13 +98,14 @@
     )
 
 
-def partial_products(mine, weights, ends):
+def partial_products(mine, weights, ends, token=None):
     mine, index, size = mine
     members, _, rows = mine.shape
     width = weights.shape[1]
     tile = tile_of(width, 1280)
 
-    def body(mine_ref, weights_ref, out_ref, token_out, *end_refs):
+    def body(mine_ref, weights_ref, *refs):
+        out_ref, token_out, *end_refs = refs[0 if token is None else 1 :]
         product = jnp.dot(
             mine_ref[...].reshape(members * size, rows),
             weights_ref[...],
@@ -123,7 +125,8 @@
         [
             (mine, (members, size, rows), fixed(0, index, 0)),
             (weights, (rows, tile), lambda j: (0, j)),
-        ],
+        ]
+        + ([] if token is None else [token_in(token)]),
         [
             ((members, size, width), jnp.bfloat16, (members, size, tile), lambda j: (0, 0, j)),
             TOKEN_OUT,
@@ -135,7 +138,7 @@
     )
 
 
-def next_payload(right, left, parts, scalars, pick):
+def next_payload(right, left, parts, scalars, pick, token=None):
     members, size, width = parts.shape
     step = size // 2
 
@@ -147,7 +150,8 @@
             jnp.bfloat16
         )
 
-    def body(s, right_ref, left_ref, of_right, of_left, right_out, left_out, token_out):
+    def body(s, right_ref, left_ref, of_right, of_left, *refs):
+        right_out, left_out, token_out = refs[-3:]
         right_out[...] = joined(right_ref[...], of_right[0], s[1] > 0)
         left_out[...] = joined(left_ref[...], of_left[0], s[3] > 0)
         token_out[...] = jnp.zeros((8, 128), jnp.float32)
@@ -163,7 +167,8 @@
             (left,) + here,
             (parts, (1, step, width), lambda i, s: (s[0], i, 0)),
             (parts, (1, step, width), lambda i, s: (s[2], i, 0)),
-        ],
+        ]
+        + ([] if token is None else [token_in(token)]),
         [flat, flat, TOKEN_OUT],
         scalars=(scalars,),
         flops=2 * size * width,
@@ -226,17 +231,17 @@
     return jnp.concatenate(rows, axis=0)
 
 
-def unit_ins(units, tile):
+def unit_ins(units, tile, first=0):
     ins = []
     for chunk in units:
         block = (chunk[0].shape[0], tile)
         members = (len(chunk) + 1) // 2
-        ins.append((chunk[0], block, lambda j, s: (0, j)))
+        ins.append((chunk[0], block, lambda j, s: (0, j + first)))
         for k in range(members - 1):
-            place = lambda j, s, k=k: (0, jnp.where(s[0] > k, j, 0))
+            place = lambda j, s, k=k: (0, jnp.where(s[0] > k, j, 0) + first)
             ins.append((chunk[1 + k], block, place))
         for m in range(members - 1):
-            place = lambda j, s, k=members - 2 - m: (0, jnp.where(s[0] > k, 0, j))
+            place = lambda j, s, k=members - 2 - m: (0, jnp.where(s[0] > k, 0, j) + first)
             ins.append((chunk[members + m], block, place))
     return ins
 
@@ -254,17 +259,19 @@
     scratch[...] = stack.T
 
 
-def weight_step(units, mine, order, kept, numer, inbox):
+def weight_step(units, mine, order, base, first, last, inbox=None, kept=None, new=False, token=None):
     members, _, rows = mine[0][0].shape
-    width = numer.shape[1] if kept is None else kept.shape[1]
+    width = base.shape[1]
     tile = tile_of(width)
+    last = width // tile if last is None else last
     count = len(units) * len(units[0])
     chunks = len(units)
     total = sum(members * size for _, _, size in mine)
+    early = inbox is None
 
     def body(s, *refs):
         units_ref, mine_refs = refs[:count], refs[count : count + chunks]
-        rest = refs[count + chunks : -1]
+        base_ref = refs[count + chunks]
         turned = refs[-1]
 
         @pl.when(pl.program_id(0) == 0)
@@ -274,33 +281,38 @@
         weight = jnp.dot(
             turned[...], stack_of(units_ref, members, s[0]), preferred_element_type=jnp.float32
         )
-        if kept is None:
-            numer_ref, kept_out, token_out = rest
-            kept_out[...] = 0.5 * (numer_ref[...] - 0.004 * weight)
-            token_out[...] = jnp.zeros((8, 128), jnp.float32)
+        if early:
+            refs[-3][...] = 0.5 * (base_ref[...] - 0.004 * weight)
+            refs[-2][...] = jnp.zeros((8, 128), jnp.float32)
         else:
-            kept_ref, inbox_ref, new_out, kept_out = rest
-            now = kept_ref[...] - 0.5 * 0.004 * weight
-            new_out[...] = now + inbox_ref[...]
-            kept_out[...] = now.astype(jnp.bfloat16)
-
-    columns = (rows, tile), lambda j, s: (0, j)
-    whole = ((rows, width), jnp.float32) + columns
+            now = base_ref[...] - 0.5 * 0.004 * weight
+            if new:
+                refs[-2][...] = now + refs[count + chunks + 1][...]
+            else:
+                refs[-2][...] = now.astype(jnp.bfloat16)
+
+    columns = (rows, tile), lambda j, s: (0, j + first)
+    ins = unit_ins(units, tile, first) + mine_ins(mine) + [(base,) + columns]
+    if new:
+        ins.append((inbox,) + columns)
+    if kept is not None:
+        ins.append((kept, (8, 128), fixed(0, 0)))
+    if token is not None:
+        ins.append(token_in(token))
+    kind = jnp.float32 if early or new else jnp.bfloat16
+    outs = [((rows, width), kind) + columns]
     return call(
         body,
         "weight_step",
-        (width // tile,),
-        unit_ins(units, tile)
-        + mine_ins(mine)
-        + ([(numer,) + columns] if kept is None else [(kept,) + columns, (inbox,) + columns]),
-        [whole, TOKEN_OUT]
-        if kept is None
-        else [whole, ((rows, width), jnp.bfloat16) + columns],
+        (last - first,),
+        ins,
+        outs + [TOKEN_OUT] * early,
         scalars=(order,),
         scratch=[pltpu.VMEM((rows, total), jnp.bfloat16)],
-        flops=2 * total * rows * width,
-        moved=2 * count * units[0][0].shape[0] * width + 12 * rows * width,
+        flops=2 * total * rows * tile * (last - first),
+        moved=(2 * count * units[0][0].shape[0] + 12 * rows) * tile * (last - first),
         vmem=52,
+        aliases={} if kept is None else {1 + count + chunks + 1: 0},
     )
 
 
@@ -314,7 +326,8 @@
     total = members * sum(sizes)
 
     def body(s, *refs):
-        weights_ref, grad_ref, acc = refs[count:]
+        weights_ref, grad_ref, token_out, acc = refs[count:]
+        token_out[...] = jnp.zeros((8, 128), jnp.float32)
         j = pl.program_id(0)
         grad = lax.dot_general(
             stack_of(refs[:count], members, s[0]),
@@ -351,14 +364,15 @@
                 jnp.bfloat16,
                 (members, sum(sizes), rows),
                 fixed(0, 0, 0),
-            )
+            ),
+            TOKEN_OUT,
         ],
         scalars=(order,),
         scratch=[pltpu.VMEM((total, rows), jnp.float32)],
         flops=2 * total * rows * width,
         moved=2 * count * sizes[0] * width + 2 * rows * width,
         vmem=50,
-    )[0]
+    )
 
 
 def passed(right, left, token):
@@ -429,12 +443,15 @@
     return lax.all_to_all(blocks, "fsdp", 0, 0, tiled=False)
 
 
-def tail(kept, units, weights, order, bit_place):
+def tail(half, early, late, mine, kept, inbox, weights, order, bit_place):
     length = lax.axis_size("rep")
     sent = lax.ppermute(
-        kept, "rep", [(i, (i + (1 << bit_place)) % length) for i in range(length)]
-    )
-    return sent, joined_rows(swapped(grad_rows(units, weights, order)))
+        half, "rep", [(i, (i + (1 << bit_place)) % length) for i in range(length)]
+    )
+    grads, token = grad_rows(early + late, weights, order)
+    back = swapped(grads)
+    new = weight_step(late, mine, order, kept, 0, None, inbox, new=True, token=token)[0]
+    return sent, joined_rows(back), new
 
 
 def local(
@@ -508,9 +525,13 @@
     for q in range(count):
         fetch(0, [q], token if q else None)
     parts = [None] * count
+    token = None
     for q in range(count):
-        parts[q], _, last, first = partial_products(mine[0][q], weights, True)
+        parts[q], token, last, first = partial_products(mine[0][q], weights, True, token)
         hint[q] = (last, first)
+        if q == 0:
+            outbox_weight = sent_weight(token)
+            token = jnp.broadcast_to(outbox_weight[None], (8, 128))
     for e in range(rounds):
         moving = [None] * count
         for q in range(count):
@@ -523,7 +544,9 @@
                 units[e - 1][q][2].append(moving[q][1])
         for t in range(1, members - 1):
             for q in range(count):
-                right, left, token = next_payload(*moving[q], parts[q], scalars(t), False)
+                right, left, token = next_payload(
+                    *moving[q], parts[q], scalars(t), False, token if (e, t, q) == (0, 1, 0) else None
+                )
                 if t == 1 and e + 1 < rounds:
                     fetch(e + 1, [q], token)
                 if e == 0:
@@ -557,21 +580,25 @@
         for q in range(count):
             if (s, q) == (1, count - 1):
                 early = [[u] + r + l for of_round in units[:-1] for u, r, l in of_round]
-                kept, done = weight_step(
-                    early, [m for of_round in mine[:-1] for m in of_round], order, None, numer, None
-                )
+                early_mine = [m for of_round in mine[:-1] for m in of_round]
+                kept, done = weight_step(early, early_mine, order, numer, 0, 3)
                 before[q] = passed(*before[q], done)
-                outbox_weight = sent_weight(done)
             if (s, q) == (2, 0):
-                before[q] = passed(*before[q], jnp.broadcast_to(outbox_weight[None], (8, 128)))
+                kept, done = weight_step(early, early_mine, order, numer, 3, None, kept=kept)
+                before[q] = passed(*before[q], done)
             before[q] = hops(*before[q], range(s, members - 1), range(1, members - s))
             units[-1][q][1].append(before[q][0])
             units[-1][q][2].append(before[q][1])
     flat = [[u] + r + l for u, r, l in units[-1]]
-    new_params, half = weight_step(flat, mine[-1], order, kept, None, inbox_params[0])
+    half = weight_step(flat, mine[-1], order, kept, 0, None, inbox_params[0])[0]
     new_weight = 0.5 * push_weight + inbox_weight
-    branches = [partial(tail, half, early + flat, weights, order, place) for place in range(levels)]
-    sent, grad_heads = lax.switch(level_index, branches)
+    branches = [
+        partial(
+            tail, half, early, flat, mine[-1], kept, inbox_params[0], weights, order, place
+        )
+        for place in range(levels)
+    ]
+    sent, grad_heads, new_params = lax.switch(level_index, branches)
     return (new_params[None], new_weight, widened(sent)[None], outbox_weight, grad_heads[None])
 
 

time: 381 us -> 364 us (0.955)
  blocking collectives: 45.1 us -> 0 us
  starting transfers between devices: 126 us -> 140 us
  Pallas kernels: 94.9 us -> 102 us
    all_to_all x1 -> x0, blocking collectives: 45.1 us -> none  [swapped(): return lax.all_to_all(blocks, 'fsdp', 0, 0, tiled=False)]
    all_to_all x4 -> x5, waiting for transfers between devices: 5.96 us -> 32.3 us  [swapped(): return lax.all_to_all(blocks, 'fsdp', 0, 0, tiled=False)]
    ppermute x40, waiting for transfers between devices: 77.6 us -> 64.3 us  [hop(): return lax.ppermute(value, 'fsdp', [(i, i + step) for i in pairs])]
    ppermute x40, starting transfers between devices: 100 us -> 108 us  [hop(): return lax.ppermute(value, 'fsdp', [(i, i + step) for i in pairs])]
    pallas_call x30 -> x32, Pallas kernels: 94.9 us -> 102 us  [call(): pl.pallas_call(body, name=name, out_shape=[jax.ShapeDtypeStruct(shape, ki...]
    ppermute x1, waiting for transfers between devices: 9.71 us -> 4.19 us  [tail(): lax.ppermute(half, 'rep', [(i, (i + (1 << bit_place)) % length) for i in...]
    ppermute x3, waiting for transfers between devices: 5.47 us -> 0.01 us  [sent_weight(): lax.ppermute(half, 'rep', [(i, (i + (1 << b)) % replicas) for i in range(...]
    all_to_all x4 -> x5, starting transfers between devices: 20.3 us -> 23.7 us  [swapped(): return lax.all_to_all(blocks, 'fsdp', 0, 0, tiled=False)]
  transfers between devices with their start and end apart: 48 -> 49, of which waited for: 22 -> 23; matrix products, arithmetic and copies ran while one was open for 0% -> 0% of each run, Pallas kernels for 20% -> 23%
where the time goes in v6:
time: 364 us; the launch traced here: 362 us
  starting transfers between devices  140 us (38%)
  Pallas kernels  102 us (28%)
  waiting for transfers between devices  101 us (28%)
  between operations  9.59 us (3%)
  local copies, waits for them, and re-layouts  8.03 us (2%)
    ppermute x40, starting transfers between devices, hop(): return lax.ppermute(value, 'fsdp', [(i, i + step) for i in pairs])  108 us
    pallas_call x32, Pallas kernels, call(): pl.pallas_call(body, name=name, out_shape=[jax.ShapeDtypeStruct(shape, ki...  102 us
    ppermute x40, waiting for transfers between devices, hop(): return lax.ppermute(value, 'fsdp', [(i, i + step) for i in pairs])  64.3 us
    all_to_all x5, waiting for transfers between devices, swapped(): return lax.all_to_all(blocks, 'fsdp', 0, 0, tiled=False)  32.3 us
    all_to_all x5, starting transfers between devices, swapped(): return lax.all_to_all(blocks, 'fsdp', 0, 0, tiled=False)  23.7 us
  transfers between devices with their start and end apart: 49, of which 23 were waited for; matrix products, arithmetic and copies ran while one was open for 0% of the time, Pallas kernels for 23%

profile of v6, /device:TPU:0, one launch (start us, length us, event | category | flops | bytes accessed | tf_op | source)
XLA Modules:
  0.0 362.1 jit_solution(3592754115832148727)
XLA Ops:
  0.6 1.8 cut_heads.4
  2.4 6.3 %all-to-all-start.3 = ((bf16[4,96,640]{2,1,0:T(8,128)(2,1)}), bf16[4,96,640]{2,1,0:T(8,128)(2,1)S(1)}, u32[]{:S(2)}, u32[]{:S(2)}) async-start(bf16[4,96,640]{2,1,0:T(8,128)(2,1)} %cut_heads.4), calls=%async_computation.3 | async-start | bytes 983040 | tf_op jit(solution)/shard_map/all_to_all | solution.py:443
  9.4 5.7 %scaled_weights.1 = (bf16[640,2560]{1,0:T(8,128)(2,1)}, f32[8,128]{1,0:T(8,128)}) custom-call(f32[640,2560]{1,0:T(8,128)} %bitcast.48, f32[1,1]{1,0:T(1,128)} %bitcast.32.one_ref), custom_call_target="tpu_custom_call" | custom-call | flops 3276800 | bytes 9830400 | tf_op jit(solution)/shard_map/scaled_weights/pallas_call | solution.py:16
  16.5 6.0 %all-to-all-done.3.mine_ref.refs_14_ = bf16[4,96,640]{2,1,0:T(8,128)(2,1)S(1)} async-done(((bf16[4,96,640]{2,1,0:T(8,128)(2,1)}), bf16[4,96,640]{2,1,0:T(8,128)(2,1)S(1)}, u32[]{:S(2)}, u32[]{:S(2)}) %all-to-all-start.3) | async-done | bytes 491552 | tf_op jit(solution)/shard_map/all_to_all | solution.py:443
  22.5 3.5 all-to-all-start.4
  26.0 4.3 %partial_products.4 = (bf16[4,96,2560]{2,1,0:T(8,128)(2,1)S(1)}, f32[8,128]{1,0:T(8,128)S(1)}, bf16[96,2560]{1,0:T(8,128)(2,1)}, bf16[96,2560]{1,0:T(8,128)(2,1)}) custom-call(bf16[4,96,640]{2,1,0:T(8,128)(2,1)S(1)} %all-to-all-done.3.mine_ref.refs_14_, bf16[640,2560]{1,0:T(8,128)(2,1)} %get-tuple-element.375.weights_ref), custom_call_target="tpu_custom_call" | custom-call | flops 1258291200 | bytes 5734400 | tf_op jit(solution)/shard_map/partial_products/pallas_call | solution.py:16
  30.3 3.9 %collective-permute-start.3 = (bf16[96,2560]{1,0:T(8,128)(2,1)}, bf16[96,2560]{1,0:T(8,128)(2,1)S(1)}, u32[]{:S(2)}, u32[]{:S(2)}) collective-permute-start(bf16[96,2560]{1,0:T(8,128)(2,1)} %get-tuple-element.376), channel_id=1, source_target_pairs={{0,1},{4,5},{8,9},{12,13},{16,17},{20,21},{24,25},{28,29}} | collective-permute-start | bytes 1474568 | tf_op jit(solution)/shard_map/ppermute | solution.py:45
  39.9 2.8 collective-permute-start.6
  42.7 2.8 collective-permute-start.5
  47.5 3.5 partial_products.5
  51.1 2.9 next_payload.10
  56.4 4.1 %all-to-all-start.5 = ((bf16[4,96,640]{2,1,0:T(8,128)(2,1)}), bf16[4,96,640]{2,1,0:T(8,128)(2,1)}, u32[]{:S(2)}, u32[]{:S(2)}) async-start(bf16[4,96,640]{2,1,0:T(8,128)(2,1)} %cut_heads.6), calls=%async_computation.5 | async-start | bytes 983040 | tf_op jit(solution)/shard_map/all_to_all | solution.py:443
  60.5 3.9 %collective-permute-start.24 = (bf16[96,2560]{1,0:T(8,128)(2,1)}, bf16[96,2560]{1,0:T(8,128)(2,1)S(1)}, u32[]{:S(2)}, u32[]{:S(2)}) collective-permute-start(bf16[96,2560]{1,0:T(8,128)(2,1)} %copy-done.24), channel_id=1, source_target_pairs={{0,1},{4,5},{8,9},{12,13},{16,17},{20,21},{24,25},{28,29}} | collective-permute-start | bytes 1474568 | tf_op jit(solution)/shard_map/ppermute | solution.py:45
  67.9 12.5 %collective-permute-done.24.right_ref = bf16[96,2560]{1,0:T(8,128)(2,1)S(1)} collective-permute-done((bf16[96,2560]{1,0:T(8,128)(2,1)}, bf16[96,2560]{1,0:T(8,128)(2,1)S(1)}, u32[]{:S(2)}, u32[]{:S(2)}) %collective-permute-start.24) | collective-permute-done | bytes 491552 | tf_op jit(solution)/shard_map/ppermute | solution.py:45
  82.0 1.6 next_payload.15
  83.6 5.1 %collective-permute-start.26 = (bf16[96,2560]{1,0:T(8,128)(2,1)}, bf16[96,2560]{1,0:T(8,128)(2,1)}, u32[]{:S(2)}, u32[]{:S(2)}) collective-permute-start(bf16[96,2560]{1,0:T(8,128)(2,1)} %get-tuple-element.398), channel_id=1, source_target_pairs={{0,1},{1,2},{4,5},{5,6},{8,9},{9,10},{12,13},{13,14},{16,17},{17,1... | collective-permute-start | bytes 1474568 | tf_op jit(solution)/shard_map/ppermute | solution.py:45
  90.9 5.4 %all-to-all-start.6 = ((bf16[4,96,640]{2,1,0:T(8,128)(2,1)}), bf16[4,96,640]{2,1,0:T(8,128)(2,1)}, u32[]{:S(2)}, u32[]{:S(2)}) async-start(bf16[4,96,640]{2,1,0:T(8,128)(2,1)} %cut_heads.7), calls=%async_computation.6 | async-start | bytes 983040 | tf_op jit(solution)/shard_map/all_to_all | solution.py:443
  96.4 2.3 next_payload.11
  98.7 3.9 %collective-permute-start.10 = (bf16[96,2560]{1,0:T(8,128)(2,1)S(1)}, bf16[96,2560]{1,0:T(8,128)(2,1)S(1)}, u32[]{:S(2)}, u32[]{:S(2)}) collective-permute-start(bf16[96,2560]{1,0:T(8,128)(2,1)S(1)} %get-tuple-element.384), channel_id=1, source_target_pairs={{0,1},{1,2},{2,3},{4,5},{5,6},{6,7},{8,9},{9,10},{10,11},{12,13},{... | collective-permute-start | bytes 1474568 | tf_op jit(solution)/shard_map/ppermute | solution.py:45
  102.7 1.6 collective-permute-start.11
  104.3 2.8 next_payload.16
  107.1 7.2 %collective-permute-start.28 = (bf16[96,2560]{1,0:T(8,128)(2,1)}, bf16[96,2560]{1,0:T(8,128)(2,1)S(1)}, u32[]{:S(2)}, u32[]{:S(2)}) collective-permute-start(bf16[96,2560]{1,0:T(8,128)(2,1)} %get-tuple-element.400), channel_id=1, source_target_pairs={{0,1},{1,2},{2,3},{4,5},{5,6},{6,7},{8,9},{9,10},{10,11},{12,13},{... | collective-permute-start | bytes 1474568 | tf_op jit(solution)/shard_map/ppermute | solution.py:45
  115.7 3.3 partial_products.6
  123.0 10.1 %collective-permute-start.12 = (bf16[96,2560]{1,0:T(8,128)(2,1)}, bf16[96,2560]{1,0:T(8,128)(2,1)}, u32[]{:S(2)}, u32[]{:S(2)}) collective-permute-start(bf16[96,2560]{1,0:T(8,128)(2,1)} %unit_gradient.4.refs_0_), channel_id=1, source_target_pairs={{0,1},{1,2},{2,3},{4,5},{5,6},{6,7},{8,9},{9,10},{10,11},{12,13},{... | collective-permute-start | bytes 1474568 | tf_op jit(solution)/shard_map/ppermute | solution.py:45
  133.1 3.7 %partial_products.7 = (bf16[4,96,2560]{2,1,0:T(8,128)(2,1)S(1)}, f32[8,128]{1,0:T(8,128)S(1)}) custom-call(bf16[4,96,640]{2,1,0:T(8,128)(2,1)} %all-to-all-done.6.mine_ref.refs_15_, bf16[640,2560]{1,0:T(8,128)(2,1)} %get-tuple-element.375.weights_ref), custom_call_target="tpu_custom_call" | custom-call | flops 1258291200 | bytes 5734400 | tf_op jit(solution)/shard_map/partial_products/pallas_call | solution.py:16
  136.8 2.2 copy-done.15
  139.0 2.3 unit_gradient.6.refs_7_
  142.6 5.3 %collective-permute-start.30 = (bf16[96,2560]{1,0:T(8,128)(2,1)}, bf16[96,2560]{1,0:T(8,128)(2,1)}, u32[]{:S(2)}, u32[]{:S(2)}) collective-permute-start(bf16[96,2560]{1,0:T(8,128)(2,1)} %unit_gradient.6.refs_7_), channel_id=1, source_target_pairs={{0,1},{1,2},{2,3},{4,5},{5,6},{6,7},{8,9},{9,10},{10,11},{12,13},{... | collective-permute-start | bytes 1474568 | tf_op jit(solution)/shard_map/ppermute | solution.py:45
  148.0 2.5 next_payload.12
  150.5 2.4 collective-permute-start.14
  154.2 2.3 collective-permute-done.30.right_ref.refs_8_
  156.6 2.5 next_payload.17
  159.0 5.7 %collective-permute-start.32 = (bf16[96,2560]{1,0:T(8,128)(2,1)S(1)}, bf16[96,2560]{1,0:T(8,128)(2,1)S(1)}, u32[]{:S(2)}, u32[]{:S(2)}) collective-permute-start(bf16[96,2560]{1,0:T(8,128)(2,1)S(1)} %get-tuple-element.405), channel_id=1, source_target_pairs={{0,1},{1,2},{2,3},{4,5},{5,6},{6,7},{8,9},{9,10},{10,11},{12,13},{... | collective-permute-start | bytes 1474568 | tf_op jit(solution)/shard_map/ppermute | solution.py:45
  168.9 5.1 %collective-permute-start.16 = (bf16[96,2560]{1,0:T(8,128)(2,1)S(1)}, bf16[96,2560]{1,0:T(8,128)(2,1)S(1)}, u32[]{:S(2)}, u32[]{:S(2)}) collective-permute-start(bf16[96,2560]{1,0:T(8,128)(2,1)S(1)} %get-tuple-element.391), channel_id=1, source_target_pairs={{0,1},{1,2},{2,3},{4,5},{5,6},{6,7},{8,9},{9,10},{10,11},{12,13},{... | collective-permute-start | bytes 1474568 | tf_op jit(solution)/shard_map/ppermute | solution.py:45
  175.4 2.2 collective-permute-done.32.right_ref.refs_9_
  177.5 3.1 collective-permute-done.33.left_ref.refs_12_
  182.0 4.6 %collective-permute-start.34 = (bf16[96,2560]{1,0:T(8,128)(2,1)S(1)}, bf16[96,2560]{1,0:T(8,128)(2,1)S(1)}, u32[]{:S(2)}, u32[]{:S(2)}) collective-permute-start(bf16[96,2560]{1,0:T(8,128)(2,1)S(1)} %get-tuple-element.407), channel_id=1, source_target_pairs={{0,1},{1,2},{2,3},{4,5},{5,6},{6,7},{8,9},{9,10},{10,11},{12,13},{... | collective-permute-start | bytes 1474568 | tf_op jit(solution)/shard_map/ppermute | solution.py:45
  188.1 3.1 collective-permute-done.17.left_ref.refs_6_
  192.5 4.6 %collective-permute-start.18 = (bf16[96,2560]{1,0:T(8,128)(2,1)S(1)}, bf16[96,2560]{1,0:T(8,128)(2,1)S(1)}, u32[]{:S(2)}, u32[]{:S(2)}) collective-permute-start(bf16[96,2560]{1,0:T(8,128)(2,1)S(1)} %get-tuple-element.393), channel_id=1, source_target_pairs={{0,1},{1,2},{2,3},{4,5},{5,6},{6,7},{8,9},{9,10},{10,11},{12,13},{... | collective-permute-start | bytes 1474568 | tf_op jit(solution)/shard_map/ppermute | solution.py:45
  197.1 1.6 collective-permute-start.19
  198.7 3.9 %collective-permute-done.35.refs_13_.left_ref = bf16[96,2560]{1,0:T(8,128)(2,1)S(1)} collective-permute-done((bf16[96,2560]{1,0:T(8,128)(2,1)S(1)}, bf16[96,2560]{1,0:T(8,128)(2,1)S(1)}, u32[]{:S(2)}, u32[]{:S(2)}) %collective-permute-start.35) | collective-permute-done | bytes 491552 | tf_op jit(solution)/shard_map/ppermute | solution.py:45
  203.9 3.7 %collective-permute-start.38 = (bf16[96,2560]{1,0:T(8,128)(2,1)S(1)}, bf16[96,2560]{1,0:T(8,128)(2,1)S(1)}, u32[]{:S(2)}, u32[]{:S(2)}) collective-permute-start(bf16[96,2560]{1,0:T(8,128)(2,1)S(1)} %get-tuple-element.413), channel_id=1, source_target_pairs={{0,1},{1,2},{2,3},{4,5},{5,6},{6,7},{8,9},{9,10},{10,11},{12,13},{... | collective-permute-start | bytes 1474568 | tf_op jit(solution)/shard_map/ppermute | solution.py:45
  209.1 4.3 %collective-permute-done.19.left_ref = bf16[96,2560]{1,0:T(8,128)(2,1)S(1)} collective-permute-done((bf16[96,2560]{1,0:T(8,128)(2,1)S(1)}, bf16[96,2560]{1,0:T(8,128)(2,1)S(1)}, u32[]{:S(2)}, u32[]{:S(2)}) %collective-permute-start.19) | collective-permute-done | bytes 491552 | tf_op jit(solution)/shard_map/ppermute | solution.py:45
  215.3 5.4 %collective-permute-start.20 = (bf16[96,2560]{1,0:T(8,128)(2,1)S(1)}, bf16[96,2560]{1,0:T(8,128)(2,1)}, u32[]{:S(2)}, u32[]{:S(2)}) collective-permute-start(bf16[96,2560]{1,0:T(8,128)(2,1)S(1)} %unit_gradient.5.refs_0_), channel_id=1, source_target_pairs={{0,1},{1,2},{2,3},{4,5},{5,6},{6,7},{8,9},{9,10},{10,11},{12,13},{... | collective-permute-start | bytes 1474568 | tf_op jit(solution)/shard_map/ppermute | solution.py:45
  220.7 3.2 collective-permute-done.39.left_ref
  225.9 4.6 %collective-permute-start.40 = (bf16[96,2560]{1,0:T(8,128)(2,1)S(1)}, bf16[96,2560]{1,0:T(8,128)(2,1)S(1)}, u32[]{:S(2)}, u32[]{:S(2)}) collective-permute-start(bf16[96,2560]{1,0:T(8,128)(2,1)S(1)} %unit_gradient.7.refs_7_), channel_id=1, source_target_pairs={{0,1},{1,2},{2,3},{4,5},{5,6},{6,7},{8,9},{9,10},{10,11},{12,13},{... | collective-permute-start | bytes 1474568 | tf_op jit(solution)/shard_map/ppermute | solution.py:45
  230.5 4.0 %collective-permute-done.22.refs_4_ = bf16[96,2560]{1,0:T(8,128)(2,1)S(1)} collective-permute-done((bf16[96,2560]{1,0:T(8,128)(2,1)S(1)}, bf16[96,2560]{1,0:T(8,128)(2,1)S(1)}, u32[]{:S(2)}, u32[]{:S(2)}) %collective-permute-start.22) | collective-permute-done | bytes 491552 | tf_op jit(solution)/shard_map/ppermute | solution.py:45
  236.7 6.2 %weight_step.9 = (f32[640,2560]{1,0:T(8,128)S(1)}, f32[8,128]{1,0:T(8,128)S(1)}) custom-call(s32[4]{0:T(128)S(1)} %and_select_fusion.s, bf16[96,2560]{1,0:T(8,128)(2,1)} %unit_gradient.4.refs_0_, bf16[96,2560]{1,0:T(8,128)(2,1)} %collective-permute-done.12.right_ref.refs_1_, bf16[96,2560]{1,0:T(8,128)(2,1)S(1)} %collective-permute-done.14.right_ref.refs_2_, ...), custom_call_target="tpu_custom_call" | custom-call | flops 1509949440 | bytes 15925248 | tf_op jit(solution)/shard_map/weight_step/pallas_call | solution.py:16
  242.9 2.1 collective-permute-done.41.left_ref.refs_11_
  247.9 4.7 %weight_step.10 = (f32[640,2560]{1,0:T(8,128)S(1)}, f32[8,128]{1,0:T(8,128)S(1)}) custom-call(s32[4]{0:T(128)S(1)} %and_select_fusion.s, bf16[96,2560]{1,0:T(8,128)(2,1)} %unit_gradient.4.refs_0_, bf16[96,2560]{1,0:T(8,128)(2,1)} %collective-permute-done.12.right_ref.refs_1_, bf16[96,2560]{1,0:T(8,128)(2,1)} %copy-done.51, ...), custom_call_target="tpu_custom_call", output_to_operand_aliasing={{0}: (18, {})} | custom-call | flops 1006632960 | bytes 10616832 | tf_op jit(solution)/shard_map/weight_step/pallas_call | solution.py:16
  252.6 2.9 collective-permute-done.23.left_ref.refs_5_
  259.8 6.3 %collective-permute-done.44.refs_12_ = bf16[96,2560]{1,0:T(8,128)(2,1)} collective-permute-done((bf16[96,2560]{1,0:T(8,128)(2,1)S(1)}, bf16[96,2560]{1,0:T(8,128)(2,1)}, u32[]{:S(2)}, u32[]{:S(2)}) %collective-permute-start.44) | collective-permute-done | bytes 491552 | tf_op jit(solution)/shard_map/ppermute | solution.py:45
  268.8 5.6 %collective-permute-done.37.refs_6_ = bf16[96,2560]{1,0:T(8,128)(2,1)} collective-permute-done((bf16[96,2560]{1,0:T(8,128)(2,1)S(1)}, bf16[96,2560]{1,0:T(8,128)(2,1)}, u32[]{:S(2)}, u32[]{:S(2)}) %collective-permute-start.37) | collective-permute-done | bytes 491552 | tf_op jit(solution)/shard_map/ppermute | solution.py:45
  274.3 5.3 %collective-permute-done.45.refs_13_ = bf16[96,2560]{1,0:T(8,128)(2,1)} collective-permute-done((bf16[96,2560]{1,0:T(8,128)(2,1)}, bf16[96,2560]{1,0:T(8,128)(2,1)}, u32[]{:S(2)}, u32[]{:S(2)}) %collective-permute-start.45) | collective-permute-done | bytes 491552 | tf_op jit(solution)/shard_map/ppermute | solution.py:45
  279.7 9.7 %weight_step.11 = bf16[640,2560]{1,0:T(8,128)(2,1)} custom-call(s32[4]{0:T(128)S(1)} %and_select_fusion.s, bf16[96,2560]{1,0:T(8,128)(2,1)S(1)} %unit_gradient.5.refs_0_, bf16[96,2560]{1,0:T(8,128)(2,1)} %collective-permute-done.20.refs_1_, bf16[96,2560]{1,0:T(8,128)(2,1)} %copy-done.41, bf16[96,2560]{1,0:T(8,128)(2,1)} %collective-permute-done.36.refs_3_, ...), custom_call_target="tpu_custom_call" | custom-call | flops 2516582400 | bytes 26542080 | tf_op jit(solution)/shard_map/weight_step/pallas_call | solution.py:16
  289.5 65.9 %conditional.1 = (bf16[640,2560]{1,0:T(8,128)(2,1)}, bf16[1,384,2560]{2,1,0:T(8,128)(2,1)}, f32[1,640,2560]{2,1,0:T(8,128)}) conditional(s32[]{:T(128)} %clamp.3, (bf16[640,2560]{1,0:T(8,128)(2,1)}, s32[4]{0:T(128)S(1)}, bf16[96,2560]{1,0:T(8,128)(2,1)}, bf16[96,2560]{1,0:T(8,128)(2,1)}, bf16[96,2560]{1,0:T(8,128)(2,1)S(1)}, ...), branch_computations={%region_1.2_spmd, %region_2.3_spmd, %region_3.4_spmd} | conditional | flops 7549747200 | bytes 88146240 | solution.py:601
  289.6 2.0 collective-permute-start.2
  291.6 13.2 %grad_rows.5 = (bf16[4,384,640]{2,1,0:T(8,128)(2,1)S(1)}, f32[8,128]{1,0:T(8,128)S(1)}) custom-call(s32[4]{0:T(128)S(1)} %get-tuple-element.287.s, bf16[96,2560]{1,0:T(8,128)(2,1)} %get-tuple-element.288.refs_0_, bf16[96,2560]{1,0:T(8,128)(2,1)} %get-tuple-element.289.refs_1_, bf16[96,2560]{1,0:T(8,128)(2,1)S(1)} %get-tuple-element.290.refs_2_, ...), custom_call_target="tpu_custom_call" | custom-call | flops 5033164800 | bytes 17039360 | tf_op jit(solution)/shard_map/cond/branch_2_fun/grad_rows/pallas_call | solution.py:16
  306.1 4.4 %all-to-all-start.2 = ((bf16[4,384,640]{2,1,0:T(8,128)(2,1)}), bf16[4,384,640]{2,1,0:T(8,128)(2,1)S(1)}, u32[]{:S(2)}, u32[]{:S(2)}) async-start(bf16[4,384,640]{2,1,0:T(8,128)(2,1)} %copy-done.19), calls=%async_computation.2 | async-start | bytes 3932160 | tf_op jit(solution)/shard_map/cond/branch_2_fun/all_to_all | solution.py:443
  310.6 12.4 %weight_step.8 = f32[640,2560]{1,0:T(8,128)} custom-call(s32[4]{0:T(128)S(1)} %get-tuple-element.287.s, bf16[96,2560]{1,0:T(8,128)(2,1)S(1)} %get-tuple-element.302.refs_14_.refs_0_, bf16[96,2560]{1,0:T(8,128)(2,1)} %get-tuple-element.303.refs_15_.refs_1_, bf16[96,2560]{1,0:T(8,128)(2,1)} %copy-done.45, ...), custom_call_target="tpu_custom_call" | custom-call | flops 2516582400 | bytes 26542080 | tf_op jit(solution)/shard_map/cond/branch_2_fun/weight_step/pallas_call | solution.py:16
  323.0 26.3 %all-to-all-done.2.blocks_ref = bf16[4,384,640]{2,1,0:T(8,128)(2,1)S(1)} async-done(((bf16[4,384,640]{2,1,0:T(8,128)(2,1)}), bf16[4,384,640]{2,1,0:T(8,128)(2,1)S(1)}, u32[]{:S(2)}, u32[]{:S(2)}) %all-to-all-start.2) | async-done | bytes 1966112 | tf_op jit(solution)/shard_map/cond/branch_2_fun/all_to_all | solution.py:443
  349.3 1.9 joined_rows.5
  351.2 4.2 %collective-permute-done.2 = bf16[640,2560]{1,0:T(8,128)(2,1)} collective-permute-done((bf16[640,2560]{1,0:T(8,128)(2,1)}, bf16[640,2560]{1,0:T(8,128)(2,1)}, u32[]{:S(2)}, u32[]{:S(2)}) %collective-permute-start.2) | collective-permute-done | bytes 3276832 | tf_op jit(solution)/shard_map/cond/branch_2_fun/ppermute | solution.py:448
  355.4 4.4 %widened.1 = f32[640,2560]{1,0:T(8,128)} custom-call(bf16[640,2560]{1,0:T(8,128)(2,1)} %get-tuple-element.420.value_ref), custom_call_target="tpu_custom_call" | custom-call | bytes 9830400 | tf_op jit(solution)/shard_map/widened/pallas_call | solution.py:16
  (185 shorter events, 51.3 us)
Async XLA Ops:
  2.4 20.1 %all-to-all-start.3 = ((bf16[4,96,640]{2,1,0:T(8,128)(2,1)}), bf16[4,96,640]{2,1,0:T(8,128)(2,1)S(1)}, u32[]{:S(2)}, u32[]{:S(2)}) async-start(bf16[4,96,640]{2,1,0:T(8,128)(2,1)} %cut_heads.4), calls=%async_computation.3 | async-start | bytes 983040 | tf_op jit(solution)/shard_map/all_to_all | solution.py:443
  22.5 24.9 %all-to-all-start.4 = ((bf16[4,96,640]{2,1,0:T(8,128)(2,1)}), bf16[4,96,640]{2,1,0:T(8,128)(2,1)S(1)}, u32[]{:S(2)}, u32[]{:S(2)}) async-start(bf16[4,96,640]{2,1,0:T(8,128)(2,1)} %cut_heads.5), calls=%async_computation.4 | async-start | bytes 983040 | tf_op jit(solution)/shard_map/all_to_all | solution.py:443
  30.3 66.0 %copy-start.2 = (bf16[4,96,2560]{2,1,0:T(8,128)(2,1)}, bf16[4,96,2560]{2,1,0:T(8,128)(2,1)S(1)}, u32[]{:S(2)}) copy-start(bf16[4,96,2560]{2,1,0:T(8,128)(2,1)S(1)} %get-tuple-element.378.of_right.of_left.own_ref) | copy-start | bytes 5898244
  30.3 20.7 %collective-permute-start.3 = (bf16[96,2560]{1,0:T(8,128)(2,1)}, bf16[96,2560]{1,0:T(8,128)(2,1)S(1)}, u32[]{:S(2)}, u32[]{:S(2)}) collective-permute-start(bf16[96,2560]{1,0:T(8,128)(2,1)} %get-tuple-element.376), channel_id=1, source_target_pairs={{0,1},{4,5},{8,9},{12,13},{16,17},{20,21},{24,25},{28,29}} | collective-permute-start | bytes 1474568 | tf_op jit(solution)/shard_map/ppermute | solution.py:45
  34.2 16.8 %collective-permute-start.4 = (bf16[96,2560]{1,0:T(8,128)(2,1)}, bf16[96,2560]{1,0:T(8,128)(2,1)}, u32[]{:S(2)}, u32[]{:S(2)}) collective-permute-start(bf16[96,2560]{1,0:T(8,128)(2,1)} %get-tuple-element.377), channel_id=1, source_target_pairs={{3,2},{7,6},{11,10},{15,14},{19,18},{23,22},{27,26},{31,30}} | collective-permute-start | bytes 1474568 | tf_op jit(solution)/shard_map/ppermute | solution.py:45
  38.9 6.6 %collective-permute-start.7 = (f32[1]{0:T(128)}, f32[1]{0:T(128)}, u32[]{:S(2)}, u32[]{:S(2)}) collective-permute-start(f32[1]{0:T(128)} %add.35), channel_id=1, source_target_pairs={{0,4},{4,8},{8,12},{12,16},{16,20},{20,24},{24,28},{28,0},{1,5},{5... | collective-permute-start | bytes 20 | tf_op jit(solution)/shard_map/ppermute | solution.py:478
  39.9 5.6 %collective-permute-start.6 = (f32[1]{0:T(128)}, f32[1]{0:T(128)}, u32[]{:S(2)}, u32[]{:S(2)}) collective-permute-start(f32[1]{0:T(128)} %add.35), channel_id=1, source_target_pairs={{0,8},{4,12},{8,16},{12,20},{16,24},{20,28},{24,0},{28,4},{1,9},{5... | collective-permute-start | bytes 20 | tf_op jit(solution)/shard_map/ppermute | solution.py:478
  42.7 4.1 %collective-permute-start.5 = (f32[1]{0:T(128)}, f32[1]{0:T(128)}, u32[]{:S(2)}, u32[]{:S(2)}) collective-permute-start(f32[1]{0:T(128)} %add.35), channel_id=1, source_target_pairs={{0,16},{4,20},{8,24},{12,28},{16,0},{20,4},{24,8},{28,12},{1,17},{... | collective-permute-start | bytes 20 | tf_op jit(solution)/shard_map/ppermute | solution.py:478
  56.4 34.5 %all-to-all-start.5 = ((bf16[4,96,640]{2,1,0:T(8,128)(2,1)}), bf16[4,96,640]{2,1,0:T(8,128)(2,1)}, u32[]{:S(2)}, u32[]{:S(2)}) async-start(bf16[4,96,640]{2,1,0:T(8,128)(2,1)} %cut_heads.6), calls=%async_computation.5 | async-start | bytes 983040 | tf_op jit(solution)/shard_map/all_to_all | solution.py:443
  60.5 19.9 %collective-permute-start.24 = (bf16[96,2560]{1,0:T(8,128)(2,1)}, bf16[96,2560]{1,0:T(8,128)(2,1)S(1)}, u32[]{:S(2)}, u32[]{:S(2)}) collective-permute-start(bf16[96,2560]{1,0:T(8,128)(2,1)} %copy-done.24), channel_id=1, source_target_pairs={{0,1},{4,5},{8,9},{12,13},{16,17},{20,21},{24,25},{28,29}} | collective-permute-start | bytes 1474568 | tf_op jit(solution)/shard_map/ppermute | solution.py:45
  64.4 16.0 %collective-permute-start.25 = (bf16[96,2560]{1,0:T(8,128)(2,1)}, bf16[96,2560]{1,0:T(8,128)(2,1)S(1)}, u32[]{:S(2)}, u32[]{:S(2)}) collective-permute-start(bf16[96,2560]{1,0:T(8,128)(2,1)} %copy-done.23), channel_id=1, source_target_pairs={{3,2},{7,6},{11,10},{15,14},{19,18},{23,22},{27,26},{31,30}} | collective-permute-start | bytes 1474568 | tf_op jit(solution)/shard_map/ppermute | solution.py:45
  65.1 31.2 %collective-permute-start.8 = (bf16[96,2560]{1,0:T(8,128)(2,1)}, bf16[96,2560]{1,0:T(8,128)(2,1)S(1)}, u32[]{:S(2)}, u32[]{:S(2)}) collective-permute-start(bf16[96,2560]{1,0:T(8,128)(2,1)} %copy-done.22), channel_id=1, source_target_pairs={{0,1},{1,2},{4,5},{5,6},{8,9},{9,10},{12,13},{13,14},{16,17},{17,1... | collective-permute-start | bytes 1474568 | tf_op jit(solution)/shard_map/ppermute | solution.py:45
  66.5 29.9 %collective-permute-start.9 = (bf16[96,2560]{1,0:T(8,128)(2,1)}, bf16[96,2560]{1,0:T(8,128)(2,1)}, u32[]{:S(2)}, u32[]{:S(2)}) collective-permute-start(bf16[96,2560]{1,0:T(8,128)(2,1)} %copy-done.21), channel_id=1, source_target_pairs={{2,1},{3,2},{6,5},{7,6},{10,9},{11,10},{14,13},{15,14},{18,17},{19... | collective-permute-start | bytes 1474568 | tf_op jit(solution)/shard_map/ppermute | solution.py:45
  83.6 20.7 %collective-permute-start.26 = (bf16[96,2560]{1,0:T(8,128)(2,1)}, bf16[96,2560]{1,0:T(8,128)(2,1)}, u32[]{:S(2)}, u32[]{:S(2)}) collective-permute-start(bf16[96,2560]{1,0:T(8,128)(2,1)} %get-tuple-element.398), channel_id=1, source_target_pairs={{0,1},{1,2},{4,5},{5,6},{8,9},{9,10},{12,13},{13,14},{16,17},{17,1... | collective-permute-start | bytes 1474568 | tf_op jit(solution)/shard_map/ppermute | solution.py:45
  88.6 15.6 %collective-permute-start.27 = (bf16[96,2560]{1,0:T(8,128)(2,1)}, bf16[96,2560]{1,0:T(8,128)(2,1)}, u32[]{:S(2)}, u32[]{:S(2)}) collective-permute-start(bf16[96,2560]{1,0:T(8,128)(2,1)} %get-tuple-element.399), channel_id=1, source_target_pairs={{2,1},{3,2},{6,5},{7,6},{10,9},{11,10},{14,13},{15,14},{18,17},{19... | collective-permute-start | bytes 1474568 | tf_op jit(solution)/shard_map/ppermute | solution.py:45
  90.9 42.2 %all-to-all-start.6 = ((bf16[4,96,640]{2,1,0:T(8,128)(2,1)}), bf16[4,96,640]{2,1,0:T(8,128)(2,1)}, u32[]{:S(2)}, u32[]{:S(2)}) async-start(bf16[4,96,640]{2,1,0:T(8,128)(2,1)} %cut_heads.7), calls=%async_computation.6 | async-start | bytes 983040 | tf_op jit(solution)/shard_map/all_to_all | solution.py:443
  98.7 21.1 %collective-permute-start.10 = (bf16[96,2560]{1,0:T(8,128)(2,1)S(1)}, bf16[96,2560]{1,0:T(8,128)(2,1)S(1)}, u32[]{:S(2)}, u32[]{:S(2)}) collective-permute-start(bf16[96,2560]{1,0:T(8,128)(2,1)S(1)} %get-tuple-element.384), channel_id=1, source_target_pairs={{0,1},{1,2},{2,3},{4,5},{5,6},{6,7},{8,9},{9,10},{10,11},{12,13},{... | collective-permute-start | bytes 1474568 | tf_op jit(solution)/shard_map/ppermute | solution.py:45
  102.7 12.9 %copy-start.67 = (f32[2560]{0:T(1024)S(1)}, f32[2560]{0:T(1024)}, u32[]{:S(2)}) copy-start(f32[2560]{0:T(1024)} %param.19) | copy-start | bytes 30724
  102.7 12.9 %copy-start.68 = (bf16[640,2560]{1,0:T(8,128)(2,1)S(1)}, bf16[640,2560]{1,0:T(8,128)(2,1)}, u32[]{:S(2)}) copy-start(bf16[640,2560]{1,0:T(8,128)(2,1)} %get-tuple-element.375.weights_ref) | copy-start | bytes 9830404
  102.7 17.6 %collective-permute-start.11 = (bf16[96,2560]{1,0:T(8,128)(2,1)S(1)}, bf16[96,2560]{1,0:T(8,128)(2,1)S(1)}, u32[]{:S(2)}, u32[]{:S(2)}) collective-permute-start(bf16[96,2560]{1,0:T(8,128)(2,1)S(1)} %get-tuple-element.385), channel_id=1, source_target_pairs={{1,0},{2,1},{3,2},{5,4},{6,5},{7,6},{9,8},{10,9},{11,10},{13,12},{... | collective-permute-start | bytes 1474568 | tf_op jit(solution)/shard_map/ppermute | solution.py:45
  104.3 16.0 %copy-start.14 = (bf16[1,384,2560]{2,1,0:T(8,128)(2,1)S(1)}, bf16[1,384,2560]{2,1,0:T(8,128)(2,1)}, u32[]{:S(2)}) copy-start(bf16[1,384,2560]{2,1,0:T(8,128)(2,1)} %param.18) | copy-start | bytes 5898244
  107.1 29.7 %collective-permute-start.28 = (bf16[96,2560]{1,0:T(8,128)(2,1)}, bf16[96,2560]{1,0:T(8,128)(2,1)S(1)}, u32[]{:S(2)}, u32[]{:S(2)}) collective-permute-start(bf16[96,2560]{1,0:T(8,128)(2,1)} %get-tuple-element.400), channel_id=1, source_target_pairs={{0,1},{1,2},{2,3},{4,5},{5,6},{6,7},{8,9},{9,10},{10,11},{12,13},{... | collective-permute-start | bytes 1474568 | tf_op jit(solution)/shard_map/ppermute | solution.py:45
  114.3 22.5 %collective-permute-start.29 = (bf16[96,2560]{1,0:T(8,128)(2,1)}, bf16[96,2560]{1,0:T(8,128)(2,1)}, u32[]{:S(2)}, u32[]{:S(2)}) collective-permute-start(bf16[96,2560]{1,0:T(8,128)(2,1)} %get-tuple-element.401), channel_id=1, source_target_pairs={{1,0},{2,1},{3,2},{5,4},{6,5},{7,6},{9,8},{10,9},{11,10},{13,12},{... | collective-permute-start | bytes 1474568 | tf_op jit(solution)/shard_map/ppermute | solution.py:45
  121.7 26.3 %collective-permute-start.13 = (bf16[96,2560]{1,0:T(8,128)(2,1)}, bf16[96,2560]{1,0:T(8,128)(2,1)}, u32[]{:S(2)}, u32[]{:S(2)}) collective-permute-start(bf16[96,2560]{1,0:T(8,128)(2,1)} %unit_gradient.4.refs_0_), channel_id=1, source_target_pairs={{1,0},{2,1},{3,2},{5,4},{6,5},{7,6},{9,8},{10,9},{11,10},{13,12},{... | collective-permute-start | bytes 1474568 | tf_op jit(solution)/shard_map/ppermute | solution.py:45
  123.0 25.0 %collective-permute-start.12 = (bf16[96,2560]{1,0:T(8,128)(2,1)}, bf16[96,2560]{1,0:T(8,128)(2,1)}, u32[]{:S(2)}, u32[]{:S(2)}) collective-permute-start(bf16[96,2560]{1,0:T(8,128)(2,1)} %unit_gradient.4.refs_0_), channel_id=1, source_target_pairs={{0,1},{1,2},{2,3},{4,5},{5,6},{6,7},{8,9},{9,10},{10,11},{12,13},{... | collective-permute-start | bytes 1474568 | tf_op jit(solution)/shard_map/ppermute | solution.py:45
  141.3 12.9 %collective-permute-start.31 = (bf16[96,2560]{1,0:T(8,128)(2,1)}, bf16[96,2560]{1,0:T(8,128)(2,1)}, u32[]{:S(2)}, u32[]{:S(2)}) collective-permute-start(bf16[96,2560]{1,0:T(8,128)(2,1)} %unit_gradient.6.refs_7_), channel_id=1, source_target_pairs={{1,0},{2,1},{3,2},{5,4},{6,5},{7,6},{9,8},{10,9},{11,10},{13,12},{... | collective-permute-start | bytes 1474568 | tf_op jit(solution)/shard_map/ppermute | solution.py:45
  142.6 14.0 %collective-permute-start.30 = (bf16[96,2560]{1,0:T(8,128)(2,1)}, bf16[96,2560]{1,0:T(8,128)(2,1)}, u32[]{:S(2)}, u32[]{:S(2)}) collective-permute-start(bf16[96,2560]{1,0:T(8,128)(2,1)} %unit_gradient.6.refs_7_), channel_id=1, source_target_pairs={{0,1},{1,2},{2,3},{4,5},{5,6},{6,7},{8,9},{9,10},{10,11},{12,13},{... | collective-permute-start | bytes 1474568 | tf_op jit(solution)/shard_map/ppermute | solution.py:45
  150.5 16.5 %collective-permute-start.14 = (bf16[96,2560]{1,0:T(8,128)(2,1)S(1)}, bf16[96,2560]{1,0:T(8,128)(2,1)S(1)}, u32[]{:S(2)}, u32[]{:S(2)}) collective-permute-start(bf16[96,2560]{1,0:T(8,128)(2,1)S(1)} %get-tuple-element.389), channel_id=1, source_target_pairs={{0,1},{1,2},{2,3},{4,5},{5,6},{6,7},{8,9},{9,10},{10,11},{12,13},{... | collective-permute-start | bytes 1474568 | tf_op jit(solution)/shard_map/ppermute | solution.py:45
  152.9 14.7 %collective-permute-start.15 = (bf16[96,2560]{1,0:T(8,128)(2,1)S(1)}, bf16[96,2560]{1,0:T(8,128)(2,1)S(1)}, u32[]{:S(2)}, u32[]{:S(2)}) collective-permute-start(bf16[96,2560]{1,0:T(8,128)(2,1)S(1)} %get-tuple-element.390), channel_id=1, source_target_pairs={{1,0},{2,1},{3,2},{5,4},{6,5},{7,6},{9,8},{10,9},{11,10},{13,12},{... | collective-permute-start | bytes 1474568 | tf_op jit(solution)/shard_map/ppermute | solution.py:45
  159.0 18.5 %collective-permute-start.32 = (bf16[96,2560]{1,0:T(8,128)(2,1)S(1)}, bf16[96,2560]{1,0:T(8,128)(2,1)S(1)}, u32[]{:S(2)}, u32[]{:S(2)}) collective-permute-start(bf16[96,2560]{1,0:T(8,128)(2,1)S(1)} %get-tuple-element.405), channel_id=1, source_target_pairs={{0,1},{1,2},{2,3},{4,5},{5,6},{6,7},{8,9},{9,10},{10,11},{12,13},{... | collective-permute-start | bytes 1474568 | tf_op jit(solution)/shard_map/ppermute | solution.py:45
  164.8 15.9 %collective-permute-start.33 = (bf16[96,2560]{1,0:T(8,128)(2,1)S(1)}, bf16[96,2560]{1,0:T(8,128)(2,1)S(1)}, u32[]{:S(2)}, u32[]{:S(2)}) collective-permute-start(bf16[96,2560]{1,0:T(8,128)(2,1)S(1)} %get-tuple-element.406), channel_id=1, source_target_pairs={{1,0},{2,1},{3,2},{5,4},{6,5},{7,6},{9,8},{10,9},{11,10},{13,12},{... | collective-permute-start | bytes 1474568 | tf_op jit(solution)/shard_map/ppermute | solution.py:45
  167.0 69.7 %copy-start.51 = (bf16[96,2560]{1,0:T(8,128)(2,1)}, bf16[96,2560]{1,0:T(8,128)(2,1)S(1)}, u32[]{:S(2)}) copy-start(bf16[96,2560]{1,0:T(8,128)(2,1)S(1)} %collective-permute-done.14.right_ref.refs_2_) | copy-start | bytes 1474564
  167.6 69.0 %copy-start.53 = (bf16[96,2560]{1,0:T(8,128)(2,1)}, bf16[96,2560]{1,0:T(8,128)(2,1)S(1)}, u32[]{:S(2)}) copy-start(bf16[96,2560]{1,0:T(8,128)(2,1)S(1)} %collective-permute-done.15.left_ref.refs_5_) | copy-start | bytes 1474564
  168.9 19.1 %collective-permute-start.16 = (bf16[96,2560]{1,0:T(8,128)(2,1)S(1)}, bf16[96,2560]{1,0:T(8,128)(2,1)S(1)}, u32[]{:S(2)}, u32[]{:S(2)}) collective-permute-start(bf16[96,2560]{1,0:T(8,128)(2,1)S(1)} %get-tuple-element.391), channel_id=1, source_target_pairs={{0,1},{1,2},{2,3},{4,5},{5,6},{6,7},{8,9},{9,10},{10,11},{12,13},{... | collective-permute-start | bytes 1474568 | tf_op jit(solution)/shard_map/ppermute | solution.py:45
  174.1 17.1 %collective-permute-start.17 = (bf16[96,2560]{1,0:T(8,128)(2,1)S(1)}, bf16[96,2560]{1,0:T(8,128)(2,1)S(1)}, u32[]{:S(2)}, u32[]{:S(2)}) collective-permute-start(bf16[96,2560]{1,0:T(8,128)(2,1)S(1)} %get-tuple-element.392), channel_id=1, source_target_pairs={{1,0},{2,1},{3,2},{5,4},{6,5},{7,6},{9,8},{10,9},{11,10},{13,12},{... | collective-permute-start | bytes 1474568 | tf_op jit(solution)/shard_map/ppermute | solution.py:45
  182.0 16.7 %collective-permute-start.34 = (bf16[96,2560]{1,0:T(8,128)(2,1)S(1)}, bf16[96,2560]{1,0:T(8,128)(2,1)S(1)}, u32[]{:S(2)}, u32[]{:S(2)}) collective-permute-start(bf16[96,2560]{1,0:T(8,128)(2,1)S(1)} %get-tuple-element.407), channel_id=1, source_target_pairs={{0,1},{1,2},{2,3},{4,5},{5,6},{6,7},{8,9},{9,10},{10,11},{12,13},{... | collective-permute-start | bytes 1474568 | tf_op jit(solution)/shard_map/ppermute | solution.py:45
  186.5 16.1 %collective-permute-start.35 = (bf16[96,2560]{1,0:T(8,128)(2,1)S(1)}, bf16[96,2560]{1,0:T(8,128)(2,1)S(1)}, u32[]{:S(2)}, u32[]{:S(2)}) collective-permute-start(bf16[96,2560]{1,0:T(8,128)(2,1)S(1)} %get-tuple-element.408), channel_id=1, source_target_pairs={{1,0},{2,1},{3,2},{5,4},{6,5},{7,6},{9,8},{10,9},{11,10},{13,12},{... | collective-permute-start | bytes 1474568 | tf_op jit(solution)/shard_map/ppermute | solution.py:45
  192.5 16.6 %collective-permute-start.18 = (bf16[96,2560]{1,0:T(8,128)(2,1)S(1)}, bf16[96,2560]{1,0:T(8,128)(2,1)S(1)}, u32[]{:S(2)}, u32[]{:S(2)}) collective-permute-start(bf16[96,2560]{1,0:T(8,128)(2,1)S(1)} %get-tuple-element.393), channel_id=1, source_target_pairs={{0,1},{1,2},{2,3},{4,5},{5,6},{6,7},{8,9},{9,10},{10,11},{12,13},{... | collective-permute-start | bytes 1474568 | tf_op jit(solution)/shard_map/ppermute | solution.py:45
  197.1 16.3 %copy-start.13 = (bf16[1,384,2560]{2,1,0:T(8,128)(2,1)S(1)}, bf16[1,384,2560]{2,1,0:T(8,128)(2,1)}, u32[]{:S(2)}) copy-start(bf16[1,384,2560]{2,1,0:T(8,128)(2,1)} %param.17) | copy-start | bytes 5898244
  197.1 16.3 %copy-start.16 = (bf16[1,384,2560]{2,1,0:T(8,128)(2,1)S(1)}, bf16[1,384,2560]{2,1,0:T(8,128)(2,1)}, u32[]{:S(2)}) copy-start(bf16[1,384,2560]{2,1,0:T(8,128)(2,1)} %param.18) | copy-start | bytes 5898244
  197.1 16.3 %collective-permute-start.19 = (bf16[96,2560]{1,0:T(8,128)(2,1)S(1)}, bf16[96,2560]{1,0:T(8,128)(2,1)S(1)}, u32[]{:S(2)}, u32[]{:S(2)}) collective-permute-start(bf16[96,2560]{1,0:T(8,128)(2,1)S(1)} %get-tuple-element.394), channel_id=1, source_target_pairs={{1,0},{2,1},{3,2},{5,4},{6,5},{7,6},{9,8},{10,9},{11,10},{13,12},{... | collective-permute-start | bytes 1474568 | tf_op jit(solution)/shard_map/ppermute | solution.py:45
  203.9 16.8 %collective-permute-start.38 = (bf16[96,2560]{1,0:T(8,128)(2,1)S(1)}, bf16[96,2560]{1,0:T(8,128)(2,1)S(1)}, u32[]{:S(2)}, u32[]{:S(2)}) collective-permute-start(bf16[96,2560]{1,0:T(8,128)(2,1)S(1)} %get-tuple-element.413), channel_id=1, source_target_pairs={{0,1},{1,2},{2,3},{4,5},{5,6},{6,7},{8,9},{9,10},{10,11},{12,13},{... | collective-permute-start | bytes 1474568 | tf_op jit(solution)/shard_map/ppermute | solution.py:45
  207.6 16.3 %collective-permute-start.39 = (bf16[96,2560]{1,0:T(8,128)(2,1)S(1)}, bf16[96,2560]{1,0:T(8,128)(2,1)S(1)}, u32[]{:S(2)}, u32[]{:S(2)}) collective-permute-start(bf16[96,2560]{1,0:T(8,128)(2,1)S(1)} %get-tuple-element.414), channel_id=1, source_target_pairs={{1,0},{2,1},{3,2},{5,4},{6,5},{7,6},{9,8},{10,9},{11,10},{13,12},{... | collective-permute-start | bytes 1474568 | tf_op jit(solution)/shard_map/ppermute | solution.py:45
  214.0 20.4 %collective-permute-start.22 = (bf16[96,2560]{1,0:T(8,128)(2,1)S(1)}, bf16[96,2560]{1,0:T(8,128)(2,1)S(1)}, u32[]{:S(2)}, u32[]{:S(2)}) collective-permute-start(bf16[96,2560]{1,0:T(8,128)(2,1)S(1)} %unit_gradient.5.refs_0_), channel_id=1, source_target_pairs={{1,0},{2,1},{3,2},{5,4},{6,5},{7,6},{9,8},{10,9},{11,10},{13,12},{... | collective-permute-start | bytes 1474568 | tf_op jit(solution)/shard_map/ppermute | solution.py:45
  215.3 20.4 %collective-permute-start.20 = (bf16[96,2560]{1,0:T(8,128)(2,1)S(1)}, bf16[96,2560]{1,0:T(8,128)(2,1)}, u32[]{:S(2)}, u32[]{:S(2)}) collective-permute-start(bf16[96,2560]{1,0:T(8,128)(2,1)S(1)} %unit_gradient.5.refs_0_), channel_id=1, source_target_pairs={{0,1},{1,2},{2,3},{4,5},{5,6},{6,7},{8,9},{9,10},{10,11},{12,13},{... | collective-permute-start | bytes 1474568 | tf_op jit(solution)/shard_map/ppermute | solution.py:45
  224.6 20.4 %collective-permute-start.41 = (bf16[96,2560]{1,0:T(8,128)(2,1)S(1)}, bf16[96,2560]{1,0:T(8,128)(2,1)S(1)}, u32[]{:S(2)}, u32[]{:S(2)}) collective-permute-start(bf16[96,2560]{1,0:T(8,128)(2,1)S(1)} %unit_gradient.7.refs_7_), channel_id=1, source_target_pairs={{1,0},{2,1},{3,2},{5,4},{6,5},{7,6},{9,8},{10,9},{11,10},{13,12},{... | collective-permute-start | bytes 1474568 | tf_op jit(solution)/shard_map/ppermute | solution.py:45
  225.9 19.1 %collective-permute-start.40 = (bf16[96,2560]{1,0:T(8,128)(2,1)S(1)}, bf16[96,2560]{1,0:T(8,128)(2,1)S(1)}, u32[]{:S(2)}, u32[]{:S(2)}) collective-permute-start(bf16[96,2560]{1,0:T(8,128)(2,1)S(1)} %unit_gradient.7.refs_7_), channel_id=1, source_target_pairs={{0,1},{1,2},{2,3},{4,5},{5,6},{6,7},{8,9},{9,10},{10,11},{12,13},{... | collective-permute-start | bytes 1474568 | tf_op jit(solution)/shard_map/ppermute | solution.py:45
  234.5 21.1 %collective-permute-start.23 = (bf16[96,2560]{1,0:T(8,128)(2,1)S(1)}, bf16[96,2560]{1,0:T(8,128)(2,1)S(1)}, u32[]{:S(2)}, u32[]{:S(2)}) collective-permute-start(bf16[96,2560]{1,0:T(8,128)(2,1)S(1)} %collective-permute-done.22.refs_4_), channel_id=1, source_target_pairs={{1,0},{2,1},{5,4},{6,5},{9,8},{10,9},{13,12},{14,13},{17,16},{18,1... | collective-permute-start | bytes 1474568 | tf_op jit(solution)/shard_map/ppermute | solution.py:45
  235.8 19.8 %collective-permute-start.21 = (bf16[96,2560]{1,0:T(8,128)(2,1)}, bf16[96,2560]{1,0:T(8,128)(2,1)S(1)}, u32[]{:S(2)}, u32[]{:S(2)}) collective-permute-start(bf16[96,2560]{1,0:T(8,128)(2,1)} %collective-permute-done.20.refs_1_), channel_id=1, source_target_pairs={{1,2},{2,3},{5,6},{6,7},{9,10},{10,11},{13,14},{14,15},{17,18},{18... | collective-permute-start | bytes 1474568 | tf_op jit(solution)/shard_map/ppermute | solution.py:45
  245.1 13.3 %collective-permute-start.42 = (bf16[96,2560]{1,0:T(8,128)(2,1)S(1)}, bf16[96,2560]{1,0:T(8,128)(2,1)}, u32[]{:S(2)}, u32[]{:S(2)}) collective-permute-start(bf16[96,2560]{1,0:T(8,128)(2,1)S(1)} %get-tuple-element.416), channel_id=1, source_target_pairs={{1,2},{2,3},{5,6},{6,7},{9,10},{10,11},{13,14},{14,15},{17,18},{18... | collective-permute-start | bytes 1474568 | tf_op jit(solution)/shard_map/ppermute | solution.py:45
  246.6 19.6 %collective-permute-start.44 = (bf16[96,2560]{1,0:T(8,128)(2,1)S(1)}, bf16[96,2560]{1,0:T(8,128)(2,1)}, u32[]{:S(2)}, u32[]{:S(2)}) collective-permute-start(bf16[96,2560]{1,0:T(8,128)(2,1)S(1)} %get-tuple-element.417), channel_id=1, source_target_pairs={{1,0},{2,1},{5,4},{6,5},{9,8},{10,9},{13,12},{14,13},{17,16},{18,1... | collective-permute-start | bytes 1474568 | tf_op jit(solution)/shard_map/ppermute | solution.py:45
  252.6 13.6 %copy-start.25 = (f32[640,2560]{1,0:T(8,128)}, f32[640,2560]{1,0:T(8,128)S(1)}, u32[]{:S(2)}) copy-start(f32[640,2560]{1,0:T(8,128)S(1)} %get-tuple-element.418.refs_16_) | copy-start | bytes 19660804
  255.6 13.1 %collective-permute-start.36 = (bf16[96,2560]{1,0:T(8,128)(2,1)S(1)}, bf16[96,2560]{1,0:T(8,128)(2,1)}, u32[]{:S(2)}, u32[]{:S(2)}) collective-permute-start(bf16[96,2560]{1,0:T(8,128)(2,1)S(1)} %get-tuple-element.411), channel_id=1, source_target_pairs={{2,3},{6,7},{10,11},{14,15},{18,19},{22,23},{26,27},{30,31}} | collective-permute-start | bytes 1474568 | tf_op jit(solution)/shard_map/ppermute | solution.py:45
  257.1 17.3 %collective-permute-start.37 = (bf16[96,2560]{1,0:T(8,128)(2,1)S(1)}, bf16[96,2560]{1,0:T(8,128)(2,1)}, u32[]{:S(2)}, u32[]{:S(2)}) collective-permute-start(bf16[96,2560]{1,0:T(8,128)(2,1)S(1)} %get-tuple-element.412), channel_id=1, source_target_pairs={{1,0},{5,4},{9,8},{13,12},{17,16},{21,20},{25,24},{29,28}} | collective-permute-start | bytes 1474568 | tf_op jit(solution)/shard_map/ppermute | solution.py:45
  258.4 16.0 %collective-permute-start.43 = (bf16[96,2560]{1,0:T(8,128)(2,1)}, bf16[96,2560]{1,0:T(8,128)(2,1)}, u32[]{:S(2)}, u32[]{:S(2)}) collective-permute-start(bf16[96,2560]{1,0:T(8,128)(2,1)} %collective-permute-done.42.refs_9_), channel_id=1, source_target_pairs={{2,3},{6,7},{10,11},{14,15},{18,19},{22,23},{26,27},{30,31}} | collective-permute-start | bytes 1474568 | tf_op jit(solution)/shard_map/ppermute | solution.py:45
  266.2 13.4 %collective-permute-start.45 = (bf16[96,2560]{1,0:T(8,128)(2,1)}, bf16[96,2560]{1,0:T(8,128)(2,1)}, u32[]{:S(2)}, u32[]{:S(2)}) collective-permute-start(bf16[96,2560]{1,0:T(8,128)(2,1)} %collective-permute-done.44.refs_12_), channel_id=1, source_target_pairs={{1,0},{5,4},{9,8},{13,12},{17,16},{21,20},{25,24},{29,28}} | collective-permute-start | bytes 1474568 | tf_op jit(solution)/shard_map/ppermute | solution.py:45
  289.5 15.3 %copy-start.30 = (bf16[96,2560]{1,0:T(8,128)(2,1)}, bf16[96,2560]{1,0:T(8,128)(2,1)S(1)}, u32[]{:S(2)}) copy-start(bf16[96,2560]{1,0:T(8,128)(2,1)S(1)} %get-tuple-element.309.refs_21_.refs_7_) | copy-start | bytes 1474564 | tf_op jit(solution)/shard_map/cond
  289.5 15.3 %copy-start.34 = (bf16[96,2560]{1,0:T(8,128)(2,1)}, bf16[96,2560]{1,0:T(8,128)(2,1)S(1)}, u32[]{:S(2)}) copy-start(bf16[96,2560]{1,0:T(8,128)(2,1)S(1)} %get-tuple-element.313.refs_25_.refs_11_) | copy-start | bytes 1474564 | tf_op jit(solution)/shard_map/cond
  289.5 15.3 %copy-start.37 = (bf16[96,2560]{1,0:T(8,128)(2,1)}, bf16[96,2560]{1,0:T(8,128)(2,1)S(1)}, u32[]{:S(2)}) copy-start(bf16[96,2560]{1,0:T(8,128)(2,1)S(1)} %get-tuple-element.310.refs_22_.refs_8_) | copy-start | bytes 1474564 | tf_op jit(solution)/shard_map/cond
  289.6 15.3 %copy-start.40 = (bf16[96,2560]{1,0:T(8,128)(2,1)}, bf16[96,2560]{1,0:T(8,128)(2,1)S(1)}, u32[]{:S(2)}) copy-start(bf16[96,2560]{1,0:T(8,128)(2,1)S(1)} %get-tuple-element.307.refs_19_.refs_5_) | copy-start | bytes 1474564 | tf_op jit(solution)/shard_map/cond
  289.6 15.3 %copy-start.45 = (bf16[96,2560]{1,0:T(8,128)(2,1)}, bf16[96,2560]{1,0:T(8,128)(2,1)S(1)}, u32[]{:S(2)}) copy-start(bf16[96,2560]{1,0:T(8,128)(2,1)S(1)} %get-tuple-element.304.refs_16_.refs_2_) | copy-start | bytes 1474564 | tf_op jit(solution)/shard_map/cond
  289.6 15.3 %copy-start.50 = (bf16[96,2560]{1,0:T(8,128)(2,1)}, bf16[96,2560]{1,0:T(8,128)(2,1)S(1)}, u32[]{:S(2)}) copy-start(bf16[96,2560]{1,0:T(8,128)(2,1)S(1)} %get-tuple-element.306.refs_18_.refs_4_) | copy-start | bytes 1474564 | tf_op jit(solution)/shard_map/cond
  289.6 65.8 %collective-permute-start.2 = (bf16[640,2560]{1,0:T(8,128)(2,1)}, bf16[640,2560]{1,0:T(8,128)(2,1)}, u32[]{:S(2)}, u32[]{:S(2)}) collective-permute-start(bf16[640,2560]{1,0:T(8,128)(2,1)} %get-tuple-element.286), channel_id=1, source_target_pairs={{0,16},{4,20},{8,24},{12,28},{16,0},{20,4},{24,8},{28,12},{1,17},{... | collective-permute-start | bytes 9830408 | tf_op jit(solution)/shard_map/cond/branch_2_fun/ppermute | solution.py:448
  306.1 43.2 %all-to-all-start.2 = ((bf16[4,384,640]{2,1,0:T(8,128)(2,1)}), bf16[4,384,640]{2,1,0:T(8,128)(2,1)S(1)}, u32[]{:S(2)}, u32[]{:S(2)}) async-start(bf16[4,384,640]{2,1,0:T(8,128)(2,1)} %copy-done.19), calls=%async_computation.2 | async-start | bytes 3932160 | tf_op jit(solution)/shard_map/cond/branch_2_fun/all_to_all | solution.py:443
  (40 other events, 234.4 us)

commit v7 on v6

--- a/solution.py
+++ b/solution.py
@@ -253,46 +253,59 @@
     ]
 
 
-def turned_into(scratch, mine_refs, order):
-    members = mine_refs[0].shape[0]
-    stack = jnp.concatenate([ref[order[k]] for ref in mine_refs for k in range(members)], axis=0)
-    scratch[...] = stack.T
-
-
-def weight_step(units, mine, order, base, first, last, inbox=None, kept=None, new=False, token=None):
+def turned_heads(mine, order):
     members, _, rows = mine[0][0].shape
+    total = sum(members * size for _, _, size in mine)
+
+    def body(s, *refs):
+        out_ref, token_out = refs[-2:]
+        stack = jnp.concatenate([ref[s[k]] for ref in refs[:-2] for k in range(members)], axis=0)
+        out_ref[...] = stack.T
+        token_out[...] = jnp.zeros((8, 128), jnp.float32)
+
+    return call(
+        body,
+        "turned_heads",
+        (1,),
+        mine_ins(mine),
+        [((rows, total), jnp.bfloat16, (rows, total), fixed(0, 0)), TOKEN_OUT],
+        scalars=(order,),
+        moved=4 * rows * total,
+        vmem=20,
+    )
+
+
+def weight_step(units, turned, order, base, first, last, inbox=None, kept=None, new=False, token=None):
+    rows, total = turned.shape
+    members = (len(units[0]) + 1) // 2
     width = base.shape[1]
     tile = tile_of(width)
     last = width // tile if last is None else last
     count = len(units) * len(units[0])
-    chunks = len(units)
-    total = sum(members * size for _, _, size in mine)
     early = inbox is None
 
     def body(s, *refs):
-        units_ref, mine_refs = refs[:count], refs[count : count + chunks]
-        base_ref = refs[count + chunks]
-        turned = refs[-1]
-
-        @pl.when(pl.program_id(0) == 0)
-        def _():
-            turned_into(turned, mine_refs, s)
-
+        turned_ref, base_ref = refs[count : count + 2]
         weight = jnp.dot(
-            turned[...], stack_of(units_ref, members, s[0]), preferred_element_type=jnp.float32
+            turned_ref[...],
+            stack_of(refs[:count], members, s[0]),
+            preferred_element_type=jnp.float32,
         )
         if early:
-            refs[-3][...] = 0.5 * (base_ref[...] - 0.004 * weight)
-            refs[-2][...] = jnp.zeros((8, 128), jnp.float32)
+            refs[-2][...] = 0.5 * (base_ref[...] - 0.004 * weight)
+            refs[-1][...] = jnp.zeros((8, 128), jnp.float32)
         else:
             now = base_ref[...] - 0.5 * 0.004 * weight
             if new:
-                refs[-2][...] = now + refs[count + chunks + 1][...]
+                refs[-1][...] = now + refs[count + 2][...]
             else:
-                refs[-2][...] = now.astype(jnp.bfloat16)
+                refs[-1][...] = now.astype(jnp.bfloat16)
 
     columns = (rows, tile), lambda j, s: (0, j + first)
-    ins = unit_ins(units, tile, first) + mine_ins(mine) + [(base,) + columns]
+    ins = unit_ins(units, tile, first) + [
+        (turned, (rows, total), fixed(0, 0)),
+        (base,) + columns,
+    ]
     if new:
         ins.append((inbox,) + columns)
     if kept is not None:
@@ -308,11 +321,10 @@
         ins,
         outs + [TOKEN_OUT] * early,
         scalars=(order,),
-        scratch=[pltpu.VMEM((rows, total), jnp.bfloat16)],
         flops=2 * total * rows * tile * (last - first),
         moved=(2 * count * units[0][0].shape[0] + 12 * rows) * tile * (last - first),
         vmem=52,
-        aliases={} if kept is None else {1 + count + chunks + 1: 0},
+        aliases={} if kept is None else {1 + count + 2: 0},
     )
 
 
@@ -395,28 +407,34 @@
     )
 
 
-def joined_rows(blocks):
-    members, tokens, rows = blocks.shape
-    step = 96
-
-    def body(blocks_ref, out_ref):
-        for k in range(members):
-            out_ref[:, k * rows : (k + 1) * rows] = blocks_ref[k]
+def joined_rows(groups):
+    members, size, rows = groups[0].shape
+    tokens = size * len(groups)
+
+    def body(*refs):
+        out_ref = refs[-1]
+        for g, blocks_ref in enumerate(refs[:-1]):
+
+            @pl.when(pl.program_id(0) == g)
+            def _(blocks_ref=blocks_ref):
+                for k in range(members):
+                    out_ref[:, k * rows : (k + 1) * rows] = blocks_ref[k]
 
     return call(
         body,
         "joined_rows",
-        (tokens // step,),
-        [(blocks, (members, step, rows), lambda i: (0, i, 0))],
+        (len(groups),),
+        [(blocks, (members, size, rows), fixed(0, 0, 0)) for blocks in groups],
         [
             (
                 (tokens, members * rows),
-                blocks.dtype,
-                (step, members * rows),
+                groups[0].dtype,
+                (size, members * rows),
                 lambda i: (i, 0),
             )
         ],
         moved=4 * members * tokens * rows,
+        vmem=24,
     )[0]
 
 
@@ -443,15 +461,16 @@
     return lax.all_to_all(blocks, "fsdp", 0, 0, tiled=False)
 
 
-def tail(half, early, late, mine, kept, inbox, weights, order, bit_place):
+def tail(half, grads, late, turned, kept, inbox, weights, order, bit_place):
     length = lax.axis_size("rep")
     sent = lax.ppermute(
         half, "rep", [(i, (i + (1 << bit_place)) % length) for i in range(length)]
     )
-    grads, token = grad_rows(early + late, weights, order)
     back = swapped(grads)
-    new = weight_step(late, mine, order, kept, 0, None, inbox, new=True, token=token)[0]
-    return sent, joined_rows(back), new
+    late_grads, token = grad_rows(late, weights, order)
+    late_back = swapped(late_grads)
+    new = weight_step(late, turned, order, kept, 0, None, inbox, new=True, token=token)[0]
+    return sent, joined_rows([back, late_back]), new
 
 
 def local(
@@ -472,16 +491,20 @@
     powers = jnp.left_shift(jnp.ones((levels,), jnp.int32), jnp.arange(levels, dtype=jnp.int32))
     level_index = jnp.sum(jnp.where(powers == offset[0], jnp.arange(levels, dtype=jnp.int32), 0))
 
-    def sent_weight(token):
+    arrived = [None] * levels
+    slots = [(1, 0), (1, 1), (2, 0)]
+
+    def levels_of(slot):
+        return [b for b in range(levels) if min(b, len(slots) - 1) == slot]
+
+    def sent_weight(token, b):
         half = 0.5 * push_weight + token[0, :1]
-        arrived = [
-            lax.ppermute(half, "rep", [(i, (i + (1 << b)) % replicas) for i in range(replicas)])
-            for b in range(levels)
-        ]
-        chosen = arrived[0]
-        for b in range(1, levels):
-            chosen = jnp.where(level_index == b, arrived[b], chosen)
-        return chosen
+        return lax.ppermute(
+            half, "rep", [(i, (i + (1 << b)) % replicas) for i in range(replicas)]
+        )
+
+    def seen(slot):
+        return jnp.broadcast_to(sum(arrived[b] for b in levels_of(slot))[None], (8, 128))
 
     order = jnp.mod(me - jnp.arange(members, dtype=jnp.int32), members)
     own = me[None]
@@ -529,9 +552,6 @@
     for q in range(count):
         parts[q], token, last, first = partial_products(mine[0][q], weights, True, token)
         hint[q] = (last, first)
-        if q == 0:
-            outbox_weight = sent_weight(token)
-            token = jnp.broadcast_to(outbox_weight[None], (8, 128))
     for e in range(rounds):
         moving = [None] * count
         for q in range(count):
@@ -544,11 +564,17 @@
                 units[e - 1][q][2].append(moving[q][1])
         for t in range(1, members - 1):
             for q in range(count):
+                order_token = token if (e, t, q) == (0, 1, 0) else None
+                if e + 1 == rounds and t == 2:
+                    order_token = seen(slots.index((1, q)))
                 right, left, token = next_payload(
-                    *moving[q], parts[q], scalars(t), False, token if (e, t, q) == (0, 1, 0) else None
+                    *moving[q], parts[q], scalars(t), False, order_token
                 )
-                if t == 1 and e + 1 < rounds:
+                if t == members - 2 and e + 1 < rounds:
                     fetch(e + 1, [q], token)
+                if e + 1 == rounds and (t, q) in slots:
+                    for b in levels_of(slots.index((t, q))):
+                        arrived[b] = sent_weight(token, b)
                 if e == 0:
                     pairs = range(t + 1), range(members - 1 - t, members)
                 else:
@@ -570,7 +596,7 @@
                 cotangent[0],
                 gain[None],
                 starts[e][q],
-                token,
+                seen(2) if (e + 1, q + 1) == (rounds, count) else token,
             )
             before[q] = hops(unit, unit, *everyone)
             units[e][q] = (unit, [before[q][0]], [before[q][1]])
@@ -580,24 +606,31 @@
         for q in range(count):
             if (s, q) == (1, count - 1):
                 early = [[u] + r + l for of_round in units[:-1] for u, r, l in of_round]
-                early_mine = [m for of_round in mine[:-1] for m in of_round]
-                kept, done = weight_step(early, early_mine, order, numer, 0, 3)
+                early_turned, _ = turned_heads([m for of_round in mine[:-1] for m in of_round], order)
+                kept, done = weight_step(early, early_turned, order, numer, 0, 3)
                 before[q] = passed(*before[q], done)
             if (s, q) == (2, 0):
-                kept, done = weight_step(early, early_mine, order, numer, 3, None, kept=kept)
+                turned, token = turned_heads(mine[-1], order)
+                kept, done = weight_step(
+                    early, early_turned, order, numer, 3, None, kept=kept, token=token
+                )
                 before[q] = passed(*before[q], done)
             before[q] = hops(*before[q], range(s, members - 1), range(1, members - s))
             units[-1][q][1].append(before[q][0])
             units[-1][q][2].append(before[q][1])
     flat = [[u] + r + l for u, r, l in units[-1]]
-    half = weight_step(flat, mine[-1], order, kept, 0, None, inbox_params[0])[0]
+    grads, _ = grad_rows(early, weights, order)
+    half = weight_step(flat, turned, order, kept, 0, None, inbox_params[0])[0]
     new_weight = 0.5 * push_weight + inbox_weight
     branches = [
         partial(
-            tail, half, early, flat, mine[-1], kept, inbox_params[0], weights, order, place
+            tail, half, grads, flat, turned, kept, inbox_params[0], weights, order, place
         )
         for place in range(levels)
     ]
+    outbox_weight = arrived[0]
+    for b in range(1, levels):
+        outbox_weight = jnp.where(level_index == b, arrived[b], outbox_weight)
     sent, grad_heads, new_params = lax.switch(level_index, branches)
     return (new_params[None], new_weight, widened(sent)[None], outbox_weight, grad_heads[None])
 

time: 364 us -> 374 us (1.027)
  waiting for transfers between devices: 101 us -> 83.3 us
  local copies, waits for them, and re-layouts: 8.03 us -> 19.6 us
  Pallas kernels: 102 us -> 111 us
  starting transfers between devices: 140 us -> 148 us
    ppermute x40, waiting for transfers between devices: 64.3 us -> 34.7 us  [hop(): return lax.ppermute(value, 'fsdp', [(i, i + step) for i in pairs])]
    all_to_all x5 -> x6, starting transfers between devices: 23.7 us -> 37.2 us  [swapped(): return lax.all_to_all(blocks, 'fsdp', 0, 0, tiled=False)]
    ppermute x1, waiting for transfers between devices: 4.19 us -> 16.6 us  [tail(): lax.ppermute(half, 'rep', [(i, (i + (1 << bit_place)) % length) for i in...]
    unnamed x94 -> x92, local copies, waits for them, and re-layouts: 6.21 us -> 16.1 us
    pallas_call x32 -> x35, Pallas kernels: 102 us -> 111 us  [call(): pl.pallas_call(body, name=name, out_shape=[jax.ShapeDtypeStruct(shape, ki...]
    all_to_all x5 -> x6, waiting for transfers between devices: 32.3 us -> 25.7 us  [swapped(): return lax.all_to_all(blocks, 'fsdp', 0, 0, tiled=False)]
    ppermute x3, waiting for transfers between devices: 0.01 us -> 6.32 us  [sent_weight(): lax.ppermute(half, 'rep', [(i, (i + (1 << b)) % replicas) for i in range(...]
  transfers between devices with their start and end apart: 49 -> 50, of which waited for: 23 -> 19; matrix products, arithmetic and copies ran while one was open for 0% -> 1% of each run, Pallas kernels for 23% -> 25%
where the time goes in v7:
time: 374 us
  starting transfers between devices  148 us (40%)
  Pallas kernels  111 us (30%)
  waiting for transfers between devices  83.3 us (22%)
  local copies, waits for them, and re-layouts  19.6 us (5%)
  between operations  10.8 us (3%)
    pallas_call x35, Pallas kernels, call(): pl.pallas_call(body, name=name, out_shape=[jax.ShapeDtypeStruct(shape, ki...  111 us
    ppermute x40, starting transfers between devices, hop(): return lax.ppermute(value, 'fsdp', [(i, i + step) for i in pairs])  105 us
    all_to_all x6, starting transfers between devices, swapped(): return lax.all_to_all(blocks, 'fsdp', 0, 0, tiled=False)  37.2 us
    ppermute x40, waiting for transfers between devices, hop(): return lax.ppermute(value, 'fsdp', [(i, i + step) for i in pairs])  34.7 us
    all_to_all x6, waiting for transfers between devices, swapped(): return lax.all_to_all(blocks, 'fsdp', 0, 0, tiled=False)  25.7 us
    ppermute x1, waiting for transfers between devices, tail(): lax.ppermute(half, 'rep', [(i, (i + (1 << bit_place)) % length) for i in...  16.6 us
    unnamed x92, local copies, waits for them, and re-layouts  16.1 us
  transfers between devices with their start and end apart: 50, of which 19 were waited for; matrix products, arithmetic and copies ran while one was open for 1% of the time, Pallas kernels for 25%

profile of v7, /device:TPU:0, one launch (start us, length us, event | category | flops | bytes accessed | tf_op | source)
XLA Modules:
  0.0 373.6 jit_solution(4987411800878752158)
XLA Ops:
  0.6 1.8 cut_heads.4
  2.4 6.3 %all-to-all-start.6 = ((bf16[4,96,640]{2,1,0:T(8,128)(2,1)}), bf16[4,96,640]{2,1,0:T(8,128)(2,1)S(1)}, u32[]{:S(2)}, u32[]{:S(2)}) async-start(bf16[4,96,640]{2,1,0:T(8,128)(2,1)} %cut_heads.4), calls=%async_computation.6 | async-start | bytes 983040 | tf_op jit(solution)/shard_map/all_to_all | solution.py:461
  9.4 5.7 %scaled_weights.1 = (bf16[640,2560]{1,0:T(8,128)(2,1)}, f32[8,128]{1,0:T(8,128)}) custom-call(f32[640,2560]{1,0:T(8,128)} %bitcast.52, f32[1,1]{1,0:T(1,128)} %bitcast.36.one_ref), custom_call_target="tpu_custom_call" | custom-call | flops 3276800 | bytes 9830400 | tf_op jit(solution)/shard_map/scaled_weights/pallas_call | solution.py:16
  16.6 6.0 %all-to-all-done.6.mine_ref.refs_0_ = bf16[4,96,640]{2,1,0:T(8,128)(2,1)S(1)} async-done(((bf16[4,96,640]{2,1,0:T(8,128)(2,1)}), bf16[4,96,640]{2,1,0:T(8,128)(2,1)S(1)}, u32[]{:S(2)}, u32[]{:S(2)}) %all-to-all-start.6) | async-done | bytes 491552 | tf_op jit(solution)/shard_map/all_to_all | solution.py:461
  22.5 3.5 all-to-all-start.7
  26.0 4.2 %partial_products.4 = (bf16[4,96,2560]{2,1,0:T(8,128)(2,1)S(1)}, f32[8,128]{1,0:T(8,128)S(1)}, bf16[96,2560]{1,0:T(8,128)(2,1)}, bf16[96,2560]{1,0:T(8,128)(2,1)}) custom-call(bf16[4,96,640]{2,1,0:T(8,128)(2,1)S(1)} %all-to-all-done.6.mine_ref.refs_0_, bf16[640,2560]{1,0:T(8,128)(2,1)} %get-tuple-element.256.weights_ref.refs_14_), custom_call_target="tpu_custom_call" | custom-call | flops 1258291200 | bytes 5734400 | tf_op jit(solution)/shard_map/partial_products/pallas_call | solution.py:16
  30.2 3.9 %collective-permute-start.3 = (bf16[96,2560]{1,0:T(8,128)(2,1)}, bf16[96,2560]{1,0:T(8,128)(2,1)S(1)}, u32[]{:S(2)}, u32[]{:S(2)}) collective-permute-start(bf16[96,2560]{1,0:T(8,128)(2,1)} %get-tuple-element.257), channel_id=1, source_target_pairs={{0,1},{4,5},{8,9},{12,13},{16,17},{20,21},{24,25},{28,29}} | collective-permute-start | bytes 1474568 | tf_op jit(solution)/shard_map/ppermute | solution.py:45
  35.7 3.6 all-to-all-done.7.mine_ref.refs_1_
  39.3 4.4 %partial_products.5 = (bf16[4,96,2560]{2,1,0:T(8,128)(2,1)S(1)}, f32[8,128]{1,0:T(8,128)S(1)}, bf16[96,2560]{1,0:T(8,128)(2,1)}, bf16[96,2560]{1,0:T(8,128)(2,1)}) custom-call(bf16[4,96,640]{2,1,0:T(8,128)(2,1)S(1)} %all-to-all-done.7.mine_ref.refs_1_, bf16[640,2560]{1,0:T(8,128)(2,1)} %get-tuple-element.256.weights_ref.refs_14_, ...), custom_call_target="tpu_custom_call" | custom-call | flops 1258291200 | bytes 5734400 | tf_op jit(solution)/shard_map/partial_products/pallas_call | solution.py:16
  45.0 2.5 next_payload.10
  47.5 3.5 collective-permute-start.5
  52.5 4.6 %collective-permute-start.22 = (bf16[96,2560]{1,0:T(8,128)(2,1)}, bf16[96,2560]{1,0:T(8,128)(2,1)S(1)}, u32[]{:S(2)}, u32[]{:S(2)}) collective-permute-start(bf16[96,2560]{1,0:T(8,128)(2,1)} %get-tuple-element.277), channel_id=1, source_target_pairs={{0,1},{4,5},{8,9},{12,13},{16,17},{20,21},{24,25},{28,29}} | collective-permute-start | bytes 1474568 | tf_op jit(solution)/shard_map/ppermute | solution.py:45
  57.9 5.1 %collective-permute-done.5.right_ref = bf16[96,2560]{1,0:T(8,128)(2,1)S(1)} collective-permute-done((bf16[96,2560]{1,0:T(8,128)(2,1)}, bf16[96,2560]{1,0:T(8,128)(2,1)S(1)}, u32[]{:S(2)}, u32[]{:S(2)}) %collective-permute-start.5) | collective-permute-done | bytes 491552 | tf_op jit(solution)/shard_map/ppermute | solution.py:45
  63.0 1.8 next_payload.11
  67.2 7.3 %all-to-all-start.8 = ((bf16[4,96,640]{2,1,0:T(8,128)(2,1)}), bf16[4,96,640]{2,1,0:T(8,128)(2,1)S(1)}, u32[]{:S(2)}, u32[]{:S(2)}) async-start(bf16[4,96,640]{2,1,0:T(8,128)(2,1)} %cut_heads.6), calls=%async_computation.8 | async-start | bytes 983040 | tf_op jit(solution)/shard_map/all_to_all | solution.py:461
  74.5 1.5 copy-done.4
  77.3 4.1 %collective-permute-start.24 = (bf16[96,2560]{1,0:T(8,128)(2,1)S(1)}, bf16[96,2560]{1,0:T(8,128)(2,1)S(1)}, u32[]{:S(2)}, u32[]{:S(2)}) collective-permute-start(bf16[96,2560]{1,0:T(8,128)(2,1)S(1)} %get-tuple-element.280), channel_id=1, source_target_pairs={{0,1},{1,2},{4,5},{5,6},{8,9},{9,10},{12,13},{13,14},{16,17},{17,1... | collective-permute-start | bytes 1474568 | tf_op jit(solution)/shard_map/ppermute | solution.py:45
  82.3 7.9 %collective-permute-done.24.right_ref = bf16[96,2560]{1,0:T(8,128)(2,1)S(1)} collective-permute-done((bf16[96,2560]{1,0:T(8,128)(2,1)S(1)}, bf16[96,2560]{1,0:T(8,128)(2,1)S(1)}, u32[]{:S(2)}, u32[]{:S(2)}) %collective-permute-start.24) | collective-permute-done | bytes 491552 | tf_op jit(solution)/shard_map/ppermute | solution.py:45
  93.5 7.8 %all-to-all-start.9 = ((bf16[4,96,640]{2,1,0:T(8,128)(2,1)}), bf16[4,96,640]{2,1,0:T(8,128)(2,1)}, u32[]{:S(2)}, u32[]{:S(2)}) async-start(bf16[4,96,640]{2,1,0:T(8,128)(2,1)} %cut_heads.7), calls=%async_computation.9 | async-start | bytes 983040 | tf_op jit(solution)/shard_map/all_to_all | solution.py:461
  101.4 5.1 %collective-permute-start.7 = (bf16[96,2560]{1,0:T(8,128)(2,1)S(1)}, bf16[96,2560]{1,0:T(8,128)(2,1)S(1)}, u32[]{:S(2)}, u32[]{:S(2)}) collective-permute-start(bf16[96,2560]{1,0:T(8,128)(2,1)S(1)} %copy-done.40), channel_id=1, source_target_pairs={{0,1},{1,2},{2,3},{4,5},{5,6},{6,7},{8,9},{9,10},{10,11},{12,13},{... | collective-permute-start | bytes 1474568 | tf_op jit(solution)/shard_map/ppermute | solution.py:45
  107.8 5.3 %collective-permute-start.26 = (bf16[96,2560]{1,0:T(8,128)(2,1)}, bf16[96,2560]{1,0:T(8,128)(2,1)}, u32[]{:S(2)}, u32[]{:S(2)}) collective-permute-start(bf16[96,2560]{1,0:T(8,128)(2,1)} %copy-done.42), channel_id=1, source_target_pairs={{0,1},{1,2},{2,3},{4,5},{5,6},{6,7},{8,9},{9,10},{10,11},{12,13},{... | collective-permute-start | bytes 1474568 | tf_op jit(solution)/shard_map/ppermute | solution.py:45
  114.4 3.4 partial_products.6
  117.9 3.3 collective-permute-done.7.right_ref
  121.2 2.5 collective-permute-done.8.left_ref
  125.6 5.3 %collective-permute-start.9 = (bf16[96,2560]{1,0:T(8,128)(2,1)S(1)}, bf16[96,2560]{1,0:T(8,128)(2,1)S(1)}, u32[]{:S(2)}, u32[]{:S(2)}) collective-permute-start(bf16[96,2560]{1,0:T(8,128)(2,1)S(1)} %unit_gradient.4.refs_0_), channel_id=1, source_target_pairs={{0,1},{1,2},{2,3},{4,5},{5,6},{6,7},{8,9},{9,10},{10,11},{12,13},{... | collective-permute-start | bytes 1474568 | tf_op jit(solution)/shard_map/ppermute | solution.py:45
  131.0 3.5 partial_products.7
  134.6 1.5 copy-done.5
  136.1 1.5 copy-done.10
  137.7 1.5 copy-done.13
  139.2 2.4 unit_gradient.6.refs_7_
  142.9 5.8 %collective-permute-start.28 = (bf16[96,2560]{1,0:T(8,128)(2,1)}, bf16[96,2560]{1,0:T(8,128)(2,1)}, u32[]{:S(2)}, u32[]{:S(2)}) collective-permute-start(bf16[96,2560]{1,0:T(8,128)(2,1)} %unit_gradient.6.refs_7_), channel_id=1, source_target_pairs={{0,1},{1,2},{2,3},{4,5},{5,6},{6,7},{8,9},{9,10},{10,11},{12,13},{... | collective-permute-start | bytes 1474568 | tf_op jit(solution)/shard_map/ppermute | solution.py:45
  148.8 1.7 copy-done.1
  151.8 3.3 collective-permute-start.11
  156.4 3.5 collective-permute-done.28.right_ref.refs_8_
  159.9 2.5 next_payload.17
  162.4 4.4 %collective-permute-start.30 = (bf16[96,2560]{1,0:T(8,128)(2,1)S(1)}, bf16[96,2560]{1,0:T(8,128)(2,1)S(1)}, u32[]{:S(2)}, u32[]{:S(2)}) collective-permute-start(bf16[96,2560]{1,0:T(8,128)(2,1)S(1)} %get-tuple-element.287), channel_id=1, source_target_pairs={{0,1},{1,2},{2,3},{4,5},{5,6},{6,7},{8,9},{9,10},{10,11},{12,13},{... | collective-permute-start | bytes 1474568 | tf_op jit(solution)/shard_map/ppermute | solution.py:45
  168.1 2.3 collective-permute-done.11.right_ref.refs_2_
  171.2 4.4 %collective-permute-start.13 = (bf16[96,2560]{1,0:T(8,128)(2,1)S(1)}, bf16[96,2560]{1,0:T(8,128)(2,1)S(1)}, u32[]{:S(2)}, u32[]{:S(2)}) collective-permute-start(bf16[96,2560]{1,0:T(8,128)(2,1)S(1)} %get-tuple-element.272), channel_id=1, source_target_pairs={{0,1},{1,2},{2,3},{4,5},{5,6},{6,7},{8,9},{9,10},{10,11},{12,13},{... | collective-permute-start | bytes 1474568 | tf_op jit(solution)/shard_map/ppermute | solution.py:45
  177.0 3.9 %collective-permute-done.30.right_ref.refs_9_ = bf16[96,2560]{1,0:T(8,128)(2,1)S(1)} collective-permute-done((bf16[96,2560]{1,0:T(8,128)(2,1)S(1)}, bf16[96,2560]{1,0:T(8,128)(2,1)S(1)}, u32[]{:S(2)}, u32[]{:S(2)}) %collective-permute-start.30) | collective-permute-done | bytes 491552 | tf_op jit(solution)/shard_map/ppermute | solution.py:45
  180.9 1.8 collective-permute-done.31.left_ref.refs_12_
  183.6 3.4 collective-permute-start.32
  190.3 3.0 collective-permute-done.15
  194.8 4.8 %collective-permute-start.16 = (bf16[96,2560]{1,0:T(8,128)(2,1)S(1)}, bf16[96,2560]{1,0:T(8,128)(2,1)S(1)}, u32[]{:S(2)}, u32[]{:S(2)}) collective-permute-start(bf16[96,2560]{1,0:T(8,128)(2,1)S(1)} %get-tuple-element.275), channel_id=1, source_target_pairs={{0,1},{1,2},{2,3},{4,5},{5,6},{6,7},{8,9},{9,10},{10,11},{12,13},{... | collective-permute-start | bytes 1474568 | tf_op jit(solution)/shard_map/ppermute | solution.py:45
  202.2 1.9 collective-permute-start.36
  204.1 2.5 collective-permute-done.36
  208.6 4.6 %collective-permute-start.37 = (bf16[96,2560]{1,0:T(8,128)(2,1)S(1)}, bf16[96,2560]{1,0:T(8,128)(2,1)S(1)}, u32[]{:S(2)}, u32[]{:S(2)}) collective-permute-start(bf16[96,2560]{1,0:T(8,128)(2,1)S(1)} %get-tuple-element.298), channel_id=1, source_target_pairs={{0,1},{1,2},{2,3},{4,5},{5,6},{6,7},{8,9},{9,10},{10,11},{12,13},{... | collective-permute-start | bytes 1474568 | tf_op jit(solution)/shard_map/ppermute | solution.py:45
  217.2 6.0 %collective-permute-start.18 = (bf16[96,2560]{1,0:T(8,128)(2,1)}, bf16[96,2560]{1,0:T(8,128)(2,1)}, u32[]{:S(2)}, u32[]{:S(2)}) collective-permute-start(bf16[96,2560]{1,0:T(8,128)(2,1)} %unit_gradient.5.refs_0_), channel_id=1, source_target_pairs={{0,1},{1,2},{2,3},{4,5},{5,6},{6,7},{8,9},{9,10},{10,11},{12,13},{... | collective-permute-start | bytes 1474568 | tf_op jit(solution)/shard_map/ppermute | solution.py:45
  224.3 2.9 collective-permute-start.39
  232.6 5.4 %collective-permute-start.40 = (bf16[96,2560]{1,0:T(8,128)(2,1)}, bf16[96,2560]{1,0:T(8,128)(2,1)}, u32[]{:S(2)}, u32[]{:S(2)}) collective-permute-start(bf16[96,2560]{1,0:T(8,128)(2,1)} %unit_gradient.7.refs_7_), channel_id=1, source_target_pairs={{0,1},{1,2},{2,3},{4,5},{5,6},{6,7},{8,9},{9,10},{10,11},{12,13},{... | collective-permute-start | bytes 1474568 | tf_op jit(solution)/shard_map/ppermute | solution.py:45
  243.0 7.8 %weight_step.9 = (f32[640,2560]{1,0:T(8,128)}, f32[8,128]{1,0:T(8,128)S(1)}) custom-call(s32[4]{0:T(128)S(1)} %and_select_fusion.s, bf16[96,2560]{1,0:T(8,128)(2,1)S(1)} %unit_gradient.4.refs_0_, bf16[96,2560]{1,0:T(8,128)(2,1)S(1)} %collective-permute-done.9.right_ref.refs_1_, bf16[96,2560]{1,0:T(8,128)(2,1)S(1)} %collective-permute-done.11.right_ref.refs_2_, ...), custom_call_target="tpu_custom_call" | custom-call | flops 1509949440 | bytes 15925248 | tf_op jit(solution)/shard_map/weight_step/pallas_call | solution.py:16
  255.0 2.9 turned_heads.3
  257.8 5.4 %weight_step.10 = (f32[640,2560]{1,0:T(8,128)}, f32[8,128]{1,0:T(8,128)S(1)}) custom-call(s32[4]{0:T(128)S(1)} %and_select_fusion.s, bf16[96,2560]{1,0:T(8,128)(2,1)S(1)} %unit_gradient.4.refs_0_, bf16[96,2560]{1,0:T(8,128)(2,1)S(1)} %collective-permute-done.9.right_ref.refs_1_, ...), custom_call_target="tpu_custom_call", output_to_operand_aliasing={{0}: (17, {})} | custom-call | flops 1006632960 | bytes 10616832 | tf_op jit(solution)/shard_map/weight_step/pallas_call | solution.py:16
  277.4 9.1 %grad_rows.7 = (bf16[4,192,640]{2,1,0:T(8,128)(2,1)}, f32[8,128]{1,0:T(8,128)}) custom-call(s32[4]{0:T(128)S(1)} %and_select_fusion.s, bf16[96,2560]{1,0:T(8,128)(2,1)S(1)} %unit_gradient.4.refs_0_, bf16[96,2560]{1,0:T(8,128)(2,1)S(1)} %collective-permute-done.9.right_ref.refs_1_, bf16[96,2560]{1,0:T(8,128)(2,1)S(1)} %copy-done.18, ...), custom_call_target="tpu_custom_call" | custom-call | flops 2516582400 | bytes 10158080 | tf_op jit(solution)/shard_map/grad_rows/pallas_call | solution.py:16
  287.1 2.5 collective-permute-done.45.refs_13_
  289.6 9.6 %weight_step.11 = bf16[640,2560]{1,0:T(8,128)(2,1)} custom-call(s32[4]{0:T(128)S(1)} %and_select_fusion.s, bf16[96,2560]{1,0:T(8,128)(2,1)} %unit_gradient.5.refs_0_, bf16[96,2560]{1,0:T(8,128)(2,1)} %collective-permute-done.18.refs_1_, bf16[96,2560]{1,0:T(8,128)(2,1)} %collective-permute-done.19.right_ref.refs_2_, ...), custom_call_target="tpu_custom_call" | custom-call | flops 2516582400 | bytes 26542080 | tf_op jit(solution)/shard_map/weight_step/pallas_call | solution.py:16
  299.2 67.0 %conditional.1 = (bf16[640,2560]{1,0:T(8,128)(2,1)}, bf16[1,384,2560]{2,1,0:T(8,128)(2,1)S(1)}, f32[1,640,2560]{2,1,0:T(8,128)}) conditional(s32[]{:T(128)} %clamp.3, (bf16[640,2560]{1,0:T(8,128)(2,1)}, bf16[4,192,640]{2,1,0:T(8,128)(2,1)}, s32[4]{0:T(128)S(1)}, bf16[96,2560]{1,0:T(8,128)(2,1)}, bf16[96,2560]{1,0:T(8,128)(2,1)}, ...), branch_computations={%region_1.2_spmd, %region_2.3_spmd, %region_3.4_spmd} | conditional | flops 5033164800 | bytes 59637888 | solution.py:634
  299.3 8.7 %all-to-all-start.2 = ((bf16[4,192,640]{2,1,0:T(8,128)(2,1)}), bf16[4,192,640]{2,1,0:T(8,128)(2,1)S(1)}, u32[]{:S(2)}, u32[]{:S(2)}) async-start(bf16[4,192,640]{2,1,0:T(8,128)(2,1)} %get-tuple-element.152), calls=%async_computation.2 | async-start | bytes 1966080 | tf_op jit(solution)/shard_map/cond/branch_1_fun/all_to_all | solution.py:461
  308.1 9.4 %grad_rows.5 = (bf16[4,192,640]{2,1,0:T(8,128)(2,1)}, f32[8,128]{1,0:T(8,128)S(1)}) custom-call(s32[4]{0:T(128)S(1)} %get-tuple-element.153.s, bf16[96,2560]{1,0:T(8,128)(2,1)} %get-tuple-element.154.refs_0_, bf16[96,2560]{1,0:T(8,128)(2,1)} %get-tuple-element.155.refs_1_, bf16[96,2560]{1,0:T(8,128)(2,1)} %get-tuple-element.156.refs_2_, ...), custom_call_target="tpu_custom_call" | custom-call | flops 2516582400 | bytes 10158080 | tf_op jit(solution)/shard_map/cond/branch_1_fun/grad_rows/pallas_call | solution.py:16
  317.5 7.8 %all-to-all-done.2.refs_0_ = bf16[4,192,640]{2,1,0:T(8,128)(2,1)S(1)} async-done(((bf16[4,192,640]{2,1,0:T(8,128)(2,1)}), bf16[4,192,640]{2,1,0:T(8,128)(2,1)S(1)}, u32[]{:S(2)}, u32[]{:S(2)}) %all-to-all-start.2) | async-done | bytes 983072 | tf_op jit(solution)/shard_map/cond/branch_1_fun/all_to_all | solution.py:461
  325.3 3.5 all-to-all-start.3
  328.8 12.3 %weight_step.7 = f32[640,2560]{1,0:T(8,128)} custom-call(s32[4]{0:T(128)S(1)} %get-tuple-element.153.s, bf16[96,2560]{1,0:T(8,128)(2,1)} %get-tuple-element.154.refs_0_, bf16[96,2560]{1,0:T(8,128)(2,1)} %get-tuple-element.155.refs_1_, bf16[96,2560]{1,0:T(8,128)(2,1)} %get-tuple-element.156.refs_2_, bf16[96,2560]{1,0:T(8,128)(2,1)} %get-tuple-element.157.refs_3_, ...), custom_call_target="tpu_custom_call" | custom-call | flops 2516582400 | bytes 26542080 | tf_op jit(solution)/shard_map/cond/branch_1_fun/weight_step/pallas_call | solution.py:16
  341.1 8.3 %all-to-all-done.3.refs_1_ = bf16[4,192,640]{2,1,0:T(8,128)(2,1)S(1)} async-done(((bf16[4,192,640]{2,1,0:T(8,128)(2,1)}), bf16[4,192,640]{2,1,0:T(8,128)(2,1)S(1)}, u32[]{:S(2)}, u32[]{:S(2)}) %all-to-all-start.3) | async-done | bytes 983072 | tf_op jit(solution)/shard_map/cond/branch_1_fun/all_to_all | solution.py:461
  349.6 16.6 %collective-permute-done.1 = bf16[640,2560]{1,0:T(8,128)(2,1)} collective-permute-done((bf16[640,2560]{1,0:T(8,128)(2,1)}, bf16[640,2560]{1,0:T(8,128)(2,1)}, u32[]{:S(2)}, u32[]{:S(2)}) %collective-permute-start.1) | collective-permute-done | bytes 3276832 | tf_op jit(solution)/shard_map/cond/branch_1_fun/ppermute | solution.py:466
  366.2 5.1 %widened.1 = f32[640,2560]{1,0:T(8,128)} custom-call(bf16[640,2560]{1,0:T(8,128)(2,1)} %get-tuple-element.308.value_ref), custom_call_target="tpu_custom_call" | custom-call | bytes 9830400 | tf_op jit(solution)/shard_map/widened/pallas_call | solution.py:16
  (176 shorter events, 64.5 us)
Async XLA Ops:
  2.4 20.1 %all-to-all-start.6 = ((bf16[4,96,640]{2,1,0:T(8,128)(2,1)}), bf16[4,96,640]{2,1,0:T(8,128)(2,1)S(1)}, u32[]{:S(2)}, u32[]{:S(2)}) async-start(bf16[4,96,640]{2,1,0:T(8,128)(2,1)} %cut_heads.4), calls=%async_computation.6 | async-start | bytes 983040 | tf_op jit(solution)/shard_map/all_to_all | solution.py:461
  22.5 21.2 %copy-start.30 = (bf16[4,96,640]{2,1,0:T(8,128)(2,1)}, bf16[4,96,640]{2,1,0:T(8,128)(2,1)S(1)}, u32[]{:S(2)}) copy-start(bf16[4,96,640]{2,1,0:T(8,128)(2,1)S(1)} %all-to-all-done.6.mine_ref.refs_0_) | copy-start | bytes 1474564
  22.5 16.7 %all-to-all-start.7 = ((bf16[4,96,640]{2,1,0:T(8,128)(2,1)}), bf16[4,96,640]{2,1,0:T(8,128)(2,1)S(1)}, u32[]{:S(2)}, u32[]{:S(2)}) async-start(bf16[4,96,640]{2,1,0:T(8,128)(2,1)} %cut_heads.5), calls=%async_computation.7 | async-start | bytes 983040 | tf_op jit(solution)/shard_map/all_to_all | solution.py:461
  30.2 14.8 %collective-permute-start.3 = (bf16[96,2560]{1,0:T(8,128)(2,1)}, bf16[96,2560]{1,0:T(8,128)(2,1)S(1)}, u32[]{:S(2)}, u32[]{:S(2)}) collective-permute-start(bf16[96,2560]{1,0:T(8,128)(2,1)} %get-tuple-element.257), channel_id=1, source_target_pairs={{0,1},{4,5},{8,9},{12,13},{16,17},{20,21},{24,25},{28,29}} | collective-permute-start | bytes 1474568 | tf_op jit(solution)/shard_map/ppermute | solution.py:45
  34.1 10.9 %collective-permute-start.4 = (bf16[96,2560]{1,0:T(8,128)(2,1)}, bf16[96,2560]{1,0:T(8,128)(2,1)}, u32[]{:S(2)}, u32[]{:S(2)}) collective-permute-start(bf16[96,2560]{1,0:T(8,128)(2,1)} %get-tuple-element.258), channel_id=1, source_target_pairs={{3,2},{7,6},{11,10},{15,14},{19,18},{23,22},{27,26},{31,30}} | collective-permute-start | bytes 1474568 | tf_op jit(solution)/shard_map/ppermute | solution.py:45
  47.5 15.5 %collective-permute-start.5 = (bf16[96,2560]{1,0:T(8,128)(2,1)}, bf16[96,2560]{1,0:T(8,128)(2,1)S(1)}, u32[]{:S(2)}, u32[]{:S(2)}) collective-permute-start(bf16[96,2560]{1,0:T(8,128)(2,1)} %get-tuple-element.263), channel_id=1, source_target_pairs={{0,1},{1,2},{4,5},{5,6},{8,9},{9,10},{12,13},{13,14},{16,17},{17,1... | collective-permute-start | bytes 1474568 | tf_op jit(solution)/shard_map/ppermute | solution.py:45
  51.0 11.9 %collective-permute-start.6 = (bf16[96,2560]{1,0:T(8,128)(2,1)}, bf16[96,2560]{1,0:T(8,128)(2,1)}, u32[]{:S(2)}, u32[]{:S(2)}) collective-permute-start(bf16[96,2560]{1,0:T(8,128)(2,1)} %get-tuple-element.264), channel_id=1, source_target_pairs={{2,1},{3,2},{6,5},{7,6},{10,9},{11,10},{14,13},{15,14},{18,17},{19... | collective-permute-start | bytes 1474568 | tf_op jit(solution)/shard_map/ppermute | solution.py:45
  52.5 22.0 %collective-permute-start.22 = (bf16[96,2560]{1,0:T(8,128)(2,1)}, bf16[96,2560]{1,0:T(8,128)(2,1)S(1)}, u32[]{:S(2)}, u32[]{:S(2)}) collective-permute-start(bf16[96,2560]{1,0:T(8,128)(2,1)} %get-tuple-element.277), channel_id=1, source_target_pairs={{0,1},{4,5},{8,9},{12,13},{16,17},{20,21},{24,25},{28,29}} | collective-permute-start | bytes 1474568 | tf_op jit(solution)/shard_map/ppermute | solution.py:45
  57.1 17.4 %collective-permute-start.23 = (bf16[96,2560]{1,0:T(8,128)(2,1)}, bf16[96,2560]{1,0:T(8,128)(2,1)S(1)}, u32[]{:S(2)}, u32[]{:S(2)}) collective-permute-start(bf16[96,2560]{1,0:T(8,128)(2,1)} %get-tuple-element.278), channel_id=1, source_target_pairs={{3,2},{7,6},{11,10},{15,14},{19,18},{23,22},{27,26},{31,30}} | collective-permute-start | bytes 1474568 | tf_op jit(solution)/shard_map/ppermute | solution.py:45
  67.2 26.4 %all-to-all-start.8 = ((bf16[4,96,640]{2,1,0:T(8,128)(2,1)}), bf16[4,96,640]{2,1,0:T(8,128)(2,1)S(1)}, u32[]{:S(2)}, u32[]{:S(2)}) async-start(bf16[4,96,640]{2,1,0:T(8,128)(2,1)} %cut_heads.6), calls=%async_computation.8 | async-start | bytes 983040 | tf_op jit(solution)/shard_map/all_to_all | solution.py:461
  77.3 12.9 %collective-permute-start.24 = (bf16[96,2560]{1,0:T(8,128)(2,1)S(1)}, bf16[96,2560]{1,0:T(8,128)(2,1)S(1)}, u32[]{:S(2)}, u32[]{:S(2)}) collective-permute-start(bf16[96,2560]{1,0:T(8,128)(2,1)S(1)} %get-tuple-element.280), channel_id=1, source_target_pairs={{0,1},{1,2},{4,5},{5,6},{8,9},{9,10},{12,13},{13,14},{16,17},{17,1... | collective-permute-start | bytes 1474568 | tf_op jit(solution)/shard_map/ppermute | solution.py:45
  81.4 20.0 %copy-start.40 = (bf16[96,2560]{1,0:T(8,128)(2,1)S(1)}, bf16[96,2560]{1,0:T(8,128)(2,1)}, u32[]{:S(2)}) copy-start(bf16[96,2560]{1,0:T(8,128)(2,1)} %copy-done.39) | copy-start | bytes 1474564
  81.4 25.0 %copy-start.38 = (bf16[96,2560]{1,0:T(8,128)(2,1)S(1)}, bf16[96,2560]{1,0:T(8,128)(2,1)}, u32[]{:S(2)}) copy-start(bf16[96,2560]{1,0:T(8,128)(2,1)} %copy-done.37) | copy-start | bytes 1474564
  81.4 33.0 %copy-start.44 = (f32[2560]{0:T(1024)S(1)}, f32[2560]{0:T(1024)}, u32[]{:S(2)}) copy-start(f32[2560]{0:T(1024)} %param.19) | copy-start | bytes 30724
  81.5 8.8 %collective-permute-start.25 = (bf16[96,2560]{1,0:T(8,128)(2,1)S(1)}, bf16[96,2560]{1,0:T(8,128)(2,1)S(1)}, u32[]{:S(2)}, u32[]{:S(2)}) collective-permute-start(bf16[96,2560]{1,0:T(8,128)(2,1)S(1)} %get-tuple-element.281), channel_id=1, source_target_pairs={{2,1},{3,2},{6,5},{7,6},{10,9},{11,10},{14,13},{15,14},{18,17},{19... | collective-permute-start | bytes 1474568 | tf_op jit(solution)/shard_map/ppermute | solution.py:45
  93.5 30.1 %copy-start.34 = (bf16[4,96,640]{2,1,0:T(8,128)(2,1)}, bf16[4,96,640]{2,1,0:T(8,128)(2,1)S(1)}, u32[]{:S(2)}) copy-start(bf16[4,96,640]{2,1,0:T(8,128)(2,1)S(1)} %all-to-all-done.8.mine_ref.refs_0_) | copy-start | bytes 1474564
  93.5 37.5 %all-to-all-start.9 = ((bf16[4,96,640]{2,1,0:T(8,128)(2,1)}), bf16[4,96,640]{2,1,0:T(8,128)(2,1)}, u32[]{:S(2)}, u32[]{:S(2)}) async-start(bf16[4,96,640]{2,1,0:T(8,128)(2,1)} %cut_heads.7), calls=%async_computation.9 | async-start | bytes 983040 | tf_op jit(solution)/shard_map/all_to_all | solution.py:461
  101.4 22.3 %copy-start.9 = (bf16[1,384,2560]{2,1,0:T(8,128)(2,1)S(1)}, bf16[1,384,2560]{2,1,0:T(8,128)(2,1)}, u32[]{:S(2)}) copy-start(bf16[1,384,2560]{2,1,0:T(8,128)(2,1)} %param.17) | copy-start | bytes 5898244
  101.4 22.3 %copy-start.12 = (bf16[1,384,2560]{2,1,0:T(8,128)(2,1)S(1)}, bf16[1,384,2560]{2,1,0:T(8,128)(2,1)}, u32[]{:S(2)}) copy-start(bf16[1,384,2560]{2,1,0:T(8,128)(2,1)} %param.18) | copy-start | bytes 5898244
  101.4 19.8 %collective-permute-start.7 = (bf16[96,2560]{1,0:T(8,128)(2,1)S(1)}, bf16[96,2560]{1,0:T(8,128)(2,1)S(1)}, u32[]{:S(2)}, u32[]{:S(2)}) collective-permute-start(bf16[96,2560]{1,0:T(8,128)(2,1)S(1)} %copy-done.40), channel_id=1, source_target_pairs={{0,1},{1,2},{2,3},{4,5},{5,6},{6,7},{8,9},{9,10},{10,11},{12,13},{... | collective-permute-start | bytes 1474568 | tf_op jit(solution)/shard_map/ppermute | solution.py:45
  106.5 17.2 %collective-permute-start.8 = (bf16[96,2560]{1,0:T(8,128)(2,1)S(1)}, bf16[96,2560]{1,0:T(8,128)(2,1)S(1)}, u32[]{:S(2)}, u32[]{:S(2)}) collective-permute-start(bf16[96,2560]{1,0:T(8,128)(2,1)S(1)} %copy-done.38), channel_id=1, source_target_pairs={{1,0},{2,1},{3,2},{5,4},{6,5},{7,6},{9,8},{10,9},{11,10},{13,12},{... | collective-permute-start | bytes 1474568 | tf_op jit(solution)/shard_map/ppermute | solution.py:45
  107.8 26.8 %collective-permute-start.26 = (bf16[96,2560]{1,0:T(8,128)(2,1)}, bf16[96,2560]{1,0:T(8,128)(2,1)}, u32[]{:S(2)}, u32[]{:S(2)}) collective-permute-start(bf16[96,2560]{1,0:T(8,128)(2,1)} %copy-done.42), channel_id=1, source_target_pairs={{0,1},{1,2},{2,3},{4,5},{5,6},{6,7},{8,9},{9,10},{10,11},{12,13},{... | collective-permute-start | bytes 1474568 | tf_op jit(solution)/shard_map/ppermute | solution.py:45
  113.1 21.4 %collective-permute-start.27 = (bf16[96,2560]{1,0:T(8,128)(2,1)}, bf16[96,2560]{1,0:T(8,128)(2,1)}, u32[]{:S(2)}, u32[]{:S(2)}) collective-permute-start(bf16[96,2560]{1,0:T(8,128)(2,1)} %copy-done.41), channel_id=1, source_target_pairs={{1,0},{2,1},{3,2},{5,4},{6,5},{7,6},{9,8},{10,9},{11,10},{13,12},{... | collective-permute-start | bytes 1474568 | tf_op jit(solution)/shard_map/ppermute | solution.py:45
  124.3 24.5 %collective-permute-start.10 = (bf16[96,2560]{1,0:T(8,128)(2,1)S(1)}, bf16[96,2560]{1,0:T(8,128)(2,1)S(1)}, u32[]{:S(2)}, u32[]{:S(2)}) collective-permute-start(bf16[96,2560]{1,0:T(8,128)(2,1)S(1)} %unit_gradient.4.refs_0_), channel_id=1, source_target_pairs={{1,0},{2,1},{3,2},{5,4},{6,5},{7,6},{9,8},{10,9},{11,10},{13,12},{... | collective-permute-start | bytes 1474568 | tf_op jit(solution)/shard_map/ppermute | solution.py:45
  125.6 23.2 %collective-permute-start.9 = (bf16[96,2560]{1,0:T(8,128)(2,1)S(1)}, bf16[96,2560]{1,0:T(8,128)(2,1)S(1)}, u32[]{:S(2)}, u32[]{:S(2)}) collective-permute-start(bf16[96,2560]{1,0:T(8,128)(2,1)S(1)} %unit_gradient.4.refs_0_), channel_id=1, source_target_pairs={{0,1},{1,2},{2,3},{4,5},{5,6},{6,7},{8,9},{9,10},{10,11},{12,13},{... | collective-permute-start | bytes 1474568 | tf_op jit(solution)/shard_map/ppermute | solution.py:45
  141.6 14.8 %collective-permute-start.29 = (bf16[96,2560]{1,0:T(8,128)(2,1)}, bf16[96,2560]{1,0:T(8,128)(2,1)}, u32[]{:S(2)}, u32[]{:S(2)}) collective-permute-start(bf16[96,2560]{1,0:T(8,128)(2,1)} %unit_gradient.6.refs_7_), channel_id=1, source_target_pairs={{1,0},{2,1},{3,2},{5,4},{6,5},{7,6},{9,8},{10,9},{11,10},{13,12},{... | collective-permute-start | bytes 1474568 | tf_op jit(solution)/shard_map/ppermute | solution.py:45
  142.9 17.0 %collective-permute-start.28 = (bf16[96,2560]{1,0:T(8,128)(2,1)}, bf16[96,2560]{1,0:T(8,128)(2,1)}, u32[]{:S(2)}, u32[]{:S(2)}) collective-permute-start(bf16[96,2560]{1,0:T(8,128)(2,1)} %unit_gradient.6.refs_7_), channel_id=1, source_target_pairs={{0,1},{1,2},{2,3},{4,5},{5,6},{6,7},{8,9},{9,10},{10,11},{12,13},{... | collective-permute-start | bytes 1474568 | tf_op jit(solution)/shard_map/ppermute | solution.py:45
  151.8 18.6 %copy-start.2 = (bf16[4,96,2560]{2,1,0:T(8,128)(2,1)S(1)}, bf16[4,96,2560]{2,1,0:T(8,128)(2,1)}, u32[]{:S(2)}) copy-start(bf16[4,96,2560]{2,1,0:T(8,128)(2,1)} %copy-done) | copy-start | bytes 5898244
  151.8 18.6 %collective-permute-start.11 = (bf16[96,2560]{1,0:T(8,128)(2,1)S(1)}, bf16[96,2560]{1,0:T(8,128)(2,1)S(1)}, u32[]{:S(2)}, u32[]{:S(2)}) collective-permute-start(bf16[96,2560]{1,0:T(8,128)(2,1)S(1)} %get-tuple-element.270), channel_id=1, source_target_pairs={{0,1},{1,2},{2,3},{4,5},{5,6},{6,7},{8,9},{9,10},{10,11},{12,13},{... | collective-permute-start | bytes 1474568 | tf_op jit(solution)/shard_map/ppermute | solution.py:45
  155.1 15.3 %collective-permute-start.12 = (bf16[96,2560]{1,0:T(8,128)(2,1)S(1)}, bf16[96,2560]{1,0:T(8,128)(2,1)S(1)}, u32[]{:S(2)}, u32[]{:S(2)}) collective-permute-start(bf16[96,2560]{1,0:T(8,128)(2,1)S(1)} %get-tuple-element.271), channel_id=1, source_target_pairs={{1,0},{2,1},{3,2},{5,4},{6,5},{7,6},{9,8},{10,9},{11,10},{13,12},{... | collective-permute-start | bytes 1474568 | tf_op jit(solution)/shard_map/ppermute | solution.py:45
  162.4 18.5 %collective-permute-start.30 = (bf16[96,2560]{1,0:T(8,128)(2,1)S(1)}, bf16[96,2560]{1,0:T(8,128)(2,1)S(1)}, u32[]{:S(2)}, u32[]{:S(2)}) collective-permute-start(bf16[96,2560]{1,0:T(8,128)(2,1)S(1)} %get-tuple-element.287), channel_id=1, source_target_pairs={{0,1},{1,2},{2,3},{4,5},{5,6},{6,7},{8,9},{9,10},{10,11},{12,13},{... | collective-permute-start | bytes 1474568 | tf_op jit(solution)/shard_map/ppermute | solution.py:45
  166.8 15.9 %collective-permute-start.31 = (bf16[96,2560]{1,0:T(8,128)(2,1)S(1)}, bf16[96,2560]{1,0:T(8,128)(2,1)S(1)}, u32[]{:S(2)}, u32[]{:S(2)}) collective-permute-start(bf16[96,2560]{1,0:T(8,128)(2,1)S(1)} %get-tuple-element.288), channel_id=1, source_target_pairs={{1,0},{2,1},{3,2},{5,4},{6,5},{7,6},{9,8},{10,9},{11,10},{13,12},{... | collective-permute-start | bytes 1474568 | tf_op jit(solution)/shard_map/ppermute | solution.py:45
  170.3 87.5 %copy-start.17 = (bf16[96,2560]{1,0:T(8,128)(2,1)}, bf16[96,2560]{1,0:T(8,128)(2,1)S(1)}, u32[]{:S(2)}) copy-start(bf16[96,2560]{1,0:T(8,128)(2,1)S(1)} %collective-permute-done.11.right_ref.refs_2_) | copy-start | bytes 1474564
  171.2 22.0 %collective-permute-start.13 = (bf16[96,2560]{1,0:T(8,128)(2,1)S(1)}, bf16[96,2560]{1,0:T(8,128)(2,1)S(1)}, u32[]{:S(2)}, u32[]{:S(2)}) collective-permute-start(bf16[96,2560]{1,0:T(8,128)(2,1)S(1)} %get-tuple-element.272), channel_id=1, source_target_pairs={{0,1},{1,2},{2,3},{4,5},{5,6},{6,7},{8,9},{9,10},{10,11},{12,13},{... | collective-permute-start | bytes 1474568 | tf_op jit(solution)/shard_map/ppermute | solution.py:45
  175.7 17.6 %collective-permute-start.14 = (bf16[96,2560]{1,0:T(8,128)(2,1)S(1)}, bf16[96,2560]{1,0:T(8,128)(2,1)S(1)}, u32[]{:S(2)}, u32[]{:S(2)}) collective-permute-start(bf16[96,2560]{1,0:T(8,128)(2,1)S(1)} %get-tuple-element.273), channel_id=1, source_target_pairs={{1,0},{2,1},{3,2},{5,4},{6,5},{7,6},{9,8},{10,9},{11,10},{13,12},{... | collective-permute-start | bytes 1474568 | tf_op jit(solution)/shard_map/ppermute | solution.py:45
  183.6 23.0 %collective-permute-start.32 = (bf16[96,2560]{1,0:T(8,128)(2,1)S(1)}, bf16[96,2560]{1,0:T(8,128)(2,1)S(1)}, u32[]{:S(2)}, u32[]{:S(2)}) collective-permute-start(bf16[96,2560]{1,0:T(8,128)(2,1)S(1)} %get-tuple-element.289), channel_id=1, source_target_pairs={{0,1},{1,2},{2,3},{4,5},{5,6},{6,7},{8,9},{9,10},{10,11},{12,13},{... | collective-permute-start | bytes 1474568 | tf_op jit(solution)/shard_map/ppermute | solution.py:45
  186.9 19.7 %collective-permute-start.33 = (bf16[96,2560]{1,0:T(8,128)(2,1)S(1)}, bf16[96,2560]{1,0:T(8,128)(2,1)S(1)}, u32[]{:S(2)}, u32[]{:S(2)}) collective-permute-start(bf16[96,2560]{1,0:T(8,128)(2,1)S(1)} %get-tuple-element.290), channel_id=1, source_target_pairs={{1,0},{2,1},{3,2},{5,4},{6,5},{7,6},{9,8},{10,9},{11,10},{13,12},{... | collective-permute-start | bytes 1474568 | tf_op jit(solution)/shard_map/ppermute | solution.py:45
  189.4 3.9 %collective-permute-start.15 = (f32[1]{0:T(128)}, f32[1]{0:T(128)}, u32[]{:S(2)}, u32[]{:S(2)}) collective-permute-start(f32[1]{0:T(128)} %add.41), channel_id=1, source_target_pairs={{0,4},{4,8},{8,12},{12,16},{16,20},{20,24},{24,28},{28,0},{1,5},{5... | collective-permute-start | bytes 20 | tf_op jit(solution)/shard_map/ppermute | solution.py:502
  193.3 64.5 %copy-start.23 = (bf16[96,2560]{1,0:T(8,128)(2,1)}, bf16[96,2560]{1,0:T(8,128)(2,1)S(1)}, u32[]{:S(2)}) copy-start(bf16[96,2560]{1,0:T(8,128)(2,1)S(1)} %collective-permute-done.13.right_ref.refs_3_) | copy-start | bytes 1474564
  194.8 19.7 %copy-start.11 = (bf16[1,384,2560]{2,1,0:T(8,128)(2,1)S(1)}, bf16[1,384,2560]{2,1,0:T(8,128)(2,1)}, u32[]{:S(2)}) copy-start(bf16[1,384,2560]{2,1,0:T(8,128)(2,1)} %param.17) | copy-start | bytes 5898244
  194.8 19.7 %copy-start.14 = (bf16[1,384,2560]{2,1,0:T(8,128)(2,1)S(1)}, bf16[1,384,2560]{2,1,0:T(8,128)(2,1)}, u32[]{:S(2)}) copy-start(bf16[1,384,2560]{2,1,0:T(8,128)(2,1)} %param.18) | copy-start | bytes 5898244
  194.8 19.7 %collective-permute-start.16 = (bf16[96,2560]{1,0:T(8,128)(2,1)S(1)}, bf16[96,2560]{1,0:T(8,128)(2,1)S(1)}, u32[]{:S(2)}, u32[]{:S(2)}) collective-permute-start(bf16[96,2560]{1,0:T(8,128)(2,1)S(1)} %get-tuple-element.275), channel_id=1, source_target_pairs={{0,1},{1,2},{2,3},{4,5},{5,6},{6,7},{8,9},{9,10},{10,11},{12,13},{... | collective-permute-start | bytes 1474568 | tf_op jit(solution)/shard_map/ppermute | solution.py:45
  199.7 14.8 %collective-permute-start.17 = (bf16[96,2560]{1,0:T(8,128)(2,1)S(1)}, bf16[96,2560]{1,0:T(8,128)(2,1)S(1)}, u32[]{:S(2)}, u32[]{:S(2)}) collective-permute-start(bf16[96,2560]{1,0:T(8,128)(2,1)S(1)} %get-tuple-element.276), channel_id=1, source_target_pairs={{1,0},{2,1},{3,2},{5,4},{6,5},{7,6},{9,8},{10,9},{11,10},{13,12},{... | collective-permute-start | bytes 1474568 | tf_op jit(solution)/shard_map/ppermute | solution.py:45
  202.2 4.4 %collective-permute-start.36 = (f32[1]{0:T(128)}, f32[1]{0:T(128)}, u32[]{:S(2)}, u32[]{:S(2)}) collective-permute-start(f32[1]{0:T(128)} %add.42), channel_id=1, source_target_pairs={{0,8},{4,12},{8,16},{12,20},{16,24},{20,28},{24,0},{28,4},{1,9},{5... | collective-permute-start | bytes 20 | tf_op jit(solution)/shard_map/ppermute | solution.py:502
  208.6 19.4 %collective-permute-start.37 = (bf16[96,2560]{1,0:T(8,128)(2,1)S(1)}, bf16[96,2560]{1,0:T(8,128)(2,1)S(1)}, u32[]{:S(2)}, u32[]{:S(2)}) collective-permute-start(bf16[96,2560]{1,0:T(8,128)(2,1)S(1)} %get-tuple-element.298), channel_id=1, source_target_pairs={{0,1},{1,2},{2,3},{4,5},{5,6},{6,7},{8,9},{9,10},{10,11},{12,13},{... | collective-permute-start | bytes 1474568 | tf_op jit(solution)/shard_map/ppermute | solution.py:45
  213.2 16.1 %collective-permute-start.38 = (bf16[96,2560]{1,0:T(8,128)(2,1)S(1)}, bf16[96,2560]{1,0:T(8,128)(2,1)S(1)}, u32[]{:S(2)}, u32[]{:S(2)}) collective-permute-start(bf16[96,2560]{1,0:T(8,128)(2,1)S(1)} %get-tuple-element.299), channel_id=1, source_target_pairs={{1,0},{2,1},{3,2},{5,4},{6,5},{7,6},{9,8},{10,9},{11,10},{13,12},{... | collective-permute-start | bytes 1474568 | tf_op jit(solution)/shard_map/ppermute | solution.py:45
  215.9 24.4 %collective-permute-start.20 = (bf16[96,2560]{1,0:T(8,128)(2,1)}, bf16[96,2560]{1,0:T(8,128)(2,1)}, u32[]{:S(2)}, u32[]{:S(2)}) collective-permute-start(bf16[96,2560]{1,0:T(8,128)(2,1)} %unit_gradient.5.refs_0_), channel_id=1, source_target_pairs={{1,0},{2,1},{3,2},{5,4},{6,5},{7,6},{9,8},{10,9},{11,10},{13,12},{... | collective-permute-start | bytes 1474568 | tf_op jit(solution)/shard_map/ppermute | solution.py:45
  217.2 24.4 %collective-permute-start.18 = (bf16[96,2560]{1,0:T(8,128)(2,1)}, bf16[96,2560]{1,0:T(8,128)(2,1)}, u32[]{:S(2)}, u32[]{:S(2)}) collective-permute-start(bf16[96,2560]{1,0:T(8,128)(2,1)} %unit_gradient.5.refs_0_), channel_id=1, source_target_pairs={{0,1},{1,2},{2,3},{4,5},{5,6},{6,7},{8,9},{9,10},{10,11},{12,13},{... | collective-permute-start | bytes 1474568 | tf_op jit(solution)/shard_map/ppermute | solution.py:45
  224.3 3.7 collective-permute-start.39
  231.3 19.5 %collective-permute-start.41 = (bf16[96,2560]{1,0:T(8,128)(2,1)}, bf16[96,2560]{1,0:T(8,128)(2,1)}, u32[]{:S(2)}, u32[]{:S(2)}) collective-permute-start(bf16[96,2560]{1,0:T(8,128)(2,1)} %unit_gradient.7.refs_7_), channel_id=1, source_target_pairs={{1,0},{2,1},{3,2},{5,4},{6,5},{7,6},{9,8},{10,9},{11,10},{13,12},{... | collective-permute-start | bytes 1474568 | tf_op jit(solution)/shard_map/ppermute | solution.py:45
  232.6 18.2 %collective-permute-start.40 = (bf16[96,2560]{1,0:T(8,128)(2,1)}, bf16[96,2560]{1,0:T(8,128)(2,1)}, u32[]{:S(2)}, u32[]{:S(2)}) collective-permute-start(bf16[96,2560]{1,0:T(8,128)(2,1)} %unit_gradient.7.refs_7_), channel_id=1, source_target_pairs={{0,1},{1,2},{2,3},{4,5},{5,6},{6,7},{8,9},{9,10},{10,11},{12,13},{... | collective-permute-start | bytes 1474568 | tf_op jit(solution)/shard_map/ppermute | solution.py:45
  240.2 23.0 %collective-permute-start.21 = (bf16[96,2560]{1,0:T(8,128)(2,1)}, bf16[96,2560]{1,0:T(8,128)(2,1)}, u32[]{:S(2)}, u32[]{:S(2)}) collective-permute-start(bf16[96,2560]{1,0:T(8,128)(2,1)} %collective-permute-done.20.refs_4_), channel_id=1, source_target_pairs={{1,0},{2,1},{5,4},{6,5},{9,8},{10,9},{13,12},{14,13},{17,16},{18,1... | collective-permute-start | bytes 1474568 | tf_op jit(solution)/shard_map/ppermute | solution.py:45
  241.5 21.7 %collective-permute-start.19 = (bf16[96,2560]{1,0:T(8,128)(2,1)}, bf16[96,2560]{1,0:T(8,128)(2,1)}, u32[]{:S(2)}, u32[]{:S(2)}) collective-permute-start(bf16[96,2560]{1,0:T(8,128)(2,1)} %collective-permute-done.18.refs_1_), channel_id=1, source_target_pairs={{1,2},{2,3},{5,6},{6,7},{9,10},{10,11},{13,14},{14,15},{17,18},{18... | collective-permute-start | bytes 1474568 | tf_op jit(solution)/shard_map/ppermute | solution.py:45
  252.2 15.2 %collective-permute-start.42 = (bf16[96,2560]{1,0:T(8,128)(2,1)S(1)}, bf16[96,2560]{1,0:T(8,128)(2,1)}, u32[]{:S(2)}, u32[]{:S(2)}) collective-permute-start(bf16[96,2560]{1,0:T(8,128)(2,1)S(1)} %get-tuple-element.302), channel_id=1, source_target_pairs={{1,2},{2,3},{5,6},{6,7},{9,10},{10,11},{13,14},{14,15},{17,18},{18... | collective-permute-start | bytes 1474568 | tf_op jit(solution)/shard_map/ppermute | solution.py:45
  253.7 15.8 %collective-permute-start.44 = (bf16[96,2560]{1,0:T(8,128)(2,1)S(1)}, bf16[96,2560]{1,0:T(8,128)(2,1)}, u32[]{:S(2)}, u32[]{:S(2)}) collective-permute-start(bf16[96,2560]{1,0:T(8,128)(2,1)S(1)} %get-tuple-element.303), channel_id=1, source_target_pairs={{1,0},{2,1},{5,4},{6,5},{9,8},{10,9},{13,12},{14,13},{17,16},{18,1... | collective-permute-start | bytes 1474568 | tf_op jit(solution)/shard_map/ppermute | solution.py:45
  257.8 17.5 %copy-start.20 = (bf16[96,2560]{1,0:T(8,128)(2,1)S(1)}, bf16[96,2560]{1,0:T(8,128)(2,1)}, u32[]{:S(2)}) copy-start(bf16[96,2560]{1,0:T(8,128)(2,1)} %copy-done.19) | copy-start | bytes 1474564
  257.8 17.5 %copy-start.26 = (bf16[96,2560]{1,0:T(8,128)(2,1)S(1)}, bf16[96,2560]{1,0:T(8,128)(2,1)}, u32[]{:S(2)}) copy-start(bf16[96,2560]{1,0:T(8,128)(2,1)} %copy-done.25) | copy-start | bytes 1474564
  264.6 22.5 %collective-permute-start.34 = (bf16[96,2560]{1,0:T(8,128)(2,1)S(1)}, bf16[96,2560]{1,0:T(8,128)(2,1)}, u32[]{:S(2)}, u32[]{:S(2)}) collective-permute-start(bf16[96,2560]{1,0:T(8,128)(2,1)S(1)} %get-tuple-element.295), channel_id=1, source_target_pairs={{2,3},{6,7},{10,11},{14,15},{18,19},{22,23},{26,27},{30,31}} | collective-permute-start | bytes 1474568 | tf_op jit(solution)/shard_map/ppermute | solution.py:45
  266.1 21.0 %collective-permute-start.35 = (bf16[96,2560]{1,0:T(8,128)(2,1)S(1)}, bf16[96,2560]{1,0:T(8,128)(2,1)}, u32[]{:S(2)}, u32[]{:S(2)}) collective-permute-start(bf16[96,2560]{1,0:T(8,128)(2,1)S(1)} %get-tuple-element.296), channel_id=1, source_target_pairs={{1,0},{5,4},{9,8},{13,12},{17,16},{21,20},{25,24},{29,28}} | collective-permute-start | bytes 1474568 | tf_op jit(solution)/shard_map/ppermute | solution.py:45
  267.4 19.7 %collective-permute-start.43 = (bf16[96,2560]{1,0:T(8,128)(2,1)}, bf16[96,2560]{1,0:T(8,128)(2,1)}, u32[]{:S(2)}, u32[]{:S(2)}) collective-permute-start(bf16[96,2560]{1,0:T(8,128)(2,1)} %collective-permute-done.42.refs_9_), channel_id=1, source_target_pairs={{2,3},{6,7},{10,11},{14,15},{18,19},{22,23},{26,27},{30,31}} | collective-permute-start | bytes 1474568 | tf_op jit(solution)/shard_map/ppermute | solution.py:45
  269.5 20.1 %collective-permute-start.45 = (bf16[96,2560]{1,0:T(8,128)(2,1)}, bf16[96,2560]{1,0:T(8,128)(2,1)}, u32[]{:S(2)}, u32[]{:S(2)}) collective-permute-start(bf16[96,2560]{1,0:T(8,128)(2,1)} %collective-permute-done.44.refs_12_), channel_id=1, source_target_pairs={{1,0},{5,4},{9,8},{13,12},{17,16},{21,20},{25,24},{29,28}} | collective-permute-start | bytes 1474568 | tf_op jit(solution)/shard_map/ppermute | solution.py:45
  299.3 66.9 %collective-permute-start.1 = (bf16[640,2560]{1,0:T(8,128)(2,1)}, bf16[640,2560]{1,0:T(8,128)(2,1)}, u32[]{:S(2)}, u32[]{:S(2)}) collective-permute-start(bf16[640,2560]{1,0:T(8,128)(2,1)} %get-tuple-element.151), channel_id=1, source_target_pairs={{0,8},{4,12},{8,16},{12,20},{16,24},{20,28},{24,0},{28,4},{1,9},{5... | collective-permute-start | bytes 9830408 | tf_op jit(solution)/shard_map/cond/branch_1_fun/ppermute | solution.py:466
  299.3 25.9 %all-to-all-start.2 = ((bf16[4,192,640]{2,1,0:T(8,128)(2,1)}), bf16[4,192,640]{2,1,0:T(8,128)(2,1)S(1)}, u32[]{:S(2)}, u32[]{:S(2)}) async-start(bf16[4,192,640]{2,1,0:T(8,128)(2,1)} %get-tuple-element.152), calls=%async_computation.2 | async-start | bytes 1966080 | tf_op jit(solution)/shard_map/cond/branch_1_fun/all_to_all | solution.py:461
  325.3 24.1 %all-to-all-start.3 = ((bf16[4,192,640]{2,1,0:T(8,128)(2,1)}), bf16[4,192,640]{2,1,0:T(8,128)(2,1)S(1)}, u32[]{:S(2)}, u32[]{:S(2)}) async-start(bf16[4,192,640]{2,1,0:T(8,128)(2,1)} %get-tuple-element.169), calls=%async_computation.3 | async-start | bytes 1966080 | tf_op jit(solution)/shard_map/cond/branch_1_fun/all_to_all | solution.py:461
  (32 other events, 210.7 us)

commit v8 on v6

--- a/solution.py
+++ b/solution.py
@@ -395,28 +395,34 @@
     )
 
 
-def joined_rows(blocks):
-    members, tokens, rows = blocks.shape
-    step = 96
-
-    def body(blocks_ref, out_ref):
-        for k in range(members):
-            out_ref[:, k * rows : (k + 1) * rows] = blocks_ref[k]
+def joined_rows(groups):
+    members, size, rows = groups[0].shape
+    tokens = size * len(groups)
+
+    def body(*refs):
+        out_ref = refs[-1]
+        for g, blocks_ref in enumerate(refs[:-1]):
+
+            @pl.when(pl.program_id(0) == g)
+            def _(blocks_ref=blocks_ref):
+                for k in range(members):
+                    out_ref[:, k * rows : (k + 1) * rows] = blocks_ref[k]
 
     return call(
         body,
         "joined_rows",
-        (tokens // step,),
-        [(blocks, (members, step, rows), lambda i: (0, i, 0))],
+        (len(groups),),
+        [(blocks, (members, size, rows), fixed(0, 0, 0)) for blocks in groups],
         [
             (
                 (tokens, members * rows),
-                blocks.dtype,
-                (step, members * rows),
+                groups[0].dtype,
+                (size, members * rows),
                 lambda i: (i, 0),
             )
         ],
         moved=4 * members * tokens * rows,
+        vmem=24,
     )[0]
 
 
@@ -443,15 +449,16 @@
     return lax.all_to_all(blocks, "fsdp", 0, 0, tiled=False)
 
 
-def tail(half, early, late, mine, kept, inbox, weights, order, bit_place):
+def tail(half, grads, late, mine, kept, inbox, weights, order, bit_place):
     length = lax.axis_size("rep")
     sent = lax.ppermute(
         half, "rep", [(i, (i + (1 << bit_place)) % length) for i in range(length)]
     )
-    grads, token = grad_rows(early + late, weights, order)
     back = swapped(grads)
+    late_grads, token = grad_rows(late, weights, order)
+    late_back = swapped(late_grads)
     new = weight_step(late, mine, order, kept, 0, None, inbox, new=True, token=token)[0]
-    return sent, joined_rows(back), new
+    return sent, joined_rows([back, late_back]), new
 
 
 def local(
@@ -472,16 +479,25 @@
     powers = jnp.left_shift(jnp.ones((levels,), jnp.int32), jnp.arange(levels, dtype=jnp.int32))
     level_index = jnp.sum(jnp.where(powers == offset[0], jnp.arange(levels, dtype=jnp.int32), 0))
 
-    def sent_weight(token):
+    arrived = [None] * levels
+    slots = [(0, 1), (1, 0), (1, 1)]
+
+    def levels_of(slot):
+        return [b for b in range(levels) if min(b, len(slots) - 1) == slot]
+
+    def sent_weight(token, b):
         half = 0.5 * push_weight + token[0, :1]
-        arrived = [
-            lax.ppermute(half, "rep", [(i, (i + (1 << b)) % replicas) for i in range(replicas)])
-            for b in range(levels)
-        ]
-        chosen = arrived[0]
-        for b in range(1, levels):
-            chosen = jnp.where(level_index == b, arrived[b], chosen)
-        return chosen
+        return lax.ppermute(
+            half, "rep", [(i, (i + (1 << b)) % replicas) for i in range(replicas)]
+        )
+
+    def pass_weight(e, t, q, token):
+        if e + 1 == rounds and (t, q) in slots:
+            for b in levels_of(slots.index((t, q))):
+                arrived[b] = sent_weight(token, b)
+
+    def seen(slot):
+        return jnp.broadcast_to(sum(arrived[b] for b in levels_of(slot))[None], (8, 128))
 
     order = jnp.mod(me - jnp.arange(members, dtype=jnp.int32), members)
     own = me[None]
@@ -529,26 +545,28 @@
     for q in range(count):
         parts[q], token, last, first = partial_products(mine[0][q], weights, True, token)
         hint[q] = (last, first)
-        if q == 0:
-            outbox_weight = sent_weight(token)
-            token = jnp.broadcast_to(outbox_weight[None], (8, 128))
     for e in range(rounds):
         moving = [None] * count
         for q in range(count):
             if e == 0:
                 moving[q] = hops(*hint[q], range(1), range(members - 1, members))
             else:
-                right, left, _ = next_payload(*before[q], parts[q], scalars(0), True)
+                right, left, token = next_payload(*before[q], parts[q], scalars(0), True)
+                pass_weight(e, 0, q, token)
                 moving[q] = hops(right, left, *everyone)
                 units[e - 1][q][1].append(moving[q][0])
                 units[e - 1][q][2].append(moving[q][1])
         for t in range(1, members - 1):
             for q in range(count):
+                order_token = token if (e, t, q) == (0, 1, 0) else None
+                if e + 1 == rounds and (t - 1, q) in slots:
+                    order_token = seen(slots.index((t - 1, q)))
                 right, left, token = next_payload(
-                    *moving[q], parts[q], scalars(t), False, token if (e, t, q) == (0, 1, 0) else None
+                    *moving[q], parts[q], scalars(t), False, order_token
                 )
-                if t == 1 and e + 1 < rounds:
-                    fetch(e + 1, [q], token)
+                if (t, q) == (1, count - 1) and e + 1 < rounds:
+                    fetch(e + 1, list(range(count)), token)
+                pass_weight(e, t, q, token)
                 if e == 0:
                     pairs = range(t + 1), range(members - 1 - t, members)
                 else:
@@ -590,14 +608,18 @@
             units[-1][q][1].append(before[q][0])
             units[-1][q][2].append(before[q][1])
     flat = [[u] + r + l for u, r, l in units[-1]]
+    grads, _ = grad_rows(early, weights, order)
     half = weight_step(flat, mine[-1], order, kept, 0, None, inbox_params[0])[0]
     new_weight = 0.5 * push_weight + inbox_weight
     branches = [
         partial(
-            tail, half, early, flat, mine[-1], kept, inbox_params[0], weights, order, place
+            tail, half, grads, flat, mine[-1], kept, inbox_params[0], weights, order, place
         )
         for place in range(levels)
     ]
+    outbox_weight = arrived[0]
+    for b in range(1, levels):
+        outbox_weight = jnp.where(level_index == b, arrived[b], outbox_weight)
     sent, grad_heads, new_params = lax.switch(level_index, branches)
     return (new_params[None], new_weight, widened(sent)[None], outbox_weight, grad_heads[None])
 

time: 364 us -> 388 us (1.066)
  waiting for transfers between devices: 101 us -> 112 us
  local copies, waits for them, and re-layouts: 8.03 us -> 17.7 us
  Pallas kernels: 102 us -> 109 us
  starting transfers between devices: 140 us -> 135 us
    unnamed x94 -> x84, local copies, waits for them, and re-layouts: 6.21 us -> 14.2 us
    ppermute x1, waiting for transfers between devices: 4.19 us -> 12.1 us  [tail(): lax.ppermute(half, 'rep', [(i, (i + (1 << bit_place)) % length) for i in...]
    pallas_call x32, Pallas kernels: 102 us -> 109 us  [call(): pl.pallas_call(body, name=name, out_shape=[jax.ShapeDtypeStruct(shape, ki...]
    ppermute x3, waiting for transfers between devices: 0.01 us -> 6.25 us  [sent_weight(): lax.ppermute(half, 'rep', [(i, (i + (1 << b)) % replicas) for i in range(...]
  transfers between devices with their start and end apart: 49 -> 49, of which waited for: 23 -> 18; matrix products, arithmetic and copies ran while one was open for 0% -> 1% of each run, Pallas kernels for 23% -> 22%
where the time goes in v8:
time: 388 us; the launch traced here: 385 us
  starting transfers between devices  135 us (35%)
  waiting for transfers between devices  112 us (29%)
  Pallas kernels  109 us (28%)
  local copies, waits for them, and re-layouts  17.7 us (5%)
  between operations  10.8 us (3%)
    pallas_call x32, Pallas kernels, call(): pl.pallas_call(body, name=name, out_shape=[jax.ShapeDtypeStruct(shape, ki...  109 us
    ppermute x40, starting transfers between devices, hop(): return lax.ppermute(value, 'fsdp', [(i, i + step) for i in pairs])  105 us
    ppermute x40, waiting for transfers between devices, hop(): return lax.ppermute(value, 'fsdp', [(i, i + step) for i in pairs])  62.6 us
    all_to_all x5, waiting for transfers between devices, swapped(): return lax.all_to_all(blocks, 'fsdp', 0, 0, tiled=False)  30.6 us
    all_to_all x5, starting transfers between devices, swapped(): return lax.all_to_all(blocks, 'fsdp', 0, 0, tiled=False)  22.2 us
    unnamed x84, local copies, waits for them, and re-layouts  14.2 us
    ppermute x1, waiting for transfers between devices, tail(): lax.ppermute(half, 'rep', [(i, (i + (1 << bit_place)) % length) for i in...  12.1 us
  transfers between devices with their start and end apart: 49, of which 18 were waited for; matrix products, arithmetic and copies ran while one was open for 1% of the time, Pallas kernels for 22%

profile of v8, /device:TPU:0, one launch (start us, length us, event | category | flops | bytes accessed | tf_op | source)
XLA Modules:
  0.0 385.2 jit_solution(2044271186670768081)
XLA Ops:
  0.6 1.8 cut_heads.3
  2.4 6.3 %all-to-all-start.6 = ((bf16[4,96,640]{2,1,0:T(8,128)(2,1)}), bf16[4,96,640]{2,1,0:T(8,128)(2,1)S(1)}, u32[]{:S(2)}, u32[]{:S(2)}) async-start(bf16[4,96,640]{2,1,0:T(8,128)(2,1)} %cut_heads.3), calls=%async_computation.6 | async-start | bytes 983040 | tf_op jit(solution)/shard_map/all_to_all | solution.py:449
  9.4 5.7 %scaled_weights.1 = (bf16[640,2560]{1,0:T(8,128)(2,1)}, f32[8,128]{1,0:T(8,128)}) custom-call(f32[640,2560]{1,0:T(8,128)} %bitcast.51, f32[1,1]{1,0:T(1,128)} %bitcast.36.one_ref), custom_call_target="tpu_custom_call" | custom-call | flops 3276800 | bytes 9830400 | tf_op jit(solution)/shard_map/scaled_weights/pallas_call | solution.py:16
  16.5 6.0 %all-to-all-done.6.mine_ref.refs_14_ = bf16[4,96,640]{2,1,0:T(8,128)(2,1)S(1)} async-done(((bf16[4,96,640]{2,1,0:T(8,128)(2,1)}), bf16[4,96,640]{2,1,0:T(8,128)(2,1)S(1)}, u32[]{:S(2)}, u32[]{:S(2)}) %all-to-all-start.6) | async-done | bytes 491552 | tf_op jit(solution)/shard_map/all_to_all | solution.py:449
  22.5 3.5 all-to-all-start.7
  26.0 3.5 partial_products.4
  32.4 6.9 %all-to-all-done.7.mine_ref.refs_15_ = bf16[4,96,640]{2,1,0:T(8,128)(2,1)S(1)} async-done(((bf16[4,96,640]{2,1,0:T(8,128)(2,1)}), bf16[4,96,640]{2,1,0:T(8,128)(2,1)S(1)}, u32[]{:S(2)}, u32[]{:S(2)}) %all-to-all-start.7) | async-done | bytes 491552 | tf_op jit(solution)/shard_map/all_to_all | solution.py:449
  39.3 4.4 %partial_products.5 = (bf16[4,96,2560]{2,1,0:T(8,128)(2,1)S(1)}, f32[8,128]{1,0:T(8,128)S(1)}, bf16[96,2560]{1,0:T(8,128)(2,1)}, bf16[96,2560]{1,0:T(8,128)(2,1)}) custom-call(bf16[4,96,640]{2,1,0:T(8,128)(2,1)S(1)} %all-to-all-done.7.mine_ref.refs_15_, bf16[640,2560]{1,0:T(8,128)(2,1)} %get-tuple-element.252.weights_ref.refs_14_, ...), custom_call_target="tpu_custom_call" | custom-call | flops 1258291200 | bytes 5734400 | tf_op jit(solution)/shard_map/partial_products/pallas_call | solution.py:16
  45.8 9.4 %collective-permute-done.9.right_ref = bf16[96,2560]{1,0:T(8,128)(2,1)S(1)} collective-permute-done((bf16[96,2560]{1,0:T(8,128)(2,1)}, bf16[96,2560]{1,0:T(8,128)(2,1)S(1)}, u32[]{:S(2)}, u32[]{:S(2)}) %collective-permute-start.9) | collective-permute-done | bytes 491552 | tf_op jit(solution)/shard_map/ppermute | solution.py:45
  58.6 4.2 %all-to-all-start.8 = ((bf16[4,192,640]{2,1,0:T(8,128)(2,1)}), bf16[4,192,640]{2,1,0:T(8,128)(2,1)}, u32[]{:S(2)}, u32[]{:S(2)}) async-start(bf16[4,192,640]{2,1,0:T(8,128)(2,1)} %cut_heads.5), calls=%async_computation.8 | async-start | bytes 1966080 | tf_op jit(solution)/shard_map/all_to_all | solution.py:449
  62.8 4.3 %collective-permute-start.3 = (bf16[96,2560]{1,0:T(8,128)(2,1)S(1)}, bf16[96,2560]{1,0:T(8,128)(2,1)S(1)}, u32[]{:S(2)}, u32[]{:S(2)}) collective-permute-start(bf16[96,2560]{1,0:T(8,128)(2,1)S(1)} %copy-done.37), channel_id=1, source_target_pairs={{0,1},{4,5},{8,9},{12,13},{16,17},{20,21},{24,25},{28,29}} | collective-permute-start | bytes 1474568 | tf_op jit(solution)/shard_map/ppermute | solution.py:45
  67.8 20.3 %collective-permute-done.3.right_ref = bf16[96,2560]{1,0:T(8,128)(2,1)S(1)} collective-permute-done((bf16[96,2560]{1,0:T(8,128)(2,1)S(1)}, bf16[96,2560]{1,0:T(8,128)(2,1)S(1)}, u32[]{:S(2)}, u32[]{:S(2)}) %collective-permute-start.3) | collective-permute-done | bytes 491552 | tf_op jit(solution)/shard_map/ppermute | solution.py:45
  88.2 1.5 copy-done.5
  89.7 1.6 next_payload.10
  91.3 4.4 %collective-permute-start.5 = (bf16[96,2560]{1,0:T(8,128)(2,1)}, bf16[96,2560]{1,0:T(8,128)(2,1)S(1)}, u32[]{:S(2)}, u32[]{:S(2)}) collective-permute-start(bf16[96,2560]{1,0:T(8,128)(2,1)} %get-tuple-element.259), channel_id=1, source_target_pairs={{0,1},{1,2},{4,5},{5,6},{8,9},{9,10},{12,13},{13,14},{16,17},{17,1... | collective-permute-start | bytes 1474568 | tf_op jit(solution)/shard_map/ppermute | solution.py:45
  97.3 4.3 %collective-permute-start.24 = (bf16[96,2560]{1,0:T(8,128)(2,1)}, bf16[96,2560]{1,0:T(8,128)(2,1)S(1)}, u32[]{:S(2)}, u32[]{:S(2)}) collective-permute-start(bf16[96,2560]{1,0:T(8,128)(2,1)} %get-tuple-element.276), channel_id=1, source_target_pairs={{0,1},{1,2},{4,5},{5,6},{8,9},{9,10},{12,13},{13,14},{16,17},{17,1... | collective-permute-start | bytes 1474568 | tf_op jit(solution)/shard_map/ppermute | solution.py:45
  102.4 5.3 %collective-permute-done.5.right_ref = bf16[96,2560]{1,0:T(8,128)(2,1)S(1)} collective-permute-done((bf16[96,2560]{1,0:T(8,128)(2,1)}, bf16[96,2560]{1,0:T(8,128)(2,1)S(1)}, u32[]{:S(2)}, u32[]{:S(2)}) %collective-permute-start.5) | collective-permute-done | bytes 491552 | tf_op jit(solution)/shard_map/ppermute | solution.py:45
  107.7 1.5 copy-done.6
  109.2 2.5 next_payload.11
  111.8 9.1 %collective-permute-start.7 = (bf16[96,2560]{1,0:T(8,128)(2,1)}, bf16[96,2560]{1,0:T(8,128)(2,1)S(1)}, u32[]{:S(2)}, u32[]{:S(2)}) collective-permute-start(bf16[96,2560]{1,0:T(8,128)(2,1)} %get-tuple-element.261), channel_id=1, source_target_pairs={{0,1},{1,2},{2,3},{4,5},{5,6},{6,7},{8,9},{9,10},{10,11},{12,13},{... | collective-permute-start | bytes 1474568 | tf_op jit(solution)/shard_map/ppermute | solution.py:45
  122.2 1.7 next_payload.16
  123.9 5.4 %collective-permute-start.26 = (bf16[96,2560]{1,0:T(8,128)(2,1)}, bf16[96,2560]{1,0:T(8,128)(2,1)}, u32[]{:S(2)}, u32[]{:S(2)}) collective-permute-start(bf16[96,2560]{1,0:T(8,128)(2,1)} %get-tuple-element.278), channel_id=1, source_target_pairs={{0,1},{1,2},{2,3},{4,5},{5,6},{6,7},{8,9},{9,10},{10,11},{12,13},{... | collective-permute-start | bytes 1474568 | tf_op jit(solution)/shard_map/ppermute | solution.py:45
  130.6 3.5 partial_products.6
  134.2 3.0 collective-permute-done.8.left_ref
  137.1 1.5 copy-done.7
  141.8 1.7 unit_gradient.4.refs_0_
  143.5 1.6 collective-permute-start.12
  145.1 4.6 %collective-permute-start.11 = (bf16[96,2560]{1,0:T(8,128)(2,1)S(1)}, bf16[96,2560]{1,0:T(8,128)(2,1)S(1)}, u32[]{:S(2)}, u32[]{:S(2)}) collective-permute-start(bf16[96,2560]{1,0:T(8,128)(2,1)S(1)} %unit_gradient.4.refs_0_), channel_id=1, source_target_pairs={{0,1},{1,2},{2,3},{4,5},{5,6},{6,7},{8,9},{9,10},{10,11},{12,13},{... | collective-permute-start | bytes 1474568 | tf_op jit(solution)/shard_map/ppermute | solution.py:45
  149.7 3.2 partial_products.7
  152.9 3.0 unit_gradient.6.refs_7_
  157.2 5.4 %collective-permute-start.28 = (bf16[96,2560]{1,0:T(8,128)(2,1)}, bf16[96,2560]{1,0:T(8,128)(2,1)}, u32[]{:S(2)}, u32[]{:S(2)}) collective-permute-start(bf16[96,2560]{1,0:T(8,128)(2,1)} %unit_gradient.6.refs_7_), channel_id=1, source_target_pairs={{0,1},{1,2},{2,3},{4,5},{5,6},{6,7},{8,9},{9,10},{10,11},{12,13},{... | collective-permute-start | bytes 1474568 | tf_op jit(solution)/shard_map/ppermute | solution.py:45
  163.9 2.3 collective-permute-start.13
  167.5 3.2 collective-permute-done.29.left_ref.refs_11_
  170.7 3.1 collective-permute-done.28.right_ref.refs_8_
  173.7 1.9 next_payload.17
  175.7 4.4 %collective-permute-start.30 = (bf16[96,2560]{1,0:T(8,128)(2,1)S(1)}, bf16[96,2560]{1,0:T(8,128)(2,1)S(1)}, u32[]{:S(2)}, u32[]{:S(2)}) collective-permute-start(bf16[96,2560]{1,0:T(8,128)(2,1)S(1)} %get-tuple-element.282), channel_id=1, source_target_pairs={{0,1},{1,2},{2,3},{4,5},{5,6},{6,7},{8,9},{9,10},{10,11},{12,13},{... | collective-permute-start | bytes 1474568 | tf_op jit(solution)/shard_map/ppermute | solution.py:45
  181.4 2.7 collective-permute-done.13.right_ref.refs_2_
  185.1 4.4 %collective-permute-start.15 = (bf16[96,2560]{1,0:T(8,128)(2,1)S(1)}, bf16[96,2560]{1,0:T(8,128)(2,1)S(1)}, u32[]{:S(2)}, u32[]{:S(2)}) collective-permute-start(bf16[96,2560]{1,0:T(8,128)(2,1)S(1)} %get-tuple-element.271), channel_id=1, source_target_pairs={{0,1},{1,2},{2,3},{4,5},{5,6},{6,7},{8,9},{9,10},{10,11},{12,13},{... | collective-permute-start | bytes 1474568 | tf_op jit(solution)/shard_map/ppermute | solution.py:45
  193.0 3.0 collective-permute-done.32
  197.5 4.6 %collective-permute-start.33 = (bf16[96,2560]{1,0:T(8,128)(2,1)S(1)}, bf16[96,2560]{1,0:T(8,128)(2,1)S(1)}, u32[]{:S(2)}, u32[]{:S(2)}) collective-permute-start(bf16[96,2560]{1,0:T(8,128)(2,1)S(1)} %get-tuple-element.285), channel_id=1, source_target_pairs={{0,1},{1,2},{2,3},{4,5},{5,6},{6,7},{8,9},{9,10},{10,11},{12,13},{... | collective-permute-start | bytes 1474568 | tf_op jit(solution)/shard_map/ppermute | solution.py:45
  204.6 2.0 collective-permute-start.17
  206.6 2.5 collective-permute-done.17
  211.1 4.8 %collective-permute-start.18 = (bf16[96,2560]{1,0:T(8,128)(2,1)S(1)}, bf16[96,2560]{1,0:T(8,128)(2,1)S(1)}, u32[]{:S(2)}, u32[]{:S(2)}) collective-permute-start(bf16[96,2560]{1,0:T(8,128)(2,1)S(1)} %get-tuple-element.274), channel_id=1, source_target_pairs={{0,1},{1,2},{2,3},{4,5},{5,6},{6,7},{8,9},{9,10},{10,11},{12,13},{... | collective-permute-start | bytes 1474568 | tf_op jit(solution)/shard_map/ppermute | solution.py:45
  218.4 2.9 collective-permute-start.37
  224.0 4.6 %collective-permute-start.38 = (bf16[96,2560]{1,0:T(8,128)(2,1)S(1)}, bf16[96,2560]{1,0:T(8,128)(2,1)S(1)}, u32[]{:S(2)}, u32[]{:S(2)}) collective-permute-start(bf16[96,2560]{1,0:T(8,128)(2,1)S(1)} %get-tuple-element.292), channel_id=1, source_target_pairs={{0,1},{1,2},{2,3},{4,5},{5,6},{6,7},{8,9},{9,10},{10,11},{12,13},{... | collective-permute-start | bytes 1474568 | tf_op jit(solution)/shard_map/ppermute | solution.py:45
  232.6 6.0 %collective-permute-start.20 = (bf16[96,2560]{1,0:T(8,128)(2,1)}, bf16[96,2560]{1,0:T(8,128)(2,1)}, u32[]{:S(2)}, u32[]{:S(2)}) collective-permute-start(bf16[96,2560]{1,0:T(8,128)(2,1)} %unit_gradient.5.refs_0_), channel_id=1, source_target_pairs={{0,1},{1,2},{2,3},{4,5},{5,6},{6,7},{8,9},{9,10},{10,11},{12,13},{... | collective-permute-start | bytes 1474568 | tf_op jit(solution)/shard_map/ppermute | solution.py:45
  238.6 6.1 %collective-permute-done.39.left_ref = bf16[96,2560]{1,0:T(8,128)(2,1)S(1)} collective-permute-done((bf16[96,2560]{1,0:T(8,128)(2,1)S(1)}, bf16[96,2560]{1,0:T(8,128)(2,1)S(1)}, u32[]{:S(2)}, u32[]{:S(2)}) %collective-permute-start.39) | collective-permute-done | bytes 491552 | tf_op jit(solution)/shard_map/ppermute | solution.py:45
  247.3 5.3 %collective-permute-start.40 = (bf16[96,2560]{1,0:T(8,128)(2,1)}, bf16[96,2560]{1,0:T(8,128)(2,1)}, u32[]{:S(2)}, u32[]{:S(2)}) collective-permute-start(bf16[96,2560]{1,0:T(8,128)(2,1)} %unit_gradient.7.refs_7_), channel_id=1, source_target_pairs={{0,1},{1,2},{2,3},{4,5},{5,6},{6,7},{8,9},{9,10},{10,11},{12,13},{... | collective-permute-start | bytes 1474568 | tf_op jit(solution)/shard_map/ppermute | solution.py:45
  252.6 2.7 collective-permute-done.22.refs_4_
  258.0 8.1 %weight_step.9 = (f32[640,2560]{1,0:T(8,128)}, f32[8,128]{1,0:T(8,128)S(1)}) custom-call(s32[4]{0:T(128)S(1)} %and_select_fusion.s, bf16[96,2560]{1,0:T(8,128)(2,1)S(1)} %unit_gradient.4.refs_0_, bf16[96,2560]{1,0:T(8,128)(2,1)S(1)} %collective-permute-done.11.right_ref.refs_1_, bf16[96,2560]{1,0:T(8,128)(2,1)S(1)} %collective-permute-done.13.right_ref.refs_2_, ...), custom_call_target="tpu_custom_call" | custom-call | flops 1509949440 | bytes 15925248 | tf_op jit(solution)/shard_map/weight_step/pallas_call | solution.py:16
  270.3 5.7 %weight_step.10 = (f32[640,2560]{1,0:T(8,128)}, f32[8,128]{1,0:T(8,128)S(1)}) custom-call(s32[4]{0:T(128)S(1)} %and_select_fusion.s, bf16[96,2560]{1,0:T(8,128)(2,1)S(1)} %unit_gradient.4.refs_0_, bf16[96,2560]{1,0:T(8,128)(2,1)S(1)} %collective-permute-done.11.right_ref.refs_1_, ...), custom_call_target="tpu_custom_call", output_to_operand_aliasing={{0}: (18, {})} | custom-call | flops 1006632960 | bytes 10616832 | tf_op jit(solution)/shard_map/weight_step/pallas_call | solution.py:16
  281.6 6.7 %collective-permute-done.44.refs_12_ = bf16[96,2560]{1,0:T(8,128)(2,1)} collective-permute-done((bf16[96,2560]{1,0:T(8,128)(2,1)S(1)}, bf16[96,2560]{1,0:T(8,128)(2,1)}, u32[]{:S(2)}, u32[]{:S(2)}) %collective-permute-start.44) | collective-permute-done | bytes 491552 | tf_op jit(solution)/shard_map/ppermute | solution.py:45
  296.9 9.1 %grad_rows.7 = (bf16[4,192,640]{2,1,0:T(8,128)(2,1)}, f32[8,128]{1,0:T(8,128)}) custom-call(s32[4]{0:T(128)S(1)} %and_select_fusion.s, bf16[96,2560]{1,0:T(8,128)(2,1)S(1)} %unit_gradient.4.refs_0_, bf16[96,2560]{1,0:T(8,128)(2,1)S(1)} %collective-permute-done.11.right_ref.refs_1_, bf16[96,2560]{1,0:T(8,128)(2,1)S(1)} %copy-done.19, ...), custom_call_target="tpu_custom_call" | custom-call | flops 2516582400 | bytes 10158080 | tf_op jit(solution)/shard_map/grad_rows/pallas_call | solution.py:16
  306.0 9.9 %weight_step.11 = bf16[640,2560]{1,0:T(8,128)(2,1)} custom-call(s32[4]{0:T(128)S(1)} %and_select_fusion.s, bf16[96,2560]{1,0:T(8,128)(2,1)} %unit_gradient.5.refs_0_, bf16[96,2560]{1,0:T(8,128)(2,1)} %collective-permute-done.20.refs_1_, bf16[96,2560]{1,0:T(8,128)(2,1)} %collective-permute-done.21.right_ref.refs_2_, ...), custom_call_target="tpu_custom_call" | custom-call | flops 2516582400 | bytes 26542080 | tf_op jit(solution)/shard_map/weight_step/pallas_call | solution.py:16
  315.9 61.9 %conditional.1 = (bf16[640,2560]{1,0:T(8,128)(2,1)}, bf16[1,384,2560]{2,1,0:T(8,128)(2,1)S(1)}, f32[1,640,2560]{2,1,0:T(8,128)}) conditional(s32[]{:T(128)} %clamp.3, (bf16[640,2560]{1,0:T(8,128)(2,1)}, bf16[4,192,640]{2,1,0:T(8,128)(2,1)}, s32[4]{0:T(128)S(1)}, bf16[96,2560]{1,0:T(8,128)(2,1)}, bf16[96,2560]{1,0:T(8,128)(2,1)}, ...), branch_computations={%region_1.2_spmd, %region_2.3_spmd, %region_3.4_spmd} | conditional | flops 5033164800 | bytes 59637888 | solution.py:623
  315.9 1.6 collective-permute-start.2
  317.6 4.7 %all-to-all-start.4 = ((bf16[4,192,640]{2,1,0:T(8,128)(2,1)}), bf16[4,192,640]{2,1,0:T(8,128)(2,1)S(1)}, u32[]{:S(2)}, u32[]{:S(2)}) async-start(bf16[4,192,640]{2,1,0:T(8,128)(2,1)} %get-tuple-element.175), calls=%async_computation.4 | async-start | bytes 1966080 | tf_op jit(solution)/shard_map/cond/branch_2_fun/all_to_all | solution.py:449
  322.2 9.4 %grad_rows.6 = (bf16[4,192,640]{2,1,0:T(8,128)(2,1)}, f32[8,128]{1,0:T(8,128)S(1)}) custom-call(s32[4]{0:T(128)S(1)} %get-tuple-element.176.s, bf16[96,2560]{1,0:T(8,128)(2,1)} %get-tuple-element.177.refs_0_, bf16[96,2560]{1,0:T(8,128)(2,1)} %get-tuple-element.178.refs_1_, bf16[96,2560]{1,0:T(8,128)(2,1)} %get-tuple-element.179.refs_2_, ...), custom_call_target="tpu_custom_call" | custom-call | flops 2516582400 | bytes 10158080 | tf_op jit(solution)/shard_map/cond/branch_2_fun/grad_rows/pallas_call | solution.py:16
  331.6 15.2 %all-to-all-done.4.refs_0_ = bf16[4,192,640]{2,1,0:T(8,128)(2,1)S(1)} async-done(((bf16[4,192,640]{2,1,0:T(8,128)(2,1)}), bf16[4,192,640]{2,1,0:T(8,128)(2,1)S(1)}, u32[]{:S(2)}, u32[]{:S(2)}) %all-to-all-start.4) | async-done | bytes 983072 | tf_op jit(solution)/shard_map/cond/branch_2_fun/all_to_all | solution.py:449
  346.9 3.5 all-to-all-start.5
  350.4 12.6 %weight_step.8 = f32[640,2560]{1,0:T(8,128)} custom-call(s32[4]{0:T(128)S(1)} %get-tuple-element.176.s, bf16[96,2560]{1,0:T(8,128)(2,1)} %get-tuple-element.177.refs_0_, bf16[96,2560]{1,0:T(8,128)(2,1)} %get-tuple-element.178.refs_1_, bf16[96,2560]{1,0:T(8,128)(2,1)} %get-tuple-element.179.refs_2_, bf16[96,2560]{1,0:T(8,128)(2,1)} %get-tuple-element.180.refs_3_, ...), custom_call_target="tpu_custom_call" | custom-call | flops 2516582400 | bytes 26542080 | tf_op jit(solution)/shard_map/cond/branch_2_fun/weight_step/pallas_call | solution.py:16
  363.0 2.5 all-to-all-done.5.refs_1_
  365.8 12.1 %collective-permute-done.2 = bf16[640,2560]{1,0:T(8,128)(2,1)} collective-permute-done((bf16[640,2560]{1,0:T(8,128)(2,1)}, bf16[640,2560]{1,0:T(8,128)(2,1)}, u32[]{:S(2)}, u32[]{:S(2)}) %collective-permute-start.2) | collective-permute-done | bytes 3276832 | tf_op jit(solution)/shard_map/cond/branch_2_fun/ppermute | solution.py:454
  377.8 5.1 %widened.1 = f32[640,2560]{1,0:T(8,128)} custom-call(bf16[640,2560]{1,0:T(8,128)(2,1)} %get-tuple-element.300.value_ref), custom_call_target="tpu_custom_call" | custom-call | bytes 9830400 | tf_op jit(solution)/shard_map/widened/pallas_call | solution.py:16
  (163 shorter events, 60.4 us)
Async XLA Ops:
  2.4 20.1 %all-to-all-start.6 = ((bf16[4,96,640]{2,1,0:T(8,128)(2,1)}), bf16[4,96,640]{2,1,0:T(8,128)(2,1)S(1)}, u32[]{:S(2)}, u32[]{:S(2)}) async-start(bf16[4,96,640]{2,1,0:T(8,128)(2,1)} %cut_heads.3), calls=%async_computation.6 | async-start | bytes 983040 | tf_op jit(solution)/shard_map/all_to_all | solution.py:449
  22.5 16.7 %copy-start.30 = (bf16[4,96,640]{2,1,0:T(8,128)(2,1)}, bf16[4,96,640]{2,1,0:T(8,128)(2,1)S(1)}, u32[]{:S(2)}) copy-start(bf16[4,96,640]{2,1,0:T(8,128)(2,1)S(1)} %all-to-all-done.6.mine_ref.refs_14_) | copy-start | bytes 1474564
  22.5 16.7 %all-to-all-start.7 = ((bf16[4,96,640]{2,1,0:T(8,128)(2,1)}), bf16[4,96,640]{2,1,0:T(8,128)(2,1)S(1)}, u32[]{:S(2)}, u32[]{:S(2)}) async-start(bf16[4,96,640]{2,1,0:T(8,128)(2,1)} %cut_heads.4), calls=%async_computation.7 | async-start | bytes 983040 | tf_op jit(solution)/shard_map/all_to_all | solution.py:449
  39.3 17.5 %copy-start.31 = (bf16[4,96,640]{2,1,0:T(8,128)(2,1)}, bf16[4,96,640]{2,1,0:T(8,128)(2,1)S(1)}, u32[]{:S(2)}) copy-start(bf16[4,96,640]{2,1,0:T(8,128)(2,1)S(1)} %all-to-all-done.7.mine_ref.refs_15_) | copy-start | bytes 1474564
  43.7 78.5 %copy-start.2 = (bf16[4,96,2560]{2,1,0:T(8,128)(2,1)}, bf16[4,96,2560]{2,1,0:T(8,128)(2,1)S(1)}, u32[]{:S(2)}) copy-start(bf16[4,96,2560]{2,1,0:T(8,128)(2,1)S(1)} %get-tuple-element.265.of_right.of_left.own_ref) | copy-start | bytes 5898244
  43.7 11.6 %collective-permute-start.9 = (bf16[96,2560]{1,0:T(8,128)(2,1)}, bf16[96,2560]{1,0:T(8,128)(2,1)S(1)}, u32[]{:S(2)}, u32[]{:S(2)}) collective-permute-start(bf16[96,2560]{1,0:T(8,128)(2,1)} %get-tuple-element.263), channel_id=1, source_target_pairs={{0,1},{4,5},{8,9},{12,13},{16,17},{20,21},{24,25},{28,29}} | collective-permute-start | bytes 1474568 | tf_op jit(solution)/shard_map/ppermute | solution.py:45
  45.0 10.2 %collective-permute-start.10 = (bf16[96,2560]{1,0:T(8,128)(2,1)}, bf16[96,2560]{1,0:T(8,128)(2,1)S(1)}, u32[]{:S(2)}, u32[]{:S(2)}) collective-permute-start(bf16[96,2560]{1,0:T(8,128)(2,1)} %get-tuple-element.264), channel_id=1, source_target_pairs={{3,2},{7,6},{11,10},{15,14},{19,18},{23,22},{27,26},{31,30}} | collective-permute-start | bytes 1474568 | tf_op jit(solution)/shard_map/ppermute | solution.py:45
  58.6 72.0 %all-to-all-start.8 = ((bf16[4,192,640]{2,1,0:T(8,128)(2,1)}), bf16[4,192,640]{2,1,0:T(8,128)(2,1)}, u32[]{:S(2)}, u32[]{:S(2)}) async-start(bf16[4,192,640]{2,1,0:T(8,128)(2,1)} %cut_heads.5), calls=%async_computation.8 | async-start | bytes 1966080 | tf_op jit(solution)/shard_map/all_to_all | solution.py:449
  62.8 25.3 %collective-permute-start.3 = (bf16[96,2560]{1,0:T(8,128)(2,1)S(1)}, bf16[96,2560]{1,0:T(8,128)(2,1)S(1)}, u32[]{:S(2)}, u32[]{:S(2)}) collective-permute-start(bf16[96,2560]{1,0:T(8,128)(2,1)S(1)} %copy-done.37), channel_id=1, source_target_pairs={{0,1},{4,5},{8,9},{12,13},{16,17},{20,21},{24,25},{28,29}} | collective-permute-start | bytes 1474568 | tf_op jit(solution)/shard_map/ppermute | solution.py:45
  67.1 21.0 %collective-permute-start.4 = (bf16[96,2560]{1,0:T(8,128)(2,1)S(1)}, bf16[96,2560]{1,0:T(8,128)(2,1)S(1)}, u32[]{:S(2)}, u32[]{:S(2)}) collective-permute-start(bf16[96,2560]{1,0:T(8,128)(2,1)S(1)} %copy-done.35), channel_id=1, source_target_pairs={{3,2},{7,6},{11,10},{15,14},{19,18},{23,22},{27,26},{31,30}} | collective-permute-start | bytes 1474568 | tf_op jit(solution)/shard_map/ppermute | solution.py:45
  91.3 16.4 %collective-permute-start.5 = (bf16[96,2560]{1,0:T(8,128)(2,1)}, bf16[96,2560]{1,0:T(8,128)(2,1)S(1)}, u32[]{:S(2)}, u32[]{:S(2)}) collective-permute-start(bf16[96,2560]{1,0:T(8,128)(2,1)} %get-tuple-element.259), channel_id=1, source_target_pairs={{0,1},{1,2},{4,5},{5,6},{8,9},{9,10},{12,13},{13,14},{16,17},{17,1... | collective-permute-start | bytes 1474568 | tf_op jit(solution)/shard_map/ppermute | solution.py:45
  95.7 11.9 %collective-permute-start.6 = (bf16[96,2560]{1,0:T(8,128)(2,1)}, bf16[96,2560]{1,0:T(8,128)(2,1)}, u32[]{:S(2)}, u32[]{:S(2)}) collective-permute-start(bf16[96,2560]{1,0:T(8,128)(2,1)} %get-tuple-element.260), channel_id=1, source_target_pairs={{2,1},{3,2},{6,5},{7,6},{10,9},{11,10},{14,13},{15,14},{18,17},{19... | collective-permute-start | bytes 1474568 | tf_op jit(solution)/shard_map/ppermute | solution.py:45
  97.3 24.9 %collective-permute-start.24 = (bf16[96,2560]{1,0:T(8,128)(2,1)}, bf16[96,2560]{1,0:T(8,128)(2,1)S(1)}, u32[]{:S(2)}, u32[]{:S(2)}) collective-permute-start(bf16[96,2560]{1,0:T(8,128)(2,1)} %get-tuple-element.276), channel_id=1, source_target_pairs={{0,1},{1,2},{4,5},{5,6},{8,9},{9,10},{12,13},{13,14},{16,17},{17,1... | collective-permute-start | bytes 1474568 | tf_op jit(solution)/shard_map/ppermute | solution.py:45
  101.6 20.6 %collective-permute-start.25 = (bf16[96,2560]{1,0:T(8,128)(2,1)}, bf16[96,2560]{1,0:T(8,128)(2,1)S(1)}, u32[]{:S(2)}, u32[]{:S(2)}) collective-permute-start(bf16[96,2560]{1,0:T(8,128)(2,1)} %copy-done.33), channel_id=1, source_target_pairs={{2,1},{3,2},{6,5},{7,6},{10,9},{11,10},{14,13},{15,14},{18,17},{19... | collective-permute-start | bytes 1474568 | tf_op jit(solution)/shard_map/ppermute | solution.py:45
  111.8 18.8 %copy-start.40 = (f32[2560]{0:T(1024)S(1)}, f32[2560]{0:T(1024)}, u32[]{:S(2)}) copy-start(f32[2560]{0:T(1024)} %param.19) | copy-start | bytes 30724
  111.8 22.4 %collective-permute-start.7 = (bf16[96,2560]{1,0:T(8,128)(2,1)}, bf16[96,2560]{1,0:T(8,128)(2,1)S(1)}, u32[]{:S(2)}, u32[]{:S(2)}) collective-permute-start(bf16[96,2560]{1,0:T(8,128)(2,1)} %get-tuple-element.261), channel_id=1, source_target_pairs={{0,1},{1,2},{2,3},{4,5},{5,6},{6,7},{8,9},{9,10},{10,11},{12,13},{... | collective-permute-start | bytes 1474568 | tf_op jit(solution)/shard_map/ppermute | solution.py:45
  120.9 16.2 %collective-permute-start.8 = (bf16[96,2560]{1,0:T(8,128)(2,1)}, bf16[96,2560]{1,0:T(8,128)(2,1)}, u32[]{:S(2)}, u32[]{:S(2)}) collective-permute-start(bf16[96,2560]{1,0:T(8,128)(2,1)} %get-tuple-element.262), channel_id=1, source_target_pairs={{1,0},{2,1},{3,2},{5,4},{6,5},{7,6},{9,8},{10,9},{11,10},{13,12},{... | collective-permute-start | bytes 1474568 | tf_op jit(solution)/shard_map/ppermute | solution.py:45
  123.9 29.0 %collective-permute-start.26 = (bf16[96,2560]{1,0:T(8,128)(2,1)}, bf16[96,2560]{1,0:T(8,128)(2,1)}, u32[]{:S(2)}, u32[]{:S(2)}) collective-permute-start(bf16[96,2560]{1,0:T(8,128)(2,1)} %get-tuple-element.278), channel_id=1, source_target_pairs={{0,1},{1,2},{2,3},{4,5},{5,6},{6,7},{8,9},{9,10},{10,11},{12,13},{... | collective-permute-start | bytes 1474568 | tf_op jit(solution)/shard_map/ppermute | solution.py:45
  129.3 23.6 %collective-permute-start.27 = (bf16[96,2560]{1,0:T(8,128)(2,1)}, bf16[96,2560]{1,0:T(8,128)(2,1)}, u32[]{:S(2)}, u32[]{:S(2)}) collective-permute-start(bf16[96,2560]{1,0:T(8,128)(2,1)} %get-tuple-element.279), channel_id=1, source_target_pairs={{1,0},{2,1},{3,2},{5,4},{6,5},{7,6},{9,8},{10,9},{11,10},{13,12},{... | collective-permute-start | bytes 1474568 | tf_op jit(solution)/shard_map/ppermute | solution.py:45
  143.5 19.1 %collective-permute-start.12 = (bf16[96,2560]{1,0:T(8,128)(2,1)S(1)}, bf16[96,2560]{1,0:T(8,128)(2,1)S(1)}, u32[]{:S(2)}, u32[]{:S(2)}) collective-permute-start(bf16[96,2560]{1,0:T(8,128)(2,1)S(1)} %unit_gradient.4.refs_0_), channel_id=1, source_target_pairs={{1,0},{2,1},{3,2},{5,4},{6,5},{7,6},{9,8},{10,9},{11,10},{13,12},{... | collective-permute-start | bytes 1474568 | tf_op jit(solution)/shard_map/ppermute | solution.py:45
  145.1 17.6 %collective-permute-start.11 = (bf16[96,2560]{1,0:T(8,128)(2,1)S(1)}, bf16[96,2560]{1,0:T(8,128)(2,1)S(1)}, u32[]{:S(2)}, u32[]{:S(2)}) collective-permute-start(bf16[96,2560]{1,0:T(8,128)(2,1)S(1)} %unit_gradient.4.refs_0_), channel_id=1, source_target_pairs={{0,1},{1,2},{2,3},{4,5},{5,6},{6,7},{8,9},{9,10},{10,11},{12,13},{... | collective-permute-start | bytes 1474568 | tf_op jit(solution)/shard_map/ppermute | solution.py:45
  155.9 14.8 %collective-permute-start.29 = (bf16[96,2560]{1,0:T(8,128)(2,1)}, bf16[96,2560]{1,0:T(8,128)(2,1)}, u32[]{:S(2)}, u32[]{:S(2)}) collective-permute-start(bf16[96,2560]{1,0:T(8,128)(2,1)} %unit_gradient.6.refs_7_), channel_id=1, source_target_pairs={{1,0},{2,1},{3,2},{5,4},{6,5},{7,6},{9,8},{10,9},{11,10},{13,12},{... | collective-permute-start | bytes 1474568 | tf_op jit(solution)/shard_map/ppermute | solution.py:45
  157.2 16.5 %collective-permute-start.28 = (bf16[96,2560]{1,0:T(8,128)(2,1)}, bf16[96,2560]{1,0:T(8,128)(2,1)}, u32[]{:S(2)}, u32[]{:S(2)}) collective-permute-start(bf16[96,2560]{1,0:T(8,128)(2,1)} %unit_gradient.6.refs_7_), channel_id=1, source_target_pairs={{0,1},{1,2},{2,3},{4,5},{5,6},{6,7},{8,9},{9,10},{10,11},{12,13},{... | collective-permute-start | bytes 1474568 | tf_op jit(solution)/shard_map/ppermute | solution.py:45
  163.9 20.3 %collective-permute-start.13 = (bf16[96,2560]{1,0:T(8,128)(2,1)S(1)}, bf16[96,2560]{1,0:T(8,128)(2,1)S(1)}, u32[]{:S(2)}, u32[]{:S(2)}) collective-permute-start(bf16[96,2560]{1,0:T(8,128)(2,1)S(1)} %get-tuple-element.269), channel_id=1, source_target_pairs={{0,1},{1,2},{2,3},{4,5},{5,6},{6,7},{8,9},{9,10},{10,11},{12,13},{... | collective-permute-start | bytes 1474568 | tf_op jit(solution)/shard_map/ppermute | solution.py:45
  166.2 18.0 %collective-permute-start.14 = (bf16[96,2560]{1,0:T(8,128)(2,1)S(1)}, bf16[96,2560]{1,0:T(8,128)(2,1)S(1)}, u32[]{:S(2)}, u32[]{:S(2)}) collective-permute-start(bf16[96,2560]{1,0:T(8,128)(2,1)S(1)} %get-tuple-element.270), channel_id=1, source_target_pairs={{1,0},{2,1},{3,2},{5,4},{6,5},{7,6},{9,8},{10,9},{11,10},{13,12},{... | collective-permute-start | bytes 1474568 | tf_op jit(solution)/shard_map/ppermute | solution.py:45
  175.7 20.3 %collective-permute-start.30 = (bf16[96,2560]{1,0:T(8,128)(2,1)S(1)}, bf16[96,2560]{1,0:T(8,128)(2,1)S(1)}, u32[]{:S(2)}, u32[]{:S(2)}) collective-permute-start(bf16[96,2560]{1,0:T(8,128)(2,1)S(1)} %get-tuple-element.282), channel_id=1, source_target_pairs={{0,1},{1,2},{2,3},{4,5},{5,6},{6,7},{8,9},{9,10},{10,11},{12,13},{... | collective-permute-start | bytes 1474568 | tf_op jit(solution)/shard_map/ppermute | solution.py:45
  180.1 15.9 %collective-permute-start.31 = (bf16[96,2560]{1,0:T(8,128)(2,1)S(1)}, bf16[96,2560]{1,0:T(8,128)(2,1)S(1)}, u32[]{:S(2)}, u32[]{:S(2)}) collective-permute-start(bf16[96,2560]{1,0:T(8,128)(2,1)S(1)} %get-tuple-element.283), channel_id=1, source_target_pairs={{1,0},{2,1},{3,2},{5,4},{6,5},{7,6},{9,8},{10,9},{11,10},{13,12},{... | collective-permute-start | bytes 1474568 | tf_op jit(solution)/shard_map/ppermute | solution.py:45
  184.2 86.1 %copy-start.18 = (bf16[96,2560]{1,0:T(8,128)(2,1)}, bf16[96,2560]{1,0:T(8,128)(2,1)S(1)}, u32[]{:S(2)}) copy-start(bf16[96,2560]{1,0:T(8,128)(2,1)S(1)} %collective-permute-done.13.right_ref.refs_2_) | copy-start | bytes 1474564
  185.1 24.0 %collective-permute-start.15 = (bf16[96,2560]{1,0:T(8,128)(2,1)S(1)}, bf16[96,2560]{1,0:T(8,128)(2,1)S(1)}, u32[]{:S(2)}, u32[]{:S(2)}) collective-permute-start(bf16[96,2560]{1,0:T(8,128)(2,1)S(1)} %get-tuple-element.271), channel_id=1, source_target_pairs={{0,1},{1,2},{2,3},{4,5},{5,6},{6,7},{8,9},{9,10},{10,11},{12,13},{... | collective-permute-start | bytes 1474568 | tf_op jit(solution)/shard_map/ppermute | solution.py:45
  189.5 19.6 %collective-permute-start.16 = (bf16[96,2560]{1,0:T(8,128)(2,1)S(1)}, bf16[96,2560]{1,0:T(8,128)(2,1)S(1)}, u32[]{:S(2)}, u32[]{:S(2)}) collective-permute-start(bf16[96,2560]{1,0:T(8,128)(2,1)S(1)} %get-tuple-element.272), channel_id=1, source_target_pairs={{1,0},{2,1},{3,2},{5,4},{6,5},{7,6},{9,8},{10,9},{11,10},{13,12},{... | collective-permute-start | bytes 1474568 | tf_op jit(solution)/shard_map/ppermute | solution.py:45
  192.0 4.0 %collective-permute-start.32 = (f32[1]{0:T(128)}, f32[1]{0:T(128)}, u32[]{:S(2)}, u32[]{:S(2)}) collective-permute-start(f32[1]{0:T(128)} %add.42), channel_id=1, source_target_pairs={{0,4},{4,8},{8,12},{12,16},{16,20},{20,24},{24,28},{28,0},{1,5},{5... | collective-permute-start | bytes 20 | tf_op jit(solution)/shard_map/ppermute | solution.py:490
  196.0 15.1 %copy-start.22 = (bf16[96,2560]{1,0:T(8,128)(2,1)}, bf16[96,2560]{1,0:T(8,128)(2,1)S(1)}, u32[]{:S(2)}) copy-start(bf16[96,2560]{1,0:T(8,128)(2,1)S(1)} %collective-permute-done.30.right_ref.refs_9_) | copy-start | bytes 1474564
  196.0 15.1 %copy-start.23 = (bf16[96,2560]{1,0:T(8,128)(2,1)}, bf16[96,2560]{1,0:T(8,128)(2,1)S(1)}, u32[]{:S(2)}) copy-start(bf16[96,2560]{1,0:T(8,128)(2,1)S(1)} %collective-permute-done.31.left_ref.refs_12_) | copy-start | bytes 1474564
  197.5 24.6 %collective-permute-start.33 = (bf16[96,2560]{1,0:T(8,128)(2,1)S(1)}, bf16[96,2560]{1,0:T(8,128)(2,1)S(1)}, u32[]{:S(2)}, u32[]{:S(2)}) collective-permute-start(bf16[96,2560]{1,0:T(8,128)(2,1)S(1)} %get-tuple-element.285), channel_id=1, source_target_pairs={{0,1},{1,2},{2,3},{4,5},{5,6},{6,7},{8,9},{9,10},{10,11},{12,13},{... | collective-permute-start | bytes 1474568 | tf_op jit(solution)/shard_map/ppermute | solution.py:45
  202.1 20.0 %collective-permute-start.34 = (bf16[96,2560]{1,0:T(8,128)(2,1)S(1)}, bf16[96,2560]{1,0:T(8,128)(2,1)S(1)}, u32[]{:S(2)}, u32[]{:S(2)}) collective-permute-start(bf16[96,2560]{1,0:T(8,128)(2,1)S(1)} %get-tuple-element.286), channel_id=1, source_target_pairs={{1,0},{2,1},{3,2},{5,4},{6,5},{7,6},{9,8},{10,9},{11,10},{13,12},{... | collective-permute-start | bytes 1474568 | tf_op jit(solution)/shard_map/ppermute | solution.py:45
  204.6 4.4 %collective-permute-start.17 = (f32[1]{0:T(128)}, f32[1]{0:T(128)}, u32[]{:S(2)}, u32[]{:S(2)}) collective-permute-start(f32[1]{0:T(128)} %add.41), channel_id=1, source_target_pairs={{0,8},{4,12},{8,16},{12,20},{16,24},{20,28},{24,0},{28,4},{1,9},{5... | collective-permute-start | bytes 20 | tf_op jit(solution)/shard_map/ppermute | solution.py:490
  209.0 61.2 %copy-start.24 = (bf16[96,2560]{1,0:T(8,128)(2,1)}, bf16[96,2560]{1,0:T(8,128)(2,1)S(1)}, u32[]{:S(2)}) copy-start(bf16[96,2560]{1,0:T(8,128)(2,1)S(1)} %collective-permute-done.15.right_ref.refs_3_) | copy-start | bytes 1474564
  209.0 15.0 %copy-start.26 = (bf16[96,2560]{1,0:T(8,128)(2,1)}, bf16[96,2560]{1,0:T(8,128)(2,1)S(1)}, u32[]{:S(2)}) copy-start(bf16[96,2560]{1,0:T(8,128)(2,1)S(1)} %collective-permute-done.16.left_ref.refs_6_) | copy-start | bytes 1474564
  211.1 18.8 %copy-start.10 = (bf16[1,384,2560]{2,1,0:T(8,128)(2,1)S(1)}, bf16[1,384,2560]{2,1,0:T(8,128)(2,1)}, u32[]{:S(2)}) copy-start(bf16[1,384,2560]{2,1,0:T(8,128)(2,1)} %param.17) | copy-start | bytes 5898244
  211.1 18.8 %copy-start.13 = (bf16[1,384,2560]{2,1,0:T(8,128)(2,1)S(1)}, bf16[1,384,2560]{2,1,0:T(8,128)(2,1)}, u32[]{:S(2)}) copy-start(bf16[1,384,2560]{2,1,0:T(8,128)(2,1)} %param.18) | copy-start | bytes 5898244
  211.1 18.8 %collective-permute-start.18 = (bf16[96,2560]{1,0:T(8,128)(2,1)S(1)}, bf16[96,2560]{1,0:T(8,128)(2,1)S(1)}, u32[]{:S(2)}, u32[]{:S(2)}) collective-permute-start(bf16[96,2560]{1,0:T(8,128)(2,1)S(1)} %get-tuple-element.274), channel_id=1, source_target_pairs={{0,1},{1,2},{2,3},{4,5},{5,6},{6,7},{8,9},{9,10},{10,11},{12,13},{... | collective-permute-start | bytes 1474568 | tf_op jit(solution)/shard_map/ppermute | solution.py:45
  215.9 14.0 %collective-permute-start.19 = (bf16[96,2560]{1,0:T(8,128)(2,1)S(1)}, bf16[96,2560]{1,0:T(8,128)(2,1)S(1)}, u32[]{:S(2)}, u32[]{:S(2)}) collective-permute-start(bf16[96,2560]{1,0:T(8,128)(2,1)S(1)} %get-tuple-element.275), channel_id=1, source_target_pairs={{1,0},{2,1},{3,2},{5,4},{6,5},{7,6},{9,8},{10,9},{11,10},{13,12},{... | collective-permute-start | bytes 1474568 | tf_op jit(solution)/shard_map/ppermute | solution.py:45
  218.4 3.7 collective-permute-start.37
  224.0 14.5 %collective-permute-start.38 = (bf16[96,2560]{1,0:T(8,128)(2,1)S(1)}, bf16[96,2560]{1,0:T(8,128)(2,1)S(1)}, u32[]{:S(2)}, u32[]{:S(2)}) collective-permute-start(bf16[96,2560]{1,0:T(8,128)(2,1)S(1)} %get-tuple-element.292), channel_id=1, source_target_pairs={{0,1},{1,2},{2,3},{4,5},{5,6},{6,7},{8,9},{9,10},{10,11},{12,13},{... | collective-permute-start | bytes 1474568 | tf_op jit(solution)/shard_map/ppermute | solution.py:45
  228.6 16.1 %collective-permute-start.39 = (bf16[96,2560]{1,0:T(8,128)(2,1)S(1)}, bf16[96,2560]{1,0:T(8,128)(2,1)S(1)}, u32[]{:S(2)}, u32[]{:S(2)}) collective-permute-start(bf16[96,2560]{1,0:T(8,128)(2,1)S(1)} %get-tuple-element.293), channel_id=1, source_target_pairs={{1,0},{2,1},{3,2},{5,4},{6,5},{7,6},{9,8},{10,9},{11,10},{13,12},{... | collective-permute-start | bytes 1474568 | tf_op jit(solution)/shard_map/ppermute | solution.py:45
  231.3 24.0 %collective-permute-start.22 = (bf16[96,2560]{1,0:T(8,128)(2,1)}, bf16[96,2560]{1,0:T(8,128)(2,1)}, u32[]{:S(2)}, u32[]{:S(2)}) collective-permute-start(bf16[96,2560]{1,0:T(8,128)(2,1)} %unit_gradient.5.refs_0_), channel_id=1, source_target_pairs={{1,0},{2,1},{3,2},{5,4},{6,5},{7,6},{9,8},{10,9},{11,10},{13,12},{... | collective-permute-start | bytes 1474568 | tf_op jit(solution)/shard_map/ppermute | solution.py:45
  232.6 24.0 %collective-permute-start.20 = (bf16[96,2560]{1,0:T(8,128)(2,1)}, bf16[96,2560]{1,0:T(8,128)(2,1)}, u32[]{:S(2)}, u32[]{:S(2)}) collective-permute-start(bf16[96,2560]{1,0:T(8,128)(2,1)} %unit_gradient.5.refs_0_), channel_id=1, source_target_pairs={{0,1},{1,2},{2,3},{4,5},{5,6},{6,7},{8,9},{9,10},{10,11},{12,13},{... | collective-permute-start | bytes 1474568 | tf_op jit(solution)/shard_map/ppermute | solution.py:45
  246.0 20.1 %collective-permute-start.41 = (bf16[96,2560]{1,0:T(8,128)(2,1)}, bf16[96,2560]{1,0:T(8,128)(2,1)}, u32[]{:S(2)}, u32[]{:S(2)}) collective-permute-start(bf16[96,2560]{1,0:T(8,128)(2,1)} %unit_gradient.7.refs_7_), channel_id=1, source_target_pairs={{1,0},{2,1},{3,2},{5,4},{6,5},{7,6},{9,8},{10,9},{11,10},{13,12},{... | collective-permute-start | bytes 1474568 | tf_op jit(solution)/shard_map/ppermute | solution.py:45
  247.3 18.8 %collective-permute-start.40 = (bf16[96,2560]{1,0:T(8,128)(2,1)}, bf16[96,2560]{1,0:T(8,128)(2,1)}, u32[]{:S(2)}, u32[]{:S(2)}) collective-permute-start(bf16[96,2560]{1,0:T(8,128)(2,1)} %unit_gradient.7.refs_7_), channel_id=1, source_target_pairs={{0,1},{1,2},{2,3},{4,5},{5,6},{6,7},{8,9},{9,10},{10,11},{12,13},{... | collective-permute-start | bytes 1474568 | tf_op jit(solution)/shard_map/ppermute | solution.py:45
  255.3 20.7 %collective-permute-start.23 = (bf16[96,2560]{1,0:T(8,128)(2,1)}, bf16[96,2560]{1,0:T(8,128)(2,1)}, u32[]{:S(2)}, u32[]{:S(2)}) collective-permute-start(bf16[96,2560]{1,0:T(8,128)(2,1)} %collective-permute-done.22.refs_4_), channel_id=1, source_target_pairs={{1,0},{2,1},{5,4},{6,5},{9,8},{10,9},{13,12},{14,13},{17,16},{18,1... | collective-permute-start | bytes 1474568 | tf_op jit(solution)/shard_map/ppermute | solution.py:45
  256.6 19.4 %collective-permute-start.21 = (bf16[96,2560]{1,0:T(8,128)(2,1)}, bf16[96,2560]{1,0:T(8,128)(2,1)}, u32[]{:S(2)}, u32[]{:S(2)}) collective-permute-start(bf16[96,2560]{1,0:T(8,128)(2,1)} %collective-permute-done.20.refs_1_), channel_id=1, source_target_pairs={{1,2},{2,3},{5,6},{6,7},{9,10},{10,11},{13,14},{14,15},{17,18},{18... | collective-permute-start | bytes 1474568 | tf_op jit(solution)/shard_map/ppermute | solution.py:45
  267.5 12.6 %collective-permute-start.42 = (bf16[96,2560]{1,0:T(8,128)(2,1)S(1)}, bf16[96,2560]{1,0:T(8,128)(2,1)}, u32[]{:S(2)}, u32[]{:S(2)}) collective-permute-start(bf16[96,2560]{1,0:T(8,128)(2,1)S(1)} %get-tuple-element.295), channel_id=1, source_target_pairs={{1,2},{2,3},{5,6},{6,7},{9,10},{10,11},{13,14},{14,15},{17,18},{18... | collective-permute-start | bytes 1474568 | tf_op jit(solution)/shard_map/ppermute | solution.py:45
  269.0 19.4 %collective-permute-start.44 = (bf16[96,2560]{1,0:T(8,128)(2,1)S(1)}, bf16[96,2560]{1,0:T(8,128)(2,1)}, u32[]{:S(2)}, u32[]{:S(2)}) collective-permute-start(bf16[96,2560]{1,0:T(8,128)(2,1)S(1)} %get-tuple-element.296), channel_id=1, source_target_pairs={{1,0},{2,1},{5,4},{6,5},{9,8},{10,9},{13,12},{14,13},{17,16},{18,1... | collective-permute-start | bytes 1474568 | tf_op jit(solution)/shard_map/ppermute | solution.py:45
  270.3 19.3 %copy-start.41 = (s32[8]{0:T(128)S(1)}, s32[8]{0:T(128)}, u32[]{:S(2)}) copy-start(s32[8]{0:T(128)} %param.20) | copy-start | bytes 100
  270.3 24.5 %copy-start.17 = (bf16[96,2560]{1,0:T(8,128)(2,1)S(1)}, bf16[96,2560]{1,0:T(8,128)(2,1)}, u32[]{:S(2)}) copy-start(bf16[96,2560]{1,0:T(8,128)(2,1)} %copy-done.16) | copy-start | bytes 1474564
  270.3 24.5 %copy-start.21 = (bf16[96,2560]{1,0:T(8,128)(2,1)S(1)}, bf16[96,2560]{1,0:T(8,128)(2,1)}, u32[]{:S(2)}) copy-start(bf16[96,2560]{1,0:T(8,128)(2,1)} %copy-done.20) | copy-start | bytes 1474564
  270.3 24.5 %copy-start.27 = (bf16[96,2560]{1,0:T(8,128)(2,1)S(1)}, bf16[96,2560]{1,0:T(8,128)(2,1)}, u32[]{:S(2)}) copy-start(bf16[96,2560]{1,0:T(8,128)(2,1)} %copy-done.26) | copy-start | bytes 1474564
  277.4 28.6 %collective-permute-start.35 = (bf16[96,2560]{1,0:T(8,128)(2,1)S(1)}, bf16[96,2560]{1,0:T(8,128)(2,1)}, u32[]{:S(2)}, u32[]{:S(2)}) collective-permute-start(bf16[96,2560]{1,0:T(8,128)(2,1)S(1)} %get-tuple-element.289), channel_id=1, source_target_pairs={{2,3},{6,7},{10,11},{14,15},{18,19},{22,23},{26,27},{30,31}} | collective-permute-start | bytes 1474568 | tf_op jit(solution)/shard_map/ppermute | solution.py:45
  278.8 27.1 %collective-permute-start.36 = (bf16[96,2560]{1,0:T(8,128)(2,1)S(1)}, bf16[96,2560]{1,0:T(8,128)(2,1)}, u32[]{:S(2)}, u32[]{:S(2)}) collective-permute-start(bf16[96,2560]{1,0:T(8,128)(2,1)S(1)} %get-tuple-element.290), channel_id=1, source_target_pairs={{1,0},{5,4},{9,8},{13,12},{17,16},{21,20},{25,24},{29,28}} | collective-permute-start | bytes 1474568 | tf_op jit(solution)/shard_map/ppermute | solution.py:45
  280.1 25.8 %collective-permute-start.43 = (bf16[96,2560]{1,0:T(8,128)(2,1)}, bf16[96,2560]{1,0:T(8,128)(2,1)}, u32[]{:S(2)}, u32[]{:S(2)}) collective-permute-start(bf16[96,2560]{1,0:T(8,128)(2,1)} %collective-permute-done.42.refs_9_), channel_id=1, source_target_pairs={{2,3},{6,7},{10,11},{14,15},{18,19},{22,23},{26,27},{30,31}} | collective-permute-start | bytes 1474568 | tf_op jit(solution)/shard_map/ppermute | solution.py:45
  288.3 17.6 %collective-permute-start.45 = (bf16[96,2560]{1,0:T(8,128)(2,1)}, bf16[96,2560]{1,0:T(8,128)(2,1)}, u32[]{:S(2)}, u32[]{:S(2)}) collective-permute-start(bf16[96,2560]{1,0:T(8,128)(2,1)} %collective-permute-done.44.refs_12_), channel_id=1, source_target_pairs={{1,0},{5,4},{9,8},{13,12},{17,16},{21,20},{25,24},{29,28}} | collective-permute-start | bytes 1474568 | tf_op jit(solution)/shard_map/ppermute | solution.py:45
  315.9 61.9 %collective-permute-start.2 = (bf16[640,2560]{1,0:T(8,128)(2,1)}, bf16[640,2560]{1,0:T(8,128)(2,1)}, u32[]{:S(2)}, u32[]{:S(2)}) collective-permute-start(bf16[640,2560]{1,0:T(8,128)(2,1)} %get-tuple-element.174), channel_id=1, source_target_pairs={{0,16},{4,20},{8,24},{12,28},{16,0},{20,4},{24,8},{28,12},{1,17},{... | collective-permute-start | bytes 9830408 | tf_op jit(solution)/shard_map/cond/branch_2_fun/ppermute | solution.py:454
  317.6 29.3 %all-to-all-start.4 = ((bf16[4,192,640]{2,1,0:T(8,128)(2,1)}), bf16[4,192,640]{2,1,0:T(8,128)(2,1)S(1)}, u32[]{:S(2)}, u32[]{:S(2)}) async-start(bf16[4,192,640]{2,1,0:T(8,128)(2,1)} %get-tuple-element.175), calls=%async_computation.4 | async-start | bytes 1966080 | tf_op jit(solution)/shard_map/cond/branch_2_fun/all_to_all | solution.py:449
  346.9 18.7 %all-to-all-start.5 = ((bf16[4,192,640]{2,1,0:T(8,128)(2,1)}), bf16[4,192,640]{2,1,0:T(8,128)(2,1)S(1)}, u32[]{:S(2)}, u32[]{:S(2)}) async-start(bf16[4,192,640]{2,1,0:T(8,128)(2,1)} %get-tuple-element.192), calls=%async_computation.5 | async-start | bytes 1966080 | tf_op jit(solution)/shard_map/cond/branch_2_fun/all_to_all | solution.py:449
  (27 other events, 148.5 us)

commit v9 on v8

--- a/solution.py
+++ b/solution.py
@@ -12,7 +12,7 @@
 TOKEN = jax.ShapeDtypeStruct((8, 128), jnp.float32)
 
 
-def call(body, name, grid, ins, outs, scalars=(), scratch=(), flops=0, moved=0, vmem=12, aliases=None):
+def call(body, name, grid, ins, outs, scalars=(), scratch=(), flops=0, moved=0, vmem=12):
     return pl.pallas_call(
         body,
         name=name,
@@ -24,7 +24,6 @@
             out_specs=[pl.BlockSpec(block, place) for _, _, block, place in outs],
             scratch_shapes=scratch,
         ),
-        input_output_aliases=aliases or {},
         compiler_params=pltpu.CompilerParams(vmem_limit_bytes=vmem * MIB),
         cost_estimate=pl.CostEstimate(flops=flops, bytes_accessed=moved, transcendentals=0),
     )(*scalars, *(array for array, _, _ in ins))
@@ -231,17 +230,17 @@
     return jnp.concatenate(rows, axis=0)
 
 
-def unit_ins(units, tile, first=0):
+def unit_ins(units, tile):
     ins = []
     for chunk in units:
         block = (chunk[0].shape[0], tile)
         members = (len(chunk) + 1) // 2
-        ins.append((chunk[0], block, lambda j, s: (0, j + first)))
+        ins.append((chunk[0], block, lambda j, s: (0, j)))
         for k in range(members - 1):
-            place = lambda j, s, k=k: (0, jnp.where(s[0] > k, j, 0) + first)
+            place = lambda j, s, k=k: (0, jnp.where(s[0] > k, j, 0))
             ins.append((chunk[1 + k], block, place))
         for m in range(members - 1):
-            place = lambda j, s, k=members - 2 - m: (0, jnp.where(s[0] > k, 0, j) + first)
+            place = lambda j, s, k=members - 2 - m: (0, jnp.where(s[0] > k, 0, j))
             ins.append((chunk[members + m], block, place))
     return ins
 
@@ -259,15 +258,14 @@
     scratch[...] = stack.T
 
 
-def weight_step(units, mine, order, base, first, last, inbox=None, kept=None, new=False, token=None):
+def weight_step(units, mine, order, base, half=False, inbox=None, token=None):
     members, _, rows = mine[0][0].shape
     width = base.shape[1]
     tile = tile_of(width)
-    last = width // tile if last is None else last
     count = len(units) * len(units[0])
     chunks = len(units)
     total = sum(members * size for _, _, size in mine)
-    early = inbox is None
+    early = inbox is None and not half
 
     def body(s, *refs):
         units_ref, mine_refs = refs[:count], refs[count : count + chunks]
@@ -286,33 +284,30 @@
             refs[-2][...] = jnp.zeros((8, 128), jnp.float32)
         else:
             now = base_ref[...] - 0.5 * 0.004 * weight
-            if new:
+            if inbox is not None:
                 refs[-2][...] = now + refs[count + chunks + 1][...]
             else:
                 refs[-2][...] = now.astype(jnp.bfloat16)
 
-    columns = (rows, tile), lambda j, s: (0, j + first)
-    ins = unit_ins(units, tile, first) + mine_ins(mine) + [(base,) + columns]
-    if new:
+    columns = (rows, tile), lambda j, s: (0, j)
+    ins = unit_ins(units, tile) + mine_ins(mine) + [(base,) + columns]
+    if inbox is not None:
         ins.append((inbox,) + columns)
-    if kept is not None:
-        ins.append((kept, (8, 128), fixed(0, 0)))
     if token is not None:
         ins.append(token_in(token))
-    kind = jnp.float32 if early or new else jnp.bfloat16
+    kind = jnp.bfloat16 if half else jnp.float32
     outs = [((rows, width), kind) + columns]
     return call(
         body,
         "weight_step",
-        (last - first,),
+        (width // tile,),
         ins,
         outs + [TOKEN_OUT] * early,
         scalars=(order,),
         scratch=[pltpu.VMEM((rows, total), jnp.bfloat16)],
-        flops=2 * total * rows * tile * (last - first),
-        moved=(2 * count * units[0][0].shape[0] + 12 * rows) * tile * (last - first),
-        vmem=52,
-        aliases={} if kept is None else {1 + count + chunks + 1: 0},
+        flops=2 * total * rows * width,
+        moved=(2 * count * units[0][0].shape[0] + 12 * rows) * width,
+        vmem=26 if early else 52,
     )
 
 
@@ -375,26 +370,6 @@
     )
 
 
-def passed(right, left, token):
-    size, width = right.shape
-    step = size // 2
-
-    def body(right_ref, left_ref, token_ref, right_out, left_out):
-        right_out[...] = right_ref[...]
-        left_out[...] = left_ref[...]
-
-    here = (step, width), lambda i: (i, 0)
-    flat = ((size, width), right.dtype) + here
-    return call(
-        body,
-        "passed",
-        (size // step,),
-        [(right,) + here, (left,) + here, token_in(token)],
-        [flat, flat],
-        moved=8 * size * width,
-    )
-
-
 def joined_rows(groups):
     members, size, rows = groups[0].shape
     tokens = size * len(groups)
@@ -457,7 +432,7 @@
     back = swapped(grads)
     late_grads, token = grad_rows(late, weights, order)
     late_back = swapped(late_grads)
-    new = weight_step(late, mine, order, kept, 0, None, inbox, new=True, token=token)[0]
+    new = weight_step(late, mine, order, kept, inbox=inbox, token=token)[0]
     return sent, joined_rows([back, late_back]), new
 
 
@@ -479,25 +454,14 @@
     powers = jnp.left_shift(jnp.ones((levels,), jnp.int32), jnp.arange(levels, dtype=jnp.int32))
     level_index = jnp.sum(jnp.where(powers == offset[0], jnp.arange(levels, dtype=jnp.int32), 0))
 
-    arrived = [None] * levels
-    slots = [(0, 1), (1, 0), (1, 1)]
-
-    def levels_of(slot):
-        return [b for b in range(levels) if min(b, len(slots) - 1) == slot]
-
-    def sent_weight(token, b):
-        half = 0.5 * push_weight + token[0, :1]
-        return lax.ppermute(
-            half, "rep", [(i, (i + (1 << b)) % replicas) for i in range(replicas)]
-        )
-
-    def pass_weight(e, t, q, token):
-        if e + 1 == rounds and (t, q) in slots:
-            for b in levels_of(slots.index((t, q))):
-                arrived[b] = sent_weight(token, b)
-
-    def seen(slot):
-        return jnp.broadcast_to(sum(arrived[b] for b in levels_of(slot))[None], (8, 128))
+    half_weight = 0.5 * push_weight
+    arrived = [
+        lax.ppermute(half_weight, "rep", [(i, (i + (1 << b)) % replicas) for i in range(replicas)])
+        for b in range(levels)
+    ]
+    outbox_weight = arrived[0]
+    for b in range(1, levels):
+        outbox_weight = jnp.where(level_index == b, arrived[b], outbox_weight)
 
     order = jnp.mod(me - jnp.arange(members, dtype=jnp.int32), members)
     own = me[None]
@@ -539,7 +503,7 @@
             mine[e][q] = (array, index, size)
 
     for q in range(count):
-        fetch(0, [q], token if q else None)
+        fetch(0, [q], token + outbox_weight[0] if q else None)
     parts = [None] * count
     token = None
     for q in range(count):
@@ -551,22 +515,18 @@
             if e == 0:
                 moving[q] = hops(*hint[q], range(1), range(members - 1, members))
             else:
-                right, left, token = next_payload(*before[q], parts[q], scalars(0), True)
-                pass_weight(e, 0, q, token)
+                right, left, _ = next_payload(*before[q], parts[q], scalars(0), True)
                 moving[q] = hops(right, left, *everyone)
                 units[e - 1][q][1].append(moving[q][0])
                 units[e - 1][q][2].append(moving[q][1])
         for t in range(1, members - 1):
             for q in range(count):
                 order_token = token if (e, t, q) == (0, 1, 0) else None
-                if e + 1 == rounds and (t - 1, q) in slots:
-                    order_token = seen(slots.index((t - 1, q)))
                 right, left, token = next_payload(
                     *moving[q], parts[q], scalars(t), False, order_token
                 )
-                if (t, q) == (1, count - 1) and e + 1 < rounds:
-                    fetch(e + 1, list(range(count)), token)
-                pass_weight(e, t, q, token)
+                if q == count - 1 and t <= count and e + 1 < rounds:
+                    fetch(e + 1, [t - 1], token)
                 if e == 0:
                     pairs = range(t + 1), range(members - 1 - t, members)
                 else:
@@ -580,6 +540,10 @@
             token = None
             if e + 1 < rounds:
                 later[q], token = partial_products(mine[e + 1][q], weights, False)
+            elif q == count - 1:
+                early = [[u] + r + l for of_round in units[:-1] for u, r, l in of_round]
+                early_mine = [m for of_round in mine[:-1] for m in of_round]
+                kept, token = weight_step(early, early_mine, order, numer)
             unit = unit_gradient(
                 *moving[q],
                 parts[q],
@@ -593,23 +557,14 @@
             before[q] = hops(unit, unit, *everyone)
             units[e][q] = (unit, [before[q][0]], [before[q][1]])
         parts = later
-    kept = None
     for s in range(1, members - 1):
         for q in range(count):
-            if (s, q) == (1, count - 1):
-                early = [[u] + r + l for of_round in units[:-1] for u, r, l in of_round]
-                early_mine = [m for of_round in mine[:-1] for m in of_round]
-                kept, done = weight_step(early, early_mine, order, numer, 0, 3)
-                before[q] = passed(*before[q], done)
-            if (s, q) == (2, 0):
-                kept, done = weight_step(early, early_mine, order, numer, 3, None, kept=kept)
-                before[q] = passed(*before[q], done)
             before[q] = hops(*before[q], range(s, members - 1), range(1, members - s))
             units[-1][q][1].append(before[q][0])
             units[-1][q][2].append(before[q][1])
     flat = [[u] + r + l for u, r, l in units[-1]]
     grads, _ = grad_rows(early, weights, order)
-    half = weight_step(flat, mine[-1], order, kept, 0, None, inbox_params[0])[0]
+    half = weight_step(flat, mine[-1], order, kept, half=True)[0]
     new_weight = 0.5 * push_weight + inbox_weight
     branches = [
         partial(
@@ -617,9 +572,6 @@
         )
         for place in range(levels)
     ]
-    outbox_weight = arrived[0]
-    for b in range(1, levels):
-        outbox_weight = jnp.where(level_index == b, arrived[b], outbox_weight)
     sent, grad_heads, new_params = lax.switch(level_index, branches)
     return (new_params[None], new_weight, widened(sent)[None], outbox_weight, grad_heads[None])
 

time: 388 us -> 366 us (0.943)
  waiting for transfers between devices: 112 us -> 99.6 us
  local copies, waits for them, and re-layouts: 17.7 us -> 9.12 us
  starting transfers between devices: 135 us -> 143 us
  Pallas kernels: 109 us -> 103 us
    all_to_all x5 -> x6, starting transfers between devices: 22.2 us -> 30.9 us  [swapped(): return lax.all_to_all(blocks, 'fsdp', 0, 0, tiled=False)]
    pallas_call x32 -> x30, Pallas kernels: 109 us -> 103 us  [call(): pl.pallas_call(body, name=name, out_shape=[jax.ShapeDtypeStruct(shape, ki...]
    ppermute x3, waiting for transfers between devices: 6.25 us -> 0.01 us  [local(): lax.ppermute(half_weight, 'rep', [(i, (i + (1 << b)) % replicas) for i in...]
    all_to_all x5 -> x6, waiting for transfers between devices: 30.6 us -> 24.8 us  [swapped(): return lax.all_to_all(blocks, 'fsdp', 0, 0, tiled=False)]
    unnamed x84, local copies, waits for them, and re-layouts: 14.2 us -> 9.11 us
  transfers between devices with their start and end apart: 49 -> 50, of which waited for: 18 -> 20; matrix products, arithmetic and copies ran while one was open for 1% -> 0% of each run, Pallas kernels for 22% -> 22%
where the time goes in v9:
time: 366 us; the launch traced here: 365 us
  starting transfers between devices  143 us (39%)
  Pallas kernels  103 us (28%)
  waiting for transfers between devices  99.6 us (27%)
  local copies, waits for them, and re-layouts  9.12 us (2%)
  between operations  8.81 us (2%)
    ppermute x40, starting transfers between devices, hop(): return lax.ppermute(value, 'fsdp', [(i, i + step) for i in pairs])  103 us
    pallas_call x30, Pallas kernels, call(): pl.pallas_call(body, name=name, out_shape=[jax.ShapeDtypeStruct(shape, ki...  103 us
    ppermute x40, waiting for transfers between devices, hop(): return lax.ppermute(value, 'fsdp', [(i, i + step) for i in pairs])  64.2 us
    all_to_all x6, starting transfers between devices, swapped(): return lax.all_to_all(blocks, 'fsdp', 0, 0, tiled=False)  30.9 us
    all_to_all x6, waiting for transfers between devices, swapped(): return lax.all_to_all(blocks, 'fsdp', 0, 0, tiled=False)  24.8 us
    ppermute x1, waiting for transfers between devices, tail(): lax.ppermute(half, 'rep', [(i, (i + (1 << bit_place)) % length) for i in...  10.6 us
    unnamed x84, local copies, waits for them, and re-layouts  9.11 us
  transfers between devices with their start and end apart: 50, of which 20 were waited for; matrix products, arithmetic and copies ran while one was open for 0% of the time, Pallas kernels for 22%

profile of v9, /device:TPU:0, one launch (start us, length us, event | category | flops | bytes accessed | tf_op | source)
XLA Modules:
  0.0 364.6 jit_solution(12080511133267089601)
XLA Ops:
  0.6 1.8 cut_heads.4
  2.4 6.3 %all-to-all-start.6 = ((bf16[4,96,640]{2,1,0:T(8,128)(2,1)}), bf16[4,96,640]{2,1,0:T(8,128)(2,1)S(1)}, u32[]{:S(2)}, u32[]{:S(2)}) async-start(bf16[4,96,640]{2,1,0:T(8,128)(2,1)} %cut_heads.4), calls=%async_computation.6 | async-start | bytes 983040 | tf_op jit(solution)/shard_map/all_to_all | solution.py:424
  10.4 2.8 collective-permute-start.6
  13.2 2.8 collective-permute-start.5
  18.0 5.7 %scaled_weights.1 = (bf16[640,2560]{1,0:T(8,128)(2,1)}, f32[8,128]{1,0:T(8,128)}) custom-call(f32[640,2560]{1,0:T(8,128)} %bitcast.44, f32[1,1]{1,0:T(1,128)} %bitcast.31.one_ref), custom_call_target="tpu_custom_call" | custom-call | flops 3276800 | bytes 9830400 | tf_op jit(solution)/shard_map/scaled_weights/pallas_call | solution.py:16
  27.1 5.1 %all-to-all-start.7 = ((bf16[4,96,640]{2,1,0:T(8,128)(2,1)}), bf16[4,96,640]{2,1,0:T(8,128)(2,1)S(1)}, u32[]{:S(2)}, u32[]{:S(2)}) async-start(bf16[4,96,640]{2,1,0:T(8,128)(2,1)} %cut_heads.5), calls=%async_computation.7 | async-start | bytes 983040 | tf_op jit(solution)/shard_map/all_to_all | solution.py:424
  32.2 3.5 partial_products.4
  37.8 7.0 %all-to-all-done.7.mine_ref.refs_15_ = bf16[4,96,640]{2,1,0:T(8,128)(2,1)S(1)} async-done(((bf16[4,96,640]{2,1,0:T(8,128)(2,1)}), bf16[4,96,640]{2,1,0:T(8,128)(2,1)S(1)}, u32[]{:S(2)}, u32[]{:S(2)}) %all-to-all-start.7) | async-done | bytes 491552 | tf_op jit(solution)/shard_map/all_to_all | solution.py:424
  44.8 4.4 %partial_products.5 = (bf16[4,96,2560]{2,1,0:T(8,128)(2,1)S(1)}, f32[8,128]{1,0:T(8,128)S(1)}, bf16[96,2560]{1,0:T(8,128)(2,1)}, bf16[96,2560]{1,0:T(8,128)(2,1)}) custom-call(bf16[4,96,640]{2,1,0:T(8,128)(2,1)S(1)} %all-to-all-done.7.mine_ref.refs_15_, bf16[640,2560]{1,0:T(8,128)(2,1)} %get-tuple-element.253.weights_ref.refs_14_, ...), custom_call_target="tpu_custom_call" | custom-call | flops 1258291200 | bytes 5734400 | tf_op jit(solution)/shard_map/partial_products/pallas_call | solution.py:16
  50.5 1.5 collective-permute-start.13
  53.5 1.5 collective-permute-start.4
  55.0 7.4 %collective-permute-done.12.right_ref = bf16[96,2560]{1,0:T(8,128)(2,1)S(1)} collective-permute-done((bf16[96,2560]{1,0:T(8,128)(2,1)}, bf16[96,2560]{1,0:T(8,128)(2,1)S(1)}, u32[]{:S(2)}, u32[]{:S(2)}) %collective-permute-start.12) | collective-permute-done | bytes 491552 | tf_op jit(solution)/shard_map/ppermute | solution.py:44
  62.5 1.8 next_payload.12
  66.8 4.7 %all-to-all-start.8 = ((bf16[4,96,640]{2,1,0:T(8,128)(2,1)}), bf16[4,96,640]{2,1,0:T(8,128)(2,1)}, u32[]{:S(2)}, u32[]{:S(2)}) async-start(bf16[4,96,640]{2,1,0:T(8,128)(2,1)} %cut_heads.6), calls=%async_computation.8 | async-start | bytes 983040 | tf_op jit(solution)/shard_map/all_to_all | solution.py:424
  71.5 3.9 %collective-permute-start.28 = (bf16[96,2560]{1,0:T(8,128)(2,1)}, bf16[96,2560]{1,0:T(8,128)(2,1)S(1)}, u32[]{:S(2)}, u32[]{:S(2)}) collective-permute-start(bf16[96,2560]{1,0:T(8,128)(2,1)} %copy-done.36), channel_id=1, source_target_pairs={{0,1},{1,2},{4,5},{5,6},{8,9},{9,10},{12,13},{13,14},{16,17},{17,1... | collective-permute-start | bytes 1474568 | tf_op jit(solution)/shard_map/ppermute | solution.py:44
  76.2 1.5 copy-done.5
  77.7 2.5 next_payload.10
  80.2 4.0 %collective-permute-start.8 = (bf16[96,2560]{1,0:T(8,128)(2,1)}, bf16[96,2560]{1,0:T(8,128)(2,1)S(1)}, u32[]{:S(2)}, u32[]{:S(2)}) collective-permute-start(bf16[96,2560]{1,0:T(8,128)(2,1)} %get-tuple-element.260), channel_id=1, source_target_pairs={{0,1},{1,2},{4,5},{5,6},{8,9},{9,10},{12,13},{13,14},{16,17},{17,1... | collective-permute-start | bytes 1474568 | tf_op jit(solution)/shard_map/ppermute | solution.py:44
  85.7 5.7 %collective-permute-done.28.right_ref = bf16[96,2560]{1,0:T(8,128)(2,1)S(1)} collective-permute-done((bf16[96,2560]{1,0:T(8,128)(2,1)}, bf16[96,2560]{1,0:T(8,128)(2,1)S(1)}, u32[]{:S(2)}, u32[]{:S(2)}) %collective-permute-start.28) | collective-permute-done | bytes 491552 | tf_op jit(solution)/shard_map/ppermute | solution.py:44
  91.5 1.6 next_payload.16
  94.0 6.6 %all-to-all-start.9 = ((bf16[4,96,640]{2,1,0:T(8,128)(2,1)}), bf16[4,96,640]{2,1,0:T(8,128)(2,1)}, u32[]{:S(2)}, u32[]{:S(2)}) async-start(bf16[4,96,640]{2,1,0:T(8,128)(2,1)} %cut_heads.7), calls=%async_computation.9 | async-start | bytes 983040 | tf_op jit(solution)/shard_map/all_to_all | solution.py:424
  102.0 1.5 copy-done.6
  103.5 2.4 next_payload.11
  105.9 12.1 %collective-permute-start.10 = (bf16[96,2560]{1,0:T(8,128)(2,1)S(1)}, bf16[96,2560]{1,0:T(8,128)(2,1)S(1)}, u32[]{:S(2)}, u32[]{:S(2)}) collective-permute-start(bf16[96,2560]{1,0:T(8,128)(2,1)S(1)} %get-tuple-element.262), channel_id=1, source_target_pairs={{0,1},{1,2},{2,3},{4,5},{5,6},{6,7},{8,9},{9,10},{10,11},{12,13},{... | collective-permute-start | bytes 1474568 | tf_op jit(solution)/shard_map/ppermute | solution.py:44
  119.3 5.4 %collective-permute-start.30 = (bf16[96,2560]{1,0:T(8,128)(2,1)}, bf16[96,2560]{1,0:T(8,128)(2,1)}, u32[]{:S(2)}, u32[]{:S(2)}) collective-permute-start(bf16[96,2560]{1,0:T(8,128)(2,1)} %get-tuple-element.278), channel_id=1, source_target_pairs={{0,1},{1,2},{2,3},{4,5},{5,6},{6,7},{8,9},{9,10},{10,11},{12,13},{... | collective-permute-start | bytes 1474568 | tf_op jit(solution)/shard_map/ppermute | solution.py:44
  125.9 3.5 partial_products.6
  129.5 4.5 %collective-permute-done.11.left_ref = bf16[96,2560]{1,0:T(8,128)(2,1)S(1)} collective-permute-done((bf16[96,2560]{1,0:T(8,128)(2,1)S(1)}, bf16[96,2560]{1,0:T(8,128)(2,1)S(1)}, u32[]{:S(2)}, u32[]{:S(2)}) %collective-permute-start.11) | collective-permute-done | bytes 491552 | tf_op jit(solution)/shard_map/ppermute | solution.py:44
  136.0 4.6 %collective-permute-start.14 = (bf16[96,2560]{1,0:T(8,128)(2,1)S(1)}, bf16[96,2560]{1,0:T(8,128)(2,1)S(1)}, u32[]{:S(2)}, u32[]{:S(2)}) collective-permute-start(bf16[96,2560]{1,0:T(8,128)(2,1)S(1)} %unit_gradient.4.refs_0_), channel_id=1, source_target_pairs={{0,1},{1,2},{2,3},{4,5},{5,6},{6,7},{8,9},{9,10},{10,11},{12,13},{... | collective-permute-start | bytes 1474568 | tf_op jit(solution)/shard_map/ppermute | solution.py:44
  140.6 3.7 %partial_products.7 = (bf16[4,96,2560]{2,1,0:T(8,128)(2,1)S(1)}, f32[8,128]{1,0:T(8,128)S(1)}) custom-call(bf16[4,96,640]{2,1,0:T(8,128)(2,1)} %all-to-all-done.9.mine_ref.refs_15_, bf16[640,2560]{1,0:T(8,128)(2,1)} %get-tuple-element.253.weights_ref.refs_14_), custom_call_target="tpu_custom_call" | custom-call | flops 1258291200 | bytes 5734400 | tf_op jit(solution)/shard_map/partial_products/pallas_call | solution.py:16
  144.4 2.2 copy-done.15
  146.6 2.4 unit_gradient.6.refs_7_
  150.3 5.4 %collective-permute-start.32 = (bf16[96,2560]{1,0:T(8,128)(2,1)}, bf16[96,2560]{1,0:T(8,128)(2,1)}, u32[]{:S(2)}, u32[]{:S(2)}) collective-permute-start(bf16[96,2560]{1,0:T(8,128)(2,1)} %unit_gradient.6.refs_7_), channel_id=1, source_target_pairs={{0,1},{1,2},{2,3},{4,5},{5,6},{6,7},{8,9},{9,10},{10,11},{12,13},{... | collective-permute-start | bytes 1474568 | tf_op jit(solution)/shard_map/ppermute | solution.py:44
  159.6 1.9 collective-permute-done.33.left_ref.refs_11_
  161.4 4.6 %collective-permute-done.32.right_ref.refs_8_ = bf16[96,2560]{1,0:T(8,128)(2,1)} collective-permute-done((bf16[96,2560]{1,0:T(8,128)(2,1)}, bf16[96,2560]{1,0:T(8,128)(2,1)}, u32[]{:S(2)}, u32[]{:S(2)}) %collective-permute-start.32) | collective-permute-done | bytes 491552 | tf_op jit(solution)/shard_map/ppermute | solution.py:44
  166.0 2.5 next_payload.17
  168.5 4.4 %collective-permute-start.34 = (bf16[96,2560]{1,0:T(8,128)(2,1)S(1)}, bf16[96,2560]{1,0:T(8,128)(2,1)S(1)}, u32[]{:S(2)}, u32[]{:S(2)}) collective-permute-start(bf16[96,2560]{1,0:T(8,128)(2,1)S(1)} %get-tuple-element.283), channel_id=1, source_target_pairs={{0,1},{1,2},{2,3},{4,5},{5,6},{6,7},{8,9},{9,10},{10,11},{12,13},{... | collective-permute-start | bytes 1474568 | tf_op jit(solution)/shard_map/ppermute | solution.py:44
  174.2 2.3 collective-permute-done.16.right_ref.refs_2_
  177.8 4.4 %collective-permute-start.18 = (bf16[96,2560]{1,0:T(8,128)(2,1)S(1)}, bf16[96,2560]{1,0:T(8,128)(2,1)S(1)}, u32[]{:S(2)}, u32[]{:S(2)}) collective-permute-start(bf16[96,2560]{1,0:T(8,128)(2,1)S(1)} %get-tuple-element.272), channel_id=1, source_target_pairs={{0,1},{1,2},{2,3},{4,5},{5,6},{6,7},{8,9},{9,10},{10,11},{12,13},{... | collective-permute-start | bytes 1474568 | tf_op jit(solution)/shard_map/ppermute | solution.py:44
  183.5 3.5 collective-permute-done.34.right_ref.refs_9_
  188.3 4.5 %collective-permute-start.36 = (bf16[96,2560]{1,0:T(8,128)(2,1)S(1)}, bf16[96,2560]{1,0:T(8,128)(2,1)S(1)}, u32[]{:S(2)}, u32[]{:S(2)}) collective-permute-start(bf16[96,2560]{1,0:T(8,128)(2,1)S(1)} %get-tuple-element.285), channel_id=1, source_target_pairs={{0,1},{1,2},{2,3},{4,5},{5,6},{6,7},{8,9},{9,10},{10,11},{12,13},{... | collective-permute-start | bytes 1474568 | tf_op jit(solution)/shard_map/ppermute | solution.py:44
  194.3 3.2 collective-permute-done.18.right_ref.refs_3_
  199.6 3.8 %collective-permute-start.20 = (bf16[96,2560]{1,0:T(8,128)(2,1)S(1)}, bf16[96,2560]{1,0:T(8,128)(2,1)S(1)}, u32[]{:S(2)}, u32[]{:S(2)}) collective-permute-start(bf16[96,2560]{1,0:T(8,128)(2,1)S(1)} %get-tuple-element.274), channel_id=1, source_target_pairs={{0,1},{1,2},{2,3},{4,5},{5,6},{6,7},{8,9},{9,10},{10,11},{12,13},{... | collective-permute-start | bytes 1474568 | tf_op jit(solution)/shard_map/ppermute | solution.py:44
  204.7 3.4 collective-permute-done.36.right_ref.refs_10_
  210.4 3.4 collective-permute-start.38
  215.3 8.2 %weight_step.8 = (f32[640,2560]{1,0:T(8,128)}, f32[8,128]{1,0:T(8,128)S(1)}) custom-call(s32[4]{0:T(128)S(1)} %and_select_fusion.s, bf16[96,2560]{1,0:T(8,128)(2,1)S(1)} %unit_gradient.4.refs_0_, bf16[96,2560]{1,0:T(8,128)(2,1)S(1)} %collective-permute-done.14.right_ref.refs_1_, bf16[96,2560]{1,0:T(8,128)(2,1)S(1)} %collective-permute-done.16.right_ref.refs_2_, ...), custom_call_target="tpu_custom_call" | custom-call | flops 2516582400 | bytes 26542080 | tf_op jit(solution)/shard_map/weight_step/pallas_call | solution.py:16
  226.1 6.2 %collective-permute-start.22 = (bf16[96,2560]{1,0:T(8,128)(2,1)}, bf16[96,2560]{1,0:T(8,128)(2,1)}, u32[]{:S(2)}, u32[]{:S(2)}) collective-permute-start(bf16[96,2560]{1,0:T(8,128)(2,1)} %unit_gradient.5.refs_0_), channel_id=1, source_target_pairs={{0,1},{1,2},{2,3},{4,5},{5,6},{6,7},{8,9},{9,10},{10,11},{12,13},{... | collective-permute-start | bytes 1474568 | tf_op jit(solution)/shard_map/ppermute | solution.py:44
  235.1 5.3 %collective-permute-start.40 = (bf16[96,2560]{1,0:T(8,128)(2,1)}, bf16[96,2560]{1,0:T(8,128)(2,1)}, u32[]{:S(2)}, u32[]{:S(2)}) collective-permute-start(bf16[96,2560]{1,0:T(8,128)(2,1)} %unit_gradient.7.refs_7_), channel_id=1, source_target_pairs={{0,1},{1,2},{2,3},{4,5},{5,6},{6,7},{8,9},{9,10},{10,11},{12,13},{... | collective-permute-start | bytes 1474568 | tf_op jit(solution)/shard_map/ppermute | solution.py:44
  240.4 1.7 collective-permute-done.25.refs_4_
  244.8 7.8 %collective-permute-done.43.refs_11_ = bf16[96,2560]{1,0:T(8,128)(2,1)} collective-permute-done((bf16[96,2560]{1,0:T(8,128)(2,1)}, bf16[96,2560]{1,0:T(8,128)(2,1)}, u32[]{:S(2)}, u32[]{:S(2)}) %collective-permute-start.43) | collective-permute-done | bytes 491552 | tf_op jit(solution)/shard_map/ppermute | solution.py:44
  253.9 1.5 collective-permute-start.41
  255.4 7.8 %collective-permute-done.26.refs_5_ = bf16[96,2560]{1,0:T(8,128)(2,1)} collective-permute-done((bf16[96,2560]{1,0:T(8,128)(2,1)}, bf16[96,2560]{1,0:T(8,128)(2,1)}, u32[]{:S(2)}, u32[]{:S(2)}) %collective-permute-start.26) | collective-permute-done | bytes 491552 | tf_op jit(solution)/shard_map/ppermute | solution.py:44
  265.9 7.4 %collective-permute-done.44.refs_12_ = bf16[96,2560]{1,0:T(8,128)(2,1)} collective-permute-done((bf16[96,2560]{1,0:T(8,128)(2,1)}, bf16[96,2560]{1,0:T(8,128)(2,1)}, u32[]{:S(2)}, u32[]{:S(2)}) %collective-permute-start.44) | collective-permute-done | bytes 491552 | tf_op jit(solution)/shard_map/ppermute | solution.py:44
  277.4 9.1 %grad_rows.7 = (bf16[4,192,640]{2,1,0:T(8,128)(2,1)}, f32[8,128]{1,0:T(8,128)}) custom-call(s32[4]{0:T(128)S(1)} %and_select_fusion.s, bf16[96,2560]{1,0:T(8,128)(2,1)S(1)} %unit_gradient.4.refs_0_, bf16[96,2560]{1,0:T(8,128)(2,1)S(1)} %collective-permute-done.14.right_ref.refs_1_, bf16[96,2560]{1,0:T(8,128)(2,1)S(1)} %copy-done.18, ...), custom_call_target="tpu_custom_call" | custom-call | flops 2516582400 | bytes 10158080 | tf_op jit(solution)/shard_map/grad_rows/pallas_call | solution.py:16
  286.5 10.0 %weight_step.9 = bf16[640,2560]{1,0:T(8,128)(2,1)} custom-call(s32[4]{0:T(128)S(1)} %and_select_fusion.s, bf16[96,2560]{1,0:T(8,128)(2,1)} %unit_gradient.5.refs_0_, bf16[96,2560]{1,0:T(8,128)(2,1)} %collective-permute-done.22.refs_1_, bf16[96,2560]{1,0:T(8,128)(2,1)} %collective-permute-done.23.refs_2_, bf16[96,2560]{1,0:T(8,128)(2,1)} %collective-permute-done.24.refs_3_, ...), custom_call_target="tpu_custom_call" | custom-call | flops 2516582400 | bytes 26542080 | tf_op jit(solution)/shard_map/weight_step/pallas_call | solution.py:16
  296.4 60.8 %conditional.1 = (bf16[640,2560]{1,0:T(8,128)(2,1)}, bf16[1,384,2560]{2,1,0:T(8,128)(2,1)S(1)}, f32[1,640,2560]{2,1,0:T(8,128)}) conditional(s32[]{:T(128)} %clamp.3, (bf16[640,2560]{1,0:T(8,128)(2,1)}, bf16[4,192,640]{2,1,0:T(8,128)(2,1)}, s32[4]{0:T(128)S(1)}, bf16[96,2560]{1,0:T(8,128)(2,1)}, bf16[96,2560]{1,0:T(8,128)(2,1)}, ...), branch_computations={%region_1.2_spmd, %region_2.3_spmd, %region_3.4_spmd} | conditional | flops 5033164800 | bytes 59637888 | solution.py:575
  296.5 2.0 collective-permute-start.1
  298.4 4.7 %all-to-all-start.2 = ((bf16[4,192,640]{2,1,0:T(8,128)(2,1)}), bf16[4,192,640]{2,1,0:T(8,128)(2,1)S(1)}, u32[]{:S(2)}, u32[]{:S(2)}) async-start(bf16[4,192,640]{2,1,0:T(8,128)(2,1)} %get-tuple-element.159), calls=%async_computation.2 | async-start | bytes 1966080 | tf_op jit(solution)/shard_map/cond/branch_1_fun/all_to_all | solution.py:424
  303.1 9.4 %grad_rows.5 = (bf16[4,192,640]{2,1,0:T(8,128)(2,1)}, f32[8,128]{1,0:T(8,128)S(1)}) custom-call(s32[4]{0:T(128)S(1)} %get-tuple-element.160.s, bf16[96,2560]{1,0:T(8,128)(2,1)} %get-tuple-element.161.refs_0_, bf16[96,2560]{1,0:T(8,128)(2,1)} %get-tuple-element.162.refs_1_, bf16[96,2560]{1,0:T(8,128)(2,1)} %get-tuple-element.163.refs_2_, ...), custom_call_target="tpu_custom_call" | custom-call | flops 2516582400 | bytes 10158080 | tf_op jit(solution)/shard_map/cond/branch_1_fun/grad_rows/pallas_call | solution.py:16
  312.5 15.3 %all-to-all-done.2.refs_0_ = bf16[4,192,640]{2,1,0:T(8,128)(2,1)S(1)} async-done(((bf16[4,192,640]{2,1,0:T(8,128)(2,1)}), bf16[4,192,640]{2,1,0:T(8,128)(2,1)S(1)}, u32[]{:S(2)}, u32[]{:S(2)}) %all-to-all-start.2) | async-done | bytes 983072 | tf_op jit(solution)/shard_map/cond/branch_1_fun/all_to_all | solution.py:424
  327.8 3.5 all-to-all-start.3
  331.3 12.6 %weight_step.6 = f32[640,2560]{1,0:T(8,128)} custom-call(s32[4]{0:T(128)S(1)} %get-tuple-element.160.s, bf16[96,2560]{1,0:T(8,128)(2,1)} %get-tuple-element.161.refs_0_, bf16[96,2560]{1,0:T(8,128)(2,1)} %get-tuple-element.162.refs_1_, bf16[96,2560]{1,0:T(8,128)(2,1)} %get-tuple-element.163.refs_2_, bf16[96,2560]{1,0:T(8,128)(2,1)} %get-tuple-element.164.refs_3_, ...), custom_call_target="tpu_custom_call" | custom-call | flops 2516582400 | bytes 26542080 | tf_op jit(solution)/shard_map/cond/branch_1_fun/weight_step/pallas_call | solution.py:16
  343.9 2.5 all-to-all-done.3.refs_1_
  346.7 10.6 %collective-permute-done.1 = bf16[640,2560]{1,0:T(8,128)(2,1)} collective-permute-done((bf16[640,2560]{1,0:T(8,128)(2,1)}, bf16[640,2560]{1,0:T(8,128)(2,1)}, u32[]{:S(2)}, u32[]{:S(2)}) %collective-permute-start.1) | collective-permute-done | bytes 3276832 | tf_op jit(solution)/shard_map/cond/branch_1_fun/ppermute | solution.py:429
  357.2 5.1 %widened.1 = f32[640,2560]{1,0:T(8,128)} custom-call(bf16[640,2560]{1,0:T(8,128)(2,1)} %get-tuple-element.293.value_ref), custom_call_target="tpu_custom_call" | custom-call | bytes 9830400 | tf_op jit(solution)/shard_map/widened/pallas_call | solution.py:16
  (159 shorter events, 53.5 us)
Async XLA Ops:
  2.4 24.7 %all-to-all-start.6 = ((bf16[4,96,640]{2,1,0:T(8,128)(2,1)}), bf16[4,96,640]{2,1,0:T(8,128)(2,1)S(1)}, u32[]{:S(2)}, u32[]{:S(2)}) async-start(bf16[4,96,640]{2,1,0:T(8,128)(2,1)} %cut_heads.4), calls=%async_computation.6 | async-start | bytes 983040 | tf_op jit(solution)/shard_map/all_to_all | solution.py:424
  9.4 14.3 %collective-permute-start.7 = (f32[1]{0:T(128)}, f32[1]{0:T(128)}, u32[]{:S(2)}, u32[]{:S(2)}) collective-permute-start(f32[1]{0:T(128)} %mul.4), channel_id=1, source_target_pairs={{0,4},{4,8},{8,12},{12,16},{16,20},{20,24},{24,28},{28,0},{1,5},{5... | collective-permute-start | bytes 20 | tf_op jit(solution)/shard_map/ppermute | solution.py:459
  10.4 13.3 %collective-permute-start.6 = (f32[1]{0:T(128)}, f32[1]{0:T(128)}, u32[]{:S(2)}, u32[]{:S(2)}) collective-permute-start(f32[1]{0:T(128)} %mul.4), channel_id=1, source_target_pairs={{0,8},{4,12},{8,16},{12,20},{16,24},{20,28},{24,0},{28,4},{1,9},{5... | collective-permute-start | bytes 20 | tf_op jit(solution)/shard_map/ppermute | solution.py:459
  13.2 11.8 %collective-permute-start.5 = (f32[1]{0:T(128)}, f32[1]{0:T(128)}, u32[]{:S(2)}, u32[]{:S(2)}) collective-permute-start(f32[1]{0:T(128)} %mul.4), channel_id=1, source_target_pairs={{0,16},{4,20},{8,24},{12,28},{16,0},{20,4},{24,8},{28,12},{1,17},{... | collective-permute-start | bytes 20 | tf_op jit(solution)/shard_map/ppermute | solution.py:459
  27.1 17.7 %all-to-all-start.7 = ((bf16[4,96,640]{2,1,0:T(8,128)(2,1)}), bf16[4,96,640]{2,1,0:T(8,128)(2,1)S(1)}, u32[]{:S(2)}, u32[]{:S(2)}) async-start(bf16[4,96,640]{2,1,0:T(8,128)(2,1)} %cut_heads.5), calls=%async_computation.7 | async-start | bytes 983040 | tf_op jit(solution)/shard_map/all_to_all | solution.py:424
  49.2 42.2 %copy-start.2 = (bf16[4,96,2560]{2,1,0:T(8,128)(2,1)}, bf16[4,96,2560]{2,1,0:T(8,128)(2,1)S(1)}, u32[]{:S(2)}) copy-start(bf16[4,96,2560]{2,1,0:T(8,128)(2,1)S(1)} %get-tuple-element.266.of_right.of_left.own_ref) | copy-start | bytes 5898244
  49.2 13.3 %collective-permute-start.12 = (bf16[96,2560]{1,0:T(8,128)(2,1)}, bf16[96,2560]{1,0:T(8,128)(2,1)S(1)}, u32[]{:S(2)}, u32[]{:S(2)}) collective-permute-start(bf16[96,2560]{1,0:T(8,128)(2,1)} %get-tuple-element.264), channel_id=1, source_target_pairs={{0,1},{4,5},{8,9},{12,13},{16,17},{20,21},{24,25},{28,29}} | collective-permute-start | bytes 1474568 | tf_op jit(solution)/shard_map/ppermute | solution.py:44
  50.5 12.0 %collective-permute-start.13 = (bf16[96,2560]{1,0:T(8,128)(2,1)}, bf16[96,2560]{1,0:T(8,128)(2,1)}, u32[]{:S(2)}, u32[]{:S(2)}) collective-permute-start(bf16[96,2560]{1,0:T(8,128)(2,1)} %get-tuple-element.265), channel_id=1, source_target_pairs={{3,2},{7,6},{11,10},{15,14},{19,18},{23,22},{27,26},{31,30}} | collective-permute-start | bytes 1474568 | tf_op jit(solution)/shard_map/ppermute | solution.py:44
  52.1 24.1 %collective-permute-start.3 = (bf16[96,2560]{1,0:T(8,128)(2,1)}, bf16[96,2560]{1,0:T(8,128)(2,1)S(1)}, u32[]{:S(2)}, u32[]{:S(2)}) collective-permute-start(bf16[96,2560]{1,0:T(8,128)(2,1)} %copy-done.34), channel_id=1, source_target_pairs={{0,1},{4,5},{8,9},{12,13},{16,17},{20,21},{24,25},{28,29}} | collective-permute-start | bytes 1474568 | tf_op jit(solution)/shard_map/ppermute | solution.py:44
  53.5 22.6 %collective-permute-start.4 = (bf16[96,2560]{1,0:T(8,128)(2,1)}, bf16[96,2560]{1,0:T(8,128)(2,1)}, u32[]{:S(2)}, u32[]{:S(2)}) collective-permute-start(bf16[96,2560]{1,0:T(8,128)(2,1)} %copy-done.33), channel_id=1, source_target_pairs={{3,2},{7,6},{11,10},{15,14},{19,18},{23,22},{27,26},{31,30}} | collective-permute-start | bytes 1474568 | tf_op jit(solution)/shard_map/ppermute | solution.py:44
  66.8 27.2 %all-to-all-start.8 = ((bf16[4,96,640]{2,1,0:T(8,128)(2,1)}), bf16[4,96,640]{2,1,0:T(8,128)(2,1)}, u32[]{:S(2)}, u32[]{:S(2)}) async-start(bf16[4,96,640]{2,1,0:T(8,128)(2,1)} %cut_heads.6), calls=%async_computation.8 | async-start | bytes 983040 | tf_op jit(solution)/shard_map/all_to_all | solution.py:424
  71.5 20.0 %collective-permute-start.28 = (bf16[96,2560]{1,0:T(8,128)(2,1)}, bf16[96,2560]{1,0:T(8,128)(2,1)S(1)}, u32[]{:S(2)}, u32[]{:S(2)}) collective-permute-start(bf16[96,2560]{1,0:T(8,128)(2,1)} %copy-done.36), channel_id=1, source_target_pairs={{0,1},{1,2},{4,5},{5,6},{8,9},{9,10},{12,13},{13,14},{16,17},{17,1... | collective-permute-start | bytes 1474568 | tf_op jit(solution)/shard_map/ppermute | solution.py:44
  75.4 16.0 %collective-permute-start.29 = (bf16[96,2560]{1,0:T(8,128)(2,1)}, bf16[96,2560]{1,0:T(8,128)(2,1)S(1)}, u32[]{:S(2)}, u32[]{:S(2)}) collective-permute-start(bf16[96,2560]{1,0:T(8,128)(2,1)} %copy-done.35), channel_id=1, source_target_pairs={{2,1},{3,2},{6,5},{7,6},{10,9},{11,10},{14,13},{15,14},{18,17},{19... | collective-permute-start | bytes 1474568 | tf_op jit(solution)/shard_map/ppermute | solution.py:44
  80.2 21.8 %collective-permute-start.8 = (bf16[96,2560]{1,0:T(8,128)(2,1)}, bf16[96,2560]{1,0:T(8,128)(2,1)S(1)}, u32[]{:S(2)}, u32[]{:S(2)}) collective-permute-start(bf16[96,2560]{1,0:T(8,128)(2,1)} %get-tuple-element.260), channel_id=1, source_target_pairs={{0,1},{1,2},{4,5},{5,6},{8,9},{9,10},{12,13},{13,14},{16,17},{17,1... | collective-permute-start | bytes 1474568 | tf_op jit(solution)/shard_map/ppermute | solution.py:44
  84.2 17.8 %collective-permute-start.9 = (bf16[96,2560]{1,0:T(8,128)(2,1)}, bf16[96,2560]{1,0:T(8,128)(2,1)}, u32[]{:S(2)}, u32[]{:S(2)}) collective-permute-start(bf16[96,2560]{1,0:T(8,128)(2,1)} %get-tuple-element.261), channel_id=1, source_target_pairs={{2,1},{3,2},{6,5},{7,6},{10,9},{11,10},{14,13},{15,14},{18,17},{19... | collective-permute-start | bytes 1474568 | tf_op jit(solution)/shard_map/ppermute | solution.py:44
  94.0 31.9 %copy-start.38 = (f32[2560]{0:T(1024)S(1)}, f32[2560]{0:T(1024)}, u32[]{:S(2)}) copy-start(f32[2560]{0:T(1024)} %param.19) | copy-start | bytes 30724
  94.0 46.6 %all-to-all-start.9 = ((bf16[4,96,640]{2,1,0:T(8,128)(2,1)}), bf16[4,96,640]{2,1,0:T(8,128)(2,1)}, u32[]{:S(2)}, u32[]{:S(2)}) async-start(bf16[4,96,640]{2,1,0:T(8,128)(2,1)} %cut_heads.7), calls=%async_computation.9 | async-start | bytes 983040 | tf_op jit(solution)/shard_map/all_to_all | solution.py:424
  103.5 30.5 %copy-start.14 = (bf16[1,384,2560]{2,1,0:T(8,128)(2,1)S(1)}, bf16[1,384,2560]{2,1,0:T(8,128)(2,1)}, u32[]{:S(2)}) copy-start(bf16[1,384,2560]{2,1,0:T(8,128)(2,1)} %param.18) | copy-start | bytes 5898244
  105.9 28.1 %copy-start.7 = (bf16[4,96,2560]{2,1,0:T(8,128)(2,1)S(1)}, bf16[4,96,2560]{2,1,0:T(8,128)(2,1)}, u32[]{:S(2)}) copy-start(bf16[4,96,2560]{2,1,0:T(8,128)(2,1)} %copy-done.4) | copy-start | bytes 5898244
  105.9 28.1 %copy-start.11 = (bf16[1,384,2560]{2,1,0:T(8,128)(2,1)S(1)}, bf16[1,384,2560]{2,1,0:T(8,128)(2,1)}, u32[]{:S(2)}) copy-start(bf16[1,384,2560]{2,1,0:T(8,128)(2,1)} %param.17) | copy-start | bytes 5898244
  105.9 23.6 %collective-permute-start.10 = (bf16[96,2560]{1,0:T(8,128)(2,1)S(1)}, bf16[96,2560]{1,0:T(8,128)(2,1)S(1)}, u32[]{:S(2)}, u32[]{:S(2)}) collective-permute-start(bf16[96,2560]{1,0:T(8,128)(2,1)S(1)} %get-tuple-element.262), channel_id=1, source_target_pairs={{0,1},{1,2},{2,3},{4,5},{5,6},{6,7},{8,9},{9,10},{10,11},{12,13},{... | collective-permute-start | bytes 1474568 | tf_op jit(solution)/shard_map/ppermute | solution.py:44
  118.0 16.1 %collective-permute-start.11 = (bf16[96,2560]{1,0:T(8,128)(2,1)S(1)}, bf16[96,2560]{1,0:T(8,128)(2,1)S(1)}, u32[]{:S(2)}, u32[]{:S(2)}) collective-permute-start(bf16[96,2560]{1,0:T(8,128)(2,1)S(1)} %get-tuple-element.263), channel_id=1, source_target_pairs={{1,0},{2,1},{3,2},{5,4},{6,5},{7,6},{9,8},{10,9},{11,10},{13,12},{... | collective-permute-start | bytes 1474568 | tf_op jit(solution)/shard_map/ppermute | solution.py:44
  119.3 25.1 %collective-permute-start.30 = (bf16[96,2560]{1,0:T(8,128)(2,1)}, bf16[96,2560]{1,0:T(8,128)(2,1)}, u32[]{:S(2)}, u32[]{:S(2)}) collective-permute-start(bf16[96,2560]{1,0:T(8,128)(2,1)} %get-tuple-element.278), channel_id=1, source_target_pairs={{0,1},{1,2},{2,3},{4,5},{5,6},{6,7},{8,9},{9,10},{10,11},{12,13},{... | collective-permute-start | bytes 1474568 | tf_op jit(solution)/shard_map/ppermute | solution.py:44
  124.6 19.7 %collective-permute-start.31 = (bf16[96,2560]{1,0:T(8,128)(2,1)}, bf16[96,2560]{1,0:T(8,128)(2,1)}, u32[]{:S(2)}, u32[]{:S(2)}) collective-permute-start(bf16[96,2560]{1,0:T(8,128)(2,1)} %get-tuple-element.279), channel_id=1, source_target_pairs={{1,0},{2,1},{3,2},{5,4},{6,5},{7,6},{9,8},{10,9},{11,10},{13,12},{... | collective-permute-start | bytes 1474568 | tf_op jit(solution)/shard_map/ppermute | solution.py:44
  134.7 21.0 %collective-permute-start.15 = (bf16[96,2560]{1,0:T(8,128)(2,1)S(1)}, bf16[96,2560]{1,0:T(8,128)(2,1)S(1)}, u32[]{:S(2)}, u32[]{:S(2)}) collective-permute-start(bf16[96,2560]{1,0:T(8,128)(2,1)S(1)} %unit_gradient.4.refs_0_), channel_id=1, source_target_pairs={{1,0},{2,1},{3,2},{5,4},{6,5},{7,6},{9,8},{10,9},{11,10},{13,12},{... | collective-permute-start | bytes 1474568 | tf_op jit(solution)/shard_map/ppermute | solution.py:44
  136.0 19.7 %collective-permute-start.14 = (bf16[96,2560]{1,0:T(8,128)(2,1)S(1)}, bf16[96,2560]{1,0:T(8,128)(2,1)S(1)}, u32[]{:S(2)}, u32[]{:S(2)}) collective-permute-start(bf16[96,2560]{1,0:T(8,128)(2,1)S(1)} %unit_gradient.4.refs_0_), channel_id=1, source_target_pairs={{0,1},{1,2},{2,3},{4,5},{5,6},{6,7},{8,9},{9,10},{10,11},{12,13},{... | collective-permute-start | bytes 1474568 | tf_op jit(solution)/shard_map/ppermute | solution.py:44
  149.0 12.5 %collective-permute-start.33 = (bf16[96,2560]{1,0:T(8,128)(2,1)}, bf16[96,2560]{1,0:T(8,128)(2,1)}, u32[]{:S(2)}, u32[]{:S(2)}) collective-permute-start(bf16[96,2560]{1,0:T(8,128)(2,1)} %unit_gradient.6.refs_7_), channel_id=1, source_target_pairs={{1,0},{2,1},{3,2},{5,4},{6,5},{7,6},{9,8},{10,9},{11,10},{13,12},{... | collective-permute-start | bytes 1474568 | tf_op jit(solution)/shard_map/ppermute | solution.py:44
  150.3 15.8 %collective-permute-start.32 = (bf16[96,2560]{1,0:T(8,128)(2,1)}, bf16[96,2560]{1,0:T(8,128)(2,1)}, u32[]{:S(2)}, u32[]{:S(2)}) collective-permute-start(bf16[96,2560]{1,0:T(8,128)(2,1)} %unit_gradient.6.refs_7_), channel_id=1, source_target_pairs={{0,1},{1,2},{2,3},{4,5},{5,6},{6,7},{8,9},{9,10},{10,11},{12,13},{... | collective-permute-start | bytes 1474568 | tf_op jit(solution)/shard_map/ppermute | solution.py:44
  156.9 19.5 %collective-permute-start.16 = (bf16[96,2560]{1,0:T(8,128)(2,1)S(1)}, bf16[96,2560]{1,0:T(8,128)(2,1)S(1)}, u32[]{:S(2)}, u32[]{:S(2)}) collective-permute-start(bf16[96,2560]{1,0:T(8,128)(2,1)S(1)} %get-tuple-element.270), channel_id=1, source_target_pairs={{0,1},{1,2},{2,3},{4,5},{5,6},{6,7},{8,9},{9,10},{10,11},{12,13},{... | collective-permute-start | bytes 1474568 | tf_op jit(solution)/shard_map/ppermute | solution.py:44
  158.3 18.2 %collective-permute-start.17 = (bf16[96,2560]{1,0:T(8,128)(2,1)S(1)}, bf16[96,2560]{1,0:T(8,128)(2,1)S(1)}, u32[]{:S(2)}, u32[]{:S(2)}) collective-permute-start(bf16[96,2560]{1,0:T(8,128)(2,1)S(1)} %get-tuple-element.271), channel_id=1, source_target_pairs={{1,0},{2,1},{3,2},{5,4},{6,5},{7,6},{9,8},{10,9},{11,10},{13,12},{... | collective-permute-start | bytes 1474568 | tf_op jit(solution)/shard_map/ppermute | solution.py:44
  168.5 18.5 %collective-permute-start.34 = (bf16[96,2560]{1,0:T(8,128)(2,1)S(1)}, bf16[96,2560]{1,0:T(8,128)(2,1)S(1)}, u32[]{:S(2)}, u32[]{:S(2)}) collective-permute-start(bf16[96,2560]{1,0:T(8,128)(2,1)S(1)} %get-tuple-element.283), channel_id=1, source_target_pairs={{0,1},{1,2},{2,3},{4,5},{5,6},{6,7},{8,9},{9,10},{10,11},{12,13},{... | collective-permute-start | bytes 1474568 | tf_op jit(solution)/shard_map/ppermute | solution.py:44
  172.9 14.1 %collective-permute-start.35 = (bf16[96,2560]{1,0:T(8,128)(2,1)S(1)}, bf16[96,2560]{1,0:T(8,128)(2,1)S(1)}, u32[]{:S(2)}, u32[]{:S(2)}) collective-permute-start(bf16[96,2560]{1,0:T(8,128)(2,1)S(1)} %get-tuple-element.284), channel_id=1, source_target_pairs={{1,0},{2,1},{3,2},{5,4},{6,5},{7,6},{9,8},{10,9},{11,10},{13,12},{... | collective-permute-start | bytes 1474568 | tf_op jit(solution)/shard_map/ppermute | solution.py:44
  176.5 38.7 %copy-start.17 = (bf16[96,2560]{1,0:T(8,128)(2,1)}, bf16[96,2560]{1,0:T(8,128)(2,1)S(1)}, u32[]{:S(2)}) copy-start(bf16[96,2560]{1,0:T(8,128)(2,1)S(1)} %collective-permute-done.16.right_ref.refs_2_) | copy-start | bytes 1474564
  176.5 38.7 %copy-start.19 = (bf16[96,2560]{1,0:T(8,128)(2,1)}, bf16[96,2560]{1,0:T(8,128)(2,1)S(1)}, u32[]{:S(2)}) copy-start(bf16[96,2560]{1,0:T(8,128)(2,1)S(1)} %collective-permute-done.17.left_ref.refs_5_) | copy-start | bytes 1474564
  177.8 19.7 %collective-permute-start.18 = (bf16[96,2560]{1,0:T(8,128)(2,1)S(1)}, bf16[96,2560]{1,0:T(8,128)(2,1)S(1)}, u32[]{:S(2)}, u32[]{:S(2)}) collective-permute-start(bf16[96,2560]{1,0:T(8,128)(2,1)S(1)} %get-tuple-element.272), channel_id=1, source_target_pairs={{0,1},{1,2},{2,3},{4,5},{5,6},{6,7},{8,9},{9,10},{10,11},{12,13},{... | collective-permute-start | bytes 1474568 | tf_op jit(solution)/shard_map/ppermute | solution.py:44
  182.2 16.1 %collective-permute-start.19 = (bf16[96,2560]{1,0:T(8,128)(2,1)S(1)}, bf16[96,2560]{1,0:T(8,128)(2,1)S(1)}, u32[]{:S(2)}, u32[]{:S(2)}) collective-permute-start(bf16[96,2560]{1,0:T(8,128)(2,1)S(1)} %get-tuple-element.273), channel_id=1, source_target_pairs={{1,0},{2,1},{3,2},{5,4},{6,5},{7,6},{9,8},{10,9},{11,10},{13,12},{... | collective-permute-start | bytes 1474568 | tf_op jit(solution)/shard_map/ppermute | solution.py:44
  187.0 28.1 %copy-start.21 = (bf16[96,2560]{1,0:T(8,128)(2,1)}, bf16[96,2560]{1,0:T(8,128)(2,1)S(1)}, u32[]{:S(2)}) copy-start(bf16[96,2560]{1,0:T(8,128)(2,1)S(1)} %collective-permute-done.34.right_ref.refs_9_) | copy-start | bytes 1474564
  187.0 28.1 %copy-start.22 = (bf16[96,2560]{1,0:T(8,128)(2,1)}, bf16[96,2560]{1,0:T(8,128)(2,1)S(1)}, u32[]{:S(2)}) copy-start(bf16[96,2560]{1,0:T(8,128)(2,1)S(1)} %collective-permute-done.35.left_ref.refs_12_) | copy-start | bytes 1474564
  187.0 28.2 %slice-start = ((s8[6553600]{0:T(1024)(128)(4,1)}), s8[4194304]{0:T(1024)(128)(4,1)S(1)}, s32[]{:S(2)}) async-start(s8[6553600]{0:T(1024)(128)(4,1)} %bitcast.45), calls=%async_computation.10 | async-start | bytes 8388608
  188.3 19.7 %collective-permute-start.36 = (bf16[96,2560]{1,0:T(8,128)(2,1)S(1)}, bf16[96,2560]{1,0:T(8,128)(2,1)S(1)}, u32[]{:S(2)}, u32[]{:S(2)}) collective-permute-start(bf16[96,2560]{1,0:T(8,128)(2,1)S(1)} %get-tuple-element.285), channel_id=1, source_target_pairs={{0,1},{1,2},{2,3},{4,5},{5,6},{6,7},{8,9},{9,10},{10,11},{12,13},{... | collective-permute-start | bytes 1474568 | tf_op jit(solution)/shard_map/ppermute | solution.py:44
  192.9 16.2 %collective-permute-start.37 = (bf16[96,2560]{1,0:T(8,128)(2,1)S(1)}, bf16[96,2560]{1,0:T(8,128)(2,1)S(1)}, u32[]{:S(2)}, u32[]{:S(2)}) collective-permute-start(bf16[96,2560]{1,0:T(8,128)(2,1)S(1)} %get-tuple-element.286), channel_id=1, source_target_pairs={{1,0},{2,1},{3,2},{5,4},{6,5},{7,6},{9,8},{10,9},{11,10},{13,12},{... | collective-permute-start | bytes 1474568 | tf_op jit(solution)/shard_map/ppermute | solution.py:44
  199.6 23.9 %collective-permute-start.20 = (bf16[96,2560]{1,0:T(8,128)(2,1)S(1)}, bf16[96,2560]{1,0:T(8,128)(2,1)S(1)}, u32[]{:S(2)}, u32[]{:S(2)}) collective-permute-start(bf16[96,2560]{1,0:T(8,128)(2,1)S(1)} %get-tuple-element.274), channel_id=1, source_target_pairs={{0,1},{1,2},{2,3},{4,5},{5,6},{6,7},{8,9},{9,10},{10,11},{12,13},{... | collective-permute-start | bytes 1474568 | tf_op jit(solution)/shard_map/ppermute | solution.py:44
  203.4 20.1 %collective-permute-start.21 = (bf16[96,2560]{1,0:T(8,128)(2,1)S(1)}, bf16[96,2560]{1,0:T(8,128)(2,1)S(1)}, u32[]{:S(2)}, u32[]{:S(2)}) collective-permute-start(bf16[96,2560]{1,0:T(8,128)(2,1)S(1)} %get-tuple-element.275), channel_id=1, source_target_pairs={{1,0},{2,1},{3,2},{5,4},{6,5},{7,6},{9,8},{10,9},{11,10},{13,12},{... | collective-permute-start | bytes 1474568 | tf_op jit(solution)/shard_map/ppermute | solution.py:44
  210.4 22.0 %collective-permute-start.38 = (bf16[96,2560]{1,0:T(8,128)(2,1)S(1)}, bf16[96,2560]{1,0:T(8,128)(2,1)S(1)}, u32[]{:S(2)}, u32[]{:S(2)}) collective-permute-start(bf16[96,2560]{1,0:T(8,128)(2,1)S(1)} %get-tuple-element.287), channel_id=1, source_target_pairs={{0,1},{1,2},{2,3},{4,5},{5,6},{6,7},{8,9},{9,10},{10,11},{12,13},{... | collective-permute-start | bytes 1474568 | tf_op jit(solution)/shard_map/ppermute | solution.py:44
  213.8 18.6 %collective-permute-start.39 = (bf16[96,2560]{1,0:T(8,128)(2,1)S(1)}, bf16[96,2560]{1,0:T(8,128)(2,1)S(1)}, u32[]{:S(2)}, u32[]{:S(2)}) collective-permute-start(bf16[96,2560]{1,0:T(8,128)(2,1)S(1)} %get-tuple-element.288), channel_id=1, source_target_pairs={{1,0},{2,1},{3,2},{5,4},{6,5},{7,6},{9,8},{10,9},{11,10},{13,12},{... | collective-permute-start | bytes 1474568 | tf_op jit(solution)/shard_map/ppermute | solution.py:44
  224.9 17.2 %collective-permute-start.25 = (bf16[96,2560]{1,0:T(8,128)(2,1)}, bf16[96,2560]{1,0:T(8,128)(2,1)}, u32[]{:S(2)}, u32[]{:S(2)}) collective-permute-start(bf16[96,2560]{1,0:T(8,128)(2,1)} %unit_gradient.5.refs_0_), channel_id=1, source_target_pairs={{1,0},{2,1},{3,2},{5,4},{6,5},{7,6},{9,8},{10,9},{11,10},{13,12},{... | collective-permute-start | bytes 1474568 | tf_op jit(solution)/shard_map/ppermute | solution.py:44
  226.1 17.2 %collective-permute-start.22 = (bf16[96,2560]{1,0:T(8,128)(2,1)}, bf16[96,2560]{1,0:T(8,128)(2,1)}, u32[]{:S(2)}, u32[]{:S(2)}) collective-permute-start(bf16[96,2560]{1,0:T(8,128)(2,1)} %unit_gradient.5.refs_0_), channel_id=1, source_target_pairs={{0,1},{1,2},{2,3},{4,5},{5,6},{6,7},{8,9},{9,10},{10,11},{12,13},{... | collective-permute-start | bytes 1474568 | tf_op jit(solution)/shard_map/ppermute | solution.py:44
  232.4 45.0 %copy-start.18 = (bf16[96,2560]{1,0:T(8,128)(2,1)S(1)}, bf16[96,2560]{1,0:T(8,128)(2,1)}, u32[]{:S(2)}) copy-start(bf16[96,2560]{1,0:T(8,128)(2,1)} %copy-done.17) | copy-start | bytes 1474564
  232.4 45.0 %copy-start.20 = (bf16[96,2560]{1,0:T(8,128)(2,1)S(1)}, bf16[96,2560]{1,0:T(8,128)(2,1)}, u32[]{:S(2)}) copy-start(bf16[96,2560]{1,0:T(8,128)(2,1)} %copy-done.19) | copy-start | bytes 1474564
  232.4 45.0 %copy-start.24 = (bf16[96,2560]{1,0:T(8,128)(2,1)S(1)}, bf16[96,2560]{1,0:T(8,128)(2,1)}, u32[]{:S(2)}) copy-start(bf16[96,2560]{1,0:T(8,128)(2,1)} %copy-done.23) | copy-start | bytes 1474564
  232.4 45.0 %copy-start.26 = (bf16[96,2560]{1,0:T(8,128)(2,1)S(1)}, bf16[96,2560]{1,0:T(8,128)(2,1)}, u32[]{:S(2)}) copy-start(bf16[96,2560]{1,0:T(8,128)(2,1)} %copy-done.25) | copy-start | bytes 1474564
  233.8 18.9 %collective-permute-start.43 = (bf16[96,2560]{1,0:T(8,128)(2,1)}, bf16[96,2560]{1,0:T(8,128)(2,1)}, u32[]{:S(2)}, u32[]{:S(2)}) collective-permute-start(bf16[96,2560]{1,0:T(8,128)(2,1)} %unit_gradient.7.refs_7_), channel_id=1, source_target_pairs={{1,0},{2,1},{3,2},{5,4},{6,5},{7,6},{9,8},{10,9},{11,10},{13,12},{... | collective-permute-start | bytes 1474568 | tf_op jit(solution)/shard_map/ppermute | solution.py:44
  235.1 18.9 %collective-permute-start.40 = (bf16[96,2560]{1,0:T(8,128)(2,1)}, bf16[96,2560]{1,0:T(8,128)(2,1)}, u32[]{:S(2)}, u32[]{:S(2)}) collective-permute-start(bf16[96,2560]{1,0:T(8,128)(2,1)} %unit_gradient.7.refs_7_), channel_id=1, source_target_pairs={{0,1},{1,2},{2,3},{4,5},{5,6},{6,7},{8,9},{9,10},{10,11},{12,13},{... | collective-permute-start | bytes 1474568 | tf_op jit(solution)/shard_map/ppermute | solution.py:44
  242.1 21.1 %collective-permute-start.26 = (bf16[96,2560]{1,0:T(8,128)(2,1)}, bf16[96,2560]{1,0:T(8,128)(2,1)}, u32[]{:S(2)}, u32[]{:S(2)}) collective-permute-start(bf16[96,2560]{1,0:T(8,128)(2,1)} %collective-permute-done.25.refs_4_), channel_id=1, source_target_pairs={{1,0},{2,1},{5,4},{6,5},{9,8},{10,9},{13,12},{14,13},{17,16},{18,1... | collective-permute-start | bytes 1474568 | tf_op jit(solution)/shard_map/ppermute | solution.py:44
  243.4 21.1 %collective-permute-start.23 = (bf16[96,2560]{1,0:T(8,128)(2,1)}, bf16[96,2560]{1,0:T(8,128)(2,1)}, u32[]{:S(2)}, u32[]{:S(2)}) collective-permute-start(bf16[96,2560]{1,0:T(8,128)(2,1)} %collective-permute-done.22.refs_1_), channel_id=1, source_target_pairs={{1,2},{2,3},{5,6},{6,7},{9,10},{10,11},{13,14},{14,15},{17,18},{18... | collective-permute-start | bytes 1474568 | tf_op jit(solution)/shard_map/ppermute | solution.py:44
  252.6 20.7 %collective-permute-start.44 = (bf16[96,2560]{1,0:T(8,128)(2,1)}, bf16[96,2560]{1,0:T(8,128)(2,1)}, u32[]{:S(2)}, u32[]{:S(2)}) collective-permute-start(bf16[96,2560]{1,0:T(8,128)(2,1)} %collective-permute-done.43.refs_11_), channel_id=1, source_target_pairs={{1,0},{2,1},{5,4},{6,5},{9,8},{10,9},{13,12},{14,13},{17,16},{18,1... | collective-permute-start | bytes 1474568 | tf_op jit(solution)/shard_map/ppermute | solution.py:44
  253.9 20.6 %collective-permute-start.41 = (bf16[96,2560]{1,0:T(8,128)(2,1)}, bf16[96,2560]{1,0:T(8,128)(2,1)}, u32[]{:S(2)}, u32[]{:S(2)}) collective-permute-start(bf16[96,2560]{1,0:T(8,128)(2,1)} %collective-permute-done.40.refs_8_), channel_id=1, source_target_pairs={{1,2},{2,3},{5,6},{6,7},{9,10},{10,11},{13,14},{14,15},{17,18},{18... | collective-permute-start | bytes 1474568 | tf_op jit(solution)/shard_map/ppermute | solution.py:44
  263.2 23.3 %collective-permute-start.27 = (bf16[96,2560]{1,0:T(8,128)(2,1)}, bf16[96,2560]{1,0:T(8,128)(2,1)}, u32[]{:S(2)}, u32[]{:S(2)}) collective-permute-start(bf16[96,2560]{1,0:T(8,128)(2,1)} %collective-permute-done.26.refs_5_), channel_id=1, source_target_pairs={{1,0},{5,4},{9,8},{13,12},{17,16},{21,20},{25,24},{29,28}} | collective-permute-start | bytes 1474568 | tf_op jit(solution)/shard_map/ppermute | solution.py:44
  264.5 22.0 %collective-permute-start.24 = (bf16[96,2560]{1,0:T(8,128)(2,1)}, bf16[96,2560]{1,0:T(8,128)(2,1)}, u32[]{:S(2)}, u32[]{:S(2)}) collective-permute-start(bf16[96,2560]{1,0:T(8,128)(2,1)} %collective-permute-done.23.refs_2_), channel_id=1, source_target_pairs={{2,3},{6,7},{10,11},{14,15},{18,19},{22,23},{26,27},{30,31}} | collective-permute-start | bytes 1474568 | tf_op jit(solution)/shard_map/ppermute | solution.py:44
  273.3 13.2 %collective-permute-start.45 = (bf16[96,2560]{1,0:T(8,128)(2,1)}, bf16[96,2560]{1,0:T(8,128)(2,1)}, u32[]{:S(2)}, u32[]{:S(2)}) collective-permute-start(bf16[96,2560]{1,0:T(8,128)(2,1)} %collective-permute-done.44.refs_12_), channel_id=1, source_target_pairs={{1,0},{5,4},{9,8},{13,12},{17,16},{21,20},{25,24},{29,28}} | collective-permute-start | bytes 1474568 | tf_op jit(solution)/shard_map/ppermute | solution.py:44
  274.6 11.9 %collective-permute-start.42 = (bf16[96,2560]{1,0:T(8,128)(2,1)}, bf16[96,2560]{1,0:T(8,128)(2,1)}, u32[]{:S(2)}, u32[]{:S(2)}) collective-permute-start(bf16[96,2560]{1,0:T(8,128)(2,1)} %collective-permute-done.41.refs_9_), channel_id=1, source_target_pairs={{2,3},{6,7},{10,11},{14,15},{18,19},{22,23},{26,27},{30,31}} | collective-permute-start | bytes 1474568 | tf_op jit(solution)/shard_map/ppermute | solution.py:44
  296.5 60.8 %collective-permute-start.1 = (bf16[640,2560]{1,0:T(8,128)(2,1)}, bf16[640,2560]{1,0:T(8,128)(2,1)}, u32[]{:S(2)}, u32[]{:S(2)}) collective-permute-start(bf16[640,2560]{1,0:T(8,128)(2,1)} %get-tuple-element.158), channel_id=1, source_target_pairs={{0,8},{4,12},{8,16},{12,20},{16,24},{20,28},{24,0},{28,4},{1,9},{5... | collective-permute-start | bytes 9830408 | tf_op jit(solution)/shard_map/cond/branch_1_fun/ppermute | solution.py:429
  298.4 29.3 %all-to-all-start.2 = ((bf16[4,192,640]{2,1,0:T(8,128)(2,1)}), bf16[4,192,640]{2,1,0:T(8,128)(2,1)S(1)}, u32[]{:S(2)}, u32[]{:S(2)}) async-start(bf16[4,192,640]{2,1,0:T(8,128)(2,1)} %get-tuple-element.159), calls=%async_computation.2 | async-start | bytes 1966080 | tf_op jit(solution)/shard_map/cond/branch_1_fun/all_to_all | solution.py:424
  327.8 18.7 %all-to-all-start.3 = ((bf16[4,192,640]{2,1,0:T(8,128)(2,1)}), bf16[4,192,640]{2,1,0:T(8,128)(2,1)S(1)}, u32[]{:S(2)}, u32[]{:S(2)}) async-start(bf16[4,192,640]{2,1,0:T(8,128)(2,1)} %get-tuple-element.176), calls=%async_computation.3 | async-start | bytes 1966080 | tf_op jit(solution)/shard_map/cond/branch_1_fun/all_to_all | solution.py:424
  (28 other events, 260.3 us)

commit v10 on v1

--- a/solution.py
+++ b/solution.py
@@ -233,17 +233,18 @@
     scratch[...] = stack.T
 
 
-def weight_step(units, mine, order, kept, numer, inbox):
+def weight_step(units, mine, order, base, half=False, inbox=None, token=None):
     members, _, rows = mine[0].shape
-    width = numer.shape[1] if kept is None else kept.shape[1]
+    width = base.shape[1]
     tile = tile_of(width)
     count = len(units) * len(units[0])
     chunks = len(units)
     total = sum(members * block.shape[1] for block in mine)
+    early = inbox is None and not half
 
     def body(s, *refs):
         units_ref, mine_refs = refs[:count], refs[count : count + chunks]
-        rest = refs[count + chunks : -1]
+        base_ref = refs[count + chunks]
         turned = refs[-1]
 
         @pl.when(pl.program_id(0) == 0)
@@ -253,33 +254,35 @@
         weight = jnp.dot(
             turned[...], stack_of(units_ref, members, s[0]), preferred_element_type=jnp.float32
         )
-        if kept is None:
-            numer_ref, kept_out, token_out = rest
-            kept_out[...] = 0.5 * (numer_ref[...] - 0.004 * weight)
-            token_out[...] = jnp.zeros((8, 128), jnp.float32)
+        if early:
+            refs[-3][...] = 0.5 * (base_ref[...] - 0.004 * weight)
+            refs[-2][...] = jnp.zeros((8, 128), jnp.float32)
         else:
-            kept_ref, inbox_ref, new_out, kept_out = rest
-            now = kept_ref[...] - 0.5 * 0.004 * weight
-            new_out[...] = now + inbox_ref[...]
-            kept_out[...] = now.astype(jnp.bfloat16)
+            now = base_ref[...] - 0.5 * 0.004 * weight
+            if inbox is not None:
+                refs[-2][...] = now + refs[count + chunks + 1][...]
+            else:
+                refs[-2][...] = now.astype(jnp.bfloat16)
 
     columns = (rows, tile), lambda j, s: (0, j)
-    whole = ((rows, width), jnp.float32) + columns
+    ins = unit_ins(units, tile) + mine_ins(mine) + [(base,) + columns]
+    if inbox is not None:
+        ins.append((inbox,) + columns)
+    if token is not None:
+        ins.append(token_in(token))
+    kind = jnp.bfloat16 if half else jnp.float32
+    outs = [((rows, width), kind) + columns]
     return call(
         body,
         "weight_step",
         (width // tile,),
-        unit_ins(units, tile)
-        + mine_ins(mine)
-        + ([(numer,) + columns] if kept is None else [(kept,) + columns, (inbox,) + columns]),
-        [whole, TOKEN_OUT]
-        if kept is None
-        else [whole, ((rows, width), jnp.bfloat16) + columns],
+        ins,
+        outs + [TOKEN_OUT] * early,
         scalars=(order,),
         scratch=[pltpu.VMEM((rows, total), jnp.bfloat16)],
         flops=2 * total * rows * width,
-        moved=2 * count * units[0][0].shape[0] * width + 12 * rows * width,
-        vmem=26,
+        moved=(2 * count * units[0][0].shape[0] + 12 * rows) * width,
+        vmem=26 if early else 52,
     )
 
 
@@ -293,7 +296,8 @@
     total = members * sum(sizes)
 
     def body(s, *refs):
-        weights_ref, grad_ref, acc = refs[count:]
+        weights_ref, grad_ref, token_out, acc = refs[count:]
+        token_out[...] = jnp.zeros((8, 128), jnp.float32)
         j = pl.program_id(0)
         grad = lax.dot_general(
             stack_of(refs[:count], members, s[0]),
@@ -330,44 +334,51 @@
                 jnp.bfloat16,
                 (members, sum(sizes), rows),
                 fixed(0, 0, 0),
-            )
+            ),
+            TOKEN_OUT,
         ],
         scalars=(order,),
         scratch=[pltpu.VMEM((total, rows), jnp.float32)],
         flops=2 * total * rows * width,
         moved=2 * count * sizes[0] * width + 2 * rows * width,
-        vmem=20,
-    )[0]
-
-
-def joined_rows(blocks):
-    members, tokens, rows = blocks.shape
-    step = 96
-
-    def body(blocks_ref, out_ref):
-        for k in range(members):
-            out_ref[:, k * rows : (k + 1) * rows] = blocks_ref[k]
+        vmem=50,
+    )
+
+
+def joined_rows(groups):
+    members, size, rows = groups[0].shape
+    tokens = size * len(groups)
+
+    def body(*refs):
+        out_ref = refs[-1]
+        for g, blocks_ref in enumerate(refs[:-1]):
+
+            @pl.when(pl.program_id(0) == g)
+            def _(blocks_ref=blocks_ref):
+                for k in range(members):
+                    out_ref[:, k * rows : (k + 1) * rows] = blocks_ref[k]
 
     return call(
         body,
         "joined_rows",
-        (tokens // step,),
-        [(blocks, (members, step, rows), lambda i: (0, i, 0))],
+        (len(groups),),
+        [(blocks, (members, size, rows), fixed(0, 0, 0)) for blocks in groups],
         [
             (
                 (tokens, members * rows),
-                blocks.dtype,
-                (step, members * rows),
+                groups[0].dtype,
+                (size, members * rows),
                 lambda i: (i, 0),
             )
         ],
         moved=4 * members * tokens * rows,
+        vmem=24,
     )[0]
 
 
 def widened(value):
     rows, width = value.shape
-    step = 160
+    step = rows // 2
 
     def body(value_ref, out_ref):
         out_ref[...] = value_ref[...].astype(jnp.float32)
@@ -388,14 +399,16 @@
     return lax.all_to_all(blocks, "fsdp", 0, 0, tiled=False)
 
 
-def tail(kept, units, weights, grads, order, bit_place):
+def tail(half, grads, late, mine, kept, inbox, weights, order, bit_place):
     length = lax.axis_size("rep")
     sent = lax.ppermute(
-        kept, "rep", [(i, (i + (1 << bit_place)) % length) for i in range(length)]
-    )
-    last = grad_rows(units, weights, order)
-    back = swapped(jnp.concatenate(grads + [last], axis=1))
-    return sent, joined_rows(back)
+        half, "rep", [(i, (i + (1 << bit_place)) % length) for i in range(length)]
+    )
+    back = swapped(grads)
+    late_grads, token = grad_rows(late, weights, order)
+    late_back = swapped(late_grads)
+    new = weight_step(late, mine, order, kept, inbox=inbox, token=token)[0]
+    return sent, joined_rows([back, late_back]), new
 
 
 def local(
@@ -453,8 +466,6 @@
     units = [[None] * count for _ in range(rounds)]
     before = [None] * count
     hint = [None] * (count - 1) + [jnp.broadcast_to(outbox_weight[None], (8, 128))]
-    kept = None
-    grads = []
 
     def fetch(e, q, token):
         piece = cut_heads(heads[0], starts[e][q], STREAMS[q][e], members, token)
@@ -489,9 +500,9 @@
                     units[e - 1][q][1].append(moving[q][0])
                     units[e - 1][q][2].append(moving[q][1])
         if e > 0:
-            flat = [[u] + r + l for u, r, l in units[e - 1]]
-            kept, done = weight_step(flat, mine[e - 1], order, kept, numer, None)
-            grads.append(grad_rows(flat, weights, order))
+            early = [[u] + r + l for u, r, l in units[e - 1]]
+            kept, done = weight_step(early, mine[e - 1], order, numer)
+            grads, _ = grad_rows(early, weights, order)
         for q in range(count):
             unit = unit_gradient(
                 *moving[q],
@@ -511,10 +522,15 @@
             units[-1][q][1].append(before[q][0])
             units[-1][q][2].append(before[q][1])
     flat = [[u] + r + l for u, r, l in units[-1]]
-    new_params, half = weight_step(flat, mine[-1], order, kept, None, inbox_params[0])
+    half = weight_step(flat, mine[-1], order, kept, half=True)[0]
     new_weight = 0.5 * push_weight + inbox_weight
-    branches = [partial(tail, half, flat, weights, grads, order, place) for place in range(levels)]
-    sent, grad_heads = lax.switch(level_index, branches)
+    branches = [
+        partial(
+            tail, half, grads, flat, mine[-1], kept, inbox_params[0], weights, order, place
+        )
+        for place in range(levels)
+    ]
+    sent, grad_heads, new_params = lax.switch(level_index, branches)
     return (new_params[None], new_weight, widened(sent)[None], outbox_weight, grad_heads[None])
 
 

time: 355 us -> 354 us (level)
  blocking collectives: 35.4 us -> 0 us
  waiting for transfers between devices: 74.6 us -> 96.3 us
  Pallas kernels: 85.4 us -> 97.2 us
  starting transfers between devices: 125 us -> 135 us
  local copies, waits for them, and re-layouts: 18.6 us -> 9.39 us
    all_to_all x1 -> x0, blocking collectives: 35.4 us -> none  [swapped(): return lax.all_to_all(blocks, 'fsdp', 0, 0, tiled=False)]
    all_to_all x4 -> x6, waiting for transfers between devices: 4.53 us -> 21.7 us  [swapped(): return lax.all_to_all(blocks, 'fsdp', 0, 0, tiled=False)]
    pallas_call x28 -> x29, Pallas kernels: 85.4 us -> 97.2 us  [call(): pl.pallas_call(body, name=name, out_shape=[jax.ShapeDtypeStruct(shape, ki...]
    unnamed x104 -> x72, local copies, waits for them, and re-layouts: 18.6 us -> 9.37 us
    all_to_all x4 -> x6, starting transfers between devices: 21.3 us -> 28.4 us  [swapped(): return lax.all_to_all(blocks, 'fsdp', 0, 0, tiled=False)]
    ppermute x1, waiting for transfers between devices: 14.7 us -> 19.1 us  [tail(): lax.ppermute(half, 'rep', [(i, (i + (1 << bit_place)) % length) for i in...]
  transfers between devices with their start and end apart: 48 -> 50, of which waited for: 14 -> 17; matrix products, arithmetic and copies ran while one was open for 1% -> 1% of each run, Pallas kernels for 20% -> 23%
where the time goes in v10:
time: 354 us; the launch traced here: 351 us
  starting transfers between devices  135 us (38%)
  Pallas kernels  97.2 us (27%)
  waiting for transfers between devices  96.3 us (27%)
  local copies, waits for them, and re-layouts  9.39 us (3%)
  between operations  8.7 us (2%)
  other arithmetic  4.54 us (1%)
    ppermute x40, starting transfers between devices, hop(): return lax.ppermute(value, 'fsdp', [(i, i + step) for i in pairs])  98.4 us
    pallas_call x29, Pallas kernels, call(): pl.pallas_call(body, name=name, out_shape=[jax.ShapeDtypeStruct(shape, ki...  97.2 us
    ppermute x40, waiting for transfers between devices, hop(): return lax.ppermute(value, 'fsdp', [(i, i + step) for i in pairs])  55.5 us
    all_to_all x6, starting transfers between devices, swapped(): return lax.all_to_all(blocks, 'fsdp', 0, 0, tiled=False)  28.4 us
    all_to_all x6, waiting for transfers between devices, swapped(): return lax.all_to_all(blocks, 'fsdp', 0, 0, tiled=False)  21.7 us
    ppermute x1, waiting for transfers between devices, tail(): lax.ppermute(half, 'rep', [(i, (i + (1 << bit_place)) % length) for i in...  19.1 us
    unnamed x72, local copies, waits for them, and re-layouts  9.37 us
  transfers between devices with their start and end apart: 50, of which 17 were waited for; matrix products, arithmetic and copies ran while one was open for 1% of the time, Pallas kernels for 23%

profile of v10, /device:TPU:0, one launch (start us, length us, event | category | flops | bytes accessed | tf_op | source)
XLA Modules:
  0.0 351.2 jit_solution(736163086794649058)
XLA Ops:
  0.7 1.5 copy-done.10
  3.0 6.3 %all-to-all-start.6 = ((bf16[4,96,640]{2,1,0:T(8,128)(2,1)}), bf16[4,96,640]{2,1,0:T(8,128)(2,1)S(1)}, u32[]{:S(2)}, u32[]{:S(2)}) async-start(bf16[4,96,640]{2,1,0:T(8,128)(2,1)} %cut_heads.4), calls=%async_computation.6 | async-start | bytes 983040 | tf_op jit(solution)/shard_map/all_to_all | solution.py:399
  11.0 2.8 collective-permute-start.24
  13.8 2.8 collective-permute-start.23
  18.7 4.4 %all-to-all-done.6.mine_ref.refs_14_ = bf16[4,96,640]{2,1,0:T(8,128)(2,1)S(1)} async-done(((bf16[4,96,640]{2,1,0:T(8,128)(2,1)}), bf16[4,96,640]{2,1,0:T(8,128)(2,1)S(1)}, u32[]{:S(2)}, u32[]{:S(2)}) %all-to-all-start.6) | async-done | bytes 491552 | tf_op jit(solution)/shard_map/all_to_all | solution.py:399
  23.1 3.5 all-to-all-start.8
  26.6 3.6 %multiply_convert_fusion.weights_ref.refs_14_ = bf16[640,2560]{1,0:T(8,128)(2,1)S(1)} fusion(f32[]{:T(128)} %bitcast.32, f32[1,640,2560]{2,1,0:T(8,128)} %param.12), kind=kLoop, calls=%fused_computation | loop fusion | flops 4915200 | bytes 9830404 | tf_op jit(solution)/shard_map/convert_element_type | solution.py:442
  30.2 3.0 partial_products.4
  33.3 3.9 %collective-permute-start.3 = (bf16[96,2560]{1,0:T(8,128)(2,1)}, bf16[96,2560]{1,0:T(8,128)(2,1)S(1)}, u32[]{:S(2)}, u32[]{:S(2)}) collective-permute-start(bf16[96,2560]{1,0:T(8,128)(2,1)} %get-tuple-element.249), channel_id=1, source_target_pairs={{0,1},{4,5},{8,9},{12,13},{16,17},{20,21},{24,25},{28,29}} | collective-permute-start | bytes 1474568 | tf_op jit(solution)/shard_map/ppermute | solution.py:44
  40.4 4.4 %partial_products.6 = (bf16[4,96,2560]{2,1,0:T(8,128)(2,1)S(1)}, bf16[96,2560]{1,0:T(8,128)(2,1)}, bf16[96,2560]{1,0:T(8,128)(2,1)}) custom-call(bf16[4,96,640]{2,1,0:T(8,128)(2,1)S(1)} %all-to-all-done.8.mine_ref.refs_15_, bf16[640,2560]{1,0:T(8,128)(2,1)} %copy-done.28, f32[8,128]{1,0:T(8,128)S(1)} %broadcast_in_dim.48.refs_0_), custom_call_target="tpu_custom_call" | custom-call | flops 1258291200 | bytes 5734400 | tf_op jit(solution)/shard_map/partial_products/pallas_call | solution.py:16
  46.1 2.1 collective-permute-start.26
  49.7 1.6 next_payload.10
  51.3 1.7 collective-permute-start.5
  54.5 5.9 %all-to-all-start.7 = ((bf16[4,96,640]{2,1,0:T(8,128)(2,1)}), bf16[4,96,640]{2,1,0:T(8,128)(2,1)}, u32[]{:S(2)}, u32[]{:S(2)}) async-start(bf16[4,96,640]{2,1,0:T(8,128)(2,1)} %cut_heads.5), calls=%async_computation.7 | async-start | bytes 983040 | tf_op jit(solution)/shard_map/all_to_all | solution.py:399
  60.4 1.5 copy-done.1
  62.0 2.8 next_payload.15
  64.7 3.9 %collective-permute-start.28 = (bf16[96,2560]{1,0:T(8,128)(2,1)}, bf16[96,2560]{1,0:T(8,128)(2,1)S(1)}, u32[]{:S(2)}, u32[]{:S(2)}) collective-permute-start(bf16[96,2560]{1,0:T(8,128)(2,1)} %get-tuple-element.268), channel_id=1, source_target_pairs={{0,1},{1,2},{4,5},{5,6},{8,9},{9,10},{12,13},{13,14},{16,17},{17,1... | collective-permute-start | bytes 1474568 | tf_op jit(solution)/shard_map/ppermute | solution.py:44
  70.2 1.6 next_payload.11
  71.8 4.2 %collective-permute-start.7 = (bf16[96,2560]{1,0:T(8,128)(2,1)}, bf16[96,2560]{1,0:T(8,128)(2,1)S(1)}, u32[]{:S(2)}, u32[]{:S(2)}) collective-permute-start(bf16[96,2560]{1,0:T(8,128)(2,1)} %get-tuple-element.254), channel_id=1, source_target_pairs={{0,1},{1,2},{2,3},{4,5},{5,6},{6,7},{8,9},{9,10},{10,11},{12,13},{... | collective-permute-start | bytes 1474568 | tf_op jit(solution)/shard_map/ppermute | solution.py:44
  77.3 11.0 %collective-permute-done.28.right_ref = bf16[96,2560]{1,0:T(8,128)(2,1)S(1)} collective-permute-done((bf16[96,2560]{1,0:T(8,128)(2,1)}, bf16[96,2560]{1,0:T(8,128)(2,1)S(1)}, u32[]{:S(2)}, u32[]{:S(2)}) %collective-permute-start.28) | collective-permute-done | bytes 491552 | tf_op jit(solution)/shard_map/ppermute | solution.py:44
  88.4 2.5 next_payload.16
  90.9 5.2 %collective-permute-start.30 = (bf16[96,2560]{1,0:T(8,128)(2,1)}, bf16[96,2560]{1,0:T(8,128)(2,1)}, u32[]{:S(2)}, u32[]{:S(2)}) collective-permute-start(bf16[96,2560]{1,0:T(8,128)(2,1)} %get-tuple-element.270), channel_id=1, source_target_pairs={{0,1},{1,2},{2,3},{4,5},{5,6},{6,7},{8,9},{9,10},{10,11},{12,13},{... | collective-permute-start | bytes 1474568 | tf_op jit(solution)/shard_map/ppermute | solution.py:44
  98.3 5.7 %all-to-all-start.9 = ((bf16[4,96,640]{2,1,0:T(8,128)(2,1)}), bf16[4,96,640]{2,1,0:T(8,128)(2,1)}, u32[]{:S(2)}, u32[]{:S(2)}) async-start(bf16[4,96,640]{2,1,0:T(8,128)(2,1)} %cut_heads.7), calls=%async_computation.9 | async-start | bytes 983040 | tf_op jit(solution)/shard_map/all_to_all | solution.py:399
  104.8 1.5 copy-done.4
  106.4 1.5 copy-done.7
  109.6 1.6 collective-permute-start.10
  111.2 4.6 %collective-permute-start.9 = (bf16[96,2560]{1,0:T(8,128)(2,1)S(1)}, bf16[96,2560]{1,0:T(8,128)(2,1)S(1)}, u32[]{:S(2)}, u32[]{:S(2)}) collective-permute-start(bf16[96,2560]{1,0:T(8,128)(2,1)S(1)} %unit_gradient.4.refs_0_), channel_id=1, source_target_pairs={{0,1},{1,2},{2,3},{4,5},{5,6},{6,7},{8,9},{9,10},{10,11},{12,13},{... | collective-permute-start | bytes 1474568 | tf_op jit(solution)/shard_map/ppermute | solution.py:44
  115.8 2.4 unit_gradient.6.refs_7_
  119.5 6.0 %collective-permute-start.32 = (bf16[96,2560]{1,0:T(8,128)(2,1)}, bf16[96,2560]{1,0:T(8,128)(2,1)}, u32[]{:S(2)}, u32[]{:S(2)}) collective-permute-start(bf16[96,2560]{1,0:T(8,128)(2,1)} %unit_gradient.6.refs_7_), channel_id=1, source_target_pairs={{0,1},{1,2},{2,3},{4,5},{5,6},{6,7},{8,9},{9,10},{10,11},{12,13},{... | collective-permute-start | bytes 1474568 | tf_op jit(solution)/shard_map/ppermute | solution.py:44
  125.6 4.3 %partial_products.5 = (bf16[4,96,2560]{2,1,0:T(8,128)(2,1)S(1)}, bf16[96,2560]{1,0:T(8,128)(2,1)}, bf16[96,2560]{1,0:T(8,128)(2,1)}) custom-call(bf16[4,96,640]{2,1,0:T(8,128)(2,1)} %all-to-all-done.7.mine_ref.refs_14_, bf16[640,2560]{1,0:T(8,128)(2,1)} %copy-done.28, f32[8,128]{1,0:T(8,128)S(1)} %get-tuple-element.257.refs_0_), custom_call_target="tpu_custom_call" | custom-call | flops 1258291200 | bytes 5734400 | tf_op jit(solution)/shard_map/partial_products/pallas_call | solution.py:16
  129.9 1.6 next_payload.12
  131.5 8.3 %collective-permute-start.11 = (bf16[96,2560]{1,0:T(8,128)(2,1)}, bf16[96,2560]{1,0:T(8,128)(2,1)}, u32[]{:S(2)}, u32[]{:S(2)}) collective-permute-start(bf16[96,2560]{1,0:T(8,128)(2,1)} %get-tuple-element.259), channel_id=1, source_target_pairs={{0,1},{1,2},{2,3},{4,5},{5,6},{6,7},{8,9},{9,10},{10,11},{12,13},{... | collective-permute-start | bytes 1474568 | tf_op jit(solution)/shard_map/ppermute | solution.py:44
  141.1 4.3 %partial_products.7 = (bf16[4,96,2560]{2,1,0:T(8,128)(2,1)S(1)}, bf16[96,2560]{1,0:T(8,128)(2,1)}, bf16[96,2560]{1,0:T(8,128)(2,1)}) custom-call(bf16[4,96,640]{2,1,0:T(8,128)(2,1)} %all-to-all-done.9.mine_ref.refs_15_, bf16[640,2560]{1,0:T(8,128)(2,1)} %copy-done.28, f32[8,128]{1,0:T(8,128)S(1)} %get-tuple-element.273.refs_0_), custom_call_target="tpu_custom_call" | custom-call | flops 1258291200 | bytes 5734400 | tf_op jit(solution)/shard_map/partial_products/pallas_call | solution.py:16
  145.4 2.5 next_payload.17
  147.9 4.6 %collective-permute-start.34 = (bf16[96,2560]{1,0:T(8,128)(2,1)S(1)}, bf16[96,2560]{1,0:T(8,128)(2,1)S(1)}, u32[]{:S(2)}, u32[]{:S(2)}) collective-permute-start(bf16[96,2560]{1,0:T(8,128)(2,1)S(1)} %get-tuple-element.275), channel_id=1, source_target_pairs={{0,1},{1,2},{2,3},{4,5},{5,6},{6,7},{8,9},{9,10},{10,11},{12,13},{... | collective-permute-start | bytes 1474568 | tf_op jit(solution)/shard_map/ppermute | solution.py:44
  154.4 2.5 next_payload.13
  156.9 4.0 %collective-permute-start.13 = (bf16[96,2560]{1,0:T(8,128)(2,1)S(1)}, bf16[96,2560]{1,0:T(8,128)(2,1)S(1)}, u32[]{:S(2)}, u32[]{:S(2)}) collective-permute-start(bf16[96,2560]{1,0:T(8,128)(2,1)S(1)} %get-tuple-element.261), channel_id=1, source_target_pairs={{0,1},{1,2},{2,3},{4,5},{5,6},{6,7},{8,9},{9,10},{10,11},{12,13},{... | collective-permute-start | bytes 1474568 | tf_op jit(solution)/shard_map/ppermute | solution.py:44
  162.1 2.0 collective-permute-done.34.right_ref.refs_9_
  164.1 4.3 %collective-permute-done.35.left_ref.refs_12_ = bf16[96,2560]{1,0:T(8,128)(2,1)S(1)} collective-permute-done((bf16[96,2560]{1,0:T(8,128)(2,1)S(1)}, bf16[96,2560]{1,0:T(8,128)(2,1)S(1)}, u32[]{:S(2)}, u32[]{:S(2)}) %collective-permute-start.35) | collective-permute-done | bytes 491552 | tf_op jit(solution)/shard_map/ppermute | solution.py:44
  169.7 2.1 collective-permute-start.36
  174.4 4.0 %collective-permute-done.14.left_ref.refs_6_ = bf16[96,2560]{1,0:T(8,128)(2,1)S(1)} collective-permute-done((bf16[96,2560]{1,0:T(8,128)(2,1)S(1)}, bf16[96,2560]{1,0:T(8,128)(2,1)S(1)}, u32[]{:S(2)}, u32[]{:S(2)}) %collective-permute-start.14) | collective-permute-done | bytes 491552 | tf_op jit(solution)/shard_map/ppermute | solution.py:44
  179.7 2.7 collective-permute-start.15
  184.9 4.0 %collective-permute-done.37.left_ref.refs_13_ = bf16[96,2560]{1,0:T(8,128)(2,1)S(1)} collective-permute-done((bf16[96,2560]{1,0:T(8,128)(2,1)S(1)}, bf16[96,2560]{1,0:T(8,128)(2,1)S(1)}, u32[]{:S(2)}, u32[]{:S(2)}) %collective-permute-start.37) | collective-permute-done | bytes 491552 | tf_op jit(solution)/shard_map/ppermute | solution.py:44
  190.2 2.5 collective-permute-start.38
  194.3 8.4 %weight_step.8 = (f32[640,2560]{1,0:T(8,128)}, f32[8,128]{1,0:T(8,128)S(1)}) custom-call(s32[4]{0:T(128)S(1)} %and_select_fusion.s, bf16[96,2560]{1,0:T(8,128)(2,1)S(1)} %unit_gradient.4.refs_0_, bf16[96,2560]{1,0:T(8,128)(2,1)S(1)} %collective-permute-done.9.right_ref.refs_1_, bf16[96,2560]{1,0:T(8,128)(2,1)} %collective-permute-done.11.right_ref.refs_2_, ...), custom_call_target="tpu_custom_call" | custom-call | flops 2516582400 | bytes 26542080 | tf_op jit(solution)/shard_map/weight_step/pallas_call | solution.py:16
  204.8 6.1 %collective-permute-start.17 = (bf16[96,2560]{1,0:T(8,128)(2,1)S(1)}, bf16[96,2560]{1,0:T(8,128)(2,1)}, u32[]{:S(2)}, u32[]{:S(2)}) collective-permute-start(bf16[96,2560]{1,0:T(8,128)(2,1)S(1)} %unit_gradient.5.refs_0_), channel_id=1, source_target_pairs={{0,1},{1,2},{2,3},{4,5},{5,6},{6,7},{8,9},{9,10},{10,11},{12,13},{... | collective-permute-start | bytes 1474568 | tf_op jit(solution)/shard_map/ppermute | solution.py:44
  212.9 5.3 %collective-permute-start.40 = (bf16[96,2560]{1,0:T(8,128)(2,1)S(1)}, bf16[96,2560]{1,0:T(8,128)(2,1)}, u32[]{:S(2)}, u32[]{:S(2)}) collective-permute-start(bf16[96,2560]{1,0:T(8,128)(2,1)S(1)} %unit_gradient.7.refs_7_), channel_id=1, source_target_pairs={{0,1},{1,2},{2,3},{4,5},{5,6},{6,7},{8,9},{9,10},{10,11},{12,13},{... | collective-permute-start | bytes 1474568 | tf_op jit(solution)/shard_map/ppermute | solution.py:44
  218.2 2.2 collective-permute-done.20.refs_4_
  223.1 7.8 %collective-permute-done.43.refs_11_ = bf16[96,2560]{1,0:T(8,128)(2,1)} collective-permute-done((bf16[96,2560]{1,0:T(8,128)(2,1)S(1)}, bf16[96,2560]{1,0:T(8,128)(2,1)}, u32[]{:S(2)}, u32[]{:S(2)}) %collective-permute-start.43) | collective-permute-done | bytes 491552 | tf_op jit(solution)/shard_map/ppermute | solution.py:44
  233.7 7.8 %collective-permute-done.21.refs_5_ = bf16[96,2560]{1,0:T(8,128)(2,1)} collective-permute-done((bf16[96,2560]{1,0:T(8,128)(2,1)}, bf16[96,2560]{1,0:T(8,128)(2,1)}, u32[]{:S(2)}, u32[]{:S(2)}) %collective-permute-start.21) | collective-permute-done | bytes 491552 | tf_op jit(solution)/shard_map/ppermute | solution.py:44
  244.2 7.8 %collective-permute-done.44.refs_12_ = bf16[96,2560]{1,0:T(8,128)(2,1)} collective-permute-done((bf16[96,2560]{1,0:T(8,128)(2,1)}, bf16[96,2560]{1,0:T(8,128)(2,1)}, u32[]{:S(2)}, u32[]{:S(2)}) %collective-permute-start.44) | collective-permute-done | bytes 491552 | tf_op jit(solution)/shard_map/ppermute | solution.py:44
  256.1 9.1 %grad_rows.7 = (bf16[4,192,640]{2,1,0:T(8,128)(2,1)}, f32[8,128]{1,0:T(8,128)}) custom-call(s32[4]{0:T(128)S(1)} %and_select_fusion.s, bf16[96,2560]{1,0:T(8,128)(2,1)S(1)} %unit_gradient.4.refs_0_, bf16[96,2560]{1,0:T(8,128)(2,1)S(1)} %collective-permute-done.9.right_ref.refs_1_, bf16[96,2560]{1,0:T(8,128)(2,1)} %collective-permute-done.11.right_ref.refs_2_, ...), custom_call_target="tpu_custom_call" | custom-call | flops 2516582400 | bytes 10158080 | tf_op jit(solution)/shard_map/grad_rows/pallas_call | solution.py:16
  265.2 1.7 collective-permute-done.45.refs_13_
  266.9 9.7 %weight_step.9 = bf16[640,2560]{1,0:T(8,128)(2,1)} custom-call(s32[4]{0:T(128)S(1)} %and_select_fusion.s, bf16[96,2560]{1,0:T(8,128)(2,1)S(1)} %copy-done.30, bf16[96,2560]{1,0:T(8,128)(2,1)} %collective-permute-done.17.refs_1_, bf16[96,2560]{1,0:T(8,128)(2,1)} %collective-permute-done.18.refs_2_, bf16[96,2560]{1,0:T(8,128)(2,1)} %collective-permute-done.19.refs_3_, ...), custom_call_target="tpu_custom_call" | custom-call | flops 2516582400 | bytes 26542080 | tf_op jit(solution)/shard_map/weight_step/pallas_call | solution.py:16
  276.6 67.2 %conditional.1 = (bf16[640,2560]{1,0:T(8,128)(2,1)}, bf16[1,384,2560]{2,1,0:T(8,128)(2,1)S(1)}, f32[1,640,2560]{2,1,0:T(8,128)}) conditional(s32[]{:T(128)} %clamp.3, (bf16[640,2560]{1,0:T(8,128)(2,1)}, bf16[4,192,640]{2,1,0:T(8,128)(2,1)}, s32[4]{0:T(128)S(1)}, bf16[96,2560]{1,0:T(8,128)(2,1)S(1)}, bf16[96,2560]{1,0:T(8,128)(2,1)}, ...), branch_computations={%region_1.2_spmd, %region_2.3_spmd, %region_3.4_spmd} | conditional | flops 5033164800 | bytes 63570104 | solution.py:533
  276.7 1.6 collective-permute-start.2
  278.2 3.5 all-to-all-start.4
  281.8 9.3 %grad_rows.6 = (bf16[4,192,640]{2,1,0:T(8,128)(2,1)}, f32[8,128]{1,0:T(8,128)S(1)}) custom-call(s32[4]{0:T(128)S(1)} %get-tuple-element.184.s, bf16[96,2560]{1,0:T(8,128)(2,1)S(1)} %get-tuple-element.185.refs_0_, bf16[96,2560]{1,0:T(8,128)(2,1)} %get-tuple-element.186.refs_1_, bf16[96,2560]{1,0:T(8,128)(2,1)} %get-tuple-element.187.refs_2_, ...), custom_call_target="tpu_custom_call" | custom-call | flops 2516582400 | bytes 10158080 | tf_op jit(solution)/shard_map/cond/branch_2_fun/grad_rows/pallas_call | solution.py:16
  291.0 9.2 %all-to-all-done.4.refs_0_ = bf16[4,192,640]{2,1,0:T(8,128)(2,1)S(1)} async-done(((bf16[4,192,640]{2,1,0:T(8,128)(2,1)}), bf16[4,192,640]{2,1,0:T(8,128)(2,1)S(1)}, u32[]{:S(2)}, u32[]{:S(2)}) %all-to-all-start.4) | async-done | bytes 983072 | tf_op jit(solution)/shard_map/cond/branch_2_fun/all_to_all | solution.py:399
  300.2 3.5 all-to-all-start.5
  303.7 12.6 %weight_step.7 = f32[640,2560]{1,0:T(8,128)} custom-call(s32[4]{0:T(128)S(1)} %get-tuple-element.184.s, bf16[96,2560]{1,0:T(8,128)(2,1)} %copy-done.33, bf16[96,2560]{1,0:T(8,128)(2,1)} %get-tuple-element.186.refs_1_, bf16[96,2560]{1,0:T(8,128)(2,1)} %get-tuple-element.187.refs_2_, bf16[96,2560]{1,0:T(8,128)(2,1)} %get-tuple-element.188.refs_3_, ...), custom_call_target="tpu_custom_call" | custom-call | flops 2516582400 | bytes 26542080 | tf_op jit(solution)/shard_map/cond/branch_2_fun/weight_step/pallas_call | solution.py:16
  316.4 8.2 %all-to-all-done.5.refs_1_ = bf16[4,192,640]{2,1,0:T(8,128)(2,1)S(1)} async-done(((bf16[4,192,640]{2,1,0:T(8,128)(2,1)}), bf16[4,192,640]{2,1,0:T(8,128)(2,1)S(1)}, u32[]{:S(2)}, u32[]{:S(2)}) %all-to-all-start.5) | async-done | bytes 983072 | tf_op jit(solution)/shard_map/cond/branch_2_fun/all_to_all | solution.py:399
  324.7 19.1 %collective-permute-done.2 = bf16[640,2560]{1,0:T(8,128)(2,1)} collective-permute-done((bf16[640,2560]{1,0:T(8,128)(2,1)}, bf16[640,2560]{1,0:T(8,128)(2,1)}, u32[]{:S(2)}, u32[]{:S(2)}) %collective-permute-start.2) | collective-permute-done | bytes 3276832 | tf_op jit(solution)/shard_map/cond/branch_2_fun/ppermute | solution.py:404
  343.8 5.1 %widened.1 = f32[640,2560]{1,0:T(8,128)} custom-call(bf16[640,2560]{1,0:T(8,128)(2,1)} %get-tuple-element.285.value_ref), custom_call_target="tpu_custom_call" | custom-call | bytes 9830400 | tf_op jit(solution)/shard_map/widened/pallas_call | solution.py:16
  (151 shorter events, 47.4 us)
Async XLA Ops:
  0.6 16.8 %copy-start.39 = (s32[8]{0:T(128)S(1)}, s32[8]{0:T(128)}, u32[]{:S(2)}) copy-start(s32[8]{0:T(128)} %param.20) | copy-start | bytes 100
  3.0 20.1 %all-to-all-start.6 = ((bf16[4,96,640]{2,1,0:T(8,128)(2,1)}), bf16[4,96,640]{2,1,0:T(8,128)(2,1)S(1)}, u32[]{:S(2)}, u32[]{:S(2)}) async-start(bf16[4,96,640]{2,1,0:T(8,128)(2,1)} %cut_heads.4), calls=%async_computation.6 | async-start | bytes 983040 | tf_op jit(solution)/shard_map/all_to_all | solution.py:399
  10.0 28.6 %collective-permute-start.25 = (f32[1]{0:T(128)}, f32[1]{0:T(128)}, u32[]{:S(2)}, u32[]{:S(2)}) collective-permute-start(f32[1]{0:T(128)} %mul.12), channel_id=1, source_target_pairs={{0,4},{4,8},{8,12},{12,16},{16,20},{20,24},{24,28},{28,0},{1,5},{5... | collective-permute-start | bytes 20 | tf_op jit(solution)/shard_map/ppermute | solution.py:433
  11.0 27.6 %collective-permute-start.24 = (f32[1]{0:T(128)}, f32[1]{0:T(128)}, u32[]{:S(2)}, u32[]{:S(2)}) collective-permute-start(f32[1]{0:T(128)} %mul.12), channel_id=1, source_target_pairs={{0,8},{4,12},{8,16},{12,20},{16,24},{20,28},{24,0},{28,4},{1,9},{5... | collective-permute-start | bytes 20 | tf_op jit(solution)/shard_map/ppermute | solution.py:433
  13.8 26.0 %collective-permute-start.23 = (f32[1]{0:T(128)}, f32[1]{0:T(128)}, u32[]{:S(2)}, u32[]{:S(2)}) collective-permute-start(f32[1]{0:T(128)} %mul.12), channel_id=1, source_target_pairs={{0,16},{4,20},{8,24},{12,28},{16,0},{20,4},{24,8},{28,12},{1,17},{... | collective-permute-start | bytes 20 | tf_op jit(solution)/shard_map/ppermute | solution.py:433
  23.1 17.3 %all-to-all-start.8 = ((bf16[4,96,640]{2,1,0:T(8,128)(2,1)}), bf16[4,96,640]{2,1,0:T(8,128)(2,1)S(1)}, u32[]{:S(2)}, u32[]{:S(2)}) async-start(bf16[4,96,640]{2,1,0:T(8,128)(2,1)} %cut_heads.6), calls=%async_computation.8 | async-start | bytes 983040 | tf_op jit(solution)/shard_map/all_to_all | solution.py:399
  33.3 16.4 %collective-permute-start.3 = (bf16[96,2560]{1,0:T(8,128)(2,1)}, bf16[96,2560]{1,0:T(8,128)(2,1)S(1)}, u32[]{:S(2)}, u32[]{:S(2)}) collective-permute-start(bf16[96,2560]{1,0:T(8,128)(2,1)} %get-tuple-element.249), channel_id=1, source_target_pairs={{0,1},{4,5},{8,9},{12,13},{16,17},{20,21},{24,25},{28,29}} | collective-permute-start | bytes 1474568 | tf_op jit(solution)/shard_map/ppermute | solution.py:44
  37.2 12.5 %collective-permute-start.4 = (bf16[96,2560]{1,0:T(8,128)(2,1)}, bf16[96,2560]{1,0:T(8,128)(2,1)S(1)}, u32[]{:S(2)}, u32[]{:S(2)}) collective-permute-start(bf16[96,2560]{1,0:T(8,128)(2,1)} %get-tuple-element.250), channel_id=1, source_target_pairs={{3,2},{7,6},{11,10},{15,14},{19,18},{23,22},{27,26},{31,30}} | collective-permute-start | bytes 1474568 | tf_op jit(solution)/shard_map/ppermute | solution.py:44
  46.1 14.3 %collective-permute-start.26 = (bf16[96,2560]{1,0:T(8,128)(2,1)}, bf16[96,2560]{1,0:T(8,128)(2,1)}, u32[]{:S(2)}, u32[]{:S(2)}) collective-permute-start(bf16[96,2560]{1,0:T(8,128)(2,1)} %get-tuple-element.265), channel_id=1, source_target_pairs={{0,1},{4,5},{8,9},{12,13},{16,17},{20,21},{24,25},{28,29}} | collective-permute-start | bytes 1474568 | tf_op jit(solution)/shard_map/ppermute | solution.py:44
  48.2 12.3 %collective-permute-start.27 = (bf16[96,2560]{1,0:T(8,128)(2,1)}, bf16[96,2560]{1,0:T(8,128)(2,1)}, u32[]{:S(2)}, u32[]{:S(2)}) collective-permute-start(bf16[96,2560]{1,0:T(8,128)(2,1)} %get-tuple-element.266), channel_id=1, source_target_pairs={{3,2},{7,6},{11,10},{15,14},{19,18},{23,22},{27,26},{31,30}} | collective-permute-start | bytes 1474568 | tf_op jit(solution)/shard_map/ppermute | solution.py:44
  51.3 19.0 %collective-permute-start.5 = (bf16[96,2560]{1,0:T(8,128)(2,1)}, bf16[96,2560]{1,0:T(8,128)(2,1)S(1)}, u32[]{:S(2)}, u32[]{:S(2)}) collective-permute-start(bf16[96,2560]{1,0:T(8,128)(2,1)} %get-tuple-element.252), channel_id=1, source_target_pairs={{0,1},{1,2},{4,5},{5,6},{8,9},{9,10},{12,13},{13,14},{16,17},{17,1... | collective-permute-start | bytes 1474568 | tf_op jit(solution)/shard_map/ppermute | solution.py:44
  53.0 17.3 %collective-permute-start.6 = (bf16[96,2560]{1,0:T(8,128)(2,1)}, bf16[96,2560]{1,0:T(8,128)(2,1)S(1)}, u32[]{:S(2)}, u32[]{:S(2)}) collective-permute-start(bf16[96,2560]{1,0:T(8,128)(2,1)} %get-tuple-element.253), channel_id=1, source_target_pairs={{2,1},{3,2},{6,5},{7,6},{10,9},{11,10},{14,13},{15,14},{18,17},{19... | collective-permute-start | bytes 1474568 | tf_op jit(solution)/shard_map/ppermute | solution.py:44
  54.5 43.7 %all-to-all-start.7 = ((bf16[4,96,640]{2,1,0:T(8,128)(2,1)}), bf16[4,96,640]{2,1,0:T(8,128)(2,1)}, u32[]{:S(2)}, u32[]{:S(2)}) async-start(bf16[4,96,640]{2,1,0:T(8,128)(2,1)} %cut_heads.5), calls=%async_computation.7 | async-start | bytes 983040 | tf_op jit(solution)/shard_map/all_to_all | solution.py:399
  64.7 23.6 %collective-permute-start.28 = (bf16[96,2560]{1,0:T(8,128)(2,1)}, bf16[96,2560]{1,0:T(8,128)(2,1)S(1)}, u32[]{:S(2)}, u32[]{:S(2)}) collective-permute-start(bf16[96,2560]{1,0:T(8,128)(2,1)} %get-tuple-element.268), channel_id=1, source_target_pairs={{0,1},{1,2},{4,5},{5,6},{8,9},{9,10},{12,13},{13,14},{16,17},{17,1... | collective-permute-start | bytes 1474568 | tf_op jit(solution)/shard_map/ppermute | solution.py:44
  68.7 19.7 %collective-permute-start.29 = (bf16[96,2560]{1,0:T(8,128)(2,1)}, bf16[96,2560]{1,0:T(8,128)(2,1)}, u32[]{:S(2)}, u32[]{:S(2)}) collective-permute-start(bf16[96,2560]{1,0:T(8,128)(2,1)} %get-tuple-element.269), channel_id=1, source_target_pairs={{2,1},{3,2},{6,5},{7,6},{10,9},{11,10},{14,13},{15,14},{18,17},{19... | collective-permute-start | bytes 1474568 | tf_op jit(solution)/shard_map/ppermute | solution.py:44
  70.1 18.2 %copy-start.2 = (bf16[4,96,2560]{2,1,0:T(8,128)(2,1)S(1)}, bf16[4,96,2560]{2,1,0:T(8,128)(2,1)}, u32[]{:S(2)}) copy-start(bf16[4,96,2560]{2,1,0:T(8,128)(2,1)} %copy-done) | copy-start | bytes 5898244
  71.8 25.5 %copy-start.13 = (bf16[1,384,2560]{2,1,0:T(8,128)(2,1)S(1)}, bf16[1,384,2560]{2,1,0:T(8,128)(2,1)}, u32[]{:S(2)}) copy-start(bf16[1,384,2560]{2,1,0:T(8,128)(2,1)} %param.16) | copy-start | bytes 5898244
  71.8 32.2 %collective-permute-start.7 = (bf16[96,2560]{1,0:T(8,128)(2,1)}, bf16[96,2560]{1,0:T(8,128)(2,1)S(1)}, u32[]{:S(2)}, u32[]{:S(2)}) collective-permute-start(bf16[96,2560]{1,0:T(8,128)(2,1)} %get-tuple-element.254), channel_id=1, source_target_pairs={{0,1},{1,2},{2,3},{4,5},{5,6},{6,7},{8,9},{9,10},{10,11},{12,13},{... | collective-permute-start | bytes 1474568 | tf_op jit(solution)/shard_map/ppermute | solution.py:44
  76.0 28.0 %copy-start.38 = (f32[2560]{0:T(1024)S(1)}, f32[2560]{0:T(1024)}, u32[]{:S(2)}) copy-start(f32[2560]{0:T(1024)} %param.19) | copy-start | bytes 30724
  76.0 28.0 %collective-permute-start.8 = (bf16[96,2560]{1,0:T(8,128)(2,1)}, bf16[96,2560]{1,0:T(8,128)(2,1)S(1)}, u32[]{:S(2)}, u32[]{:S(2)}) collective-permute-start(bf16[96,2560]{1,0:T(8,128)(2,1)} %get-tuple-element.255), channel_id=1, source_target_pairs={{1,0},{2,1},{3,2},{5,4},{6,5},{7,6},{9,8},{10,9},{11,10},{13,12},{... | collective-permute-start | bytes 1474568 | tf_op jit(solution)/shard_map/ppermute | solution.py:44
  90.9 24.9 %collective-permute-start.30 = (bf16[96,2560]{1,0:T(8,128)(2,1)}, bf16[96,2560]{1,0:T(8,128)(2,1)}, u32[]{:S(2)}, u32[]{:S(2)}) collective-permute-start(bf16[96,2560]{1,0:T(8,128)(2,1)} %get-tuple-element.270), channel_id=1, source_target_pairs={{0,1},{1,2},{2,3},{4,5},{5,6},{6,7},{8,9},{9,10},{10,11},{12,13},{... | collective-permute-start | bytes 1474568 | tf_op jit(solution)/shard_map/ppermute | solution.py:44
  96.1 19.7 %collective-permute-start.31 = (bf16[96,2560]{1,0:T(8,128)(2,1)}, bf16[96,2560]{1,0:T(8,128)(2,1)}, u32[]{:S(2)}, u32[]{:S(2)}) collective-permute-start(bf16[96,2560]{1,0:T(8,128)(2,1)} %get-tuple-element.271), channel_id=1, source_target_pairs={{1,0},{2,1},{3,2},{5,4},{6,5},{7,6},{9,8},{10,9},{11,10},{13,12},{... | collective-permute-start | bytes 1474568 | tf_op jit(solution)/shard_map/ppermute | solution.py:44
  98.3 42.8 %all-to-all-start.9 = ((bf16[4,96,640]{2,1,0:T(8,128)(2,1)}), bf16[4,96,640]{2,1,0:T(8,128)(2,1)}, u32[]{:S(2)}, u32[]{:S(2)}) async-start(bf16[4,96,640]{2,1,0:T(8,128)(2,1)} %cut_heads.7), calls=%async_computation.9 | async-start | bytes 983040 | tf_op jit(solution)/shard_map/all_to_all | solution.py:399
  109.6 20.3 %collective-permute-start.10 = (bf16[96,2560]{1,0:T(8,128)(2,1)S(1)}, bf16[96,2560]{1,0:T(8,128)(2,1)S(1)}, u32[]{:S(2)}, u32[]{:S(2)}) collective-permute-start(bf16[96,2560]{1,0:T(8,128)(2,1)S(1)} %unit_gradient.4.refs_0_), channel_id=1, source_target_pairs={{1,0},{2,1},{3,2},{5,4},{6,5},{7,6},{9,8},{10,9},{11,10},{13,12},{... | collective-permute-start | bytes 1474568 | tf_op jit(solution)/shard_map/ppermute | solution.py:44
  111.2 18.8 %collective-permute-start.9 = (bf16[96,2560]{1,0:T(8,128)(2,1)S(1)}, bf16[96,2560]{1,0:T(8,128)(2,1)S(1)}, u32[]{:S(2)}, u32[]{:S(2)}) collective-permute-start(bf16[96,2560]{1,0:T(8,128)(2,1)S(1)} %unit_gradient.4.refs_0_), channel_id=1, source_target_pairs={{0,1},{1,2},{2,3},{4,5},{5,6},{6,7},{8,9},{9,10},{10,11},{12,13},{... | collective-permute-start | bytes 1474568 | tf_op jit(solution)/shard_map/ppermute | solution.py:44
  118.2 27.2 %collective-permute-start.33 = (bf16[96,2560]{1,0:T(8,128)(2,1)}, bf16[96,2560]{1,0:T(8,128)(2,1)}, u32[]{:S(2)}, u32[]{:S(2)}) collective-permute-start(bf16[96,2560]{1,0:T(8,128)(2,1)} %unit_gradient.6.refs_7_), channel_id=1, source_target_pairs={{1,0},{2,1},{3,2},{5,4},{6,5},{7,6},{9,8},{10,9},{11,10},{13,12},{... | collective-permute-start | bytes 1474568 | tf_op jit(solution)/shard_map/ppermute | solution.py:44
  119.5 25.9 %collective-permute-start.32 = (bf16[96,2560]{1,0:T(8,128)(2,1)}, bf16[96,2560]{1,0:T(8,128)(2,1)}, u32[]{:S(2)}, u32[]{:S(2)}) collective-permute-start(bf16[96,2560]{1,0:T(8,128)(2,1)} %unit_gradient.6.refs_7_), channel_id=1, source_target_pairs={{0,1},{1,2},{2,3},{4,5},{5,6},{6,7},{8,9},{9,10},{10,11},{12,13},{... | collective-permute-start | bytes 1474568 | tf_op jit(solution)/shard_map/ppermute | solution.py:44
  131.5 22.3 %collective-permute-start.11 = (bf16[96,2560]{1,0:T(8,128)(2,1)}, bf16[96,2560]{1,0:T(8,128)(2,1)}, u32[]{:S(2)}, u32[]{:S(2)}) collective-permute-start(bf16[96,2560]{1,0:T(8,128)(2,1)} %get-tuple-element.259), channel_id=1, source_target_pairs={{0,1},{1,2},{2,3},{4,5},{5,6},{6,7},{8,9},{9,10},{10,11},{12,13},{... | collective-permute-start | bytes 1474568 | tf_op jit(solution)/shard_map/ppermute | solution.py:44
  139.8 14.6 %collective-permute-start.12 = (bf16[96,2560]{1,0:T(8,128)(2,1)}, bf16[96,2560]{1,0:T(8,128)(2,1)}, u32[]{:S(2)}, u32[]{:S(2)}) collective-permute-start(bf16[96,2560]{1,0:T(8,128)(2,1)} %get-tuple-element.260), channel_id=1, source_target_pairs={{1,0},{2,1},{3,2},{5,4},{6,5},{7,6},{9,8},{10,9},{11,10},{13,12},{... | collective-permute-start | bytes 1474568 | tf_op jit(solution)/shard_map/ppermute | solution.py:44
  147.9 16.2 %collective-permute-start.34 = (bf16[96,2560]{1,0:T(8,128)(2,1)S(1)}, bf16[96,2560]{1,0:T(8,128)(2,1)S(1)}, u32[]{:S(2)}, u32[]{:S(2)}) collective-permute-start(bf16[96,2560]{1,0:T(8,128)(2,1)S(1)} %get-tuple-element.275), channel_id=1, source_target_pairs={{0,1},{1,2},{2,3},{4,5},{5,6},{6,7},{8,9},{9,10},{10,11},{12,13},{... | collective-permute-start | bytes 1474568 | tf_op jit(solution)/shard_map/ppermute | solution.py:44
  152.5 15.9 %collective-permute-start.35 = (bf16[96,2560]{1,0:T(8,128)(2,1)S(1)}, bf16[96,2560]{1,0:T(8,128)(2,1)S(1)}, u32[]{:S(2)}, u32[]{:S(2)}) collective-permute-start(bf16[96,2560]{1,0:T(8,128)(2,1)S(1)} %get-tuple-element.276), channel_id=1, source_target_pairs={{1,0},{2,1},{3,2},{5,4},{6,5},{7,6},{9,8},{10,9},{11,10},{13,12},{... | collective-permute-start | bytes 1474568 | tf_op jit(solution)/shard_map/ppermute | solution.py:44
  156.9 17.5 %collective-permute-start.13 = (bf16[96,2560]{1,0:T(8,128)(2,1)S(1)}, bf16[96,2560]{1,0:T(8,128)(2,1)S(1)}, u32[]{:S(2)}, u32[]{:S(2)}) collective-permute-start(bf16[96,2560]{1,0:T(8,128)(2,1)S(1)} %get-tuple-element.261), channel_id=1, source_target_pairs={{0,1},{1,2},{2,3},{4,5},{5,6},{6,7},{8,9},{9,10},{10,11},{12,13},{... | collective-permute-start | bytes 1474568 | tf_op jit(solution)/shard_map/ppermute | solution.py:44
  160.8 17.5 %collective-permute-start.14 = (bf16[96,2560]{1,0:T(8,128)(2,1)S(1)}, bf16[96,2560]{1,0:T(8,128)(2,1)S(1)}, u32[]{:S(2)}, u32[]{:S(2)}) collective-permute-start(bf16[96,2560]{1,0:T(8,128)(2,1)S(1)} %get-tuple-element.262), channel_id=1, source_target_pairs={{1,0},{2,1},{3,2},{5,4},{6,5},{7,6},{9,8},{10,9},{11,10},{13,12},{... | collective-permute-start | bytes 1474568 | tf_op jit(solution)/shard_map/ppermute | solution.py:44
  164.1 30.1 %copy-start.14 = (bf16[96,2560]{1,0:T(8,128)(2,1)}, bf16[96,2560]{1,0:T(8,128)(2,1)S(1)}, u32[]{:S(2)}) copy-start(bf16[96,2560]{1,0:T(8,128)(2,1)S(1)} %collective-permute-done.34.right_ref.refs_9_) | copy-start | bytes 1474564
  168.4 25.9 %copy-start.15 = (bf16[96,2560]{1,0:T(8,128)(2,1)}, bf16[96,2560]{1,0:T(8,128)(2,1)S(1)}, u32[]{:S(2)}) copy-start(bf16[96,2560]{1,0:T(8,128)(2,1)S(1)} %collective-permute-done.35.left_ref.refs_12_) | copy-start | bytes 1474564
  168.4 25.9 %slice-start = ((s8[6553600]{0:T(1024)(128)(4,1)}), s8[4194304]{0:T(1024)(128)(4,1)S(1)}, s32[]{:S(2)}) async-start(s8[6553600]{0:T(1024)(128)(4,1)} %bitcast.45), calls=%async_computation.10 | async-start | bytes 8388608
  169.7 15.2 %collective-permute-start.36 = (bf16[96,2560]{1,0:T(8,128)(2,1)S(1)}, bf16[96,2560]{1,0:T(8,128)(2,1)S(1)}, u32[]{:S(2)}, u32[]{:S(2)}) collective-permute-start(bf16[96,2560]{1,0:T(8,128)(2,1)S(1)} %get-tuple-element.277), channel_id=1, source_target_pairs={{0,1},{1,2},{2,3},{4,5},{5,6},{6,7},{8,9},{9,10},{10,11},{12,13},{... | collective-permute-start | bytes 1474568 | tf_op jit(solution)/shard_map/ppermute | solution.py:44
  171.8 22.5 %slice-start.1 = ((s8[6553600]{0:T(1024)(128)(4,1)}), s8[2359296]{0:T(1024)(128)(4,1)S(1)}, s32[]{:S(2)}) async-start(s8[6553600]{0:T(1024)(128)(4,1)} %bitcast.45), calls=%async_computation.11 | async-start | bytes 4718592
  171.8 17.1 %collective-permute-start.37 = (bf16[96,2560]{1,0:T(8,128)(2,1)S(1)}, bf16[96,2560]{1,0:T(8,128)(2,1)S(1)}, u32[]{:S(2)}, u32[]{:S(2)}) collective-permute-start(bf16[96,2560]{1,0:T(8,128)(2,1)S(1)} %get-tuple-element.278), channel_id=1, source_target_pairs={{1,0},{2,1},{3,2},{5,4},{6,5},{7,6},{9,8},{10,9},{11,10},{13,12},{... | collective-permute-start | bytes 1474568 | tf_op jit(solution)/shard_map/ppermute | solution.py:44
  174.4 19.9 %copy-start.16 = (bf16[96,2560]{1,0:T(8,128)(2,1)}, bf16[96,2560]{1,0:T(8,128)(2,1)S(1)}, u32[]{:S(2)}) copy-start(bf16[96,2560]{1,0:T(8,128)(2,1)S(1)} %collective-permute-done.13.right_ref.refs_3_) | copy-start | bytes 1474564
  178.3 15.9 %copy-start.18 = (bf16[96,2560]{1,0:T(8,128)(2,1)}, bf16[96,2560]{1,0:T(8,128)(2,1)S(1)}, u32[]{:S(2)}) copy-start(bf16[96,2560]{1,0:T(8,128)(2,1)S(1)} %collective-permute-done.14.left_ref.refs_6_) | copy-start | bytes 1474564
  179.7 23.1 %collective-permute-start.15 = (bf16[96,2560]{1,0:T(8,128)(2,1)S(1)}, bf16[96,2560]{1,0:T(8,128)(2,1)S(1)}, u32[]{:S(2)}, u32[]{:S(2)}) collective-permute-start(bf16[96,2560]{1,0:T(8,128)(2,1)S(1)} %get-tuple-element.263), channel_id=1, source_target_pairs={{0,1},{1,2},{2,3},{4,5},{5,6},{6,7},{8,9},{9,10},{10,11},{12,13},{... | collective-permute-start | bytes 1474568 | tf_op jit(solution)/shard_map/ppermute | solution.py:44
  182.3 20.5 %collective-permute-start.16 = (bf16[96,2560]{1,0:T(8,128)(2,1)S(1)}, bf16[96,2560]{1,0:T(8,128)(2,1)S(1)}, u32[]{:S(2)}, u32[]{:S(2)}) collective-permute-start(bf16[96,2560]{1,0:T(8,128)(2,1)S(1)} %get-tuple-element.264), channel_id=1, source_target_pairs={{1,0},{2,1},{3,2},{5,4},{6,5},{7,6},{9,8},{10,9},{11,10},{13,12},{... | collective-permute-start | bytes 1474568 | tf_op jit(solution)/shard_map/ppermute | solution.py:44
  184.9 17.9 %copy-start.20 = (bf16[96,2560]{1,0:T(8,128)(2,1)}, bf16[96,2560]{1,0:T(8,128)(2,1)S(1)}, u32[]{:S(2)}) copy-start(bf16[96,2560]{1,0:T(8,128)(2,1)S(1)} %collective-permute-done.36.right_ref.refs_10_) | copy-start | bytes 1474564
  190.2 20.7 %collective-permute-start.38 = (bf16[96,2560]{1,0:T(8,128)(2,1)S(1)}, bf16[96,2560]{1,0:T(8,128)(2,1)S(1)}, u32[]{:S(2)}, u32[]{:S(2)}) collective-permute-start(bf16[96,2560]{1,0:T(8,128)(2,1)S(1)} %get-tuple-element.279), channel_id=1, source_target_pairs={{0,1},{1,2},{2,3},{4,5},{5,6},{6,7},{8,9},{9,10},{10,11},{12,13},{... | collective-permute-start | bytes 1474568 | tf_op jit(solution)/shard_map/ppermute | solution.py:44
  192.7 18.1 %collective-permute-start.39 = (bf16[96,2560]{1,0:T(8,128)(2,1)S(1)}, bf16[96,2560]{1,0:T(8,128)(2,1)S(1)}, u32[]{:S(2)}, u32[]{:S(2)}) collective-permute-start(bf16[96,2560]{1,0:T(8,128)(2,1)S(1)} %get-tuple-element.280), channel_id=1, source_target_pairs={{1,0},{2,1},{3,2},{5,4},{6,5},{7,6},{9,8},{10,9},{11,10},{13,12},{... | collective-permute-start | bytes 1474568 | tf_op jit(solution)/shard_map/ppermute | solution.py:44
  203.5 16.9 %collective-permute-start.20 = (bf16[96,2560]{1,0:T(8,128)(2,1)S(1)}, bf16[96,2560]{1,0:T(8,128)(2,1)}, u32[]{:S(2)}, u32[]{:S(2)}) collective-permute-start(bf16[96,2560]{1,0:T(8,128)(2,1)S(1)} %unit_gradient.5.refs_0_), channel_id=1, source_target_pairs={{1,0},{2,1},{3,2},{5,4},{6,5},{7,6},{9,8},{10,9},{11,10},{13,12},{... | collective-permute-start | bytes 1474568 | tf_op jit(solution)/shard_map/ppermute | solution.py:44
  204.8 16.9 %collective-permute-start.17 = (bf16[96,2560]{1,0:T(8,128)(2,1)S(1)}, bf16[96,2560]{1,0:T(8,128)(2,1)}, u32[]{:S(2)}, u32[]{:S(2)}) collective-permute-start(bf16[96,2560]{1,0:T(8,128)(2,1)S(1)} %unit_gradient.5.refs_0_), channel_id=1, source_target_pairs={{0,1},{1,2},{2,3},{4,5},{5,6},{6,7},{8,9},{9,10},{10,11},{12,13},{... | collective-permute-start | bytes 1474568 | tf_op jit(solution)/shard_map/ppermute | solution.py:44
  210.9 45.2 %copy-start.17 = (bf16[96,2560]{1,0:T(8,128)(2,1)S(1)}, bf16[96,2560]{1,0:T(8,128)(2,1)}, u32[]{:S(2)}) copy-start(bf16[96,2560]{1,0:T(8,128)(2,1)} %copy-done.16) | copy-start | bytes 1474564
  210.9 45.2 %copy-start.19 = (bf16[96,2560]{1,0:T(8,128)(2,1)S(1)}, bf16[96,2560]{1,0:T(8,128)(2,1)}, u32[]{:S(2)}) copy-start(bf16[96,2560]{1,0:T(8,128)(2,1)} %copy-done.18) | copy-start | bytes 1474564
  211.6 19.4 %collective-permute-start.43 = (bf16[96,2560]{1,0:T(8,128)(2,1)S(1)}, bf16[96,2560]{1,0:T(8,128)(2,1)}, u32[]{:S(2)}, u32[]{:S(2)}) collective-permute-start(bf16[96,2560]{1,0:T(8,128)(2,1)S(1)} %unit_gradient.7.refs_7_), channel_id=1, source_target_pairs={{1,0},{2,1},{3,2},{5,4},{6,5},{7,6},{9,8},{10,9},{11,10},{13,12},{... | collective-permute-start | bytes 1474568 | tf_op jit(solution)/shard_map/ppermute | solution.py:44
  212.9 19.3 %collective-permute-start.40 = (bf16[96,2560]{1,0:T(8,128)(2,1)S(1)}, bf16[96,2560]{1,0:T(8,128)(2,1)}, u32[]{:S(2)}, u32[]{:S(2)}) collective-permute-start(bf16[96,2560]{1,0:T(8,128)(2,1)S(1)} %unit_gradient.7.refs_7_), channel_id=1, source_target_pairs={{0,1},{1,2},{2,3},{4,5},{5,6},{6,7},{8,9},{9,10},{10,11},{12,13},{... | collective-permute-start | bytes 1474568 | tf_op jit(solution)/shard_map/ppermute | solution.py:44
  220.4 21.1 %collective-permute-start.21 = (bf16[96,2560]{1,0:T(8,128)(2,1)}, bf16[96,2560]{1,0:T(8,128)(2,1)}, u32[]{:S(2)}, u32[]{:S(2)}) collective-permute-start(bf16[96,2560]{1,0:T(8,128)(2,1)} %collective-permute-done.20.refs_4_), channel_id=1, source_target_pairs={{1,0},{2,1},{5,4},{6,5},{9,8},{10,9},{13,12},{14,13},{17,16},{18,1... | collective-permute-start | bytes 1474568 | tf_op jit(solution)/shard_map/ppermute | solution.py:44
  221.7 21.1 %collective-permute-start.18 = (bf16[96,2560]{1,0:T(8,128)(2,1)}, bf16[96,2560]{1,0:T(8,128)(2,1)}, u32[]{:S(2)}, u32[]{:S(2)}) collective-permute-start(bf16[96,2560]{1,0:T(8,128)(2,1)} %collective-permute-done.17.refs_1_), channel_id=1, source_target_pairs={{1,2},{2,3},{5,6},{6,7},{9,10},{10,11},{13,14},{14,15},{17,18},{18... | collective-permute-start | bytes 1474568 | tf_op jit(solution)/shard_map/ppermute | solution.py:44
  230.9 21.1 %collective-permute-start.44 = (bf16[96,2560]{1,0:T(8,128)(2,1)}, bf16[96,2560]{1,0:T(8,128)(2,1)}, u32[]{:S(2)}, u32[]{:S(2)}) collective-permute-start(bf16[96,2560]{1,0:T(8,128)(2,1)} %collective-permute-done.43.refs_11_), channel_id=1, source_target_pairs={{1,0},{2,1},{5,4},{6,5},{9,8},{10,9},{13,12},{14,13},{17,16},{18,1... | collective-permute-start | bytes 1474568 | tf_op jit(solution)/shard_map/ppermute | solution.py:44
  232.2 21.1 %collective-permute-start.41 = (bf16[96,2560]{1,0:T(8,128)(2,1)}, bf16[96,2560]{1,0:T(8,128)(2,1)}, u32[]{:S(2)}, u32[]{:S(2)}) collective-permute-start(bf16[96,2560]{1,0:T(8,128)(2,1)} %collective-permute-done.40.refs_8_), channel_id=1, source_target_pairs={{1,2},{2,3},{5,6},{6,7},{9,10},{10,11},{13,14},{14,15},{17,18},{18... | collective-permute-start | bytes 1474568 | tf_op jit(solution)/shard_map/ppermute | solution.py:44
  241.5 23.8 %collective-permute-start.22 = (bf16[96,2560]{1,0:T(8,128)(2,1)}, bf16[96,2560]{1,0:T(8,128)(2,1)}, u32[]{:S(2)}, u32[]{:S(2)}) collective-permute-start(bf16[96,2560]{1,0:T(8,128)(2,1)} %collective-permute-done.21.refs_5_), channel_id=1, source_target_pairs={{1,0},{5,4},{9,8},{13,12},{17,16},{21,20},{25,24},{29,28}} | collective-permute-start | bytes 1474568 | tf_op jit(solution)/shard_map/ppermute | solution.py:44
  242.8 22.5 %collective-permute-start.19 = (bf16[96,2560]{1,0:T(8,128)(2,1)}, bf16[96,2560]{1,0:T(8,128)(2,1)}, u32[]{:S(2)}, u32[]{:S(2)}) collective-permute-start(bf16[96,2560]{1,0:T(8,128)(2,1)} %collective-permute-done.18.refs_2_), channel_id=1, source_target_pairs={{2,3},{6,7},{10,11},{14,15},{18,19},{22,23},{26,27},{30,31}} | collective-permute-start | bytes 1474568 | tf_op jit(solution)/shard_map/ppermute | solution.py:44
  252.0 14.9 %collective-permute-start.45 = (bf16[96,2560]{1,0:T(8,128)(2,1)}, bf16[96,2560]{1,0:T(8,128)(2,1)}, u32[]{:S(2)}, u32[]{:S(2)}) collective-permute-start(bf16[96,2560]{1,0:T(8,128)(2,1)} %collective-permute-done.44.refs_12_), channel_id=1, source_target_pairs={{1,0},{5,4},{9,8},{13,12},{17,16},{21,20},{25,24},{29,28}} | collective-permute-start | bytes 1474568 | tf_op jit(solution)/shard_map/ppermute | solution.py:44
  253.3 13.6 %collective-permute-start.42 = (bf16[96,2560]{1,0:T(8,128)(2,1)}, bf16[96,2560]{1,0:T(8,128)(2,1)}, u32[]{:S(2)}, u32[]{:S(2)}) collective-permute-start(bf16[96,2560]{1,0:T(8,128)(2,1)} %collective-permute-done.41.refs_9_), channel_id=1, source_target_pairs={{2,3},{6,7},{10,11},{14,15},{18,19},{22,23},{26,27},{30,31}} | collective-permute-start | bytes 1474568 | tf_op jit(solution)/shard_map/ppermute | solution.py:44
  276.7 23.6 %copy-start.33 = (bf16[96,2560]{1,0:T(8,128)(2,1)}, bf16[96,2560]{1,0:T(8,128)(2,1)S(1)}, u32[]{:S(2)}) copy-start(bf16[96,2560]{1,0:T(8,128)(2,1)S(1)} %get-tuple-element.185.refs_0_) | copy-start | bytes 1474564 | tf_op jit(solution)/shard_map/cond
  276.7 67.2 %collective-permute-start.2 = (bf16[640,2560]{1,0:T(8,128)(2,1)}, bf16[640,2560]{1,0:T(8,128)(2,1)}, u32[]{:S(2)}, u32[]{:S(2)}) collective-permute-start(bf16[640,2560]{1,0:T(8,128)(2,1)} %get-tuple-element.182), channel_id=1, source_target_pairs={{0,16},{4,20},{8,24},{12,28},{16,0},{20,4},{24,8},{28,12},{1,17},{... | collective-permute-start | bytes 9830408 | tf_op jit(solution)/shard_map/cond/branch_2_fun/ppermute | solution.py:404
  278.2 22.0 %all-to-all-start.4 = ((bf16[4,192,640]{2,1,0:T(8,128)(2,1)}), bf16[4,192,640]{2,1,0:T(8,128)(2,1)S(1)}, u32[]{:S(2)}, u32[]{:S(2)}) async-start(bf16[4,192,640]{2,1,0:T(8,128)(2,1)} %get-tuple-element.183), calls=%async_computation.4 | async-start | bytes 1966080 | tf_op jit(solution)/shard_map/cond/branch_2_fun/all_to_all | solution.py:399
  300.2 24.3 %all-to-all-start.5 = ((bf16[4,192,640]{2,1,0:T(8,128)(2,1)}), bf16[4,192,640]{2,1,0:T(8,128)(2,1)S(1)}, u32[]{:S(2)}, u32[]{:S(2)}) async-start(bf16[4,192,640]{2,1,0:T(8,128)(2,1)} %get-tuple-element.200), calls=%async_computation.5 | async-start | bytes 1966080 | tf_op jit(solution)/shard_map/cond/branch_2_fun/all_to_all | solution.py:399
  (24 other events, 171.9 us)

commit v11 on v10

--- a/solution.py
+++ b/solution.py
@@ -72,6 +72,20 @@
         + ([] if token is None else [token_in(token)]),
         [((members, size, rows), heads.dtype, (members, step, rows), lambda i: (0, i, 0))],
         moved=4 * size * inner,
+    )[0]
+
+
+def token_of(weights):
+    def body(weights_ref, token_out):
+        token_out[...] = jnp.zeros((8, 128), jnp.float32)
+
+    return call(
+        body,
+        "token_of",
+        (1,),
+        [(weights, (16, 128), fixed(0, 0))],
+        [TOKEN_OUT],
+        moved=8192,
     )[0]
 
 
@@ -472,7 +486,7 @@
         mine[e][q] = swapped(piece)
 
     for q in range(count):
-        fetch(0, q, None)
+        fetch(0, q, token_of(weights) if q else None)
     done = None
     for e in range(rounds):
         parts, moving = [None] * count, [None] * count

time: 354 us -> 362 us (1.023)
  waiting for transfers between devices: 96.3 us -> 101 us
    pallas_call x29 -> x30, Pallas kernels: 97.2 us -> 99.2 us  [call(): pl.pallas_call(body, name=name, out_shape=[jax.ShapeDtypeStruct(shape, ki...]
    unnamed x72 -> x68, local copies, waits for them, and re-layouts: 9.37 us -> 10.3 us
  transfers between devices with their start and end apart: 50 -> 50, of which waited for: 17 -> 16; matrix products, arithmetic and copies ran while one was open for 1% -> 1% of each run, Pallas kernels for 23% -> 23%
where the time goes in v11:
time: 362 us; the launch traced here: 360 us
  starting transfers between devices  136 us (38%)
  waiting for transfers between devices  101 us (28%)
  Pallas kernels  99.2 us (27%)
  local copies, waits for them, and re-layouts  10.3 us (3%)
  between operations  8.71 us (2%)
  other arithmetic  4.54 us (1%)
    ppermute x40, starting transfers between devices, hop(): return lax.ppermute(value, 'fsdp', [(i, i + step) for i in pairs])  100 us
    pallas_call x30, Pallas kernels, call(): pl.pallas_call(body, name=name, out_shape=[jax.ShapeDtypeStruct(shape, ki...  99.2 us
    ppermute x40, waiting for transfers between devices, hop(): return lax.ppermute(value, 'fsdp', [(i, i + step) for i in pairs])  56.9 us
    all_to_all x6, starting transfers between devices, swapped(): return lax.all_to_all(blocks, 'fsdp', 0, 0, tiled=False)  27.9 us
    all_to_all x6, waiting for transfers between devices, swapped(): return lax.all_to_all(blocks, 'fsdp', 0, 0, tiled=False)  24.8 us
    ppermute x1, waiting for transfers between devices, tail(): lax.ppermute(half, 'rep', [(i, (i + (1 << bit_place)) % length) for i in...  19.4 us
    unnamed x68, local copies, waits for them, and re-layouts  10.3 us
  transfers between devices with their start and end apart: 50, of which 16 were waited for; matrix products, arithmetic and copies ran while one was open for 1% of the time, Pallas kernels for 23%

profile of v11, /device:TPU:0, one launch (start us, length us, event | category | flops | bytes accessed | tf_op | source)
XLA Modules:
  0.0 360.2 jit_solution(15044066497520693142)
XLA Ops:
  0.6 1.5 copy-done.10
  3.0 6.3 %all-to-all-start.6 = ((bf16[4,96,640]{2,1,0:T(8,128)(2,1)}), bf16[4,96,640]{2,1,0:T(8,128)(2,1)S(1)}, u32[]{:S(2)}, u32[]{:S(2)}) async-start(bf16[4,96,640]{2,1,0:T(8,128)(2,1)} %cut_heads.4), calls=%async_computation.6 | async-start | bytes 983040 | tf_op jit(solution)/shard_map/all_to_all | solution.py:413
  9.9 3.6 %multiply_convert_fusion.weights_ref.refs_14_ = bf16[640,2560]{1,0:T(8,128)(2,1)S(1)} fusion(f32[]{:T(128)} %bitcast.32, f32[1,640,2560]{2,1,0:T(8,128)} %param.12), kind=kLoop, calls=%fused_computation | loop fusion | flops 4915200 | bytes 9830404 | tf_op jit(solution)/shard_map/convert_element_type | solution.py:456
  13.6 1.7 copy-done.26
  17.1 6.0 %all-to-all-done.6.mine_ref.refs_14_ = bf16[4,96,640]{2,1,0:T(8,128)(2,1)S(1)} async-done(((bf16[4,96,640]{2,1,0:T(8,128)(2,1)}), bf16[4,96,640]{2,1,0:T(8,128)(2,1)S(1)}, u32[]{:S(2)}, u32[]{:S(2)}) %all-to-all-start.6) | async-done | bytes 491552 | tf_op jit(solution)/shard_map/all_to_all | solution.py:413
  23.1 3.5 all-to-all-start.8
  27.6 2.8 collective-permute-start.24
  30.4 2.8 collective-permute-start.23
  34.5 4.2 %partial_products.4 = (bf16[4,96,2560]{2,1,0:T(8,128)(2,1)S(1)}, bf16[96,2560]{1,0:T(8,128)(2,1)}, bf16[96,2560]{1,0:T(8,128)(2,1)}) custom-call(bf16[4,96,640]{2,1,0:T(8,128)(2,1)S(1)} %all-to-all-done.6.mine_ref.refs_14_, bf16[640,2560]{1,0:T(8,128)(2,1)} %copy-done.26), custom_call_target="tpu_custom_call" | custom-call | flops 1258291200 | bytes 5734400 | tf_op jit(solution)/shard_map/partial_products/pallas_call | solution.py:16
  38.7 3.8 %collective-permute-start.3 = (bf16[96,2560]{1,0:T(8,128)(2,1)}, bf16[96,2560]{1,0:T(8,128)(2,1)S(1)}, u32[]{:S(2)}, u32[]{:S(2)}) collective-permute-start(bf16[96,2560]{1,0:T(8,128)(2,1)} %get-tuple-element.249), channel_id=1, source_target_pairs={{0,1},{4,5},{8,9},{12,13},{16,17},{20,21},{24,25},{28,29}} | collective-permute-start | bytes 1474568 | tf_op jit(solution)/shard_map/ppermute | solution.py:44
  46.6 4.4 %partial_products.6 = (bf16[4,96,2560]{2,1,0:T(8,128)(2,1)S(1)}, bf16[96,2560]{1,0:T(8,128)(2,1)}, bf16[96,2560]{1,0:T(8,128)(2,1)}) custom-call(bf16[4,96,640]{2,1,0:T(8,128)(2,1)S(1)} %all-to-all-done.8.mine_ref.refs_15_, bf16[640,2560]{1,0:T(8,128)(2,1)} %copy-done.26, f32[8,128]{1,0:T(8,128)S(1)} %broadcast_in_dim.48.refs_0_), custom_call_target="tpu_custom_call" | custom-call | flops 1258291200 | bytes 5734400 | tf_op jit(solution)/shard_map/partial_products/pallas_call | solution.py:16
  55.1 2.5 next_payload.10
  60.5 6.2 %all-to-all-start.7 = ((bf16[4,96,640]{2,1,0:T(8,128)(2,1)}), bf16[4,96,640]{2,1,0:T(8,128)(2,1)}, u32[]{:S(2)}, u32[]{:S(2)}) async-start(bf16[4,96,640]{2,1,0:T(8,128)(2,1)} %cut_heads.5), calls=%async_computation.7 | async-start | bytes 983040 | tf_op jit(solution)/shard_map/all_to_all | solution.py:413
  66.7 1.5 copy-done.1
  68.3 2.5 next_payload.15
  70.8 3.9 %collective-permute-start.28 = (bf16[96,2560]{1,0:T(8,128)(2,1)}, bf16[96,2560]{1,0:T(8,128)(2,1)S(1)}, u32[]{:S(2)}, u32[]{:S(2)}) collective-permute-start(bf16[96,2560]{1,0:T(8,128)(2,1)} %get-tuple-element.268), channel_id=1, source_target_pairs={{0,1},{1,2},{4,5},{5,6},{8,9},{9,10},{12,13},{13,14},{16,17},{17,1... | collective-permute-start | bytes 1474568 | tf_op jit(solution)/shard_map/ppermute | solution.py:44
  76.3 1.6 next_payload.11
  77.9 4.2 %collective-permute-start.7 = (bf16[96,2560]{1,0:T(8,128)(2,1)}, bf16[96,2560]{1,0:T(8,128)(2,1)S(1)}, u32[]{:S(2)}, u32[]{:S(2)}) collective-permute-start(bf16[96,2560]{1,0:T(8,128)(2,1)} %get-tuple-element.254), channel_id=1, source_target_pairs={{0,1},{1,2},{2,3},{4,5},{5,6},{6,7},{8,9},{9,10},{10,11},{12,13},{... | collective-permute-start | bytes 1474568 | tf_op jit(solution)/shard_map/ppermute | solution.py:44
  83.4 11.1 %collective-permute-done.28.right_ref = bf16[96,2560]{1,0:T(8,128)(2,1)S(1)} collective-permute-done((bf16[96,2560]{1,0:T(8,128)(2,1)}, bf16[96,2560]{1,0:T(8,128)(2,1)S(1)}, u32[]{:S(2)}, u32[]{:S(2)}) %collective-permute-start.28) | collective-permute-done | bytes 491552 | tf_op jit(solution)/shard_map/ppermute | solution.py:44
  94.5 2.5 next_payload.16
  97.0 5.8 %collective-permute-start.30 = (bf16[96,2560]{1,0:T(8,128)(2,1)}, bf16[96,2560]{1,0:T(8,128)(2,1)}, u32[]{:S(2)}, u32[]{:S(2)}) collective-permute-start(bf16[96,2560]{1,0:T(8,128)(2,1)} %get-tuple-element.270), channel_id=1, source_target_pairs={{0,1},{1,2},{2,3},{4,5},{5,6},{6,7},{8,9},{9,10},{10,11},{12,13},{... | collective-permute-start | bytes 1474568 | tf_op jit(solution)/shard_map/ppermute | solution.py:44
  105.1 4.4 %all-to-all-start.9 = ((bf16[4,96,640]{2,1,0:T(8,128)(2,1)}), bf16[4,96,640]{2,1,0:T(8,128)(2,1)}, u32[]{:S(2)}, u32[]{:S(2)}) async-start(bf16[4,96,640]{2,1,0:T(8,128)(2,1)} %cut_heads.7), calls=%async_computation.9 | async-start | bytes 983040 | tf_op jit(solution)/shard_map/all_to_all | solution.py:413
  109.5 1.5 copy-done.4
  111.1 1.5 copy-done.7
  113.3 1.6 collective-permute-start.10
  114.8 5.0 %collective-permute-start.9 = (bf16[96,2560]{1,0:T(8,128)(2,1)S(1)}, bf16[96,2560]{1,0:T(8,128)(2,1)S(1)}, u32[]{:S(2)}, u32[]{:S(2)}) collective-permute-start(bf16[96,2560]{1,0:T(8,128)(2,1)S(1)} %unit_gradient.4.refs_0_), channel_id=1, source_target_pairs={{0,1},{1,2},{2,3},{4,5},{5,6},{6,7},{8,9},{9,10},{10,11},{12,13},{... | collective-permute-start | bytes 1474568 | tf_op jit(solution)/shard_map/ppermute | solution.py:44
  119.8 2.4 unit_gradient.6.refs_7_
  123.5 7.5 %collective-permute-start.32 = (bf16[96,2560]{1,0:T(8,128)(2,1)}, bf16[96,2560]{1,0:T(8,128)(2,1)}, u32[]{:S(2)}, u32[]{:S(2)}) collective-permute-start(bf16[96,2560]{1,0:T(8,128)(2,1)} %unit_gradient.6.refs_7_), channel_id=1, source_target_pairs={{0,1},{1,2},{2,3},{4,5},{5,6},{6,7},{8,9},{9,10},{10,11},{12,13},{... | collective-permute-start | bytes 1474568 | tf_op jit(solution)/shard_map/ppermute | solution.py:44
  131.1 4.3 %partial_products.5 = (bf16[4,96,2560]{2,1,0:T(8,128)(2,1)S(1)}, bf16[96,2560]{1,0:T(8,128)(2,1)}, bf16[96,2560]{1,0:T(8,128)(2,1)}) custom-call(bf16[4,96,640]{2,1,0:T(8,128)(2,1)} %all-to-all-done.7.mine_ref.refs_14_, bf16[640,2560]{1,0:T(8,128)(2,1)} %copy-done.26, f32[8,128]{1,0:T(8,128)S(1)} %get-tuple-element.257.refs_0_), custom_call_target="tpu_custom_call" | custom-call | flops 1258291200 | bytes 5734400 | tf_op jit(solution)/shard_map/partial_products/pallas_call | solution.py:16
  135.4 1.6 next_payload.12
  137.0 8.3 %collective-permute-start.11 = (bf16[96,2560]{1,0:T(8,128)(2,1)}, bf16[96,2560]{1,0:T(8,128)(2,1)}, u32[]{:S(2)}, u32[]{:S(2)}) collective-permute-start(bf16[96,2560]{1,0:T(8,128)(2,1)} %get-tuple-element.259), channel_id=1, source_target_pairs={{0,1},{1,2},{2,3},{4,5},{5,6},{6,7},{8,9},{9,10},{10,11},{12,13},{... | collective-permute-start | bytes 1474568 | tf_op jit(solution)/shard_map/ppermute | solution.py:44
  146.5 4.4 %partial_products.7 = (bf16[4,96,2560]{2,1,0:T(8,128)(2,1)S(1)}, bf16[96,2560]{1,0:T(8,128)(2,1)}, bf16[96,2560]{1,0:T(8,128)(2,1)}) custom-call(bf16[4,96,640]{2,1,0:T(8,128)(2,1)} %all-to-all-done.9.mine_ref.refs_15_, bf16[640,2560]{1,0:T(8,128)(2,1)} %copy-done.26, f32[8,128]{1,0:T(8,128)S(1)} %get-tuple-element.273.refs_0_), custom_call_target="tpu_custom_call" | custom-call | flops 1258291200 | bytes 5734400 | tf_op jit(solution)/shard_map/partial_products/pallas_call | solution.py:16
  150.9 2.5 next_payload.17
  153.4 4.6 %collective-permute-start.34 = (bf16[96,2560]{1,0:T(8,128)(2,1)S(1)}, bf16[96,2560]{1,0:T(8,128)(2,1)S(1)}, u32[]{:S(2)}, u32[]{:S(2)}) collective-permute-start(bf16[96,2560]{1,0:T(8,128)(2,1)S(1)} %get-tuple-element.275), channel_id=1, source_target_pairs={{0,1},{1,2},{2,3},{4,5},{5,6},{6,7},{8,9},{9,10},{10,11},{12,13},{... | collective-permute-start | bytes 1474568 | tf_op jit(solution)/shard_map/ppermute | solution.py:44
  159.3 2.5 next_payload.13
  161.8 4.8 %collective-permute-start.13 = (bf16[96,2560]{1,0:T(8,128)(2,1)S(1)}, bf16[96,2560]{1,0:T(8,128)(2,1)S(1)}, u32[]{:S(2)}, u32[]{:S(2)}) collective-permute-start(bf16[96,2560]{1,0:T(8,128)(2,1)S(1)} %get-tuple-element.261), channel_id=1, source_target_pairs={{0,1},{1,2},{2,3},{4,5},{5,6},{6,7},{8,9},{9,10},{10,11},{12,13},{... | collective-permute-start | bytes 1474568 | tf_op jit(solution)/shard_map/ppermute | solution.py:44
  167.8 1.7 collective-permute-done.34.right_ref.refs_9_
  169.5 4.3 %collective-permute-done.35.left_ref.refs_12_ = bf16[96,2560]{1,0:T(8,128)(2,1)S(1)} collective-permute-done((bf16[96,2560]{1,0:T(8,128)(2,1)S(1)}, bf16[96,2560]{1,0:T(8,128)(2,1)S(1)}, u32[]{:S(2)}, u32[]{:S(2)}) %collective-permute-start.35) | collective-permute-done | bytes 491552 | tf_op jit(solution)/shard_map/ppermute | solution.py:44
  175.2 2.2 collective-permute-start.36
  180.1 4.3 %collective-permute-done.14.left_ref.refs_6_ = bf16[96,2560]{1,0:T(8,128)(2,1)S(1)} collective-permute-done((bf16[96,2560]{1,0:T(8,128)(2,1)S(1)}, bf16[96,2560]{1,0:T(8,128)(2,1)S(1)}, u32[]{:S(2)}, u32[]{:S(2)}) %collective-permute-start.14) | collective-permute-done | bytes 491552 | tf_op jit(solution)/shard_map/ppermute | solution.py:44
  185.7 2.2 collective-permute-start.15
  190.6 4.3 %collective-permute-done.37.left_ref.refs_13_ = bf16[96,2560]{1,0:T(8,128)(2,1)S(1)} collective-permute-done((bf16[96,2560]{1,0:T(8,128)(2,1)S(1)}, bf16[96,2560]{1,0:T(8,128)(2,1)S(1)}, u32[]{:S(2)}, u32[]{:S(2)}) %collective-permute-start.37) | collective-permute-done | bytes 491552 | tf_op jit(solution)/shard_map/ppermute | solution.py:44
  196.3 2.1 collective-permute-start.38
  198.3 1.5 collective-permute-start.39
  199.9 8.4 %weight_step.8 = (f32[640,2560]{1,0:T(8,128)}, f32[8,128]{1,0:T(8,128)S(1)}) custom-call(s32[4]{0:T(128)S(1)} %and_select_fusion.s, bf16[96,2560]{1,0:T(8,128)(2,1)S(1)} %unit_gradient.4.refs_0_, bf16[96,2560]{1,0:T(8,128)(2,1)S(1)} %collective-permute-done.9.right_ref.refs_1_, bf16[96,2560]{1,0:T(8,128)(2,1)} %collective-permute-done.11.right_ref.refs_2_, ...), custom_call_target="tpu_custom_call" | custom-call | flops 2516582400 | bytes 26542080 | tf_op jit(solution)/shard_map/weight_step/pallas_call | solution.py:16
  210.4 6.1 %collective-permute-start.17 = (bf16[96,2560]{1,0:T(8,128)(2,1)S(1)}, bf16[96,2560]{1,0:T(8,128)(2,1)}, u32[]{:S(2)}, u32[]{:S(2)}) collective-permute-start(bf16[96,2560]{1,0:T(8,128)(2,1)S(1)} %unit_gradient.5.refs_0_), channel_id=1, source_target_pairs={{0,1},{1,2},{2,3},{4,5},{5,6},{6,7},{8,9},{9,10},{10,11},{12,13},{... | collective-permute-start | bytes 1474568 | tf_op jit(solution)/shard_map/ppermute | solution.py:44
  218.5 5.3 %collective-permute-start.40 = (bf16[96,2560]{1,0:T(8,128)(2,1)S(1)}, bf16[96,2560]{1,0:T(8,128)(2,1)}, u32[]{:S(2)}, u32[]{:S(2)}) collective-permute-start(bf16[96,2560]{1,0:T(8,128)(2,1)S(1)} %unit_gradient.7.refs_7_), channel_id=1, source_target_pairs={{0,1},{1,2},{2,3},{4,5},{5,6},{6,7},{8,9},{9,10},{10,11},{12,13},{... | collective-permute-start | bytes 1474568 | tf_op jit(solution)/shard_map/ppermute | solution.py:44
  223.8 2.8 collective-permute-done.20.refs_4_
  229.4 7.8 %collective-permute-done.43.refs_11_ = bf16[96,2560]{1,0:T(8,128)(2,1)} collective-permute-done((bf16[96,2560]{1,0:T(8,128)(2,1)S(1)}, bf16[96,2560]{1,0:T(8,128)(2,1)}, u32[]{:S(2)}, u32[]{:S(2)}) %collective-permute-start.43) | collective-permute-done | bytes 491552 | tf_op jit(solution)/shard_map/ppermute | solution.py:44
  239.9 7.8 %collective-permute-done.21.refs_5_ = bf16[96,2560]{1,0:T(8,128)(2,1)} collective-permute-done((bf16[96,2560]{1,0:T(8,128)(2,1)}, bf16[96,2560]{1,0:T(8,128)(2,1)}, u32[]{:S(2)}, u32[]{:S(2)}) %collective-permute-start.21) | collective-permute-done | bytes 491552 | tf_op jit(solution)/shard_map/ppermute | solution.py:44
  250.5 7.8 %collective-permute-done.44.refs_12_ = bf16[96,2560]{1,0:T(8,128)(2,1)} collective-permute-done((bf16[96,2560]{1,0:T(8,128)(2,1)}, bf16[96,2560]{1,0:T(8,128)(2,1)}, u32[]{:S(2)}, u32[]{:S(2)}) %collective-permute-start.44) | collective-permute-done | bytes 491552 | tf_op jit(solution)/shard_map/ppermute | solution.py:44
  259.5 1.5 collective-permute-start.42
  262.4 9.1 %grad_rows.7 = (bf16[4,192,640]{2,1,0:T(8,128)(2,1)}, f32[8,128]{1,0:T(8,128)}) custom-call(s32[4]{0:T(128)S(1)} %and_select_fusion.s, bf16[96,2560]{1,0:T(8,128)(2,1)S(1)} %unit_gradient.4.refs_0_, bf16[96,2560]{1,0:T(8,128)(2,1)S(1)} %collective-permute-done.9.right_ref.refs_1_, bf16[96,2560]{1,0:T(8,128)(2,1)} %collective-permute-done.11.right_ref.refs_2_, ...), custom_call_target="tpu_custom_call" | custom-call | flops 2516582400 | bytes 10158080 | tf_op jit(solution)/shard_map/grad_rows/pallas_call | solution.py:16
  271.5 2.2 collective-permute-done.45.refs_13_
  273.7 9.6 %weight_step.9 = bf16[640,2560]{1,0:T(8,128)(2,1)} custom-call(s32[4]{0:T(128)S(1)} %and_select_fusion.s, bf16[96,2560]{1,0:T(8,128)(2,1)S(1)} %copy-done.28, bf16[96,2560]{1,0:T(8,128)(2,1)} %collective-permute-done.17.refs_1_, bf16[96,2560]{1,0:T(8,128)(2,1)} %collective-permute-done.18.refs_2_, bf16[96,2560]{1,0:T(8,128)(2,1)} %collective-permute-done.19.refs_3_, ...), custom_call_target="tpu_custom_call" | custom-call | flops 2516582400 | bytes 26542080 | tf_op jit(solution)/shard_map/weight_step/pallas_call | solution.py:16
  283.4 69.4 %conditional.1 = (bf16[640,2560]{1,0:T(8,128)(2,1)}, bf16[1,384,2560]{2,1,0:T(8,128)(2,1)S(1)}, f32[1,640,2560]{2,1,0:T(8,128)}) conditional(s32[]{:T(128)} %clamp.3, (bf16[640,2560]{1,0:T(8,128)(2,1)}, bf16[4,192,640]{2,1,0:T(8,128)(2,1)}, s32[4]{0:T(128)S(1)}, bf16[96,2560]{1,0:T(8,128)(2,1)S(1)}, bf16[96,2560]{1,0:T(8,128)(2,1)}, ...), branch_computations={%region_1.2_spmd, %region_2.3_spmd, %region_3.4_spmd} | conditional | flops 5033164800 | bytes 63570104 | solution.py:547
  284.8 4.1 %all-to-all-start.2 = ((bf16[4,192,640]{2,1,0:T(8,128)(2,1)}), bf16[4,192,640]{2,1,0:T(8,128)(2,1)S(1)}, u32[]{:S(2)}, u32[]{:S(2)}) async-start(bf16[4,192,640]{2,1,0:T(8,128)(2,1)} %get-tuple-element.159), calls=%async_computation.2 | async-start | bytes 1966080 | tf_op jit(solution)/shard_map/cond/branch_1_fun/all_to_all | solution.py:413
  288.9 9.3 %grad_rows.5 = (bf16[4,192,640]{2,1,0:T(8,128)(2,1)}, f32[8,128]{1,0:T(8,128)S(1)}) custom-call(s32[4]{0:T(128)S(1)} %get-tuple-element.160.s, bf16[96,2560]{1,0:T(8,128)(2,1)S(1)} %get-tuple-element.161.refs_0_, bf16[96,2560]{1,0:T(8,128)(2,1)} %get-tuple-element.162.refs_1_, bf16[96,2560]{1,0:T(8,128)(2,1)} %get-tuple-element.163.refs_2_, ...), custom_call_target="tpu_custom_call" | custom-call | flops 2516582400 | bytes 10158080 | tf_op jit(solution)/shard_map/cond/branch_1_fun/grad_rows/pallas_call | solution.py:16
  298.2 10.2 %all-to-all-done.2.refs_0_ = bf16[4,192,640]{2,1,0:T(8,128)(2,1)S(1)} async-done(((bf16[4,192,640]{2,1,0:T(8,128)(2,1)}), bf16[4,192,640]{2,1,0:T(8,128)(2,1)S(1)}, u32[]{:S(2)}, u32[]{:S(2)}) %all-to-all-start.2) | async-done | bytes 983072 | tf_op jit(solution)/shard_map/cond/branch_1_fun/all_to_all | solution.py:413
  308.4 3.5 all-to-all-start.3
  311.9 12.6 %weight_step.6 = f32[640,2560]{1,0:T(8,128)} custom-call(s32[4]{0:T(128)S(1)} %get-tuple-element.160.s, bf16[96,2560]{1,0:T(8,128)(2,1)} %copy-done.30, bf16[96,2560]{1,0:T(8,128)(2,1)} %get-tuple-element.162.refs_1_, bf16[96,2560]{1,0:T(8,128)(2,1)} %get-tuple-element.163.refs_2_, bf16[96,2560]{1,0:T(8,128)(2,1)} %get-tuple-element.164.refs_3_, ...), custom_call_target="tpu_custom_call" | custom-call | flops 2516582400 | bytes 26542080 | tf_op jit(solution)/shard_map/cond/branch_1_fun/weight_step/pallas_call | solution.py:16
  324.6 8.6 %all-to-all-done.3.refs_1_ = bf16[4,192,640]{2,1,0:T(8,128)(2,1)S(1)} async-done(((bf16[4,192,640]{2,1,0:T(8,128)(2,1)}), bf16[4,192,640]{2,1,0:T(8,128)(2,1)S(1)}, u32[]{:S(2)}, u32[]{:S(2)}) %all-to-all-start.3) | async-done | bytes 983072 | tf_op jit(solution)/shard_map/cond/branch_1_fun/all_to_all | solution.py:413
  333.4 19.4 %collective-permute-done.1 = bf16[640,2560]{1,0:T(8,128)(2,1)} collective-permute-done((bf16[640,2560]{1,0:T(8,128)(2,1)}, bf16[640,2560]{1,0:T(8,128)(2,1)}, u32[]{:S(2)}, u32[]{:S(2)}) %collective-permute-start.1) | collective-permute-done | bytes 3276832 | tf_op jit(solution)/shard_map/cond/branch_1_fun/ppermute | solution.py:418
  352.8 5.1 %widened.1 = f32[640,2560]{1,0:T(8,128)} custom-call(bf16[640,2560]{1,0:T(8,128)(2,1)} %get-tuple-element.285.value_ref), custom_call_target="tpu_custom_call" | custom-call | bytes 9830400 | tf_op jit(solution)/shard_map/widened/pallas_call | solution.py:16
  (148 shorter events, 48.1 us)
Async XLA Ops:
  3.0 20.1 %all-to-all-start.6 = ((bf16[4,96,640]{2,1,0:T(8,128)(2,1)}), bf16[4,96,640]{2,1,0:T(8,128)(2,1)S(1)}, u32[]{:S(2)}, u32[]{:S(2)}) async-start(bf16[4,96,640]{2,1,0:T(8,128)(2,1)} %cut_heads.4), calls=%async_computation.6 | async-start | bytes 983040 | tf_op jit(solution)/shard_map/all_to_all | solution.py:413
  13.6 19.6 %copy-start.37 = (s32[8]{0:T(128)S(1)}, s32[8]{0:T(128)}, u32[]{:S(2)}) copy-start(s32[8]{0:T(128)} %param.20) | copy-start | bytes 100
  23.1 27.9 %copy-start.22 = (bf16[4,96,640]{2,1,0:T(8,128)(2,1)}, bf16[4,96,640]{2,1,0:T(8,128)(2,1)S(1)}, u32[]{:S(2)}) copy-start(bf16[4,96,640]{2,1,0:T(8,128)(2,1)S(1)} %all-to-all-done.6.mine_ref.refs_14_) | copy-start | bytes 1474564
  23.1 23.4 %all-to-all-start.8 = ((bf16[4,96,640]{2,1,0:T(8,128)(2,1)}), bf16[4,96,640]{2,1,0:T(8,128)(2,1)S(1)}, u32[]{:S(2)}, u32[]{:S(2)}) async-start(bf16[4,96,640]{2,1,0:T(8,128)(2,1)} %cut_heads.6), calls=%async_computation.8 | async-start | bytes 983040 | tf_op jit(solution)/shard_map/all_to_all | solution.py:413
  26.6 18.1 %collective-permute-start.25 = (f32[1]{0:T(128)}, f32[1]{0:T(128)}, u32[]{:S(2)}, u32[]{:S(2)}) collective-permute-start(f32[1]{0:T(128)} %mul.12), channel_id=1, source_target_pairs={{0,4},{4,8},{8,12},{12,16},{16,20},{20,24},{24,28},{28,0},{1,5},{5... | collective-permute-start | bytes 20 | tf_op jit(solution)/shard_map/ppermute | solution.py:447
  27.6 17.1 %collective-permute-start.24 = (f32[1]{0:T(128)}, f32[1]{0:T(128)}, u32[]{:S(2)}, u32[]{:S(2)}) collective-permute-start(f32[1]{0:T(128)} %mul.12), channel_id=1, source_target_pairs={{0,8},{4,12},{8,16},{12,20},{16,24},{20,28},{24,0},{28,4},{1,9},{5... | collective-permute-start | bytes 20 | tf_op jit(solution)/shard_map/ppermute | solution.py:447
  30.4 15.5 %collective-permute-start.23 = (f32[1]{0:T(128)}, f32[1]{0:T(128)}, u32[]{:S(2)}, u32[]{:S(2)}) collective-permute-start(f32[1]{0:T(128)} %mul.12), channel_id=1, source_target_pairs={{0,16},{4,20},{8,24},{12,28},{16,0},{20,4},{24,8},{28,12},{1,17},{... | collective-permute-start | bytes 20 | tf_op jit(solution)/shard_map/ppermute | solution.py:447
  38.7 16.4 %collective-permute-start.3 = (bf16[96,2560]{1,0:T(8,128)(2,1)}, bf16[96,2560]{1,0:T(8,128)(2,1)S(1)}, u32[]{:S(2)}, u32[]{:S(2)}) collective-permute-start(bf16[96,2560]{1,0:T(8,128)(2,1)} %get-tuple-element.249), channel_id=1, source_target_pairs={{0,1},{4,5},{8,9},{12,13},{16,17},{20,21},{24,25},{28,29}} | collective-permute-start | bytes 1474568 | tf_op jit(solution)/shard_map/ppermute | solution.py:44
  42.6 12.6 %collective-permute-start.4 = (bf16[96,2560]{1,0:T(8,128)(2,1)}, bf16[96,2560]{1,0:T(8,128)(2,1)}, u32[]{:S(2)}, u32[]{:S(2)}) collective-permute-start(bf16[96,2560]{1,0:T(8,128)(2,1)} %get-tuple-element.250), channel_id=1, source_target_pairs={{3,2},{7,6},{11,10},{15,14},{19,18},{23,22},{27,26},{31,30}} | collective-permute-start | bytes 1474568 | tf_op jit(solution)/shard_map/ppermute | solution.py:44
  52.3 14.4 %collective-permute-start.26 = (bf16[96,2560]{1,0:T(8,128)(2,1)}, bf16[96,2560]{1,0:T(8,128)(2,1)S(1)}, u32[]{:S(2)}, u32[]{:S(2)}) collective-permute-start(bf16[96,2560]{1,0:T(8,128)(2,1)} %get-tuple-element.265), channel_id=1, source_target_pairs={{0,1},{4,5},{8,9},{12,13},{16,17},{20,21},{24,25},{28,29}} | collective-permute-start | bytes 1474568 | tf_op jit(solution)/shard_map/ppermute | solution.py:44
  53.6 13.1 %collective-permute-start.27 = (bf16[96,2560]{1,0:T(8,128)(2,1)}, bf16[96,2560]{1,0:T(8,128)(2,1)}, u32[]{:S(2)}, u32[]{:S(2)}) collective-permute-start(bf16[96,2560]{1,0:T(8,128)(2,1)} %get-tuple-element.266), channel_id=1, source_target_pairs={{3,2},{7,6},{11,10},{15,14},{19,18},{23,22},{27,26},{31,30}} | collective-permute-start | bytes 1474568 | tf_op jit(solution)/shard_map/ppermute | solution.py:44
  57.7 18.7 %collective-permute-start.5 = (bf16[96,2560]{1,0:T(8,128)(2,1)}, bf16[96,2560]{1,0:T(8,128)(2,1)S(1)}, u32[]{:S(2)}, u32[]{:S(2)}) collective-permute-start(bf16[96,2560]{1,0:T(8,128)(2,1)} %get-tuple-element.252), channel_id=1, source_target_pairs={{0,1},{1,2},{4,5},{5,6},{8,9},{9,10},{12,13},{13,14},{16,17},{17,1... | collective-permute-start | bytes 1474568 | tf_op jit(solution)/shard_map/ppermute | solution.py:44
  59.0 17.3 %collective-permute-start.6 = (bf16[96,2560]{1,0:T(8,128)(2,1)}, bf16[96,2560]{1,0:T(8,128)(2,1)S(1)}, u32[]{:S(2)}, u32[]{:S(2)}) collective-permute-start(bf16[96,2560]{1,0:T(8,128)(2,1)} %get-tuple-element.253), channel_id=1, source_target_pairs={{2,1},{3,2},{6,5},{7,6},{10,9},{11,10},{14,13},{15,14},{18,17},{19... | collective-permute-start | bytes 1474568 | tf_op jit(solution)/shard_map/ppermute | solution.py:44
  60.5 44.6 %all-to-all-start.7 = ((bf16[4,96,640]{2,1,0:T(8,128)(2,1)}), bf16[4,96,640]{2,1,0:T(8,128)(2,1)}, u32[]{:S(2)}, u32[]{:S(2)}) async-start(bf16[4,96,640]{2,1,0:T(8,128)(2,1)} %cut_heads.5), calls=%async_computation.7 | async-start | bytes 983040 | tf_op jit(solution)/shard_map/all_to_all | solution.py:413
  70.8 23.7 %collective-permute-start.28 = (bf16[96,2560]{1,0:T(8,128)(2,1)}, bf16[96,2560]{1,0:T(8,128)(2,1)S(1)}, u32[]{:S(2)}, u32[]{:S(2)}) collective-permute-start(bf16[96,2560]{1,0:T(8,128)(2,1)} %get-tuple-element.268), channel_id=1, source_target_pairs={{0,1},{1,2},{4,5},{5,6},{8,9},{9,10},{12,13},{13,14},{16,17},{17,1... | collective-permute-start | bytes 1474568 | tf_op jit(solution)/shard_map/ppermute | solution.py:44
  74.8 19.7 %collective-permute-start.29 = (bf16[96,2560]{1,0:T(8,128)(2,1)}, bf16[96,2560]{1,0:T(8,128)(2,1)}, u32[]{:S(2)}, u32[]{:S(2)}) collective-permute-start(bf16[96,2560]{1,0:T(8,128)(2,1)} %get-tuple-element.269), channel_id=1, source_target_pairs={{2,1},{3,2},{6,5},{7,6},{10,9},{11,10},{14,13},{15,14},{18,17},{19... | collective-permute-start | bytes 1474568 | tf_op jit(solution)/shard_map/ppermute | solution.py:44
  76.2 18.3 %copy-start.2 = (bf16[4,96,2560]{2,1,0:T(8,128)(2,1)S(1)}, bf16[4,96,2560]{2,1,0:T(8,128)(2,1)}, u32[]{:S(2)}) copy-start(bf16[4,96,2560]{2,1,0:T(8,128)(2,1)} %copy-done) | copy-start | bytes 5898244
  77.9 26.3 %copy-start.13 = (bf16[1,384,2560]{2,1,0:T(8,128)(2,1)S(1)}, bf16[1,384,2560]{2,1,0:T(8,128)(2,1)}, u32[]{:S(2)}) copy-start(bf16[1,384,2560]{2,1,0:T(8,128)(2,1)} %param.16) | copy-start | bytes 5898244
  77.9 31.6 %collective-permute-start.7 = (bf16[96,2560]{1,0:T(8,128)(2,1)}, bf16[96,2560]{1,0:T(8,128)(2,1)S(1)}, u32[]{:S(2)}, u32[]{:S(2)}) collective-permute-start(bf16[96,2560]{1,0:T(8,128)(2,1)} %get-tuple-element.254), channel_id=1, source_target_pairs={{0,1},{1,2},{2,3},{4,5},{5,6},{6,7},{8,9},{9,10},{10,11},{12,13},{... | collective-permute-start | bytes 1474568 | tf_op jit(solution)/shard_map/ppermute | solution.py:44
  82.1 27.4 %copy-start.36 = (f32[2560]{0:T(1024)S(1)}, f32[2560]{0:T(1024)}, u32[]{:S(2)}) copy-start(f32[2560]{0:T(1024)} %param.19) | copy-start | bytes 30724
  82.1 27.4 %collective-permute-start.8 = (bf16[96,2560]{1,0:T(8,128)(2,1)}, bf16[96,2560]{1,0:T(8,128)(2,1)S(1)}, u32[]{:S(2)}, u32[]{:S(2)}) collective-permute-start(bf16[96,2560]{1,0:T(8,128)(2,1)} %get-tuple-element.255), channel_id=1, source_target_pairs={{1,0},{2,1},{3,2},{5,4},{6,5},{7,6},{9,8},{10,9},{11,10},{13,12},{... | collective-permute-start | bytes 1474568 | tf_op jit(solution)/shard_map/ppermute | solution.py:44
  97.0 22.7 %collective-permute-start.30 = (bf16[96,2560]{1,0:T(8,128)(2,1)}, bf16[96,2560]{1,0:T(8,128)(2,1)}, u32[]{:S(2)}, u32[]{:S(2)}) collective-permute-start(bf16[96,2560]{1,0:T(8,128)(2,1)} %get-tuple-element.270), channel_id=1, source_target_pairs={{0,1},{1,2},{2,3},{4,5},{5,6},{6,7},{8,9},{9,10},{10,11},{12,13},{... | collective-permute-start | bytes 1474568 | tf_op jit(solution)/shard_map/ppermute | solution.py:44
  102.9 16.9 %collective-permute-start.31 = (bf16[96,2560]{1,0:T(8,128)(2,1)}, bf16[96,2560]{1,0:T(8,128)(2,1)}, u32[]{:S(2)}, u32[]{:S(2)}) collective-permute-start(bf16[96,2560]{1,0:T(8,128)(2,1)} %get-tuple-element.271), channel_id=1, source_target_pairs={{1,0},{2,1},{3,2},{5,4},{6,5},{7,6},{9,8},{10,9},{11,10},{13,12},{... | collective-permute-start | bytes 1474568 | tf_op jit(solution)/shard_map/ppermute | solution.py:44
  105.1 41.5 %all-to-all-start.9 = ((bf16[4,96,640]{2,1,0:T(8,128)(2,1)}), bf16[4,96,640]{2,1,0:T(8,128)(2,1)}, u32[]{:S(2)}, u32[]{:S(2)}) async-start(bf16[4,96,640]{2,1,0:T(8,128)(2,1)} %cut_heads.7), calls=%async_computation.9 | async-start | bytes 983040 | tf_op jit(solution)/shard_map/all_to_all | solution.py:413
  113.3 22.1 %collective-permute-start.10 = (bf16[96,2560]{1,0:T(8,128)(2,1)S(1)}, bf16[96,2560]{1,0:T(8,128)(2,1)S(1)}, u32[]{:S(2)}, u32[]{:S(2)}) collective-permute-start(bf16[96,2560]{1,0:T(8,128)(2,1)S(1)} %unit_gradient.4.refs_0_), channel_id=1, source_target_pairs={{1,0},{2,1},{3,2},{5,4},{6,5},{7,6},{9,8},{10,9},{11,10},{13,12},{... | collective-permute-start | bytes 1474568 | tf_op jit(solution)/shard_map/ppermute | solution.py:44
  114.8 20.6 %collective-permute-start.9 = (bf16[96,2560]{1,0:T(8,128)(2,1)S(1)}, bf16[96,2560]{1,0:T(8,128)(2,1)S(1)}, u32[]{:S(2)}, u32[]{:S(2)}) collective-permute-start(bf16[96,2560]{1,0:T(8,128)(2,1)S(1)} %unit_gradient.4.refs_0_), channel_id=1, source_target_pairs={{0,1},{1,2},{2,3},{4,5},{5,6},{6,7},{8,9},{9,10},{10,11},{12,13},{... | collective-permute-start | bytes 1474568 | tf_op jit(solution)/shard_map/ppermute | solution.py:44
  122.3 28.7 %collective-permute-start.33 = (bf16[96,2560]{1,0:T(8,128)(2,1)}, bf16[96,2560]{1,0:T(8,128)(2,1)}, u32[]{:S(2)}, u32[]{:S(2)}) collective-permute-start(bf16[96,2560]{1,0:T(8,128)(2,1)} %unit_gradient.6.refs_7_), channel_id=1, source_target_pairs={{1,0},{2,1},{3,2},{5,4},{6,5},{7,6},{9,8},{10,9},{11,10},{13,12},{... | collective-permute-start | bytes 1474568 | tf_op jit(solution)/shard_map/ppermute | solution.py:44
  123.5 27.4 %collective-permute-start.32 = (bf16[96,2560]{1,0:T(8,128)(2,1)}, bf16[96,2560]{1,0:T(8,128)(2,1)}, u32[]{:S(2)}, u32[]{:S(2)}) collective-permute-start(bf16[96,2560]{1,0:T(8,128)(2,1)} %unit_gradient.6.refs_7_), channel_id=1, source_target_pairs={{0,1},{1,2},{2,3},{4,5},{5,6},{6,7},{8,9},{9,10},{10,11},{12,13},{... | collective-permute-start | bytes 1474568 | tf_op jit(solution)/shard_map/ppermute | solution.py:44
  137.0 22.3 %collective-permute-start.11 = (bf16[96,2560]{1,0:T(8,128)(2,1)}, bf16[96,2560]{1,0:T(8,128)(2,1)}, u32[]{:S(2)}, u32[]{:S(2)}) collective-permute-start(bf16[96,2560]{1,0:T(8,128)(2,1)} %get-tuple-element.259), channel_id=1, source_target_pairs={{0,1},{1,2},{2,3},{4,5},{5,6},{6,7},{8,9},{9,10},{10,11},{12,13},{... | collective-permute-start | bytes 1474568 | tf_op jit(solution)/shard_map/ppermute | solution.py:44
  145.2 14.0 %collective-permute-start.12 = (bf16[96,2560]{1,0:T(8,128)(2,1)}, bf16[96,2560]{1,0:T(8,128)(2,1)}, u32[]{:S(2)}, u32[]{:S(2)}) collective-permute-start(bf16[96,2560]{1,0:T(8,128)(2,1)} %get-tuple-element.260), channel_id=1, source_target_pairs={{1,0},{2,1},{3,2},{5,4},{6,5},{7,6},{9,8},{10,9},{11,10},{13,12},{... | collective-permute-start | bytes 1474568 | tf_op jit(solution)/shard_map/ppermute | solution.py:44
  153.4 16.1 %collective-permute-start.34 = (bf16[96,2560]{1,0:T(8,128)(2,1)S(1)}, bf16[96,2560]{1,0:T(8,128)(2,1)S(1)}, u32[]{:S(2)}, u32[]{:S(2)}) collective-permute-start(bf16[96,2560]{1,0:T(8,128)(2,1)S(1)} %get-tuple-element.275), channel_id=1, source_target_pairs={{0,1},{1,2},{2,3},{4,5},{5,6},{6,7},{8,9},{9,10},{10,11},{12,13},{... | collective-permute-start | bytes 1474568 | tf_op jit(solution)/shard_map/ppermute | solution.py:44
  158.0 15.9 %collective-permute-start.35 = (bf16[96,2560]{1,0:T(8,128)(2,1)S(1)}, bf16[96,2560]{1,0:T(8,128)(2,1)S(1)}, u32[]{:S(2)}, u32[]{:S(2)}) collective-permute-start(bf16[96,2560]{1,0:T(8,128)(2,1)S(1)} %get-tuple-element.276), channel_id=1, source_target_pairs={{1,0},{2,1},{3,2},{5,4},{6,5},{7,6},{9,8},{10,9},{11,10},{13,12},{... | collective-permute-start | bytes 1474568 | tf_op jit(solution)/shard_map/ppermute | solution.py:44
  161.8 18.3 %collective-permute-start.13 = (bf16[96,2560]{1,0:T(8,128)(2,1)S(1)}, bf16[96,2560]{1,0:T(8,128)(2,1)S(1)}, u32[]{:S(2)}, u32[]{:S(2)}) collective-permute-start(bf16[96,2560]{1,0:T(8,128)(2,1)S(1)} %get-tuple-element.261), channel_id=1, source_target_pairs={{0,1},{1,2},{2,3},{4,5},{5,6},{6,7},{8,9},{9,10},{10,11},{12,13},{... | collective-permute-start | bytes 1474568 | tf_op jit(solution)/shard_map/ppermute | solution.py:44
  166.5 17.9 %collective-permute-start.14 = (bf16[96,2560]{1,0:T(8,128)(2,1)S(1)}, bf16[96,2560]{1,0:T(8,128)(2,1)S(1)}, u32[]{:S(2)}, u32[]{:S(2)}) collective-permute-start(bf16[96,2560]{1,0:T(8,128)(2,1)S(1)} %get-tuple-element.262), channel_id=1, source_target_pairs={{1,0},{2,1},{3,2},{5,4},{6,5},{7,6},{9,8},{10,9},{11,10},{13,12},{... | collective-permute-start | bytes 1474568 | tf_op jit(solution)/shard_map/ppermute | solution.py:44
  169.5 30.3 %copy-start.14 = (bf16[96,2560]{1,0:T(8,128)(2,1)}, bf16[96,2560]{1,0:T(8,128)(2,1)S(1)}, u32[]{:S(2)}) copy-start(bf16[96,2560]{1,0:T(8,128)(2,1)S(1)} %collective-permute-done.34.right_ref.refs_9_) | copy-start | bytes 1474564
  173.9 26.0 %copy-start.15 = (bf16[96,2560]{1,0:T(8,128)(2,1)}, bf16[96,2560]{1,0:T(8,128)(2,1)S(1)}, u32[]{:S(2)}) copy-start(bf16[96,2560]{1,0:T(8,128)(2,1)S(1)} %collective-permute-done.35.left_ref.refs_12_) | copy-start | bytes 1474564
  173.9 26.0 %slice-start = ((s8[6553600]{0:T(1024)(128)(4,1)}), s8[4194304]{0:T(1024)(128)(4,1)S(1)}, s32[]{:S(2)}) async-start(s8[6553600]{0:T(1024)(128)(4,1)} %bitcast.45), calls=%async_computation.10 | async-start | bytes 8388608
  175.2 15.4 %collective-permute-start.36 = (bf16[96,2560]{1,0:T(8,128)(2,1)S(1)}, bf16[96,2560]{1,0:T(8,128)(2,1)S(1)}, u32[]{:S(2)}, u32[]{:S(2)}) collective-permute-start(bf16[96,2560]{1,0:T(8,128)(2,1)S(1)} %get-tuple-element.277), channel_id=1, source_target_pairs={{0,1},{1,2},{2,3},{4,5},{5,6},{6,7},{8,9},{9,10},{10,11},{12,13},{... | collective-permute-start | bytes 1474568 | tf_op jit(solution)/shard_map/ppermute | solution.py:44
  177.4 22.5 %slice-start.1 = ((s8[6553600]{0:T(1024)(128)(4,1)}), s8[2359296]{0:T(1024)(128)(4,1)S(1)}, s32[]{:S(2)}) async-start(s8[6553600]{0:T(1024)(128)(4,1)} %bitcast.45), calls=%async_computation.11 | async-start | bytes 4718592
  177.4 17.5 %collective-permute-start.37 = (bf16[96,2560]{1,0:T(8,128)(2,1)S(1)}, bf16[96,2560]{1,0:T(8,128)(2,1)S(1)}, u32[]{:S(2)}, u32[]{:S(2)}) collective-permute-start(bf16[96,2560]{1,0:T(8,128)(2,1)S(1)} %get-tuple-element.278), channel_id=1, source_target_pairs={{1,0},{2,1},{3,2},{5,4},{6,5},{7,6},{9,8},{10,9},{11,10},{13,12},{... | collective-permute-start | bytes 1474568 | tf_op jit(solution)/shard_map/ppermute | solution.py:44
  180.1 19.8 %copy-start.16 = (bf16[96,2560]{1,0:T(8,128)(2,1)}, bf16[96,2560]{1,0:T(8,128)(2,1)S(1)}, u32[]{:S(2)}) copy-start(bf16[96,2560]{1,0:T(8,128)(2,1)S(1)} %collective-permute-done.13.right_ref.refs_3_) | copy-start | bytes 1474564
  185.7 22.7 %collective-permute-start.15 = (bf16[96,2560]{1,0:T(8,128)(2,1)S(1)}, bf16[96,2560]{1,0:T(8,128)(2,1)S(1)}, u32[]{:S(2)}, u32[]{:S(2)}) collective-permute-start(bf16[96,2560]{1,0:T(8,128)(2,1)S(1)} %get-tuple-element.263), channel_id=1, source_target_pairs={{0,1},{1,2},{2,3},{4,5},{5,6},{6,7},{8,9},{9,10},{10,11},{12,13},{... | collective-permute-start | bytes 1474568 | tf_op jit(solution)/shard_map/ppermute | solution.py:44
  187.9 20.5 %collective-permute-start.16 = (bf16[96,2560]{1,0:T(8,128)(2,1)S(1)}, bf16[96,2560]{1,0:T(8,128)(2,1)S(1)}, u32[]{:S(2)}, u32[]{:S(2)}) collective-permute-start(bf16[96,2560]{1,0:T(8,128)(2,1)S(1)} %get-tuple-element.264), channel_id=1, source_target_pairs={{1,0},{2,1},{3,2},{5,4},{6,5},{7,6},{9,8},{10,9},{11,10},{13,12},{... | collective-permute-start | bytes 1474568 | tf_op jit(solution)/shard_map/ppermute | solution.py:44
  190.6 17.8 %copy-start.20 = (bf16[96,2560]{1,0:T(8,128)(2,1)}, bf16[96,2560]{1,0:T(8,128)(2,1)S(1)}, u32[]{:S(2)}) copy-start(bf16[96,2560]{1,0:T(8,128)(2,1)S(1)} %collective-permute-done.36.right_ref.refs_10_) | copy-start | bytes 1474564
  196.3 20.2 %collective-permute-start.38 = (bf16[96,2560]{1,0:T(8,128)(2,1)S(1)}, bf16[96,2560]{1,0:T(8,128)(2,1)S(1)}, u32[]{:S(2)}, u32[]{:S(2)}) collective-permute-start(bf16[96,2560]{1,0:T(8,128)(2,1)S(1)} %get-tuple-element.279), channel_id=1, source_target_pairs={{0,1},{1,2},{2,3},{4,5},{5,6},{6,7},{8,9},{9,10},{10,11},{12,13},{... | collective-permute-start | bytes 1474568 | tf_op jit(solution)/shard_map/ppermute | solution.py:44
  198.3 18.2 %collective-permute-start.39 = (bf16[96,2560]{1,0:T(8,128)(2,1)S(1)}, bf16[96,2560]{1,0:T(8,128)(2,1)S(1)}, u32[]{:S(2)}, u32[]{:S(2)}) collective-permute-start(bf16[96,2560]{1,0:T(8,128)(2,1)S(1)} %get-tuple-element.280), channel_id=1, source_target_pairs={{1,0},{2,1},{3,2},{5,4},{6,5},{7,6},{9,8},{10,9},{11,10},{13,12},{... | collective-permute-start | bytes 1474568 | tf_op jit(solution)/shard_map/ppermute | solution.py:44
  209.1 17.5 %collective-permute-start.20 = (bf16[96,2560]{1,0:T(8,128)(2,1)S(1)}, bf16[96,2560]{1,0:T(8,128)(2,1)}, u32[]{:S(2)}, u32[]{:S(2)}) collective-permute-start(bf16[96,2560]{1,0:T(8,128)(2,1)S(1)} %unit_gradient.5.refs_0_), channel_id=1, source_target_pairs={{1,0},{2,1},{3,2},{5,4},{6,5},{7,6},{9,8},{10,9},{11,10},{13,12},{... | collective-permute-start | bytes 1474568 | tf_op jit(solution)/shard_map/ppermute | solution.py:44
  210.4 17.5 %collective-permute-start.17 = (bf16[96,2560]{1,0:T(8,128)(2,1)S(1)}, bf16[96,2560]{1,0:T(8,128)(2,1)}, u32[]{:S(2)}, u32[]{:S(2)}) collective-permute-start(bf16[96,2560]{1,0:T(8,128)(2,1)S(1)} %unit_gradient.5.refs_0_), channel_id=1, source_target_pairs={{0,1},{1,2},{2,3},{4,5},{5,6},{6,7},{8,9},{9,10},{10,11},{12,13},{... | collective-permute-start | bytes 1474568 | tf_op jit(solution)/shard_map/ppermute | solution.py:44
  216.5 45.8 %copy-start.17 = (bf16[96,2560]{1,0:T(8,128)(2,1)S(1)}, bf16[96,2560]{1,0:T(8,128)(2,1)}, u32[]{:S(2)}) copy-start(bf16[96,2560]{1,0:T(8,128)(2,1)} %copy-done.16) | copy-start | bytes 1474564
  216.5 45.8 %copy-start.19 = (bf16[96,2560]{1,0:T(8,128)(2,1)S(1)}, bf16[96,2560]{1,0:T(8,128)(2,1)}, u32[]{:S(2)}) copy-start(bf16[96,2560]{1,0:T(8,128)(2,1)} %copy-done.18) | copy-start | bytes 1474564
  217.2 20.0 %collective-permute-start.43 = (bf16[96,2560]{1,0:T(8,128)(2,1)S(1)}, bf16[96,2560]{1,0:T(8,128)(2,1)}, u32[]{:S(2)}, u32[]{:S(2)}) collective-permute-start(bf16[96,2560]{1,0:T(8,128)(2,1)S(1)} %unit_gradient.7.refs_7_), channel_id=1, source_target_pairs={{1,0},{2,1},{3,2},{5,4},{6,5},{7,6},{9,8},{10,9},{11,10},{13,12},{... | collective-permute-start | bytes 1474568 | tf_op jit(solution)/shard_map/ppermute | solution.py:44
  218.5 20.0 %collective-permute-start.40 = (bf16[96,2560]{1,0:T(8,128)(2,1)S(1)}, bf16[96,2560]{1,0:T(8,128)(2,1)}, u32[]{:S(2)}, u32[]{:S(2)}) collective-permute-start(bf16[96,2560]{1,0:T(8,128)(2,1)S(1)} %unit_gradient.7.refs_7_), channel_id=1, source_target_pairs={{0,1},{1,2},{2,3},{4,5},{5,6},{6,7},{8,9},{9,10},{10,11},{12,13},{... | collective-permute-start | bytes 1474568 | tf_op jit(solution)/shard_map/ppermute | solution.py:44
  226.7 21.1 %collective-permute-start.21 = (bf16[96,2560]{1,0:T(8,128)(2,1)}, bf16[96,2560]{1,0:T(8,128)(2,1)}, u32[]{:S(2)}, u32[]{:S(2)}) collective-permute-start(bf16[96,2560]{1,0:T(8,128)(2,1)} %collective-permute-done.20.refs_4_), channel_id=1, source_target_pairs={{1,0},{2,1},{5,4},{6,5},{9,8},{10,9},{13,12},{14,13},{17,16},{18,1... | collective-permute-start | bytes 1474568 | tf_op jit(solution)/shard_map/ppermute | solution.py:44
  227.9 21.1 %collective-permute-start.18 = (bf16[96,2560]{1,0:T(8,128)(2,1)}, bf16[96,2560]{1,0:T(8,128)(2,1)}, u32[]{:S(2)}, u32[]{:S(2)}) collective-permute-start(bf16[96,2560]{1,0:T(8,128)(2,1)} %collective-permute-done.17.refs_1_), channel_id=1, source_target_pairs={{1,2},{2,3},{5,6},{6,7},{9,10},{10,11},{13,14},{14,15},{17,18},{18... | collective-permute-start | bytes 1474568 | tf_op jit(solution)/shard_map/ppermute | solution.py:44
  237.2 21.1 %collective-permute-start.44 = (bf16[96,2560]{1,0:T(8,128)(2,1)}, bf16[96,2560]{1,0:T(8,128)(2,1)}, u32[]{:S(2)}, u32[]{:S(2)}) collective-permute-start(bf16[96,2560]{1,0:T(8,128)(2,1)} %collective-permute-done.43.refs_11_), channel_id=1, source_target_pairs={{1,0},{2,1},{5,4},{6,5},{9,8},{10,9},{13,12},{14,13},{17,16},{18,1... | collective-permute-start | bytes 1474568 | tf_op jit(solution)/shard_map/ppermute | solution.py:44
  238.5 21.1 %collective-permute-start.41 = (bf16[96,2560]{1,0:T(8,128)(2,1)}, bf16[96,2560]{1,0:T(8,128)(2,1)}, u32[]{:S(2)}, u32[]{:S(2)}) collective-permute-start(bf16[96,2560]{1,0:T(8,128)(2,1)} %collective-permute-done.40.refs_8_), channel_id=1, source_target_pairs={{1,2},{2,3},{5,6},{6,7},{9,10},{10,11},{13,14},{14,15},{17,18},{18... | collective-permute-start | bytes 1474568 | tf_op jit(solution)/shard_map/ppermute | solution.py:44
  247.7 23.8 %collective-permute-start.22 = (bf16[96,2560]{1,0:T(8,128)(2,1)}, bf16[96,2560]{1,0:T(8,128)(2,1)}, u32[]{:S(2)}, u32[]{:S(2)}) collective-permute-start(bf16[96,2560]{1,0:T(8,128)(2,1)} %collective-permute-done.21.refs_5_), channel_id=1, source_target_pairs={{1,0},{5,4},{9,8},{13,12},{17,16},{21,20},{25,24},{29,28}} | collective-permute-start | bytes 1474568 | tf_op jit(solution)/shard_map/ppermute | solution.py:44
  249.0 22.5 %collective-permute-start.19 = (bf16[96,2560]{1,0:T(8,128)(2,1)}, bf16[96,2560]{1,0:T(8,128)(2,1)}, u32[]{:S(2)}, u32[]{:S(2)}) collective-permute-start(bf16[96,2560]{1,0:T(8,128)(2,1)} %collective-permute-done.18.refs_2_), channel_id=1, source_target_pairs={{2,3},{6,7},{10,11},{14,15},{18,19},{22,23},{26,27},{30,31}} | collective-permute-start | bytes 1474568 | tf_op jit(solution)/shard_map/ppermute | solution.py:44
  258.2 15.5 %collective-permute-start.45 = (bf16[96,2560]{1,0:T(8,128)(2,1)}, bf16[96,2560]{1,0:T(8,128)(2,1)}, u32[]{:S(2)}, u32[]{:S(2)}) collective-permute-start(bf16[96,2560]{1,0:T(8,128)(2,1)} %collective-permute-done.44.refs_12_), channel_id=1, source_target_pairs={{1,0},{5,4},{9,8},{13,12},{17,16},{21,20},{25,24},{29,28}} | collective-permute-start | bytes 1474568 | tf_op jit(solution)/shard_map/ppermute | solution.py:44
  259.5 14.2 %collective-permute-start.42 = (bf16[96,2560]{1,0:T(8,128)(2,1)}, bf16[96,2560]{1,0:T(8,128)(2,1)}, u32[]{:S(2)}, u32[]{:S(2)}) collective-permute-start(bf16[96,2560]{1,0:T(8,128)(2,1)} %collective-permute-done.41.refs_9_), channel_id=1, source_target_pairs={{2,3},{6,7},{10,11},{14,15},{18,19},{22,23},{26,27},{30,31}} | collective-permute-start | bytes 1474568 | tf_op jit(solution)/shard_map/ppermute | solution.py:44
  283.4 25.0 %copy-start.30 = (bf16[96,2560]{1,0:T(8,128)(2,1)}, bf16[96,2560]{1,0:T(8,128)(2,1)S(1)}, u32[]{:S(2)}) copy-start(bf16[96,2560]{1,0:T(8,128)(2,1)S(1)} %get-tuple-element.161.refs_0_) | copy-start | bytes 1474564 | tf_op jit(solution)/shard_map/cond
  283.4 69.3 %collective-permute-start.1 = (bf16[640,2560]{1,0:T(8,128)(2,1)}, bf16[640,2560]{1,0:T(8,128)(2,1)}, u32[]{:S(2)}, u32[]{:S(2)}) collective-permute-start(bf16[640,2560]{1,0:T(8,128)(2,1)} %get-tuple-element.158), channel_id=1, source_target_pairs={{0,8},{4,12},{8,16},{12,20},{16,24},{20,28},{24,0},{28,4},{1,9},{5... | collective-permute-start | bytes 9830408 | tf_op jit(solution)/shard_map/cond/branch_1_fun/ppermute | solution.py:418
  284.8 23.6 %all-to-all-start.2 = ((bf16[4,192,640]{2,1,0:T(8,128)(2,1)}), bf16[4,192,640]{2,1,0:T(8,128)(2,1)S(1)}, u32[]{:S(2)}, u32[]{:S(2)}) async-start(bf16[4,192,640]{2,1,0:T(8,128)(2,1)} %get-tuple-element.159), calls=%async_computation.2 | async-start | bytes 1966080 | tf_op jit(solution)/shard_map/cond/branch_1_fun/all_to_all | solution.py:413
  308.4 24.8 %all-to-all-start.3 = ((bf16[4,192,640]{2,1,0:T(8,128)(2,1)}), bf16[4,192,640]{2,1,0:T(8,128)(2,1)S(1)}, u32[]{:S(2)}, u32[]{:S(2)}) async-start(bf16[4,192,640]{2,1,0:T(8,128)(2,1)} %get-tuple-element.176), calls=%async_computation.3 | async-start | bytes 1966080 | tf_op jit(solution)/shard_map/cond/branch_1_fun/all_to_all | solution.py:413
  (22 other events, 162.9 us)

commit v12 on v11

--- a/solution.py
+++ b/solution.py
@@ -486,7 +486,7 @@
         mine[e][q] = swapped(piece)
 
     for q in range(count):
-        fetch(0, q, token_of(weights) if q else None)
+        fetch(0, q, token_of(weights) + outbox_weight[0] if q else None)
     done = None
     for e in range(rounds):
         parts, moving = [None] * count, [None] * count

time: 362 us -> 358 us (0.989)
  waiting for transfers between devices: 101 us -> 83.6 us
  starting transfers between devices: 136 us -> 149 us
    ppermute x40, waiting for transfers between devices: 56.9 us -> 46.1 us  [hop(): return lax.ppermute(value, 'fsdp', [(i, i + step) for i in pairs])]
    ppermute x40, starting transfers between devices: 100 us -> 111 us  [hop(): return lax.ppermute(value, 'fsdp', [(i, i + step) for i in pairs])]
    all_to_all x6, waiting for transfers between devices: 24.8 us -> 15.3 us  [swapped(): return lax.all_to_all(blocks, 'fsdp', 0, 0, tiled=False)]
    unnamed x68 -> x66, local copies, waits for them, and re-layouts: 10.3 us -> 10.6 us
  transfers between devices with their start and end apart: 50 -> 50, of which waited for: 16 -> 16; matrix products, arithmetic and copies ran while one was open for 1% -> 2% of each run, Pallas kernels for 23% -> 24%
where the time goes in v12:
time: 358 us; the launch traced here: 359 us
  starting transfers between devices  149 us (42%)
  Pallas kernels  100 us (28%)
  waiting for transfers between devices  83.6 us (23%)
  local copies, waits for them, and re-layouts  10.7 us (3%)
  between operations  8.77 us (2%)
  other arithmetic  6.27 us (2%)
    ppermute x40, starting transfers between devices, hop(): return lax.ppermute(value, 'fsdp', [(i, i + step) for i in pairs])  111 us
    pallas_call x30, Pallas kernels, call(): pl.pallas_call(body, name=name, out_shape=[jax.ShapeDtypeStruct(shape, ki...  100 us
    ppermute x40, waiting for transfers between devices, hop(): return lax.ppermute(value, 'fsdp', [(i, i + step) for i in pairs])  46.1 us
    all_to_all x6, starting transfers between devices, swapped(): return lax.all_to_all(blocks, 'fsdp', 0, 0, tiled=False)  28.8 us
    ppermute x1, waiting for transfers between devices, tail(): lax.ppermute(half, 'rep', [(i, (i + (1 << bit_place)) % length) for i in...  22.2 us
    all_to_all x6, waiting for transfers between devices, swapped(): return lax.all_to_all(blocks, 'fsdp', 0, 0, tiled=False)  15.3 us
    unnamed x66, local copies, waits for them, and re-layouts  10.6 us
    ppermute x3, starting transfers between devices, local(): lax.ppermute(half_weight, 'rep', [(i, (i + (1 << b)) % replicas) for i in...  7.93 us
  transfers between devices with their start and end apart: 50, of which 16 were waited for; matrix products, arithmetic and copies ran while one was open for 2% of the time, Pallas kernels for 24%

profile of v12, /device:TPU:0, one launch (start us, length us, event | category | flops | bytes accessed | tf_op | source)
XLA Modules:
  0.0 358.7 jit_solution(15799654499646319863)
XLA Ops:
  2.6 3.8 %collective-permute-start.24 = (f32[1]{0:T(128)}, f32[1]{0:T(128)}, u32[]{:S(2)}, u32[]{:S(2)}) collective-permute-start(f32[1]{0:T(128)} %mul.12), channel_id=1, source_target_pairs={{0,8},{4,12},{8,16},{12,20},{16,24},{20,28},{24,0},{28,4},{1,9},{5... | collective-permute-start | bytes 20 | tf_op jit(solution)/shard_map/ppermute | solution.py:447
  6.4 2.8 collective-permute-start.23
  9.2 1.5 copy-done.10
  11.6 4.9 %all-to-all-start.6 = ((bf16[4,96,640]{2,1,0:T(8,128)(2,1)}), bf16[4,96,640]{2,1,0:T(8,128)(2,1)S(1)}, u32[]{:S(2)}, u32[]{:S(2)}) async-start(bf16[4,96,640]{2,1,0:T(8,128)(2,1)} %cut_heads.4), calls=%async_computation.6 | async-start | bytes 983040 | tf_op jit(solution)/shard_map/all_to_all | solution.py:413
  16.4 5.4 %multiply_convert_fusion.weights_ref.refs_14_ = bf16[640,2560]{1,0:T(8,128)(2,1)} fusion(f32[]{:T(128)} %bitcast.32, f32[1,640,2560]{2,1,0:T(8,128)} %param.12), kind=kLoop, calls=%fused_computation | loop fusion | flops 4915200 | bytes 9830404 | tf_op jit(solution)/shard_map/convert_element_type | solution.py:456
  27.2 2.0 all-to-all-done.6.mine_ref.refs_14_
  29.2 3.5 all-to-all-start.8
  32.6 4.2 %partial_products.4 = (bf16[4,96,2560]{2,1,0:T(8,128)(2,1)S(1)}, bf16[96,2560]{1,0:T(8,128)(2,1)}, bf16[96,2560]{1,0:T(8,128)(2,1)}) custom-call(bf16[4,96,640]{2,1,0:T(8,128)(2,1)S(1)} %all-to-all-done.6.mine_ref.refs_14_, bf16[640,2560]{1,0:T(8,128)(2,1)} %multiply_convert_fusion.weights_ref.refs_14_), custom_call_target="tpu_custom_call" | custom-call | flops 1258291200 | bytes 5734400 | tf_op jit(solution)/shard_map/partial_products/pallas_call | solution.py:16
  38.1 4.7 %collective-permute-start.3 = (bf16[96,2560]{1,0:T(8,128)(2,1)}, bf16[96,2560]{1,0:T(8,128)(2,1)}, u32[]{:S(2)}, u32[]{:S(2)}) collective-permute-start(bf16[96,2560]{1,0:T(8,128)(2,1)} %get-tuple-element.249), channel_id=1, source_target_pairs={{0,1},{4,5},{8,9},{12,13},{16,17},{20,21},{24,25},{28,29}} | collective-permute-start | bytes 1474568 | tf_op jit(solution)/shard_map/ppermute | solution.py:44
  44.2 1.5 all-to-all-done.8.mine_ref.refs_15_
  45.7 4.4 %partial_products.6 = (bf16[4,96,2560]{2,1,0:T(8,128)(2,1)S(1)}, bf16[96,2560]{1,0:T(8,128)(2,1)}, bf16[96,2560]{1,0:T(8,128)(2,1)}) custom-call(bf16[4,96,640]{2,1,0:T(8,128)(2,1)S(1)} %all-to-all-done.8.mine_ref.refs_15_, bf16[640,2560]{1,0:T(8,128)(2,1)} %multiply_convert_fusion.weights_ref.refs_14_, f32[8,128]{1,0:T(8,128)S(1)} %add.38.refs_0_), custom_call_target="tpu_custom_call" | custom-call | flops 1258291200 | bytes 5734400 | tf_op jit(solution)/shard_map/partial_products/pallas_call | solution.py:16
  52.3 1.5 copy-done.1
  53.8 2.8 next_payload.10
  56.6 4.0 %collective-permute-start.5 = (bf16[96,2560]{1,0:T(8,128)(2,1)}, bf16[96,2560]{1,0:T(8,128)(2,1)S(1)}, u32[]{:S(2)}, u32[]{:S(2)}) collective-permute-start(bf16[96,2560]{1,0:T(8,128)(2,1)} %get-tuple-element.252), channel_id=1, source_target_pairs={{0,1},{1,2},{4,5},{5,6},{8,9},{9,10},{12,13},{13,14},{16,17},{17,1... | collective-permute-start | bytes 1474568 | tf_op jit(solution)/shard_map/ppermute | solution.py:44
  62.9 7.9 %all-to-all-start.7 = ((bf16[4,96,640]{2,1,0:T(8,128)(2,1)}), bf16[4,96,640]{2,1,0:T(8,128)(2,1)}, u32[]{:S(2)}, u32[]{:S(2)}) async-start(bf16[4,96,640]{2,1,0:T(8,128)(2,1)} %cut_heads.5), calls=%async_computation.7 | async-start | bytes 983040 | tf_op jit(solution)/shard_map/all_to_all | solution.py:413
  70.8 1.6 next_payload.15
  72.4 3.9 %collective-permute-start.28 = (bf16[96,2560]{1,0:T(8,128)(2,1)}, bf16[96,2560]{1,0:T(8,128)(2,1)S(1)}, u32[]{:S(2)}, u32[]{:S(2)}) collective-permute-start(bf16[96,2560]{1,0:T(8,128)(2,1)} %get-tuple-element.268), channel_id=1, source_target_pairs={{0,1},{1,2},{4,5},{5,6},{8,9},{9,10},{12,13},{13,14},{16,17},{17,1... | collective-permute-start | bytes 1474568 | tf_op jit(solution)/shard_map/ppermute | solution.py:44
  77.1 1.5 copy-done.2
  78.7 2.5 next_payload.11
  81.2 10.0 %collective-permute-start.7 = (bf16[96,2560]{1,0:T(8,128)(2,1)}, bf16[96,2560]{1,0:T(8,128)(2,1)S(1)}, u32[]{:S(2)}, u32[]{:S(2)}) collective-permute-start(bf16[96,2560]{1,0:T(8,128)(2,1)} %get-tuple-element.254), channel_id=1, source_target_pairs={{0,1},{1,2},{2,3},{4,5},{5,6},{6,7},{8,9},{9,10},{10,11},{12,13},{... | collective-permute-start | bytes 1474568 | tf_op jit(solution)/shard_map/ppermute | solution.py:44
  92.5 1.6 next_payload.16
  94.1 12.2 %collective-permute-start.30 = (bf16[96,2560]{1,0:T(8,128)(2,1)}, bf16[96,2560]{1,0:T(8,128)(2,1)}, u32[]{:S(2)}, u32[]{:S(2)}) collective-permute-start(bf16[96,2560]{1,0:T(8,128)(2,1)} %get-tuple-element.270), channel_id=1, source_target_pairs={{0,1},{1,2},{2,3},{4,5},{5,6},{6,7},{8,9},{9,10},{10,11},{12,13},{... | collective-permute-start | bytes 1474568 | tf_op jit(solution)/shard_map/ppermute | solution.py:44
  108.6 4.1 %all-to-all-start.9 = ((bf16[4,96,640]{2,1,0:T(8,128)(2,1)}), bf16[4,96,640]{2,1,0:T(8,128)(2,1)}, u32[]{:S(2)}, u32[]{:S(2)}) async-start(bf16[4,96,640]{2,1,0:T(8,128)(2,1)} %cut_heads.7), calls=%async_computation.9 | async-start | bytes 983040 | tf_op jit(solution)/shard_map/all_to_all | solution.py:413
  112.8 1.5 copy-done.3
  114.3 1.5 copy-done.4
  115.8 1.5 copy-done.7
  117.4 1.7 unit_gradient.4.refs_0_
  120.4 5.2 %collective-permute-start.9 = (bf16[96,2560]{1,0:T(8,128)(2,1)S(1)}, bf16[96,2560]{1,0:T(8,128)(2,1)S(1)}, u32[]{:S(2)}, u32[]{:S(2)}) collective-permute-start(bf16[96,2560]{1,0:T(8,128)(2,1)S(1)} %unit_gradient.4.refs_0_), channel_id=1, source_target_pairs={{0,1},{1,2},{2,3},{4,5},{5,6},{6,7},{8,9},{9,10},{10,11},{12,13},{... | collective-permute-start | bytes 1474568 | tf_op jit(solution)/shard_map/ppermute | solution.py:44
  125.7 2.4 unit_gradient.6.refs_7_
  129.4 5.7 %collective-permute-start.32 = (bf16[96,2560]{1,0:T(8,128)(2,1)}, bf16[96,2560]{1,0:T(8,128)(2,1)}, u32[]{:S(2)}, u32[]{:S(2)}) collective-permute-start(bf16[96,2560]{1,0:T(8,128)(2,1)} %unit_gradient.6.refs_7_), channel_id=1, source_target_pairs={{0,1},{1,2},{2,3},{4,5},{5,6},{6,7},{8,9},{9,10},{10,11},{12,13},{... | collective-permute-start | bytes 1474568 | tf_op jit(solution)/shard_map/ppermute | solution.py:44
  135.1 4.3 %partial_products.5 = (bf16[4,96,2560]{2,1,0:T(8,128)(2,1)S(1)}, bf16[96,2560]{1,0:T(8,128)(2,1)}, bf16[96,2560]{1,0:T(8,128)(2,1)}) custom-call(bf16[4,96,640]{2,1,0:T(8,128)(2,1)} %all-to-all-done.7.mine_ref.refs_14_, bf16[640,2560]{1,0:T(8,128)(2,1)} %multiply_convert_fusion.weights_ref.refs_14_, f32[8,128]{1,0:T(8,128)S(1)} %get-tuple-element.257.refs_0_), custom_call_target="tpu_custom_call" | custom-call | flops 1258291200 | bytes 5734400 | tf_op jit(solution)/shard_map/partial_products/pallas_call | solution.py:16
  139.7 1.6 next_payload.12
  141.2 7.2 %collective-permute-start.11 = (bf16[96,2560]{1,0:T(8,128)(2,1)}, bf16[96,2560]{1,0:T(8,128)(2,1)}, u32[]{:S(2)}, u32[]{:S(2)}) collective-permute-start(bf16[96,2560]{1,0:T(8,128)(2,1)} %get-tuple-element.259), channel_id=1, source_target_pairs={{0,1},{1,2},{2,3},{4,5},{5,6},{6,7},{8,9},{9,10},{10,11},{12,13},{... | collective-permute-start | bytes 1474568 | tf_op jit(solution)/shard_map/ppermute | solution.py:44
  149.7 4.4 %partial_products.7 = (bf16[4,96,2560]{2,1,0:T(8,128)(2,1)S(1)}, bf16[96,2560]{1,0:T(8,128)(2,1)}, bf16[96,2560]{1,0:T(8,128)(2,1)}) custom-call(bf16[4,96,640]{2,1,0:T(8,128)(2,1)} %all-to-all-done.9.mine_ref.refs_15_, bf16[640,2560]{1,0:T(8,128)(2,1)} %multiply_convert_fusion.weights_ref.refs_14_, f32[8,128]{1,0:T(8,128)S(1)} %get-tuple-element.273.refs_0_), custom_call_target="tpu_custom_call" | custom-call | flops 1258291200 | bytes 5734400 | tf_op jit(solution)/shard_map/partial_products/pallas_call | solution.py:16
  154.1 2.5 next_payload.17
  156.6 4.6 %collective-permute-start.34 = (bf16[96,2560]{1,0:T(8,128)(2,1)S(1)}, bf16[96,2560]{1,0:T(8,128)(2,1)S(1)}, u32[]{:S(2)}, u32[]{:S(2)}) collective-permute-start(bf16[96,2560]{1,0:T(8,128)(2,1)S(1)} %get-tuple-element.275), channel_id=1, source_target_pairs={{0,1},{1,2},{2,3},{4,5},{5,6},{6,7},{8,9},{9,10},{10,11},{12,13},{... | collective-permute-start | bytes 1474568 | tf_op jit(solution)/shard_map/ppermute | solution.py:44
  162.5 1.8 collective-permute-done.12.left_ref.refs_5_
  164.3 2.5 next_payload.13
  166.7 3.0 collective-permute-start.13
  171.3 5.7 %collective-permute-done.35.left_ref.refs_12_ = bf16[96,2560]{1,0:T(8,128)(2,1)S(1)} collective-permute-done((bf16[96,2560]{1,0:T(8,128)(2,1)S(1)}, bf16[96,2560]{1,0:T(8,128)(2,1)S(1)}, u32[]{:S(2)}, u32[]{:S(2)}) %collective-permute-start.35) | collective-permute-done | bytes 491552 | tf_op jit(solution)/shard_map/ppermute | solution.py:44
  178.4 2.2 collective-permute-start.36
  182.0 5.5 %collective-permute-done.14.left_ref.refs_6_ = bf16[96,2560]{1,0:T(8,128)(2,1)S(1)} collective-permute-done((bf16[96,2560]{1,0:T(8,128)(2,1)S(1)}, bf16[96,2560]{1,0:T(8,128)(2,1)S(1)}, u32[]{:S(2)}, u32[]{:S(2)}) %collective-permute-start.14) | collective-permute-done | bytes 491552 | tf_op jit(solution)/shard_map/ppermute | solution.py:44
  188.9 2.2 collective-permute-start.15
  192.4 5.7 %collective-permute-done.37.left_ref.refs_13_ = bf16[96,2560]{1,0:T(8,128)(2,1)S(1)} collective-permute-done((bf16[96,2560]{1,0:T(8,128)(2,1)S(1)}, bf16[96,2560]{1,0:T(8,128)(2,1)S(1)}, u32[]{:S(2)}, u32[]{:S(2)}) %collective-permute-start.37) | collective-permute-done | bytes 491552 | tf_op jit(solution)/shard_map/ppermute | solution.py:44
  199.4 2.1 collective-permute-start.38
  203.1 8.5 %weight_step.8 = (f32[640,2560]{1,0:T(8,128)}, f32[8,128]{1,0:T(8,128)S(1)}) custom-call(s32[4]{0:T(128)S(1)} %and_select_fusion.s, bf16[96,2560]{1,0:T(8,128)(2,1)S(1)} %unit_gradient.4.refs_0_, bf16[96,2560]{1,0:T(8,128)(2,1)S(1)} %collective-permute-done.9.right_ref.refs_1_, bf16[96,2560]{1,0:T(8,128)(2,1)} %collective-permute-done.11.right_ref.refs_2_, ...), custom_call_target="tpu_custom_call" | custom-call | flops 2516582400 | bytes 26542080 | tf_op jit(solution)/shard_map/weight_step/pallas_call | solution.py:16
  213.6 6.1 %collective-permute-start.17 = (bf16[96,2560]{1,0:T(8,128)(2,1)S(1)}, bf16[96,2560]{1,0:T(8,128)(2,1)}, u32[]{:S(2)}, u32[]{:S(2)}) collective-permute-start(bf16[96,2560]{1,0:T(8,128)(2,1)S(1)} %unit_gradient.5.refs_0_), channel_id=1, source_target_pairs={{0,1},{1,2},{2,3},{4,5},{5,6},{6,7},{8,9},{9,10},{10,11},{12,13},{... | collective-permute-start | bytes 1474568 | tf_op jit(solution)/shard_map/ppermute | solution.py:44
  221.6 5.3 %collective-permute-start.40 = (bf16[96,2560]{1,0:T(8,128)(2,1)S(1)}, bf16[96,2560]{1,0:T(8,128)(2,1)}, u32[]{:S(2)}, u32[]{:S(2)}) collective-permute-start(bf16[96,2560]{1,0:T(8,128)(2,1)S(1)} %unit_gradient.7.refs_7_), channel_id=1, source_target_pairs={{0,1},{1,2},{2,3},{4,5},{5,6},{6,7},{8,9},{9,10},{10,11},{12,13},{... | collective-permute-start | bytes 1474568 | tf_op jit(solution)/shard_map/ppermute | solution.py:44
  227.0 2.8 collective-permute-done.20.refs_4_
  232.6 7.8 %collective-permute-done.43.refs_11_ = bf16[96,2560]{1,0:T(8,128)(2,1)} collective-permute-done((bf16[96,2560]{1,0:T(8,128)(2,1)S(1)}, bf16[96,2560]{1,0:T(8,128)(2,1)}, u32[]{:S(2)}, u32[]{:S(2)}) %collective-permute-start.43) | collective-permute-done | bytes 491552 | tf_op jit(solution)/shard_map/ppermute | solution.py:44
  243.1 7.8 %collective-permute-done.21.refs_5_ = bf16[96,2560]{1,0:T(8,128)(2,1)} collective-permute-done((bf16[96,2560]{1,0:T(8,128)(2,1)}, bf16[96,2560]{1,0:T(8,128)(2,1)}, u32[]{:S(2)}, u32[]{:S(2)}) %collective-permute-start.21) | collective-permute-done | bytes 491552 | tf_op jit(solution)/shard_map/ppermute | solution.py:44
  253.6 7.8 %collective-permute-done.44.refs_12_ = bf16[96,2560]{1,0:T(8,128)(2,1)} collective-permute-done((bf16[96,2560]{1,0:T(8,128)(2,1)}, bf16[96,2560]{1,0:T(8,128)(2,1)}, u32[]{:S(2)}, u32[]{:S(2)}) %collective-permute-start.44) | collective-permute-done | bytes 491552 | tf_op jit(solution)/shard_map/ppermute | solution.py:44
  265.5 9.1 %grad_rows.7 = (bf16[4,192,640]{2,1,0:T(8,128)(2,1)}, f32[8,128]{1,0:T(8,128)}) custom-call(s32[4]{0:T(128)S(1)} %and_select_fusion.s, bf16[96,2560]{1,0:T(8,128)(2,1)S(1)} %unit_gradient.4.refs_0_, bf16[96,2560]{1,0:T(8,128)(2,1)S(1)} %collective-permute-done.9.right_ref.refs_1_, bf16[96,2560]{1,0:T(8,128)(2,1)} %collective-permute-done.11.right_ref.refs_2_, ...), custom_call_target="tpu_custom_call" | custom-call | flops 2516582400 | bytes 10158080 | tf_op jit(solution)/shard_map/grad_rows/pallas_call | solution.py:16
  275.3 9.7 %weight_step.9 = bf16[640,2560]{1,0:T(8,128)(2,1)} custom-call(s32[4]{0:T(128)S(1)} %and_select_fusion.s, bf16[96,2560]{1,0:T(8,128)(2,1)S(1)} %copy-done.27, bf16[96,2560]{1,0:T(8,128)(2,1)} %collective-permute-done.17.refs_1_, bf16[96,2560]{1,0:T(8,128)(2,1)} %collective-permute-done.18.refs_2_, bf16[96,2560]{1,0:T(8,128)(2,1)} %collective-permute-done.19.refs_3_, ...), custom_call_target="tpu_custom_call" | custom-call | flops 2516582400 | bytes 26542080 | tf_op jit(solution)/shard_map/weight_step/pallas_call | solution.py:16
  285.0 66.3 %conditional.1 = (bf16[640,2560]{1,0:T(8,128)(2,1)}, bf16[1,384,2560]{2,1,0:T(8,128)(2,1)S(1)}, f32[1,640,2560]{2,1,0:T(8,128)}) conditional(s32[]{:T(128)} %clamp.3, (bf16[640,2560]{1,0:T(8,128)(2,1)}, bf16[4,192,640]{2,1,0:T(8,128)(2,1)}, s32[4]{0:T(128)S(1)}, bf16[96,2560]{1,0:T(8,128)(2,1)S(1)}, bf16[96,2560]{1,0:T(8,128)(2,1)}, ...), branch_computations={%region_1.2_spmd, %region_2.3_spmd, %region_3.4_spmd} | conditional | flops 5033164800 | bytes 59637888 | solution.py:547
  285.0 1.9 collective-permute-start.2
  286.9 4.9 %all-to-all-start.4 = ((bf16[4,192,640]{2,1,0:T(8,128)(2,1)}), bf16[4,192,640]{2,1,0:T(8,128)(2,1)S(1)}, u32[]{:S(2)}, u32[]{:S(2)}) async-start(bf16[4,192,640]{2,1,0:T(8,128)(2,1)} %get-tuple-element.183), calls=%async_computation.4 | async-start | bytes 1966080 | tf_op jit(solution)/shard_map/cond/branch_2_fun/all_to_all | solution.py:413
  291.8 9.3 %grad_rows.6 = (bf16[4,192,640]{2,1,0:T(8,128)(2,1)}, f32[8,128]{1,0:T(8,128)S(1)}) custom-call(s32[4]{0:T(128)S(1)} %get-tuple-element.184.s, bf16[96,2560]{1,0:T(8,128)(2,1)S(1)} %get-tuple-element.185.refs_0_, bf16[96,2560]{1,0:T(8,128)(2,1)} %get-tuple-element.186.refs_1_, bf16[96,2560]{1,0:T(8,128)(2,1)} %get-tuple-element.187.refs_2_, ...), custom_call_target="tpu_custom_call" | custom-call | flops 2516582400 | bytes 10158080 | tf_op jit(solution)/shard_map/cond/branch_2_fun/grad_rows/pallas_call | solution.py:16
  301.1 6.9 %all-to-all-done.4.refs_0_ = bf16[4,192,640]{2,1,0:T(8,128)(2,1)S(1)} async-done(((bf16[4,192,640]{2,1,0:T(8,128)(2,1)}), bf16[4,192,640]{2,1,0:T(8,128)(2,1)S(1)}, u32[]{:S(2)}, u32[]{:S(2)}) %all-to-all-start.4) | async-done | bytes 983072 | tf_op jit(solution)/shard_map/cond/branch_2_fun/all_to_all | solution.py:413
  308.0 3.5 all-to-all-start.5
  311.5 12.4 %weight_step.7 = f32[640,2560]{1,0:T(8,128)} custom-call(s32[4]{0:T(128)S(1)} %get-tuple-element.184.s, bf16[96,2560]{1,0:T(8,128)(2,1)S(1)} %get-tuple-element.185.refs_0_, bf16[96,2560]{1,0:T(8,128)(2,1)} %get-tuple-element.186.refs_1_, bf16[96,2560]{1,0:T(8,128)(2,1)} %get-tuple-element.187.refs_2_, bf16[96,2560]{1,0:T(8,128)(2,1)} %get-tuple-element.188.refs_3_, ...), custom_call_target="tpu_custom_call" | custom-call | flops 2516582400 | bytes 26542080 | tf_op jit(solution)/shard_map/cond/branch_2_fun/weight_step/pallas_call | solution.py:16
  323.9 5.0 %all-to-all-done.5.refs_1_ = bf16[4,192,640]{2,1,0:T(8,128)(2,1)S(1)} async-done(((bf16[4,192,640]{2,1,0:T(8,128)(2,1)}), bf16[4,192,640]{2,1,0:T(8,128)(2,1)S(1)}, u32[]{:S(2)}, u32[]{:S(2)}) %all-to-all-start.5) | async-done | bytes 983072 | tf_op jit(solution)/shard_map/cond/branch_2_fun/all_to_all | solution.py:413
  329.1 22.2 %collective-permute-done.2 = bf16[640,2560]{1,0:T(8,128)(2,1)} collective-permute-done((bf16[640,2560]{1,0:T(8,128)(2,1)}, bf16[640,2560]{1,0:T(8,128)(2,1)}, u32[]{:S(2)}, u32[]{:S(2)}) %collective-permute-start.2) | collective-permute-done | bytes 3276832 | tf_op jit(solution)/shard_map/cond/branch_2_fun/ppermute | solution.py:418
  351.3 5.1 %widened.1 = f32[640,2560]{1,0:T(8,128)} custom-call(bf16[640,2560]{1,0:T(8,128)(2,1)} %get-tuple-element.285.value_ref), custom_call_target="tpu_custom_call" | custom-call | bytes 9830400 | tf_op jit(solution)/shard_map/widened/pallas_call | solution.py:16
  (143 shorter events, 46.7 us)
Async XLA Ops:
  1.3 23.2 %collective-permute-start.25 = (f32[1]{0:T(128)}, f32[1]{0:T(128)}, u32[]{:S(2)}, u32[]{:S(2)}) collective-permute-start(f32[1]{0:T(128)} %mul.12), channel_id=1, source_target_pairs={{0,4},{4,8},{8,12},{12,16},{16,20},{20,24},{24,28},{28,0},{1,5},{5... | collective-permute-start | bytes 20 | tf_op jit(solution)/shard_map/ppermute | solution.py:447
  2.6 21.8 %collective-permute-start.24 = (f32[1]{0:T(128)}, f32[1]{0:T(128)}, u32[]{:S(2)}, u32[]{:S(2)}) collective-permute-start(f32[1]{0:T(128)} %mul.12), channel_id=1, source_target_pairs={{0,8},{4,12},{8,16},{12,20},{16,24},{20,28},{24,0},{28,4},{1,9},{5... | collective-permute-start | bytes 20 | tf_op jit(solution)/shard_map/ppermute | solution.py:447
  6.4 19.2 %collective-permute-start.23 = (f32[1]{0:T(128)}, f32[1]{0:T(128)}, u32[]{:S(2)}, u32[]{:S(2)}) collective-permute-start(f32[1]{0:T(128)} %mul.12), channel_id=1, source_target_pairs={{0,16},{4,20},{8,24},{12,28},{16,0},{20,4},{24,8},{28,12},{1,17},{... | collective-permute-start | bytes 20 | tf_op jit(solution)/shard_map/ppermute | solution.py:447
  11.6 17.6 %all-to-all-start.6 = ((bf16[4,96,640]{2,1,0:T(8,128)(2,1)}), bf16[4,96,640]{2,1,0:T(8,128)(2,1)S(1)}, u32[]{:S(2)}, u32[]{:S(2)}) async-start(bf16[4,96,640]{2,1,0:T(8,128)(2,1)} %cut_heads.4), calls=%async_computation.6 | async-start | bytes 983040 | tf_op jit(solution)/shard_map/all_to_all | solution.py:413
  29.2 21.0 %copy-start.22 = (bf16[4,96,640]{2,1,0:T(8,128)(2,1)}, bf16[4,96,640]{2,1,0:T(8,128)(2,1)S(1)}, u32[]{:S(2)}) copy-start(bf16[4,96,640]{2,1,0:T(8,128)(2,1)S(1)} %all-to-all-done.6.mine_ref.refs_14_) | copy-start | bytes 1474564
  29.2 16.6 %all-to-all-start.8 = ((bf16[4,96,640]{2,1,0:T(8,128)(2,1)}), bf16[4,96,640]{2,1,0:T(8,128)(2,1)S(1)}, u32[]{:S(2)}, u32[]{:S(2)}) async-start(bf16[4,96,640]{2,1,0:T(8,128)(2,1)} %cut_heads.6), calls=%async_computation.8 | async-start | bytes 983040 | tf_op jit(solution)/shard_map/all_to_all | solution.py:413
  38.1 14.2 %collective-permute-start.3 = (bf16[96,2560]{1,0:T(8,128)(2,1)}, bf16[96,2560]{1,0:T(8,128)(2,1)}, u32[]{:S(2)}, u32[]{:S(2)}) collective-permute-start(bf16[96,2560]{1,0:T(8,128)(2,1)} %get-tuple-element.249), channel_id=1, source_target_pairs={{0,1},{4,5},{8,9},{12,13},{16,17},{20,21},{24,25},{28,29}} | collective-permute-start | bytes 1474568 | tf_op jit(solution)/shard_map/ppermute | solution.py:44
  42.8 9.5 %collective-permute-start.4 = (bf16[96,2560]{1,0:T(8,128)(2,1)}, bf16[96,2560]{1,0:T(8,128)(2,1)}, u32[]{:S(2)}, u32[]{:S(2)}) collective-permute-start(bf16[96,2560]{1,0:T(8,128)(2,1)} %get-tuple-element.250), channel_id=1, source_target_pairs={{3,2},{7,6},{11,10},{15,14},{19,18},{23,22},{27,26},{31,30}} | collective-permute-start | bytes 1474568 | tf_op jit(solution)/shard_map/ppermute | solution.py:44
  50.2 20.6 %collective-permute-start.26 = (bf16[96,2560]{1,0:T(8,128)(2,1)}, bf16[96,2560]{1,0:T(8,128)(2,1)S(1)}, u32[]{:S(2)}, u32[]{:S(2)}) collective-permute-start(bf16[96,2560]{1,0:T(8,128)(2,1)} %get-tuple-element.265), channel_id=1, source_target_pairs={{0,1},{4,5},{8,9},{12,13},{16,17},{20,21},{24,25},{28,29}} | collective-permute-start | bytes 1474568 | tf_op jit(solution)/shard_map/ppermute | solution.py:44
  51.5 19.3 %collective-permute-start.27 = (bf16[96,2560]{1,0:T(8,128)(2,1)}, bf16[96,2560]{1,0:T(8,128)(2,1)S(1)}, u32[]{:S(2)}, u32[]{:S(2)}) collective-permute-start(bf16[96,2560]{1,0:T(8,128)(2,1)} %get-tuple-element.266), channel_id=1, source_target_pairs={{3,2},{7,6},{11,10},{15,14},{19,18},{23,22},{27,26},{31,30}} | collective-permute-start | bytes 1474568 | tf_op jit(solution)/shard_map/ppermute | solution.py:44
  56.6 20.5 %collective-permute-start.5 = (bf16[96,2560]{1,0:T(8,128)(2,1)}, bf16[96,2560]{1,0:T(8,128)(2,1)S(1)}, u32[]{:S(2)}, u32[]{:S(2)}) collective-permute-start(bf16[96,2560]{1,0:T(8,128)(2,1)} %get-tuple-element.252), channel_id=1, source_target_pairs={{0,1},{1,2},{4,5},{5,6},{8,9},{9,10},{12,13},{13,14},{16,17},{17,1... | collective-permute-start | bytes 1474568 | tf_op jit(solution)/shard_map/ppermute | solution.py:44
  60.6 16.5 %collective-permute-start.6 = (bf16[96,2560]{1,0:T(8,128)(2,1)}, bf16[96,2560]{1,0:T(8,128)(2,1)}, u32[]{:S(2)}, u32[]{:S(2)}) collective-permute-start(bf16[96,2560]{1,0:T(8,128)(2,1)} %get-tuple-element.253), channel_id=1, source_target_pairs={{2,1},{3,2},{6,5},{7,6},{10,9},{11,10},{14,13},{15,14},{18,17},{19... | collective-permute-start | bytes 1474568 | tf_op jit(solution)/shard_map/ppermute | solution.py:44
  62.9 45.7 %all-to-all-start.7 = ((bf16[4,96,640]{2,1,0:T(8,128)(2,1)}), bf16[4,96,640]{2,1,0:T(8,128)(2,1)}, u32[]{:S(2)}, u32[]{:S(2)}) async-start(bf16[4,96,640]{2,1,0:T(8,128)(2,1)} %cut_heads.5), calls=%async_computation.7 | async-start | bytes 983040 | tf_op jit(solution)/shard_map/all_to_all | solution.py:413
  72.4 20.1 %collective-permute-start.28 = (bf16[96,2560]{1,0:T(8,128)(2,1)}, bf16[96,2560]{1,0:T(8,128)(2,1)S(1)}, u32[]{:S(2)}, u32[]{:S(2)}) collective-permute-start(bf16[96,2560]{1,0:T(8,128)(2,1)} %get-tuple-element.268), channel_id=1, source_target_pairs={{0,1},{1,2},{4,5},{5,6},{8,9},{9,10},{12,13},{13,14},{16,17},{17,1... | collective-permute-start | bytes 1474568 | tf_op jit(solution)/shard_map/ppermute | solution.py:44
  76.3 16.2 %collective-permute-start.29 = (bf16[96,2560]{1,0:T(8,128)(2,1)}, bf16[96,2560]{1,0:T(8,128)(2,1)S(1)}, u32[]{:S(2)}, u32[]{:S(2)}) collective-permute-start(bf16[96,2560]{1,0:T(8,128)(2,1)} %get-tuple-element.269), channel_id=1, source_target_pairs={{2,1},{3,2},{6,5},{7,6},{10,9},{11,10},{14,13},{15,14},{18,17},{19... | collective-permute-start | bytes 1474568 | tf_op jit(solution)/shard_map/ppermute | solution.py:44
  81.2 26.4 %copy-start.13 = (bf16[1,384,2560]{2,1,0:T(8,128)(2,1)S(1)}, bf16[1,384,2560]{2,1,0:T(8,128)(2,1)}, u32[]{:S(2)}) copy-start(bf16[1,384,2560]{2,1,0:T(8,128)(2,1)} %param.16) | copy-start | bytes 5898244
  81.2 31.5 %collective-permute-start.7 = (bf16[96,2560]{1,0:T(8,128)(2,1)}, bf16[96,2560]{1,0:T(8,128)(2,1)S(1)}, u32[]{:S(2)}, u32[]{:S(2)}) collective-permute-start(bf16[96,2560]{1,0:T(8,128)(2,1)} %get-tuple-element.254), channel_id=1, source_target_pairs={{0,1},{1,2},{2,3},{4,5},{5,6},{6,7},{8,9},{9,10},{10,11},{12,13},{... | collective-permute-start | bytes 1474568 | tf_op jit(solution)/shard_map/ppermute | solution.py:44
  91.2 21.5 %copy-start.29 = (f32[2560]{0:T(1024)S(1)}, f32[2560]{0:T(1024)}, u32[]{:S(2)}) copy-start(f32[2560]{0:T(1024)} %param.19) | copy-start | bytes 30724
  91.2 21.5 %collective-permute-start.8 = (bf16[96,2560]{1,0:T(8,128)(2,1)}, bf16[96,2560]{1,0:T(8,128)(2,1)}, u32[]{:S(2)}, u32[]{:S(2)}) collective-permute-start(bf16[96,2560]{1,0:T(8,128)(2,1)} %get-tuple-element.255), channel_id=1, source_target_pairs={{1,0},{2,1},{3,2},{5,4},{6,5},{7,6},{9,8},{10,9},{11,10},{13,12},{... | collective-permute-start | bytes 1474568 | tf_op jit(solution)/shard_map/ppermute | solution.py:44
  94.1 31.6 %collective-permute-start.30 = (bf16[96,2560]{1,0:T(8,128)(2,1)}, bf16[96,2560]{1,0:T(8,128)(2,1)}, u32[]{:S(2)}, u32[]{:S(2)}) collective-permute-start(bf16[96,2560]{1,0:T(8,128)(2,1)} %get-tuple-element.270), channel_id=1, source_target_pairs={{0,1},{1,2},{2,3},{4,5},{5,6},{6,7},{8,9},{9,10},{10,11},{12,13},{... | collective-permute-start | bytes 1474568 | tf_op jit(solution)/shard_map/ppermute | solution.py:44
  106.4 19.3 %collective-permute-start.31 = (bf16[96,2560]{1,0:T(8,128)(2,1)}, bf16[96,2560]{1,0:T(8,128)(2,1)}, u32[]{:S(2)}, u32[]{:S(2)}) collective-permute-start(bf16[96,2560]{1,0:T(8,128)(2,1)} %get-tuple-element.271), channel_id=1, source_target_pairs={{1,0},{2,1},{3,2},{5,4},{6,5},{7,6},{9,8},{10,9},{11,10},{13,12},{... | collective-permute-start | bytes 1474568 | tf_op jit(solution)/shard_map/ppermute | solution.py:44
  108.6 41.2 %all-to-all-start.9 = ((bf16[4,96,640]{2,1,0:T(8,128)(2,1)}), bf16[4,96,640]{2,1,0:T(8,128)(2,1)}, u32[]{:S(2)}, u32[]{:S(2)}) async-start(bf16[4,96,640]{2,1,0:T(8,128)(2,1)} %cut_heads.7), calls=%async_computation.9 | async-start | bytes 983040 | tf_op jit(solution)/shard_map/all_to_all | solution.py:413
  119.1 20.5 %collective-permute-start.10 = (bf16[96,2560]{1,0:T(8,128)(2,1)S(1)}, bf16[96,2560]{1,0:T(8,128)(2,1)S(1)}, u32[]{:S(2)}, u32[]{:S(2)}) collective-permute-start(bf16[96,2560]{1,0:T(8,128)(2,1)S(1)} %unit_gradient.4.refs_0_), channel_id=1, source_target_pairs={{1,0},{2,1},{3,2},{5,4},{6,5},{7,6},{9,8},{10,9},{11,10},{13,12},{... | collective-permute-start | bytes 1474568 | tf_op jit(solution)/shard_map/ppermute | solution.py:44
  120.4 19.2 %collective-permute-start.9 = (bf16[96,2560]{1,0:T(8,128)(2,1)S(1)}, bf16[96,2560]{1,0:T(8,128)(2,1)S(1)}, u32[]{:S(2)}, u32[]{:S(2)}) collective-permute-start(bf16[96,2560]{1,0:T(8,128)(2,1)S(1)} %unit_gradient.4.refs_0_), channel_id=1, source_target_pairs={{0,1},{1,2},{2,3},{4,5},{5,6},{6,7},{8,9},{9,10},{10,11},{12,13},{... | collective-permute-start | bytes 1474568 | tf_op jit(solution)/shard_map/ppermute | solution.py:44
  128.1 26.0 %collective-permute-start.33 = (bf16[96,2560]{1,0:T(8,128)(2,1)}, bf16[96,2560]{1,0:T(8,128)(2,1)}, u32[]{:S(2)}, u32[]{:S(2)}) collective-permute-start(bf16[96,2560]{1,0:T(8,128)(2,1)} %unit_gradient.6.refs_7_), channel_id=1, source_target_pairs={{1,0},{2,1},{3,2},{5,4},{6,5},{7,6},{9,8},{10,9},{11,10},{13,12},{... | collective-permute-start | bytes 1474568 | tf_op jit(solution)/shard_map/ppermute | solution.py:44
  129.4 24.7 %collective-permute-start.32 = (bf16[96,2560]{1,0:T(8,128)(2,1)}, bf16[96,2560]{1,0:T(8,128)(2,1)}, u32[]{:S(2)}, u32[]{:S(2)}) collective-permute-start(bf16[96,2560]{1,0:T(8,128)(2,1)} %unit_gradient.6.refs_7_), channel_id=1, source_target_pairs={{0,1},{1,2},{2,3},{4,5},{5,6},{6,7},{8,9},{9,10},{10,11},{12,13},{... | collective-permute-start | bytes 1474568 | tf_op jit(solution)/shard_map/ppermute | solution.py:44
  141.2 21.2 %collective-permute-start.11 = (bf16[96,2560]{1,0:T(8,128)(2,1)}, bf16[96,2560]{1,0:T(8,128)(2,1)}, u32[]{:S(2)}, u32[]{:S(2)}) collective-permute-start(bf16[96,2560]{1,0:T(8,128)(2,1)} %get-tuple-element.259), channel_id=1, source_target_pairs={{0,1},{1,2},{2,3},{4,5},{5,6},{6,7},{8,9},{9,10},{10,11},{12,13},{... | collective-permute-start | bytes 1474568 | tf_op jit(solution)/shard_map/ppermute | solution.py:44
  148.4 15.9 %collective-permute-start.12 = (bf16[96,2560]{1,0:T(8,128)(2,1)}, bf16[96,2560]{1,0:T(8,128)(2,1)}, u32[]{:S(2)}, u32[]{:S(2)}) collective-permute-start(bf16[96,2560]{1,0:T(8,128)(2,1)} %get-tuple-element.260), channel_id=1, source_target_pairs={{1,0},{2,1},{3,2},{5,4},{6,5},{7,6},{9,8},{10,9},{11,10},{13,12},{... | collective-permute-start | bytes 1474568 | tf_op jit(solution)/shard_map/ppermute | solution.py:44
  156.6 14.7 %collective-permute-start.34 = (bf16[96,2560]{1,0:T(8,128)(2,1)S(1)}, bf16[96,2560]{1,0:T(8,128)(2,1)S(1)}, u32[]{:S(2)}, u32[]{:S(2)}) collective-permute-start(bf16[96,2560]{1,0:T(8,128)(2,1)S(1)} %get-tuple-element.275), channel_id=1, source_target_pairs={{0,1},{1,2},{2,3},{4,5},{5,6},{6,7},{8,9},{9,10},{10,11},{12,13},{... | collective-permute-start | bytes 1474568 | tf_op jit(solution)/shard_map/ppermute | solution.py:44
  161.1 15.9 %collective-permute-start.35 = (bf16[96,2560]{1,0:T(8,128)(2,1)S(1)}, bf16[96,2560]{1,0:T(8,128)(2,1)S(1)}, u32[]{:S(2)}, u32[]{:S(2)}) collective-permute-start(bf16[96,2560]{1,0:T(8,128)(2,1)S(1)} %get-tuple-element.276), channel_id=1, source_target_pairs={{1,0},{2,1},{3,2},{5,4},{6,5},{7,6},{9,8},{10,9},{11,10},{13,12},{... | collective-permute-start | bytes 1474568 | tf_op jit(solution)/shard_map/ppermute | solution.py:44
  166.7 15.3 %collective-permute-start.13 = (bf16[96,2560]{1,0:T(8,128)(2,1)S(1)}, bf16[96,2560]{1,0:T(8,128)(2,1)S(1)}, u32[]{:S(2)}, u32[]{:S(2)}) collective-permute-start(bf16[96,2560]{1,0:T(8,128)(2,1)S(1)} %get-tuple-element.261), channel_id=1, source_target_pairs={{0,1},{1,2},{2,3},{4,5},{5,6},{6,7},{8,9},{9,10},{10,11},{12,13},{... | collective-permute-start | bytes 1474568 | tf_op jit(solution)/shard_map/ppermute | solution.py:44
  169.7 17.8 %collective-permute-start.14 = (bf16[96,2560]{1,0:T(8,128)(2,1)S(1)}, bf16[96,2560]{1,0:T(8,128)(2,1)S(1)}, u32[]{:S(2)}, u32[]{:S(2)}) collective-permute-start(bf16[96,2560]{1,0:T(8,128)(2,1)S(1)} %get-tuple-element.262), channel_id=1, source_target_pairs={{1,0},{2,1},{3,2},{5,4},{6,5},{7,6},{9,8},{10,9},{11,10},{13,12},{... | collective-permute-start | bytes 1474568 | tf_op jit(solution)/shard_map/ppermute | solution.py:44
  171.3 31.7 %copy-start.14 = (bf16[96,2560]{1,0:T(8,128)(2,1)}, bf16[96,2560]{1,0:T(8,128)(2,1)S(1)}, u32[]{:S(2)}) copy-start(bf16[96,2560]{1,0:T(8,128)(2,1)S(1)} %collective-permute-done.34.right_ref.refs_9_) | copy-start | bytes 1474564
  177.0 26.0 %copy-start.15 = (bf16[96,2560]{1,0:T(8,128)(2,1)}, bf16[96,2560]{1,0:T(8,128)(2,1)S(1)}, u32[]{:S(2)}) copy-start(bf16[96,2560]{1,0:T(8,128)(2,1)S(1)} %collective-permute-done.35.left_ref.refs_12_) | copy-start | bytes 1474564
  177.0 26.0 %slice-start = ((s8[6553600]{0:T(1024)(128)(4,1)}), s8[4194304]{0:T(1024)(128)(4,1)S(1)}, s32[]{:S(2)}) async-start(s8[6553600]{0:T(1024)(128)(4,1)} %bitcast.45), calls=%async_computation.10 | async-start | bytes 8388608
  178.4 14.1 %collective-permute-start.36 = (bf16[96,2560]{1,0:T(8,128)(2,1)S(1)}, bf16[96,2560]{1,0:T(8,128)(2,1)S(1)}, u32[]{:S(2)}, u32[]{:S(2)}) collective-permute-start(bf16[96,2560]{1,0:T(8,128)(2,1)S(1)} %get-tuple-element.277), channel_id=1, source_target_pairs={{0,1},{1,2},{2,3},{4,5},{5,6},{6,7},{8,9},{9,10},{10,11},{12,13},{... | collective-permute-start | bytes 1474568 | tf_op jit(solution)/shard_map/ppermute | solution.py:44
  180.6 22.5 %slice-start.1 = ((s8[6553600]{0:T(1024)(128)(4,1)}), s8[2359296]{0:T(1024)(128)(4,1)S(1)}, s32[]{:S(2)}) async-start(s8[6553600]{0:T(1024)(128)(4,1)} %bitcast.45), calls=%async_computation.11 | async-start | bytes 4718592
  180.6 17.5 %collective-permute-start.37 = (bf16[96,2560]{1,0:T(8,128)(2,1)S(1)}, bf16[96,2560]{1,0:T(8,128)(2,1)S(1)}, u32[]{:S(2)}, u32[]{:S(2)}) collective-permute-start(bf16[96,2560]{1,0:T(8,128)(2,1)S(1)} %get-tuple-element.278), channel_id=1, source_target_pairs={{1,0},{2,1},{3,2},{5,4},{6,5},{7,6},{9,8},{10,9},{11,10},{13,12},{... | collective-permute-start | bytes 1474568 | tf_op jit(solution)/shard_map/ppermute | solution.py:44
  182.0 21.0 %copy-start.16 = (bf16[96,2560]{1,0:T(8,128)(2,1)}, bf16[96,2560]{1,0:T(8,128)(2,1)S(1)}, u32[]{:S(2)}) copy-start(bf16[96,2560]{1,0:T(8,128)(2,1)S(1)} %collective-permute-done.13.right_ref.refs_3_) | copy-start | bytes 1474564
  187.6 15.5 %copy-start.18 = (bf16[96,2560]{1,0:T(8,128)(2,1)}, bf16[96,2560]{1,0:T(8,128)(2,1)S(1)}, u32[]{:S(2)}) copy-start(bf16[96,2560]{1,0:T(8,128)(2,1)S(1)} %collective-permute-done.14.left_ref.refs_6_) | copy-start | bytes 1474564
  188.9 14.2 %copy-start.23 = (bf16[4,96,640]{2,1,0:T(8,128)(2,1)S(1)}, bf16[4,96,640]{2,1,0:T(8,128)(2,1)}, u32[]{:S(2)}) copy-start(bf16[4,96,640]{2,1,0:T(8,128)(2,1)} %copy-done.22) | copy-start | bytes 1474564
  188.9 14.2 %copy-start.25 = (bf16[4,96,640]{2,1,0:T(8,128)(2,1)S(1)}, bf16[4,96,640]{2,1,0:T(8,128)(2,1)}, u32[]{:S(2)}) copy-start(bf16[4,96,640]{2,1,0:T(8,128)(2,1)} %copy-done.24) | copy-start | bytes 1474564
  188.9 22.7 %collective-permute-start.15 = (bf16[96,2560]{1,0:T(8,128)(2,1)S(1)}, bf16[96,2560]{1,0:T(8,128)(2,1)S(1)}, u32[]{:S(2)}, u32[]{:S(2)}) collective-permute-start(bf16[96,2560]{1,0:T(8,128)(2,1)S(1)} %get-tuple-element.263), channel_id=1, source_target_pairs={{0,1},{1,2},{2,3},{4,5},{5,6},{6,7},{8,9},{9,10},{10,11},{12,13},{... | collective-permute-start | bytes 1474568 | tf_op jit(solution)/shard_map/ppermute | solution.py:44
  191.1 20.5 %collective-permute-start.16 = (bf16[96,2560]{1,0:T(8,128)(2,1)S(1)}, bf16[96,2560]{1,0:T(8,128)(2,1)S(1)}, u32[]{:S(2)}, u32[]{:S(2)}) collective-permute-start(bf16[96,2560]{1,0:T(8,128)(2,1)S(1)} %get-tuple-element.264), channel_id=1, source_target_pairs={{1,0},{2,1},{3,2},{5,4},{6,5},{7,6},{9,8},{10,9},{11,10},{13,12},{... | collective-permute-start | bytes 1474568 | tf_op jit(solution)/shard_map/ppermute | solution.py:44
  192.4 19.2 %copy-start.20 = (bf16[96,2560]{1,0:T(8,128)(2,1)}, bf16[96,2560]{1,0:T(8,128)(2,1)S(1)}, u32[]{:S(2)}) copy-start(bf16[96,2560]{1,0:T(8,128)(2,1)S(1)} %collective-permute-done.36.right_ref.refs_10_) | copy-start | bytes 1474564
  199.4 20.2 %collective-permute-start.38 = (bf16[96,2560]{1,0:T(8,128)(2,1)S(1)}, bf16[96,2560]{1,0:T(8,128)(2,1)S(1)}, u32[]{:S(2)}, u32[]{:S(2)}) collective-permute-start(bf16[96,2560]{1,0:T(8,128)(2,1)S(1)} %get-tuple-element.279), channel_id=1, source_target_pairs={{0,1},{1,2},{2,3},{4,5},{5,6},{6,7},{8,9},{9,10},{10,11},{12,13},{... | collective-permute-start | bytes 1474568 | tf_op jit(solution)/shard_map/ppermute | solution.py:44
  201.5 18.2 %collective-permute-start.39 = (bf16[96,2560]{1,0:T(8,128)(2,1)S(1)}, bf16[96,2560]{1,0:T(8,128)(2,1)S(1)}, u32[]{:S(2)}, u32[]{:S(2)}) collective-permute-start(bf16[96,2560]{1,0:T(8,128)(2,1)S(1)} %get-tuple-element.280), channel_id=1, source_target_pairs={{1,0},{2,1},{3,2},{5,4},{6,5},{7,6},{9,8},{10,9},{11,10},{13,12},{... | collective-permute-start | bytes 1474568 | tf_op jit(solution)/shard_map/ppermute | solution.py:44
  212.3 17.5 %collective-permute-start.20 = (bf16[96,2560]{1,0:T(8,128)(2,1)S(1)}, bf16[96,2560]{1,0:T(8,128)(2,1)}, u32[]{:S(2)}, u32[]{:S(2)}) collective-permute-start(bf16[96,2560]{1,0:T(8,128)(2,1)S(1)} %unit_gradient.5.refs_0_), channel_id=1, source_target_pairs={{1,0},{2,1},{3,2},{5,4},{6,5},{7,6},{9,8},{10,9},{11,10},{13,12},{... | collective-permute-start | bytes 1474568 | tf_op jit(solution)/shard_map/ppermute | solution.py:44
  213.6 17.5 %collective-permute-start.17 = (bf16[96,2560]{1,0:T(8,128)(2,1)S(1)}, bf16[96,2560]{1,0:T(8,128)(2,1)}, u32[]{:S(2)}, u32[]{:S(2)}) collective-permute-start(bf16[96,2560]{1,0:T(8,128)(2,1)S(1)} %unit_gradient.5.refs_0_), channel_id=1, source_target_pairs={{0,1},{1,2},{2,3},{4,5},{5,6},{6,7},{8,9},{9,10},{10,11},{12,13},{... | collective-permute-start | bytes 1474568 | tf_op jit(solution)/shard_map/ppermute | solution.py:44
  219.7 45.8 %copy-start.17 = (bf16[96,2560]{1,0:T(8,128)(2,1)S(1)}, bf16[96,2560]{1,0:T(8,128)(2,1)}, u32[]{:S(2)}) copy-start(bf16[96,2560]{1,0:T(8,128)(2,1)} %copy-done.16) | copy-start | bytes 1474564
  219.7 45.8 %copy-start.19 = (bf16[96,2560]{1,0:T(8,128)(2,1)S(1)}, bf16[96,2560]{1,0:T(8,128)(2,1)}, u32[]{:S(2)}) copy-start(bf16[96,2560]{1,0:T(8,128)(2,1)} %copy-done.18) | copy-start | bytes 1474564
  220.3 20.0 %collective-permute-start.43 = (bf16[96,2560]{1,0:T(8,128)(2,1)S(1)}, bf16[96,2560]{1,0:T(8,128)(2,1)}, u32[]{:S(2)}, u32[]{:S(2)}) collective-permute-start(bf16[96,2560]{1,0:T(8,128)(2,1)S(1)} %unit_gradient.7.refs_7_), channel_id=1, source_target_pairs={{1,0},{2,1},{3,2},{5,4},{6,5},{7,6},{9,8},{10,9},{11,10},{13,12},{... | collective-permute-start | bytes 1474568 | tf_op jit(solution)/shard_map/ppermute | solution.py:44
  221.6 20.0 %collective-permute-start.40 = (bf16[96,2560]{1,0:T(8,128)(2,1)S(1)}, bf16[96,2560]{1,0:T(8,128)(2,1)}, u32[]{:S(2)}, u32[]{:S(2)}) collective-permute-start(bf16[96,2560]{1,0:T(8,128)(2,1)S(1)} %unit_gradient.7.refs_7_), channel_id=1, source_target_pairs={{0,1},{1,2},{2,3},{4,5},{5,6},{6,7},{8,9},{9,10},{10,11},{12,13},{... | collective-permute-start | bytes 1474568 | tf_op jit(solution)/shard_map/ppermute | solution.py:44
  229.8 21.1 %collective-permute-start.21 = (bf16[96,2560]{1,0:T(8,128)(2,1)}, bf16[96,2560]{1,0:T(8,128)(2,1)}, u32[]{:S(2)}, u32[]{:S(2)}) collective-permute-start(bf16[96,2560]{1,0:T(8,128)(2,1)} %collective-permute-done.20.refs_4_), channel_id=1, source_target_pairs={{1,0},{2,1},{5,4},{6,5},{9,8},{10,9},{13,12},{14,13},{17,16},{18,1... | collective-permute-start | bytes 1474568 | tf_op jit(solution)/shard_map/ppermute | solution.py:44
  231.1 21.1 %collective-permute-start.18 = (bf16[96,2560]{1,0:T(8,128)(2,1)}, bf16[96,2560]{1,0:T(8,128)(2,1)}, u32[]{:S(2)}, u32[]{:S(2)}) collective-permute-start(bf16[96,2560]{1,0:T(8,128)(2,1)} %collective-permute-done.17.refs_1_), channel_id=1, source_target_pairs={{1,2},{2,3},{5,6},{6,7},{9,10},{10,11},{13,14},{14,15},{17,18},{18... | collective-permute-start | bytes 1474568 | tf_op jit(solution)/shard_map/ppermute | solution.py:44
  240.3 21.1 %collective-permute-start.44 = (bf16[96,2560]{1,0:T(8,128)(2,1)}, bf16[96,2560]{1,0:T(8,128)(2,1)}, u32[]{:S(2)}, u32[]{:S(2)}) collective-permute-start(bf16[96,2560]{1,0:T(8,128)(2,1)} %collective-permute-done.43.refs_11_), channel_id=1, source_target_pairs={{1,0},{2,1},{5,4},{6,5},{9,8},{10,9},{13,12},{14,13},{17,16},{18,1... | collective-permute-start | bytes 1474568 | tf_op jit(solution)/shard_map/ppermute | solution.py:44
  241.6 21.1 %collective-permute-start.41 = (bf16[96,2560]{1,0:T(8,128)(2,1)}, bf16[96,2560]{1,0:T(8,128)(2,1)}, u32[]{:S(2)}, u32[]{:S(2)}) collective-permute-start(bf16[96,2560]{1,0:T(8,128)(2,1)} %collective-permute-done.40.refs_8_), channel_id=1, source_target_pairs={{1,2},{2,3},{5,6},{6,7},{9,10},{10,11},{13,14},{14,15},{17,18},{18... | collective-permute-start | bytes 1474568 | tf_op jit(solution)/shard_map/ppermute | solution.py:44
  250.9 23.7 %collective-permute-start.22 = (bf16[96,2560]{1,0:T(8,128)(2,1)}, bf16[96,2560]{1,0:T(8,128)(2,1)}, u32[]{:S(2)}, u32[]{:S(2)}) collective-permute-start(bf16[96,2560]{1,0:T(8,128)(2,1)} %collective-permute-done.21.refs_5_), channel_id=1, source_target_pairs={{1,0},{5,4},{9,8},{13,12},{17,16},{21,20},{25,24},{29,28}} | collective-permute-start | bytes 1474568 | tf_op jit(solution)/shard_map/ppermute | solution.py:44
  252.2 22.4 %collective-permute-start.19 = (bf16[96,2560]{1,0:T(8,128)(2,1)}, bf16[96,2560]{1,0:T(8,128)(2,1)}, u32[]{:S(2)}, u32[]{:S(2)}) collective-permute-start(bf16[96,2560]{1,0:T(8,128)(2,1)} %collective-permute-done.18.refs_2_), channel_id=1, source_target_pairs={{2,3},{6,7},{10,11},{14,15},{18,19},{22,23},{26,27},{30,31}} | collective-permute-start | bytes 1474568 | tf_op jit(solution)/shard_map/ppermute | solution.py:44
  261.4 13.9 %collective-permute-start.45 = (bf16[96,2560]{1,0:T(8,128)(2,1)}, bf16[96,2560]{1,0:T(8,128)(2,1)}, u32[]{:S(2)}, u32[]{:S(2)}) collective-permute-start(bf16[96,2560]{1,0:T(8,128)(2,1)} %collective-permute-done.44.refs_12_), channel_id=1, source_target_pairs={{1,0},{5,4},{9,8},{13,12},{17,16},{21,20},{25,24},{29,28}} | collective-permute-start | bytes 1474568 | tf_op jit(solution)/shard_map/ppermute | solution.py:44
  262.7 12.6 %collective-permute-start.42 = (bf16[96,2560]{1,0:T(8,128)(2,1)}, bf16[96,2560]{1,0:T(8,128)(2,1)}, u32[]{:S(2)}, u32[]{:S(2)}) collective-permute-start(bf16[96,2560]{1,0:T(8,128)(2,1)} %collective-permute-done.41.refs_9_), channel_id=1, source_target_pairs={{2,3},{6,7},{10,11},{14,15},{18,19},{22,23},{26,27},{30,31}} | collective-permute-start | bytes 1474568 | tf_op jit(solution)/shard_map/ppermute | solution.py:44
  285.0 66.3 %collective-permute-start.2 = (bf16[640,2560]{1,0:T(8,128)(2,1)}, bf16[640,2560]{1,0:T(8,128)(2,1)}, u32[]{:S(2)}, u32[]{:S(2)}) collective-permute-start(bf16[640,2560]{1,0:T(8,128)(2,1)} %get-tuple-element.182), channel_id=1, source_target_pairs={{0,16},{4,20},{8,24},{12,28},{16,0},{20,4},{24,8},{28,12},{1,17},{... | collective-permute-start | bytes 9830408 | tf_op jit(solution)/shard_map/cond/branch_2_fun/ppermute | solution.py:418
  286.9 21.0 %all-to-all-start.4 = ((bf16[4,192,640]{2,1,0:T(8,128)(2,1)}), bf16[4,192,640]{2,1,0:T(8,128)(2,1)S(1)}, u32[]{:S(2)}, u32[]{:S(2)}) async-start(bf16[4,192,640]{2,1,0:T(8,128)(2,1)} %get-tuple-element.183), calls=%async_computation.4 | async-start | bytes 1966080 | tf_op jit(solution)/shard_map/cond/branch_2_fun/all_to_all | solution.py:413
  308.0 21.0 %all-to-all-start.5 = ((bf16[4,192,640]{2,1,0:T(8,128)(2,1)}), bf16[4,192,640]{2,1,0:T(8,128)(2,1)S(1)}, u32[]{:S(2)}, u32[]{:S(2)}) async-start(bf16[4,192,640]{2,1,0:T(8,128)(2,1)} %get-tuple-element.200), calls=%async_computation.5 | async-start | bytes 1966080 | tf_op jit(solution)/shard_map/cond/branch_2_fun/all_to_all | solution.py:413
  (19 other events, 109.7 us)
